TPU v7x, 32 devices: a whole 2x2x4 slice. The times are simulated.
32 devices in a mesh: row: 16 (over z, x, core), col: 2 (over y).
Axes of the slice: x: 2, y: 2, z: 4, core: 2. Of those that a mesh axis runs over, the one named last changes fastest.
Arguments:
- p_tiles: bfloat16 [128, 2, 128, 128], P(('row', 'col')), may hold values from -0.5 to 0.5
- p_cols: int32 [128, 2], P(('row', 'col')), may hold values from 0 to 15, as said below
- q_tiles: bfloat16 [128, 6, 128, 128], P(('row', 'col')), may hold values from -1.796875 to 1.796875
- q_cols: int32 [128, 6], P(('row', 'col')), may hold values from 0 to 15, all different within a row
Outputs:
- coarse: float32 [2048, 2048], P('row', 'col')
Inputs may be any that keep to these rules, and one draw needn't show every extreme that they name: `p_cols`: the 2 coarse tiles in one row differ; among the fine blocks held by the devices of one index of col, every coarse tile is named at least once and at most 16 times, and some tile exactly 16 times. `q_cols`: the 6 coarse tiles in one row differ; every coarse tile appears somewhere.
All inputs are finite; a program needn't handle non-finite values.
Results may differ from a plain program's by a relative error of at most 0.0003.
Values may be sent and summed in bfloat16 or wider, within the bound.
No kernel may reach another device: no remote copies, remote signals or barrier semaphores. Data moves between devices by JAX's collectives and lax.ppermute only.
A program may use at most 128 MiB of HBM per device.

v0:
```python
import math

import jax
import jax.numpy as jnp
from jax import lax
from jax.sharding import PartitionSpec as P


def spread_tiles(tile_set, columns, tile_count):
    blocks, per_block, extent, _ = tile_set.shape
    flipped = jnp.swapaxes(tile_set, 2, 3)
    fine_ids = jnp.broadcast_to(jnp.arange(blocks, dtype=jnp.int32)[:, None], (blocks, per_block))
    placed = jnp.zeros((tile_count, extent, blocks, extent), tile_set.dtype)
    placed = placed.at[columns, :, fine_ids, :].set(flipped)
    return placed.reshape(tile_count * extent, blocks * extent)


def fold_tiles(summed, transposed, tile_set, columns):
    blocks, per_block, extent, _ = tile_set.shape
    height = transposed.shape[0]
    bundle = math.gcd(blocks, 8)
    tile_groups = tile_set.reshape(blocks // bundle, bundle, per_block, extent, extent)
    column_groups = columns.reshape(blocks // bundle, bundle * per_block)

    def one_group(running, inputs):
        position, bundle_tiles, coarse_ids = inputs
        offset = position * bundle * extent
        stripe = lax.dynamic_slice_in_dim(transposed, offset, bundle * extent, 1).reshape(
            height, bundle, extent
        )
        product = jnp.einsum(
            "rfa,fkab->rfkb", stripe, bundle_tiles, preferred_element_type=jnp.float32
        )
        tiled = running.reshape(height, -1, extent)
        tiled = tiled.at[:, coarse_ids, :].add(product.reshape(height, bundle * per_block, extent))
        return (tiled.reshape(height, -1), None)

    counter = jnp.arange(blocks // bundle, dtype=jnp.int32)
    summed, _ = lax.scan(one_group, summed, (counter, tile_groups, column_groups))
    return summed


def body(p_tiles, p_cols, q_tiles, q_cols):
    extent = p_tiles.shape[2]
    tile_count = lax.axis_size("row")
    expanded = spread_tiles(p_tiles, p_cols, tile_count)
    transposed = lax.all_to_all(expanded, "row", split_axis=0, concat_axis=1, tiled=True)
    empty = jnp.zeros((transposed.shape[0], tile_count * extent), jnp.float32)
    partial_sum = fold_tiles(
        empty,
        transposed,
        lax.all_gather(q_tiles, "row", axis=0, tiled=True),
        lax.all_gather(q_cols, "row", axis=0, tiled=True),
    )
    return lax.psum_scatter(partial_sum, "col", scatter_dimension=1, tiled=True)


def solution(mesh):
    placed = (
        P(("row", "col"), None, None, None),
        P(("row", "col"), None),
        P(("row", "col"), None, None, None),
        P(("row", "col"), None),
    )
    return jax.shard_map(
        body, mesh=mesh, in_specs=placed, out_specs=P("row", "col"), check_vma=False
    )
```

profile of v0, /device:TPU:1, one launch (start us, length us, event | category | flops | bytes accessed | tf_op | source)
XLA Modules:
  0.0 310.4 jit_solution(5984395358838034556)
XLA Ops:
  6.5 0.7 all-gather.3.cloned.1.call-update
  7.3 1.1 copy.23
  8.4 0.7 or_select_fusion
  9.8 0.9 scatter_fusion.1
  10.6 2.6 copy.24
  13.3 7.5 %all-to-all-start = ((bf16[16,128,512]{1,2,0:T(8,128)(2,1)}), bf16[16,128,512]{1,2,0:T(8,128)(2,1)}, u32[]{:S(2)}, u32[]{:S(2)}) async-start(bf16[16,128,512]{1,2,0:T(8,128)(2,1)} %bitcast.65), calls=%async_computation | async-start | bytes 4194304 | tf_op jit(solution)/shard_map/all_to_all | solution.py:47
  20.8 75.3 %all-gather = s32[16,4,6]{2,1,0:T(4,128)S(1)} all-gather(s32[1,4,6]{2,1,0:T(4,128)S(1)} %bitcast.68), channel_id=1, replica_groups=mesh['row'=16,'col'=2] {'row'}, dimensions={0}, use_global_device_ids=true | all-gather | bytes 1632 | tf_op jit(solution)/shard_map/all_gather | solution.py:53
  96.1 52.8 %all-gather.3.cloned.1.call-done = bf16[64,6,128,128]{3,2,1,0:T(8,128)(2,1)} async-done(((bf16[4,6,128,128]{3,2,1,0:T(8,128)(2,1)}), bf16[64,6,128,128]{3,2,1,0:T(8,128)(2,1)}) %all-gather.3.cloned.1.call-update) | async-done | bytes 12582928 | tf_op jit(solution)/shard_map/all_gather | solution.py:52
  149.0 1.1 broadcast_in_dim.8
  150.0 131.4 %while.12 = (s32[]{:T(128)}, f32[128,2048]{0,1:T(8,128)}, s32[8,48]{1,0:T(8,128)S(1)}, bf16[8,8,6,128,128]{4,3,2,1,0:T(8,128)(2,1)}, s32[8]{0:T(128)S(1)}, /*ind...) while((s32[]{:T(128)}, f32[128,2048]{0,1:T(8,128)}, s32[8,48]{1,0:T(8,128)S(1)}, ...), condition=%wide.region_3.4_spmd, body=%wide.region_1.3_spmd.sunk | while | flops 202113168 | bytes 25429224 | solution.py:39
  150.0 0.7 dynamic_slice.46
  151.4 1.0 constant_dynamic-slice_fusion.3
  152.4 2.1 fusion.17
  154.4 2.4 copy.35
  156.8 1.6 copy.34
  158.4 6.7 %scatter_fusion = f32[128,16,128]{2,0,1:T(8,128)S(1)} fusion(f32[128,16,128]{2,0,1:T(8,128)S(1)} %copy.34, s32[48]{0:T(128)S(1)} %fusion.16, f32[48,128,128]{2,1,0:T(8,128)} %bitcast.61), kind=kCustom, calls=%fused_computation.clone.1 | custom fusion | flops 786432 | bytes 9437376 | tf_op jit(solution)/shard_map/while/body/eval_jaxpr/scatter-add | solution.py:35
  165.1 1.4 copy.36
  167.8 1.0 constant_dynamic-slice_fusion.3
  168.8 2.1 fusion.17
  170.9 2.4 copy.35
  173.2 1.6 copy.34
  174.8 6.7 %scatter_fusion = f32[128,16,128]{2,0,1:T(8,128)S(1)} fusion(f32[128,16,128]{2,0,1:T(8,128)S(1)} %copy.34, s32[48]{0:T(128)S(1)} %fusion.16, f32[48,128,128]{2,1,0:T(8,128)} %bitcast.61), kind=kCustom, calls=%fused_computation.clone.1 | custom fusion | flops 786432 | bytes 9437376 | tf_op jit(solution)/shard_map/while/body/eval_jaxpr/scatter-add | solution.py:35
  181.5 1.4 copy.36
  184.2 1.0 constant_dynamic-slice_fusion.3
  185.2 2.1 fusion.17
  187.3 2.4 copy.35
  189.7 1.6 copy.34
  191.2 6.7 %scatter_fusion = f32[128,16,128]{2,0,1:T(8,128)S(1)} fusion(f32[128,16,128]{2,0,1:T(8,128)S(1)} %copy.34, s32[48]{0:T(128)S(1)} %fusion.16, f32[48,128,128]{2,1,0:T(8,128)} %bitcast.61), kind=kCustom, calls=%fused_computation.clone.1 | custom fusion | flops 786432 | bytes 9437376 | tf_op jit(solution)/shard_map/while/body/eval_jaxpr/scatter-add | solution.py:35
  198.0 1.4 copy.36
  199.3 0.7 dynamic_slice.46
  200.7 1.0 constant_dynamic-slice_fusion.3
  201.6 2.1 fusion.17
  203.7 2.4 copy.35
  206.1 1.6 copy.34
  207.6 6.7 %scatter_fusion = f32[128,16,128]{2,0,1:T(8,128)S(1)} fusion(f32[128,16,128]{2,0,1:T(8,128)S(1)} %copy.34, s32[48]{0:T(128)S(1)} %fusion.16, f32[48,128,128]{2,1,0:T(8,128)} %bitcast.61), kind=kCustom, calls=%fused_computation.clone.1 | custom fusion | flops 786432 | bytes 9437376 | tf_op jit(solution)/shard_map/while/body/eval_jaxpr/scatter-add | solution.py:35
  214.4 1.4 copy.36
  215.7 0.7 dynamic_slice.46
  217.1 1.0 constant_dynamic-slice_fusion.3
  218.1 2.1 fusion.17
  220.1 2.4 copy.35
  222.5 1.6 copy.34
  224.1 6.7 %scatter_fusion = f32[128,16,128]{2,0,1:T(8,128)S(1)} fusion(f32[128,16,128]{2,0,1:T(8,128)S(1)} %copy.34, s32[48]{0:T(128)S(1)} %fusion.16, f32[48,128,128]{2,1,0:T(8,128)} %bitcast.61), kind=kCustom, calls=%fused_computation.clone.1 | custom fusion | flops 786432 | bytes 9437376 | tf_op jit(solution)/shard_map/while/body/eval_jaxpr/scatter-add | solution.py:35
  230.8 1.4 copy.36
  233.5 1.0 constant_dynamic-slice_fusion.3
  234.5 2.1 fusion.17
  236.6 2.4 copy.35
  238.9 1.6 copy.34
  240.5 6.7 %scatter_fusion = f32[128,16,128]{2,0,1:T(8,128)S(1)} fusion(f32[128,16,128]{2,0,1:T(8,128)S(1)} %copy.34, s32[48]{0:T(128)S(1)} %fusion.16, f32[48,128,128]{2,1,0:T(8,128)} %bitcast.61), kind=kCustom, calls=%fused_computation.clone.1 | custom fusion | flops 786432 | bytes 9437376 | tf_op jit(solution)/shard_map/while/body/eval_jaxpr/scatter-add | solution.py:35
  247.2 1.4 copy.36
  248.6 0.7 dynamic_slice.46
  249.9 1.0 constant_dynamic-slice_fusion.3
  250.9 2.1 fusion.17
  253.0 2.4 copy.35
  255.4 1.6 copy.34
  256.9 6.7 %scatter_fusion = f32[128,16,128]{2,0,1:T(8,128)S(1)} fusion(f32[128,16,128]{2,0,1:T(8,128)S(1)} %copy.34, s32[48]{0:T(128)S(1)} %fusion.16, f32[48,128,128]{2,1,0:T(8,128)} %bitcast.61), kind=kCustom, calls=%fused_computation.clone.1 | custom fusion | flops 786432 | bytes 9437376 | tf_op jit(solution)/shard_map/while/body/eval_jaxpr/scatter-add | solution.py:35
  263.7 1.4 copy.36
  266.4 1.0 constant_dynamic-slice_fusion.3
  267.4 2.1 fusion.17
  269.4 2.4 copy.35
  271.8 1.6 copy.34
  273.4 6.7 %scatter_fusion = f32[128,16,128]{2,0,1:T(8,128)S(1)} fusion(f32[128,16,128]{2,0,1:T(8,128)S(1)} %copy.34, s32[48]{0:T(128)S(1)} %fusion.16, f32[48,128,128]{2,1,0:T(8,128)} %bitcast.61), kind=kCustom, calls=%fused_computation.clone.1 | custom fusion | flops 786432 | bytes 9437376 | tf_op jit(solution)/shard_map/while/body/eval_jaxpr/scatter-add | solution.py:35
  280.1 1.4 copy.36
  281.4 2.5 copy.26
  284.0 19.6 %reduce-scatter.2.cloned.1.call-done = f32[128,1024]{1,0:T(8,128)} async-done(((f32[128,2048]{1,0:T(8,128)}), f32[128,1024]{1,0:T(8,128)}) %reduce-scatter.2.cloned.1.call-update) | async-done | bytes 524304 | tf_op jit(solution)/shard_map/reduce_scatter | solution.py:55
  (23 shorter events, 3.5 us)
Async XLA Ops:
  6.5 142.4 %all-gather.3.cloned.1.call-start = ((), (), s32[]{:S(2)}) async-start(), calls=%async_computation.2 | async-start | bytes 13369344 | tf_op jit(solution)/shard_map/all_gather | solution.py:52
  13.3 7.5 %copy-start = (s32[4,6]{1,0:T(4,128)S(1)}, s32[4,6]{1,0:T(4,128)}, u32[]{:S(2)}) copy-start(s32[4,6]{1,0:T(4,128)} %param.9) | copy-start | bytes 292
  13.3 82.9 %all-to-all-start = ((bf16[16,128,512]{1,2,0:T(8,128)(2,1)}), bf16[16,128,512]{1,2,0:T(8,128)(2,1)}, u32[]{:S(2)}, u32[]{:S(2)}) async-start(bf16[16,128,512]{1,2,0:T(8,128)(2,1)} %bitcast.65), calls=%async_computation | async-start | bytes 4194304 | tf_op jit(solution)/shard_map/all_to_all | solution.py:47
  20.7 282.9 %reduce-scatter.2.cloned.1.call-start = ((), (), s32[]{:S(2)}) async-start(), calls=%async_computation.3 | async-start | bytes 1572864 | tf_op jit(solution)/shard_map/reduce_scatter | solution.py:55
Sparse Core Ops, SparseCore 0:
  9.6 139.2 all-gather.2
  284.1 19.4 reduce-scatter.1
where the time goes:
time: 313 us; the launch traced here: 310 us
  blocking collectives  75.3 us (24%)
  waiting for transfers between devices  73.1 us (23%)
  local copies, waits for them, and re-layouts  64.3 us (21%)
  other arithmetic  54.6 us (17%)
  matrix products  16.5 us (5%)
  between operations  13.4 us (4%)
  starting transfers between devices  7.49 us (2%)
  loops' own time  5.79 us (2%)
    all_gather x1, blocking collectives, body(): lax.all_gather(q_cols, 'row', axis=0, tiled=True)  75.3 us
    scatter-add x8, other arithmetic, one_group(): tiled.at[:, coarse_ids, :]  53.8 us
    all_gather x1, waiting for transfers between devices, body(): lax.all_gather(q_tiles, 'row', axis=0, tiled=True)  52.8 us
    reduce_scatter x1, waiting for transfers between devices, body(): return lax.psum_scatter(partial_sum, 'col', scatter_dimension=1, tiled=True)  19.6 us
    reshape x8, local copies, waits for them, and re-layouts, one_group(): product.reshape(height, bundle * per_block, extent)  18.9 us
    dot_general x8, matrix products, one_group(): jnp.einsum('rfa,fkab->rfkb', stripe, bundle_tiles, preferred_element_type...  16.5 us
    reshape x8, local copies, waits for them, and re-layouts, one_group(): tiled = running.reshape(height, -1, extent)  12.4 us
    scatter-add x8, local copies, waits for them, and re-layouts, one_group(): tiled.at[:, coarse_ids, :]  10.9 us
  transfers between devices with their start and end apart: 3, of which 2 were waited for; matrix products, arithmetic and copies ran while one was open for 2% of the time, Pallas kernels for 0%

commit v1 on v0

v1 whole, which is shorter than its diff:
```python
import functools

import jax
import jax.numpy as jnp
from jax import lax
from jax.experimental import pallas as pl
from jax.experimental.pallas import tpu as pltpu
from jax.sharding import Mesh
from jax.sharding import PartitionSpec as P

SEATS = 8


def slice_kernel(q_ref, out_ref):
    blocks, per_block, extent, _ = q_ref.shape
    strip = extent // SEATS
    for f in range(blocks):
        for k in range(per_block):
            flipped = q_ref[f, k].T
            for j in range(SEATS):
                out_ref[j, f, k] = flipped[j * strip:(j + 1) * strip]


def product_kernel(tile_count, p_ids, q_ids, q_ref, p_ref, acc_ref):
    blocks, rows, _ = q_ref.shape
    per_p = p_ref.shape[1]
    strip = acc_ref.shape[1]
    per_q = rows // strip
    acc_ref[...] = jnp.zeros_like(acc_ref)

    def one_block(f, carry):
        left = q_ref[f]
        for k in range(per_p):
            product = jnp.dot(left, p_ref[f, k], preferred_element_type=jnp.float32)
            base = p_ids[f * per_p + k] * tile_count
            for l in range(per_q):
                spot = base + q_ids[f * per_q + l]
                acc_ref[spot] += product[l * strip:(l + 1) * strip]
        return carry

    lax.fori_loop(0, blocks, one_block, 0)


def finish_kernel(x_ref, out_ref):
    seats, tiles, strip, extent = x_ref.shape
    for t in range(tiles):
        stacked = x_ref[:, t].reshape(seats * strip, extent)
        out_ref[:, t * extent:(t + 1) * extent] = stacked.T


def body(p_tiles, p_cols, q_tiles, q_cols):
    blocks, per_p, extent, _ = p_tiles.shape
    per_q = q_tiles.shape[1]
    planes = lax.axis_size("plane")
    side, cols = lax.axis_size("side"), lax.axis_size("col")
    tile_count = planes * side
    strip = extent // SEATS
    seat = ("side", "col")

    sliced = pl.pallas_call(
        slice_kernel,
        out_shape=jax.ShapeDtypeStruct((SEATS, blocks, per_q, strip, extent), q_tiles.dtype),
        name="cut_columns",
    )(q_tiles)
    q_here = lax.all_to_all(sliced, seat, split_axis=0, concat_axis=0, tiled=True)
    p_here = lax.all_gather(p_tiles, seat, axis=0, tiled=True)
    ids = jnp.concatenate([p_cols, q_cols], axis=1)
    ids = lax.all_gather(ids, seat, axis=0, tiled=True)

    total = SEATS * blocks
    acc = pl.pallas_call(
        functools.partial(product_kernel, tile_count),
        out_shape=jax.ShapeDtypeStruct((tile_count * tile_count, strip, extent), jnp.float32),
        grid_spec=pltpu.PrefetchScalarGridSpec(
            num_scalar_prefetch=2,
            grid=(),
            in_specs=[pl.BlockSpec(memory_space=pltpu.VMEM)] * 2,
            out_specs=pl.BlockSpec(memory_space=pltpu.VMEM),
        ),
        compiler_params=pltpu.CompilerParams(vmem_limit_bytes=40 << 20),
        name="products",
    )(
        ids[:, :per_p].reshape(-1),
        ids[:, per_p:].reshape(-1),
        q_here.reshape(total, per_q * strip, extent),
        p_here.reshape(total, per_p, extent, extent),
    )

    parts = acc.reshape(planes, side * tile_count, strip, extent)
    here = lax.axis_index("plane")

    def pick(place):
        place = jnp.clip(place, 0, planes - 1)
        return lax.dynamic_index_in_dim(parts, place, 0, keepdims=False)

    up = down = None
    for step in range(planes - 1):
        send_up = pick(planes - 1 - step + here)
        send_down = pick(here - (planes - 1 - step))
        if step:
            send_up, send_down = send_up + up, send_down + down
        up = lax.ppermute(send_up, "plane", [(z, z + 1) for z in range(step + 1)])
        down = lax.ppermute(
            send_down, "plane", [(planes - 1 - z, planes - 2 - z) for z in range(step + 1)]
        )
    summed = pick(here)
    if planes > 1:
        summed = summed + up + down

    mine = summed.reshape(SEATS, tile_count // cols, strip, extent)
    landed = lax.all_to_all(mine, seat, split_axis=0, concat_axis=0, tiled=True)
    return pl.pallas_call(
        finish_kernel,
        out_shape=jax.ShapeDtypeStruct((extent, tile_count // cols * extent), jnp.float32),
        name="turn",
    )(landed)


def solution(mesh):
    rows, cols = mesh.devices.shape
    side = SEATS // cols
    inner = Mesh(mesh.devices.reshape(rows // side, side, cols), ("plane", "side", "col"))
    every = ("plane", "side", "col")
    placed = (
        P(every, None, None, None),
        P(every, None),
        P(every, None, None, None),
        P(every, None),
    )
    return jax.shard_map(
        body, mesh=inner, in_specs=placed, out_specs=P(("plane", "side"), "col"), check_vma=False
    )
```

time: 313 us -> 136 us (0.43)
  local copies, waits for them, and re-layouts: 64.3 us -> 2.84 us
  other arithmetic: 54.6 us -> 3.25 us
  blocking collectives: 75.3 us -> 40.3 us
  waiting for transfers between devices: 73.1 us -> 44.7 us
  matrix products: 16.5 us -> 0 us
  starting transfers between devices: 7.49 us -> 20.6 us
  Pallas kernels: 0 us -> 10.2 us
  loops' own time: 5.79 us -> 0 us
    scatter-add x8 -> x0, other arithmetic: 53.8 us -> none  [one_group(): tiled.at[:, coarse_ids, :]]
    all_gather x1, blocking collectives: 75.3 us -> 25 us  [body(): ids = lax.all_gather(ids, seat, axis=0, tiled=True)]
    all_gather x1, waiting for transfers between devices: 52.8 us -> 3.93 us  [body(): p_here = lax.all_gather(p_tiles, seat, axis=0, tiled=True)]
    ppermute x0 -> x6, waiting for transfers between devices: none -> 40.1 us  [the longest x3 27 us: body(): up = lax.ppermute(send_up, 'plane', [(z, z + 1) for z in range(step + 1)])]
    reshape x17 -> x2, local copies, waits for them, and re-layouts: 31.4 us -> 0.21 us  [the longest x1 0.11 us: body(): ids[:, per_p:].reshape(-1)]
    reduce_scatter x1 -> x0, waiting for transfers between devices: 19.6 us -> none  [body(): return lax.psum_scatter(partial_sum, 'col', scatter_dimension=1, tiled=True)]
    dot_general x8 -> x0, matrix products: 16.5 us -> none  [one_group(): jnp.einsum('rfa,fkab->rfkb', stripe, bundle_tiles, preferred_element_type...]
    ppermute x0 -> x6, starting transfers between devices: none -> 15.4 us  [the longest x3 12 us: body(): up = lax.ppermute(send_up, 'plane', [(z, z + 1) for z in range(step + 1)])]
  transfers between devices with their start and end apart: 3 -> 8, of which waited for: 2 -> 5; matrix products, arithmetic and copies ran while one was open for 2% -> 1% of each run, Pallas kernels for 0% -> 2%
where the time goes in v1:
time: 136 us; the launch traced here: 135 us
  waiting for transfers between devices  44.7 us (33%)
  blocking collectives  40.3 us (30%)
  starting transfers between devices  20.6 us (15%)
  between operations  13.5 us (10%)
  Pallas kernels  10.2 us (7%)
  other arithmetic  3.25 us (2%)
  local copies, waits for them, and re-layouts  2.84 us (2%)
    ppermute x3, waiting for transfers between devices, body(): up = lax.ppermute(send_up, 'plane', [(z, z + 1) for z in range(step + 1)])  27 us
    all_gather x1, blocking collectives, body(): ids = lax.all_gather(ids, seat, axis=0, tiled=True)  25 us
    all_to_all x1, blocking collectives, body(): landed = lax.all_to_all(mine, seat, split_axis=0, concat_axis=0, tiled=True)  15.3 us
    ppermute x3, waiting for transfers between devices, body(): lax.ppermute(send_down, 'plane', [(planes - 1 - z, planes - 2 - z) for z...  13.1 us
    ppermute x3, starting transfers between devices, body(): up = lax.ppermute(send_up, 'plane', [(z, z + 1) for z in range(step + 1)])  12 us
    pallas_call x1, Pallas kernels, body(): pl.pallas_call(functools.partial(product_kernel, tile_count), out_shape=j...  5.91 us
    all_to_all x1, starting transfers between devices, body(): lax.all_to_all(sliced, seat, split_axis=0, concat_axis=0, tiled=True)  5.22 us
    all_gather x1, waiting for transfers between devices, body(): p_here = lax.all_gather(p_tiles, seat, axis=0, tiled=True)  3.93 us
  transfers between devices with their start and end apart: 8, of which 5 were waited for; matrix products, arithmetic and copies ran while one was open for 1% of the time, Pallas kernels for 2%

profile of v1, /device:TPU:1, one launch (start us, length us, event | category | flops | bytes accessed | tf_op | source)
XLA Modules:
  0.0 135.5 jit_solution(5075178101865656838)
XLA Ops:
  6.5 0.0 copy-start.2
  6.5 0.0 copy-start.1
  6.5 0.0 all-gather.3.cloned.1.call-start
  6.5 0.7 all-gather.3.cloned.1.call-update
  7.3 2.3 %cut_columns.1 = bf16[8,4,6,16,128]{4,3,2,1,0:T(8,128)(2,1)} custom-call(bf16[4,6,128,128]{3,2,1,0:T(8,128)(2,1)} %q_ref.1), custom_call_target="tpu_custom_call" | custom-call | tf_op jit(solution)/shard_map/cut_columns/pallas_call | solution.py:60
  9.5 5.2 %all-to-all-start = ((bf16[8,4,6,16,128]{4,3,2,1,0:T(8,128)(2,1)}), bf16[8,4,6,16,128]{4,3,2,1,0:T(8,128)(2,1)S(1)}, u32[]{:S(2)}, u32[]{:S(2)}) async-start(bf16[8,4,6,16,128]{4,3,2,1,0:T(8,128)(2,1)} %cut_columns.1), calls=%async_computation | async-start | bytes 1572864 | tf_op jit(solution)/shard_map/all_to_all | solution.py:65
  14.8 0.0 copy-done.2
  14.8 0.1 copy.7
  14.9 0.0 copy-done.1
  14.9 0.1 add_bitcast_fusion
  14.9 25.0 %all-gather = s32[8,4,8]{2,1,0:T(4,128)S(1)} all-gather(s32[1,4,8]{2,1,0:T(4,128)S(1)} %add_bitcast_fusion), channel_id=1, replica_groups=mesh['plane'=4,'side'=4,'col'=2] {'side','col'}, dimensions={0}, use_global_device_ids=true | all-gather | bytes 1152 | tf_op jit(solution)/shard_map/all_gather | solution.py:68
  39.9 0.1 slice.9
  40.0 0.1 reshape.16.q_ids
  40.1 0.1 reshape.15.p_ids
  40.2 0.0 all-to-all-done
  40.2 3.9 %all-gather.3.cloned.1.call-done.p_ref = bf16[32,2,128,128]{3,2,1,0:T(8,128)(2,1)} async-done(((bf16[4,2,128,128]{3,2,1,0:T(8,128)(2,1)}), bf16[32,2,128,128]{3,2,1,0:T(8,128)(2,1)}) %all-gather.3.cloned.1.call-update) | async-done | bytes 2097168 | tf_op jit(solution)/shard_map/all_gather | solution.py:66
  44.1 0.0 copy-start
  44.1 1.6 %copy-done = bf16[32,2,128,128]{3,2,1,0:T(8,128)(2,1)S(1)} copy-done((bf16[32,2,128,128]{3,2,1,0:T(8,128)(2,1)S(1)}, bf16[32,2,128,128]{3,2,1,0:T(8,128)(2,1)}, u32[]{:S(2)}) %copy-start) | copy-done | bytes 2097176
  45.7 5.9 %products.1 = f32[256,16,128]{2,1,0:T(8,128)S(1)} custom-call(s32[64]{0:T(128)S(1)} %reshape.15.p_ids, s32[192]{0:T(256)S(1)} %reshape.16.q_ids, bf16[32,96,128]{2,1,0:T(8,128)(2,1)S(1)} %bitcast.28, bf16[32,2,128,128]{3,2,1,0:T(8,128)(2,1)S(1)} %copy-done), custom_call_target="tpu_custom_call" | custom-call | tf_op jit(solution)/shard_map/products/pallas_call | solution.py:71
  51.7 0.9 dynamic-slice_bitcast_fusion.1
  52.5 3.1 %collective-permute-start = (f32[64,16,128]{2,1,0:T(8,128)S(1)}, f32[64,16,128]{2,1,0:T(8,128)S(1)}, u32[]{:S(2)}, u32[]{:S(2)}) collective-permute-start(f32[64,16,128]{2,1,0:T(8,128)S(1)} %get-tuple-element.7), channel_id=1, source_target_pairs={{0,8},{1,9},{2,10},{3,11},{4,12},{5,13},{6,14},{7,15}} | collective-permute-start | bytes 1572872 | tf_op jit(solution)/shard_map/ppermute | solution.py:102
  55.7 1.5 %collective-permute-start.3 = (f32[64,16,128]{2,1,0:T(8,128)}, f32[64,16,128]{2,1,0:T(8,128)}, u32[]{:S(2)}, u32[]{:S(2)}) collective-permute-start(f32[64,16,128]{2,1,0:T(8,128)} %get-tuple-element.8), channel_id=1, source_target_pairs={{24,16},{25,17},{26,18},{27,19},{28,20},{29,21},{30,22},{31,23}} | collective-permute-start | bytes 1572872 | tf_op jit(solution)/shard_map/ppermute | solution.py:103
  57.1 9.6 %collective-permute-done = f32[64,16,128]{2,1,0:T(8,128)S(1)} collective-permute-done((f32[64,16,128]{2,1,0:T(8,128)S(1)}, f32[64,16,128]{2,1,0:T(8,128)S(1)}, u32[]{:S(2)}, u32[]{:S(2)}) %collective-permute-start) | collective-permute-done | bytes 524320 | tf_op jit(solution)/shard_map/ppermute | solution.py:102
  66.7 0.1 bitcast_add_fusion.2
  66.8 4.1 %collective-permute-start.1 = (f32[64,16,128]{2,1,0:T(8,128)S(1)}, f32[64,16,128]{2,1,0:T(8,128)S(1)}, u32[]{:S(2)}, u32[]{:S(2)}) collective-permute-start(f32[64,16,128]{2,1,0:T(8,128)S(1)} %bitcast_add_fusion.2), channel_id=1, source_target_pairs={{0,8},{8,16},{1,9},{9,17},{2,10},{10,18},{3,11},{11,19},{4,12},{12... | collective-permute-start | bytes 1572872 | tf_op jit(solution)/shard_map/ppermute | solution.py:102
  70.9 0.0 collective-permute-done.3
  70.9 10.1 %collective-permute-done.1 = f32[64,16,128]{2,1,0:T(8,128)S(1)} collective-permute-done((f32[64,16,128]{2,1,0:T(8,128)S(1)}, f32[64,16,128]{2,1,0:T(8,128)S(1)}, u32[]{:S(2)}, u32[]{:S(2)}) %collective-permute-start.1) | collective-permute-done | bytes 524320 | tf_op jit(solution)/shard_map/ppermute | solution.py:102
  81.0 2.1 %bitcast_add_fusion.3 = (f32[64,16,128]{2,1,0:T(8,128)}, f32[64,16,128]{2,1,0:T(8,128)}) fusion(f32[64,16,128]{2,1,0:T(8,128)S(1)} %collective-permute-done.1, f32[4,64,16,128]{3,2,1,0:T(8,128)S(1)} %bitcast.25, s32[]{:T(128)S(6)} %min.23, f32[64,16,128]{2,1,0:T(8,128)} %collective-permute-done.3, s32[]{:T(128)S(6)} %min.27), kind=kLoop, calls=%fused_computation.3 | loop fusion | flops 262144 | bytes 3145736 | tf_op jit(solution)/shard_map/add | solution.py:101
  83.2 0.7 collective-permute-start.4
  83.8 4.7 %collective-permute-start.2 = (f32[64,16,128]{2,1,0:T(8,128)}, f32[64,16,128]{2,1,0:T(8,128)S(1)}, u32[]{:S(2)}, u32[]{:S(2)}) collective-permute-start(f32[64,16,128]{2,1,0:T(8,128)} %get-tuple-element.5), channel_id=1, source_target_pairs={{0,8},{8,16},{16,24},{1,9},{9,17},{17,25},{2,10},{10,18},{18,26},{... | collective-permute-start | bytes 1572872 | tf_op jit(solution)/shard_map/ppermute | solution.py:102
  88.6 0.0 collective-permute-done.4
  88.6 0.9 bitcast_add_fusion.1
  89.5 1.3 collective-permute-start.5
  90.8 7.3 %collective-permute-done.2 = f32[64,16,128]{2,1,0:T(8,128)S(1)} collective-permute-done((f32[64,16,128]{2,1,0:T(8,128)}, f32[64,16,128]{2,1,0:T(8,128)S(1)}, u32[]{:S(2)}, u32[]{:S(2)}) %collective-permute-start.2) | collective-permute-done | bytes 524320 | tf_op jit(solution)/shard_map/ppermute | solution.py:102
  98.1 13.1 %collective-permute-done.5 = f32[64,16,128]{2,1,0:T(8,128)S(1)} collective-permute-done((f32[64,16,128]{2,1,0:T(8,128)}, f32[64,16,128]{2,1,0:T(8,128)S(1)}, u32[]{:S(2)}, u32[]{:S(2)}) %collective-permute-start.5) | collective-permute-done | bytes 524320 | tf_op jit(solution)/shard_map/ppermute | solution.py:103
  111.2 0.1 fusion
  111.3 15.3 %all_to_all.10.x_ref = f32[8,8,16,128]{3,2,1,0:T(8,128)} all-to-all(f32[8,8,16,128]{3,2,1,0:T(8,128)S(1)} %bitcast.29), channel_id=1, replica_groups=mesh['plane'=4,'side'=4,'col'=2] {'side','col'}, dimensions={0} | all-to-all | bytes 1048576 | tf_op jit(solution)/shard_map/all_to_all | solution.py:111
  126.6 2.0 %turn.1 = f32[128,1024]{1,0:T(8,128)} custom-call(f32[8,8,16,128]{3,2,1,0:T(8,128)} %all_to_all.10.x_ref), custom_call_target="tpu_custom_call" | custom-call | tf_op jit(solution)/shard_map/turn/pallas_call | solution.py:112
Async XLA Ops:
  6.5 8.2 %copy-start.2 = (s32[4,2]{0,1:T(2,128)S(1)}, s32[4,2]{0,1:T(2,128)}, u32[]{:S(2)}) copy-start(s32[4,2]{0,1:T(2,128)} %param.5) | copy-start | bytes 100
  6.5 8.3 %copy-start.1 = (s32[4,6]{1,0:T(4,128)S(1)}, s32[4,6]{1,0:T(4,128)}, u32[]{:S(2)}) copy-start(s32[4,6]{1,0:T(4,128)} %param.7) | copy-start | bytes 292
  6.5 37.6 %all-gather.3.cloned.1.call-start = ((), (), s32[]{:S(2)}) async-start(), calls=%async_computation.2 | async-start | bytes 2359296 | tf_op jit(solution)/shard_map/all_gather | solution.py:66
  9.5 30.7 %all-to-all-start = ((bf16[8,4,6,16,128]{4,3,2,1,0:T(8,128)(2,1)}), bf16[8,4,6,16,128]{4,3,2,1,0:T(8,128)(2,1)S(1)}, u32[]{:S(2)}, u32[]{:S(2)}) async-start(bf16[8,4,6,16,128]{4,3,2,1,0:T(8,128)(2,1)} %cut_columns.1), calls=%async_computation | async-start | bytes 1572864 | tf_op jit(solution)/shard_map/all_to_all | solution.py:65
  44.1 1.6 %copy-start = (bf16[32,2,128,128]{3,2,1,0:T(8,128)(2,1)S(1)}, bf16[32,2,128,128]{3,2,1,0:T(8,128)(2,1)}, u32[]{:S(2)}) copy-start(bf16[32,2,128,128]{3,2,1,0:T(8,128)(2,1)} %all-gather.3.cloned.1.call-done.p_ref) | copy-start | bytes 6291460
  52.5 14.2 %collective-permute-start = (f32[64,16,128]{2,1,0:T(8,128)S(1)}, f32[64,16,128]{2,1,0:T(8,128)S(1)}, u32[]{:S(2)}, u32[]{:S(2)}) collective-permute-start(f32[64,16,128]{2,1,0:T(8,128)S(1)} %get-tuple-element.7), channel_id=1, source_target_pairs={{0,8},{1,9},{2,10},{3,11},{4,12},{5,13},{6,14},{7,15}} | collective-permute-start | bytes 1572872 | tf_op jit(solution)/shard_map/ppermute | solution.py:102
  55.7 15.2 %collective-permute-start.3 = (f32[64,16,128]{2,1,0:T(8,128)}, f32[64,16,128]{2,1,0:T(8,128)}, u32[]{:S(2)}, u32[]{:S(2)}) collective-permute-start(f32[64,16,128]{2,1,0:T(8,128)} %get-tuple-element.8), channel_id=1, source_target_pairs={{24,16},{25,17},{26,18},{27,19},{28,20},{29,21},{30,22},{31,23}} | collective-permute-start | bytes 1572872 | tf_op jit(solution)/shard_map/ppermute | solution.py:103
  66.8 14.2 %collective-permute-start.1 = (f32[64,16,128]{2,1,0:T(8,128)S(1)}, f32[64,16,128]{2,1,0:T(8,128)S(1)}, u32[]{:S(2)}, u32[]{:S(2)}) collective-permute-start(f32[64,16,128]{2,1,0:T(8,128)S(1)} %bitcast_add_fusion.2), channel_id=1, source_target_pairs={{0,8},{8,16},{1,9},{9,17},{2,10},{10,18},{3,11},{11,19},{4,12},{12... | collective-permute-start | bytes 1572872 | tf_op jit(solution)/shard_map/ppermute | solution.py:102
  83.2 5.4 %collective-permute-start.4 = (f32[64,16,128]{2,1,0:T(8,128)}, f32[64,16,128]{2,1,0:T(8,128)S(1)}, u32[]{:S(2)}, u32[]{:S(2)}) collective-permute-start(f32[64,16,128]{2,1,0:T(8,128)} %get-tuple-element.6), channel_id=1, source_target_pairs={{24,16},{16,8},{25,17},{17,9},{26,18},{18,10},{27,19},{19,11},{28,... | collective-permute-start | bytes 1572872 | tf_op jit(solution)/shard_map/ppermute | solution.py:103
  83.8 14.2 %collective-permute-start.2 = (f32[64,16,128]{2,1,0:T(8,128)}, f32[64,16,128]{2,1,0:T(8,128)S(1)}, u32[]{:S(2)}, u32[]{:S(2)}) collective-permute-start(f32[64,16,128]{2,1,0:T(8,128)} %get-tuple-element.5), channel_id=1, source_target_pairs={{0,8},{8,16},{16,24},{1,9},{9,17},{17,25},{2,10},{10,18},{18,26},{... | collective-permute-start | bytes 1572872 | tf_op jit(solution)/shard_map/ppermute | solution.py:102
  89.5 21.7 %collective-permute-start.5 = (f32[64,16,128]{2,1,0:T(8,128)}, f32[64,16,128]{2,1,0:T(8,128)S(1)}, u32[]{:S(2)}, u32[]{:S(2)}) collective-permute-start(f32[64,16,128]{2,1,0:T(8,128)} %bitcast_add_fusion.1), channel_id=1, source_target_pairs={{24,16},{16,8},{8,0},{25,17},{17,9},{9,1},{26,18},{18,10},{10,2},{... | collective-permute-start | bytes 1572872 | tf_op jit(solution)/shard_map/ppermute | solution.py:103
Sparse Core Ops, SparseCore 0:
  9.2 34.8 all-gather.2

commit v2 on v1

--- a/solution.py
+++ b/solution.py
@@ -8,17 +8,17 @@
 from jax.sharding import Mesh
 from jax.sharding import PartitionSpec as P
 
-SEATS = 8
+SEATS = 16
 
 
 def slice_kernel(q_ref, out_ref):
     blocks, per_block, extent, _ = q_ref.shape
     strip = extent // SEATS
     for f in range(blocks):
-        for k in range(per_block):
-            flipped = q_ref[f, k].T
-            for j in range(SEATS):
-                out_ref[j, f, k] = flipped[j * strip:(j + 1) * strip]
+        flipped = [q_ref[f, k].astype(jnp.float32).T for k in range(per_block)]
+        for j in range(SEATS):
+            pieces = [tile[j * strip:(j + 1) * strip] for tile in flipped]
+            out_ref[j, f] = jnp.concatenate(pieces, axis=0).astype(out_ref.dtype)
 
 
 def product_kernel(tile_count, p_ids, q_ids, q_ref, p_ref, acc_ref):
@@ -38,7 +38,7 @@
                 acc_ref[spot] += product[l * strip:(l + 1) * strip]
         return carry
 
-    lax.fori_loop(0, blocks, one_block, 0)
+    lax.fori_loop(0, blocks, one_block, 0, unroll=2)
 
 
 def finish_kernel(x_ref, out_ref):
@@ -59,7 +59,7 @@
 
     sliced = pl.pallas_call(
         slice_kernel,
-        out_shape=jax.ShapeDtypeStruct((SEATS, blocks, per_q, strip, extent), q_tiles.dtype),
+        out_shape=jax.ShapeDtypeStruct((SEATS, blocks, per_q * strip, extent), q_tiles.dtype),
         name="cut_columns",
     )(q_tiles)
     q_here = lax.all_to_all(sliced, seat, split_axis=0, concat_axis=0, tiled=True)
@@ -89,23 +89,12 @@
     parts = acc.reshape(planes, side * tile_count, strip, extent)
     here = lax.axis_index("plane")
 
-    def pick(place):
-        place = jnp.clip(place, 0, planes - 1)
-        return lax.dynamic_index_in_dim(parts, place, 0, keepdims=False)
-
-    up = down = None
-    for step in range(planes - 1):
-        send_up = pick(planes - 1 - step + here)
-        send_down = pick(here - (planes - 1 - step))
-        if step:
-            send_up, send_down = send_up + up, send_down + down
-        up = lax.ppermute(send_up, "plane", [(z, z + 1) for z in range(step + 1)])
-        down = lax.ppermute(
-            send_down, "plane", [(planes - 1 - z, planes - 2 - z) for z in range(step + 1)]
-        )
-    summed = pick(here)
-    if planes > 1:
-        summed = summed + up + down
+    if planes == 2:
+        away = lax.dynamic_index_in_dim(parts, 1 - here, 0, keepdims=False)
+        kept = lax.dynamic_index_in_dim(parts, here, 0, keepdims=False)
+        summed = kept + lax.ppermute(away, "plane", [(0, 1), (1, 0)])
+    else:
+        summed = lax.psum_scatter(parts, "plane", scatter_dimension=0, tiled=False)
 
     mine = summed.reshape(SEATS, tile_count // cols, strip, extent)
     landed = lax.all_to_all(mine, seat, split_axis=0, concat_axis=0, tiled=True)

time: 136 us -> 124 us (0.912)
  starting transfers between devices: 20.6 us -> 8.7 us
  blocking collectives: 40.3 us -> 46.7 us
  waiting for transfers between devices: 44.7 us -> 38.4 us
  other arithmetic: 3.25 us -> 0.82 us
  Pallas kernels: 10.2 us -> 12 us
    ppermute x6 -> x1, waiting for transfers between devices: 40.1 us -> 23.5 us  [body(): summed = kept + lax.ppermute(away, 'plane', [(0, 1), (1, 0)])]
    ppermute x6 -> x1, starting transfers between devices: 15.4 us -> 2.44 us  [body(): summed = kept + lax.ppermute(away, 'plane', [(0, 1), (1, 0)])]
    all_gather x1, waiting for transfers between devices: 3.93 us -> 14.2 us  [body(): p_here = lax.all_gather(p_tiles, seat, axis=0, tiled=True)]
    all_gather x1, blocking collectives: 25 us -> 33.5 us  [body(): ids = lax.all_gather(ids, seat, axis=0, tiled=True)]
    add x4 -> x1, other arithmetic: 3.17 us -> 0.07 us  [body(): summed = kept + lax.ppermute(away, 'plane', [(0, 1), (1, 0)])]
    all_to_all x1, blocking collectives: 15.3 us -> 13.3 us  [body(): landed = lax.all_to_all(mine, seat, split_axis=0, concat_axis=0, tiled=True)]
    pallas_call x1, Pallas kernels: 5.91 us -> 7.66 us  [body(): pl.pallas_call(functools.partial(product_kernel, tile_count), out_shape=j...]
    unnamed x7 -> x3, local copies, waits for them, and re-layouts: 1.69 us -> 2.95 us
  transfers between devices with their start and end apart: 8 -> 3, of which waited for: 5 -> 2; matrix products, arithmetic and copies ran while one was open for 1% -> 2% of each run, Pallas kernels for 2% -> 2%
where the time goes in v2:
time: 124 us; the launch traced here: 123 us
  blocking collectives  46.7 us (38%)
  waiting for transfers between devices  38.4 us (31%)
  between operations  13.4 us (11%)
  Pallas kernels  12 us (10%)
  starting transfers between devices  8.7 us (7%)
  local copies, waits for them, and re-layouts  3.35 us (3%)
    all_gather x1, blocking collectives, body(): ids = lax.all_gather(ids, seat, axis=0, tiled=True)  33.5 us
    ppermute x1, waiting for transfers between devices, body(): summed = kept + lax.ppermute(away, 'plane', [(0, 1), (1, 0)])  23.5 us
    all_gather x1, waiting for transfers between devices, body(): p_here = lax.all_gather(p_tiles, seat, axis=0, tiled=True)  14.2 us
    all_to_all x1, blocking collectives, body(): landed = lax.all_to_all(mine, seat, split_axis=0, concat_axis=0, tiled=True)  13.3 us
    pallas_call x1, Pallas kernels, body(): pl.pallas_call(functools.partial(product_kernel, tile_count), out_shape=j...  7.66 us
    all_to_all x1, starting transfers between devices, body(): lax.all_to_all(sliced, seat, split_axis=0, concat_axis=0, tiled=True)  6.25 us
    unnamed x3, local copies, waits for them, and re-layouts  2.95 us
  transfers between devices with their start and end apart: 3, of which 2 were waited for; matrix products, arithmetic and copies ran while one was open for 2% of the time, Pallas kernels for 2%

profile of v2, /device:TPU:1, one launch (start us, length us, event | category | flops | bytes accessed | tf_op | source)
XLA Modules:
  0.0 123.4 jit_solution(10214643410841091058)
XLA Ops:
  6.5 0.0 all-gather.3.cloned.1.call-start
  6.5 0.7 all-gather.3.cloned.1.call-update
  7.3 2.3 %cut_columns.1 = bf16[16,4,48,128]{3,2,1,0:T(8,128)(2,1)} custom-call(bf16[4,6,128,128]{3,2,1,0:T(8,128)(2,1)} %q_ref.1), custom_call_target="tpu_custom_call" | custom-call | tf_op jit(solution)/shard_map/cut_columns/pallas_call | solution.py:60
  9.5 6.3 %all-to-all-start = ((bf16[16,4,48,128]{3,2,1,0:T(8,128)(2,1)}), bf16[16,4,48,128]{3,2,1,0:T(8,128)(2,1)S(1)}, u32[]{:S(2)}, u32[]{:S(2)}) async-start(bf16[16,4,48,128]{3,2,1,0:T(8,128)(2,1)} %cut_columns.1), calls=%async_computation | async-start | bytes 1572864 | tf_op jit(solution)/shard_map/all_to_all | solution.py:65
  15.8 0.8 copy.7
  16.6 0.8 add_bitcast_fusion
  17.3 33.5 %all-gather = s32[16,4,8]{2,1,0:T(4,128)S(1)} all-gather(s32[1,4,8]{2,1,0:T(4,128)S(1)} %add_bitcast_fusion), channel_id=1, replica_groups=mesh['plane'=2,'side'=8,'col'=2] {'side','col'}, dimensions={0}, use_global_device_ids=true | all-gather | bytes 2176 | tf_op jit(solution)/shard_map/all_gather | solution.py:68
  50.8 0.1 slice.9
  50.9 0.1 reshape.15.p_ids
  51.0 0.1 reshape.16.q_ids
  51.1 0.0 all-to-all-done
  51.2 14.2 %all-gather.3.cloned.1.call-done.p_ref = bf16[64,2,128,128]{3,2,1,0:T(8,128)(2,1)} async-done(((bf16[4,2,128,128]{3,2,1,0:T(8,128)(2,1)}), bf16[64,2,128,128]{3,2,1,0:T(8,128)(2,1)}) %all-gather.3.cloned.1.call-update) | async-done | bytes 4194320 | tf_op jit(solution)/shard_map/all_gather | solution.py:66
  65.4 0.0 copy-start
  65.4 2.2 %copy-done = bf16[64,2,128,128]{3,2,1,0:T(8,128)(2,1)S(1)} copy-done((bf16[64,2,128,128]{3,2,1,0:T(8,128)(2,1)S(1)}, bf16[64,2,128,128]{3,2,1,0:T(8,128)(2,1)}, u32[]{:S(2)}) %copy-start) | copy-done | bytes 4194328
  67.6 7.7 %products.1 = f32[256,8,128]{2,1,0:T(8,128)S(1)} custom-call(s32[128]{0:T(128)S(1)} %reshape.15.p_ids, s32[384]{0:T(512)S(1)} %reshape.16.q_ids, bf16[64,48,128]{2,1,0:T(8,128)(2,1)S(1)} %bitcast.13, bf16[64,2,128,128]{3,2,1,0:T(8,128)(2,1)S(1)} %copy-done), custom_call_target="tpu_custom_call" | custom-call | tf_op jit(solution)/shard_map/products/pallas_call | solution.py:71
  75.3 2.4 %collective-permute-start = (f32[128,8,128]{2,1,0:T(8,128)S(1)}, f32[128,8,128]{2,1,0:T(8,128)S(1)}, u32[]{:S(2)}, u32[]{:S(2)}) collective-permute-start(f32[128,8,128]{2,1,0:T(8,128)S(1)} %dynamic-slice_bitcast_fusion), channel_id=1, source_target_pairs={{0,16},{16,0},{1,17},{17,1},{2,18},{18,2},{3,19},{19,3},{4,20},{20... | collective-permute-start | bytes 1572872 | tf_op jit(solution)/shard_map/ppermute | solution.py:95
  77.7 23.5 %collective-permute-done = f32[128,8,128]{2,1,0:T(8,128)S(1)} collective-permute-done((f32[128,8,128]{2,1,0:T(8,128)S(1)}, f32[128,8,128]{2,1,0:T(8,128)S(1)}, u32[]{:S(2)}, u32[]{:S(2)}) %collective-permute-start) | collective-permute-done | bytes 524320 | tf_op jit(solution)/shard_map/ppermute | solution.py:95
  101.2 0.1 bitcast_add_fusion
  101.3 13.3 %all_to_all.10.x_ref = f32[16,8,8,128]{3,2,1,0:T(8,128)} all-to-all(f32[16,8,8,128]{3,2,1,0:T(8,128)S(1)} %bitcast.14), channel_id=1, replica_groups=mesh['plane'=2,'side'=8,'col'=2] {'side','col'}, dimensions={0} | all-to-all | bytes 1048576 | tf_op jit(solution)/shard_map/all_to_all | solution.py:100
  114.6 2.0 %turn.1 = f32[128,1024]{1,0:T(8,128)} custom-call(f32[16,8,8,128]{3,2,1,0:T(8,128)} %all_to_all.10.x_ref), custom_call_target="tpu_custom_call" | custom-call | tf_op jit(solution)/shard_map/turn/pallas_call | solution.py:101
  (1 shorter events, 0.0 us)
Async XLA Ops:
  6.5 58.8 %all-gather.3.cloned.1.call-start = ((), (), s32[]{:S(2)}) async-start(), calls=%async_computation.2 | async-start | bytes 4456448 | tf_op jit(solution)/shard_map/all_gather | solution.py:66
  9.5 41.6 %all-to-all-start = ((bf16[16,4,48,128]{3,2,1,0:T(8,128)(2,1)}), bf16[16,4,48,128]{3,2,1,0:T(8,128)(2,1)S(1)}, u32[]{:S(2)}, u32[]{:S(2)}) async-start(bf16[16,4,48,128]{3,2,1,0:T(8,128)(2,1)} %cut_columns.1), calls=%async_computation | async-start | bytes 1572864 | tf_op jit(solution)/shard_map/all_to_all | solution.py:65
  65.4 2.2 %copy-start = (bf16[64,2,128,128]{3,2,1,0:T(8,128)(2,1)S(1)}, bf16[64,2,128,128]{3,2,1,0:T(8,128)(2,1)}, u32[]{:S(2)}) copy-start(bf16[64,2,128,128]{3,2,1,0:T(8,128)(2,1)} %all-gather.3.cloned.1.call-done.p_ref) | copy-start | bytes 12582916
  75.3 25.9 %collective-permute-start = (f32[128,8,128]{2,1,0:T(8,128)S(1)}, f32[128,8,128]{2,1,0:T(8,128)S(1)}, u32[]{:S(2)}, u32[]{:S(2)}) collective-permute-start(f32[128,8,128]{2,1,0:T(8,128)S(1)} %dynamic-slice_bitcast_fusion), channel_id=1, source_target_pairs={{0,16},{16,0},{1,17},{17,1},{2,18},{18,2},{3,19},{19,3},{4,20},{20... | collective-permute-start | bytes 1572872 | tf_op jit(solution)/shard_map/ppermute | solution.py:95
Sparse Core Ops, SparseCore 0:
  8.9 56.4 all-gather.2

commit v3 on v2

v3 whole, which is shorter than its diff:
```python
import functools

import jax
import jax.numpy as jnp
from jax import lax
from jax.experimental import pallas as pl
from jax.experimental.pallas import tpu as pltpu
from jax.sharding import Mesh
from jax.sharding import PartitionSpec as P

SEATS = 16
SUB = 8


def offsets():
    pairs, cores, cols = (lax.axis_size(name) for name in ("pair", "core", "col"))
    far_first = [(a, b) for a in reversed(range(pairs)) for b in reversed(range(cols))]
    return [(a, b, c) for a, b in far_first for c in range(cores)]


def origin(a, b, c):
    pairs, cores, cols = (lax.axis_size(name) for name in ("pair", "core", "col"))
    pair = lax.rem(lax.axis_index("pair") + (pairs - a), pairs)
    core = lax.rem(lax.axis_index("core") + (cores - c), cores)
    return (pair * cores + core) * cols + lax.rem(lax.axis_index("col") + (cols - b), cols)


def slice_kernel(p_ids, q_ids, q_ref, out_ref):
    blocks, per_q, extent, _ = q_ref.shape
    per_p = p_ids.shape[1]
    strip = extent // SEATS
    rows = per_q * strip
    lane = lax.broadcasted_iota(jnp.int32, (2 * SUB, extent), 1)
    ids = jnp.zeros((2 * SUB, extent), jnp.int32)
    for f in range(blocks):
        for k in range(per_p + per_q):
            value = p_ids[f, k] if k < per_p else q_ids[f, k - per_p]
            ids = jnp.where(lane == f * (per_p + per_q) + k, value, ids)
    ids = ids.astype(out_ref.dtype)
    for f in range(blocks):
        flipped = [q_ref[f, k].astype(jnp.float32).T for k in range(per_q)]
        for j in range(SEATS):
            pieces = [tile[j * strip:(j + 1) * strip] for tile in flipped]
            out_ref[j, f * rows:(f + 1) * rows] = jnp.concatenate(pieces, axis=0).astype(out_ref.dtype)
    for j in range(SEATS):
        out_ref[j, blocks * rows:] = ids


def product_kernel(tile_count, q_ref, *rest):
    p_refs, (acc_ref, wide_ids, ids, id_sem) = rest[:SEATS], rest[SEATS:]
    blocks, per_p, extent, _ = p_refs[0].shape
    strip = acc_ref.shape[1]
    rows = (q_ref.shape[1] - 2 * SUB) // blocks
    per_q = rows // strip
    for s in range(SEATS):
        wide_ids[s:s + 1] = q_ref[s, blocks * rows:, :].astype(jnp.int32)[:1]
    id_copy = pltpu.make_async_copy(wide_ids, ids, id_sem)
    id_copy.start()
    acc_ref[...] = jnp.zeros_like(acc_ref)
    id_copy.wait()
    for (a, b, c), p_ref in zip(offsets(), p_refs):
        seat = origin(a, b, c)
        for f in range(blocks):
            left = q_ref[seat, f * rows:(f + 1) * rows]
            first = f * (per_p + per_q)
            for k in range(per_p):
                product = jnp.dot(left, p_ref[f, k], preferred_element_type=jnp.float32)
                base = ids[seat, first + k] * tile_count
                for l in range(per_q):
                    spot = base + ids[seat, first + per_p + l]
                    acc_ref[spot] += product[l * strip:(l + 1) * strip]


def finish_kernel(x_ref, out_ref):
    seats, tiles, strip, extent = x_ref.shape
    for t in range(tiles):
        stacked = x_ref[:, t].reshape(seats * strip, extent)
        out_ref[:, t * extent:(t + 1) * extent] = stacked.T


def body(p_tiles, p_cols, q_tiles, q_cols):
    blocks, per_p, extent, _ = p_tiles.shape
    per_q = q_tiles.shape[1]
    planes = lax.axis_size("plane")
    pairs, cores, cols = lax.axis_size("pair"), lax.axis_size("core"), lax.axis_size("col")
    tile_count = planes * pairs * cores
    strip = extent // SEATS
    height = blocks * per_q * strip + 2 * SUB
    seat = ("pair", "core", "col")

    sliced = pl.pallas_call(
        slice_kernel,
        out_shape=jax.ShapeDtypeStruct((SEATS, height, extent), q_tiles.dtype),
        in_specs=[pl.BlockSpec(memory_space=pltpu.SMEM)] * 2 + [pl.BlockSpec(memory_space=pltpu.VMEM)],
        name="cut_columns",
    )(p_cols, q_cols, q_tiles)
    p_tiles, sliced = lax.optimization_barrier((p_tiles, sliced))
    q_here = lax.all_to_all(sliced, seat, split_axis=0, concat_axis=0, tiled=True)

    near = {}
    for a, b, c in offsets():
        if c == 0:
            moved = p_tiles
            if a or b:
                hops = []
                for i in range(pairs):
                    for j in range(cols):
                        hops.append((i * cols + j, (i + a) % pairs * cols + (j + b) % cols))
                moved = lax.ppermute(p_tiles, ("pair", "col"), hops)
        else:
            hops = [(i, (i + c) % cores) for i in range(cores)]
            moved = lax.ppermute(near[a, b, 0], "core", hops)
        near[a, b, c] = moved

    acc = pl.pallas_call(
        functools.partial(product_kernel, tile_count),
        out_shape=jax.ShapeDtypeStruct((tile_count * tile_count, strip, extent), jnp.float32),
        scratch_shapes=[
            pltpu.VMEM((SEATS, extent), jnp.int32),
            pltpu.SMEM((SEATS, extent), jnp.int32),
            pltpu.SemaphoreType.DMA,
        ],
        compiler_params=pltpu.CompilerParams(vmem_limit_bytes=24 << 20),
        name="products",
    )(q_here, *near.values())

    parts = acc.reshape(planes, pairs * cores * tile_count, strip, extent)
    here = lax.axis_index("plane")

    if planes == 2:
        away = lax.dynamic_index_in_dim(parts, 1 - here, 0, keepdims=False)
        kept = lax.dynamic_index_in_dim(parts, here, 0, keepdims=False)
        summed = kept + lax.ppermute(away, "plane", [(0, 1), (1, 0)])
    else:
        summed = lax.psum_scatter(parts, "plane", scatter_dimension=0, tiled=False)

    mine = summed.reshape(SEATS, tile_count // cols, strip, extent)
    landed = lax.all_to_all(mine, seat, split_axis=0, concat_axis=0, tiled=True)
    return pl.pallas_call(
        finish_kernel,
        out_shape=jax.ShapeDtypeStruct((extent, tile_count // cols * extent), jnp.float32),
        name="turn",
    )(landed)


def solution(mesh):
    rows, cols = mesh.devices.shape
    pairs = SEATS // (2 * cols)
    shape = (rows // (2 * pairs), pairs, 2, cols)
    every = ("plane", "pair", "core", "col")
    inner = Mesh(mesh.devices.reshape(shape), every)
    placed = (
        P(every, None, None, None),
        P(every, None),
        P(every, None, None, None),
        P(every, None),
    )
    return jax.shard_map(
        body, mesh=inner, in_specs=placed, out_specs=P(every[:3], "col"), check_vma=False
    )
```

time: 124 us -> 110 us (0.89)
  blocking collectives: 46.7 us -> 13.4 us
  starting transfers between devices: 8.7 us -> 25.5 us
  between operations: 13.4 us -> 0.07 us
  local copies, waits for them, and re-layouts: 3.35 us -> 12.9 us
  waiting for transfers between devices: 38.4 us -> 46.7 us
  Pallas kernels: 12 us -> 10.5 us
    all_gather x1 -> x0, blocking collectives: 33.5 us -> none  [body(): ids = lax.all_gather(ids, seat, axis=0, tiled=True)]
    ppermute x0 -> x15, waiting for transfers between devices: none -> 23.2 us  [the longest x7 23.2 us: body(): moved = lax.ppermute(p_tiles, ('pair', 'col'), hops)]
    ppermute x0 -> x15, starting transfers between devices: none -> 16.7 us  [the longest x7 11.3 us: body(): moved = lax.ppermute(p_tiles, ('pair', 'col'), hops)]
    all_gather x1 -> x0, waiting for transfers between devices: 14.2 us -> none  [body(): p_here = lax.all_gather(p_tiles, seat, axis=0, tiled=True)]
    unnamed x3 -> x31, local copies, waits for them, and re-layouts: 2.95 us -> 12.9 us
    pallas_call x1, Pallas kernels: 7.66 us -> 6.13 us  [body(): pl.pallas_call(functools.partial(product_kernel, tile_count), out_shape=j...]
  transfers between devices with their start and end apart: 3 -> 17, of which waited for: 2 -> 6; matrix products, arithmetic and copies ran while one was open for 2% -> 0% of each run, Pallas kernels for 2% -> 0%
where the time goes in v3:
time: 110 us; the launch traced here: 109 us
  waiting for transfers between devices  46.7 us (42%)
  starting transfers between devices  25.5 us (23%)
  blocking collectives  13.4 us (12%)
  local copies, waits for them, and re-layouts  12.9 us (12%)
  Pallas kernels  10.5 us (10%)
    ppermute x1, waiting for transfers between devices, body(): summed = kept + lax.ppermute(away, 'plane', [(0, 1), (1, 0)])  23.5 us
    ppermute x7, waiting for transfers between devices, body(): moved = lax.ppermute(p_tiles, ('pair', 'col'), hops)  23.2 us
    all_to_all x1, blocking collectives, body(): landed = lax.all_to_all(mine, seat, split_axis=0, concat_axis=0, tiled=True)  13.4 us
    unnamed x31, local copies, waits for them, and re-layouts  12.9 us
    ppermute x7, starting transfers between devices, body(): moved = lax.ppermute(p_tiles, ('pair', 'col'), hops)  11.3 us
    all_to_all x1, starting transfers between devices, body(): lax.all_to_all(sliced, seat, split_axis=0, concat_axis=0, tiled=True)  6.38 us
    pallas_call x1, Pallas kernels, body(): pl.pallas_call(functools.partial(product_kernel, tile_count), out_shape=j...  6.13 us
    ppermute x8, starting transfers between devices, body(): moved = lax.ppermute(near[a, b, 0], 'core', hops)  5.41 us
  transfers between devices with their start and end apart: 17, of which 6 were waited for; matrix products, arithmetic and copies ran while one was open for 0% of the time, Pallas kernels for 0%

profile of v3, /device:TPU:1, one launch (start us, length us, event | category | flops | bytes accessed | tf_op | source)
XLA Modules:
  0.0 109.1 jit_solution(9764728261804669377)
XLA Ops:
  0.0 1.3 %copy.5.p_ids = s32[4,2]{1,0:T(4,128)} copy(s32[4,2]{0,1:T(2,128)} %param.5) | data formatting | bytes 64 | tf_op args[1]
  1.3 2.3 %cut_columns.1 = bf16[16,208,128]{2,1,0:T(8,128)(2,1)} custom-call(s32[4,2]{1,0:T(4,128)} %copy.5.p_ids, s32[4,6]{1,0:T(4,128)} %q_ids.1, bf16[4,6,128,128]{3,2,1,0:T(8,128)(2,1)} %q_ref.1), custom_call_target="tpu_custom_call" | custom-call | tf_op jit(solution)/shard_map/cut_columns/pallas_call | solution.py:91
  3.7 0.0 copy-start
  3.7 6.4 %all-to-all-start = ((bf16[16,208,128]{2,1,0:T(8,128)(2,1)}), bf16[16,208,128]{2,1,0:T(8,128)(2,1)S(1)}, u32[]{:S(2)}, u32[]{:S(2)}) async-start(bf16[16,208,128]{2,1,0:T(8,128)(2,1)} %cut_columns.1), calls=%async_computation | async-start | bytes 1703936 | tf_op jit(solution)/shard_map/all_to_all | solution.py:98
  10.1 0.0 copy-done
  10.1 3.2 %collective-permute-start = (bf16[4,2,128,128]{3,2,1,0:T(8,128)(2,1)S(1)}, bf16[4,2,128,128]{3,2,1,0:T(8,128)(2,1)S(1)}, u32[]{:S(2)}, u32[]{:S(2)}) collective-permute-start(bf16[4,2,128,128]{3,2,1,0:T(8,128)(2,1)S(1)} %copy-done), channel_id=1, source_target_pairs={{0,13},{1,12},{4,1},{5,0},{8,5},{9,4},{12,9},{13,8},{2,15},{3,14},... | collective-permute-start | bytes 786440 | tf_op jit(solution)/shard_map/ppermute | solution.py:109
  13.3 0.0 collective-permute-start.10
  13.3 0.3 collective-permute-start.12
  13.6 2.4 %collective-permute-start.2 = (bf16[4,2,128,128]{3,2,1,0:T(8,128)(2,1)S(1)}, bf16[4,2,128,128]{3,2,1,0:T(8,128)(2,1)S(1)}, u32[]{:S(2)}, u32[]{:S(2)}) collective-permute-start(bf16[4,2,128,128]{3,2,1,0:T(8,128)(2,1)S(1)} %copy-done), channel_id=1, source_target_pairs={{0,12},{1,13},{4,0},{5,1},{8,4},{9,5},{12,8},{13,9},{2,14},{3,15},... | collective-permute-start | bytes 786440 | tf_op jit(solution)/shard_map/ppermute | solution.py:109
  16.0 1.2 %collective-permute-start.4 = (bf16[4,2,128,128]{3,2,1,0:T(8,128)(2,1)S(1)}, bf16[4,2,128,128]{3,2,1,0:T(8,128)(2,1)S(1)}, u32[]{:S(2)}, u32[]{:S(2)}) collective-permute-start(bf16[4,2,128,128]{3,2,1,0:T(8,128)(2,1)S(1)} %copy-done), channel_id=1, source_target_pairs={{0,9},{1,8},{4,13},{5,12},{8,1},{9,0},{12,5},{13,4},{2,11},{3,10},... | collective-permute-start | bytes 786440 | tf_op jit(solution)/shard_map/ppermute | solution.py:109
  17.1 17.8 %collective-permute-done.rest_0_ = bf16[4,2,128,128]{3,2,1,0:T(8,128)(2,1)S(1)} collective-permute-done((bf16[4,2,128,128]{3,2,1,0:T(8,128)(2,1)S(1)}, bf16[4,2,128,128]{3,2,1,0:T(8,128)(2,1)S(1)}, u32[]{:S(2)}, u32[]{:S(2)}) %collective-permute-start) | collective-permute-done | bytes 262176 | tf_op jit(solution)/shard_map/ppermute | solution.py:109
  35.0 1.2 %collective-permute-start.6 = (bf16[4,2,128,128]{3,2,1,0:T(8,128)(2,1)S(1)}, bf16[4,2,128,128]{3,2,1,0:T(8,128)(2,1)S(1)}, u32[]{:S(2)}, u32[]{:S(2)}) collective-permute-start(bf16[4,2,128,128]{3,2,1,0:T(8,128)(2,1)S(1)} %copy-done), channel_id=1, source_target_pairs={{0,8},{1,9},{4,12},{5,13},{8,0},{9,1},{12,4},{13,5},{2,10},{3,11},... | collective-permute-start | bytes 786440 | tf_op jit(solution)/shard_map/ppermute | solution.py:109
  36.2 0.4 collective-permute-done.10.rest_10_
  36.6 3.0 %collective-permute-start.8 = (bf16[4,2,128,128]{3,2,1,0:T(8,128)(2,1)S(1)}, bf16[4,2,128,128]{3,2,1,0:T(8,128)(2,1)S(1)}, u32[]{:S(2)}, u32[]{:S(2)}) collective-permute-start(bf16[4,2,128,128]{3,2,1,0:T(8,128)(2,1)S(1)} %copy-done), channel_id=1, source_target_pairs={{0,5},{1,4},{4,9},{5,8},{8,13},{9,12},{12,1},{13,0},{2,7},{3,6},{6... | collective-permute-start | bytes 786440 | tf_op jit(solution)/shard_map/ppermute | solution.py:109
  39.6 0.0 collective-permute-done.12.rest_12_
  39.6 1.2 %collective-permute-start.14 = (bf16[4,2,128,128]{3,2,1,0:T(8,128)(2,1)S(1)}, bf16[4,2,128,128]{3,2,1,0:T(8,128)(2,1)S(1)}, u32[]{:S(2)}, u32[]{:S(2)}) collective-permute-start(bf16[4,2,128,128]{3,2,1,0:T(8,128)(2,1)S(1)} %copy-done), channel_id=1, source_target_pairs={{0,2},{2,0},{1,3},{3,1},{4,6},{6,4},{5,7},{7,5},{8,10},{10,8},{9,1... | collective-permute-start | bytes 786440 | tf_op jit(solution)/shard_map/ppermute | solution.py:112
  40.7 0.0 collective-permute-done.2.rest_2_
  40.7 0.1 collective-permute-start.1
  40.8 0.3 collective-permute-done.4.rest_4_
  41.1 1.3 %collective-permute-start.11 = (bf16[4,2,128,128]{3,2,1,0:T(8,128)(2,1)S(1)}, bf16[4,2,128,128]{3,2,1,0:T(8,128)(2,1)S(1)}, u32[]{:S(2)}, u32[]{:S(2)}) collective-permute-start(bf16[4,2,128,128]{3,2,1,0:T(8,128)(2,1)S(1)} %collective-permute-done.10.rest_10_), channel_id=1, source_target_pairs={{0,2},{2,0},{1,3},{3,1},{4,6},{6,4},{5,7},{7,5},{8,10},{10,8},{9,1... | collective-permute-start | bytes 786440 | tf_op jit(solution)/shard_map/ppermute | solution.py:112
  42.4 3.4 %collective-permute-done.6.rest_6_ = bf16[4,2,128,128]{3,2,1,0:T(8,128)(2,1)S(1)} collective-permute-done((bf16[4,2,128,128]{3,2,1,0:T(8,128)(2,1)S(1)}, bf16[4,2,128,128]{3,2,1,0:T(8,128)(2,1)S(1)}, u32[]{:S(2)}, u32[]{:S(2)}) %collective-permute-start.6) | collective-permute-done | bytes 262176 | tf_op jit(solution)/shard_map/ppermute | solution.py:109
  45.8 0.9 collective-permute-start.13
  46.7 1.3 %collective-permute-done.8.rest_8_ = bf16[4,2,128,128]{3,2,1,0:T(8,128)(2,1)S(1)} collective-permute-done((bf16[4,2,128,128]{3,2,1,0:T(8,128)(2,1)S(1)}, bf16[4,2,128,128]{3,2,1,0:T(8,128)(2,1)S(1)}, u32[]{:S(2)}, u32[]{:S(2)}) %collective-permute-start.8) | collective-permute-done | bytes 262176 | tf_op jit(solution)/shard_map/ppermute | solution.py:109
  48.0 1.5 %collective-permute-start.3 = (bf16[4,2,128,128]{3,2,1,0:T(8,128)(2,1)S(1)}, bf16[4,2,128,128]{3,2,1,0:T(8,128)(2,1)}, u32[]{:S(2)}, u32[]{:S(2)}) collective-permute-start(bf16[4,2,128,128]{3,2,1,0:T(8,128)(2,1)S(1)} %collective-permute-done.2.rest_2_), channel_id=1, source_target_pairs={{0,2},{2,0},{1,3},{3,1},{4,6},{6,4},{5,7},{7,5},{8,10},{10,8},{9,1... | collective-permute-start | bytes 786440 | tf_op jit(solution)/shard_map/ppermute | solution.py:112
  49.4 0.0 collective-permute-done.14.rest_15_
  49.4 0.0 copy-start.5
  49.4 0.7 copy-done.5
  50.1 0.0 collective-permute-start.5
  50.1 0.0 collective-permute-done.1.rest_1_
  50.2 0.0 copy-start.7
  50.2 0.7 copy-done.7
  50.9 0.5 collective-permute-start.7
  51.4 0.0 copy-start.1
  51.4 0.7 copy-done.1
  52.1 0.0 collective-permute-done.11.rest_11_
  52.1 0.0 copy-start.9
  52.1 0.7 copy-done.9
  52.8 0.0 collective-permute-start.9
  52.8 0.0 copy-start.3
  52.8 0.7 copy-done.3
  53.5 0.0 collective-permute-done.13.rest_13_
  53.5 0.0 collective-permute-done.3.rest_3_
  53.5 0.0 collective-permute-done.5.rest_5_
  53.5 0.0 copy-start.11
  53.5 0.7 copy-done.11
  54.2 0.0 collective-permute-done.7.rest_7_
  54.2 0.0 copy-start.13
  54.2 0.7 copy-done.13
  54.9 0.0 collective-permute-done.9.rest_9_
  54.9 0.0 all-to-all-done.q_ref
  54.9 0.0 copy-start.2
  54.9 0.9 copy-done.2
  55.9 0.9 copy-done.4
  56.8 0.9 copy-done.6
  57.8 0.9 copy-done.8
  58.7 0.9 copy-done.10
  59.7 0.9 copy-done.12
  60.6 0.9 copy-done.14
  61.6 6.1 %products.1 = f32[256,8,128]{2,1,0:T(8,128)S(1)} custom-call(bf16[16,208,128]{2,1,0:T(8,128)(2,1)S(1)} %all-to-all-done.q_ref, bf16[4,2,128,128]{3,2,1,0:T(8,128)(2,1)S(1)} %collective-permute-done.rest_0_, bf16[4,2,128,128]{3,2,1,0:T(8,128)(2,1)S(1)} %copy-done.8, bf16[4,2,128,128]{3,2,1,0:T(8,128)(2,1)S(1)} %collective-permute-done.2.rest_2_, ...), custom_call_target="tpu_custom_call" | custom-call | tf_op jit(solution)/shard_map/products/pallas_call | solution.py:115
  67.8 2.4 %collective-permute-start.15 = (f32[128,8,128]{2,1,0:T(8,128)S(1)}, f32[128,8,128]{2,1,0:T(8,128)S(1)}, u32[]{:S(2)}, u32[]{:S(2)}) collective-permute-start(f32[128,8,128]{2,1,0:T(8,128)S(1)} %dynamic-slice_bitcast_fusion), channel_id=1, source_target_pairs={{0,16},{16,0},{1,17},{17,1},{2,18},{18,2},{3,19},{19,3},{4,20},{20... | collective-permute-start | bytes 1572872 | tf_op jit(solution)/shard_map/ppermute | solution.py:133
  70.1 23.5 %collective-permute-done.15 = f32[128,8,128]{2,1,0:T(8,128)S(1)} collective-permute-done((f32[128,8,128]{2,1,0:T(8,128)S(1)}, f32[128,8,128]{2,1,0:T(8,128)S(1)}, u32[]{:S(2)}, u32[]{:S(2)}) %collective-permute-start.15) | collective-permute-done | bytes 524320 | tf_op jit(solution)/shard_map/ppermute | solution.py:133
  93.6 0.1 bitcast_add_fusion
  93.7 13.4 %all_to_all.10.x_ref = f32[16,8,8,128]{3,2,1,0:T(8,128)} all-to-all(f32[16,8,8,128]{3,2,1,0:T(8,128)S(1)} %bitcast.8), channel_id=1, replica_groups=mesh['plane'=2,'pair'=4,'core'=2,'col'=2] {'pair','core','col'}, dimensions={0} | all-to-all | bytes 1048576 | tf_op jit(solution)/shard_map/all_to_all | solution.py:138
  107.0 2.0 %turn.1 = f32[128,1024]{1,0:T(8,128)} custom-call(f32[16,8,8,128]{3,2,1,0:T(8,128)} %all_to_all.10.x_ref), custom_call_target="tpu_custom_call" | custom-call | tf_op jit(solution)/shard_map/turn/pallas_call | solution.py:139
  (7 shorter events, 0.1 us)
Async XLA Ops:
  3.7 6.4 %copy-start = (bf16[4,2,128,128]{3,2,1,0:T(8,128)(2,1)S(1)}, bf16[4,2,128,128]{3,2,1,0:T(8,128)(2,1)}, u32[]{:S(2)}) copy-start(bf16[4,2,128,128]{3,2,1,0:T(8,128)(2,1)} %rest_14_) | copy-start | bytes 786436
  3.7 51.2 %all-to-all-start = ((bf16[16,208,128]{2,1,0:T(8,128)(2,1)}), bf16[16,208,128]{2,1,0:T(8,128)(2,1)S(1)}, u32[]{:S(2)}, u32[]{:S(2)}) async-start(bf16[16,208,128]{2,1,0:T(8,128)(2,1)} %cut_columns.1), calls=%async_computation | async-start | bytes 1703936 | tf_op jit(solution)/shard_map/all_to_all | solution.py:98
  10.1 24.9 %collective-permute-start = (bf16[4,2,128,128]{3,2,1,0:T(8,128)(2,1)S(1)}, bf16[4,2,128,128]{3,2,1,0:T(8,128)(2,1)S(1)}, u32[]{:S(2)}, u32[]{:S(2)}) collective-permute-start(bf16[4,2,128,128]{3,2,1,0:T(8,128)(2,1)S(1)} %copy-done), channel_id=1, source_target_pairs={{0,13},{1,12},{4,1},{5,0},{8,5},{9,4},{12,9},{13,8},{2,15},{3,14},... | collective-permute-start | bytes 786440 | tf_op jit(solution)/shard_map/ppermute | solution.py:109
  13.3 23.3 %collective-permute-start.10 = (bf16[4,2,128,128]{3,2,1,0:T(8,128)(2,1)S(1)}, bf16[4,2,128,128]{3,2,1,0:T(8,128)(2,1)S(1)}, u32[]{:S(2)}, u32[]{:S(2)}) collective-permute-start(bf16[4,2,128,128]{3,2,1,0:T(8,128)(2,1)S(1)} %copy-done), channel_id=1, source_target_pairs={{0,4},{1,5},{4,8},{5,9},{8,12},{9,13},{12,0},{13,1},{2,6},{3,7},{6... | collective-permute-start | bytes 786440 | tf_op jit(solution)/shard_map/ppermute | solution.py:109
  13.3 26.3 %collective-permute-start.12 = (bf16[4,2,128,128]{3,2,1,0:T(8,128)(2,1)S(1)}, bf16[4,2,128,128]{3,2,1,0:T(8,128)(2,1)S(1)}, u32[]{:S(2)}, u32[]{:S(2)}) collective-permute-start(bf16[4,2,128,128]{3,2,1,0:T(8,128)(2,1)S(1)} %copy-done), channel_id=1, source_target_pairs={{0,1},{1,0},{4,5},{5,4},{8,9},{9,8},{12,13},{13,12},{2,3},{3,2},{6... | collective-permute-start | bytes 786440 | tf_op jit(solution)/shard_map/ppermute | solution.py:109
  13.6 27.1 %collective-permute-start.2 = (bf16[4,2,128,128]{3,2,1,0:T(8,128)(2,1)S(1)}, bf16[4,2,128,128]{3,2,1,0:T(8,128)(2,1)S(1)}, u32[]{:S(2)}, u32[]{:S(2)}) collective-permute-start(bf16[4,2,128,128]{3,2,1,0:T(8,128)(2,1)S(1)} %copy-done), channel_id=1, source_target_pairs={{0,12},{1,13},{4,0},{5,1},{8,4},{9,5},{12,8},{13,9},{2,14},{3,15},... | collective-permute-start | bytes 786440 | tf_op jit(solution)/shard_map/ppermute | solution.py:109
  16.0 25.1 %collective-permute-start.4 = (bf16[4,2,128,128]{3,2,1,0:T(8,128)(2,1)S(1)}, bf16[4,2,128,128]{3,2,1,0:T(8,128)(2,1)S(1)}, u32[]{:S(2)}, u32[]{:S(2)}) collective-permute-start(bf16[4,2,128,128]{3,2,1,0:T(8,128)(2,1)S(1)} %copy-done), channel_id=1, source_target_pairs={{0,9},{1,8},{4,13},{5,12},{8,1},{9,0},{12,5},{13,4},{2,11},{3,10},... | collective-permute-start | bytes 786440 | tf_op jit(solution)/shard_map/ppermute | solution.py:109
  35.0 10.8 %collective-permute-start.6 = (bf16[4,2,128,128]{3,2,1,0:T(8,128)(2,1)S(1)}, bf16[4,2,128,128]{3,2,1,0:T(8,128)(2,1)S(1)}, u32[]{:S(2)}, u32[]{:S(2)}) collective-permute-start(bf16[4,2,128,128]{3,2,1,0:T(8,128)(2,1)S(1)} %copy-done), channel_id=1, source_target_pairs={{0,8},{1,9},{4,12},{5,13},{8,0},{9,1},{12,4},{13,5},{2,10},{3,11},... | collective-permute-start | bytes 786440 | tf_op jit(solution)/shard_map/ppermute | solution.py:109
  36.6 11.4 %collective-permute-start.8 = (bf16[4,2,128,128]{3,2,1,0:T(8,128)(2,1)S(1)}, bf16[4,2,128,128]{3,2,1,0:T(8,128)(2,1)S(1)}, u32[]{:S(2)}, u32[]{:S(2)}) collective-permute-start(bf16[4,2,128,128]{3,2,1,0:T(8,128)(2,1)S(1)} %copy-done), channel_id=1, source_target_pairs={{0,5},{1,4},{4,9},{5,8},{8,13},{9,12},{12,1},{13,0},{2,7},{3,6},{6... | collective-permute-start | bytes 786440 | tf_op jit(solution)/shard_map/ppermute | solution.py:109
  39.6 9.9 %collective-permute-start.14 = (bf16[4,2,128,128]{3,2,1,0:T(8,128)(2,1)S(1)}, bf16[4,2,128,128]{3,2,1,0:T(8,128)(2,1)S(1)}, u32[]{:S(2)}, u32[]{:S(2)}) collective-permute-start(bf16[4,2,128,128]{3,2,1,0:T(8,128)(2,1)S(1)} %copy-done), channel_id=1, source_target_pairs={{0,2},{2,0},{1,3},{3,1},{4,6},{6,4},{5,7},{7,5},{8,10},{10,8},{9,1... | collective-permute-start | bytes 786440 | tf_op jit(solution)/shard_map/ppermute | solution.py:112
  40.7 9.4 %collective-permute-start.1 = (bf16[4,2,128,128]{3,2,1,0:T(8,128)(2,1)S(1)}, bf16[4,2,128,128]{3,2,1,0:T(8,128)(2,1)S(1)}, u32[]{:S(2)}, u32[]{:S(2)}) collective-permute-start(bf16[4,2,128,128]{3,2,1,0:T(8,128)(2,1)S(1)} %collective-permute-done.rest_0_), channel_id=1, source_target_pairs={{0,2},{2,0},{1,3},{3,1},{4,6},{6,4},{5,7},{7,5},{8,10},{10,8},{9,1... | collective-permute-start | bytes 786440 | tf_op jit(solution)/shard_map/ppermute | solution.py:112
  41.1 11.0 %collective-permute-start.11 = (bf16[4,2,128,128]{3,2,1,0:T(8,128)(2,1)S(1)}, bf16[4,2,128,128]{3,2,1,0:T(8,128)(2,1)S(1)}, u32[]{:S(2)}, u32[]{:S(2)}) collective-permute-start(bf16[4,2,128,128]{3,2,1,0:T(8,128)(2,1)S(1)} %collective-permute-done.10.rest_10_), channel_id=1, source_target_pairs={{0,2},{2,0},{1,3},{3,1},{4,6},{6,4},{5,7},{7,5},{8,10},{10,8},{9,1... | collective-permute-start | bytes 786440 | tf_op jit(solution)/shard_map/ppermute | solution.py:112
  45.8 7.7 %collective-permute-start.13 = (bf16[4,2,128,128]{3,2,1,0:T(8,128)(2,1)S(1)}, bf16[4,2,128,128]{3,2,1,0:T(8,128)(2,1)}, u32[]{:S(2)}, u32[]{:S(2)}) collective-permute-start(bf16[4,2,128,128]{3,2,1,0:T(8,128)(2,1)S(1)} %collective-permute-done.12.rest_12_), channel_id=1, source_target_pairs={{0,2},{2,0},{1,3},{3,1},{4,6},{6,4},{5,7},{7,5},{8,10},{10,8},{9,1... | collective-permute-start | bytes 786440 | tf_op jit(solution)/shard_map/ppermute | solution.py:112
  48.0 5.5 %collective-permute-start.3 = (bf16[4,2,128,128]{3,2,1,0:T(8,128)(2,1)S(1)}, bf16[4,2,128,128]{3,2,1,0:T(8,128)(2,1)}, u32[]{:S(2)}, u32[]{:S(2)}) collective-permute-start(bf16[4,2,128,128]{3,2,1,0:T(8,128)(2,1)S(1)} %collective-permute-done.2.rest_2_), channel_id=1, source_target_pairs={{0,2},{2,0},{1,3},{3,1},{4,6},{6,4},{5,7},{7,5},{8,10},{10,8},{9,1... | collective-permute-start | bytes 786440 | tf_op jit(solution)/shard_map/ppermute | solution.py:112
  49.4 0.7 copy-start.5
  50.1 3.4 %collective-permute-start.5 = (bf16[4,2,128,128]{3,2,1,0:T(8,128)(2,1)S(1)}, bf16[4,2,128,128]{3,2,1,0:T(8,128)(2,1)S(1)}, u32[]{:S(2)}, u32[]{:S(2)}) collective-permute-start(bf16[4,2,128,128]{3,2,1,0:T(8,128)(2,1)S(1)} %collective-permute-done.4.rest_4_), channel_id=1, source_target_pairs={{0,2},{2,0},{1,3},{3,1},{4,6},{6,4},{5,7},{7,5},{8,10},{10,8},{9,1... | collective-permute-start | bytes 786440 | tf_op jit(solution)/shard_map/ppermute | solution.py:112
  50.2 0.7 copy-start.7
  50.9 3.3 %collective-permute-start.7 = (bf16[4,2,128,128]{3,2,1,0:T(8,128)(2,1)S(1)}, bf16[4,2,128,128]{3,2,1,0:T(8,128)(2,1)S(1)}, u32[]{:S(2)}, u32[]{:S(2)}) collective-permute-start(bf16[4,2,128,128]{3,2,1,0:T(8,128)(2,1)S(1)} %collective-permute-done.6.rest_6_), channel_id=1, source_target_pairs={{0,2},{2,0},{1,3},{3,1},{4,6},{6,4},{5,7},{7,5},{8,10},{10,8},{9,1... | collective-permute-start | bytes 786440 | tf_op jit(solution)/shard_map/ppermute | solution.py:112
  51.4 0.7 copy-start.1
  52.1 0.7 copy-start.9
  52.8 2.1 %collective-permute-start.9 = (bf16[4,2,128,128]{3,2,1,0:T(8,128)(2,1)S(1)}, bf16[4,2,128,128]{3,2,1,0:T(8,128)(2,1)}, u32[]{:S(2)}, u32[]{:S(2)}) collective-permute-start(bf16[4,2,128,128]{3,2,1,0:T(8,128)(2,1)S(1)} %collective-permute-done.8.rest_8_), channel_id=1, source_target_pairs={{0,2},{2,0},{1,3},{3,1},{4,6},{6,4},{5,7},{7,5},{8,10},{10,8},{9,1... | collective-permute-start | bytes 786440 | tf_op jit(solution)/shard_map/ppermute | solution.py:112
  52.8 0.7 copy-start.3
  53.5 0.7 copy-start.11
  54.2 0.7 copy-start.13
  54.9 1.0 copy-start.2
  55.9 0.9 copy-start.4
  56.8 0.9 copy-start.6
  57.8 0.9 copy-start.8
  58.7 0.9 copy-start.10
  59.7 0.9 copy-start.12
  60.6 0.9 copy-start.14
  67.8 25.9 %collective-permute-start.15 = (f32[128,8,128]{2,1,0:T(8,128)S(1)}, f32[128,8,128]{2,1,0:T(8,128)S(1)}, u32[]{:S(2)}, u32[]{:S(2)}) collective-permute-start(f32[128,8,128]{2,1,0:T(8,128)S(1)} %dynamic-slice_bitcast_fusion), channel_id=1, source_target_pairs={{0,16},{16,0},{1,17},{17,1},{2,18},{18,2},{3,19},{19,3},{4,20},{20... | collective-permute-start | bytes 1572872 | tf_op jit(solution)/shard_map/ppermute | solution.py:133

commit v4 on v3

v4 whole, which is shorter than its diff:
```python
import functools

import jax
import jax.numpy as jnp
from jax import lax
from jax.experimental import pallas as pl
from jax.experimental.pallas import tpu as pltpu
from jax.sharding import Mesh
from jax.sharding import PartitionSpec as P

SEATS = 16
SUB = 8


def axes(core, cols):
    bits = [bit for bit in (1, 2, 4, 8) if bit != cols]
    return bits[core:] + bits[:core]


def origin(step, swapped, seat, cols):
    first = lax.rem(seat // cols, 2)
    if swapped:
        seat, first = seat ^ cols, 1 - first
    masks = []
    for core in range(2):
        d = axes(core, cols)
        masks.append((0, d[0], d[1], d[2], d[0] ^ d[1], d[1] ^ d[2], d[2] ^ d[0], 7 * 2 + 1 - cols)[step])
    return seat ^ jnp.where(first == 0, masks[0], masks[1])


def slice_kernel(p_ids, q_ids, q_ref, out_ref):
    blocks, per_q, extent, _ = q_ref.shape
    per_p = p_ids.shape[0]
    strip = extent // SEATS
    rows = per_q * strip
    lane = lax.broadcasted_iota(jnp.int32, (2 * SUB, extent), 1)
    ids = jnp.zeros((2 * SUB, extent), jnp.int32)
    for f in range(blocks):
        for k in range(per_p + per_q):
            value = p_ids[k, f] if k < per_p else q_ids[f, k - per_p]
            ids = jnp.where(lane == f * (per_p + per_q) + k, value, ids)
    ids = ids.astype(out_ref.dtype)
    for f in range(blocks):
        flipped = [q_ref[f, k].astype(jnp.float32).T for k in range(per_q)]
        for j in range(SEATS):
            pieces = [tile[j * strip:(j + 1) * strip] for tile in flipped]
            out_ref[j, f * rows:(f + 1) * rows] = jnp.concatenate(pieces, axis=0).astype(out_ref.dtype)
    for j in range(SEATS):
        out_ref[j, blocks * rows:] = ids


def product_kernel(tile_count, cols, q_ref, *rest):
    p_refs, (acc_ref, held, p_sems, wide_ids, ids, id_sem) = rest[:SEATS], rest[SEATS:]
    blocks, per_p, extent, _ = p_refs[0].shape
    strip = acc_ref.shape[1]
    rows = (q_ref.shape[1] - 2 * SUB) // blocks
    per_q = rows // strip
    copies = [pltpu.make_async_copy(p_refs[i], held.at[i], p_sems.at[i]) for i in range(SEATS)]
    for copy in copies:
        copy.start()
    for s in range(SEATS):
        wide_ids[s:s + 1] = q_ref[s, blocks * rows:, :].astype(jnp.int32)[:1]
    id_copy = pltpu.make_async_copy(wide_ids, ids, id_sem)
    id_copy.start()
    acc_ref[...] = jnp.zeros_like(acc_ref)
    id_copy.wait()
    here = lax.axis_index(("pair", "core", "col"))
    for i in range(SEATS):
        copies[i].wait()
        seat = origin(i // 2, i % 2, here, cols)
        for f in range(blocks):
            left = q_ref[seat, f * rows:(f + 1) * rows]
            first = f * (per_p + per_q)
            for k in range(per_p):
                product = jnp.dot(left, held[i, f, k], preferred_element_type=jnp.float32)
                base = ids[seat, first + k] * tile_count
                for l in range(per_q):
                    spot = base + ids[seat, first + per_p + l]
                    acc_ref[spot] += product[l * strip:(l + 1) * strip]


def finish_kernel(x_ref, out_ref):
    planes, seats, tiles, strip, extent = x_ref.shape
    for t in range(tiles):
        whole = x_ref[0, :, t]
        for z in range(1, planes):
            whole = whole + x_ref[z, :, t]
        out_ref[:, t * extent:(t + 1) * extent] = whole.reshape(seats * strip, extent).T


def body(p_tiles, p_cols, q_tiles, q_cols):
    blocks, per_p, extent, _ = p_tiles.shape
    per_q = q_tiles.shape[1]
    planes = lax.axis_size("plane")
    pairs, cores, cols = lax.axis_size("pair"), lax.axis_size("core"), lax.axis_size("col")
    tile_count = planes * pairs * cores
    strip = extent // SEATS
    height = blocks * per_q * strip + 2 * SUB
    seat = ("pair", "core", "col")

    sliced = pl.pallas_call(
        slice_kernel,
        out_shape=jax.ShapeDtypeStruct((SEATS, height, extent), q_tiles.dtype),
        in_specs=[pl.BlockSpec(memory_space=pltpu.SMEM)] * 2 + [pl.BlockSpec(memory_space=pltpu.VMEM)],
        name="cut_columns",
    )(p_cols.T, q_cols, q_tiles)
    q_here = lax.all_to_all(sliced, seat, split_axis=0, concat_axis=0, tiled=True)

    def along(values, step):
        hops = [(s, s ^ axes(s // cols % 2, cols)[step]) for s in range(SEATS)]
        return lax.ppermute(values, seat, hops)

    def across(values):
        return lax.ppermute(values, seat, [(s, s ^ cols) for s in range(SEATS)])

    one, two, three = (along(p_tiles, step) for step in range(3))
    one, two, three, _ = lax.optimization_barrier((one, two, three, sliced))
    sets = [p_tiles, one, two, three, along(one, 1), along(two, 2), along(three, 0)]
    sets.append(along(sets[4], 2))
    sets = [each for kept in sets for each in (kept, across(kept))]

    acc = pl.pallas_call(
        functools.partial(product_kernel, tile_count, cols),
        out_shape=jax.ShapeDtypeStruct((tile_count * tile_count, strip, extent), jnp.float32),
        in_specs=[pl.BlockSpec(memory_space=pltpu.VMEM)]
        + [pl.BlockSpec(memory_space=pl.ANY)] * SEATS,
        scratch_shapes=[
            pltpu.VMEM((SEATS, blocks, per_p, extent, extent), p_tiles.dtype),
            pltpu.SemaphoreType.DMA((SEATS,)),
            pltpu.VMEM((SEATS, extent), jnp.int32),
            pltpu.SMEM((SEATS, extent), jnp.int32),
            pltpu.SemaphoreType.DMA,
        ],
        compiler_params=pltpu.CompilerParams(vmem_limit_bytes=60 << 20),
        name="products",
    )(q_here, *sets)

    every = ("plane",) + seat
    parts = acc.reshape(planes * SEATS, tile_count // cols, strip, extent)
    landed = lax.all_to_all(parts, every, split_axis=0, concat_axis=0, tiled=True)
    return pl.pallas_call(
        finish_kernel,
        out_shape=jax.ShapeDtypeStruct((extent, tile_count // cols * extent), jnp.float32),
        name="turn",
    )(landed.reshape(planes, SEATS, tile_count // cols, strip, extent))


def solution(mesh):
    rows, cols = mesh.devices.shape
    pairs = SEATS // (2 * cols)
    shape = (rows // (2 * pairs), pairs, 2, cols)
    every = ("plane", "pair", "core", "col")
    inner = Mesh(mesh.devices.reshape(shape), every)
    placed = (
        P(every, None, None, None),
        P(every, None),
        P(every, None, None, None),
        P(every, None),
    )
    return jax.shard_map(
        body, mesh=inner, in_specs=placed, out_specs=P(every[:3], "col"), check_vma=False
    )
```

time: 110 us -> 86.8 us (0.79)
  waiting for transfers between devices: 46.7 us -> 17.7 us
  blocking collectives: 13.4 us -> 30 us
  local copies, waits for them, and re-layouts: 12.9 us -> 2.48 us
  starting transfers between devices: 25.5 us -> 22.7 us
  Pallas kernels: 10.5 us -> 13 us
    ppermute x16 -> x15, waiting for transfers between devices: 46.7 us -> 17.7 us  [the longest x7 17.6 us: along(): return lax.ppermute(values, seat, hops)]
    all_to_all x1, blocking collectives: 13.4 us -> 30 us  [body(): lax.all_to_all(parts, every, split_axis=0, concat_axis=0, tiled=True)]
    unnamed x31 -> x32, local copies, waits for them, and re-layouts: 12.9 us -> 2.48 us
    ppermute x16 -> x15, starting transfers between devices: 19.1 us -> 16.3 us  [the longest x7 8.93 us: along(): return lax.ppermute(values, seat, hops)]
    pallas_call x1, Pallas kernels: 6.13 us -> 8.49 us  [body(): pl.pallas_call(functools.partial(product_kernel, tile_count, cols), out_s...]
  transfers between devices with their start and end apart: 17 -> 16, of which waited for: 6 -> 4; matrix products, arithmetic and copies ran while one was open for 0% -> 0% of each run, Pallas kernels for 0% -> 0%
where the time goes in v4:
time: 86.8 us; the launch traced here: 86 us
  blocking collectives  30 us (35%)
  starting transfers between devices  22.7 us (26%)
  waiting for transfers between devices  17.7 us (20%)
  Pallas kernels  13 us (15%)
  local copies, waits for them, and re-layouts  2.48 us (3%)
    all_to_all x1, blocking collectives, body(): lax.all_to_all(parts, every, split_axis=0, concat_axis=0, tiled=True)  30 us
    ppermute x7, waiting for transfers between devices, along(): return lax.ppermute(values, seat, hops)  17.6 us
    ppermute x7, starting transfers between devices, along(): return lax.ppermute(values, seat, hops)  8.93 us
    pallas_call x1, Pallas kernels, body(): pl.pallas_call(functools.partial(product_kernel, tile_count, cols), out_s...  8.49 us
    ppermute x8, starting transfers between devices, across(): return lax.ppermute(values, seat, [(s, s ^ cols) for s in range(SEATS)])  7.35 us
    all_to_all x1, starting transfers between devices, body(): lax.all_to_all(sliced, seat, split_axis=0, concat_axis=0, tiled=True)  6.38 us
    unnamed x32, local copies, waits for them, and re-layouts  2.48 us
    pallas_call x1, Pallas kernels, body(): pl.pallas_call(slice_kernel, out_shape=jax.ShapeDtypeStruct((SEATS, heigh...  2.34 us
  transfers between devices with their start and end apart: 16, of which 4 were waited for; matrix products, arithmetic and copies ran while one was open for 0% of the time, Pallas kernels for 0%

profile of v4, /device:TPU:1, one launch (start us, length us, event | category | flops | bytes accessed | tf_op | source)
XLA Modules:
  0.0 86.0 jit_solution(12368111701412809774)
XLA Ops:
  0.0 2.3 %cut_columns.1 = bf16[16,208,128]{2,1,0:T(8,128)(2,1)} custom-call(s32[2,4]{1,0:T(2,128)} %bitcast.5, s32[4,6]{1,0:T(4,128)} %q_ids.1, bf16[4,6,128,128]{3,2,1,0:T(8,128)(2,1)} %q_ref.1), custom_call_target="tpu_custom_call" | custom-call | tf_op jit(solution)/shard_map/cut_columns/pallas_call | solution.py:101
  2.3 0.0 copy-start.1
  2.3 6.4 %all-to-all-start = ((bf16[16,208,128]{2,1,0:T(8,128)(2,1)}), bf16[16,208,128]{2,1,0:T(8,128)(2,1)S(1)}, u32[]{:S(2)}, u32[]{:S(2)}) async-start(bf16[16,208,128]{2,1,0:T(8,128)(2,1)} %cut_columns.1), calls=%async_computation | async-start | bytes 1703936 | tf_op jit(solution)/shard_map/all_to_all | solution.py:107
  8.7 0.0 copy-done.1
  8.7 1.5 %collective-permute-start.2 = (bf16[4,2,128,128]{3,2,1,0:T(8,128)(2,1)S(1)}, bf16[4,2,128,128]{3,2,1,0:T(8,128)(2,1)S(1)}, u32[]{:S(2)}, u32[]{:S(2)}) collective-permute-start(bf16[4,2,128,128]{3,2,1,0:T(8,128)(2,1)S(1)} %copy-done.1), channel_id=1, source_target_pairs={{0,4},{1,5},{2,10},{3,11},{4,0},{5,1},{6,14},{7,15},{8,12},{9,13},... | collective-permute-start | bytes 786440 | tf_op jit(solution)/shard_map/ppermute | solution.py:111
  10.2 1.2 %collective-permute-start.1 = (bf16[4,2,128,128]{3,2,1,0:T(8,128)(2,1)S(1)}, bf16[4,2,128,128]{3,2,1,0:T(8,128)(2,1)S(1)}, u32[]{:S(2)}, u32[]{:S(2)}) collective-permute-start(bf16[4,2,128,128]{3,2,1,0:T(8,128)(2,1)S(1)} %copy-done.1), channel_id=1, source_target_pairs={{0,1},{1,0},{2,6},{3,7},{4,5},{5,4},{6,2},{7,3},{8,9},{9,8},{10,14... | collective-permute-start | bytes 786440 | tf_op jit(solution)/shard_map/ppermute | solution.py:111
  11.4 1.2 %collective-permute-start.3 = (bf16[4,2,128,128]{3,2,1,0:T(8,128)(2,1)S(1)}, bf16[4,2,128,128]{3,2,1,0:T(8,128)(2,1)S(1)}, u32[]{:S(2)}, u32[]{:S(2)}) collective-permute-start(bf16[4,2,128,128]{3,2,1,0:T(8,128)(2,1)S(1)} %copy-done.1), channel_id=1, source_target_pairs={{0,8},{1,9},{2,3},{3,2},{4,12},{5,13},{6,7},{7,6},{8,0},{9,1},{10,... | collective-permute-start | bytes 786440 | tf_op jit(solution)/shard_map/ppermute | solution.py:111
  12.6 1.2 %collective-permute-start = (bf16[4,2,128,128]{3,2,1,0:T(8,128)(2,1)S(1)}, bf16[4,2,128,128]{3,2,1,0:T(8,128)(2,1)S(1)}, u32[]{:S(2)}, u32[]{:S(2)}) collective-permute-start(bf16[4,2,128,128]{3,2,1,0:T(8,128)(2,1)S(1)} %copy-done.1), channel_id=1, source_target_pairs={{0,2},{1,3},{2,0},{3,1},{4,6},{5,7},{6,4},{7,5},{8,10},{9,11},{10,... | collective-permute-start | bytes 786440 | tf_op jit(solution)/shard_map/ppermute | solution.py:114
  13.8 12.8 %collective-permute-done.2.rest_4_ = bf16[4,2,128,128]{3,2,1,0:T(8,128)(2,1)S(1)} collective-permute-done((bf16[4,2,128,128]{3,2,1,0:T(8,128)(2,1)S(1)}, bf16[4,2,128,128]{3,2,1,0:T(8,128)(2,1)S(1)}, u32[]{:S(2)}, u32[]{:S(2)}) %collective-permute-start.2) | collective-permute-done | bytes 262176 | tf_op jit(solution)/shard_map/ppermute | solution.py:111
  26.5 0.0 copy-start.2
  26.5 0.8 collective-permute-done.1.rest_2_
  27.3 0.0 copy-start.3
  27.3 0.0 collective-permute-done.3.rest_6_
  27.3 0.0 copy-start.4
  27.3 1.2 %collective-permute-start.7 = (bf16[4,2,128,128]{3,2,1,0:T(8,128)(2,1)S(1)}, bf16[4,2,128,128]{3,2,1,0:T(8,128)(2,1)S(1)}, u32[]{:S(2)}, u32[]{:S(2)}) collective-permute-start(bf16[4,2,128,128]{3,2,1,0:T(8,128)(2,1)S(1)} %collective-permute-done.1.rest_2_), channel_id=1, source_target_pairs={{0,4},{1,5},{2,10},{3,11},{4,0},{5,1},{6,14},{7,15},{8,12},{9,13},... | collective-permute-start | bytes 786440 | tf_op jit(solution)/shard_map/ppermute | solution.py:111
  28.5 0.0 collective-permute-start.4
  28.5 1.1 %collective-permute-start.9 = (bf16[4,2,128,128]{3,2,1,0:T(8,128)(2,1)S(1)}, bf16[4,2,128,128]{3,2,1,0:T(8,128)(2,1)S(1)}, u32[]{:S(2)}, u32[]{:S(2)}) collective-permute-start(bf16[4,2,128,128]{3,2,1,0:T(8,128)(2,1)S(1)} %collective-permute-done.2.rest_4_), channel_id=1, source_target_pairs={{0,8},{1,9},{2,3},{3,2},{4,12},{5,13},{6,7},{7,6},{8,0},{9,1},{10,... | collective-permute-start | bytes 786440 | tf_op jit(solution)/shard_map/ppermute | solution.py:111
  29.6 0.1 collective-permute-start.5
  29.7 0.0 collective-permute-done.rest_1_
  29.7 0.0 copy-start.5
  29.7 1.5 %collective-permute-start.11 = (bf16[4,2,128,128]{3,2,1,0:T(8,128)(2,1)S(1)}, bf16[4,2,128,128]{3,2,1,0:T(8,128)(2,1)S(1)}, u32[]{:S(2)}, u32[]{:S(2)}) collective-permute-start(bf16[4,2,128,128]{3,2,1,0:T(8,128)(2,1)S(1)} %collective-permute-done.3.rest_6_), channel_id=1, source_target_pairs={{0,1},{1,0},{2,6},{3,7},{4,5},{5,4},{6,2},{7,3},{8,9},{9,8},{10,14... | collective-permute-start | bytes 786440 | tf_op jit(solution)/shard_map/ppermute | solution.py:111
  31.3 2.2 %collective-permute-done.7.rest_8_ = bf16[4,2,128,128]{3,2,1,0:T(8,128)(2,1)S(1)} collective-permute-done((bf16[4,2,128,128]{3,2,1,0:T(8,128)(2,1)S(1)}, bf16[4,2,128,128]{3,2,1,0:T(8,128)(2,1)S(1)}, u32[]{:S(2)}, u32[]{:S(2)}) %collective-permute-start.7) | collective-permute-done | bytes 262176 | tf_op jit(solution)/shard_map/ppermute | solution.py:111
  33.5 0.0 copy-start.6
  33.5 1.3 %collective-permute-start.13 = (bf16[4,2,128,128]{3,2,1,0:T(8,128)(2,1)S(1)}, bf16[4,2,128,128]{3,2,1,0:T(8,128)(2,1)S(1)}, u32[]{:S(2)}, u32[]{:S(2)}) collective-permute-start(bf16[4,2,128,128]{3,2,1,0:T(8,128)(2,1)S(1)} %collective-permute-done.7.rest_8_), channel_id=1, source_target_pairs={{0,8},{1,9},{2,3},{3,2},{4,12},{5,13},{6,7},{7,6},{8,0},{9,1},{10,... | collective-permute-start | bytes 786440 | tf_op jit(solution)/shard_map/ppermute | solution.py:111
  34.8 0.0 collective-permute-done.4.rest_3_
  34.8 0.0 copy-start.7
  34.8 2.3 %collective-permute-start.6 = (bf16[4,2,128,128]{3,2,1,0:T(8,128)(2,1)S(1)}, bf16[4,2,128,128]{3,2,1,0:T(8,128)(2,1)S(1)}, u32[]{:S(2)}, u32[]{:S(2)}) collective-permute-start(bf16[4,2,128,128]{3,2,1,0:T(8,128)(2,1)S(1)} %collective-permute-done.3.rest_6_), channel_id=1, source_target_pairs={{0,2},{1,3},{2,0},{3,1},{4,6},{5,7},{6,4},{7,5},{8,10},{9,11},{10,... | collective-permute-start | bytes 786440 | tf_op jit(solution)/shard_map/ppermute | solution.py:114
  37.1 0.0 collective-permute-done.9.rest_10_
  37.1 0.0 copy-start.8
  37.1 0.1 collective-permute-start.8
  37.1 0.0 collective-permute-done.5.rest_5_
  37.1 0.0 copy-start.9
  37.2 0.4 collective-permute-start.10
  37.6 0.0 collective-permute-done.11.rest_12_
  37.6 0.2 collective-permute-start.12
  37.8 1.9 %collective-permute-done.13.rest_14_ = bf16[4,2,128,128]{3,2,1,0:T(8,128)(2,1)S(1)} collective-permute-done((bf16[4,2,128,128]{3,2,1,0:T(8,128)(2,1)S(1)}, bf16[4,2,128,128]{3,2,1,0:T(8,128)(2,1)S(1)}, u32[]{:S(2)}, u32[]{:S(2)}) %collective-permute-start.13) | collective-permute-done | bytes 262176 | tf_op jit(solution)/shard_map/ppermute | solution.py:111
  39.6 3.1 %collective-permute-start.14 = (bf16[4,2,128,128]{3,2,1,0:T(8,128)(2,1)S(1)}, bf16[4,2,128,128]{3,2,1,0:T(8,128)(2,1)}, u32[]{:S(2)}, u32[]{:S(2)}) collective-permute-start(bf16[4,2,128,128]{3,2,1,0:T(8,128)(2,1)S(1)} %collective-permute-done.13.rest_14_), channel_id=1, source_target_pairs={{0,2},{1,3},{2,0},{3,1},{4,6},{5,7},{6,4},{7,5},{8,10},{9,11},{10,... | collective-permute-start | bytes 786440 | tf_op jit(solution)/shard_map/ppermute | solution.py:114
  42.7 0.0 collective-permute-done.6.rest_7_
  42.7 0.0 collective-permute-done.8.rest_9_
  42.7 0.0 copy-start.13
  42.7 0.0 collective-permute-done.10.rest_11_
  42.7 0.0 copy-start.14
  42.7 0.0 collective-permute-done.12.rest_13_
  42.8 0.6 copy-done.12
  43.4 0.1 copy-done.13
  43.5 0.1 copy-done.14
  43.6 0.7 copy-done.15
  44.3 0.0 collective-permute-done.14.rest_15_
  44.3 0.0 all-to-all-done.q_ref
  44.3 0.0 copy-done.2
  44.3 0.0 copy-done.3
  44.3 0.0 copy-done.4
  44.3 0.0 copy-done.5
  44.3 0.0 copy-done.6
  44.3 0.0 copy-done.7
  44.3 0.0 copy-done.8
  44.3 0.0 copy-done.9
  44.4 0.0 copy-done.10
  44.4 0.0 copy-done.11
  44.4 0.0 copy-start
  44.4 0.9 %copy-done = bf16[16,208,128]{2,1,0:T(8,128)(2,1)} copy-done((bf16[16,208,128]{2,1,0:T(8,128)(2,1)}, bf16[16,208,128]{2,1,0:T(8,128)(2,1)S(1)}, u32[]{:S(2)}) %copy-start) | copy-done | bytes 851992
  45.3 8.5 %products.1 = f32[256,8,128]{2,1,0:T(8,128)} custom-call(bf16[16,208,128]{2,1,0:T(8,128)(2,1)} %copy-done, bf16[4,2,128,128]{3,2,1,0:T(8,128)(2,1)} %rest_0_.1, bf16[4,2,128,128]{3,2,1,0:T(8,128)(2,1)} %copy-done.5, bf16[4,2,128,128]{3,2,1,0:T(8,128)(2,1)} %copy-done.3, bf16[4,2,128,128]{3,2,1,0:T(8,128)(2,1)} %copy-done.7, ...), custom_call_target="tpu_custom_call" | custom-call | tf_op jit(solution)/shard_map/products/pallas_call | solution.py:122
  53.8 30.0 %all_to_all.10 = f32[32,8,8,128]{3,2,1,0:T(8,128)} all-to-all(f32[32,8,8,128]{3,2,1,0:T(8,128)} %bitcast.4), channel_id=1, replica_groups=mesh['plane'=2,'pair'=4,'core'=2,'col'=2] {'plane','pair','core','col'}, dimensions={0} | all-to-all | bytes 2097152 | tf_op jit(solution)/shard_map/all_to_all | solution.py:140
  83.8 2.2 %turn.1 = f32[128,1024]{1,0:T(8,128)} custom-call(f32[2,16,8,8,128]{4,3,2,1,0:T(8,128)} %bitcast.3), custom_call_target="tpu_custom_call" | custom-call | tf_op jit(solution)/shard_map/turn/pallas_call | solution.py:141
  (4 shorter events, 0.0 us)
Async XLA Ops:
  2.3 6.4 %copy-start.1 = (bf16[4,2,128,128]{3,2,1,0:T(8,128)(2,1)S(1)}, bf16[4,2,128,128]{3,2,1,0:T(8,128)(2,1)}, u32[]{:S(2)}) copy-start(bf16[4,2,128,128]{3,2,1,0:T(8,128)(2,1)} %rest_0_.1) | copy-start | bytes 786436
  2.3 41.9 %all-to-all-start = ((bf16[16,208,128]{2,1,0:T(8,128)(2,1)}), bf16[16,208,128]{2,1,0:T(8,128)(2,1)S(1)}, u32[]{:S(2)}, u32[]{:S(2)}) async-start(bf16[16,208,128]{2,1,0:T(8,128)(2,1)} %cut_columns.1), calls=%async_computation | async-start | bytes 1703936 | tf_op jit(solution)/shard_map/all_to_all | solution.py:107
  8.7 17.8 %collective-permute-start.2 = (bf16[4,2,128,128]{3,2,1,0:T(8,128)(2,1)S(1)}, bf16[4,2,128,128]{3,2,1,0:T(8,128)(2,1)S(1)}, u32[]{:S(2)}, u32[]{:S(2)}) collective-permute-start(bf16[4,2,128,128]{3,2,1,0:T(8,128)(2,1)S(1)} %copy-done.1), channel_id=1, source_target_pairs={{0,4},{1,5},{2,10},{3,11},{4,0},{5,1},{6,14},{7,15},{8,12},{9,13},... | collective-permute-start | bytes 786440 | tf_op jit(solution)/shard_map/ppermute | solution.py:111
  10.2 17.1 %collective-permute-start.1 = (bf16[4,2,128,128]{3,2,1,0:T(8,128)(2,1)S(1)}, bf16[4,2,128,128]{3,2,1,0:T(8,128)(2,1)S(1)}, u32[]{:S(2)}, u32[]{:S(2)}) collective-permute-start(bf16[4,2,128,128]{3,2,1,0:T(8,128)(2,1)S(1)} %copy-done.1), channel_id=1, source_target_pairs={{0,1},{1,0},{2,6},{3,7},{4,5},{5,4},{6,2},{7,3},{8,9},{9,8},{10,14... | collective-permute-start | bytes 786440 | tf_op jit(solution)/shard_map/ppermute | solution.py:111
  11.4 15.9 %collective-permute-start.3 = (bf16[4,2,128,128]{3,2,1,0:T(8,128)(2,1)S(1)}, bf16[4,2,128,128]{3,2,1,0:T(8,128)(2,1)S(1)}, u32[]{:S(2)}, u32[]{:S(2)}) collective-permute-start(bf16[4,2,128,128]{3,2,1,0:T(8,128)(2,1)S(1)} %copy-done.1), channel_id=1, source_target_pairs={{0,8},{1,9},{2,3},{3,2},{4,12},{5,13},{6,7},{7,6},{8,0},{9,1},{10,... | collective-permute-start | bytes 786440 | tf_op jit(solution)/shard_map/ppermute | solution.py:111
  12.6 17.2 %collective-permute-start = (bf16[4,2,128,128]{3,2,1,0:T(8,128)(2,1)S(1)}, bf16[4,2,128,128]{3,2,1,0:T(8,128)(2,1)S(1)}, u32[]{:S(2)}, u32[]{:S(2)}) collective-permute-start(bf16[4,2,128,128]{3,2,1,0:T(8,128)(2,1)S(1)} %copy-done.1), channel_id=1, source_target_pairs={{0,2},{1,3},{2,0},{3,1},{4,6},{5,7},{6,4},{7,5},{8,10},{9,11},{10,... | collective-permute-start | bytes 786440 | tf_op jit(solution)/shard_map/ppermute | solution.py:114
  26.5 17.8 %copy-start.2 = (bf16[4,2,128,128]{3,2,1,0:T(8,128)(2,1)}, bf16[4,2,128,128]{3,2,1,0:T(8,128)(2,1)S(1)}, u32[]{:S(2)}) copy-start(bf16[4,2,128,128]{3,2,1,0:T(8,128)(2,1)S(1)} %collective-permute-done.2.rest_4_) | copy-start | bytes 786436
  27.3 17.0 %copy-start.3 = (bf16[4,2,128,128]{3,2,1,0:T(8,128)(2,1)}, bf16[4,2,128,128]{3,2,1,0:T(8,128)(2,1)S(1)}, u32[]{:S(2)}) copy-start(bf16[4,2,128,128]{3,2,1,0:T(8,128)(2,1)S(1)} %collective-permute-done.1.rest_2_) | copy-start | bytes 786436
  27.3 17.0 %copy-start.4 = (bf16[4,2,128,128]{3,2,1,0:T(8,128)(2,1)}, bf16[4,2,128,128]{3,2,1,0:T(8,128)(2,1)S(1)}, u32[]{:S(2)}) copy-start(bf16[4,2,128,128]{3,2,1,0:T(8,128)(2,1)S(1)} %collective-permute-done.3.rest_6_) | copy-start | bytes 786436
  27.3 6.2 %collective-permute-start.7 = (bf16[4,2,128,128]{3,2,1,0:T(8,128)(2,1)S(1)}, bf16[4,2,128,128]{3,2,1,0:T(8,128)(2,1)S(1)}, u32[]{:S(2)}, u32[]{:S(2)}) collective-permute-start(bf16[4,2,128,128]{3,2,1,0:T(8,128)(2,1)S(1)} %collective-permute-done.1.rest_2_), channel_id=1, source_target_pairs={{0,4},{1,5},{2,10},{3,11},{4,0},{5,1},{6,14},{7,15},{8,12},{9,13},... | collective-permute-start | bytes 786440 | tf_op jit(solution)/shard_map/ppermute | solution.py:111
  28.5 6.3 %collective-permute-start.4 = (bf16[4,2,128,128]{3,2,1,0:T(8,128)(2,1)S(1)}, bf16[4,2,128,128]{3,2,1,0:T(8,128)(2,1)S(1)}, u32[]{:S(2)}, u32[]{:S(2)}) collective-permute-start(bf16[4,2,128,128]{3,2,1,0:T(8,128)(2,1)S(1)} %collective-permute-done.1.rest_2_), channel_id=1, source_target_pairs={{0,2},{1,3},{2,0},{3,1},{4,6},{5,7},{6,4},{7,5},{8,10},{9,11},{10,... | collective-permute-start | bytes 786440 | tf_op jit(solution)/shard_map/ppermute | solution.py:114
  28.5 8.6 %collective-permute-start.9 = (bf16[4,2,128,128]{3,2,1,0:T(8,128)(2,1)S(1)}, bf16[4,2,128,128]{3,2,1,0:T(8,128)(2,1)S(1)}, u32[]{:S(2)}, u32[]{:S(2)}) collective-permute-start(bf16[4,2,128,128]{3,2,1,0:T(8,128)(2,1)S(1)} %collective-permute-done.2.rest_4_), channel_id=1, source_target_pairs={{0,8},{1,9},{2,3},{3,2},{4,12},{5,13},{6,7},{7,6},{8,0},{9,1},{10,... | collective-permute-start | bytes 786440 | tf_op jit(solution)/shard_map/ppermute | solution.py:111
  29.6 7.5 %collective-permute-start.5 = (bf16[4,2,128,128]{3,2,1,0:T(8,128)(2,1)S(1)}, bf16[4,2,128,128]{3,2,1,0:T(8,128)(2,1)S(1)}, u32[]{:S(2)}, u32[]{:S(2)}) collective-permute-start(bf16[4,2,128,128]{3,2,1,0:T(8,128)(2,1)S(1)} %collective-permute-done.2.rest_4_), channel_id=1, source_target_pairs={{0,2},{1,3},{2,0},{3,1},{4,6},{5,7},{6,4},{7,5},{8,10},{9,11},{10,... | collective-permute-start | bytes 786440 | tf_op jit(solution)/shard_map/ppermute | solution.py:114
  29.7 14.6 %copy-start.5 = (bf16[4,2,128,128]{3,2,1,0:T(8,128)(2,1)}, bf16[4,2,128,128]{3,2,1,0:T(8,128)(2,1)S(1)}, u32[]{:S(2)}) copy-start(bf16[4,2,128,128]{3,2,1,0:T(8,128)(2,1)S(1)} %collective-permute-done.rest_1_) | copy-start | bytes 786436
  29.7 7.9 %collective-permute-start.11 = (bf16[4,2,128,128]{3,2,1,0:T(8,128)(2,1)S(1)}, bf16[4,2,128,128]{3,2,1,0:T(8,128)(2,1)S(1)}, u32[]{:S(2)}, u32[]{:S(2)}) collective-permute-start(bf16[4,2,128,128]{3,2,1,0:T(8,128)(2,1)S(1)} %collective-permute-done.3.rest_6_), channel_id=1, source_target_pairs={{0,1},{1,0},{2,6},{3,7},{4,5},{5,4},{6,2},{7,3},{8,9},{9,8},{10,14... | collective-permute-start | bytes 786440 | tf_op jit(solution)/shard_map/ppermute | solution.py:111
  33.5 10.8 %copy-start.6 = (bf16[4,2,128,128]{3,2,1,0:T(8,128)(2,1)}, bf16[4,2,128,128]{3,2,1,0:T(8,128)(2,1)S(1)}, u32[]{:S(2)}) copy-start(bf16[4,2,128,128]{3,2,1,0:T(8,128)(2,1)S(1)} %collective-permute-done.7.rest_8_) | copy-start | bytes 786436
  33.5 6.1 %collective-permute-start.13 = (bf16[4,2,128,128]{3,2,1,0:T(8,128)(2,1)S(1)}, bf16[4,2,128,128]{3,2,1,0:T(8,128)(2,1)S(1)}, u32[]{:S(2)}, u32[]{:S(2)}) collective-permute-start(bf16[4,2,128,128]{3,2,1,0:T(8,128)(2,1)S(1)} %collective-permute-done.7.rest_8_), channel_id=1, source_target_pairs={{0,8},{1,9},{2,3},{3,2},{4,12},{5,13},{6,7},{7,6},{8,0},{9,1},{10,... | collective-permute-start | bytes 786440 | tf_op jit(solution)/shard_map/ppermute | solution.py:111
  34.8 9.6 %copy-start.7 = (bf16[4,2,128,128]{3,2,1,0:T(8,128)(2,1)}, bf16[4,2,128,128]{3,2,1,0:T(8,128)(2,1)S(1)}, u32[]{:S(2)}) copy-start(bf16[4,2,128,128]{3,2,1,0:T(8,128)(2,1)S(1)} %collective-permute-done.4.rest_3_) | copy-start | bytes 786436
  34.8 7.9 %collective-permute-start.6 = (bf16[4,2,128,128]{3,2,1,0:T(8,128)(2,1)S(1)}, bf16[4,2,128,128]{3,2,1,0:T(8,128)(2,1)S(1)}, u32[]{:S(2)}, u32[]{:S(2)}) collective-permute-start(bf16[4,2,128,128]{3,2,1,0:T(8,128)(2,1)S(1)} %collective-permute-done.3.rest_6_), channel_id=1, source_target_pairs={{0,2},{1,3},{2,0},{3,1},{4,6},{5,7},{6,4},{7,5},{8,10},{9,11},{10,... | collective-permute-start | bytes 786440 | tf_op jit(solution)/shard_map/ppermute | solution.py:114
  37.1 7.3 %copy-start.8 = (bf16[4,2,128,128]{3,2,1,0:T(8,128)(2,1)}, bf16[4,2,128,128]{3,2,1,0:T(8,128)(2,1)S(1)}, u32[]{:S(2)}) copy-start(bf16[4,2,128,128]{3,2,1,0:T(8,128)(2,1)S(1)} %collective-permute-done.9.rest_10_) | copy-start | bytes 786436
  37.1 5.7 %collective-permute-start.8 = (bf16[4,2,128,128]{3,2,1,0:T(8,128)(2,1)S(1)}, bf16[4,2,128,128]{3,2,1,0:T(8,128)(2,1)S(1)}, u32[]{:S(2)}, u32[]{:S(2)}) collective-permute-start(bf16[4,2,128,128]{3,2,1,0:T(8,128)(2,1)S(1)} %collective-permute-done.7.rest_8_), channel_id=1, source_target_pairs={{0,2},{1,3},{2,0},{3,1},{4,6},{5,7},{6,4},{7,5},{8,10},{9,11},{10,... | collective-permute-start | bytes 786440 | tf_op jit(solution)/shard_map/ppermute | solution.py:114
  37.1 7.2 %copy-start.9 = (bf16[4,2,128,128]{3,2,1,0:T(8,128)(2,1)}, bf16[4,2,128,128]{3,2,1,0:T(8,128)(2,1)S(1)}, u32[]{:S(2)}) copy-start(bf16[4,2,128,128]{3,2,1,0:T(8,128)(2,1)S(1)} %collective-permute-done.5.rest_5_) | copy-start | bytes 786436
  37.2 5.6 %collective-permute-start.10 = (bf16[4,2,128,128]{3,2,1,0:T(8,128)(2,1)S(1)}, bf16[4,2,128,128]{3,2,1,0:T(8,128)(2,1)S(1)}, u32[]{:S(2)}, u32[]{:S(2)}) collective-permute-start(bf16[4,2,128,128]{3,2,1,0:T(8,128)(2,1)S(1)} %collective-permute-done.9.rest_10_), channel_id=1, source_target_pairs={{0,2},{1,3},{2,0},{3,1},{4,6},{5,7},{6,4},{7,5},{8,10},{9,11},{10,... | collective-permute-start | bytes 786440 | tf_op jit(solution)/shard_map/ppermute | solution.py:114
  37.6 6.8 %copy-start.10 = (bf16[4,2,128,128]{3,2,1,0:T(8,128)(2,1)}, bf16[4,2,128,128]{3,2,1,0:T(8,128)(2,1)S(1)}, u32[]{:S(2)}) copy-start(bf16[4,2,128,128]{3,2,1,0:T(8,128)(2,1)S(1)} %collective-permute-done.11.rest_12_) | copy-start | bytes 786436
  37.6 5.2 %collective-permute-start.12 = (bf16[4,2,128,128]{3,2,1,0:T(8,128)(2,1)S(1)}, bf16[4,2,128,128]{3,2,1,0:T(8,128)(2,1)S(1)}, u32[]{:S(2)}, u32[]{:S(2)}) collective-permute-start(bf16[4,2,128,128]{3,2,1,0:T(8,128)(2,1)S(1)} %collective-permute-done.11.rest_12_), channel_id=1, source_target_pairs={{0,2},{1,3},{2,0},{3,1},{4,6},{5,7},{6,4},{7,5},{8,10},{9,11},{10,... | collective-permute-start | bytes 786440 | tf_op jit(solution)/shard_map/ppermute | solution.py:114
  39.6 4.7 %copy-start.11 = (bf16[4,2,128,128]{3,2,1,0:T(8,128)(2,1)}, bf16[4,2,128,128]{3,2,1,0:T(8,128)(2,1)S(1)}, u32[]{:S(2)}) copy-start(bf16[4,2,128,128]{3,2,1,0:T(8,128)(2,1)S(1)} %collective-permute-done.13.rest_14_) | copy-start | bytes 786436
  39.6 4.6 %collective-permute-start.14 = (bf16[4,2,128,128]{3,2,1,0:T(8,128)(2,1)S(1)}, bf16[4,2,128,128]{3,2,1,0:T(8,128)(2,1)}, u32[]{:S(2)}, u32[]{:S(2)}) collective-permute-start(bf16[4,2,128,128]{3,2,1,0:T(8,128)(2,1)S(1)} %collective-permute-done.13.rest_14_), channel_id=1, source_target_pairs={{0,2},{1,3},{2,0},{3,1},{4,6},{5,7},{6,4},{7,5},{8,10},{9,11},{10,... | collective-permute-start | bytes 786440 | tf_op jit(solution)/shard_map/ppermute | solution.py:114
  42.7 0.7 copy-start.12
  42.7 0.8 copy-start.13
  42.7 0.8 copy-start.14
  43.6 0.7 copy-start.15
  44.4 0.9 %copy-start = (bf16[16,208,128]{2,1,0:T(8,128)(2,1)}, bf16[16,208,128]{2,1,0:T(8,128)(2,1)S(1)}, u32[]{:S(2)}) copy-start(bf16[16,208,128]{2,1,0:T(8,128)(2,1)S(1)} %all-to-all-done.q_ref) | copy-start | bytes 2555908

commit v5 on v4

--- a/solution.py
+++ b/solution.py
@@ -49,34 +49,59 @@
         out_ref[j, blocks * rows:] = ids
 
 
-def product_kernel(tile_count, cols, q_ref, *rest):
-    p_refs, (acc_ref, held, p_sems, wide_ids, ids, id_sem) = rest[:SEATS], rest[SEATS:]
+def product_kernel(tile_count, cols, steps, q_ref, *rest):
+    count = 2 * len(steps)
+    p_refs, (acc_ref, wide_ids, ids, id_sem) = rest[:count], rest[-4:]
     blocks, per_p, extent, _ = p_refs[0].shape
     strip = acc_ref.shape[1]
     rows = (q_ref.shape[1] - 2 * SUB) // blocks
     per_q = rows // strip
-    copies = [pltpu.make_async_copy(p_refs[i], held.at[i], p_sems.at[i]) for i in range(SEATS)]
-    for copy in copies:
-        copy.start()
     for s in range(SEATS):
         wide_ids[s:s + 1] = q_ref[s, blocks * rows:, :].astype(jnp.int32)[:1]
     id_copy = pltpu.make_async_copy(wide_ids, ids, id_sem)
     id_copy.start()
-    acc_ref[...] = jnp.zeros_like(acc_ref)
+    if len(rest) == count + 4:
+        acc_ref[...] = jnp.zeros_like(acc_ref)
+    else:
+        acc_ref[...] = rest[count][...]
+    here = lax.axis_index(("pair", "core", "col"))
     id_copy.wait()
-    here = lax.axis_index(("pair", "core", "col"))
-    for i in range(SEATS):
-        copies[i].wait()
-        seat = origin(i // 2, i % 2, here, cols)
+    for i in range(count):
+        seat = origin(steps[i // 2], i % 2, here, cols)
         for f in range(blocks):
             left = q_ref[seat, f * rows:(f + 1) * rows]
             first = f * (per_p + per_q)
             for k in range(per_p):
-                product = jnp.dot(left, held[i, f, k], preferred_element_type=jnp.float32)
+                product = jnp.dot(left, p_refs[i][f, k], preferred_element_type=jnp.float32)
                 base = ids[seat, first + k] * tile_count
                 for l in range(per_q):
                     spot = base + ids[seat, first + per_p + l]
                     acc_ref[spot] += product[l * strip:(l + 1) * strip]
+
+
+def add_products(q_here, sets, steps, acc, tile_count, cols, strip):
+    per_p, extent = sets[0].shape[1:3]
+    operands = [q_here, *sets] + ([] if acc is None else [acc])
+    rows = q_here.shape[1] - 2 * SUB
+    return pl.pallas_call(
+        functools.partial(product_kernel, tile_count, cols, steps),
+        out_shape=jax.ShapeDtypeStruct((tile_count * tile_count, strip, extent), jnp.float32),
+        in_specs=[pl.BlockSpec(memory_space=pltpu.VMEM)] * len(operands),
+        out_specs=pl.BlockSpec(memory_space=pltpu.VMEM),
+        scratch_shapes=[
+            pltpu.VMEM((SEATS, extent), jnp.int32),
+            pltpu.SMEM((SEATS, extent), jnp.int32),
+            pltpu.SemaphoreType.DMA,
+        ],
+        input_output_aliases={} if acc is None else {len(operands) - 1: 0},
+        cost_estimate=pl.CostEstimate(
+            flops=2 * len(sets) * per_p * rows * extent * extent,
+            bytes_accessed=len(sets) * (1 << 20),
+            transcendentals=0,
+        ),
+        compiler_params=pltpu.CompilerParams(vmem_limit_bytes=24 << 20),
+        name="products",
+    )(*operands)
 
 
 def finish_kernel(x_ref, out_ref):
@@ -91,9 +116,8 @@
 def body(p_tiles, p_cols, q_tiles, q_cols):
     blocks, per_p, extent, _ = p_tiles.shape
     per_q = q_tiles.shape[1]
-    planes = lax.axis_size("plane")
-    pairs, cores, cols = lax.axis_size("pair"), lax.axis_size("core"), lax.axis_size("col")
-    tile_count = planes * pairs * cores
+    planes, cols = lax.axis_size("plane"), lax.axis_size("col")
+    tile_count = planes * SEATS // cols
     strip = extent // SEATS
     height = blocks * per_q * strip + 2 * SUB
     seat = ("pair", "core", "col")
@@ -102,10 +126,9 @@
         slice_kernel,
         out_shape=jax.ShapeDtypeStruct((SEATS, height, extent), q_tiles.dtype),
         in_specs=[pl.BlockSpec(memory_space=pltpu.SMEM)] * 2 + [pl.BlockSpec(memory_space=pltpu.VMEM)],
+        cost_estimate=pl.CostEstimate(flops=0, bytes_accessed=8 << 20, transcendentals=0),
         name="cut_columns",
     )(p_cols.T, q_cols, q_tiles)
-    q_here = lax.all_to_all(sliced, seat, split_axis=0, concat_axis=0, tiled=True)
-
     def along(values, step):
         hops = [(s, s ^ axes(s // cols % 2, cols)[step]) for s in range(SEATS)]
         return lax.ppermute(values, seat, hops)
@@ -114,27 +137,15 @@
         return lax.ppermute(values, seat, [(s, s ^ cols) for s in range(SEATS)])
 
     one, two, three = (along(p_tiles, step) for step in range(3))
-    one, two, three, _ = lax.optimization_barrier((one, two, three, sliced))
-    sets = [p_tiles, one, two, three, along(one, 1), along(two, 2), along(three, 0)]
-    sets.append(along(sets[4], 2))
-    sets = [each for kept in sets for each in (kept, across(kept))]
-
-    acc = pl.pallas_call(
-        functools.partial(product_kernel, tile_count, cols),
-        out_shape=jax.ShapeDtypeStruct((tile_count * tile_count, strip, extent), jnp.float32),
-        in_specs=[pl.BlockSpec(memory_space=pltpu.VMEM)]
-        + [pl.BlockSpec(memory_space=pl.ANY)] * SEATS,
-        scratch_shapes=[
-            pltpu.VMEM((SEATS, blocks, per_p, extent, extent), p_tiles.dtype),
-            pltpu.SemaphoreType.DMA((SEATS,)),
-            pltpu.VMEM((SEATS, extent), jnp.int32),
-            pltpu.SMEM((SEATS, extent), jnp.int32),
-            pltpu.SemaphoreType.DMA,
-        ],
-        compiler_params=pltpu.CompilerParams(vmem_limit_bytes=60 << 20),
-        name="products",
-    )(q_here, *sets)
-
+    one, two, three, sliced = lax.optimization_barrier((one, two, three, sliced))
+    q_here = lax.all_to_all(sliced, seat, split_axis=0, concat_axis=0, tiled=True)
+    four, five, six = along(one, 1), along(two, 2), along(three, 0)
+    seven = along(four, 2)
+    acc = None
+    sets = (p_tiles, one, two, three, four, five, six, seven)
+    for steps in ((0, 1, 2, 3), (4, 5, 6), (7,)):
+        batch = [each for step in steps for each in (sets[step], across(sets[step]))]
+        acc = add_products(q_here, batch, steps, acc, tile_count, cols, strip)
     every = ("plane",) + seat
     parts = acc.reshape(planes * SEATS, tile_count // cols, strip, extent)
     landed = lax.all_to_all(parts, every, split_axis=0, concat_axis=0, tiled=True)

time: 86.8 us -> 86.9 us (level)
  local copies, waits for them, and re-layouts: 2.48 us -> 7.59 us
  starting transfers between devices: 22.7 us -> 19.8 us
  waiting for transfers between devices: 17.7 us -> 16.5 us
  Pallas kernels: 13 us -> 12 us
    unnamed x32 -> x22, local copies, waits for them, and re-layouts: 2.48 us -> 7.59 us
    ppermute x8, starting transfers between devices: 7.35 us -> 5.2 us  [across(): return lax.ppermute(values, seat, [(s, s ^ cols) for s in range(SEATS)])]
    all_to_all x1, starting transfers between devices: 6.38 us -> 4.85 us  [body(): lax.all_to_all(sliced, seat, split_axis=0, concat_axis=0, tiled=True)]
    ppermute x7, waiting for transfers between devices: 17.6 us -> 16.4 us  [along(): return lax.ppermute(values, seat, hops)]
    pallas_call x1 -> x3, Pallas kernels: 8.49 us -> 7.49 us  [add_products(): pl.pallas_call(functools.partial(product_kernel, tile_count, cols, steps)...]
  transfers between devices with their start and end apart: 16 -> 16, of which waited for: 4 -> 4; matrix products, arithmetic and copies ran while one was open for 0% -> 0% of each run, Pallas kernels for 0% -> 10%
where the time goes in v5:
time: 86.9 us; the launch traced here: 86 us
  blocking collectives  30 us (35%)
  starting transfers between devices  19.8 us (23%)
  waiting for transfers between devices  16.5 us (19%)
  Pallas kernels  12 us (14%)
  local copies, waits for them, and re-layouts  7.59 us (9%)
    all_to_all x1, blocking collectives, body(): lax.all_to_all(parts, every, split_axis=0, concat_axis=0, tiled=True)  30 us
    ppermute x7, waiting for transfers between devices, along(): return lax.ppermute(values, seat, hops)  16.4 us
    ppermute x7, starting transfers between devices, along(): return lax.ppermute(values, seat, hops)  9.76 us
    unnamed x22, local copies, waits for them, and re-layouts  7.59 us
    pallas_call x3, Pallas kernels, add_products(): pl.pallas_call(functools.partial(product_kernel, tile_count, cols, steps)...  7.49 us
    ppermute x8, starting transfers between devices, across(): return lax.ppermute(values, seat, [(s, s ^ cols) for s in range(SEATS)])  5.2 us
    all_to_all x1, starting transfers between devices, body(): lax.all_to_all(sliced, seat, split_axis=0, concat_axis=0, tiled=True)  4.85 us
    pallas_call x1, Pallas kernels, body(): pl.pallas_call(slice_kernel, out_shape=jax.ShapeDtypeStruct((SEATS, heigh...  2.34 us
  transfers between devices with their start and end apart: 16, of which 4 were waited for; matrix products, arithmetic and copies ran while one was open for 0% of the time, Pallas kernels for 10%

profile of v5, /device:TPU:1, one launch (start us, length us, event | category | flops | bytes accessed | tf_op | source)
XLA Modules:
  0.0 86.0 jit_solution(2798280742759694859)
XLA Ops:
  0.0 2.0 %collective-permute-start = (bf16[4,2,128,128]{3,2,1,0:T(8,128)(2,1)}, bf16[4,2,128,128]{3,2,1,0:T(8,128)(2,1)S(1)}, u32[]{:S(2)}, u32[]{:S(2)}) collective-permute-start(bf16[4,2,128,128]{3,2,1,0:T(8,128)(2,1)} %rest_0_.1), channel_id=1, source_target_pairs={{0,1},{1,0},{2,6},{3,7},{4,5},{5,4},{6,2},{7,3},{8,9},{9,8},{10,14... | collective-permute-start | bytes 786440 | tf_op jit(solution)/shard_map/ppermute | solution.py:134
  2.0 1.3 %collective-permute-start.1 = (bf16[4,2,128,128]{3,2,1,0:T(8,128)(2,1)}, bf16[4,2,128,128]{3,2,1,0:T(8,128)(2,1)S(1)}, u32[]{:S(2)}, u32[]{:S(2)}) collective-permute-start(bf16[4,2,128,128]{3,2,1,0:T(8,128)(2,1)} %rest_0_.1), channel_id=1, source_target_pairs={{0,4},{1,5},{2,10},{3,11},{4,0},{5,1},{6,14},{7,15},{8,12},{9,13},... | collective-permute-start | bytes 786440 | tf_op jit(solution)/shard_map/ppermute | solution.py:134
  3.3 1.2 %collective-permute-start.2 = (bf16[4,2,128,128]{3,2,1,0:T(8,128)(2,1)}, bf16[4,2,128,128]{3,2,1,0:T(8,128)(2,1)}, u32[]{:S(2)}, u32[]{:S(2)}) collective-permute-start(bf16[4,2,128,128]{3,2,1,0:T(8,128)(2,1)} %rest_0_.1), channel_id=1, source_target_pairs={{0,8},{1,9},{2,3},{3,2},{4,12},{5,13},{6,7},{7,6},{8,0},{9,1},{10,... | collective-permute-start | bytes 786440 | tf_op jit(solution)/shard_map/ppermute | solution.py:134
  4.6 2.3 %cut_columns.1 = bf16[16,208,128]{2,1,0:T(8,128)(2,1)} custom-call(s32[2,4]{1,0:T(2,128)} %bitcast.5, s32[4,6]{1,0:T(4,128)} %q_ids.1, bf16[4,6,128,128]{3,2,1,0:T(8,128)(2,1)} %q_ref.1), custom_call_target="tpu_custom_call" | custom-call | bytes 8388608 | tf_op jit(solution)/shard_map/cut_columns/pallas_call | solution.py:125
  6.9 0.0 copy-start
  6.9 0.0 collective-permute-done.rest_2_
  6.9 0.8 collective-permute-done.1.rest_4_
  7.8 0.0 copy-start.1
  7.8 2.3 %collective-permute-done.2.rest_6_ = bf16[4,2,128,128]{3,2,1,0:T(8,128)(2,1)} collective-permute-done((bf16[4,2,128,128]{3,2,1,0:T(8,128)(2,1)}, bf16[4,2,128,128]{3,2,1,0:T(8,128)(2,1)}, u32[]{:S(2)}, u32[]{:S(2)}) %collective-permute-start.2) | collective-permute-done | bytes 262176 | tf_op jit(solution)/shard_map/ppermute | solution.py:134
  10.1 4.9 %all-to-all-start = ((bf16[16,208,128]{2,1,0:T(8,128)(2,1)}), bf16[16,208,128]{2,1,0:T(8,128)(2,1)S(1)}, u32[]{:S(2)}, u32[]{:S(2)}) async-start(bf16[16,208,128]{2,1,0:T(8,128)(2,1)} %cut_columns.1), calls=%async_computation | async-start | bytes 1703936 | tf_op jit(solution)/shard_map/all_to_all | solution.py:141
  15.0 0.0 copy-done
  15.0 0.2 collective-permute-start.11
  15.1 1.6 %collective-permute-start.3 = (bf16[4,2,128,128]{3,2,1,0:T(8,128)(2,1)S(1)}, bf16[4,2,128,128]{3,2,1,0:T(8,128)(2,1)S(1)}, u32[]{:S(2)}, u32[]{:S(2)}) collective-permute-start(bf16[4,2,128,128]{3,2,1,0:T(8,128)(2,1)S(1)} %collective-permute-done.rest_2_), channel_id=1, source_target_pairs={{0,4},{1,5},{2,10},{3,11},{4,0},{5,1},{6,14},{7,15},{8,12},{9,13},... | collective-permute-start | bytes 786440 | tf_op jit(solution)/shard_map/ppermute | solution.py:134
  16.8 0.4 collective-permute-start.12
  17.2 0.1 collective-permute-start.13
  17.3 1.2 %collective-permute-start.9 = (bf16[4,2,128,128]{3,2,1,0:T(8,128)(2,1)}, bf16[4,2,128,128]{3,2,1,0:T(8,128)(2,1)S(1)}, u32[]{:S(2)}, u32[]{:S(2)}) collective-permute-start(bf16[4,2,128,128]{3,2,1,0:T(8,128)(2,1)} %collective-permute-done.2.rest_6_), channel_id=1, source_target_pairs={{0,1},{1,0},{2,6},{3,7},{4,5},{5,4},{6,2},{7,3},{8,9},{9,8},{10,14... | collective-permute-start | bytes 786440 | tf_op jit(solution)/shard_map/ppermute | solution.py:134
  18.5 0.0 collective-permute-done.11.rest_1_
  18.5 0.0 copy-done.1
  18.5 0.0 copy-start.3
  18.5 0.7 copy-done.3
  19.2 1.2 %collective-permute-start.7 = (bf16[4,2,128,128]{3,2,1,0:T(8,128)(2,1)S(1)}, bf16[4,2,128,128]{3,2,1,0:T(8,128)(2,1)S(1)}, u32[]{:S(2)}, u32[]{:S(2)}) collective-permute-start(bf16[4,2,128,128]{3,2,1,0:T(8,128)(2,1)S(1)} %collective-permute-done.1.rest_4_), channel_id=1, source_target_pairs={{0,8},{1,9},{2,3},{3,2},{4,12},{5,13},{6,7},{7,6},{8,0},{9,1},{10,... | collective-permute-start | bytes 786440 | tf_op jit(solution)/shard_map/ppermute | solution.py:134
  20.4 12.4 %collective-permute-done.3.rest_0_ = bf16[4,2,128,128]{3,2,1,0:T(8,128)(2,1)S(1)} collective-permute-done((bf16[4,2,128,128]{3,2,1,0:T(8,128)(2,1)S(1)}, bf16[4,2,128,128]{3,2,1,0:T(8,128)(2,1)S(1)}, u32[]{:S(2)}, u32[]{:S(2)}) %collective-permute-start.3) | collective-permute-done | bytes 262176 | tf_op jit(solution)/shard_map/ppermute | solution.py:134
  32.8 1.2 %collective-permute-start.4 = (bf16[4,2,128,128]{3,2,1,0:T(8,128)(2,1)S(1)}, bf16[4,2,128,128]{3,2,1,0:T(8,128)(2,1)S(1)}, u32[]{:S(2)}, u32[]{:S(2)}) collective-permute-start(bf16[4,2,128,128]{3,2,1,0:T(8,128)(2,1)S(1)} %collective-permute-done.3.rest_0_), channel_id=1, source_target_pairs={{0,8},{1,9},{2,3},{3,2},{4,12},{5,13},{6,7},{7,6},{8,0},{9,1},{10,... | collective-permute-start | bytes 786440 | tf_op jit(solution)/shard_map/ppermute | solution.py:134
  33.9 0.0 collective-permute-done.12.rest_3_
  33.9 0.0 copy-start.5
  33.9 0.7 copy-done.5
  34.6 1.5 %collective-permute-start.14 = (bf16[4,2,128,128]{3,2,1,0:T(8,128)(2,1)}, bf16[4,2,128,128]{3,2,1,0:T(8,128)(2,1)S(1)}, u32[]{:S(2)}, u32[]{:S(2)}) collective-permute-start(bf16[4,2,128,128]{3,2,1,0:T(8,128)(2,1)} %collective-permute-done.2.rest_6_), channel_id=1, source_target_pairs={{0,2},{1,3},{2,0},{3,1},{4,6},{5,7},{6,4},{7,5},{8,10},{9,11},{10,... | collective-permute-start | bytes 786440 | tf_op jit(solution)/shard_map/ppermute | solution.py:137
  36.1 0.0 collective-permute-done.13.rest_5_
  36.1 0.0 copy-start.7
  36.1 0.7 copy-done.7
  36.8 0.0 collective-permute-start.6
  36.8 0.0 collective-permute-done.9.rest_4_
  36.8 0.5 collective-permute-start.10
  37.3 0.0 collective-permute-done.7.rest_2_
  37.3 0.1 collective-permute-start.8
  37.4 0.9 %collective-permute-done.4.rest_0_ = bf16[4,2,128,128]{3,2,1,0:T(8,128)(2,1)S(1)} collective-permute-done((bf16[4,2,128,128]{3,2,1,0:T(8,128)(2,1)S(1)}, bf16[4,2,128,128]{3,2,1,0:T(8,128)(2,1)S(1)}, u32[]{:S(2)}, u32[]{:S(2)}) %collective-permute-start.4) | collective-permute-done | bytes 262176 | tf_op jit(solution)/shard_map/ppermute | solution.py:134
  38.3 2.5 %collective-permute-start.5 = (bf16[4,2,128,128]{3,2,1,0:T(8,128)(2,1)S(1)}, bf16[4,2,128,128]{3,2,1,0:T(8,128)(2,1)S(1)}, u32[]{:S(2)}, u32[]{:S(2)}) collective-permute-start(bf16[4,2,128,128]{3,2,1,0:T(8,128)(2,1)S(1)} %collective-permute-done.4.rest_0_), channel_id=1, source_target_pairs={{0,2},{1,3},{2,0},{3,1},{4,6},{5,7},{6,4},{7,5},{8,10},{9,11},{10,... | collective-permute-start | bytes 786440 | tf_op jit(solution)/shard_map/ppermute | solution.py:137
  40.8 0.0 collective-permute-done.14.rest_7_
  40.8 0.0 copy-start.9
  40.8 0.7 copy-done.9
  41.5 0.0 all-to-all-done.q_ref
  41.5 0.0 copy-start.2
  41.5 0.9 %copy-done.2 = bf16[4,2,128,128]{3,2,1,0:T(8,128)(2,1)S(1)} copy-done((bf16[4,2,128,128]{3,2,1,0:T(8,128)(2,1)S(1)}, bf16[4,2,128,128]{3,2,1,0:T(8,128)(2,1)}, u32[]{:S(2)}) %copy-start.2) | copy-done | bytes 262168
  42.4 0.0 copy-start.4
  42.4 0.9 %copy-done.4 = bf16[4,2,128,128]{3,2,1,0:T(8,128)(2,1)S(1)} copy-done((bf16[4,2,128,128]{3,2,1,0:T(8,128)(2,1)S(1)}, bf16[4,2,128,128]{3,2,1,0:T(8,128)(2,1)}, u32[]{:S(2)}) %copy-start.4) | copy-done | bytes 262168
  43.4 0.0 copy-start.6
  43.4 0.9 %copy-done.6 = bf16[4,2,128,128]{3,2,1,0:T(8,128)(2,1)S(1)} copy-done((bf16[4,2,128,128]{3,2,1,0:T(8,128)(2,1)S(1)}, bf16[4,2,128,128]{3,2,1,0:T(8,128)(2,1)}, u32[]{:S(2)}) %copy-start.6) | copy-done | bytes 262168
  44.3 0.0 copy-start.8
  44.3 0.9 %copy-done.8 = bf16[4,2,128,128]{3,2,1,0:T(8,128)(2,1)S(1)} copy-done((bf16[4,2,128,128]{3,2,1,0:T(8,128)(2,1)S(1)}, bf16[4,2,128,128]{3,2,1,0:T(8,128)(2,1)}, u32[]{:S(2)}) %copy-start.8) | copy-done | bytes 262168
  45.3 0.0 copy-start.10
  45.3 0.9 %copy-done.10 = bf16[4,2,128,128]{3,2,1,0:T(8,128)(2,1)S(1)} copy-done((bf16[4,2,128,128]{3,2,1,0:T(8,128)(2,1)S(1)}, bf16[4,2,128,128]{3,2,1,0:T(8,128)(2,1)}, u32[]{:S(2)}) %copy-start.10) | copy-done | bytes 262168
  46.2 3.9 %products.3.rest_6_ = f32[256,8,128]{2,1,0:T(8,128)S(1)} custom-call(bf16[16,208,128]{2,1,0:T(8,128)(2,1)S(1)} %all-to-all-done.q_ref, bf16[4,2,128,128]{3,2,1,0:T(8,128)(2,1)S(1)} %copy-done, bf16[4,2,128,128]{3,2,1,0:T(8,128)(2,1)S(1)} %copy-done.4, bf16[4,2,128,128]{3,2,1,0:T(8,128)(2,1)S(1)} %collective-permute-done.rest_2_, ...), custom_call_target="tpu_custom_call" | custom-call | flops 100663296 | bytes 8388608 | tf_op jit(solution)/shard_map/products/pallas_call | solution.py:86
  50.1 0.0 collective-permute-done.6.rest_1_
  50.1 0.0 collective-permute-done.10.rest_5_
  50.1 0.0 collective-permute-done.8.rest_3_
  50.1 2.3 %products.4.rest_2_ = f32[256,8,128]{2,1,0:T(8,128)S(1)} custom-call(bf16[16,208,128]{2,1,0:T(8,128)(2,1)S(1)} %all-to-all-done.q_ref, bf16[4,2,128,128]{3,2,1,0:T(8,128)(2,1)S(1)} %collective-permute-done.3.rest_0_, bf16[4,2,128,128]{3,2,1,0:T(8,128)(2,1)S(1)} %collective-permute-done.6.rest_1_, ...), custom_call_target="tpu_custom_call", output_to_operand_aliasing={{}: (7, {})} | custom-call | flops 75497472 | bytes 6291456 | tf_op jit(solution)/shard_map/products/pallas_call | solution.py:86
  52.5 0.0 collective-permute-done.5.rest_1_
  52.5 1.3 %products.5 = f32[256,8,128]{2,1,0:T(8,128)S(1)} custom-call(bf16[16,208,128]{2,1,0:T(8,128)(2,1)S(1)} %all-to-all-done.q_ref, bf16[4,2,128,128]{3,2,1,0:T(8,128)(2,1)S(1)} %collective-permute-done.4.rest_0_, bf16[4,2,128,128]{3,2,1,0:T(8,128)(2,1)S(1)} %collective-permute-done.5.rest_1_, ...), custom_call_target="tpu_custom_call", output_to_operand_aliasing={{}: (3, {})} | custom-call | flops 25165824 | bytes 2097152 | tf_op jit(solution)/shard_map/products/pallas_call | solution.py:86
  53.8 30.0 %all_to_all.10 = f32[32,8,8,128]{3,2,1,0:T(8,128)} all-to-all(f32[32,8,8,128]{3,2,1,0:T(8,128)S(1)} %bitcast.3), channel_id=1, replica_groups=mesh['plane'=2,'pair'=4,'core'=2,'col'=2] {'plane','pair','core','col'}, dimensions={0} | all-to-all | bytes 2097152 | tf_op jit(solution)/shard_map/all_to_all | solution.py:151
  83.8 2.2 %turn.1 = f32[128,1024]{1,0:T(8,128)} custom-call(f32[2,16,8,8,128]{4,3,2,1,0:T(8,128)} %bitcast.4), custom_call_target="tpu_custom_call" | custom-call | tf_op jit(solution)/shard_map/turn/pallas_call | solution.py:152
Async XLA Ops:
  0.0 6.9 %collective-permute-start = (bf16[4,2,128,128]{3,2,1,0:T(8,128)(2,1)}, bf16[4,2,128,128]{3,2,1,0:T(8,128)(2,1)S(1)}, u32[]{:S(2)}, u32[]{:S(2)}) collective-permute-start(bf16[4,2,128,128]{3,2,1,0:T(8,128)(2,1)} %rest_0_.1), channel_id=1, source_target_pairs={{0,1},{1,0},{2,6},{3,7},{4,5},{5,4},{6,2},{7,3},{8,9},{9,8},{10,14... | collective-permute-start | bytes 786440 | tf_op jit(solution)/shard_map/ppermute | solution.py:134
  2.0 5.7 %collective-permute-start.1 = (bf16[4,2,128,128]{3,2,1,0:T(8,128)(2,1)}, bf16[4,2,128,128]{3,2,1,0:T(8,128)(2,1)S(1)}, u32[]{:S(2)}, u32[]{:S(2)}) collective-permute-start(bf16[4,2,128,128]{3,2,1,0:T(8,128)(2,1)} %rest_0_.1), channel_id=1, source_target_pairs={{0,4},{1,5},{2,10},{3,11},{4,0},{5,1},{6,14},{7,15},{8,12},{9,13},... | collective-permute-start | bytes 786440 | tf_op jit(solution)/shard_map/ppermute | solution.py:134
  3.3 6.8 %collective-permute-start.2 = (bf16[4,2,128,128]{3,2,1,0:T(8,128)(2,1)}, bf16[4,2,128,128]{3,2,1,0:T(8,128)(2,1)}, u32[]{:S(2)}, u32[]{:S(2)}) collective-permute-start(bf16[4,2,128,128]{3,2,1,0:T(8,128)(2,1)} %rest_0_.1), channel_id=1, source_target_pairs={{0,8},{1,9},{2,3},{3,2},{4,12},{5,13},{6,7},{7,6},{8,0},{9,1},{10,... | collective-permute-start | bytes 786440 | tf_op jit(solution)/shard_map/ppermute | solution.py:134
  6.9 8.0 %copy-start = (bf16[4,2,128,128]{3,2,1,0:T(8,128)(2,1)S(1)}, bf16[4,2,128,128]{3,2,1,0:T(8,128)(2,1)}, u32[]{:S(2)}) copy-start(bf16[4,2,128,128]{3,2,1,0:T(8,128)(2,1)} %rest_0_.1) | copy-start | bytes 786436
  7.8 10.7 %copy-start.1 = (bf16[4,2,128,128]{3,2,1,0:T(8,128)(2,1)}, bf16[4,2,128,128]{3,2,1,0:T(8,128)(2,1)S(1)}, u32[]{:S(2)}) copy-start(bf16[4,2,128,128]{3,2,1,0:T(8,128)(2,1)S(1)} %collective-permute-done.1.rest_4_) | copy-start | bytes 786436
  10.1 31.4 %all-to-all-start = ((bf16[16,208,128]{2,1,0:T(8,128)(2,1)}), bf16[16,208,128]{2,1,0:T(8,128)(2,1)S(1)}, u32[]{:S(2)}, u32[]{:S(2)}) async-start(bf16[16,208,128]{2,1,0:T(8,128)(2,1)} %cut_columns.1), calls=%async_computation | async-start | bytes 1703936 | tf_op jit(solution)/shard_map/all_to_all | solution.py:141
  15.0 3.5 %collective-permute-start.11 = (bf16[4,2,128,128]{3,2,1,0:T(8,128)(2,1)S(1)}, bf16[4,2,128,128]{3,2,1,0:T(8,128)(2,1)S(1)}, u32[]{:S(2)}, u32[]{:S(2)}) collective-permute-start(bf16[4,2,128,128]{3,2,1,0:T(8,128)(2,1)S(1)} %copy-done), channel_id=1, source_target_pairs={{0,2},{1,3},{2,0},{3,1},{4,6},{5,7},{6,4},{7,5},{8,10},{9,11},{10,... | collective-permute-start | bytes 786440 | tf_op jit(solution)/shard_map/ppermute | solution.py:137
  15.1 17.6 %collective-permute-start.3 = (bf16[4,2,128,128]{3,2,1,0:T(8,128)(2,1)S(1)}, bf16[4,2,128,128]{3,2,1,0:T(8,128)(2,1)S(1)}, u32[]{:S(2)}, u32[]{:S(2)}) collective-permute-start(bf16[4,2,128,128]{3,2,1,0:T(8,128)(2,1)S(1)} %collective-permute-done.rest_2_), channel_id=1, source_target_pairs={{0,4},{1,5},{2,10},{3,11},{4,0},{5,1},{6,14},{7,15},{8,12},{9,13},... | collective-permute-start | bytes 786440 | tf_op jit(solution)/shard_map/ppermute | solution.py:134
  16.8 17.2 %collective-permute-start.12 = (bf16[4,2,128,128]{3,2,1,0:T(8,128)(2,1)S(1)}, bf16[4,2,128,128]{3,2,1,0:T(8,128)(2,1)S(1)}, u32[]{:S(2)}, u32[]{:S(2)}) collective-permute-start(bf16[4,2,128,128]{3,2,1,0:T(8,128)(2,1)S(1)} %collective-permute-done.rest_2_), channel_id=1, source_target_pairs={{0,2},{1,3},{2,0},{3,1},{4,6},{5,7},{6,4},{7,5},{8,10},{9,11},{10,... | collective-permute-start | bytes 786440 | tf_op jit(solution)/shard_map/ppermute | solution.py:137
  17.2 18.9 %collective-permute-start.13 = (bf16[4,2,128,128]{3,2,1,0:T(8,128)(2,1)S(1)}, bf16[4,2,128,128]{3,2,1,0:T(8,128)(2,1)S(1)}, u32[]{:S(2)}, u32[]{:S(2)}) collective-permute-start(bf16[4,2,128,128]{3,2,1,0:T(8,128)(2,1)S(1)} %collective-permute-done.1.rest_4_), channel_id=1, source_target_pairs={{0,2},{1,3},{2,0},{3,1},{4,6},{5,7},{6,4},{7,5},{8,10},{9,11},{10,... | collective-permute-start | bytes 786440 | tf_op jit(solution)/shard_map/ppermute | solution.py:137
  17.3 19.5 %collective-permute-start.9 = (bf16[4,2,128,128]{3,2,1,0:T(8,128)(2,1)}, bf16[4,2,128,128]{3,2,1,0:T(8,128)(2,1)S(1)}, u32[]{:S(2)}, u32[]{:S(2)}) collective-permute-start(bf16[4,2,128,128]{3,2,1,0:T(8,128)(2,1)} %collective-permute-done.2.rest_6_), channel_id=1, source_target_pairs={{0,1},{1,0},{2,6},{3,7},{4,5},{5,4},{6,2},{7,3},{8,9},{9,8},{10,14... | collective-permute-start | bytes 786440 | tf_op jit(solution)/shard_map/ppermute | solution.py:134
  18.5 0.7 copy-start.3
  19.2 18.2 %collective-permute-start.7 = (bf16[4,2,128,128]{3,2,1,0:T(8,128)(2,1)S(1)}, bf16[4,2,128,128]{3,2,1,0:T(8,128)(2,1)S(1)}, u32[]{:S(2)}, u32[]{:S(2)}) collective-permute-start(bf16[4,2,128,128]{3,2,1,0:T(8,128)(2,1)S(1)} %collective-permute-done.1.rest_4_), channel_id=1, source_target_pairs={{0,8},{1,9},{2,3},{3,2},{4,12},{5,13},{6,7},{7,6},{8,0},{9,1},{10,... | collective-permute-start | bytes 786440 | tf_op jit(solution)/shard_map/ppermute | solution.py:134
  32.8 5.5 %collective-permute-start.4 = (bf16[4,2,128,128]{3,2,1,0:T(8,128)(2,1)S(1)}, bf16[4,2,128,128]{3,2,1,0:T(8,128)(2,1)S(1)}, u32[]{:S(2)}, u32[]{:S(2)}) collective-permute-start(bf16[4,2,128,128]{3,2,1,0:T(8,128)(2,1)S(1)} %collective-permute-done.3.rest_0_), channel_id=1, source_target_pairs={{0,8},{1,9},{2,3},{3,2},{4,12},{5,13},{6,7},{7,6},{8,0},{9,1},{10,... | collective-permute-start | bytes 786440 | tf_op jit(solution)/shard_map/ppermute | solution.py:134
  33.9 0.7 copy-start.5
  34.6 6.1 %collective-permute-start.14 = (bf16[4,2,128,128]{3,2,1,0:T(8,128)(2,1)}, bf16[4,2,128,128]{3,2,1,0:T(8,128)(2,1)S(1)}, u32[]{:S(2)}, u32[]{:S(2)}) collective-permute-start(bf16[4,2,128,128]{3,2,1,0:T(8,128)(2,1)} %collective-permute-done.2.rest_6_), channel_id=1, source_target_pairs={{0,2},{1,3},{2,0},{3,1},{4,6},{5,7},{6,4},{7,5},{8,10},{9,11},{10,... | collective-permute-start | bytes 786440 | tf_op jit(solution)/shard_map/ppermute | solution.py:137
  36.1 0.7 copy-start.7
  36.8 13.3 %collective-permute-start.6 = (bf16[4,2,128,128]{3,2,1,0:T(8,128)(2,1)S(1)}, bf16[4,2,128,128]{3,2,1,0:T(8,128)(2,1)S(1)}, u32[]{:S(2)}, u32[]{:S(2)}) collective-permute-start(bf16[4,2,128,128]{3,2,1,0:T(8,128)(2,1)S(1)} %collective-permute-done.3.rest_0_), channel_id=1, source_target_pairs={{0,2},{1,3},{2,0},{3,1},{4,6},{5,7},{6,4},{7,5},{8,10},{9,11},{10,... | collective-permute-start | bytes 786440 | tf_op jit(solution)/shard_map/ppermute | solution.py:137
  36.8 13.3 %collective-permute-start.10 = (bf16[4,2,128,128]{3,2,1,0:T(8,128)(2,1)S(1)}, bf16[4,2,128,128]{3,2,1,0:T(8,128)(2,1)S(1)}, u32[]{:S(2)}, u32[]{:S(2)}) collective-permute-start(bf16[4,2,128,128]{3,2,1,0:T(8,128)(2,1)S(1)} %collective-permute-done.9.rest_4_), channel_id=1, source_target_pairs={{0,2},{1,3},{2,0},{3,1},{4,6},{5,7},{6,4},{7,5},{8,10},{9,11},{10,... | collective-permute-start | bytes 786440 | tf_op jit(solution)/shard_map/ppermute | solution.py:137
  37.3 12.8 %collective-permute-start.8 = (bf16[4,2,128,128]{3,2,1,0:T(8,128)(2,1)S(1)}, bf16[4,2,128,128]{3,2,1,0:T(8,128)(2,1)S(1)}, u32[]{:S(2)}, u32[]{:S(2)}) collective-permute-start(bf16[4,2,128,128]{3,2,1,0:T(8,128)(2,1)S(1)} %collective-permute-done.7.rest_2_), channel_id=1, source_target_pairs={{0,2},{1,3},{2,0},{3,1},{4,6},{5,7},{6,4},{7,5},{8,10},{9,11},{10,... | collective-permute-start | bytes 786440 | tf_op jit(solution)/shard_map/ppermute | solution.py:137
  38.3 14.2 %collective-permute-start.5 = (bf16[4,2,128,128]{3,2,1,0:T(8,128)(2,1)S(1)}, bf16[4,2,128,128]{3,2,1,0:T(8,128)(2,1)S(1)}, u32[]{:S(2)}, u32[]{:S(2)}) collective-permute-start(bf16[4,2,128,128]{3,2,1,0:T(8,128)(2,1)S(1)} %collective-permute-done.4.rest_0_), channel_id=1, source_target_pairs={{0,2},{1,3},{2,0},{3,1},{4,6},{5,7},{6,4},{7,5},{8,10},{9,11},{10,... | collective-permute-start | bytes 786440 | tf_op jit(solution)/shard_map/ppermute | solution.py:137
  40.8 0.7 copy-start.9
  41.5 1.0 %copy-start.2 = (bf16[4,2,128,128]{3,2,1,0:T(8,128)(2,1)S(1)}, bf16[4,2,128,128]{3,2,1,0:T(8,128)(2,1)}, u32[]{:S(2)}) copy-start(bf16[4,2,128,128]{3,2,1,0:T(8,128)(2,1)} %copy-done.1) | copy-start | bytes 786436
  42.4 0.9 %copy-start.4 = (bf16[4,2,128,128]{3,2,1,0:T(8,128)(2,1)S(1)}, bf16[4,2,128,128]{3,2,1,0:T(8,128)(2,1)}, u32[]{:S(2)}) copy-start(bf16[4,2,128,128]{3,2,1,0:T(8,128)(2,1)} %copy-done.3) | copy-start | bytes 786436
  43.4 0.9 %copy-start.6 = (bf16[4,2,128,128]{3,2,1,0:T(8,128)(2,1)S(1)}, bf16[4,2,128,128]{3,2,1,0:T(8,128)(2,1)}, u32[]{:S(2)}) copy-start(bf16[4,2,128,128]{3,2,1,0:T(8,128)(2,1)} %copy-done.5) | copy-start | bytes 786436
  44.3 0.9 %copy-start.8 = (bf16[4,2,128,128]{3,2,1,0:T(8,128)(2,1)S(1)}, bf16[4,2,128,128]{3,2,1,0:T(8,128)(2,1)}, u32[]{:S(2)}) copy-start(bf16[4,2,128,128]{3,2,1,0:T(8,128)(2,1)} %copy-done.7) | copy-start | bytes 786436
  45.3 0.9 %copy-start.10 = (bf16[4,2,128,128]{3,2,1,0:T(8,128)(2,1)S(1)}, bf16[4,2,128,128]{3,2,1,0:T(8,128)(2,1)}, u32[]{:S(2)}) copy-start(bf16[4,2,128,128]{3,2,1,0:T(8,128)(2,1)} %copy-done.9) | copy-start | bytes 786436

commit v6 on v5

--- a/solution.py
+++ b/solution.py
@@ -49,8 +49,8 @@
         out_ref[j, blocks * rows:] = ids
 
 
-def product_kernel(tile_count, cols, steps, q_ref, *rest):
-    count = 2 * len(steps)
+def product_kernel(tile_count, cols, routes, q_ref, *rest):
+    count = len(routes)
     p_refs, (acc_ref, wide_ids, ids, id_sem) = rest[:count], rest[-4:]
     blocks, per_p, extent, _ = p_refs[0].shape
     strip = acc_ref.shape[1]
@@ -67,7 +67,7 @@
     here = lax.axis_index(("pair", "core", "col"))
     id_copy.wait()
     for i in range(count):
-        seat = origin(steps[i // 2], i % 2, here, cols)
+        seat = origin(*routes[i], here, cols)
         for f in range(blocks):
             left = q_ref[seat, f * rows:(f + 1) * rows]
             first = f * (per_p + per_q)
@@ -79,12 +79,12 @@
                     acc_ref[spot] += product[l * strip:(l + 1) * strip]
 
 
-def add_products(q_here, sets, steps, acc, tile_count, cols, strip):
+def add_products(q_here, sets, routes, acc, tile_count, cols, strip):
     per_p, extent = sets[0].shape[1:3]
     operands = [q_here, *sets] + ([] if acc is None else [acc])
     rows = q_here.shape[1] - 2 * SUB
     return pl.pallas_call(
-        functools.partial(product_kernel, tile_count, cols, steps),
+        functools.partial(product_kernel, tile_count, cols, routes),
         out_shape=jax.ShapeDtypeStruct((tile_count * tile_count, strip, extent), jnp.float32),
         in_specs=[pl.BlockSpec(memory_space=pltpu.VMEM)] * len(operands),
         out_specs=pl.BlockSpec(memory_space=pltpu.VMEM),
@@ -99,7 +99,7 @@
             bytes_accessed=len(sets) * (1 << 20),
             transcendentals=0,
         ),
-        compiler_params=pltpu.CompilerParams(vmem_limit_bytes=24 << 20),
+        compiler_params=pltpu.CompilerParams(vmem_limit_bytes=16 << 20),
         name="products",
     )(*operands)
 
@@ -127,6 +127,7 @@
         out_shape=jax.ShapeDtypeStruct((SEATS, height, extent), q_tiles.dtype),
         in_specs=[pl.BlockSpec(memory_space=pltpu.SMEM)] * 2 + [pl.BlockSpec(memory_space=pltpu.VMEM)],
         cost_estimate=pl.CostEstimate(flops=0, bytes_accessed=8 << 20, transcendentals=0),
+        compiler_params=pltpu.CompilerParams(vmem_limit_bytes=8 << 20),
         name="cut_columns",
     )(p_cols.T, q_cols, q_tiles)
     def along(values, step):
@@ -136,22 +137,33 @@
     def across(values):
         return lax.ppermute(values, seat, [(s, s ^ cols) for s in range(SEATS)])
 
-    one, two, three = (along(p_tiles, step) for step in range(3))
-    one, two, three, sliced = lax.optimization_barrier((one, two, three, sliced))
+    def opposite(values):
+        return lax.ppermute(values, seat, [(s, s ^ (SEATS - 1 - cols)) for s in range(SEATS)])
+
+    def add(acc, sets, routes):
+        return add_products(q_here, sets, routes, acc, tile_count, cols, strip)
+
+    beside = across(p_tiles)
+    first = [along(p_tiles, step) for step in range(3)] + [opposite(p_tiles)]
+    sliced, beside = lax.optimization_barrier((sliced, beside))
     q_here = lax.all_to_all(sliced, seat, split_axis=0, concat_axis=0, tiled=True)
-    four, five, six = along(one, 1), along(two, 2), along(three, 0)
-    seven = along(four, 2)
-    acc = None
-    sets = (p_tiles, one, two, three, four, five, six, seven)
-    for steps in ((0, 1, 2, 3), (4, 5, 6), (7,)):
-        batch = [each for step in steps for each in (sets[step], across(sets[step]))]
-        acc = add_products(q_here, batch, steps, acc, tile_count, cols, strip)
+    second = [along(first[step], (step + 1) % 3) for step in range(3)]
+    sets = [p_tiles, beside] + first + [across(each) for each in first]
+    steps = (1, 2, 3, 7)
+    acc = add(
+        None, sets, [(0, 0), (0, 1)] + [(step, 0) for step in steps] + [(step, 1) for step in steps]
+    )
+    *second, acc = lax.optimization_barrier((*second, acc))
+    crossed = [across(each) for each in second]
+    acc = add(acc, second, [(4, 0), (5, 0), (6, 0)])
+    acc = add(acc, crossed, [(4, 1), (5, 1), (6, 1)])
     every = ("plane",) + seat
     parts = acc.reshape(planes * SEATS, tile_count // cols, strip, extent)
     landed = lax.all_to_all(parts, every, split_axis=0, concat_axis=0, tiled=True)
     return pl.pallas_call(
         finish_kernel,
         out_shape=jax.ShapeDtypeStruct((extent, tile_count // cols * extent), jnp.float32),
+        compiler_params=pltpu.CompilerParams(vmem_limit_bytes=16 << 20),
         name="turn",
     )(landed.reshape(planes, SEATS, tile_count // cols, strip, extent))
 

time: 86.9 us -> 83.3 us (0.959)
  waiting for transfers between devices: 16.5 us -> 13.2 us
  Pallas kernels: 12 us -> 9.29 us
  starting transfers between devices: 19.8 us -> 22.2 us
    ppermute x8, starting transfers between devices: 5.2 us -> 10.4 us  [across(): return lax.ppermute(values, seat, [(s, s ^ cols) for s in range(SEATS)])]
    ppermute x7 -> x6, starting transfers between devices: 9.76 us -> 5.43 us  [along(): return lax.ppermute(values, seat, hops)]
    ppermute x7 -> x6, waiting for transfers between devices: 16.4 us -> 13.2 us  [along(): return lax.ppermute(values, seat, hops)]
    all_to_all x1, starting transfers between devices: 4.85 us -> 6.39 us  [body(): lax.all_to_all(sliced, seat, split_axis=0, concat_axis=0, tiled=True)]
    pallas_call x1, Pallas kernels: 2.22 us -> 1 us  [body(): pl.pallas_call(finish_kernel, out_shape=jax.ShapeDtypeStruct((extent, til...]
    pallas_call x3, Pallas kernels: 7.49 us -> 6.52 us  [add_products(): pl.pallas_call(functools.partial(product_kernel, tile_count, cols, routes...]
    unnamed x22 -> x20, local copies, waits for them, and re-layouts: 7.59 us -> 7.42 us
  transfers between devices with their start and end apart: 16 -> 16, of which waited for: 4 -> 1; matrix products, arithmetic and copies ran while one was open for 0% -> 0% of each run, Pallas kernels for 10% -> 8%
where the time goes in v6:
time: 83.3 us; the launch traced here: 82.5 us
  blocking collectives  30.2 us (36%)
  starting transfers between devices  22.2 us (27%)
  waiting for transfers between devices  13.2 us (16%)
  Pallas kernels  9.29 us (11%)
  local copies, waits for them, and re-layouts  7.42 us (9%)
    all_to_all x1, blocking collectives, body(): lax.all_to_all(parts, every, split_axis=0, concat_axis=0, tiled=True)  30.2 us
    ppermute x6, waiting for transfers between devices, along(): return lax.ppermute(values, seat, hops)  13.2 us
    ppermute x8, starting transfers between devices, across(): return lax.ppermute(values, seat, [(s, s ^ cols) for s in range(SEATS)])  10.4 us
    unnamed x20, local copies, waits for them, and re-layouts  7.42 us
    pallas_call x3, Pallas kernels, add_products(): pl.pallas_call(functools.partial(product_kernel, tile_count, cols, routes...  6.52 us
    all_to_all x1, starting transfers between devices, body(): lax.all_to_all(sliced, seat, split_axis=0, concat_axis=0, tiled=True)  6.39 us
    ppermute x6, starting transfers between devices, along(): return lax.ppermute(values, seat, hops)  5.43 us
    pallas_call x1, Pallas kernels, body(): pl.pallas_call(slice_kernel, out_shape=jax.ShapeDtypeStruct((SEATS, heigh...  1.77 us
  transfers between devices with their start and end apart: 16, of which 1 were waited for; matrix products, arithmetic and copies ran while one was open for 0% of the time, Pallas kernels for 8%

profile of v6, /device:TPU:1, one launch (start us, length us, event | category | flops | bytes accessed | tf_op | source)
XLA Modules:
  0.0 82.5 jit_solution(14912322663869049570)
XLA Ops:
  0.0 0.0 copy-start.9
  0.0 0.1 collective-permute-start
  0.1 0.6 copy-done.9
  0.7 0.0 copy-start
  0.7 1.1 %copy-done = bf16[4,6,128,128]{3,2,1,0:T(8,128)(2,1)S(1)} copy-done((bf16[4,6,128,128]{3,2,1,0:T(8,128)(2,1)S(1)}, bf16[4,6,128,128]{3,2,1,0:T(8,128)(2,1)}, u32[]{:S(2)}) %copy-start) | copy-done | bytes 786456
  1.8 0.0 copy-start.8
  1.8 0.7 copy-done.8
  2.5 1.8 %cut_columns.1 = bf16[16,208,128]{2,1,0:T(8,128)(2,1)} custom-call(s32[2,4]{1,0:T(2,128)S(1)} %bitcast.5, s32[4,6]{1,0:T(4,128)S(1)} %copy-done.8, bf16[4,6,128,128]{3,2,1,0:T(8,128)(2,1)S(1)} %copy-done), custom_call_target="tpu_custom_call" | custom-call | bytes 8388608 | tf_op jit(solution)/shard_map/cut_columns/pallas_call | solution.py:125
  4.3 0.0 copy-start.1
  4.3 0.0 collective-permute-done.rest_1_
  4.3 6.4 %all-to-all-start = ((bf16[16,208,128]{2,1,0:T(8,128)(2,1)}), bf16[16,208,128]{2,1,0:T(8,128)(2,1)S(1)}, u32[]{:S(2)}, u32[]{:S(2)}) async-start(bf16[16,208,128]{2,1,0:T(8,128)(2,1)} %cut_columns.1), calls=%async_computation | async-start | bytes 1703936 | tf_op jit(solution)/shard_map/all_to_all | solution.py:149
  10.7 0.0 copy-done.1
  10.7 1.4 %collective-permute-start.5 = (bf16[4,2,128,128]{3,2,1,0:T(8,128)(2,1)S(1)}, bf16[4,2,128,128]{3,2,1,0:T(8,128)(2,1)S(1)}, u32[]{:S(2)}, u32[]{:S(2)}) collective-permute-start(bf16[4,2,128,128]{3,2,1,0:T(8,128)(2,1)S(1)} %copy-done.1), channel_id=1, source_target_pairs={{0,8},{1,9},{2,3},{3,2},{4,12},{5,13},{6,7},{7,6},{8,0},{9,1},{10,... | collective-permute-start | bytes 786440 | tf_op jit(solution)/shard_map/ppermute | solution.py:135
  12.1 1.2 %collective-permute-start.1 = (bf16[4,2,128,128]{3,2,1,0:T(8,128)(2,1)S(1)}, bf16[4,2,128,128]{3,2,1,0:T(8,128)(2,1)S(1)}, u32[]{:S(2)}, u32[]{:S(2)}) collective-permute-start(bf16[4,2,128,128]{3,2,1,0:T(8,128)(2,1)S(1)} %copy-done.1), channel_id=1, source_target_pairs={{0,1},{1,0},{2,6},{3,7},{4,5},{5,4},{6,2},{7,3},{8,9},{9,8},{10,14... | collective-permute-start | bytes 786440 | tf_op jit(solution)/shard_map/ppermute | solution.py:135
  13.3 1.2 %collective-permute-start.3 = (bf16[4,2,128,128]{3,2,1,0:T(8,128)(2,1)S(1)}, bf16[4,2,128,128]{3,2,1,0:T(8,128)(2,1)S(1)}, u32[]{:S(2)}, u32[]{:S(2)}) collective-permute-start(bf16[4,2,128,128]{3,2,1,0:T(8,128)(2,1)S(1)} %copy-done.1), channel_id=1, source_target_pairs={{0,4},{1,5},{2,10},{3,11},{4,0},{5,1},{6,14},{7,15},{8,12},{9,13},... | collective-permute-start | bytes 786440 | tf_op jit(solution)/shard_map/ppermute | solution.py:135
  14.5 0.1 collective-permute-start.7
  14.6 13.2 %collective-permute-done.5.rest_4_ = bf16[4,2,128,128]{3,2,1,0:T(8,128)(2,1)S(1)} collective-permute-done((bf16[4,2,128,128]{3,2,1,0:T(8,128)(2,1)S(1)}, bf16[4,2,128,128]{3,2,1,0:T(8,128)(2,1)S(1)}, u32[]{:S(2)}, u32[]{:S(2)}) %collective-permute-start.5) | collective-permute-done | bytes 262176 | tf_op jit(solution)/shard_map/ppermute | solution.py:135
  27.8 2.0 %collective-permute-start.10 = (bf16[4,2,128,128]{3,2,1,0:T(8,128)(2,1)S(1)}, bf16[4,2,128,128]{3,2,1,0:T(8,128)(2,1)S(1)}, u32[]{:S(2)}, u32[]{:S(2)}) collective-permute-start(bf16[4,2,128,128]{3,2,1,0:T(8,128)(2,1)S(1)} %collective-permute-done.5.rest_4_), channel_id=1, source_target_pairs={{0,2},{1,3},{2,0},{3,1},{4,6},{5,7},{6,4},{7,5},{8,10},{9,11},{10,... | collective-permute-start | bytes 786440 | tf_op jit(solution)/shard_map/ppermute | solution.py:138
  29.8 0.0 collective-permute-done.1.rest_2_
  29.8 0.0 collective-permute-start.8
  29.8 0.0 collective-permute-done.3.rest_3_
  29.8 5.9 %collective-permute-start.9 = (bf16[4,2,128,128]{3,2,1,0:T(8,128)(2,1)S(1)}, bf16[4,2,128,128]{3,2,1,0:T(8,128)(2,1)S(1)}, u32[]{:S(2)}, u32[]{:S(2)}) collective-permute-start(bf16[4,2,128,128]{3,2,1,0:T(8,128)(2,1)S(1)} %collective-permute-done.3.rest_3_), channel_id=1, source_target_pairs={{0,2},{1,3},{2,0},{3,1},{4,6},{5,7},{6,4},{7,5},{8,10},{9,11},{10,... | collective-permute-start | bytes 786440 | tf_op jit(solution)/shard_map/ppermute | solution.py:138
  35.7 0.0 collective-permute-done.7.rest_5_
  35.7 0.4 collective-permute-start.11
  36.2 0.4 collective-permute-start.2
  36.6 0.0 collective-permute-done.10.rest_8_
  36.6 1.1 %collective-permute-start.4 = (bf16[4,2,128,128]{3,2,1,0:T(8,128)(2,1)S(1)}, bf16[4,2,128,128]{3,2,1,0:T(8,128)(2,1)S(1)}, u32[]{:S(2)}, u32[]{:S(2)}) collective-permute-start(bf16[4,2,128,128]{3,2,1,0:T(8,128)(2,1)S(1)} %collective-permute-done.3.rest_3_), channel_id=1, source_target_pairs={{0,8},{1,9},{2,3},{3,2},{4,12},{5,13},{6,7},{7,6},{8,0},{9,1},{10,... | collective-permute-start | bytes 786440 | tf_op jit(solution)/shard_map/ppermute | solution.py:135
  37.7 0.0 collective-permute-done.8.rest_6_
  37.7 0.0 copy-start.2
  37.7 0.7 copy-done.2
  38.4 0.1 collective-permute-start.6
  38.5 0.0 collective-permute-done.9.rest_7_
  38.5 0.0 copy-start.4
  38.5 0.7 copy-done.4
  39.2 0.0 collective-permute-done.11.rest_9_
  39.2 0.0 copy-start.6
  39.2 0.7 copy-done.6
  39.9 0.0 all-to-all-done.q_ref
  39.9 0.0 copy-start.3
  39.9 0.9 %copy-done.3 = bf16[4,2,128,128]{3,2,1,0:T(8,128)(2,1)S(1)} copy-done((bf16[4,2,128,128]{3,2,1,0:T(8,128)(2,1)S(1)}, bf16[4,2,128,128]{3,2,1,0:T(8,128)(2,1)}, u32[]{:S(2)}) %copy-start.3) | copy-done | bytes 262168
  40.9 0.0 copy-start.5
  40.9 0.9 %copy-done.5 = bf16[4,2,128,128]{3,2,1,0:T(8,128)(2,1)S(1)} copy-done((bf16[4,2,128,128]{3,2,1,0:T(8,128)(2,1)S(1)}, bf16[4,2,128,128]{3,2,1,0:T(8,128)(2,1)}, u32[]{:S(2)}) %copy-start.5) | copy-done | bytes 262168
  41.8 0.0 copy-start.7
  41.8 0.9 %copy-done.7 = bf16[4,2,128,128]{3,2,1,0:T(8,128)(2,1)S(1)} copy-done((bf16[4,2,128,128]{3,2,1,0:T(8,128)(2,1)S(1)}, bf16[4,2,128,128]{3,2,1,0:T(8,128)(2,1)}, u32[]{:S(2)}) %copy-start.7) | copy-done | bytes 262168
  42.8 3.4 %products.3.rest_3_ = f32[256,8,128]{2,1,0:T(8,128)S(1)} custom-call(bf16[16,208,128]{2,1,0:T(8,128)(2,1)S(1)} %all-to-all-done.q_ref, bf16[4,2,128,128]{3,2,1,0:T(8,128)(2,1)S(1)} %copy-done.1, bf16[4,2,128,128]{3,2,1,0:T(8,128)(2,1)S(1)} %collective-permute-done.rest_1_, bf16[4,2,128,128]{3,2,1,0:T(8,128)(2,1)S(1)} %collective-permute-done.1.rest_2_, ...), custom_call_target="tpu_custom_call" | custom-call | flops 125829120 | bytes 10485760 | tf_op jit(solution)/shard_map/products/pallas_call | solution.py:86
  46.2 0.0 collective-permute-done.2.rest_0_
  46.2 0.0 collective-permute-done.4.rest_1_
  46.2 0.0 collective-permute-done.6.rest_2_
  46.3 1.4 %collective-permute-start.12 = (bf16[4,2,128,128]{3,2,1,0:T(8,128)(2,1)S(1)}, bf16[4,2,128,128]{3,2,1,0:T(8,128)(2,1)S(1)}, u32[]{:S(2)}, u32[]{:S(2)}) collective-permute-start(bf16[4,2,128,128]{3,2,1,0:T(8,128)(2,1)S(1)} %collective-permute-done.2.rest_0_), channel_id=1, source_target_pairs={{0,2},{1,3},{2,0},{3,1},{4,6},{5,7},{6,4},{7,5},{8,10},{9,11},{10,... | collective-permute-start | bytes 786440 | tf_op jit(solution)/shard_map/ppermute | solution.py:138
  47.7 0.1 collective-permute-start.13
  47.8 0.4 collective-permute-start.14
  48.2 1.5 %products.4.rest_3_ = f32[256,8,128]{2,1,0:T(8,128)S(1)} custom-call(bf16[16,208,128]{2,1,0:T(8,128)(2,1)S(1)} %all-to-all-done.q_ref, bf16[4,2,128,128]{3,2,1,0:T(8,128)(2,1)S(1)} %collective-permute-done.2.rest_0_, bf16[4,2,128,128]{3,2,1,0:T(8,128)(2,1)S(1)} %collective-permute-done.4.rest_1_, ...), custom_call_target="tpu_custom_call", output_to_operand_aliasing={{}: (4, {})} | custom-call | flops 37748736 | bytes 3145728 | tf_op jit(solution)/shard_map/products/pallas_call | solution.py:86
  49.7 0.0 collective-permute-done.12.rest_0_
  49.7 0.0 collective-permute-done.13.rest_1_
  49.7 0.0 collective-permute-done.14.rest_2_
  49.8 1.5 %products.5 = f32[256,8,128]{2,1,0:T(8,128)S(1)} custom-call(bf16[16,208,128]{2,1,0:T(8,128)(2,1)S(1)} %all-to-all-done.q_ref, bf16[4,2,128,128]{3,2,1,0:T(8,128)(2,1)S(1)} %collective-permute-done.12.rest_0_, bf16[4,2,128,128]{3,2,1,0:T(8,128)(2,1)S(1)} %collective-permute-done.13.rest_1_, ...), custom_call_target="tpu_custom_call", output_to_operand_aliasing={{}: (4, {})} | custom-call | flops 37748736 | bytes 3145728 | tf_op jit(solution)/shard_map/products/pallas_call | solution.py:86
  51.3 30.2 %all_to_all.10 = f32[32,8,8,128]{3,2,1,0:T(8,128)S(1)} all-to-all(f32[32,8,8,128]{3,2,1,0:T(8,128)S(1)} %bitcast.3), channel_id=1, replica_groups=mesh['plane'=2,'pair'=4,'core'=2,'col'=2] {'plane','pair','core','col'}, dimensions={0} | all-to-all | bytes 2097152 | tf_op jit(solution)/shard_map/all_to_all | solution.py:162
  81.5 1.0 %turn.1 = f32[128,1024]{1,0:T(8,128)} custom-call(f32[2,16,8,8,128]{4,3,2,1,0:T(8,128)S(1)} %bitcast.4), custom_call_target="tpu_custom_call" | custom-call | tf_op jit(solution)/shard_map/turn/pallas_call | solution.py:163
Async XLA Ops:
  0.0 0.7 copy-start.9
  0.0 4.3 %collective-permute-start = (bf16[4,2,128,128]{3,2,1,0:T(8,128)(2,1)}, bf16[4,2,128,128]{3,2,1,0:T(8,128)(2,1)S(1)}, u32[]{:S(2)}, u32[]{:S(2)}) collective-permute-start(bf16[4,2,128,128]{3,2,1,0:T(8,128)(2,1)} %rest_0_.1), channel_id=1, source_target_pairs={{0,2},{1,3},{2,0},{3,1},{4,6},{5,7},{6,4},{7,5},{8,10},{9,11},{10,... | collective-permute-start | bytes 786440 | tf_op jit(solution)/shard_map/ppermute | solution.py:138
  0.7 1.1 %copy-start = (bf16[4,6,128,128]{3,2,1,0:T(8,128)(2,1)S(1)}, bf16[4,6,128,128]{3,2,1,0:T(8,128)(2,1)}, u32[]{:S(2)}) copy-start(bf16[4,6,128,128]{3,2,1,0:T(8,128)(2,1)} %q_ref.1) | copy-start | bytes 2359300
  1.8 0.7 copy-start.8
  4.3 6.4 %copy-start.1 = (bf16[4,2,128,128]{3,2,1,0:T(8,128)(2,1)S(1)}, bf16[4,2,128,128]{3,2,1,0:T(8,128)(2,1)}, u32[]{:S(2)}) copy-start(bf16[4,2,128,128]{3,2,1,0:T(8,128)(2,1)} %rest_0_.1) | copy-start | bytes 786436
  4.3 35.6 %all-to-all-start = ((bf16[16,208,128]{2,1,0:T(8,128)(2,1)}), bf16[16,208,128]{2,1,0:T(8,128)(2,1)S(1)}, u32[]{:S(2)}, u32[]{:S(2)}) async-start(bf16[16,208,128]{2,1,0:T(8,128)(2,1)} %cut_columns.1), calls=%async_computation | async-start | bytes 1703936 | tf_op jit(solution)/shard_map/all_to_all | solution.py:149
  10.7 17.1 %collective-permute-start.5 = (bf16[4,2,128,128]{3,2,1,0:T(8,128)(2,1)S(1)}, bf16[4,2,128,128]{3,2,1,0:T(8,128)(2,1)S(1)}, u32[]{:S(2)}, u32[]{:S(2)}) collective-permute-start(bf16[4,2,128,128]{3,2,1,0:T(8,128)(2,1)S(1)} %copy-done.1), channel_id=1, source_target_pairs={{0,8},{1,9},{2,3},{3,2},{4,12},{5,13},{6,7},{7,6},{8,0},{9,1},{10,... | collective-permute-start | bytes 786440 | tf_op jit(solution)/shard_map/ppermute | solution.py:135
  12.1 17.7 %collective-permute-start.1 = (bf16[4,2,128,128]{3,2,1,0:T(8,128)(2,1)S(1)}, bf16[4,2,128,128]{3,2,1,0:T(8,128)(2,1)S(1)}, u32[]{:S(2)}, u32[]{:S(2)}) collective-permute-start(bf16[4,2,128,128]{3,2,1,0:T(8,128)(2,1)S(1)} %copy-done.1), channel_id=1, source_target_pairs={{0,1},{1,0},{2,6},{3,7},{4,5},{5,4},{6,2},{7,3},{8,9},{9,8},{10,14... | collective-permute-start | bytes 786440 | tf_op jit(solution)/shard_map/ppermute | solution.py:135
  13.3 16.5 %collective-permute-start.3 = (bf16[4,2,128,128]{3,2,1,0:T(8,128)(2,1)S(1)}, bf16[4,2,128,128]{3,2,1,0:T(8,128)(2,1)S(1)}, u32[]{:S(2)}, u32[]{:S(2)}) collective-permute-start(bf16[4,2,128,128]{3,2,1,0:T(8,128)(2,1)S(1)} %copy-done.1), channel_id=1, source_target_pairs={{0,4},{1,5},{2,10},{3,11},{4,0},{5,1},{6,14},{7,15},{8,12},{9,13},... | collective-permute-start | bytes 786440 | tf_op jit(solution)/shard_map/ppermute | solution.py:135
  14.5 21.2 %collective-permute-start.7 = (bf16[4,2,128,128]{3,2,1,0:T(8,128)(2,1)S(1)}, bf16[4,2,128,128]{3,2,1,0:T(8,128)(2,1)S(1)}, u32[]{:S(2)}, u32[]{:S(2)}) collective-permute-start(bf16[4,2,128,128]{3,2,1,0:T(8,128)(2,1)S(1)} %copy-done.1), channel_id=1, source_target_pairs={{0,13},{1,12},{2,15},{3,14},{4,9},{5,8},{6,11},{7,10},{8,5},{9,4},... | collective-permute-start | bytes 786440 | tf_op jit(solution)/shard_map/ppermute | solution.py:141
  27.8 8.8 %collective-permute-start.10 = (bf16[4,2,128,128]{3,2,1,0:T(8,128)(2,1)S(1)}, bf16[4,2,128,128]{3,2,1,0:T(8,128)(2,1)S(1)}, u32[]{:S(2)}, u32[]{:S(2)}) collective-permute-start(bf16[4,2,128,128]{3,2,1,0:T(8,128)(2,1)S(1)} %collective-permute-done.5.rest_4_), channel_id=1, source_target_pairs={{0,2},{1,3},{2,0},{3,1},{4,6},{5,7},{6,4},{7,5},{8,10},{9,11},{10,... | collective-permute-start | bytes 786440 | tf_op jit(solution)/shard_map/ppermute | solution.py:138
  29.8 7.9 %collective-permute-start.8 = (bf16[4,2,128,128]{3,2,1,0:T(8,128)(2,1)S(1)}, bf16[4,2,128,128]{3,2,1,0:T(8,128)(2,1)S(1)}, u32[]{:S(2)}, u32[]{:S(2)}) collective-permute-start(bf16[4,2,128,128]{3,2,1,0:T(8,128)(2,1)S(1)} %collective-permute-done.1.rest_2_), channel_id=1, source_target_pairs={{0,2},{1,3},{2,0},{3,1},{4,6},{5,7},{6,4},{7,5},{8,10},{9,11},{10,... | collective-permute-start | bytes 786440 | tf_op jit(solution)/shard_map/ppermute | solution.py:138
  29.8 8.7 %collective-permute-start.9 = (bf16[4,2,128,128]{3,2,1,0:T(8,128)(2,1)S(1)}, bf16[4,2,128,128]{3,2,1,0:T(8,128)(2,1)S(1)}, u32[]{:S(2)}, u32[]{:S(2)}) collective-permute-start(bf16[4,2,128,128]{3,2,1,0:T(8,128)(2,1)S(1)} %collective-permute-done.3.rest_3_), channel_id=1, source_target_pairs={{0,2},{1,3},{2,0},{3,1},{4,6},{5,7},{6,4},{7,5},{8,10},{9,11},{10,... | collective-permute-start | bytes 786440 | tf_op jit(solution)/shard_map/ppermute | solution.py:138
  35.7 3.5 %collective-permute-start.11 = (bf16[4,2,128,128]{3,2,1,0:T(8,128)(2,1)S(1)}, bf16[4,2,128,128]{3,2,1,0:T(8,128)(2,1)S(1)}, u32[]{:S(2)}, u32[]{:S(2)}) collective-permute-start(bf16[4,2,128,128]{3,2,1,0:T(8,128)(2,1)S(1)} %collective-permute-done.7.rest_5_), channel_id=1, source_target_pairs={{0,2},{1,3},{2,0},{3,1},{4,6},{5,7},{6,4},{7,5},{8,10},{9,11},{10,... | collective-permute-start | bytes 786440 | tf_op jit(solution)/shard_map/ppermute | solution.py:138
  36.2 10.1 %collective-permute-start.2 = (bf16[4,2,128,128]{3,2,1,0:T(8,128)(2,1)S(1)}, bf16[4,2,128,128]{3,2,1,0:T(8,128)(2,1)S(1)}, u32[]{:S(2)}, u32[]{:S(2)}) collective-permute-start(bf16[4,2,128,128]{3,2,1,0:T(8,128)(2,1)S(1)} %collective-permute-done.1.rest_2_), channel_id=1, source_target_pairs={{0,4},{1,5},{2,10},{3,11},{4,0},{5,1},{6,14},{7,15},{8,12},{9,13},... | collective-permute-start | bytes 786440 | tf_op jit(solution)/shard_map/ppermute | solution.py:135
  36.6 9.7 %collective-permute-start.4 = (bf16[4,2,128,128]{3,2,1,0:T(8,128)(2,1)S(1)}, bf16[4,2,128,128]{3,2,1,0:T(8,128)(2,1)S(1)}, u32[]{:S(2)}, u32[]{:S(2)}) collective-permute-start(bf16[4,2,128,128]{3,2,1,0:T(8,128)(2,1)S(1)} %collective-permute-done.3.rest_3_), channel_id=1, source_target_pairs={{0,8},{1,9},{2,3},{3,2},{4,12},{5,13},{6,7},{7,6},{8,0},{9,1},{10,... | collective-permute-start | bytes 786440 | tf_op jit(solution)/shard_map/ppermute | solution.py:135
  37.7 0.7 copy-start.2
  38.4 7.9 %collective-permute-start.6 = (bf16[4,2,128,128]{3,2,1,0:T(8,128)(2,1)S(1)}, bf16[4,2,128,128]{3,2,1,0:T(8,128)(2,1)S(1)}, u32[]{:S(2)}, u32[]{:S(2)}) collective-permute-start(bf16[4,2,128,128]{3,2,1,0:T(8,128)(2,1)S(1)} %collective-permute-done.5.rest_4_), channel_id=1, source_target_pairs={{0,1},{1,0},{2,6},{3,7},{4,5},{5,4},{6,2},{7,3},{8,9},{9,8},{10,14... | collective-permute-start | bytes 786440 | tf_op jit(solution)/shard_map/ppermute | solution.py:135
  38.5 0.7 copy-start.4
  39.2 0.7 copy-start.6
  39.9 1.0 %copy-start.3 = (bf16[4,2,128,128]{3,2,1,0:T(8,128)(2,1)S(1)}, bf16[4,2,128,128]{3,2,1,0:T(8,128)(2,1)}, u32[]{:S(2)}) copy-start(bf16[4,2,128,128]{3,2,1,0:T(8,128)(2,1)} %copy-done.2) | copy-start | bytes 786436
  40.9 0.9 %copy-start.5 = (bf16[4,2,128,128]{3,2,1,0:T(8,128)(2,1)S(1)}, bf16[4,2,128,128]{3,2,1,0:T(8,128)(2,1)}, u32[]{:S(2)}) copy-start(bf16[4,2,128,128]{3,2,1,0:T(8,128)(2,1)} %copy-done.4) | copy-start | bytes 786436
  41.8 0.9 %copy-start.7 = (bf16[4,2,128,128]{3,2,1,0:T(8,128)(2,1)S(1)}, bf16[4,2,128,128]{3,2,1,0:T(8,128)(2,1)}, u32[]{:S(2)}) copy-start(bf16[4,2,128,128]{3,2,1,0:T(8,128)(2,1)} %copy-done.6) | copy-start | bytes 786436
  46.3 3.5 %collective-permute-start.12 = (bf16[4,2,128,128]{3,2,1,0:T(8,128)(2,1)S(1)}, bf16[4,2,128,128]{3,2,1,0:T(8,128)(2,1)S(1)}, u32[]{:S(2)}, u32[]{:S(2)}) collective-permute-start(bf16[4,2,128,128]{3,2,1,0:T(8,128)(2,1)S(1)} %collective-permute-done.2.rest_0_), channel_id=1, source_target_pairs={{0,2},{1,3},{2,0},{3,1},{4,6},{5,7},{6,4},{7,5},{8,10},{9,11},{10,... | collective-permute-start | bytes 786440 | tf_op jit(solution)/shard_map/ppermute | solution.py:138
  47.7 2.1 %collective-permute-start.13 = (bf16[4,2,128,128]{3,2,1,0:T(8,128)(2,1)S(1)}, bf16[4,2,128,128]{3,2,1,0:T(8,128)(2,1)S(1)}, u32[]{:S(2)}, u32[]{:S(2)}) collective-permute-start(bf16[4,2,128,128]{3,2,1,0:T(8,128)(2,1)S(1)} %collective-permute-done.4.rest_1_), channel_id=1, source_target_pairs={{0,2},{1,3},{2,0},{3,1},{4,6},{5,7},{6,4},{7,5},{8,10},{9,11},{10,... | collective-permute-start | bytes 786440 | tf_op jit(solution)/shard_map/ppermute | solution.py:138
  47.8 2.0 %collective-permute-start.14 = (bf16[4,2,128,128]{3,2,1,0:T(8,128)(2,1)S(1)}, bf16[4,2,128,128]{3,2,1,0:T(8,128)(2,1)S(1)}, u32[]{:S(2)}, u32[]{:S(2)}) collective-permute-start(bf16[4,2,128,128]{3,2,1,0:T(8,128)(2,1)S(1)} %collective-permute-done.6.rest_2_), channel_id=1, source_target_pairs={{0,2},{1,3},{2,0},{3,1},{4,6},{5,7},{6,4},{7,5},{8,10},{9,11},{10,... | collective-permute-start | bytes 786440 | tf_op jit(solution)/shard_map/ppermute | solution.py:138

commit v7 on v6

--- a/solution.py
+++ b/solution.py
@@ -51,28 +51,32 @@
 
 def product_kernel(tile_count, cols, routes, q_ref, *rest):
     count = len(routes)
-    p_refs, (acc_ref, wide_ids, ids, id_sem) = rest[:count], rest[-4:]
+    p_refs, (acc_ref, held, p_sems, wide_ids, ids, id_sem) = rest[:count], rest[-6:]
     blocks, per_p, extent, _ = p_refs[0].shape
     strip = acc_ref.shape[1]
     rows = (q_ref.shape[1] - 2 * SUB) // blocks
     per_q = rows // strip
+    copies = [pltpu.make_async_copy(p_refs[i], held.at[i], p_sems.at[i]) for i in range(count)]
+    for copy in copies:
+        copy.start()
     for s in range(SEATS):
         wide_ids[s:s + 1] = q_ref[s, blocks * rows:, :].astype(jnp.int32)[:1]
     id_copy = pltpu.make_async_copy(wide_ids, ids, id_sem)
     id_copy.start()
-    if len(rest) == count + 4:
+    if len(rest) == count + 6:
         acc_ref[...] = jnp.zeros_like(acc_ref)
     else:
         acc_ref[...] = rest[count][...]
     here = lax.axis_index(("pair", "core", "col"))
     id_copy.wait()
     for i in range(count):
+        copies[i].wait()
         seat = origin(*routes[i], here, cols)
         for f in range(blocks):
             left = q_ref[seat, f * rows:(f + 1) * rows]
             first = f * (per_p + per_q)
             for k in range(per_p):
-                product = jnp.dot(left, p_refs[i][f, k], preferred_element_type=jnp.float32)
+                product = jnp.dot(left, held[i, f, k], preferred_element_type=jnp.float32)
                 base = ids[seat, first + k] * tile_count
                 for l in range(per_q):
                     spot = base + ids[seat, first + per_p + l]
@@ -81,14 +85,18 @@
 
 def add_products(q_here, sets, routes, acc, tile_count, cols, strip):
     per_p, extent = sets[0].shape[1:3]
-    operands = [q_here, *sets] + ([] if acc is None else [acc])
+    more = [] if acc is None else [acc]
+    operands = [q_here, *sets, *more]
+    in_vmem = pl.BlockSpec(memory_space=pltpu.VMEM)
     rows = q_here.shape[1] - 2 * SUB
     return pl.pallas_call(
         functools.partial(product_kernel, tile_count, cols, routes),
         out_shape=jax.ShapeDtypeStruct((tile_count * tile_count, strip, extent), jnp.float32),
-        in_specs=[pl.BlockSpec(memory_space=pltpu.VMEM)] * len(operands),
+        in_specs=[in_vmem] + [pl.BlockSpec(memory_space=pl.ANY)] * len(sets) + [in_vmem] * len(more),
         out_specs=pl.BlockSpec(memory_space=pltpu.VMEM),
         scratch_shapes=[
+            pltpu.VMEM((len(sets),) + sets[0].shape, sets[0].dtype),
+            pltpu.SemaphoreType.DMA((len(sets),)),
             pltpu.VMEM((SEATS, extent), jnp.int32),
             pltpu.SMEM((SEATS, extent), jnp.int32),
             pltpu.SemaphoreType.DMA,
@@ -127,9 +135,9 @@
         out_shape=jax.ShapeDtypeStruct((SEATS, height, extent), q_tiles.dtype),
         in_specs=[pl.BlockSpec(memory_space=pltpu.SMEM)] * 2 + [pl.BlockSpec(memory_space=pltpu.VMEM)],
         cost_estimate=pl.CostEstimate(flops=0, bytes_accessed=8 << 20, transcendentals=0),
-        compiler_params=pltpu.CompilerParams(vmem_limit_bytes=8 << 20),
         name="cut_columns",
     )(p_cols.T, q_cols, q_tiles)
+
     def along(values, step):
         hops = [(s, s ^ axes(s // cols % 2, cols)[step]) for s in range(SEATS)]
         return lax.ppermute(values, seat, hops)
@@ -145,15 +153,15 @@
 
     beside = across(p_tiles)
     first = [along(p_tiles, step) for step in range(3)] + [opposite(p_tiles)]
-    sliced, beside = lax.optimization_barrier((sliced, beside))
+    sliced, *first[:3] = lax.optimization_barrier((sliced, *first[:3]))
     q_here = lax.all_to_all(sliced, seat, split_axis=0, concat_axis=0, tiled=True)
     second = [along(first[step], (step + 1) % 3) for step in range(3)]
+    first = lax.optimization_barrier(first)
     sets = [p_tiles, beside] + first + [across(each) for each in first]
     steps = (1, 2, 3, 7)
     acc = add(
         None, sets, [(0, 0), (0, 1)] + [(step, 0) for step in steps] + [(step, 1) for step in steps]
     )
-    *second, acc = lax.optimization_barrier((*second, acc))
     crossed = [across(each) for each in second]
     acc = add(acc, second, [(4, 0), (5, 0), (6, 0)])
     acc = add(acc, crossed, [(4, 1), (5, 1), (6, 1)])

time: 83.3 us -> 92.4 us (1.11)
  waiting for transfers between devices: 13.2 us -> 20.1 us
  local copies, waits for them, and re-layouts: 7.42 us -> 9.97 us
  Pallas kernels: 9.29 us -> 11.1 us
  starting transfers between devices: 22.2 us -> 20.7 us
    ppermute x1, waiting for transfers between devices: 0.01 us -> 15 us  [opposite(): lax.ppermute(values, seat, [(s, s ^ SEATS - 1 - cols) for s in range(SEAT...]
    ppermute x6, waiting for transfers between devices: 13.2 us -> 5.09 us  [along(): return lax.ppermute(values, seat, hops)]
    ppermute x8, starting transfers between devices: 10.4 us -> 6.3 us  [across(): return lax.ppermute(values, seat, [(s, s ^ cols) for s in range(SEATS)])]
    ppermute x1, starting transfers between devices: 0.07 us -> 3.32 us  [opposite(): lax.ppermute(values, seat, [(s, s ^ SEATS - 1 - cols) for s in range(SEAT...]
    unnamed x20 -> x26, local copies, waits for them, and re-layouts: 7.42 us -> 9.97 us
    all_to_all x1, starting transfers between devices: 6.39 us -> 3.99 us  [body(): lax.all_to_all(sliced, seat, split_axis=0, concat_axis=0, tiled=True)]
    ppermute x6, starting transfers between devices: 5.43 us -> 7.05 us  [along(): return lax.ppermute(values, seat, hops)]
    pallas_call x3, Pallas kernels: 6.52 us -> 7.73 us  [add_products(): pl.pallas_call(functools.partial(product_kernel, tile_count, cols, routes...]
  transfers between devices with their start and end apart: 16 -> 16, of which waited for: 1 -> 4; matrix products, arithmetic and copies ran while one was open for 0% -> 0% of each run, Pallas kernels for 8% -> 9%
where the time goes in v7:
time: 92.4 us; the launch traced here: 91.6 us
  blocking collectives  29.7 us (32%)
  starting transfers between devices  20.7 us (22%)
  waiting for transfers between devices  20.1 us (22%)
  Pallas kernels  11.1 us (12%)
  local copies, waits for them, and re-layouts  9.97 us (11%)
    all_to_all x1, blocking collectives, body(): lax.all_to_all(parts, every, split_axis=0, concat_axis=0, tiled=True)  29.7 us
    ppermute x1, waiting for transfers between devices, opposite(): lax.ppermute(values, seat, [(s, s ^ SEATS - 1 - cols) for s in range(SEAT...  15 us
    unnamed x26, local copies, waits for them, and re-layouts  9.97 us
    pallas_call x3, Pallas kernels, add_products(): pl.pallas_call(functools.partial(product_kernel, tile_count, cols, routes...  7.73 us
    ppermute x6, starting transfers between devices, along(): return lax.ppermute(values, seat, hops)  7.05 us
    ppermute x8, starting transfers between devices, across(): return lax.ppermute(values, seat, [(s, s ^ cols) for s in range(SEATS)])  6.3 us
    ppermute x6, waiting for transfers between devices, along(): return lax.ppermute(values, seat, hops)  5.09 us
    all_to_all x1, starting transfers between devices, body(): lax.all_to_all(sliced, seat, split_axis=0, concat_axis=0, tiled=True)  3.99 us
  transfers between devices with their start and end apart: 16, of which 4 were waited for; matrix products, arithmetic and copies ran while one was open for 0% of the time, Pallas kernels for 9%

profile of v7, /device:TPU:1, one launch (start us, length us, event | category | flops | bytes accessed | tf_op | source)
XLA Modules:
  0.0 91.6 jit_solution(11531210432332261860)
XLA Ops:
  0.0 2.1 %collective-permute-start.2 = (bf16[4,2,128,128]{3,2,1,0:T(8,128)(2,1)}, bf16[4,2,128,128]{3,2,1,0:T(8,128)(2,1)S(1)}, u32[]{:S(2)}, u32[]{:S(2)}) collective-permute-start(bf16[4,2,128,128]{3,2,1,0:T(8,128)(2,1)} %rest_0_.1), channel_id=1, source_target_pairs={{0,8},{1,9},{2,3},{3,2},{4,12},{5,13},{6,7},{7,6},{8,0},{9,1},{10,... | collective-permute-start | bytes 786440 | tf_op jit(solution)/shard_map/ppermute | solution.py:143
  2.1 1.3 %collective-permute-start.1 = (bf16[4,2,128,128]{3,2,1,0:T(8,128)(2,1)}, bf16[4,2,128,128]{3,2,1,0:T(8,128)(2,1)S(1)}, u32[]{:S(2)}, u32[]{:S(2)}) collective-permute-start(bf16[4,2,128,128]{3,2,1,0:T(8,128)(2,1)} %rest_0_.1), channel_id=1, source_target_pairs={{0,4},{1,5},{2,10},{3,11},{4,0},{5,1},{6,14},{7,15},{8,12},{9,13},... | collective-permute-start | bytes 786440 | tf_op jit(solution)/shard_map/ppermute | solution.py:143
  3.4 1.2 %collective-permute-start = (bf16[4,2,128,128]{3,2,1,0:T(8,128)(2,1)}, bf16[4,2,128,128]{3,2,1,0:T(8,128)(2,1)S(1)}, u32[]{:S(2)}, u32[]{:S(2)}) collective-permute-start(bf16[4,2,128,128]{3,2,1,0:T(8,128)(2,1)} %rest_0_.1), channel_id=1, source_target_pairs={{0,1},{1,0},{2,6},{3,7},{4,5},{5,4},{6,2},{7,3},{8,9},{9,8},{10,14... | collective-permute-start | bytes 786440 | tf_op jit(solution)/shard_map/ppermute | solution.py:143
  4.6 2.3 %cut_columns.1 = bf16[16,208,128]{2,1,0:T(8,128)(2,1)} custom-call(s32[2,4]{1,0:T(2,128)} %bitcast.5, s32[4,6]{1,0:T(4,128)} %q_ids.1, bf16[4,6,128,128]{3,2,1,0:T(8,128)(2,1)} %q_ref.1), custom_call_target="tpu_custom_call" | custom-call | bytes 8388608 | tf_op jit(solution)/shard_map/cut_columns/pallas_call | solution.py:133
  6.9 0.0 copy-start
  6.9 0.0 collective-permute-done.2.rest_4_
  6.9 3.1 %collective-permute-done.1.rest_3_ = bf16[4,2,128,128]{3,2,1,0:T(8,128)(2,1)S(1)} collective-permute-done((bf16[4,2,128,128]{3,2,1,0:T(8,128)(2,1)}, bf16[4,2,128,128]{3,2,1,0:T(8,128)(2,1)S(1)}, u32[]{:S(2)}, u32[]{:S(2)}) %collective-permute-start.1) | collective-permute-done | bytes 262176 | tf_op jit(solution)/shard_map/ppermute | solution.py:143
  10.1 1.7 %collective-permute-done.rest_2_ = bf16[4,2,128,128]{3,2,1,0:T(8,128)(2,1)S(1)} collective-permute-done((bf16[4,2,128,128]{3,2,1,0:T(8,128)(2,1)}, bf16[4,2,128,128]{3,2,1,0:T(8,128)(2,1)S(1)}, u32[]{:S(2)}, u32[]{:S(2)}) %collective-permute-start) | collective-permute-done | bytes 262176 | tf_op jit(solution)/shard_map/ppermute | solution.py:143
  11.7 4.0 %all-to-all-start = ((bf16[16,208,128]{2,1,0:T(8,128)(2,1)}), bf16[16,208,128]{2,1,0:T(8,128)(2,1)S(1)}, u32[]{:S(2)}, u32[]{:S(2)}) async-start(bf16[16,208,128]{2,1,0:T(8,128)(2,1)} %cut_columns.1), calls=%async_computation | async-start | bytes 1703936 | tf_op jit(solution)/shard_map/all_to_all | solution.py:157
  15.7 0.0 copy-done
  15.7 3.3 %collective-permute-start.10 = (bf16[4,2,128,128]{3,2,1,0:T(8,128)(2,1)S(1)}, bf16[4,2,128,128]{3,2,1,0:T(8,128)(2,1)S(1)}, u32[]{:S(2)}, u32[]{:S(2)}) collective-permute-start(bf16[4,2,128,128]{3,2,1,0:T(8,128)(2,1)S(1)} %copy-done), channel_id=1, source_target_pairs={{0,13},{1,12},{2,15},{3,14},{4,9},{5,8},{6,11},{7,10},{8,5},{9,4},... | collective-permute-start | bytes 786440 | tf_op jit(solution)/shard_map/ppermute | solution.py:149
  19.1 0.6 collective-permute-start.9
  19.7 15.0 %collective-permute-done.10.rest_5_ = bf16[4,2,128,128]{3,2,1,0:T(8,128)(2,1)S(1)} collective-permute-done((bf16[4,2,128,128]{3,2,1,0:T(8,128)(2,1)S(1)}, bf16[4,2,128,128]{3,2,1,0:T(8,128)(2,1)S(1)}, u32[]{:S(2)}, u32[]{:S(2)}) %collective-permute-start.10) | collective-permute-done | bytes 262176 | tf_op jit(solution)/shard_map/ppermute | solution.py:149
  34.7 0.9 %collective-permute-start.11 = (bf16[4,2,128,128]{3,2,1,0:T(8,128)(2,1)S(1)}, bf16[4,2,128,128]{3,2,1,0:T(8,128)(2,1)S(1)}, u32[]{:S(2)}, u32[]{:S(2)}) collective-permute-start(bf16[4,2,128,128]{3,2,1,0:T(8,128)(2,1)S(1)} %collective-permute-done.rest_2_), channel_id=1, source_target_pairs={{0,2},{1,3},{2,0},{3,1},{4,6},{5,7},{6,4},{7,5},{8,10},{9,11},{10,... | collective-permute-start | bytes 786440 | tf_op jit(solution)/shard_map/ppermute | solution.py:146
  35.6 0.0 collective-permute-start.12
  35.6 0.2 collective-permute-start.3
  35.8 0.3 collective-permute-start.5
  36.1 0.0 collective-permute-done.9.rest_1_
  36.1 0.0 copy-start.3
  36.1 0.7 copy-done.3
  36.8 2.0 %collective-permute-start.7 = (bf16[4,2,128,128]{3,2,1,0:T(8,128)(2,1)S(1)}, bf16[4,2,128,128]{3,2,1,0:T(8,128)(2,1)S(1)}, u32[]{:S(2)}, u32[]{:S(2)}) collective-permute-start(bf16[4,2,128,128]{3,2,1,0:T(8,128)(2,1)S(1)} %collective-permute-done.2.rest_4_), channel_id=1, source_target_pairs={{0,1},{1,0},{2,6},{3,7},{4,5},{5,4},{6,2},{7,3},{8,9},{9,8},{10,14... | collective-permute-start | bytes 786440 | tf_op jit(solution)/shard_map/ppermute | solution.py:143
  38.8 0.0 collective-permute-done.11.rest_6_
  38.8 0.0 copy-start.5
  38.8 0.7 copy-done.5
  39.5 1.3 %collective-permute-start.13 = (bf16[4,2,128,128]{3,2,1,0:T(8,128)(2,1)S(1)}, bf16[4,2,128,128]{3,2,1,0:T(8,128)(2,1)S(1)}, u32[]{:S(2)}, u32[]{:S(2)}) collective-permute-start(bf16[4,2,128,128]{3,2,1,0:T(8,128)(2,1)S(1)} %collective-permute-done.2.rest_4_), channel_id=1, source_target_pairs={{0,2},{1,3},{2,0},{3,1},{4,6},{5,7},{6,4},{7,5},{8,10},{9,11},{10,... | collective-permute-start | bytes 786440 | tf_op jit(solution)/shard_map/ppermute | solution.py:146
  40.9 0.0 collective-permute-done.12.rest_7_
  40.9 0.0 copy-start.7
  40.9 0.7 copy-done.7
  41.6 0.0 collective-permute-start.14
  41.6 0.0 copy-start.1
  41.6 0.7 copy-done.1
  42.3 0.0 collective-permute-done.3.rest_0_
  42.3 2.3 %collective-permute-start.4 = (bf16[4,2,128,128]{3,2,1,0:T(8,128)(2,1)S(1)}, bf16[4,2,128,128]{3,2,1,0:T(8,128)(2,1)S(1)}, u32[]{:S(2)}, u32[]{:S(2)}) collective-permute-start(bf16[4,2,128,128]{3,2,1,0:T(8,128)(2,1)S(1)} %collective-permute-done.3.rest_0_), channel_id=1, source_target_pairs={{0,2},{1,3},{2,0},{3,1},{4,6},{5,7},{6,4},{7,5},{8,10},{9,11},{10,... | collective-permute-start | bytes 786440 | tf_op jit(solution)/shard_map/ppermute | solution.py:146
  44.6 0.0 collective-permute-done.5.rest_1_
  44.6 0.0 collective-permute-start.6
  44.7 0.3 collective-permute-done.7.rest_2_
  44.9 1.0 %collective-permute-start.8 = (bf16[4,2,128,128]{3,2,1,0:T(8,128)(2,1)S(1)}, bf16[4,2,128,128]{3,2,1,0:T(8,128)(2,1)S(1)}, u32[]{:S(2)}, u32[]{:S(2)}) collective-permute-start(bf16[4,2,128,128]{3,2,1,0:T(8,128)(2,1)S(1)} %collective-permute-done.7.rest_2_), channel_id=1, source_target_pairs={{0,2},{1,3},{2,0},{3,1},{4,6},{5,7},{6,4},{7,5},{8,10},{9,11},{10,... | collective-permute-start | bytes 786440 | tf_op jit(solution)/shard_map/ppermute | solution.py:146
  46.0 0.0 collective-permute-done.13.rest_8_
  46.0 0.0 copy-start.9
  46.0 0.7 copy-done.9
  46.7 0.0 collective-permute-done.14.rest_9_
  46.7 0.0 copy-start.11
  46.7 0.7 copy-done.11
  47.4 0.0 all-to-all-done.q_ref
  47.4 0.0 copy-start.2
  47.4 0.9 %copy-done.2 = bf16[4,2,128,128]{3,2,1,0:T(8,128)(2,1)S(1)} copy-done((bf16[4,2,128,128]{3,2,1,0:T(8,128)(2,1)S(1)}, bf16[4,2,128,128]{3,2,1,0:T(8,128)(2,1)}, u32[]{:S(2)}) %copy-start.2) | copy-done | bytes 262168
  48.4 0.0 copy-start.4
  48.4 0.9 %copy-done.4 = bf16[4,2,128,128]{3,2,1,0:T(8,128)(2,1)S(1)} copy-done((bf16[4,2,128,128]{3,2,1,0:T(8,128)(2,1)S(1)}, bf16[4,2,128,128]{3,2,1,0:T(8,128)(2,1)}, u32[]{:S(2)}) %copy-start.4) | copy-done | bytes 262168
  49.3 0.0 copy-start.6
  49.3 0.9 %copy-done.6 = bf16[4,2,128,128]{3,2,1,0:T(8,128)(2,1)S(1)} copy-done((bf16[4,2,128,128]{3,2,1,0:T(8,128)(2,1)S(1)}, bf16[4,2,128,128]{3,2,1,0:T(8,128)(2,1)}, u32[]{:S(2)}) %copy-start.6) | copy-done | bytes 262168
  50.3 0.0 copy-start.8
  50.3 0.9 %copy-done.8 = bf16[4,2,128,128]{3,2,1,0:T(8,128)(2,1)S(1)} copy-done((bf16[4,2,128,128]{3,2,1,0:T(8,128)(2,1)S(1)}, bf16[4,2,128,128]{3,2,1,0:T(8,128)(2,1)}, u32[]{:S(2)}) %copy-start.8) | copy-done | bytes 262168
  51.2 0.0 copy-start.10
  51.2 0.9 %copy-done.10 = bf16[4,2,128,128]{3,2,1,0:T(8,128)(2,1)S(1)} copy-done((bf16[4,2,128,128]{3,2,1,0:T(8,128)(2,1)S(1)}, bf16[4,2,128,128]{3,2,1,0:T(8,128)(2,1)}, u32[]{:S(2)}) %copy-start.10) | copy-done | bytes 262168
  52.2 0.0 copy-start.12
  52.2 0.9 %copy-done.12 = bf16[4,2,128,128]{3,2,1,0:T(8,128)(2,1)S(1)} copy-done((bf16[4,2,128,128]{3,2,1,0:T(8,128)(2,1)S(1)}, bf16[4,2,128,128]{3,2,1,0:T(8,128)(2,1)}, u32[]{:S(2)}) %copy-start.12) | copy-done | bytes 262168
  53.1 4.2 %products.3.rest_3_ = f32[256,8,128]{2,1,0:T(8,128)S(1)} custom-call(bf16[16,208,128]{2,1,0:T(8,128)(2,1)S(1)} %all-to-all-done.q_ref, bf16[4,2,128,128]{3,2,1,0:T(8,128)(2,1)S(1)} %copy-done, bf16[4,2,128,128]{3,2,1,0:T(8,128)(2,1)S(1)} %copy-done.4, bf16[4,2,128,128]{3,2,1,0:T(8,128)(2,1)S(1)} %collective-permute-done.rest_2_, ...), custom_call_target="tpu_custom_call" | custom-call | flops 125829120 | bytes 10485760 | tf_op jit(solution)/shard_map/products/pallas_call | solution.py:92
  57.4 1.7 %products.4.rest_3_ = f32[256,8,128]{2,1,0:T(8,128)S(1)} custom-call(bf16[16,208,128]{2,1,0:T(8,128)(2,1)S(1)} %all-to-all-done.q_ref, bf16[4,2,128,128]{3,2,1,0:T(8,128)(2,1)S(1)} %collective-permute-done.3.rest_0_, bf16[4,2,128,128]{3,2,1,0:T(8,128)(2,1)S(1)} %collective-permute-done.5.rest_1_, ...), custom_call_target="tpu_custom_call", output_to_operand_aliasing={{}: (4, {})} | custom-call | flops 37748736 | bytes 3145728 | tf_op jit(solution)/shard_map/products/pallas_call | solution.py:92
  59.1 0.0 collective-permute-done.4.rest_0_
  59.1 0.0 collective-permute-done.6.rest_1_
  59.1 0.0 collective-permute-done.8.rest_2_
  59.2 1.7 %products.5 = f32[256,8,128]{2,1,0:T(8,128)S(1)} custom-call(bf16[16,208,128]{2,1,0:T(8,128)(2,1)S(1)} %all-to-all-done.q_ref, bf16[4,2,128,128]{3,2,1,0:T(8,128)(2,1)S(1)} %collective-permute-done.4.rest_0_, bf16[4,2,128,128]{3,2,1,0:T(8,128)(2,1)S(1)} %collective-permute-done.6.rest_1_, ...), custom_call_target="tpu_custom_call", output_to_operand_aliasing={{}: (4, {})} | custom-call | flops 37748736 | bytes 3145728 | tf_op jit(solution)/shard_map/products/pallas_call | solution.py:92
  60.9 29.7 %all_to_all.10 = f32[32,8,8,128]{3,2,1,0:T(8,128)S(1)} all-to-all(f32[32,8,8,128]{3,2,1,0:T(8,128)S(1)} %bitcast.3), channel_id=1, replica_groups=mesh['plane'=2,'pair'=4,'core'=2,'col'=2] {'plane','pair','core','col'}, dimensions={0} | all-to-all | bytes 2097152 | tf_op jit(solution)/shard_map/all_to_all | solution.py:170
  90.6 1.0 %turn.1 = f32[128,1024]{1,0:T(8,128)} custom-call(f32[2,16,8,8,128]{4,3,2,1,0:T(8,128)S(1)} %bitcast.4), custom_call_target="tpu_custom_call" | custom-call | tf_op jit(solution)/shard_map/turn/pallas_call | solution.py:171
Async XLA Ops:
  0.0 6.9 %collective-permute-start.2 = (bf16[4,2,128,128]{3,2,1,0:T(8,128)(2,1)}, bf16[4,2,128,128]{3,2,1,0:T(8,128)(2,1)S(1)}, u32[]{:S(2)}, u32[]{:S(2)}) collective-permute-start(bf16[4,2,128,128]{3,2,1,0:T(8,128)(2,1)} %rest_0_.1), channel_id=1, source_target_pairs={{0,8},{1,9},{2,3},{3,2},{4,12},{5,13},{6,7},{7,6},{8,0},{9,1},{10,... | collective-permute-start | bytes 786440 | tf_op jit(solution)/shard_map/ppermute | solution.py:143
  2.1 8.0 %collective-permute-start.1 = (bf16[4,2,128,128]{3,2,1,0:T(8,128)(2,1)}, bf16[4,2,128,128]{3,2,1,0:T(8,128)(2,1)S(1)}, u32[]{:S(2)}, u32[]{:S(2)}) collective-permute-start(bf16[4,2,128,128]{3,2,1,0:T(8,128)(2,1)} %rest_0_.1), channel_id=1, source_target_pairs={{0,4},{1,5},{2,10},{3,11},{4,0},{5,1},{6,14},{7,15},{8,12},{9,13},... | collective-permute-start | bytes 786440 | tf_op jit(solution)/shard_map/ppermute | solution.py:143
  3.4 8.4 %collective-permute-start = (bf16[4,2,128,128]{3,2,1,0:T(8,128)(2,1)}, bf16[4,2,128,128]{3,2,1,0:T(8,128)(2,1)S(1)}, u32[]{:S(2)}, u32[]{:S(2)}) collective-permute-start(bf16[4,2,128,128]{3,2,1,0:T(8,128)(2,1)} %rest_0_.1), channel_id=1, source_target_pairs={{0,1},{1,0},{2,6},{3,7},{4,5},{5,4},{6,2},{7,3},{8,9},{9,8},{10,14... | collective-permute-start | bytes 786440 | tf_op jit(solution)/shard_map/ppermute | solution.py:143
  6.9 8.8 %copy-start = (bf16[4,2,128,128]{3,2,1,0:T(8,128)(2,1)S(1)}, bf16[4,2,128,128]{3,2,1,0:T(8,128)(2,1)}, u32[]{:S(2)}) copy-start(bf16[4,2,128,128]{3,2,1,0:T(8,128)(2,1)} %rest_0_.1) | copy-start | bytes 786436
  11.7 35.7 %all-to-all-start = ((bf16[16,208,128]{2,1,0:T(8,128)(2,1)}), bf16[16,208,128]{2,1,0:T(8,128)(2,1)S(1)}, u32[]{:S(2)}, u32[]{:S(2)}) async-start(bf16[16,208,128]{2,1,0:T(8,128)(2,1)} %cut_columns.1), calls=%async_computation | async-start | bytes 1703936 | tf_op jit(solution)/shard_map/all_to_all | solution.py:157
  15.7 19.0 %collective-permute-start.10 = (bf16[4,2,128,128]{3,2,1,0:T(8,128)(2,1)S(1)}, bf16[4,2,128,128]{3,2,1,0:T(8,128)(2,1)S(1)}, u32[]{:S(2)}, u32[]{:S(2)}) collective-permute-start(bf16[4,2,128,128]{3,2,1,0:T(8,128)(2,1)S(1)} %copy-done), channel_id=1, source_target_pairs={{0,13},{1,12},{2,15},{3,14},{4,9},{5,8},{6,11},{7,10},{8,5},{9,4},... | collective-permute-start | bytes 786440 | tf_op jit(solution)/shard_map/ppermute | solution.py:149
  19.1 17.0 %collective-permute-start.9 = (bf16[4,2,128,128]{3,2,1,0:T(8,128)(2,1)S(1)}, bf16[4,2,128,128]{3,2,1,0:T(8,128)(2,1)S(1)}, u32[]{:S(2)}, u32[]{:S(2)}) collective-permute-start(bf16[4,2,128,128]{3,2,1,0:T(8,128)(2,1)S(1)} %copy-done), channel_id=1, source_target_pairs={{0,2},{1,3},{2,0},{3,1},{4,6},{5,7},{6,4},{7,5},{8,10},{9,11},{10,... | collective-permute-start | bytes 786440 | tf_op jit(solution)/shard_map/ppermute | solution.py:146
  34.7 4.1 %collective-permute-start.11 = (bf16[4,2,128,128]{3,2,1,0:T(8,128)(2,1)S(1)}, bf16[4,2,128,128]{3,2,1,0:T(8,128)(2,1)S(1)}, u32[]{:S(2)}, u32[]{:S(2)}) collective-permute-start(bf16[4,2,128,128]{3,2,1,0:T(8,128)(2,1)S(1)} %collective-permute-done.rest_2_), channel_id=1, source_target_pairs={{0,2},{1,3},{2,0},{3,1},{4,6},{5,7},{6,4},{7,5},{8,10},{9,11},{10,... | collective-permute-start | bytes 786440 | tf_op jit(solution)/shard_map/ppermute | solution.py:146
  35.6 5.3 %collective-permute-start.12 = (bf16[4,2,128,128]{3,2,1,0:T(8,128)(2,1)S(1)}, bf16[4,2,128,128]{3,2,1,0:T(8,128)(2,1)S(1)}, u32[]{:S(2)}, u32[]{:S(2)}) collective-permute-start(bf16[4,2,128,128]{3,2,1,0:T(8,128)(2,1)S(1)} %collective-permute-done.1.rest_3_), channel_id=1, source_target_pairs={{0,2},{1,3},{2,0},{3,1},{4,6},{5,7},{6,4},{7,5},{8,10},{9,11},{10,... | collective-permute-start | bytes 786440 | tf_op jit(solution)/shard_map/ppermute | solution.py:146
  35.6 6.7 %collective-permute-start.3 = (bf16[4,2,128,128]{3,2,1,0:T(8,128)(2,1)S(1)}, bf16[4,2,128,128]{3,2,1,0:T(8,128)(2,1)S(1)}, u32[]{:S(2)}, u32[]{:S(2)}) collective-permute-start(bf16[4,2,128,128]{3,2,1,0:T(8,128)(2,1)S(1)} %collective-permute-done.rest_2_), channel_id=1, source_target_pairs={{0,4},{1,5},{2,10},{3,11},{4,0},{5,1},{6,14},{7,15},{8,12},{9,13},... | collective-permute-start | bytes 786440 | tf_op jit(solution)/shard_map/ppermute | solution.py:143
  35.8 8.8 %collective-permute-start.5 = (bf16[4,2,128,128]{3,2,1,0:T(8,128)(2,1)S(1)}, bf16[4,2,128,128]{3,2,1,0:T(8,128)(2,1)S(1)}, u32[]{:S(2)}, u32[]{:S(2)}) collective-permute-start(bf16[4,2,128,128]{3,2,1,0:T(8,128)(2,1)S(1)} %collective-permute-done.1.rest_3_), channel_id=1, source_target_pairs={{0,8},{1,9},{2,3},{3,2},{4,12},{5,13},{6,7},{7,6},{8,0},{9,1},{10,... | collective-permute-start | bytes 786440 | tf_op jit(solution)/shard_map/ppermute | solution.py:143
  36.1 0.7 copy-start.3
  36.8 8.2 %collective-permute-start.7 = (bf16[4,2,128,128]{3,2,1,0:T(8,128)(2,1)S(1)}, bf16[4,2,128,128]{3,2,1,0:T(8,128)(2,1)S(1)}, u32[]{:S(2)}, u32[]{:S(2)}) collective-permute-start(bf16[4,2,128,128]{3,2,1,0:T(8,128)(2,1)S(1)} %collective-permute-done.2.rest_4_), channel_id=1, source_target_pairs={{0,1},{1,0},{2,6},{3,7},{4,5},{5,4},{6,2},{7,3},{8,9},{9,8},{10,14... | collective-permute-start | bytes 786440 | tf_op jit(solution)/shard_map/ppermute | solution.py:143
  38.8 0.7 copy-start.5
  39.5 6.4 %collective-permute-start.13 = (bf16[4,2,128,128]{3,2,1,0:T(8,128)(2,1)S(1)}, bf16[4,2,128,128]{3,2,1,0:T(8,128)(2,1)S(1)}, u32[]{:S(2)}, u32[]{:S(2)}) collective-permute-start(bf16[4,2,128,128]{3,2,1,0:T(8,128)(2,1)S(1)} %collective-permute-done.2.rest_4_), channel_id=1, source_target_pairs={{0,2},{1,3},{2,0},{3,1},{4,6},{5,7},{6,4},{7,5},{8,10},{9,11},{10,... | collective-permute-start | bytes 786440 | tf_op jit(solution)/shard_map/ppermute | solution.py:146
  40.9 0.7 copy-start.7
  41.6 5.1 %collective-permute-start.14 = (bf16[4,2,128,128]{3,2,1,0:T(8,128)(2,1)S(1)}, bf16[4,2,128,128]{3,2,1,0:T(8,128)(2,1)S(1)}, u32[]{:S(2)}, u32[]{:S(2)}) collective-permute-start(bf16[4,2,128,128]{3,2,1,0:T(8,128)(2,1)S(1)} %collective-permute-done.10.rest_5_), channel_id=1, source_target_pairs={{0,2},{1,3},{2,0},{3,1},{4,6},{5,7},{6,4},{7,5},{8,10},{9,11},{10,... | collective-permute-start | bytes 786440 | tf_op jit(solution)/shard_map/ppermute | solution.py:146
  41.6 0.7 copy-start.1
  42.3 16.8 %collective-permute-start.4 = (bf16[4,2,128,128]{3,2,1,0:T(8,128)(2,1)S(1)}, bf16[4,2,128,128]{3,2,1,0:T(8,128)(2,1)S(1)}, u32[]{:S(2)}, u32[]{:S(2)}) collective-permute-start(bf16[4,2,128,128]{3,2,1,0:T(8,128)(2,1)S(1)} %collective-permute-done.3.rest_0_), channel_id=1, source_target_pairs={{0,2},{1,3},{2,0},{3,1},{4,6},{5,7},{6,4},{7,5},{8,10},{9,11},{10,... | collective-permute-start | bytes 786440 | tf_op jit(solution)/shard_map/ppermute | solution.py:146
  44.6 14.5 %collective-permute-start.6 = (bf16[4,2,128,128]{3,2,1,0:T(8,128)(2,1)S(1)}, bf16[4,2,128,128]{3,2,1,0:T(8,128)(2,1)S(1)}, u32[]{:S(2)}, u32[]{:S(2)}) collective-permute-start(bf16[4,2,128,128]{3,2,1,0:T(8,128)(2,1)S(1)} %collective-permute-done.5.rest_1_), channel_id=1, source_target_pairs={{0,2},{1,3},{2,0},{3,1},{4,6},{5,7},{6,4},{7,5},{8,10},{9,11},{10,... | collective-permute-start | bytes 786440 | tf_op jit(solution)/shard_map/ppermute | solution.py:146
  44.9 14.2 %collective-permute-start.8 = (bf16[4,2,128,128]{3,2,1,0:T(8,128)(2,1)S(1)}, bf16[4,2,128,128]{3,2,1,0:T(8,128)(2,1)S(1)}, u32[]{:S(2)}, u32[]{:S(2)}) collective-permute-start(bf16[4,2,128,128]{3,2,1,0:T(8,128)(2,1)S(1)} %collective-permute-done.7.rest_2_), channel_id=1, source_target_pairs={{0,2},{1,3},{2,0},{3,1},{4,6},{5,7},{6,4},{7,5},{8,10},{9,11},{10,... | collective-permute-start | bytes 786440 | tf_op jit(solution)/shard_map/ppermute | solution.py:146
  46.0 0.7 copy-start.9
  46.7 0.7 copy-start.11
  47.4 1.0 %copy-start.2 = (bf16[4,2,128,128]{3,2,1,0:T(8,128)(2,1)S(1)}, bf16[4,2,128,128]{3,2,1,0:T(8,128)(2,1)}, u32[]{:S(2)}) copy-start(bf16[4,2,128,128]{3,2,1,0:T(8,128)(2,1)} %copy-done.1) | copy-start | bytes 786436
  48.4 0.9 %copy-start.4 = (bf16[4,2,128,128]{3,2,1,0:T(8,128)(2,1)S(1)}, bf16[4,2,128,128]{3,2,1,0:T(8,128)(2,1)}, u32[]{:S(2)}) copy-start(bf16[4,2,128,128]{3,2,1,0:T(8,128)(2,1)} %copy-done.3) | copy-start | bytes 786436
  49.3 0.9 %copy-start.6 = (bf16[4,2,128,128]{3,2,1,0:T(8,128)(2,1)S(1)}, bf16[4,2,128,128]{3,2,1,0:T(8,128)(2,1)}, u32[]{:S(2)}) copy-start(bf16[4,2,128,128]{3,2,1,0:T(8,128)(2,1)} %copy-done.5) | copy-start | bytes 786436
  50.3 0.9 %copy-start.8 = (bf16[4,2,128,128]{3,2,1,0:T(8,128)(2,1)S(1)}, bf16[4,2,128,128]{3,2,1,0:T(8,128)(2,1)}, u32[]{:S(2)}) copy-start(bf16[4,2,128,128]{3,2,1,0:T(8,128)(2,1)} %copy-done.7) | copy-start | bytes 786436
  51.2 0.9 %copy-start.10 = (bf16[4,2,128,128]{3,2,1,0:T(8,128)(2,1)S(1)}, bf16[4,2,128,128]{3,2,1,0:T(8,128)(2,1)}, u32[]{:S(2)}) copy-start(bf16[4,2,128,128]{3,2,1,0:T(8,128)(2,1)} %copy-done.9) | copy-start | bytes 786436
  52.2 0.9 %copy-start.12 = (bf16[4,2,128,128]{3,2,1,0:T(8,128)(2,1)S(1)}, bf16[4,2,128,128]{3,2,1,0:T(8,128)(2,1)}, u32[]{:S(2)}) copy-start(bf16[4,2,128,128]{3,2,1,0:T(8,128)(2,1)} %copy-done.11) | copy-start | bytes 786436

commit v8 on v6

--- a/solution.py
+++ b/solution.py
@@ -127,9 +127,9 @@
         out_shape=jax.ShapeDtypeStruct((SEATS, height, extent), q_tiles.dtype),
         in_specs=[pl.BlockSpec(memory_space=pltpu.SMEM)] * 2 + [pl.BlockSpec(memory_space=pltpu.VMEM)],
         cost_estimate=pl.CostEstimate(flops=0, bytes_accessed=8 << 20, transcendentals=0),
-        compiler_params=pltpu.CompilerParams(vmem_limit_bytes=8 << 20),
         name="cut_columns",
     )(p_cols.T, q_cols, q_tiles)
+
     def along(values, step):
         hops = [(s, s ^ axes(s // cols % 2, cols)[step]) for s in range(SEATS)]
         return lax.ppermute(values, seat, hops)
@@ -137,26 +137,20 @@
     def across(values):
         return lax.ppermute(values, seat, [(s, s ^ cols) for s in range(SEATS)])
 
-    def opposite(values):
-        return lax.ppermute(values, seat, [(s, s ^ (SEATS - 1 - cols)) for s in range(SEATS)])
-
     def add(acc, sets, routes):
         return add_products(q_here, sets, routes, acc, tile_count, cols, strip)
 
-    beside = across(p_tiles)
-    first = [along(p_tiles, step) for step in range(3)] + [opposite(p_tiles)]
-    sliced, beside = lax.optimization_barrier((sliced, beside))
+    first = [along(p_tiles, step) for step in range(3)]
+    sliced, *first = lax.optimization_barrier((sliced, *first))
     q_here = lax.all_to_all(sliced, seat, split_axis=0, concat_axis=0, tiled=True)
     second = [along(first[step], (step + 1) % 3) for step in range(3)]
-    sets = [p_tiles, beside] + first + [across(each) for each in first]
-    steps = (1, 2, 3, 7)
-    acc = add(
-        None, sets, [(0, 0), (0, 1)] + [(step, 0) for step in steps] + [(step, 1) for step in steps]
-    )
-    *second, acc = lax.optimization_barrier((*second, acc))
-    crossed = [across(each) for each in second]
-    acc = add(acc, second, [(4, 0), (5, 0), (6, 0)])
-    acc = add(acc, crossed, [(4, 1), (5, 1), (6, 1)])
+    sets = [p_tiles] + first + [across(each) for each in [p_tiles] + first]
+    q_here, *second = lax.optimization_barrier((q_here, *second))
+    third = along(second[0], 2)
+    acc = add(None, sets, [(step, swapped) for swapped in (0, 1) for step in range(4)])
+    sets = second + [across(each) for each in second]
+    acc = add(acc, sets, [(step, swapped) for swapped in (0, 1) for step in (4, 5, 6)])
+    acc = add(acc, [third, across(third)], [(7, 0), (7, 1)])
     every = ("plane",) + seat
     parts = acc.reshape(planes * SEATS, tile_count // cols, strip, extent)
     landed = lax.all_to_all(parts, every, split_axis=0, concat_axis=0, tiled=True)

time: 83.3 us -> 79.8 us (0.958)
  waiting for transfers between devices: 13.2 us -> 21 us
  local copies, waits for them, and re-layouts: 7.42 us -> 0.01 us
  starting transfers between devices: 22.2 us -> 18.4 us
    ppermute x6 -> x7, waiting for transfers between devices: 13.2 us -> 21 us  [along(): return lax.ppermute(values, seat, hops)]
    unnamed x20 -> x2, local copies, waits for them, and re-layouts: 7.42 us -> 0.01 us
    ppermute x8, starting transfers between devices: 10.4 us -> 4.7 us  [across(): return lax.ppermute(values, seat, [(s, s ^ cols) for s in range(SEATS)])]
    ppermute x6 -> x7, starting transfers between devices: 5.43 us -> 9.65 us  [along(): return lax.ppermute(values, seat, hops)]
    all_to_all x1, starting transfers between devices: 6.39 us -> 3.99 us  [body(): lax.all_to_all(sliced, seat, split_axis=0, concat_axis=0, tiled=True)]
  transfers between devices with their start and end apart: 16 -> 16, of which waited for: 1 -> 4; matrix products, arithmetic and copies ran while one was open for 0% -> 0% of each run, Pallas kernels for 8% -> 10%
where the time goes in v8:
time: 79.8 us; the launch traced here: 79.1 us
  blocking collectives  29.9 us (37%)
  waiting for transfers between devices  21 us (26%)
  starting transfers between devices  18.4 us (23%)
  Pallas kernels  9.84 us (12%)
    all_to_all x1, blocking collectives, body(): lax.all_to_all(parts, every, split_axis=0, concat_axis=0, tiled=True)  29.9 us
    ppermute x7, waiting for transfers between devices, along(): return lax.ppermute(values, seat, hops)  21 us
    ppermute x7, starting transfers between devices, along(): return lax.ppermute(values, seat, hops)  9.65 us
    pallas_call x3, Pallas kernels, add_products(): pl.pallas_call(functools.partial(product_kernel, tile_count, cols, routes...  6.53 us
    ppermute x8, starting transfers between devices, across(): return lax.ppermute(values, seat, [(s, s ^ cols) for s in range(SEATS)])  4.7 us
    all_to_all x1, starting transfers between devices, body(): lax.all_to_all(sliced, seat, split_axis=0, concat_axis=0, tiled=True)  3.99 us
    pallas_call x1, Pallas kernels, body(): pl.pallas_call(slice_kernel, out_shape=jax.ShapeDtypeStruct((SEATS, heigh...  2.31 us
  transfers between devices with their start and end apart: 16, of which 4 were waited for; matrix products, arithmetic and copies ran while one was open for 0% of the time, Pallas kernels for 10%

profile of v8, /device:TPU:1, one launch (start us, length us, event | category | flops | bytes accessed | tf_op | source)
XLA Modules:
  0.0 79.1 jit_solution(1563634704359875229)
XLA Ops:
  0.0 2.1 %collective-permute-start.2 = (bf16[4,2,128,128]{3,2,1,0:T(8,128)(2,1)}, bf16[4,2,128,128]{3,2,1,0:T(8,128)(2,1)S(1)}, u32[]{:S(2)}, u32[]{:S(2)}) collective-permute-start(bf16[4,2,128,128]{3,2,1,0:T(8,128)(2,1)} %rest_0_.1), channel_id=1, source_target_pairs={{0,8},{1,9},{2,3},{3,2},{4,12},{5,13},{6,7},{7,6},{8,0},{9,1},{10,... | collective-permute-start | bytes 786440 | tf_op jit(solution)/shard_map/ppermute | solution.py:135
  2.1 1.3 %collective-permute-start.1 = (bf16[4,2,128,128]{3,2,1,0:T(8,128)(2,1)}, bf16[4,2,128,128]{3,2,1,0:T(8,128)(2,1)S(1)}, u32[]{:S(2)}, u32[]{:S(2)}) collective-permute-start(bf16[4,2,128,128]{3,2,1,0:T(8,128)(2,1)} %rest_0_.1), channel_id=1, source_target_pairs={{0,4},{1,5},{2,10},{3,11},{4,0},{5,1},{6,14},{7,15},{8,12},{9,13},... | collective-permute-start | bytes 786440 | tf_op jit(solution)/shard_map/ppermute | solution.py:135
  3.4 1.2 %collective-permute-start = (bf16[4,2,128,128]{3,2,1,0:T(8,128)(2,1)}, bf16[4,2,128,128]{3,2,1,0:T(8,128)(2,1)S(1)}, u32[]{:S(2)}, u32[]{:S(2)}) collective-permute-start(bf16[4,2,128,128]{3,2,1,0:T(8,128)(2,1)} %rest_0_.1), channel_id=1, source_target_pairs={{0,1},{1,0},{2,6},{3,7},{4,5},{5,4},{6,2},{7,3},{8,9},{9,8},{10,14... | collective-permute-start | bytes 786440 | tf_op jit(solution)/shard_map/ppermute | solution.py:135
  4.6 2.3 %cut_columns.1 = bf16[16,208,128]{2,1,0:T(8,128)(2,1)} custom-call(s32[2,4]{1,0:T(2,128)} %bitcast.5, s32[4,6]{1,0:T(4,128)} %q_ids.1, bf16[4,6,128,128]{3,2,1,0:T(8,128)(2,1)} %q_ref.1), custom_call_target="tpu_custom_call" | custom-call | bytes 8388608 | tf_op jit(solution)/shard_map/cut_columns/pallas_call | solution.py:125
  6.9 0.0 copy-start
  6.9 0.0 collective-permute-done.2.rest_3_
  6.9 3.2 %collective-permute-done.1.rest_2_ = bf16[4,2,128,128]{3,2,1,0:T(8,128)(2,1)S(1)} collective-permute-done((bf16[4,2,128,128]{3,2,1,0:T(8,128)(2,1)}, bf16[4,2,128,128]{3,2,1,0:T(8,128)(2,1)S(1)}, u32[]{:S(2)}, u32[]{:S(2)}) %collective-permute-start.1) | collective-permute-done | bytes 262176 | tf_op jit(solution)/shard_map/ppermute | solution.py:135
  10.1 1.7 %collective-permute-done.rest_1_ = bf16[4,2,128,128]{3,2,1,0:T(8,128)(2,1)S(1)} collective-permute-done((bf16[4,2,128,128]{3,2,1,0:T(8,128)(2,1)}, bf16[4,2,128,128]{3,2,1,0:T(8,128)(2,1)S(1)}, u32[]{:S(2)}, u32[]{:S(2)}) %collective-permute-start) | collective-permute-done | bytes 262176 | tf_op jit(solution)/shard_map/ppermute | solution.py:135
  11.7 4.0 %all-to-all-start = ((bf16[16,208,128]{2,1,0:T(8,128)(2,1)}), bf16[16,208,128]{2,1,0:T(8,128)(2,1)S(1)}, u32[]{:S(2)}, u32[]{:S(2)}) async-start(bf16[16,208,128]{2,1,0:T(8,128)(2,1)} %cut_columns.1), calls=%async_computation | async-start | bytes 1703936 | tf_op jit(solution)/shard_map/all_to_all | solution.py:145
  15.7 1.4 %collective-permute-start.3 = (bf16[4,2,128,128]{3,2,1,0:T(8,128)(2,1)S(1)}, bf16[4,2,128,128]{3,2,1,0:T(8,128)(2,1)S(1)}, u32[]{:S(2)}, u32[]{:S(2)}) collective-permute-start(bf16[4,2,128,128]{3,2,1,0:T(8,128)(2,1)S(1)} %collective-permute-done.rest_1_), channel_id=1, source_target_pairs={{0,4},{1,5},{2,10},{3,11},{4,0},{5,1},{6,14},{7,15},{8,12},{9,13},... | collective-permute-start | bytes 786440 | tf_op jit(solution)/shard_map/ppermute | solution.py:135
  17.1 1.2 %collective-permute-start.4 = (bf16[4,2,128,128]{3,2,1,0:T(8,128)(2,1)S(1)}, bf16[4,2,128,128]{3,2,1,0:T(8,128)(2,1)S(1)}, u32[]{:S(2)}, u32[]{:S(2)}) collective-permute-start(bf16[4,2,128,128]{3,2,1,0:T(8,128)(2,1)S(1)} %collective-permute-done.1.rest_2_), channel_id=1, source_target_pairs={{0,8},{1,9},{2,3},{3,2},{4,12},{5,13},{6,7},{7,6},{8,0},{9,1},{10,... | collective-permute-start | bytes 786440 | tf_op jit(solution)/shard_map/ppermute | solution.py:135
  18.3 1.2 %collective-permute-start.5 = (bf16[4,2,128,128]{3,2,1,0:T(8,128)(2,1)S(1)}, bf16[4,2,128,128]{3,2,1,0:T(8,128)(2,1)S(1)}, u32[]{:S(2)}, u32[]{:S(2)}) collective-permute-start(bf16[4,2,128,128]{3,2,1,0:T(8,128)(2,1)S(1)} %collective-permute-done.2.rest_3_), channel_id=1, source_target_pairs={{0,1},{1,0},{2,6},{3,7},{4,5},{5,4},{6,2},{7,3},{8,9},{9,8},{10,14... | collective-permute-start | bytes 786440 | tf_op jit(solution)/shard_map/ppermute | solution.py:135
  19.5 0.0 copy-done
  19.6 1.2 %collective-permute-start.11 = (bf16[4,2,128,128]{3,2,1,0:T(8,128)(2,1)S(1)}, bf16[4,2,128,128]{3,2,1,0:T(8,128)(2,1)S(1)}, u32[]{:S(2)}, u32[]{:S(2)}) collective-permute-start(bf16[4,2,128,128]{3,2,1,0:T(8,128)(2,1)S(1)} %copy-done), channel_id=1, source_target_pairs={{0,2},{1,3},{2,0},{3,1},{4,6},{5,7},{6,4},{7,5},{8,10},{9,11},{10,... | collective-permute-start | bytes 786440 | tf_op jit(solution)/shard_map/ppermute | solution.py:138
  20.8 0.0 collective-permute-start.12
  20.8 12.8 %collective-permute-done.3.rest_0_ = bf16[4,2,128,128]{3,2,1,0:T(8,128)(2,1)S(1)} collective-permute-done((bf16[4,2,128,128]{3,2,1,0:T(8,128)(2,1)S(1)}, bf16[4,2,128,128]{3,2,1,0:T(8,128)(2,1)S(1)}, u32[]{:S(2)}, u32[]{:S(2)}) %collective-permute-start.3) | collective-permute-done | bytes 262176 | tf_op jit(solution)/shard_map/ppermute | solution.py:135
  33.6 1.6 %collective-permute-start.13 = (bf16[4,2,128,128]{3,2,1,0:T(8,128)(2,1)S(1)}, bf16[4,2,128,128]{3,2,1,0:T(8,128)(2,1)S(1)}, u32[]{:S(2)}, u32[]{:S(2)}) collective-permute-start(bf16[4,2,128,128]{3,2,1,0:T(8,128)(2,1)S(1)} %collective-permute-done.1.rest_2_), channel_id=1, source_target_pairs={{0,2},{1,3},{2,0},{3,1},{4,6},{5,7},{6,4},{7,5},{8,10},{9,11},{10,... | collective-permute-start | bytes 786440 | tf_op jit(solution)/shard_map/ppermute | solution.py:138
  35.2 0.0 collective-permute-done.4.rest_1_
  35.2 0.0 collective-permute-done.5.rest_2_
  35.2 0.0 all-to-all-done.q_ref
  35.2 1.3 %collective-permute-start.6 = (bf16[4,2,128,128]{3,2,1,0:T(8,128)(2,1)S(1)}, bf16[4,2,128,128]{3,2,1,0:T(8,128)(2,1)S(1)}, u32[]{:S(2)}, u32[]{:S(2)}) collective-permute-start(bf16[4,2,128,128]{3,2,1,0:T(8,128)(2,1)S(1)} %collective-permute-done.3.rest_0_), channel_id=1, source_target_pairs={{0,8},{1,9},{2,3},{3,2},{4,12},{5,13},{6,7},{7,6},{8,0},{9,1},{10,... | collective-permute-start | bytes 786440 | tf_op jit(solution)/shard_map/ppermute | solution.py:135
  36.5 0.0 collective-permute-start.14
  36.5 0.0 collective-permute-done.11.rest_4_
  36.5 0.5 collective-permute-start.9
  37.0 0.0 collective-permute-done.12.rest_5_
  37.0 0.1 collective-permute-start.10
  37.0 0.0 collective-permute-done.13.rest_6_
  37.0 0.4 collective-permute-start.8
  37.5 3.3 %collective-permute-done.6.rest_0_ = bf16[4,2,128,128]{3,2,1,0:T(8,128)(2,1)S(1)} collective-permute-done((bf16[4,2,128,128]{3,2,1,0:T(8,128)(2,1)S(1)}, bf16[4,2,128,128]{3,2,1,0:T(8,128)(2,1)S(1)}, u32[]{:S(2)}, u32[]{:S(2)}) %collective-permute-start.6) | collective-permute-done | bytes 262176 | tf_op jit(solution)/shard_map/ppermute | solution.py:135
  40.8 0.9 %collective-permute-start.7 = (bf16[4,2,128,128]{3,2,1,0:T(8,128)(2,1)S(1)}, bf16[4,2,128,128]{3,2,1,0:T(8,128)(2,1)S(1)}, u32[]{:S(2)}, u32[]{:S(2)}) collective-permute-start(bf16[4,2,128,128]{3,2,1,0:T(8,128)(2,1)S(1)} %collective-permute-done.6.rest_0_), channel_id=1, source_target_pairs={{0,2},{1,3},{2,0},{3,1},{4,6},{5,7},{6,4},{7,5},{8,10},{9,11},{10,... | collective-permute-start | bytes 786440 | tf_op jit(solution)/shard_map/ppermute | solution.py:138
  41.7 0.0 collective-permute-done.14.rest_7_
  41.7 2.9 %products.3.rest_6_ = f32[256,8,128]{2,1,0:T(8,128)S(1)} custom-call(bf16[16,208,128]{2,1,0:T(8,128)(2,1)S(1)} %all-to-all-done.q_ref, bf16[4,2,128,128]{3,2,1,0:T(8,128)(2,1)S(1)} %copy-done, bf16[4,2,128,128]{3,2,1,0:T(8,128)(2,1)S(1)} %collective-permute-done.rest_1_, bf16[4,2,128,128]{3,2,1,0:T(8,128)(2,1)S(1)} %collective-permute-done.1.rest_2_, ...), custom_call_target="tpu_custom_call" | custom-call | flops 100663296 | bytes 8388608 | tf_op jit(solution)/shard_map/products/pallas_call | solution.py:86
  44.6 0.0 collective-permute-done.9.rest_4_
  44.6 0.0 collective-permute-done.10.rest_5_
  44.6 0.0 collective-permute-done.8.rest_3_
  44.6 2.3 %products.4.rest_2_ = f32[256,8,128]{2,1,0:T(8,128)S(1)} custom-call(bf16[16,208,128]{2,1,0:T(8,128)(2,1)S(1)} %all-to-all-done.q_ref, bf16[4,2,128,128]{3,2,1,0:T(8,128)(2,1)S(1)} %collective-permute-done.3.rest_0_, bf16[4,2,128,128]{3,2,1,0:T(8,128)(2,1)S(1)} %collective-permute-done.4.rest_1_, ...), custom_call_target="tpu_custom_call", output_to_operand_aliasing={{}: (7, {})} | custom-call | flops 75497472 | bytes 6291456 | tf_op jit(solution)/shard_map/products/pallas_call | solution.py:86
  46.9 0.0 collective-permute-done.7.rest_1_
  47.0 1.3 %products.5 = f32[256,8,128]{2,1,0:T(8,128)S(1)} custom-call(bf16[16,208,128]{2,1,0:T(8,128)(2,1)S(1)} %all-to-all-done.q_ref, bf16[4,2,128,128]{3,2,1,0:T(8,128)(2,1)S(1)} %collective-permute-done.6.rest_0_, bf16[4,2,128,128]{3,2,1,0:T(8,128)(2,1)S(1)} %collective-permute-done.7.rest_1_, ...), custom_call_target="tpu_custom_call", output_to_operand_aliasing={{}: (3, {})} | custom-call | flops 25165824 | bytes 2097152 | tf_op jit(solution)/shard_map/products/pallas_call | solution.py:86
  48.3 29.9 %all_to_all.10 = f32[32,8,8,128]{3,2,1,0:T(8,128)S(1)} all-to-all(f32[32,8,8,128]{3,2,1,0:T(8,128)S(1)} %bitcast.3), channel_id=1, replica_groups=mesh['plane'=2,'pair'=4,'core'=2,'col'=2] {'plane','pair','core','col'}, dimensions={0} | all-to-all | bytes 2097152 | tf_op jit(solution)/shard_map/all_to_all | solution.py:156
  78.1 1.0 %turn.1 = f32[128,1024]{1,0:T(8,128)} custom-call(f32[2,16,8,8,128]{4,3,2,1,0:T(8,128)S(1)} %bitcast.4), custom_call_target="tpu_custom_call" | custom-call | tf_op jit(solution)/shard_map/turn/pallas_call | solution.py:157
Async XLA Ops:
  0.0 6.9 %collective-permute-start.2 = (bf16[4,2,128,128]{3,2,1,0:T(8,128)(2,1)}, bf16[4,2,128,128]{3,2,1,0:T(8,128)(2,1)S(1)}, u32[]{:S(2)}, u32[]{:S(2)}) collective-permute-start(bf16[4,2,128,128]{3,2,1,0:T(8,128)(2,1)} %rest_0_.1), channel_id=1, source_target_pairs={{0,8},{1,9},{2,3},{3,2},{4,12},{5,13},{6,7},{7,6},{8,0},{9,1},{10,... | collective-permute-start | bytes 786440 | tf_op jit(solution)/shard_map/ppermute | solution.py:135
  2.1 8.0 %collective-permute-start.1 = (bf16[4,2,128,128]{3,2,1,0:T(8,128)(2,1)}, bf16[4,2,128,128]{3,2,1,0:T(8,128)(2,1)S(1)}, u32[]{:S(2)}, u32[]{:S(2)}) collective-permute-start(bf16[4,2,128,128]{3,2,1,0:T(8,128)(2,1)} %rest_0_.1), channel_id=1, source_target_pairs={{0,4},{1,5},{2,10},{3,11},{4,0},{5,1},{6,14},{7,15},{8,12},{9,13},... | collective-permute-start | bytes 786440 | tf_op jit(solution)/shard_map/ppermute | solution.py:135
  3.4 8.4 %collective-permute-start = (bf16[4,2,128,128]{3,2,1,0:T(8,128)(2,1)}, bf16[4,2,128,128]{3,2,1,0:T(8,128)(2,1)S(1)}, u32[]{:S(2)}, u32[]{:S(2)}) collective-permute-start(bf16[4,2,128,128]{3,2,1,0:T(8,128)(2,1)} %rest_0_.1), channel_id=1, source_target_pairs={{0,1},{1,0},{2,6},{3,7},{4,5},{5,4},{6,2},{7,3},{8,9},{9,8},{10,14... | collective-permute-start | bytes 786440 | tf_op jit(solution)/shard_map/ppermute | solution.py:135
  6.9 12.7 %copy-start = (bf16[4,2,128,128]{3,2,1,0:T(8,128)(2,1)S(1)}, bf16[4,2,128,128]{3,2,1,0:T(8,128)(2,1)}, u32[]{:S(2)}) copy-start(bf16[4,2,128,128]{3,2,1,0:T(8,128)(2,1)} %rest_0_.1) | copy-start | bytes 786436
  11.7 23.5 %all-to-all-start = ((bf16[16,208,128]{2,1,0:T(8,128)(2,1)}), bf16[16,208,128]{2,1,0:T(8,128)(2,1)S(1)}, u32[]{:S(2)}, u32[]{:S(2)}) async-start(bf16[16,208,128]{2,1,0:T(8,128)(2,1)} %cut_columns.1), calls=%async_computation | async-start | bytes 1703936 | tf_op jit(solution)/shard_map/all_to_all | solution.py:145
  15.7 17.9 %collective-permute-start.3 = (bf16[4,2,128,128]{3,2,1,0:T(8,128)(2,1)S(1)}, bf16[4,2,128,128]{3,2,1,0:T(8,128)(2,1)S(1)}, u32[]{:S(2)}, u32[]{:S(2)}) collective-permute-start(bf16[4,2,128,128]{3,2,1,0:T(8,128)(2,1)S(1)} %collective-permute-done.rest_1_), channel_id=1, source_target_pairs={{0,4},{1,5},{2,10},{3,11},{4,0},{5,1},{6,14},{7,15},{8,12},{9,13},... | collective-permute-start | bytes 786440 | tf_op jit(solution)/shard_map/ppermute | solution.py:135
  17.1 18.0 %collective-permute-start.4 = (bf16[4,2,128,128]{3,2,1,0:T(8,128)(2,1)S(1)}, bf16[4,2,128,128]{3,2,1,0:T(8,128)(2,1)S(1)}, u32[]{:S(2)}, u32[]{:S(2)}) collective-permute-start(bf16[4,2,128,128]{3,2,1,0:T(8,128)(2,1)S(1)} %collective-permute-done.1.rest_2_), channel_id=1, source_target_pairs={{0,8},{1,9},{2,3},{3,2},{4,12},{5,13},{6,7},{7,6},{8,0},{9,1},{10,... | collective-permute-start | bytes 786440 | tf_op jit(solution)/shard_map/ppermute | solution.py:135
  18.3 16.9 %collective-permute-start.5 = (bf16[4,2,128,128]{3,2,1,0:T(8,128)(2,1)S(1)}, bf16[4,2,128,128]{3,2,1,0:T(8,128)(2,1)S(1)}, u32[]{:S(2)}, u32[]{:S(2)}) collective-permute-start(bf16[4,2,128,128]{3,2,1,0:T(8,128)(2,1)S(1)} %collective-permute-done.2.rest_3_), channel_id=1, source_target_pairs={{0,1},{1,0},{2,6},{3,7},{4,5},{5,4},{6,2},{7,3},{8,9},{9,8},{10,14... | collective-permute-start | bytes 786440 | tf_op jit(solution)/shard_map/ppermute | solution.py:135
  19.6 16.9 %collective-permute-start.11 = (bf16[4,2,128,128]{3,2,1,0:T(8,128)(2,1)S(1)}, bf16[4,2,128,128]{3,2,1,0:T(8,128)(2,1)S(1)}, u32[]{:S(2)}, u32[]{:S(2)}) collective-permute-start(bf16[4,2,128,128]{3,2,1,0:T(8,128)(2,1)S(1)} %copy-done), channel_id=1, source_target_pairs={{0,2},{1,3},{2,0},{3,1},{4,6},{5,7},{6,4},{7,5},{8,10},{9,11},{10,... | collective-permute-start | bytes 786440 | tf_op jit(solution)/shard_map/ppermute | solution.py:138
  20.8 16.2 %collective-permute-start.12 = (bf16[4,2,128,128]{3,2,1,0:T(8,128)(2,1)S(1)}, bf16[4,2,128,128]{3,2,1,0:T(8,128)(2,1)S(1)}, u32[]{:S(2)}, u32[]{:S(2)}) collective-permute-start(bf16[4,2,128,128]{3,2,1,0:T(8,128)(2,1)S(1)} %collective-permute-done.rest_1_), channel_id=1, source_target_pairs={{0,2},{1,3},{2,0},{3,1},{4,6},{5,7},{6,4},{7,5},{8,10},{9,11},{10,... | collective-permute-start | bytes 786440 | tf_op jit(solution)/shard_map/ppermute | solution.py:138
  33.6 3.5 %collective-permute-start.13 = (bf16[4,2,128,128]{3,2,1,0:T(8,128)(2,1)S(1)}, bf16[4,2,128,128]{3,2,1,0:T(8,128)(2,1)S(1)}, u32[]{:S(2)}, u32[]{:S(2)}) collective-permute-start(bf16[4,2,128,128]{3,2,1,0:T(8,128)(2,1)S(1)} %collective-permute-done.1.rest_2_), channel_id=1, source_target_pairs={{0,2},{1,3},{2,0},{3,1},{4,6},{5,7},{6,4},{7,5},{8,10},{9,11},{10,... | collective-permute-start | bytes 786440 | tf_op jit(solution)/shard_map/ppermute | solution.py:138
  35.2 5.6 %collective-permute-start.6 = (bf16[4,2,128,128]{3,2,1,0:T(8,128)(2,1)S(1)}, bf16[4,2,128,128]{3,2,1,0:T(8,128)(2,1)S(1)}, u32[]{:S(2)}, u32[]{:S(2)}) collective-permute-start(bf16[4,2,128,128]{3,2,1,0:T(8,128)(2,1)S(1)} %collective-permute-done.3.rest_0_), channel_id=1, source_target_pairs={{0,8},{1,9},{2,3},{3,2},{4,12},{5,13},{6,7},{7,6},{8,0},{9,1},{10,... | collective-permute-start | bytes 786440 | tf_op jit(solution)/shard_map/ppermute | solution.py:135
  36.5 5.2 %collective-permute-start.14 = (bf16[4,2,128,128]{3,2,1,0:T(8,128)(2,1)S(1)}, bf16[4,2,128,128]{3,2,1,0:T(8,128)(2,1)S(1)}, u32[]{:S(2)}, u32[]{:S(2)}) collective-permute-start(bf16[4,2,128,128]{3,2,1,0:T(8,128)(2,1)S(1)} %collective-permute-done.2.rest_3_), channel_id=1, source_target_pairs={{0,2},{1,3},{2,0},{3,1},{4,6},{5,7},{6,4},{7,5},{8,10},{9,11},{10,... | collective-permute-start | bytes 786440 | tf_op jit(solution)/shard_map/ppermute | solution.py:138
  36.5 8.1 %collective-permute-start.9 = (bf16[4,2,128,128]{3,2,1,0:T(8,128)(2,1)S(1)}, bf16[4,2,128,128]{3,2,1,0:T(8,128)(2,1)S(1)}, u32[]{:S(2)}, u32[]{:S(2)}) collective-permute-start(bf16[4,2,128,128]{3,2,1,0:T(8,128)(2,1)S(1)} %collective-permute-done.4.rest_1_), channel_id=1, source_target_pairs={{0,2},{1,3},{2,0},{3,1},{4,6},{5,7},{6,4},{7,5},{8,10},{9,11},{10,... | collective-permute-start | bytes 786440 | tf_op jit(solution)/shard_map/ppermute | solution.py:138
  37.0 7.6 %collective-permute-start.10 = (bf16[4,2,128,128]{3,2,1,0:T(8,128)(2,1)S(1)}, bf16[4,2,128,128]{3,2,1,0:T(8,128)(2,1)S(1)}, u32[]{:S(2)}, u32[]{:S(2)}) collective-permute-start(bf16[4,2,128,128]{3,2,1,0:T(8,128)(2,1)S(1)} %collective-permute-done.5.rest_2_), channel_id=1, source_target_pairs={{0,2},{1,3},{2,0},{3,1},{4,6},{5,7},{6,4},{7,5},{8,10},{9,11},{10,... | collective-permute-start | bytes 786440 | tf_op jit(solution)/shard_map/ppermute | solution.py:138
  37.0 7.5 %collective-permute-start.8 = (bf16[4,2,128,128]{3,2,1,0:T(8,128)(2,1)S(1)}, bf16[4,2,128,128]{3,2,1,0:T(8,128)(2,1)S(1)}, u32[]{:S(2)}, u32[]{:S(2)}) collective-permute-start(bf16[4,2,128,128]{3,2,1,0:T(8,128)(2,1)S(1)} %collective-permute-done.3.rest_0_), channel_id=1, source_target_pairs={{0,2},{1,3},{2,0},{3,1},{4,6},{5,7},{6,4},{7,5},{8,10},{9,11},{10,... | collective-permute-start | bytes 786440 | tf_op jit(solution)/shard_map/ppermute | solution.py:138
  40.8 6.2 %collective-permute-start.7 = (bf16[4,2,128,128]{3,2,1,0:T(8,128)(2,1)S(1)}, bf16[4,2,128,128]{3,2,1,0:T(8,128)(2,1)S(1)}, u32[]{:S(2)}, u32[]{:S(2)}) collective-permute-start(bf16[4,2,128,128]{3,2,1,0:T(8,128)(2,1)S(1)} %collective-permute-done.6.rest_0_), channel_id=1, source_target_pairs={{0,2},{1,3},{2,0},{3,1},{4,6},{5,7},{6,4},{7,5},{8,10},{9,11},{10,... | collective-permute-start | bytes 786440 | tf_op jit(solution)/shard_map/ppermute | solution.py:138

commit v9 on v8

--- a/solution.py
+++ b/solution.py
@@ -10,6 +10,7 @@
 
 SEATS = 16
 SUB = 8
+FLOOR = 100
 
 
 def axes(core, cols):
@@ -104,13 +105,49 @@
     )(*operands)
 
 
+def code_kernel(acc_ref, out_ref):
+    tiles = acc_ref.shape[1]
+    extra = 24 // tiles
+    half = 1 << (15 + extra)
+    for d in range(acc_ref.shape[0]):
+        values = [acc_ref[d, t] for t in range(tiles)]
+        left = functools.reduce(jnp.maximum, [jnp.abs(value) for value in values]) * 2.0**FLOOR
+        scale = jnp.full(left.shape, 2.0 ** (FLOOR - 1) * half, jnp.float32)
+        last = jnp.zeros(left.shape, jnp.int32)
+        for i in reversed(range(7)):
+            big = left >= 2.0 ** (1 << i)
+            down = jnp.where(big, 2.0 ** -(1 << i), 1.0)
+            left, scale = left * down, scale * down
+            last = jnp.where(big, last + (1 << i), last)
+        low = []
+        for t, value in enumerate(values):
+            whole = jnp.floor(value * scale + 0.5).astype(jnp.int32)
+            whole = jnp.minimum(whole, half - 1) + half
+            low.append(whole & 0xFFFF)
+            last = last | ((whole >> 16) << (8 + extra * t))
+        for j in range(tiles // 2):
+            out_ref[d, j] = low[2 * j] | (low[2 * j + 1] << 16)
+        out_ref[d, tiles // 2] = last
+
+
 def finish_kernel(x_ref, out_ref):
-    planes, seats, tiles, strip, extent = x_ref.shape
+    planes, seats, words, strip, extent = x_ref.shape
+    tiles = 2 * (words - 1)
+    extra = 24 // tiles
+    half = 1 << (15 + extra)
+    wholes = [None] * tiles
+    for z in range(planes):
+        last = x_ref[z, :, words - 1]
+        scale = jnp.full(last.shape, 2.0 ** (1 - FLOOR) / half, jnp.float32)
+        for i in range(7):
+            scale = scale * jnp.where((last >> i) & 1 == 1, 2.0 ** (1 << i), 1.0)
+        for t in range(tiles):
+            whole = (x_ref[z, :, t // 2] >> (16 * (t % 2))) & 0xFFFF
+            whole = whole | (((last >> (8 + extra * t)) & ((1 << extra) - 1)) << 16)
+            value = (whole - half).astype(jnp.float32) * scale
+            wholes[t] = value if z == 0 else wholes[t] + value
     for t in range(tiles):
-        whole = x_ref[0, :, t]
-        for z in range(1, planes):
-            whole = whole + x_ref[z, :, t]
-        out_ref[:, t * extent:(t + 1) * extent] = whole.reshape(seats * strip, extent).T
+        out_ref[:, t * extent:(t + 1) * extent] = wholes[t].reshape(seats * strip, extent).T
 
 
 def body(p_tiles, p_cols, q_tiles, q_cols):
@@ -148,18 +185,26 @@
     q_here, *second = lax.optimization_barrier((q_here, *second))
     third = along(second[0], 2)
     acc = add(None, sets, [(step, swapped) for swapped in (0, 1) for step in range(4)])
+    third, acc = lax.optimization_barrier((third, acc))
     sets = second + [across(each) for each in second]
     acc = add(acc, sets, [(step, swapped) for swapped in (0, 1) for step in (4, 5, 6)])
     acc = add(acc, [third, across(third)], [(7, 0), (7, 1)])
     every = ("plane",) + seat
-    parts = acc.reshape(planes * SEATS, tile_count // cols, strip, extent)
-    landed = lax.all_to_all(parts, every, split_axis=0, concat_axis=0, tiled=True)
+    tiles = tile_count // cols
+    words = tiles // 2 + 1
+    coded = pl.pallas_call(
+        code_kernel,
+        out_shape=jax.ShapeDtypeStruct((planes * SEATS, words, strip, extent), jnp.int32),
+        compiler_params=pltpu.CompilerParams(vmem_limit_bytes=16 << 20),
+        name="code",
+    )(acc.reshape(planes * SEATS, tiles, strip, extent))
+    landed = lax.all_to_all(coded, every, split_axis=0, concat_axis=0, tiled=True)
     return pl.pallas_call(
         finish_kernel,
-        out_shape=jax.ShapeDtypeStruct((extent, tile_count // cols * extent), jnp.float32),
+        out_shape=jax.ShapeDtypeStruct((extent, tiles * extent), jnp.float32),
         compiler_params=pltpu.CompilerParams(vmem_limit_bytes=16 << 20),
         name="turn",
-    )(landed.reshape(planes, SEATS, tile_count // cols, strip, extent))
+    )(landed.reshape(planes, SEATS, words, strip, extent))
 
 
 def solution(mesh):

time: 79.8 us -> 70.1 us (0.88)
  blocking collectives: 29.9 us -> 22.2 us
  waiting for transfers between devices: 21 us -> 17.7 us
  Pallas kernels: 9.84 us -> 11.7 us
    all_to_all x1, blocking collectives: 29.9 us -> 22.2 us  [body(): lax.all_to_all(coded, every, split_axis=0, concat_axis=0, tiled=True)]
    ppermute x7, waiting for transfers between devices: 21 us -> 17.7 us  [along(): return lax.ppermute(values, seat, hops)]
    pallas_call x3, Pallas kernels: 6.53 us -> 7.47 us  [add_products(): pl.pallas_call(functools.partial(product_kernel, tile_count, cols, routes...]
  transfers between devices with their start and end apart: 16 -> 16, of which waited for: 4 -> 3; matrix products, arithmetic and copies ran while one was open for 0% -> 0% of each run, Pallas kernels for 10% -> 12%
where the time goes in v9:
time: 70.1 us; the launch traced here: 69.9 us
  blocking collectives  22.2 us (32%)
  starting transfers between devices  18.2 us (26%)
  waiting for transfers between devices  17.7 us (25%)
  Pallas kernels  11.7 us (17%)
    all_to_all x1, blocking collectives, body(): lax.all_to_all(coded, every, split_axis=0, concat_axis=0, tiled=True)  22.2 us
    ppermute x7, waiting for transfers between devices, along(): return lax.ppermute(values, seat, hops)  17.7 us
    ppermute x7, starting transfers between devices, along(): return lax.ppermute(values, seat, hops)  9.65 us
    pallas_call x3, Pallas kernels, add_products(): pl.pallas_call(functools.partial(product_kernel, tile_count, cols, routes...  7.47 us
    ppermute x8, starting transfers between devices, across(): return lax.ppermute(values, seat, [(s, s ^ cols) for s in range(SEATS)])  4.56 us
    all_to_all x1, starting transfers between devices, body(): lax.all_to_all(sliced, seat, split_axis=0, concat_axis=0, tiled=True)  3.99 us
    pallas_call x1, Pallas kernels, body(): pl.pallas_call(slice_kernel, out_shape=jax.ShapeDtypeStruct((SEATS, heigh...  2.31 us
  transfers between devices with their start and end apart: 16, of which 3 were waited for; matrix products, arithmetic and copies ran while one was open for 0% of the time, Pallas kernels for 12%

profile of v9, /device:TPU:1, one launch (start us, length us, event | category | flops | bytes accessed | tf_op | source)
XLA Modules:
  0.0 69.9 jit_solution(9862696697737948824)
XLA Ops:
  0.0 2.1 %collective-permute-start.2 = (bf16[4,2,128,128]{3,2,1,0:T(8,128)(2,1)}, bf16[4,2,128,128]{3,2,1,0:T(8,128)(2,1)S(1)}, u32[]{:S(2)}, u32[]{:S(2)}) collective-permute-start(bf16[4,2,128,128]{3,2,1,0:T(8,128)(2,1)} %rest_0_.1), channel_id=1, source_target_pairs={{0,8},{1,9},{2,3},{3,2},{4,12},{5,13},{6,7},{7,6},{8,0},{9,1},{10,... | collective-permute-start | bytes 786440 | tf_op jit(solution)/shard_map/ppermute | solution.py:172
  2.1 1.3 %collective-permute-start.1 = (bf16[4,2,128,128]{3,2,1,0:T(8,128)(2,1)}, bf16[4,2,128,128]{3,2,1,0:T(8,128)(2,1)S(1)}, u32[]{:S(2)}, u32[]{:S(2)}) collective-permute-start(bf16[4,2,128,128]{3,2,1,0:T(8,128)(2,1)} %rest_0_.1), channel_id=1, source_target_pairs={{0,4},{1,5},{2,10},{3,11},{4,0},{5,1},{6,14},{7,15},{8,12},{9,13},... | collective-permute-start | bytes 786440 | tf_op jit(solution)/shard_map/ppermute | solution.py:172
  3.4 1.2 %collective-permute-start = (bf16[4,2,128,128]{3,2,1,0:T(8,128)(2,1)}, bf16[4,2,128,128]{3,2,1,0:T(8,128)(2,1)S(1)}, u32[]{:S(2)}, u32[]{:S(2)}) collective-permute-start(bf16[4,2,128,128]{3,2,1,0:T(8,128)(2,1)} %rest_0_.1), channel_id=1, source_target_pairs={{0,1},{1,0},{2,6},{3,7},{4,5},{5,4},{6,2},{7,3},{8,9},{9,8},{10,14... | collective-permute-start | bytes 786440 | tf_op jit(solution)/shard_map/ppermute | solution.py:172
  4.6 2.3 %cut_columns.1 = bf16[16,208,128]{2,1,0:T(8,128)(2,1)} custom-call(s32[2,4]{1,0:T(2,128)} %bitcast.5, s32[4,6]{1,0:T(4,128)} %q_ids.1, bf16[4,6,128,128]{3,2,1,0:T(8,128)(2,1)} %q_ref.1), custom_call_target="tpu_custom_call" | custom-call | bytes 8388608 | tf_op jit(solution)/shard_map/cut_columns/pallas_call | solution.py:162
  6.9 0.0 copy-start
  6.9 0.0 collective-permute-done.2.rest_3_
  6.9 3.2 %collective-permute-done.1.rest_2_ = bf16[4,2,128,128]{3,2,1,0:T(8,128)(2,1)S(1)} collective-permute-done((bf16[4,2,128,128]{3,2,1,0:T(8,128)(2,1)}, bf16[4,2,128,128]{3,2,1,0:T(8,128)(2,1)S(1)}, u32[]{:S(2)}, u32[]{:S(2)}) %collective-permute-start.1) | collective-permute-done | bytes 262176 | tf_op jit(solution)/shard_map/ppermute | solution.py:172
  10.1 1.7 %collective-permute-done.rest_1_ = bf16[4,2,128,128]{3,2,1,0:T(8,128)(2,1)S(1)} collective-permute-done((bf16[4,2,128,128]{3,2,1,0:T(8,128)(2,1)}, bf16[4,2,128,128]{3,2,1,0:T(8,128)(2,1)S(1)}, u32[]{:S(2)}, u32[]{:S(2)}) %collective-permute-start) | collective-permute-done | bytes 262176 | tf_op jit(solution)/shard_map/ppermute | solution.py:172
  11.7 4.0 %all-to-all-start = ((bf16[16,208,128]{2,1,0:T(8,128)(2,1)}), bf16[16,208,128]{2,1,0:T(8,128)(2,1)S(1)}, u32[]{:S(2)}, u32[]{:S(2)}) async-start(bf16[16,208,128]{2,1,0:T(8,128)(2,1)} %cut_columns.1), calls=%async_computation | async-start | bytes 1703936 | tf_op jit(solution)/shard_map/all_to_all | solution.py:182
  15.7 1.4 %collective-permute-start.3 = (bf16[4,2,128,128]{3,2,1,0:T(8,128)(2,1)S(1)}, bf16[4,2,128,128]{3,2,1,0:T(8,128)(2,1)S(1)}, u32[]{:S(2)}, u32[]{:S(2)}) collective-permute-start(bf16[4,2,128,128]{3,2,1,0:T(8,128)(2,1)S(1)} %collective-permute-done.rest_1_), channel_id=1, source_target_pairs={{0,4},{1,5},{2,10},{3,11},{4,0},{5,1},{6,14},{7,15},{8,12},{9,13},... | collective-permute-start | bytes 786440 | tf_op jit(solution)/shard_map/ppermute | solution.py:172
  17.1 1.2 %collective-permute-start.4 = (bf16[4,2,128,128]{3,2,1,0:T(8,128)(2,1)S(1)}, bf16[4,2,128,128]{3,2,1,0:T(8,128)(2,1)S(1)}, u32[]{:S(2)}, u32[]{:S(2)}) collective-permute-start(bf16[4,2,128,128]{3,2,1,0:T(8,128)(2,1)S(1)} %collective-permute-done.1.rest_2_), channel_id=1, source_target_pairs={{0,8},{1,9},{2,3},{3,2},{4,12},{5,13},{6,7},{7,6},{8,0},{9,1},{10,... | collective-permute-start | bytes 786440 | tf_op jit(solution)/shard_map/ppermute | solution.py:172
  18.3 1.2 %collective-permute-start.5 = (bf16[4,2,128,128]{3,2,1,0:T(8,128)(2,1)S(1)}, bf16[4,2,128,128]{3,2,1,0:T(8,128)(2,1)S(1)}, u32[]{:S(2)}, u32[]{:S(2)}) collective-permute-start(bf16[4,2,128,128]{3,2,1,0:T(8,128)(2,1)S(1)} %collective-permute-done.2.rest_3_), channel_id=1, source_target_pairs={{0,1},{1,0},{2,6},{3,7},{4,5},{5,4},{6,2},{7,3},{8,9},{9,8},{10,14... | collective-permute-start | bytes 786440 | tf_op jit(solution)/shard_map/ppermute | solution.py:172
  19.5 0.0 copy-done
  19.6 1.2 %collective-permute-start.7 = (bf16[4,2,128,128]{3,2,1,0:T(8,128)(2,1)S(1)}, bf16[4,2,128,128]{3,2,1,0:T(8,128)(2,1)S(1)}, u32[]{:S(2)}, u32[]{:S(2)}) collective-permute-start(bf16[4,2,128,128]{3,2,1,0:T(8,128)(2,1)S(1)} %copy-done), channel_id=1, source_target_pairs={{0,2},{1,3},{2,0},{3,1},{4,6},{5,7},{6,4},{7,5},{8,10},{9,11},{10,... | collective-permute-start | bytes 786440 | tf_op jit(solution)/shard_map/ppermute | solution.py:175
  20.8 0.0 collective-permute-start.8
  20.8 12.8 %collective-permute-done.3.rest_0_ = bf16[4,2,128,128]{3,2,1,0:T(8,128)(2,1)S(1)} collective-permute-done((bf16[4,2,128,128]{3,2,1,0:T(8,128)(2,1)S(1)}, bf16[4,2,128,128]{3,2,1,0:T(8,128)(2,1)S(1)}, u32[]{:S(2)}, u32[]{:S(2)}) %collective-permute-start.3) | collective-permute-done | bytes 262176 | tf_op jit(solution)/shard_map/ppermute | solution.py:172
  33.6 1.6 %collective-permute-start.9 = (bf16[4,2,128,128]{3,2,1,0:T(8,128)(2,1)S(1)}, bf16[4,2,128,128]{3,2,1,0:T(8,128)(2,1)S(1)}, u32[]{:S(2)}, u32[]{:S(2)}) collective-permute-start(bf16[4,2,128,128]{3,2,1,0:T(8,128)(2,1)S(1)} %collective-permute-done.1.rest_2_), channel_id=1, source_target_pairs={{0,2},{1,3},{2,0},{3,1},{4,6},{5,7},{6,4},{7,5},{8,10},{9,11},{10,... | collective-permute-start | bytes 786440 | tf_op jit(solution)/shard_map/ppermute | solution.py:175
  35.2 0.0 collective-permute-done.4.rest_1_
  35.2 0.0 collective-permute-start.10
  35.2 0.0 collective-permute-done.5.rest_2_
  35.2 0.0 all-to-all-done.q_ref
  35.2 1.3 %collective-permute-start.6 = (bf16[4,2,128,128]{3,2,1,0:T(8,128)(2,1)S(1)}, bf16[4,2,128,128]{3,2,1,0:T(8,128)(2,1)S(1)}, u32[]{:S(2)}, u32[]{:S(2)}) collective-permute-start(bf16[4,2,128,128]{3,2,1,0:T(8,128)(2,1)S(1)} %collective-permute-done.3.rest_0_), channel_id=1, source_target_pairs={{0,8},{1,9},{2,3},{3,2},{4,12},{5,13},{6,7},{7,6},{8,0},{9,1},{10,... | collective-permute-start | bytes 786440 | tf_op jit(solution)/shard_map/ppermute | solution.py:172
  36.5 0.0 collective-permute-done.7.rest_4_
  36.5 0.2 collective-permute-start.12
  36.7 0.0 collective-permute-done.8.rest_5_
  36.7 0.3 collective-permute-start.13
  37.0 0.0 collective-permute-done.9.rest_6_
  37.0 0.2 collective-permute-start.14
  37.2 0.0 collective-permute-done.10.rest_7_
  37.2 3.9 %products.3.rest_6_ = f32[256,8,128]{2,1,0:T(8,128)S(1)} custom-call(bf16[16,208,128]{2,1,0:T(8,128)(2,1)S(1)} %all-to-all-done.q_ref, bf16[4,2,128,128]{3,2,1,0:T(8,128)(2,1)S(1)} %copy-done, bf16[4,2,128,128]{3,2,1,0:T(8,128)(2,1)S(1)} %collective-permute-done.rest_1_, bf16[4,2,128,128]{3,2,1,0:T(8,128)(2,1)S(1)} %collective-permute-done.1.rest_2_, ...), custom_call_target="tpu_custom_call" | custom-call | flops 100663296 | bytes 8388608 | tf_op jit(solution)/shard_map/products/pallas_call | solution.py:87
  41.1 0.0 collective-permute-done.6.rest_0_
  41.1 1.0 %collective-permute-start.11 = (bf16[4,2,128,128]{3,2,1,0:T(8,128)(2,1)S(1)}, bf16[4,2,128,128]{3,2,1,0:T(8,128)(2,1)S(1)}, u32[]{:S(2)}, u32[]{:S(2)}) collective-permute-start(bf16[4,2,128,128]{3,2,1,0:T(8,128)(2,1)S(1)} %collective-permute-done.6.rest_0_), channel_id=1, source_target_pairs={{0,2},{1,3},{2,0},{3,1},{4,6},{5,7},{6,4},{7,5},{8,10},{9,11},{10,... | collective-permute-start | bytes 786440 | tf_op jit(solution)/shard_map/ppermute | solution.py:175
  42.1 0.0 collective-permute-done.13.rest_4_
  42.1 0.0 collective-permute-done.14.rest_5_
  42.1 0.0 collective-permute-done.12.rest_3_
  42.1 2.3 %products.4.rest_2_ = f32[256,8,128]{2,1,0:T(8,128)S(1)} custom-call(bf16[16,208,128]{2,1,0:T(8,128)(2,1)S(1)} %all-to-all-done.q_ref, bf16[4,2,128,128]{3,2,1,0:T(8,128)(2,1)S(1)} %collective-permute-done.3.rest_0_, bf16[4,2,128,128]{3,2,1,0:T(8,128)(2,1)S(1)} %collective-permute-done.4.rest_1_, ...), custom_call_target="tpu_custom_call", output_to_operand_aliasing={{}: (7, {})} | custom-call | flops 75497472 | bytes 6291456 | tf_op jit(solution)/shard_map/products/pallas_call | solution.py:87
  44.4 0.0 collective-permute-done.11.rest_1_
  44.4 1.3 %products.5 = f32[256,8,128]{2,1,0:T(8,128)S(1)} custom-call(bf16[16,208,128]{2,1,0:T(8,128)(2,1)S(1)} %all-to-all-done.q_ref, bf16[4,2,128,128]{3,2,1,0:T(8,128)(2,1)S(1)} %collective-permute-done.6.rest_0_, bf16[4,2,128,128]{3,2,1,0:T(8,128)(2,1)S(1)} %collective-permute-done.11.rest_1_, ...), custom_call_target="tpu_custom_call", output_to_operand_aliasing={{}: (3, {})} | custom-call | flops 25165824 | bytes 2097152 | tf_op jit(solution)/shard_map/products/pallas_call | solution.py:87
  45.7 0.6 code.1
  46.4 22.2 %all_to_all.10 = s32[32,5,8,128]{3,2,1,0:T(8,128)S(1)} all-to-all(s32[32,5,8,128]{3,2,1,0:T(8,128)S(1)} %code.1), channel_id=1, replica_groups=mesh['plane'=2,'pair'=4,'core'=2,'col'=2] {'plane','pair','core','col'}, dimensions={0} | all-to-all | bytes 1310720 | tf_op jit(solution)/shard_map/all_to_all | solution.py:201
  68.6 1.3 %turn.1 = f32[128,1024]{1,0:T(8,128)} custom-call(s32[2,16,5,8,128]{4,3,2,1,0:T(8,128)S(1)} %bitcast.4), custom_call_target="tpu_custom_call" | custom-call | tf_op jit(solution)/shard_map/turn/pallas_call | solution.py:202
Async XLA Ops:
  0.0 6.9 %collective-permute-start.2 = (bf16[4,2,128,128]{3,2,1,0:T(8,128)(2,1)}, bf16[4,2,128,128]{3,2,1,0:T(8,128)(2,1)S(1)}, u32[]{:S(2)}, u32[]{:S(2)}) collective-permute-start(bf16[4,2,128,128]{3,2,1,0:T(8,128)(2,1)} %rest_0_.1), channel_id=1, source_target_pairs={{0,8},{1,9},{2,3},{3,2},{4,12},{5,13},{6,7},{7,6},{8,0},{9,1},{10,... | collective-permute-start | bytes 786440 | tf_op jit(solution)/shard_map/ppermute | solution.py:172
  2.1 8.0 %collective-permute-start.1 = (bf16[4,2,128,128]{3,2,1,0:T(8,128)(2,1)}, bf16[4,2,128,128]{3,2,1,0:T(8,128)(2,1)S(1)}, u32[]{:S(2)}, u32[]{:S(2)}) collective-permute-start(bf16[4,2,128,128]{3,2,1,0:T(8,128)(2,1)} %rest_0_.1), channel_id=1, source_target_pairs={{0,4},{1,5},{2,10},{3,11},{4,0},{5,1},{6,14},{7,15},{8,12},{9,13},... | collective-permute-start | bytes 786440 | tf_op jit(solution)/shard_map/ppermute | solution.py:172
  3.4 8.4 %collective-permute-start = (bf16[4,2,128,128]{3,2,1,0:T(8,128)(2,1)}, bf16[4,2,128,128]{3,2,1,0:T(8,128)(2,1)S(1)}, u32[]{:S(2)}, u32[]{:S(2)}) collective-permute-start(bf16[4,2,128,128]{3,2,1,0:T(8,128)(2,1)} %rest_0_.1), channel_id=1, source_target_pairs={{0,1},{1,0},{2,6},{3,7},{4,5},{5,4},{6,2},{7,3},{8,9},{9,8},{10,14... | collective-permute-start | bytes 786440 | tf_op jit(solution)/shard_map/ppermute | solution.py:172
  6.9 12.7 %copy-start = (bf16[4,2,128,128]{3,2,1,0:T(8,128)(2,1)S(1)}, bf16[4,2,128,128]{3,2,1,0:T(8,128)(2,1)}, u32[]{:S(2)}) copy-start(bf16[4,2,128,128]{3,2,1,0:T(8,128)(2,1)} %rest_0_.1) | copy-start | bytes 786436
  11.7 23.5 %all-to-all-start = ((bf16[16,208,128]{2,1,0:T(8,128)(2,1)}), bf16[16,208,128]{2,1,0:T(8,128)(2,1)S(1)}, u32[]{:S(2)}, u32[]{:S(2)}) async-start(bf16[16,208,128]{2,1,0:T(8,128)(2,1)} %cut_columns.1), calls=%async_computation | async-start | bytes 1703936 | tf_op jit(solution)/shard_map/all_to_all | solution.py:182
  15.7 17.9 %collective-permute-start.3 = (bf16[4,2,128,128]{3,2,1,0:T(8,128)(2,1)S(1)}, bf16[4,2,128,128]{3,2,1,0:T(8,128)(2,1)S(1)}, u32[]{:S(2)}, u32[]{:S(2)}) collective-permute-start(bf16[4,2,128,128]{3,2,1,0:T(8,128)(2,1)S(1)} %collective-permute-done.rest_1_), channel_id=1, source_target_pairs={{0,4},{1,5},{2,10},{3,11},{4,0},{5,1},{6,14},{7,15},{8,12},{9,13},... | collective-permute-start | bytes 786440 | tf_op jit(solution)/shard_map/ppermute | solution.py:172
  17.1 18.0 %collective-permute-start.4 = (bf16[4,2,128,128]{3,2,1,0:T(8,128)(2,1)S(1)}, bf16[4,2,128,128]{3,2,1,0:T(8,128)(2,1)S(1)}, u32[]{:S(2)}, u32[]{:S(2)}) collective-permute-start(bf16[4,2,128,128]{3,2,1,0:T(8,128)(2,1)S(1)} %collective-permute-done.1.rest_2_), channel_id=1, source_target_pairs={{0,8},{1,9},{2,3},{3,2},{4,12},{5,13},{6,7},{7,6},{8,0},{9,1},{10,... | collective-permute-start | bytes 786440 | tf_op jit(solution)/shard_map/ppermute | solution.py:172
  18.3 16.9 %collective-permute-start.5 = (bf16[4,2,128,128]{3,2,1,0:T(8,128)(2,1)S(1)}, bf16[4,2,128,128]{3,2,1,0:T(8,128)(2,1)S(1)}, u32[]{:S(2)}, u32[]{:S(2)}) collective-permute-start(bf16[4,2,128,128]{3,2,1,0:T(8,128)(2,1)S(1)} %collective-permute-done.2.rest_3_), channel_id=1, source_target_pairs={{0,1},{1,0},{2,6},{3,7},{4,5},{5,4},{6,2},{7,3},{8,9},{9,8},{10,14... | collective-permute-start | bytes 786440 | tf_op jit(solution)/shard_map/ppermute | solution.py:172
  19.6 16.9 %collective-permute-start.7 = (bf16[4,2,128,128]{3,2,1,0:T(8,128)(2,1)S(1)}, bf16[4,2,128,128]{3,2,1,0:T(8,128)(2,1)S(1)}, u32[]{:S(2)}, u32[]{:S(2)}) collective-permute-start(bf16[4,2,128,128]{3,2,1,0:T(8,128)(2,1)S(1)} %copy-done), channel_id=1, source_target_pairs={{0,2},{1,3},{2,0},{3,1},{4,6},{5,7},{6,4},{7,5},{8,10},{9,11},{10,... | collective-permute-start | bytes 786440 | tf_op jit(solution)/shard_map/ppermute | solution.py:175
  20.8 15.9 %collective-permute-start.8 = (bf16[4,2,128,128]{3,2,1,0:T(8,128)(2,1)S(1)}, bf16[4,2,128,128]{3,2,1,0:T(8,128)(2,1)S(1)}, u32[]{:S(2)}, u32[]{:S(2)}) collective-permute-start(bf16[4,2,128,128]{3,2,1,0:T(8,128)(2,1)S(1)} %collective-permute-done.rest_1_), channel_id=1, source_target_pairs={{0,2},{1,3},{2,0},{3,1},{4,6},{5,7},{6,4},{7,5},{8,10},{9,11},{10,... | collective-permute-start | bytes 786440 | tf_op jit(solution)/shard_map/ppermute | solution.py:175
  33.6 3.4 %collective-permute-start.9 = (bf16[4,2,128,128]{3,2,1,0:T(8,128)(2,1)S(1)}, bf16[4,2,128,128]{3,2,1,0:T(8,128)(2,1)S(1)}, u32[]{:S(2)}, u32[]{:S(2)}) collective-permute-start(bf16[4,2,128,128]{3,2,1,0:T(8,128)(2,1)S(1)} %collective-permute-done.1.rest_2_), channel_id=1, source_target_pairs={{0,2},{1,3},{2,0},{3,1},{4,6},{5,7},{6,4},{7,5},{8,10},{9,11},{10,... | collective-permute-start | bytes 786440 | tf_op jit(solution)/shard_map/ppermute | solution.py:175
  35.2 2.0 %collective-permute-start.10 = (bf16[4,2,128,128]{3,2,1,0:T(8,128)(2,1)S(1)}, bf16[4,2,128,128]{3,2,1,0:T(8,128)(2,1)}, u32[]{:S(2)}, u32[]{:S(2)}) collective-permute-start(bf16[4,2,128,128]{3,2,1,0:T(8,128)(2,1)S(1)} %collective-permute-done.2.rest_3_), channel_id=1, source_target_pairs={{0,2},{1,3},{2,0},{3,1},{4,6},{5,7},{6,4},{7,5},{8,10},{9,11},{10,... | collective-permute-start | bytes 786440 | tf_op jit(solution)/shard_map/ppermute | solution.py:175
  35.2 5.8 %collective-permute-start.6 = (bf16[4,2,128,128]{3,2,1,0:T(8,128)(2,1)S(1)}, bf16[4,2,128,128]{3,2,1,0:T(8,128)(2,1)S(1)}, u32[]{:S(2)}, u32[]{:S(2)}) collective-permute-start(bf16[4,2,128,128]{3,2,1,0:T(8,128)(2,1)S(1)} %collective-permute-done.3.rest_0_), channel_id=1, source_target_pairs={{0,8},{1,9},{2,3},{3,2},{4,12},{5,13},{6,7},{7,6},{8,0},{9,1},{10,... | collective-permute-start | bytes 786440 | tf_op jit(solution)/shard_map/ppermute | solution.py:172
  36.5 5.6 %collective-permute-start.12 = (bf16[4,2,128,128]{3,2,1,0:T(8,128)(2,1)S(1)}, bf16[4,2,128,128]{3,2,1,0:T(8,128)(2,1)S(1)}, u32[]{:S(2)}, u32[]{:S(2)}) collective-permute-start(bf16[4,2,128,128]{3,2,1,0:T(8,128)(2,1)S(1)} %collective-permute-done.3.rest_0_), channel_id=1, source_target_pairs={{0,2},{1,3},{2,0},{3,1},{4,6},{5,7},{6,4},{7,5},{8,10},{9,11},{10,... | collective-permute-start | bytes 786440 | tf_op jit(solution)/shard_map/ppermute | solution.py:175
  36.7 5.4 %collective-permute-start.13 = (bf16[4,2,128,128]{3,2,1,0:T(8,128)(2,1)S(1)}, bf16[4,2,128,128]{3,2,1,0:T(8,128)(2,1)S(1)}, u32[]{:S(2)}, u32[]{:S(2)}) collective-permute-start(bf16[4,2,128,128]{3,2,1,0:T(8,128)(2,1)S(1)} %collective-permute-done.4.rest_1_), channel_id=1, source_target_pairs={{0,2},{1,3},{2,0},{3,1},{4,6},{5,7},{6,4},{7,5},{8,10},{9,11},{10,... | collective-permute-start | bytes 786440 | tf_op jit(solution)/shard_map/ppermute | solution.py:175
  37.0 5.1 %collective-permute-start.14 = (bf16[4,2,128,128]{3,2,1,0:T(8,128)(2,1)S(1)}, bf16[4,2,128,128]{3,2,1,0:T(8,128)(2,1)S(1)}, u32[]{:S(2)}, u32[]{:S(2)}) collective-permute-start(bf16[4,2,128,128]{3,2,1,0:T(8,128)(2,1)S(1)} %collective-permute-done.5.rest_2_), channel_id=1, source_target_pairs={{0,2},{1,3},{2,0},{3,1},{4,6},{5,7},{6,4},{7,5},{8,10},{9,11},{10,... | collective-permute-start | bytes 786440 | tf_op jit(solution)/shard_map/ppermute | solution.py:175
  41.1 3.4 %collective-permute-start.11 = (bf16[4,2,128,128]{3,2,1,0:T(8,128)(2,1)S(1)}, bf16[4,2,128,128]{3,2,1,0:T(8,128)(2,1)S(1)}, u32[]{:S(2)}, u32[]{:S(2)}) collective-permute-start(bf16[4,2,128,128]{3,2,1,0:T(8,128)(2,1)S(1)} %collective-permute-done.6.rest_0_), channel_id=1, source_target_pairs={{0,2},{1,3},{2,0},{3,1},{4,6},{5,7},{6,4},{7,5},{8,10},{9,11},{10,... | collective-permute-start | bytes 786440 | tf_op jit(solution)/shard_map/ppermute | solution.py:175

commit v10 on v9

--- a/solution.py
+++ b/solution.py
@@ -50,9 +50,10 @@
         out_ref[j, blocks * rows:] = ids
 
 
-def product_kernel(tile_count, cols, routes, q_ref, *rest):
+def product_kernel(tile_count, cols, routes, first, coded, q_ref, *rest):
     count = len(routes)
-    p_refs, (acc_ref, wide_ids, ids, id_sem) = rest[:count], rest[-4:]
+    p_refs, (out_ref, wide_ids, ids, id_sem, *sums) = rest[:count], rest[count + (not first):]
+    acc_ref = sums[0] if coded else out_ref
     blocks, per_p, extent, _ = p_refs[0].shape
     strip = acc_ref.shape[1]
     rows = (q_ref.shape[1] - 2 * SUB) // blocks
@@ -61,7 +62,7 @@
         wide_ids[s:s + 1] = q_ref[s, blocks * rows:, :].astype(jnp.int32)[:1]
     id_copy = pltpu.make_async_copy(wide_ids, ids, id_sem)
     id_copy.start()
-    if len(rest) == count + 4:
+    if first:
         acc_ref[...] = jnp.zeros_like(acc_ref)
     else:
         acc_ref[...] = rest[count][...]
@@ -71,46 +72,53 @@
         seat = origin(*routes[i], here, cols)
         for f in range(blocks):
             left = q_ref[seat, f * rows:(f + 1) * rows]
-            first = f * (per_p + per_q)
+            start = f * (per_p + per_q)
             for k in range(per_p):
                 product = jnp.dot(left, p_refs[i][f, k], preferred_element_type=jnp.float32)
-                base = ids[seat, first + k] * tile_count
+                base = ids[seat, start + k] * tile_count
                 for l in range(per_q):
-                    spot = base + ids[seat, first + per_p + l]
+                    spot = base + ids[seat, start + per_p + l]
                     acc_ref[spot] += product[l * strip:(l + 1) * strip]
-
-
-def add_products(q_here, sets, routes, acc, tile_count, cols, strip):
+    if coded:
+        code(acc_ref, out_ref, tile_count // cols)
+
+
+def add_products(q_here, sets, routes, acc, tile_count, cols, coded=False):
     per_p, extent = sets[0].shape[1:3]
+    rows = q_here.shape[1] - 2 * SUB
+    sums = jax.ShapeDtypeStruct((tile_count * tile_count, extent // SEATS, extent), jnp.float32)
+    made = sums
+    if coded:
+        shape = (tile_count * cols, tile_count // cols // 2 + 1) + sums.shape[1:]
+        made = jax.ShapeDtypeStruct(shape, jnp.int32)
     operands = [q_here, *sets] + ([] if acc is None else [acc])
-    rows = q_here.shape[1] - 2 * SUB
     return pl.pallas_call(
-        functools.partial(product_kernel, tile_count, cols, routes),
-        out_shape=jax.ShapeDtypeStruct((tile_count * tile_count, strip, extent), jnp.float32),
+        functools.partial(product_kernel, tile_count, cols, routes, acc is None, coded),
+        out_shape=made,
         in_specs=[pl.BlockSpec(memory_space=pltpu.VMEM)] * len(operands),
         out_specs=pl.BlockSpec(memory_space=pltpu.VMEM),
         scratch_shapes=[
             pltpu.VMEM((SEATS, extent), jnp.int32),
             pltpu.SMEM((SEATS, extent), jnp.int32),
             pltpu.SemaphoreType.DMA,
-        ],
-        input_output_aliases={} if acc is None else {len(operands) - 1: 0},
+        ]
+        + [pltpu.VMEM(sums.shape, sums.dtype)] * coded,
+        input_output_aliases={} if acc is None or coded else {len(operands) - 1: 0},
         cost_estimate=pl.CostEstimate(
             flops=2 * len(sets) * per_p * rows * extent * extent,
             bytes_accessed=len(sets) * (1 << 20),
             transcendentals=0,
         ),
-        compiler_params=pltpu.CompilerParams(vmem_limit_bytes=16 << 20),
+        compiler_params=pltpu.CompilerParams(vmem_limit_bytes=24 << 20),
         name="products",
     )(*operands)
 
 
-def code_kernel(acc_ref, out_ref):
-    tiles = acc_ref.shape[1]
+def code(acc_ref, out_ref, tiles):
     extra = 24 // tiles
     half = 1 << (15 + extra)
-    for d in range(acc_ref.shape[0]):
-        values = [acc_ref[d, t] for t in range(tiles)]
+    for d in range(out_ref.shape[0]):
+        values = [acc_ref[d * tiles + t] for t in range(tiles)]
         left = functools.reduce(jnp.maximum, [jnp.abs(value) for value in values]) * 2.0**FLOOR
         scale = jnp.full(left.shape, 2.0 ** (FLOOR - 1) * half, jnp.float32)
         last = jnp.zeros(left.shape, jnp.int32)
@@ -174,37 +182,34 @@
     def across(values):
         return lax.ppermute(values, seat, [(s, s ^ cols) for s in range(SEATS)])
 
-    def add(acc, sets, routes):
-        return add_products(q_here, sets, routes, acc, tile_count, cols, strip)
+    def add(acc, sets, routes, coded=False):
+        return add_products(q_here, sets, routes, acc, tile_count, cols, coded)
 
     first = [along(p_tiles, step) for step in range(3)]
     sliced, *first = lax.optimization_barrier((sliced, *first))
     q_here = lax.all_to_all(sliced, seat, split_axis=0, concat_axis=0, tiled=True)
     second = [along(first[step], (step + 1) % 3) for step in range(3)]
-    sets = [p_tiles] + first + [across(each) for each in [p_tiles] + first]
-    q_here, *second = lax.optimization_barrier((q_here, *second))
+    crossed = [across(each) for each in [p_tiles] + first]
+    q_here, second, crossed = lax.optimization_barrier((q_here, second, crossed))
     third = along(second[0], 2)
-    acc = add(None, sets, [(step, swapped) for swapped in (0, 1) for step in range(4)])
+    acc = add(
+        None,
+        [p_tiles] + first + crossed,
+        [(step, swapped) for swapped in (0, 1) for step in range(4)],
+    )
     third, acc = lax.optimization_barrier((third, acc))
     sets = second + [across(each) for each in second]
     acc = add(acc, sets, [(step, swapped) for swapped in (0, 1) for step in (4, 5, 6)])
-    acc = add(acc, [third, across(third)], [(7, 0), (7, 1)])
+    coded = add(acc, [third, across(third)], [(7, 0), (7, 1)], coded=True)
     every = ("plane",) + seat
     tiles = tile_count // cols
-    words = tiles // 2 + 1
-    coded = pl.pallas_call(
-        code_kernel,
-        out_shape=jax.ShapeDtypeStruct((planes * SEATS, words, strip, extent), jnp.int32),
-        compiler_params=pltpu.CompilerParams(vmem_limit_bytes=16 << 20),
-        name="code",
-    )(acc.reshape(planes * SEATS, tiles, strip, extent))
     landed = lax.all_to_all(coded, every, split_axis=0, concat_axis=0, tiled=True)
     return pl.pallas_call(
         finish_kernel,
         out_shape=jax.ShapeDtypeStruct((extent, tiles * extent), jnp.float32),
         compiler_params=pltpu.CompilerParams(vmem_limit_bytes=16 << 20),
         name="turn",
-    )(landed.reshape(planes, SEATS, words, strip, extent))
+    )(landed.reshape((planes, SEATS) + landed.shape[1:]))
 
 
 def solution(mesh):

time: 70.1 us -> 70.3 us (level)
  local copies, waits for them, and re-layouts: 0.01 us -> 1.65 us
  starting transfers between devices: 18.2 us -> 17.1 us
  Pallas kernels: 11.7 us -> 10.7 us
    unnamed x2 -> x6, local copies, waits for them, and re-layouts: 0.01 us -> 1.65 us
    ppermute x7, starting transfers between devices: 9.65 us -> 8.72 us  [along(): return lax.ppermute(values, seat, hops)]
  transfers between devices with their start and end apart: 16 -> 16, of which waited for: 3 -> 3; matrix products, arithmetic and copies ran while one was open for 0% -> 0% of each run, Pallas kernels for 12% -> 11%
where the time goes in v10:
time: 70.3 us; the launch traced here: 70 us
  blocking collectives  22.2 us (32%)
  waiting for transfers between devices  18.2 us (26%)
  starting transfers between devices  17.1 us (24%)
  Pallas kernels  10.7 us (15%)
  local copies, waits for them, and re-layouts  1.65 us (2%)
    all_to_all x1, blocking collectives, body(): lax.all_to_all(coded, every, split_axis=0, concat_axis=0, tiled=True)  22.2 us
    ppermute x7, waiting for transfers between devices, along(): return lax.ppermute(values, seat, hops)  18.2 us
    ppermute x7, starting transfers between devices, along(): return lax.ppermute(values, seat, hops)  8.72 us
    pallas_call x3, Pallas kernels, add_products(): pl.pallas_call(functools.partial(product_kernel, tile_count, cols, routes...  7.14 us
    ppermute x8, starting transfers between devices, across(): return lax.ppermute(values, seat, [(s, s ^ cols) for s in range(SEATS)])  4.42 us
    all_to_all x1, starting transfers between devices, body(): lax.all_to_all(sliced, seat, split_axis=0, concat_axis=0, tiled=True)  3.99 us
    pallas_call x1, Pallas kernels, body(): pl.pallas_call(slice_kernel, out_shape=jax.ShapeDtypeStruct((SEATS, heigh...  2.32 us
    unnamed x6, local copies, waits for them, and re-layouts  1.65 us
  transfers between devices with their start and end apart: 16, of which 3 were waited for; matrix products, arithmetic and copies ran while one was open for 0% of the time, Pallas kernels for 11%

profile of v10, /device:TPU:1, one launch (start us, length us, event | category | flops | bytes accessed | tf_op | source)
XLA Modules:
  0.0 70.0 jit_solution(14892311565628228361)
XLA Ops:
  0.0 2.1 %collective-permute-start.2 = (bf16[4,2,128,128]{3,2,1,0:T(8,128)(2,1)}, bf16[4,2,128,128]{3,2,1,0:T(8,128)(2,1)S(1)}, u32[]{:S(2)}, u32[]{:S(2)}) collective-permute-start(bf16[4,2,128,128]{3,2,1,0:T(8,128)(2,1)} %rest_0_.1), channel_id=1, source_target_pairs={{0,8},{1,9},{2,3},{3,2},{4,12},{5,13},{6,7},{7,6},{8,0},{9,1},{10,... | collective-permute-start | bytes 786440 | tf_op jit(solution)/shard_map/ppermute | solution.py:180
  2.1 1.3 %collective-permute-start.1 = (bf16[4,2,128,128]{3,2,1,0:T(8,128)(2,1)}, bf16[4,2,128,128]{3,2,1,0:T(8,128)(2,1)S(1)}, u32[]{:S(2)}, u32[]{:S(2)}) collective-permute-start(bf16[4,2,128,128]{3,2,1,0:T(8,128)(2,1)} %rest_0_.1), channel_id=1, source_target_pairs={{0,4},{1,5},{2,10},{3,11},{4,0},{5,1},{6,14},{7,15},{8,12},{9,13},... | collective-permute-start | bytes 786440 | tf_op jit(solution)/shard_map/ppermute | solution.py:180
  3.4 1.2 %collective-permute-start = (bf16[4,2,128,128]{3,2,1,0:T(8,128)(2,1)}, bf16[4,2,128,128]{3,2,1,0:T(8,128)(2,1)S(1)}, u32[]{:S(2)}, u32[]{:S(2)}) collective-permute-start(bf16[4,2,128,128]{3,2,1,0:T(8,128)(2,1)} %rest_0_.1), channel_id=1, source_target_pairs={{0,1},{1,0},{2,6},{3,7},{4,5},{5,4},{6,2},{7,3},{8,9},{9,8},{10,14... | collective-permute-start | bytes 786440 | tf_op jit(solution)/shard_map/ppermute | solution.py:180
  4.6 2.3 %cut_columns.1 = bf16[16,208,128]{2,1,0:T(8,128)(2,1)} custom-call(s32[2,4]{1,0:T(2,128)} %bitcast.3, s32[4,6]{1,0:T(4,128)} %q_ids.1, bf16[4,6,128,128]{3,2,1,0:T(8,128)(2,1)} %q_ref.1), custom_call_target="tpu_custom_call" | custom-call | bytes 8388608 | tf_op jit(solution)/shard_map/cut_columns/pallas_call | solution.py:170
  6.9 0.0 copy-start
  6.9 0.0 collective-permute-done.2.rest_3_
  6.9 3.1 %collective-permute-done.1.rest_2_ = bf16[4,2,128,128]{3,2,1,0:T(8,128)(2,1)S(1)} collective-permute-done((bf16[4,2,128,128]{3,2,1,0:T(8,128)(2,1)}, bf16[4,2,128,128]{3,2,1,0:T(8,128)(2,1)S(1)}, u32[]{:S(2)}, u32[]{:S(2)}) %collective-permute-start.1) | collective-permute-done | bytes 262176 | tf_op jit(solution)/shard_map/ppermute | solution.py:180
  10.1 1.7 %collective-permute-done.rest_1_ = bf16[4,2,128,128]{3,2,1,0:T(8,128)(2,1)S(1)} collective-permute-done((bf16[4,2,128,128]{3,2,1,0:T(8,128)(2,1)}, bf16[4,2,128,128]{3,2,1,0:T(8,128)(2,1)S(1)}, u32[]{:S(2)}, u32[]{:S(2)}) %collective-permute-start) | collective-permute-done | bytes 262176 | tf_op jit(solution)/shard_map/ppermute | solution.py:180
  11.7 4.0 %all-to-all-start = ((bf16[16,208,128]{2,1,0:T(8,128)(2,1)}), bf16[16,208,128]{2,1,0:T(8,128)(2,1)S(1)}, u32[]{:S(2)}, u32[]{:S(2)}) async-start(bf16[16,208,128]{2,1,0:T(8,128)(2,1)} %cut_columns.1), calls=%async_computation | async-start | bytes 1703936 | tf_op jit(solution)/shard_map/all_to_all | solution.py:190
  15.7 0.0 copy-done
  15.7 0.3 collective-permute-start.6
  16.0 0.3 collective-permute-start.7
  16.3 1.4 %collective-permute-start.3 = (bf16[4,2,128,128]{3,2,1,0:T(8,128)(2,1)S(1)}, bf16[4,2,128,128]{3,2,1,0:T(8,128)(2,1)S(1)}, u32[]{:S(2)}, u32[]{:S(2)}) collective-permute-start(bf16[4,2,128,128]{3,2,1,0:T(8,128)(2,1)S(1)} %collective-permute-done.rest_1_), channel_id=1, source_target_pairs={{0,4},{1,5},{2,10},{3,11},{4,0},{5,1},{6,14},{7,15},{8,12},{9,13},... | collective-permute-start | bytes 786440 | tf_op jit(solution)/shard_map/ppermute | solution.py:180
  17.7 0.6 collective-permute-start.8
  18.3 1.2 %collective-permute-start.4 = (bf16[4,2,128,128]{3,2,1,0:T(8,128)(2,1)S(1)}, bf16[4,2,128,128]{3,2,1,0:T(8,128)(2,1)S(1)}, u32[]{:S(2)}, u32[]{:S(2)}) collective-permute-start(bf16[4,2,128,128]{3,2,1,0:T(8,128)(2,1)S(1)} %collective-permute-done.1.rest_2_), channel_id=1, source_target_pairs={{0,8},{1,9},{2,3},{3,2},{4,12},{5,13},{6,7},{7,6},{8,0},{9,1},{10,... | collective-permute-start | bytes 786440 | tf_op jit(solution)/shard_map/ppermute | solution.py:180
  19.5 0.0 collective-permute-done.6.rest_4_
  19.5 0.3 collective-permute-start.9
  19.9 0.0 collective-permute-done.7.rest_5_
  19.9 0.3 collective-permute-start.5
  20.2 13.4 %collective-permute-done.3.rest_0_ = bf16[4,2,128,128]{3,2,1,0:T(8,128)(2,1)S(1)} collective-permute-done((bf16[4,2,128,128]{3,2,1,0:T(8,128)(2,1)S(1)}, bf16[4,2,128,128]{3,2,1,0:T(8,128)(2,1)S(1)}, u32[]{:S(2)}, u32[]{:S(2)}) %collective-permute-start.3) | collective-permute-done | bytes 262176 | tf_op jit(solution)/shard_map/ppermute | solution.py:180
  33.6 0.0 collective-permute-done.8.rest_6_
  33.6 0.0 collective-permute-done.4.rest_1_
  33.6 0.0 collective-permute-done.9.rest_7_
  33.6 0.0 copy-start.1
  33.6 0.7 copy-done.1
  34.3 0.0 collective-permute-done.5.rest_2_
  34.3 0.0 all-to-all-done.q_ref
  34.3 1.2 %collective-permute-start.10 = (bf16[4,2,128,128]{3,2,1,0:T(8,128)(2,1)S(1)}, bf16[4,2,128,128]{3,2,1,0:T(8,128)(2,1)S(1)}, u32[]{:S(2)}, u32[]{:S(2)}) collective-permute-start(bf16[4,2,128,128]{3,2,1,0:T(8,128)(2,1)S(1)} %collective-permute-done.3.rest_0_), channel_id=1, source_target_pairs={{0,8},{1,9},{2,3},{3,2},{4,12},{5,13},{6,7},{7,6},{8,0},{9,1},{10,... | collective-permute-start | bytes 786440 | tf_op jit(solution)/shard_map/ppermute | solution.py:180
  35.5 1.4 %collective-permute-start.12 = (bf16[4,2,128,128]{3,2,1,0:T(8,128)(2,1)S(1)}, bf16[4,2,128,128]{3,2,1,0:T(8,128)(2,1)S(1)}, u32[]{:S(2)}, u32[]{:S(2)}) collective-permute-start(bf16[4,2,128,128]{3,2,1,0:T(8,128)(2,1)S(1)} %collective-permute-done.3.rest_0_), channel_id=1, source_target_pairs={{0,2},{1,3},{2,0},{3,1},{4,6},{5,7},{6,4},{7,5},{8,10},{9,11},{10,... | collective-permute-start | bytes 786440 | tf_op jit(solution)/shard_map/ppermute | solution.py:183
  36.9 0.0 collective-permute-start.13
  36.9 0.5 collective-permute-start.14
  37.4 0.0 copy-start.2
  37.4 0.9 %copy-done.2 = bf16[4,2,128,128]{3,2,1,0:T(8,128)(2,1)S(1)} copy-done((bf16[4,2,128,128]{3,2,1,0:T(8,128)(2,1)S(1)}, bf16[4,2,128,128]{3,2,1,0:T(8,128)(2,1)}, u32[]{:S(2)}) %copy-start.2) | copy-done | bytes 262168
  38.3 2.9 %products.3.rest_6_ = f32[256,8,128]{2,1,0:T(8,128)S(1)} custom-call(bf16[16,208,128]{2,1,0:T(8,128)(2,1)S(1)} %all-to-all-done.q_ref, bf16[4,2,128,128]{3,2,1,0:T(8,128)(2,1)S(1)} %copy-done, bf16[4,2,128,128]{3,2,1,0:T(8,128)(2,1)S(1)} %collective-permute-done.rest_1_, bf16[4,2,128,128]{3,2,1,0:T(8,128)(2,1)S(1)} %collective-permute-done.1.rest_2_, ...), custom_call_target="tpu_custom_call" | custom-call | flops 100663296 | bytes 8388608 | tf_op jit(solution)/shard_map/products/pallas_call | solution.py:95
  41.2 0.0 collective-permute-done.10.rest_0_
  41.3 1.0 %collective-permute-start.11 = (bf16[4,2,128,128]{3,2,1,0:T(8,128)(2,1)S(1)}, bf16[4,2,128,128]{3,2,1,0:T(8,128)(2,1)S(1)}, u32[]{:S(2)}, u32[]{:S(2)}) collective-permute-start(bf16[4,2,128,128]{3,2,1,0:T(8,128)(2,1)S(1)} %collective-permute-done.10.rest_0_), channel_id=1, source_target_pairs={{0,2},{1,3},{2,0},{3,1},{4,6},{5,7},{6,4},{7,5},{8,10},{9,11},{10,... | collective-permute-start | bytes 786440 | tf_op jit(solution)/shard_map/ppermute | solution.py:183
  42.3 0.0 collective-permute-done.13.rest_4_
  42.3 0.0 collective-permute-done.14.rest_5_
  42.3 0.0 collective-permute-done.12.rest_3_
  42.3 2.3 %products.4.rest_2_ = f32[256,8,128]{2,1,0:T(8,128)S(1)} custom-call(bf16[16,208,128]{2,1,0:T(8,128)(2,1)S(1)} %all-to-all-done.q_ref, bf16[4,2,128,128]{3,2,1,0:T(8,128)(2,1)S(1)} %collective-permute-done.3.rest_0_, bf16[4,2,128,128]{3,2,1,0:T(8,128)(2,1)S(1)} %collective-permute-done.4.rest_1_, ...), custom_call_target="tpu_custom_call", output_to_operand_aliasing={{}: (7, {})} | custom-call | flops 75497472 | bytes 6291456 | tf_op jit(solution)/shard_map/products/pallas_call | solution.py:95
  44.6 0.0 collective-permute-done.11.rest_1_
  44.7 1.9 %products.5 = s32[32,5,8,128]{3,2,1,0:T(8,128)S(1)} custom-call(bf16[16,208,128]{2,1,0:T(8,128)(2,1)S(1)} %all-to-all-done.q_ref, bf16[4,2,128,128]{3,2,1,0:T(8,128)(2,1)S(1)} %collective-permute-done.10.rest_0_, bf16[4,2,128,128]{3,2,1,0:T(8,128)(2,1)S(1)} %collective-permute-done.11.rest_1_, f32[256,8,128]{2,1,0:T(8,128)S(1)} %products.4.rest_2_), custom_call_target="tpu_custom_call" | custom-call | flops 25165824 | bytes 2097152 | tf_op jit(solution)/shard_map/products/pallas_call | solution.py:95
  46.6 22.2 %all_to_all.10 = s32[32,5,8,128]{3,2,1,0:T(8,128)S(1)} all-to-all(s32[32,5,8,128]{3,2,1,0:T(8,128)S(1)} %products.5), channel_id=1, replica_groups=mesh['plane'=2,'pair'=4,'core'=2,'col'=2] {'plane','pair','core','col'}, dimensions={0} | all-to-all | bytes 1310720 | tf_op jit(solution)/shard_map/all_to_all | solution.py:206
  68.8 1.3 %turn.1 = f32[128,1024]{1,0:T(8,128)} custom-call(s32[2,16,5,8,128]{4,3,2,1,0:T(8,128)S(1)} %bitcast.2), custom_call_target="tpu_custom_call" | custom-call | tf_op jit(solution)/shard_map/turn/pallas_call | solution.py:207
Async XLA Ops:
  0.0 6.9 %collective-permute-start.2 = (bf16[4,2,128,128]{3,2,1,0:T(8,128)(2,1)}, bf16[4,2,128,128]{3,2,1,0:T(8,128)(2,1)S(1)}, u32[]{:S(2)}, u32[]{:S(2)}) collective-permute-start(bf16[4,2,128,128]{3,2,1,0:T(8,128)(2,1)} %rest_0_.1), channel_id=1, source_target_pairs={{0,8},{1,9},{2,3},{3,2},{4,12},{5,13},{6,7},{7,6},{8,0},{9,1},{10,... | collective-permute-start | bytes 786440 | tf_op jit(solution)/shard_map/ppermute | solution.py:180
  2.1 8.0 %collective-permute-start.1 = (bf16[4,2,128,128]{3,2,1,0:T(8,128)(2,1)}, bf16[4,2,128,128]{3,2,1,0:T(8,128)(2,1)S(1)}, u32[]{:S(2)}, u32[]{:S(2)}) collective-permute-start(bf16[4,2,128,128]{3,2,1,0:T(8,128)(2,1)} %rest_0_.1), channel_id=1, source_target_pairs={{0,4},{1,5},{2,10},{3,11},{4,0},{5,1},{6,14},{7,15},{8,12},{9,13},... | collective-permute-start | bytes 786440 | tf_op jit(solution)/shard_map/ppermute | solution.py:180
  3.4 8.4 %collective-permute-start = (bf16[4,2,128,128]{3,2,1,0:T(8,128)(2,1)}, bf16[4,2,128,128]{3,2,1,0:T(8,128)(2,1)S(1)}, u32[]{:S(2)}, u32[]{:S(2)}) collective-permute-start(bf16[4,2,128,128]{3,2,1,0:T(8,128)(2,1)} %rest_0_.1), channel_id=1, source_target_pairs={{0,1},{1,0},{2,6},{3,7},{4,5},{5,4},{6,2},{7,3},{8,9},{9,8},{10,14... | collective-permute-start | bytes 786440 | tf_op jit(solution)/shard_map/ppermute | solution.py:180
  6.9 8.8 %copy-start = (bf16[4,2,128,128]{3,2,1,0:T(8,128)(2,1)S(1)}, bf16[4,2,128,128]{3,2,1,0:T(8,128)(2,1)}, u32[]{:S(2)}) copy-start(bf16[4,2,128,128]{3,2,1,0:T(8,128)(2,1)} %rest_0_.1) | copy-start | bytes 786436
  11.7 22.6 %all-to-all-start = ((bf16[16,208,128]{2,1,0:T(8,128)(2,1)}), bf16[16,208,128]{2,1,0:T(8,128)(2,1)S(1)}, u32[]{:S(2)}, u32[]{:S(2)}) async-start(bf16[16,208,128]{2,1,0:T(8,128)(2,1)} %cut_columns.1), calls=%async_computation | async-start | bytes 1703936 | tf_op jit(solution)/shard_map/all_to_all | solution.py:190
  15.7 3.8 %collective-permute-start.6 = (bf16[4,2,128,128]{3,2,1,0:T(8,128)(2,1)S(1)}, bf16[4,2,128,128]{3,2,1,0:T(8,128)(2,1)S(1)}, u32[]{:S(2)}, u32[]{:S(2)}) collective-permute-start(bf16[4,2,128,128]{3,2,1,0:T(8,128)(2,1)S(1)} %copy-done), channel_id=1, source_target_pairs={{0,2},{1,3},{2,0},{3,1},{4,6},{5,7},{6,4},{7,5},{8,10},{9,11},{10,... | collective-permute-start | bytes 786440 | tf_op jit(solution)/shard_map/ppermute | solution.py:183
  16.0 3.9 %collective-permute-start.7 = (bf16[4,2,128,128]{3,2,1,0:T(8,128)(2,1)S(1)}, bf16[4,2,128,128]{3,2,1,0:T(8,128)(2,1)S(1)}, u32[]{:S(2)}, u32[]{:S(2)}) collective-permute-start(bf16[4,2,128,128]{3,2,1,0:T(8,128)(2,1)S(1)} %collective-permute-done.rest_1_), channel_id=1, source_target_pairs={{0,2},{1,3},{2,0},{3,1},{4,6},{5,7},{6,4},{7,5},{8,10},{9,11},{10,... | collective-permute-start | bytes 786440 | tf_op jit(solution)/shard_map/ppermute | solution.py:183
  16.3 17.3 %collective-permute-start.3 = (bf16[4,2,128,128]{3,2,1,0:T(8,128)(2,1)S(1)}, bf16[4,2,128,128]{3,2,1,0:T(8,128)(2,1)S(1)}, u32[]{:S(2)}, u32[]{:S(2)}) collective-permute-start(bf16[4,2,128,128]{3,2,1,0:T(8,128)(2,1)S(1)} %collective-permute-done.rest_1_), channel_id=1, source_target_pairs={{0,4},{1,5},{2,10},{3,11},{4,0},{5,1},{6,14},{7,15},{8,12},{9,13},... | collective-permute-start | bytes 786440 | tf_op jit(solution)/shard_map/ppermute | solution.py:180
  17.7 15.9 %collective-permute-start.8 = (bf16[4,2,128,128]{3,2,1,0:T(8,128)(2,1)S(1)}, bf16[4,2,128,128]{3,2,1,0:T(8,128)(2,1)S(1)}, u32[]{:S(2)}, u32[]{:S(2)}) collective-permute-start(bf16[4,2,128,128]{3,2,1,0:T(8,128)(2,1)S(1)} %collective-permute-done.1.rest_2_), channel_id=1, source_target_pairs={{0,2},{1,3},{2,0},{3,1},{4,6},{5,7},{6,4},{7,5},{8,10},{9,11},{10,... | collective-permute-start | bytes 786440 | tf_op jit(solution)/shard_map/ppermute | solution.py:183
  18.3 15.2 %collective-permute-start.4 = (bf16[4,2,128,128]{3,2,1,0:T(8,128)(2,1)S(1)}, bf16[4,2,128,128]{3,2,1,0:T(8,128)(2,1)S(1)}, u32[]{:S(2)}, u32[]{:S(2)}) collective-permute-start(bf16[4,2,128,128]{3,2,1,0:T(8,128)(2,1)S(1)} %collective-permute-done.1.rest_2_), channel_id=1, source_target_pairs={{0,8},{1,9},{2,3},{3,2},{4,12},{5,13},{6,7},{7,6},{8,0},{9,1},{10,... | collective-permute-start | bytes 786440 | tf_op jit(solution)/shard_map/ppermute | solution.py:180
  19.5 14.1 %collective-permute-start.9 = (bf16[4,2,128,128]{3,2,1,0:T(8,128)(2,1)S(1)}, bf16[4,2,128,128]{3,2,1,0:T(8,128)(2,1)S(1)}, u32[]{:S(2)}, u32[]{:S(2)}) collective-permute-start(bf16[4,2,128,128]{3,2,1,0:T(8,128)(2,1)S(1)} %collective-permute-done.2.rest_3_), channel_id=1, source_target_pairs={{0,2},{1,3},{2,0},{3,1},{4,6},{5,7},{6,4},{7,5},{8,10},{9,11},{10,... | collective-permute-start | bytes 786440 | tf_op jit(solution)/shard_map/ppermute | solution.py:183
  19.9 14.4 %collective-permute-start.5 = (bf16[4,2,128,128]{3,2,1,0:T(8,128)(2,1)S(1)}, bf16[4,2,128,128]{3,2,1,0:T(8,128)(2,1)S(1)}, u32[]{:S(2)}, u32[]{:S(2)}) collective-permute-start(bf16[4,2,128,128]{3,2,1,0:T(8,128)(2,1)S(1)} %collective-permute-done.2.rest_3_), channel_id=1, source_target_pairs={{0,1},{1,0},{2,6},{3,7},{4,5},{5,4},{6,2},{7,3},{8,9},{9,8},{10,14... | collective-permute-start | bytes 786440 | tf_op jit(solution)/shard_map/ppermute | solution.py:180
  33.6 0.7 %copy-start.1 = (bf16[4,2,128,128]{3,2,1,0:T(8,128)(2,1)}, bf16[4,2,128,128]{3,2,1,0:T(8,128)(2,1)S(1)}, u32[]{:S(2)}) copy-start(bf16[4,2,128,128]{3,2,1,0:T(8,128)(2,1)S(1)} %collective-permute-done.9.rest_7_) | copy-start | bytes 786436
  34.3 6.9 %collective-permute-start.10 = (bf16[4,2,128,128]{3,2,1,0:T(8,128)(2,1)S(1)}, bf16[4,2,128,128]{3,2,1,0:T(8,128)(2,1)S(1)}, u32[]{:S(2)}, u32[]{:S(2)}) collective-permute-start(bf16[4,2,128,128]{3,2,1,0:T(8,128)(2,1)S(1)} %collective-permute-done.3.rest_0_), channel_id=1, source_target_pairs={{0,8},{1,9},{2,3},{3,2},{4,12},{5,13},{6,7},{7,6},{8,0},{9,1},{10,... | collective-permute-start | bytes 786440 | tf_op jit(solution)/shard_map/ppermute | solution.py:180
  35.5 6.8 %collective-permute-start.12 = (bf16[4,2,128,128]{3,2,1,0:T(8,128)(2,1)S(1)}, bf16[4,2,128,128]{3,2,1,0:T(8,128)(2,1)S(1)}, u32[]{:S(2)}, u32[]{:S(2)}) collective-permute-start(bf16[4,2,128,128]{3,2,1,0:T(8,128)(2,1)S(1)} %collective-permute-done.3.rest_0_), channel_id=1, source_target_pairs={{0,2},{1,3},{2,0},{3,1},{4,6},{5,7},{6,4},{7,5},{8,10},{9,11},{10,... | collective-permute-start | bytes 786440 | tf_op jit(solution)/shard_map/ppermute | solution.py:183
  36.9 5.4 %collective-permute-start.13 = (bf16[4,2,128,128]{3,2,1,0:T(8,128)(2,1)S(1)}, bf16[4,2,128,128]{3,2,1,0:T(8,128)(2,1)S(1)}, u32[]{:S(2)}, u32[]{:S(2)}) collective-permute-start(bf16[4,2,128,128]{3,2,1,0:T(8,128)(2,1)S(1)} %collective-permute-done.4.rest_1_), channel_id=1, source_target_pairs={{0,2},{1,3},{2,0},{3,1},{4,6},{5,7},{6,4},{7,5},{8,10},{9,11},{10,... | collective-permute-start | bytes 786440 | tf_op jit(solution)/shard_map/ppermute | solution.py:183
  36.9 5.4 %collective-permute-start.14 = (bf16[4,2,128,128]{3,2,1,0:T(8,128)(2,1)S(1)}, bf16[4,2,128,128]{3,2,1,0:T(8,128)(2,1)S(1)}, u32[]{:S(2)}, u32[]{:S(2)}) collective-permute-start(bf16[4,2,128,128]{3,2,1,0:T(8,128)(2,1)S(1)} %collective-permute-done.5.rest_2_), channel_id=1, source_target_pairs={{0,2},{1,3},{2,0},{3,1},{4,6},{5,7},{6,4},{7,5},{8,10},{9,11},{10,... | collective-permute-start | bytes 786440 | tf_op jit(solution)/shard_map/ppermute | solution.py:183
  37.4 0.9 %copy-start.2 = (bf16[4,2,128,128]{3,2,1,0:T(8,128)(2,1)S(1)}, bf16[4,2,128,128]{3,2,1,0:T(8,128)(2,1)}, u32[]{:S(2)}) copy-start(bf16[4,2,128,128]{3,2,1,0:T(8,128)(2,1)} %copy-done.1) | copy-start | bytes 786436
  41.3 3.4 %collective-permute-start.11 = (bf16[4,2,128,128]{3,2,1,0:T(8,128)(2,1)S(1)}, bf16[4,2,128,128]{3,2,1,0:T(8,128)(2,1)S(1)}, u32[]{:S(2)}, u32[]{:S(2)}) collective-permute-start(bf16[4,2,128,128]{3,2,1,0:T(8,128)(2,1)S(1)} %collective-permute-done.10.rest_0_), channel_id=1, source_target_pairs={{0,2},{1,3},{2,0},{3,1},{4,6},{5,7},{6,4},{7,5},{8,10},{9,11},{10,... | collective-permute-start | bytes 786440 | tf_op jit(solution)/shard_map/ppermute | solution.py:183

commit v11 on v10

--- a/solution.py
+++ b/solution.py
@@ -50,9 +50,25 @@
         out_ref[j, blocks * rows:] = ids
 
 
-def product_kernel(tile_count, cols, routes, first, coded, q_ref, *rest):
+def start_kernel(*refs):
+    refs[-1][...] = jnp.zeros_like(refs[-1])
+
+
+def start_sums(after, shape):
+    return pl.pallas_call(
+        start_kernel,
+        out_shape=jax.ShapeDtypeStruct(shape, jnp.float32),
+        in_specs=[pl.BlockSpec(memory_space=pl.ANY)] * len(after),
+        out_specs=pl.BlockSpec(memory_space=pltpu.VMEM),
+        cost_estimate=pl.CostEstimate(flops=0, bytes_accessed=256 << 20, transcendentals=0),
+        compiler_params=pltpu.CompilerParams(vmem_limit_bytes=4 << 20),
+        name="start_sums",
+    )(*after)
+
+
+def product_kernel(tile_count, cols, routes, coded, q_ref, *rest):
     count = len(routes)
-    p_refs, (out_ref, wide_ids, ids, id_sem, *sums) = rest[:count], rest[count + (not first):]
+    p_refs, (out_ref, wide_ids, ids, id_sem, *sums) = rest[:count], rest[count + 1:]
     acc_ref = sums[0] if coded else out_ref
     blocks, per_p, extent, _ = p_refs[0].shape
     strip = acc_ref.shape[1]
@@ -62,10 +78,7 @@
         wide_ids[s:s + 1] = q_ref[s, blocks * rows:, :].astype(jnp.int32)[:1]
     id_copy = pltpu.make_async_copy(wide_ids, ids, id_sem)
     id_copy.start()
-    if first:
-        acc_ref[...] = jnp.zeros_like(acc_ref)
-    else:
-        acc_ref[...] = rest[count][...]
+    acc_ref[...] = rest[count][...]
     here = lax.axis_index(("pair", "core", "col"))
     id_copy.wait()
     for i in range(count):
@@ -91,9 +104,9 @@
     if coded:
         shape = (tile_count * cols, tile_count // cols // 2 + 1) + sums.shape[1:]
         made = jax.ShapeDtypeStruct(shape, jnp.int32)
-    operands = [q_here, *sets] + ([] if acc is None else [acc])
+    operands = [q_here, *sets, acc]
     return pl.pallas_call(
-        functools.partial(product_kernel, tile_count, cols, routes, acc is None, coded),
+        functools.partial(product_kernel, tile_count, cols, routes, coded),
         out_shape=made,
         in_specs=[pl.BlockSpec(memory_space=pltpu.VMEM)] * len(operands),
         out_specs=pl.BlockSpec(memory_space=pltpu.VMEM),
@@ -103,10 +116,10 @@
             pltpu.SemaphoreType.DMA,
         ]
         + [pltpu.VMEM(sums.shape, sums.dtype)] * coded,
-        input_output_aliases={} if acc is None or coded else {len(operands) - 1: 0},
+        input_output_aliases={} if coded else {len(operands) - 1: 0},
         cost_estimate=pl.CostEstimate(
             flops=2 * len(sets) * per_p * rows * extent * extent,
-            bytes_accessed=len(sets) * (1 << 20),
+            bytes_accessed=len(sets) * (1 << 18),
             transcendentals=0,
         ),
         compiler_params=pltpu.CompilerParams(vmem_limit_bytes=24 << 20),
@@ -186,14 +199,15 @@
         return add_products(q_here, sets, routes, acc, tile_count, cols, coded)
 
     first = [along(p_tiles, step) for step in range(3)]
-    sliced, *first = lax.optimization_barrier((sliced, *first))
-    q_here = lax.all_to_all(sliced, seat, split_axis=0, concat_axis=0, tiled=True)
+    sliced, first = lax.optimization_barrier((sliced, first))
     second = [along(first[step], (step + 1) % 3) for step in range(3)]
     crossed = [across(each) for each in [p_tiles] + first]
-    q_here, second, crossed = lax.optimization_barrier((q_here, second, crossed))
+    q_here = lax.all_to_all(sliced, seat, split_axis=0, concat_axis=0, tiled=True)
+    acc = start_sums(second, (tile_count * tile_count, strip, extent))
     third = along(second[0], 2)
+    q_here, second, acc = lax.optimization_barrier((q_here, second, acc))
     acc = add(
-        None,
+        acc,
         [p_tiles] + first + crossed,
         [(step, swapped) for swapped in (0, 1) for step in range(4)],
     )

time: 70.3 us -> 70.4 us (level)
  Pallas kernels: 10.7 us -> 12.9 us
  waiting for transfers between devices: 18.2 us -> 16.1 us
  starting transfers between devices: 17.1 us -> 18.8 us
  local copies, waits for them, and re-layouts: 1.65 us -> 0.01 us
    ppermute x7, waiting for transfers between devices: 18.2 us -> 16.1 us  [along(): return lax.ppermute(values, seat, hops)]
    pallas_call x3, Pallas kernels: 7.14 us -> 9.29 us  [add_products(): pl.pallas_call(functools.partial(product_kernel, tile_count, cols, routes...]
    unnamed x6 -> x2, local copies, waits for them, and re-layouts: 1.65 us -> 0.01 us
    ppermute x7, starting transfers between devices: 8.72 us -> 9.58 us  [along(): return lax.ppermute(values, seat, hops)]
    all_to_all x1, starting transfers between devices: 3.99 us -> 4.84 us  [body(): lax.all_to_all(sliced, seat, split_axis=0, concat_axis=0, tiled=True)]
  transfers between devices with their start and end apart: 16 -> 16, of which waited for: 3 -> 3; matrix products, arithmetic and copies ran while one was open for 0% -> 0% of each run, Pallas kernels for 11% -> 13%
where the time goes in v11:
time: 70.4 us; the launch traced here: 70.1 us
  blocking collectives  22.2 us (32%)
  starting transfers between devices  18.8 us (27%)
  waiting for transfers between devices  16.1 us (23%)
  Pallas kernels  12.9 us (18%)
    all_to_all x1, blocking collectives, body(): lax.all_to_all(coded, every, split_axis=0, concat_axis=0, tiled=True)  22.2 us
    ppermute x7, waiting for transfers between devices, along(): return lax.ppermute(values, seat, hops)  16.1 us
    ppermute x7, starting transfers between devices, along(): return lax.ppermute(values, seat, hops)  9.58 us
    pallas_call x3, Pallas kernels, add_products(): pl.pallas_call(functools.partial(product_kernel, tile_count, cols, routes...  9.29 us
    all_to_all x1, starting transfers between devices, body(): lax.all_to_all(sliced, seat, split_axis=0, concat_axis=0, tiled=True)  4.84 us
    ppermute x8, starting transfers between devices, across(): return lax.ppermute(values, seat, [(s, s ^ cols) for s in range(SEATS)])  4.34 us
    pallas_call x1, Pallas kernels, body(): pl.pallas_call(slice_kernel, out_shape=jax.ShapeDtypeStruct((SEATS, heigh...  2.31 us
  transfers between devices with their start and end apart: 16, of which 3 were waited for; matrix products, arithmetic and copies ran while one was open for 0% of the time, Pallas kernels for 13%

profile of v11, /device:TPU:1, one launch (start us, length us, event | category | flops | bytes accessed | tf_op | source)
XLA Modules:
  0.0 70.1 jit_solution(13056978051656110593)
XLA Ops:
  0.0 2.0 %collective-permute-start = (bf16[4,2,128,128]{3,2,1,0:T(8,128)(2,1)}, bf16[4,2,128,128]{3,2,1,0:T(8,128)(2,1)S(1)}, u32[]{:S(2)}, u32[]{:S(2)}) collective-permute-start(bf16[4,2,128,128]{3,2,1,0:T(8,128)(2,1)} %rest_0_.1), channel_id=1, source_target_pairs={{0,1},{1,0},{2,6},{3,7},{4,5},{5,4},{6,2},{7,3},{8,9},{9,8},{10,14... | collective-permute-start | bytes 786440 | tf_op jit(solution)/shard_map/ppermute | solution.py:193
  2.0 1.3 %collective-permute-start.1 = (bf16[4,2,128,128]{3,2,1,0:T(8,128)(2,1)}, bf16[4,2,128,128]{3,2,1,0:T(8,128)(2,1)S(1)}, u32[]{:S(2)}, u32[]{:S(2)}) collective-permute-start(bf16[4,2,128,128]{3,2,1,0:T(8,128)(2,1)} %rest_0_.1), channel_id=1, source_target_pairs={{0,4},{1,5},{2,10},{3,11},{4,0},{5,1},{6,14},{7,15},{8,12},{9,13},... | collective-permute-start | bytes 786440 | tf_op jit(solution)/shard_map/ppermute | solution.py:193
  3.3 1.2 %collective-permute-start.2 = (bf16[4,2,128,128]{3,2,1,0:T(8,128)(2,1)}, bf16[4,2,128,128]{3,2,1,0:T(8,128)(2,1)}, u32[]{:S(2)}, u32[]{:S(2)}) collective-permute-start(bf16[4,2,128,128]{3,2,1,0:T(8,128)(2,1)} %rest_0_.1), channel_id=1, source_target_pairs={{0,8},{1,9},{2,3},{3,2},{4,12},{5,13},{6,7},{7,6},{8,0},{9,1},{10,... | collective-permute-start | bytes 786440 | tf_op jit(solution)/shard_map/ppermute | solution.py:193
  4.6 2.3 %cut_columns.1 = bf16[16,208,128]{2,1,0:T(8,128)(2,1)} custom-call(s32[2,4]{1,0:T(2,128)} %bitcast.3, s32[4,6]{1,0:T(4,128)} %q_ids.1, bf16[4,6,128,128]{3,2,1,0:T(8,128)(2,1)} %q_ref.1), custom_call_target="tpu_custom_call" | custom-call | bytes 8388608 | tf_op jit(solution)/shard_map/cut_columns/pallas_call | solution.py:183
  6.9 0.0 copy-start
  6.9 0.0 collective-permute-done.rest_1_
  6.9 0.9 %collective-permute-done.1.rest_2_ = bf16[4,2,128,128]{3,2,1,0:T(8,128)(2,1)S(1)} collective-permute-done((bf16[4,2,128,128]{3,2,1,0:T(8,128)(2,1)}, bf16[4,2,128,128]{3,2,1,0:T(8,128)(2,1)S(1)}, u32[]{:S(2)}, u32[]{:S(2)}) %collective-permute-start.1) | collective-permute-done | bytes 262176 | tf_op jit(solution)/shard_map/ppermute | solution.py:193
  7.8 2.3 %collective-permute-done.2.rest_3_ = bf16[4,2,128,128]{3,2,1,0:T(8,128)(2,1)} collective-permute-done((bf16[4,2,128,128]{3,2,1,0:T(8,128)(2,1)}, bf16[4,2,128,128]{3,2,1,0:T(8,128)(2,1)}, u32[]{:S(2)}, u32[]{:S(2)}) %collective-permute-start.2) | collective-permute-done | bytes 262176 | tf_op jit(solution)/shard_map/ppermute | solution.py:193
  10.1 4.8 %all-to-all-start = ((bf16[16,208,128]{2,1,0:T(8,128)(2,1)}), bf16[16,208,128]{2,1,0:T(8,128)(2,1)S(1)}, u32[]{:S(2)}, u32[]{:S(2)}) async-start(bf16[16,208,128]{2,1,0:T(8,128)(2,1)} %cut_columns.1), calls=%async_computation | async-start | bytes 1703936 | tf_op jit(solution)/shard_map/all_to_all | solution.py:205
  14.9 1.4 %collective-permute-start.3 = (bf16[4,2,128,128]{3,2,1,0:T(8,128)(2,1)S(1)}, bf16[4,2,128,128]{3,2,1,0:T(8,128)(2,1)S(1)}, u32[]{:S(2)}, u32[]{:S(2)}) collective-permute-start(bf16[4,2,128,128]{3,2,1,0:T(8,128)(2,1)S(1)} %collective-permute-done.rest_1_), channel_id=1, source_target_pairs={{0,4},{1,5},{2,10},{3,11},{4,0},{5,1},{6,14},{7,15},{8,12},{9,13},... | collective-permute-start | bytes 786440 | tf_op jit(solution)/shard_map/ppermute | solution.py:193
  16.3 1.2 %collective-permute-start.4 = (bf16[4,2,128,128]{3,2,1,0:T(8,128)(2,1)S(1)}, bf16[4,2,128,128]{3,2,1,0:T(8,128)(2,1)S(1)}, u32[]{:S(2)}, u32[]{:S(2)}) collective-permute-start(bf16[4,2,128,128]{3,2,1,0:T(8,128)(2,1)S(1)} %collective-permute-done.1.rest_2_), channel_id=1, source_target_pairs={{0,8},{1,9},{2,3},{3,2},{4,12},{5,13},{6,7},{7,6},{8,0},{9,1},{10,... | collective-permute-start | bytes 786440 | tf_op jit(solution)/shard_map/ppermute | solution.py:193
  17.5 1.2 %collective-permute-start.5 = (bf16[4,2,128,128]{3,2,1,0:T(8,128)(2,1)}, bf16[4,2,128,128]{3,2,1,0:T(8,128)(2,1)S(1)}, u32[]{:S(2)}, u32[]{:S(2)}) collective-permute-start(bf16[4,2,128,128]{3,2,1,0:T(8,128)(2,1)} %collective-permute-done.2.rest_3_), channel_id=1, source_target_pairs={{0,1},{1,0},{2,6},{3,7},{4,5},{5,4},{6,2},{7,3},{8,9},{9,8},{10,14... | collective-permute-start | bytes 786440 | tf_op jit(solution)/shard_map/ppermute | solution.py:193
  18.7 0.0 copy-done
  18.7 1.2 %collective-permute-start.7 = (bf16[4,2,128,128]{3,2,1,0:T(8,128)(2,1)S(1)}, bf16[4,2,128,128]{3,2,1,0:T(8,128)(2,1)}, u32[]{:S(2)}, u32[]{:S(2)}) collective-permute-start(bf16[4,2,128,128]{3,2,1,0:T(8,128)(2,1)S(1)} %copy-done), channel_id=1, source_target_pairs={{0,2},{1,3},{2,0},{3,1},{4,6},{5,7},{6,4},{7,5},{8,10},{9,11},{10,... | collective-permute-start | bytes 786440 | tf_op jit(solution)/shard_map/ppermute | solution.py:196
  19.9 0.0 collective-permute-start.10
  19.9 12.8 %collective-permute-done.3.refs_0_.rest_0_ = bf16[4,2,128,128]{3,2,1,0:T(8,128)(2,1)S(1)} collective-permute-done((bf16[4,2,128,128]{3,2,1,0:T(8,128)(2,1)S(1)}, bf16[4,2,128,128]{3,2,1,0:T(8,128)(2,1)S(1)}, u32[]{:S(2)}, u32[]{:S(2)}) %collective-permute-start.3) | collective-permute-done | bytes 262176 | tf_op jit(solution)/shard_map/ppermute | solution.py:193
  32.7 1.6 %collective-permute-start.8 = (bf16[4,2,128,128]{3,2,1,0:T(8,128)(2,1)S(1)}, bf16[4,2,128,128]{3,2,1,0:T(8,128)(2,1)}, u32[]{:S(2)}, u32[]{:S(2)}) collective-permute-start(bf16[4,2,128,128]{3,2,1,0:T(8,128)(2,1)S(1)} %collective-permute-done.rest_1_), channel_id=1, source_target_pairs={{0,2},{1,3},{2,0},{3,1},{4,6},{5,7},{6,4},{7,5},{8,10},{9,11},{10,... | collective-permute-start | bytes 786440 | tf_op jit(solution)/shard_map/ppermute | solution.py:196
  34.4 0.0 collective-permute-done.4.refs_1_.rest_1_
  34.4 0.0 collective-permute-start.9
  34.4 0.0 collective-permute-done.5.refs_2_.rest_2_
  34.4 1.2 %collective-permute-start.6 = (bf16[4,2,128,128]{3,2,1,0:T(8,128)(2,1)S(1)}, bf16[4,2,128,128]{3,2,1,0:T(8,128)(2,1)}, u32[]{:S(2)}, u32[]{:S(2)}) collective-permute-start(bf16[4,2,128,128]{3,2,1,0:T(8,128)(2,1)S(1)} %collective-permute-done.3.refs_0_.rest_0_), channel_id=1, source_target_pairs={{0,8},{1,9},{2,3},{3,2},{4,12},{5,13},{6,7},{7,6},{8,0},{9,1},{10,... | collective-permute-start | bytes 786440 | tf_op jit(solution)/shard_map/ppermute | solution.py:193
  35.6 0.1 start_sums.1.rest_8_
  35.7 0.0 all-to-all-done.q_ref
  35.7 0.0 collective-permute-done.7.rest_4_
  35.7 0.3 collective-permute-start.12
  36.1 0.0 collective-permute-done.10.rest_7_
  36.1 0.3 collective-permute-start.13
  36.3 0.0 collective-permute-done.8.rest_5_
  36.3 0.3 collective-permute-start.14
  36.6 0.0 collective-permute-done.9.rest_6_
  36.6 4.1 %products.3.rest_6_ = f32[256,8,128]{2,1,0:T(8,128)S(1)} custom-call(bf16[16,208,128]{2,1,0:T(8,128)(2,1)S(1)} %all-to-all-done.q_ref, bf16[4,2,128,128]{3,2,1,0:T(8,128)(2,1)S(1)} %copy-done, bf16[4,2,128,128]{3,2,1,0:T(8,128)(2,1)S(1)} %collective-permute-done.rest_1_, ...), custom_call_target="tpu_custom_call", output_to_operand_aliasing={{}: (9, {})} | custom-call | flops 100663296 | bytes 2097152 | tf_op jit(solution)/shard_map/products/pallas_call | solution.py:108
  40.7 0.0 collective-permute-done.6.rest_0_
  40.7 0.7 collective-permute-start.11
  41.4 0.0 collective-permute-done.12.rest_3_
  41.4 0.0 collective-permute-done.13.rest_4_
  41.4 0.0 collective-permute-done.14.rest_5_
  41.4 2.3 %products.4.rest_2_ = f32[256,8,128]{2,1,0:T(8,128)S(1)} custom-call(bf16[16,208,128]{2,1,0:T(8,128)(2,1)S(1)} %all-to-all-done.q_ref, bf16[4,2,128,128]{3,2,1,0:T(8,128)(2,1)S(1)} %collective-permute-done.3.refs_0_.rest_0_, bf16[4,2,128,128]{3,2,1,0:T(8,128)(2,1)S(1)} %collective-permute-done.4.refs_1_.rest_1_, ...), custom_call_target="tpu_custom_call", output_to_operand_aliasing={{}: (7, {})} | custom-call | flops 75497472 | bytes 1572864 | tf_op jit(solution)/shard_map/products/pallas_call | solution.py:108
  43.7 0.0 collective-permute-done.11.rest_1_
  43.7 2.9 %products.5 = s32[32,5,8,128]{3,2,1,0:T(8,128)S(1)} custom-call(bf16[16,208,128]{2,1,0:T(8,128)(2,1)S(1)} %all-to-all-done.q_ref, bf16[4,2,128,128]{3,2,1,0:T(8,128)(2,1)} %collective-permute-done.6.rest_0_, bf16[4,2,128,128]{3,2,1,0:T(8,128)(2,1)S(1)} %collective-permute-done.11.rest_1_, f32[256,8,128]{2,1,0:T(8,128)S(1)} %products.4.rest_2_), custom_call_target="tpu_custom_call" | custom-call | flops 25165824 | bytes 524288 | tf_op jit(solution)/shard_map/products/pallas_call | solution.py:108
  46.6 22.2 %all_to_all.10 = s32[32,5,8,128]{3,2,1,0:T(8,128)S(1)} all-to-all(s32[32,5,8,128]{3,2,1,0:T(8,128)S(1)} %products.5), channel_id=1, replica_groups=mesh['plane'=2,'pair'=4,'core'=2,'col'=2] {'plane','pair','core','col'}, dimensions={0} | all-to-all | bytes 1310720 | tf_op jit(solution)/shard_map/all_to_all | solution.py:220
  68.8 1.3 %turn.1 = f32[128,1024]{1,0:T(8,128)} custom-call(s32[2,16,5,8,128]{4,3,2,1,0:T(8,128)S(1)} %bitcast.2), custom_call_target="tpu_custom_call" | custom-call | tf_op jit(solution)/shard_map/turn/pallas_call | solution.py:221
Async XLA Ops:
  0.0 6.9 %collective-permute-start = (bf16[4,2,128,128]{3,2,1,0:T(8,128)(2,1)}, bf16[4,2,128,128]{3,2,1,0:T(8,128)(2,1)S(1)}, u32[]{:S(2)}, u32[]{:S(2)}) collective-permute-start(bf16[4,2,128,128]{3,2,1,0:T(8,128)(2,1)} %rest_0_.1), channel_id=1, source_target_pairs={{0,1},{1,0},{2,6},{3,7},{4,5},{5,4},{6,2},{7,3},{8,9},{9,8},{10,14... | collective-permute-start | bytes 786440 | tf_op jit(solution)/shard_map/ppermute | solution.py:193
  2.0 5.7 %collective-permute-start.1 = (bf16[4,2,128,128]{3,2,1,0:T(8,128)(2,1)}, bf16[4,2,128,128]{3,2,1,0:T(8,128)(2,1)S(1)}, u32[]{:S(2)}, u32[]{:S(2)}) collective-permute-start(bf16[4,2,128,128]{3,2,1,0:T(8,128)(2,1)} %rest_0_.1), channel_id=1, source_target_pairs={{0,4},{1,5},{2,10},{3,11},{4,0},{5,1},{6,14},{7,15},{8,12},{9,13},... | collective-permute-start | bytes 786440 | tf_op jit(solution)/shard_map/ppermute | solution.py:193
  3.3 6.8 %collective-permute-start.2 = (bf16[4,2,128,128]{3,2,1,0:T(8,128)(2,1)}, bf16[4,2,128,128]{3,2,1,0:T(8,128)(2,1)}, u32[]{:S(2)}, u32[]{:S(2)}) collective-permute-start(bf16[4,2,128,128]{3,2,1,0:T(8,128)(2,1)} %rest_0_.1), channel_id=1, source_target_pairs={{0,8},{1,9},{2,3},{3,2},{4,12},{5,13},{6,7},{7,6},{8,0},{9,1},{10,... | collective-permute-start | bytes 786440 | tf_op jit(solution)/shard_map/ppermute | solution.py:193
  6.9 11.8 %copy-start = (bf16[4,2,128,128]{3,2,1,0:T(8,128)(2,1)S(1)}, bf16[4,2,128,128]{3,2,1,0:T(8,128)(2,1)}, u32[]{:S(2)}) copy-start(bf16[4,2,128,128]{3,2,1,0:T(8,128)(2,1)} %rest_0_.1) | copy-start | bytes 786436
  10.1 25.6 %all-to-all-start = ((bf16[16,208,128]{2,1,0:T(8,128)(2,1)}), bf16[16,208,128]{2,1,0:T(8,128)(2,1)S(1)}, u32[]{:S(2)}, u32[]{:S(2)}) async-start(bf16[16,208,128]{2,1,0:T(8,128)(2,1)} %cut_columns.1), calls=%async_computation | async-start | bytes 1703936 | tf_op jit(solution)/shard_map/all_to_all | solution.py:205
  14.9 17.8 %collective-permute-start.3 = (bf16[4,2,128,128]{3,2,1,0:T(8,128)(2,1)S(1)}, bf16[4,2,128,128]{3,2,1,0:T(8,128)(2,1)S(1)}, u32[]{:S(2)}, u32[]{:S(2)}) collective-permute-start(bf16[4,2,128,128]{3,2,1,0:T(8,128)(2,1)S(1)} %collective-permute-done.rest_1_), channel_id=1, source_target_pairs={{0,4},{1,5},{2,10},{3,11},{4,0},{5,1},{6,14},{7,15},{8,12},{9,13},... | collective-permute-start | bytes 786440 | tf_op jit(solution)/shard_map/ppermute | solution.py:193
  16.3 18.1 %collective-permute-start.4 = (bf16[4,2,128,128]{3,2,1,0:T(8,128)(2,1)S(1)}, bf16[4,2,128,128]{3,2,1,0:T(8,128)(2,1)S(1)}, u32[]{:S(2)}, u32[]{:S(2)}) collective-permute-start(bf16[4,2,128,128]{3,2,1,0:T(8,128)(2,1)S(1)} %collective-permute-done.1.rest_2_), channel_id=1, source_target_pairs={{0,8},{1,9},{2,3},{3,2},{4,12},{5,13},{6,7},{7,6},{8,0},{9,1},{10,... | collective-permute-start | bytes 786440 | tf_op jit(solution)/shard_map/ppermute | solution.py:193
  17.5 16.9 %collective-permute-start.5 = (bf16[4,2,128,128]{3,2,1,0:T(8,128)(2,1)}, bf16[4,2,128,128]{3,2,1,0:T(8,128)(2,1)S(1)}, u32[]{:S(2)}, u32[]{:S(2)}) collective-permute-start(bf16[4,2,128,128]{3,2,1,0:T(8,128)(2,1)} %collective-permute-done.2.rest_3_), channel_id=1, source_target_pairs={{0,1},{1,0},{2,6},{3,7},{4,5},{5,4},{6,2},{7,3},{8,9},{9,8},{10,14... | collective-permute-start | bytes 786440 | tf_op jit(solution)/shard_map/ppermute | solution.py:193
  18.7 17.0 %collective-permute-start.7 = (bf16[4,2,128,128]{3,2,1,0:T(8,128)(2,1)S(1)}, bf16[4,2,128,128]{3,2,1,0:T(8,128)(2,1)}, u32[]{:S(2)}, u32[]{:S(2)}) collective-permute-start(bf16[4,2,128,128]{3,2,1,0:T(8,128)(2,1)S(1)} %copy-done), channel_id=1, source_target_pairs={{0,2},{1,3},{2,0},{3,1},{4,6},{5,7},{6,4},{7,5},{8,10},{9,11},{10,... | collective-permute-start | bytes 786440 | tf_op jit(solution)/shard_map/ppermute | solution.py:196
  19.9 16.2 %collective-permute-start.10 = (bf16[4,2,128,128]{3,2,1,0:T(8,128)(2,1)}, bf16[4,2,128,128]{3,2,1,0:T(8,128)(2,1)}, u32[]{:S(2)}, u32[]{:S(2)}) collective-permute-start(bf16[4,2,128,128]{3,2,1,0:T(8,128)(2,1)} %collective-permute-done.2.rest_3_), channel_id=1, source_target_pairs={{0,2},{1,3},{2,0},{3,1},{4,6},{5,7},{6,4},{7,5},{8,10},{9,11},{10,... | collective-permute-start | bytes 786440 | tf_op jit(solution)/shard_map/ppermute | solution.py:196
  32.7 3.6 %collective-permute-start.8 = (bf16[4,2,128,128]{3,2,1,0:T(8,128)(2,1)S(1)}, bf16[4,2,128,128]{3,2,1,0:T(8,128)(2,1)}, u32[]{:S(2)}, u32[]{:S(2)}) collective-permute-start(bf16[4,2,128,128]{3,2,1,0:T(8,128)(2,1)S(1)} %collective-permute-done.rest_1_), channel_id=1, source_target_pairs={{0,2},{1,3},{2,0},{3,1},{4,6},{5,7},{6,4},{7,5},{8,10},{9,11},{10,... | collective-permute-start | bytes 786440 | tf_op jit(solution)/shard_map/ppermute | solution.py:196
  34.4 2.2 %collective-permute-start.9 = (bf16[4,2,128,128]{3,2,1,0:T(8,128)(2,1)S(1)}, bf16[4,2,128,128]{3,2,1,0:T(8,128)(2,1)}, u32[]{:S(2)}, u32[]{:S(2)}) collective-permute-start(bf16[4,2,128,128]{3,2,1,0:T(8,128)(2,1)S(1)} %collective-permute-done.1.rest_2_), channel_id=1, source_target_pairs={{0,2},{1,3},{2,0},{3,1},{4,6},{5,7},{6,4},{7,5},{8,10},{9,11},{10,... | collective-permute-start | bytes 786440 | tf_op jit(solution)/shard_map/ppermute | solution.py:196
  34.4 6.3 %collective-permute-start.6 = (bf16[4,2,128,128]{3,2,1,0:T(8,128)(2,1)S(1)}, bf16[4,2,128,128]{3,2,1,0:T(8,128)(2,1)}, u32[]{:S(2)}, u32[]{:S(2)}) collective-permute-start(bf16[4,2,128,128]{3,2,1,0:T(8,128)(2,1)S(1)} %collective-permute-done.3.refs_0_.rest_0_), channel_id=1, source_target_pairs={{0,8},{1,9},{2,3},{3,2},{4,12},{5,13},{6,7},{7,6},{8,0},{9,1},{10,... | collective-permute-start | bytes 786440 | tf_op jit(solution)/shard_map/ppermute | solution.py:193
  35.7 5.6 %collective-permute-start.12 = (bf16[4,2,128,128]{3,2,1,0:T(8,128)(2,1)S(1)}, bf16[4,2,128,128]{3,2,1,0:T(8,128)(2,1)S(1)}, u32[]{:S(2)}, u32[]{:S(2)}) collective-permute-start(bf16[4,2,128,128]{3,2,1,0:T(8,128)(2,1)S(1)} %collective-permute-done.3.refs_0_.rest_0_), channel_id=1, source_target_pairs={{0,2},{1,3},{2,0},{3,1},{4,6},{5,7},{6,4},{7,5},{8,10},{9,11},{10,... | collective-permute-start | bytes 786440 | tf_op jit(solution)/shard_map/ppermute | solution.py:196
  36.1 5.3 %collective-permute-start.13 = (bf16[4,2,128,128]{3,2,1,0:T(8,128)(2,1)S(1)}, bf16[4,2,128,128]{3,2,1,0:T(8,128)(2,1)S(1)}, u32[]{:S(2)}, u32[]{:S(2)}) collective-permute-start(bf16[4,2,128,128]{3,2,1,0:T(8,128)(2,1)S(1)} %collective-permute-done.4.refs_1_.rest_1_), channel_id=1, source_target_pairs={{0,2},{1,3},{2,0},{3,1},{4,6},{5,7},{6,4},{7,5},{8,10},{9,11},{10,... | collective-permute-start | bytes 786440 | tf_op jit(solution)/shard_map/ppermute | solution.py:196
  36.3 5.1 %collective-permute-start.14 = (bf16[4,2,128,128]{3,2,1,0:T(8,128)(2,1)S(1)}, bf16[4,2,128,128]{3,2,1,0:T(8,128)(2,1)S(1)}, u32[]{:S(2)}, u32[]{:S(2)}) collective-permute-start(bf16[4,2,128,128]{3,2,1,0:T(8,128)(2,1)S(1)} %collective-permute-done.5.refs_2_.rest_2_), channel_id=1, source_target_pairs={{0,2},{1,3},{2,0},{3,1},{4,6},{5,7},{6,4},{7,5},{8,10},{9,11},{10,... | collective-permute-start | bytes 786440 | tf_op jit(solution)/shard_map/ppermute | solution.py:196
  40.7 3.0 %collective-permute-start.11 = (bf16[4,2,128,128]{3,2,1,0:T(8,128)(2,1)}, bf16[4,2,128,128]{3,2,1,0:T(8,128)(2,1)S(1)}, u32[]{:S(2)}, u32[]{:S(2)}) collective-permute-start(bf16[4,2,128,128]{3,2,1,0:T(8,128)(2,1)} %collective-permute-done.6.rest_0_), channel_id=1, source_target_pairs={{0,2},{1,3},{2,0},{3,1},{4,6},{5,7},{6,4},{7,5},{8,10},{9,11},{10,... | collective-permute-start | bytes 786440 | tf_op jit(solution)/shard_map/ppermute | solution.py:196

commit v12 on v10

--- a/solution.py
+++ b/solution.py
@@ -106,7 +106,7 @@
         input_output_aliases={} if acc is None or coded else {len(operands) - 1: 0},
         cost_estimate=pl.CostEstimate(
             flops=2 * len(sets) * per_p * rows * extent * extent,
-            bytes_accessed=len(sets) * (1 << 20),
+            bytes_accessed=len(sets) * (1 << 18),
             transcendentals=0,
         ),
         compiler_params=pltpu.CompilerParams(vmem_limit_bytes=24 << 20),
@@ -186,12 +186,13 @@
         return add_products(q_here, sets, routes, acc, tile_count, cols, coded)
 
     first = [along(p_tiles, step) for step in range(3)]
-    sliced, *first = lax.optimization_barrier((sliced, *first))
+    sliced, first = lax.optimization_barrier((sliced, first))
+    second = [along(first[step], (step + 1) % 3) for step in range(3)]
+    sliced, second = lax.optimization_barrier((sliced, second))
+    third = along(second[0], 2)
+    crossed = [across(each) for each in [p_tiles] + first]
     q_here = lax.all_to_all(sliced, seat, split_axis=0, concat_axis=0, tiled=True)
-    second = [along(first[step], (step + 1) % 3) for step in range(3)]
-    crossed = [across(each) for each in [p_tiles] + first]
-    q_here, second, crossed = lax.optimization_barrier((q_here, second, crossed))
-    third = along(second[0], 2)
+    q_here, second = lax.optimization_barrier((q_here, second))
     acc = add(
         None,
         [p_tiles] + first + crossed,

time: 70.3 us -> 71.5 us (1.017)
  waiting for transfers between devices: 18.2 us -> 22.4 us
  starting transfers between devices: 17.1 us -> 14.9 us
  local copies, waits for them, and re-layouts: 1.65 us -> 0.01 us
  Pallas kernels: 10.7 us -> 11.7 us
    all_to_all x1, waiting for transfers between devices: 0.01 us -> 11.6 us  [body(): lax.all_to_all(sliced, seat, split_axis=0, concat_axis=0, tiled=True)]
    ppermute x7, waiting for transfers between devices: 18.2 us -> 10.8 us  [along(): return lax.ppermute(values, seat, hops)]
    ppermute x8, starting transfers between devices: 4.42 us -> 2.17 us  [across(): return lax.ppermute(values, seat, [(s, s ^ cols) for s in range(SEATS)])]
    unnamed x6 -> x2, local copies, waits for them, and re-layouts: 1.65 us -> 0.01 us
    all_to_all x1, starting transfers between devices: 3.99 us -> 5.38 us  [body(): lax.all_to_all(sliced, seat, split_axis=0, concat_axis=0, tiled=True)]
    ppermute x7, starting transfers between devices: 8.72 us -> 7.34 us  [along(): return lax.ppermute(values, seat, hops)]
    pallas_call x3, Pallas kernels: 7.14 us -> 8.16 us  [add_products(): pl.pallas_call(functools.partial(product_kernel, tile_count, cols, routes...]
  transfers between devices with their start and end apart: 16 -> 16, of which waited for: 3 -> 5; matrix products, arithmetic and copies ran while one was open for 0% -> 0% of each run, Pallas kernels for 11% -> 12%
where the time goes in v12:
time: 71.5 us; the launch traced here: 71.3 us
  waiting for transfers between devices  22.4 us (31%)
  blocking collectives  22.2 us (31%)
  starting transfers between devices  14.9 us (21%)
  Pallas kernels  11.7 us (16%)
    all_to_all x1, blocking collectives, body(): lax.all_to_all(coded, every, split_axis=0, concat_axis=0, tiled=True)  22.2 us
    all_to_all x1, waiting for transfers between devices, body(): lax.all_to_all(sliced, seat, split_axis=0, concat_axis=0, tiled=True)  11.6 us
    ppermute x7, waiting for transfers between devices, along(): return lax.ppermute(values, seat, hops)  10.8 us
    pallas_call x3, Pallas kernels, add_products(): pl.pallas_call(functools.partial(product_kernel, tile_count, cols, routes...  8.16 us
    ppermute x7, starting transfers between devices, along(): return lax.ppermute(values, seat, hops)  7.34 us
    all_to_all x1, starting transfers between devices, body(): lax.all_to_all(sliced, seat, split_axis=0, concat_axis=0, tiled=True)  5.38 us
    pallas_call x1, Pallas kernels, body(): pl.pallas_call(slice_kernel, out_shape=jax.ShapeDtypeStruct((SEATS, heigh...  2.31 us
    ppermute x8, starting transfers between devices, across(): return lax.ppermute(values, seat, [(s, s ^ cols) for s in range(SEATS)])  2.17 us
  transfers between devices with their start and end apart: 16, of which 5 were waited for; matrix products, arithmetic and copies ran while one was open for 0% of the time, Pallas kernels for 12%

profile of v12, /device:TPU:1, one launch (start us, length us, event | category | flops | bytes accessed | tf_op | source)
XLA Modules:
  0.0 71.3 jit_solution(6775978777918383151)
XLA Ops:
  0.0 2.1 %collective-permute-start.2 = (bf16[4,2,128,128]{3,2,1,0:T(8,128)(2,1)}, bf16[4,2,128,128]{3,2,1,0:T(8,128)(2,1)S(1)}, u32[]{:S(2)}, u32[]{:S(2)}) collective-permute-start(bf16[4,2,128,128]{3,2,1,0:T(8,128)(2,1)} %rest_0_.1), channel_id=1, source_target_pairs={{0,8},{1,9},{2,3},{3,2},{4,12},{5,13},{6,7},{7,6},{8,0},{9,1},{10,... | collective-permute-start | bytes 786440 | tf_op jit(solution)/shard_map/ppermute | solution.py:180
  2.1 1.3 %collective-permute-start.1 = (bf16[4,2,128,128]{3,2,1,0:T(8,128)(2,1)}, bf16[4,2,128,128]{3,2,1,0:T(8,128)(2,1)S(1)}, u32[]{:S(2)}, u32[]{:S(2)}) collective-permute-start(bf16[4,2,128,128]{3,2,1,0:T(8,128)(2,1)} %rest_0_.1), channel_id=1, source_target_pairs={{0,4},{1,5},{2,10},{3,11},{4,0},{5,1},{6,14},{7,15},{8,12},{9,13},... | collective-permute-start | bytes 786440 | tf_op jit(solution)/shard_map/ppermute | solution.py:180
  3.4 1.2 %collective-permute-start = (bf16[4,2,128,128]{3,2,1,0:T(8,128)(2,1)}, bf16[4,2,128,128]{3,2,1,0:T(8,128)(2,1)S(1)}, u32[]{:S(2)}, u32[]{:S(2)}) collective-permute-start(bf16[4,2,128,128]{3,2,1,0:T(8,128)(2,1)} %rest_0_.1), channel_id=1, source_target_pairs={{0,1},{1,0},{2,6},{3,7},{4,5},{5,4},{6,2},{7,3},{8,9},{9,8},{10,14... | collective-permute-start | bytes 786440 | tf_op jit(solution)/shard_map/ppermute | solution.py:180
  4.6 2.3 %cut_columns.1 = bf16[16,208,128]{2,1,0:T(8,128)(2,1)} custom-call(s32[2,4]{1,0:T(2,128)} %bitcast.3, s32[4,6]{1,0:T(4,128)} %q_ids.1, bf16[4,6,128,128]{3,2,1,0:T(8,128)(2,1)} %q_ref.1), custom_call_target="tpu_custom_call" | custom-call | bytes 8388608 | tf_op jit(solution)/shard_map/cut_columns/pallas_call | solution.py:170
  6.9 0.0 copy-start
  6.9 0.0 collective-permute-done.2.rest_3_
  6.9 3.2 %collective-permute-done.1.rest_2_ = bf16[4,2,128,128]{3,2,1,0:T(8,128)(2,1)S(1)} collective-permute-done((bf16[4,2,128,128]{3,2,1,0:T(8,128)(2,1)}, bf16[4,2,128,128]{3,2,1,0:T(8,128)(2,1)S(1)}, u32[]{:S(2)}, u32[]{:S(2)}) %collective-permute-start.1) | collective-permute-done | bytes 262176 | tf_op jit(solution)/shard_map/ppermute | solution.py:180
  10.1 1.7 %collective-permute-done.rest_1_ = bf16[4,2,128,128]{3,2,1,0:T(8,128)(2,1)S(1)} collective-permute-done((bf16[4,2,128,128]{3,2,1,0:T(8,128)(2,1)}, bf16[4,2,128,128]{3,2,1,0:T(8,128)(2,1)S(1)}, u32[]{:S(2)}, u32[]{:S(2)}) %collective-permute-start) | collective-permute-done | bytes 262176 | tf_op jit(solution)/shard_map/ppermute | solution.py:180
  11.7 0.0 collective-permute-start.3
  11.7 0.0 collective-permute-start.4
  11.7 1.4 %collective-permute-start.5 = (bf16[4,2,128,128]{3,2,1,0:T(8,128)(2,1)S(1)}, bf16[4,2,128,128]{3,2,1,0:T(8,128)(2,1)S(1)}, u32[]{:S(2)}, u32[]{:S(2)}) collective-permute-start(bf16[4,2,128,128]{3,2,1,0:T(8,128)(2,1)S(1)} %collective-permute-done.2.rest_3_), channel_id=1, source_target_pairs={{0,1},{1,0},{2,6},{3,7},{4,5},{5,4},{6,2},{7,3},{8,9},{9,8},{10,14... | collective-permute-start | bytes 786440 | tf_op jit(solution)/shard_map/ppermute | solution.py:180
  13.1 4.3 %collective-permute-done.3.rest_0_ = bf16[4,2,128,128]{3,2,1,0:T(8,128)(2,1)S(1)} collective-permute-done((bf16[4,2,128,128]{3,2,1,0:T(8,128)(2,1)S(1)}, bf16[4,2,128,128]{3,2,1,0:T(8,128)(2,1)S(1)}, u32[]{:S(2)}, u32[]{:S(2)}) %collective-permute-start.3) | collective-permute-done | bytes 262176 | tf_op jit(solution)/shard_map/ppermute | solution.py:180
  17.5 0.0 collective-permute-done.4.rest_1_
  17.5 1.6 %collective-permute-done.5.rest_2_ = bf16[4,2,128,128]{3,2,1,0:T(8,128)(2,1)S(1)} collective-permute-done((bf16[4,2,128,128]{3,2,1,0:T(8,128)(2,1)S(1)}, bf16[4,2,128,128]{3,2,1,0:T(8,128)(2,1)S(1)}, u32[]{:S(2)}, u32[]{:S(2)}) %collective-permute-start.5) | collective-permute-done | bytes 262176 | tf_op jit(solution)/shard_map/ppermute | solution.py:180
  19.0 5.4 %all-to-all-start = ((bf16[16,208,128]{2,1,0:T(8,128)(2,1)}), bf16[16,208,128]{2,1,0:T(8,128)(2,1)S(1)}, u32[]{:S(2)}, u32[]{:S(2)}) async-start(bf16[16,208,128]{2,1,0:T(8,128)(2,1)} %cut_columns.1), calls=%async_computation | async-start | bytes 1703936 | tf_op jit(solution)/shard_map/all_to_all | solution.py:194
  24.4 0.0 copy-done
  24.4 0.2 collective-permute-start.7
  24.6 0.4 collective-permute-start.8
  25.0 0.1 collective-permute-start.9
  25.1 0.4 collective-permute-start.10
  25.5 1.4 %collective-permute-start.6 = (bf16[4,2,128,128]{3,2,1,0:T(8,128)(2,1)S(1)}, bf16[4,2,128,128]{3,2,1,0:T(8,128)(2,1)S(1)}, u32[]{:S(2)}, u32[]{:S(2)}) collective-permute-start(bf16[4,2,128,128]{3,2,1,0:T(8,128)(2,1)S(1)} %collective-permute-done.3.rest_0_), channel_id=1, source_target_pairs={{0,8},{1,9},{2,3},{3,2},{4,12},{5,13},{6,7},{7,6},{8,0},{9,1},{10,... | collective-permute-start | bytes 786440 | tf_op jit(solution)/shard_map/ppermute | solution.py:180
  26.9 11.6 %all-to-all-done.q_ref = bf16[16,208,128]{2,1,0:T(8,128)(2,1)S(1)} async-done(((bf16[16,208,128]{2,1,0:T(8,128)(2,1)}), bf16[16,208,128]{2,1,0:T(8,128)(2,1)S(1)}, u32[]{:S(2)}, u32[]{:S(2)}) %all-to-all-start) | async-done | bytes 852000 | tf_op jit(solution)/shard_map/all_to_all | solution.py:194
  38.5 0.0 collective-permute-done.7.rest_4_
  38.5 0.0 collective-permute-start.12
  38.5 0.0 collective-permute-done.8.rest_5_
  38.5 0.5 collective-permute-start.13
  39.0 0.0 collective-permute-done.9.rest_6_
  39.0 0.1 collective-permute-start.14
  39.1 0.0 collective-permute-done.10.rest_7_
  39.1 3.9 %products.3.rest_6_ = f32[256,8,128]{2,1,0:T(8,128)S(1)} custom-call(bf16[16,208,128]{2,1,0:T(8,128)(2,1)S(1)} %all-to-all-done.q_ref, bf16[4,2,128,128]{3,2,1,0:T(8,128)(2,1)S(1)} %copy-done, bf16[4,2,128,128]{3,2,1,0:T(8,128)(2,1)S(1)} %collective-permute-done.rest_1_, bf16[4,2,128,128]{3,2,1,0:T(8,128)(2,1)S(1)} %collective-permute-done.1.rest_2_, ...), custom_call_target="tpu_custom_call" | custom-call | flops 100663296 | bytes 2097152 | tf_op jit(solution)/shard_map/products/pallas_call | solution.py:95
  43.0 0.0 collective-permute-done.6.rest_0_
  43.0 0.5 collective-permute-start.11
  43.5 0.0 collective-permute-done.12.rest_3_
  43.6 0.0 collective-permute-done.13.rest_4_
  43.6 0.0 collective-permute-done.14.rest_5_
  43.6 2.3 %products.4.rest_2_ = f32[256,8,128]{2,1,0:T(8,128)S(1)} custom-call(bf16[16,208,128]{2,1,0:T(8,128)(2,1)S(1)} %all-to-all-done.q_ref, bf16[4,2,128,128]{3,2,1,0:T(8,128)(2,1)S(1)} %collective-permute-done.3.rest_0_, bf16[4,2,128,128]{3,2,1,0:T(8,128)(2,1)S(1)} %collective-permute-done.4.rest_1_, ...), custom_call_target="tpu_custom_call", output_to_operand_aliasing={{}: (7, {})} | custom-call | flops 75497472 | bytes 1572864 | tf_op jit(solution)/shard_map/products/pallas_call | solution.py:95
  45.9 0.0 collective-permute-done.11.rest_1_
  45.9 1.9 %products.5 = s32[32,5,8,128]{3,2,1,0:T(8,128)S(1)} custom-call(bf16[16,208,128]{2,1,0:T(8,128)(2,1)S(1)} %all-to-all-done.q_ref, bf16[4,2,128,128]{3,2,1,0:T(8,128)(2,1)S(1)} %collective-permute-done.6.rest_0_, bf16[4,2,128,128]{3,2,1,0:T(8,128)(2,1)S(1)} %collective-permute-done.11.rest_1_, f32[256,8,128]{2,1,0:T(8,128)S(1)} %products.4.rest_2_), custom_call_target="tpu_custom_call" | custom-call | flops 25165824 | bytes 524288 | tf_op jit(solution)/shard_map/products/pallas_call | solution.py:95
  47.8 22.2 %all_to_all.10 = s32[32,5,8,128]{3,2,1,0:T(8,128)S(1)} all-to-all(s32[32,5,8,128]{3,2,1,0:T(8,128)S(1)} %products.5), channel_id=1, replica_groups=mesh['plane'=2,'pair'=4,'core'=2,'col'=2] {'plane','pair','core','col'}, dimensions={0} | all-to-all | bytes 1310720 | tf_op jit(solution)/shard_map/all_to_all | solution.py:207
  70.0 1.3 %turn.1 = f32[128,1024]{1,0:T(8,128)} custom-call(s32[2,16,5,8,128]{4,3,2,1,0:T(8,128)S(1)} %bitcast.2), custom_call_target="tpu_custom_call" | custom-call | tf_op jit(solution)/shard_map/turn/pallas_call | solution.py:208
Async XLA Ops:
  0.0 6.9 %collective-permute-start.2 = (bf16[4,2,128,128]{3,2,1,0:T(8,128)(2,1)}, bf16[4,2,128,128]{3,2,1,0:T(8,128)(2,1)S(1)}, u32[]{:S(2)}, u32[]{:S(2)}) collective-permute-start(bf16[4,2,128,128]{3,2,1,0:T(8,128)(2,1)} %rest_0_.1), channel_id=1, source_target_pairs={{0,8},{1,9},{2,3},{3,2},{4,12},{5,13},{6,7},{7,6},{8,0},{9,1},{10,... | collective-permute-start | bytes 786440 | tf_op jit(solution)/shard_map/ppermute | solution.py:180
  2.1 8.0 %collective-permute-start.1 = (bf16[4,2,128,128]{3,2,1,0:T(8,128)(2,1)}, bf16[4,2,128,128]{3,2,1,0:T(8,128)(2,1)S(1)}, u32[]{:S(2)}, u32[]{:S(2)}) collective-permute-start(bf16[4,2,128,128]{3,2,1,0:T(8,128)(2,1)} %rest_0_.1), channel_id=1, source_target_pairs={{0,4},{1,5},{2,10},{3,11},{4,0},{5,1},{6,14},{7,15},{8,12},{9,13},... | collective-permute-start | bytes 786440 | tf_op jit(solution)/shard_map/ppermute | solution.py:180
  3.4 8.4 %collective-permute-start = (bf16[4,2,128,128]{3,2,1,0:T(8,128)(2,1)}, bf16[4,2,128,128]{3,2,1,0:T(8,128)(2,1)S(1)}, u32[]{:S(2)}, u32[]{:S(2)}) collective-permute-start(bf16[4,2,128,128]{3,2,1,0:T(8,128)(2,1)} %rest_0_.1), channel_id=1, source_target_pairs={{0,1},{1,0},{2,6},{3,7},{4,5},{5,4},{6,2},{7,3},{8,9},{9,8},{10,14... | collective-permute-start | bytes 786440 | tf_op jit(solution)/shard_map/ppermute | solution.py:180
  6.9 17.5 %copy-start = (bf16[4,2,128,128]{3,2,1,0:T(8,128)(2,1)S(1)}, bf16[4,2,128,128]{3,2,1,0:T(8,128)(2,1)}, u32[]{:S(2)}) copy-start(bf16[4,2,128,128]{3,2,1,0:T(8,128)(2,1)} %rest_0_.1) | copy-start | bytes 786436
  11.7 5.7 %collective-permute-start.3 = (bf16[4,2,128,128]{3,2,1,0:T(8,128)(2,1)S(1)}, bf16[4,2,128,128]{3,2,1,0:T(8,128)(2,1)S(1)}, u32[]{:S(2)}, u32[]{:S(2)}) collective-permute-start(bf16[4,2,128,128]{3,2,1,0:T(8,128)(2,1)S(1)} %collective-permute-done.rest_1_), channel_id=1, source_target_pairs={{0,4},{1,5},{2,10},{3,11},{4,0},{5,1},{6,14},{7,15},{8,12},{9,13},... | collective-permute-start | bytes 786440 | tf_op jit(solution)/shard_map/ppermute | solution.py:180
  11.7 5.7 %collective-permute-start.4 = (bf16[4,2,128,128]{3,2,1,0:T(8,128)(2,1)S(1)}, bf16[4,2,128,128]{3,2,1,0:T(8,128)(2,1)S(1)}, u32[]{:S(2)}, u32[]{:S(2)}) collective-permute-start(bf16[4,2,128,128]{3,2,1,0:T(8,128)(2,1)S(1)} %collective-permute-done.1.rest_2_), channel_id=1, source_target_pairs={{0,8},{1,9},{2,3},{3,2},{4,12},{5,13},{6,7},{7,6},{8,0},{9,1},{10,... | collective-permute-start | bytes 786440 | tf_op jit(solution)/shard_map/ppermute | solution.py:180
  11.7 7.3 %collective-permute-start.5 = (bf16[4,2,128,128]{3,2,1,0:T(8,128)(2,1)S(1)}, bf16[4,2,128,128]{3,2,1,0:T(8,128)(2,1)S(1)}, u32[]{:S(2)}, u32[]{:S(2)}) collective-permute-start(bf16[4,2,128,128]{3,2,1,0:T(8,128)(2,1)S(1)} %collective-permute-done.2.rest_3_), channel_id=1, source_target_pairs={{0,1},{1,0},{2,6},{3,7},{4,5},{5,4},{6,2},{7,3},{8,9},{9,8},{10,14... | collective-permute-start | bytes 786440 | tf_op jit(solution)/shard_map/ppermute | solution.py:180
  19.0 19.5 %all-to-all-start = ((bf16[16,208,128]{2,1,0:T(8,128)(2,1)}), bf16[16,208,128]{2,1,0:T(8,128)(2,1)S(1)}, u32[]{:S(2)}, u32[]{:S(2)}) async-start(bf16[16,208,128]{2,1,0:T(8,128)(2,1)} %cut_columns.1), calls=%async_computation | async-start | bytes 1703936 | tf_op jit(solution)/shard_map/all_to_all | solution.py:194
  24.4 14.1 %collective-permute-start.7 = (bf16[4,2,128,128]{3,2,1,0:T(8,128)(2,1)S(1)}, bf16[4,2,128,128]{3,2,1,0:T(8,128)(2,1)S(1)}, u32[]{:S(2)}, u32[]{:S(2)}) collective-permute-start(bf16[4,2,128,128]{3,2,1,0:T(8,128)(2,1)S(1)} %copy-done), channel_id=1, source_target_pairs={{0,2},{1,3},{2,0},{3,1},{4,6},{5,7},{6,4},{7,5},{8,10},{9,11},{10,... | collective-permute-start | bytes 786440 | tf_op jit(solution)/shard_map/ppermute | solution.py:183
  24.6 13.9 %collective-permute-start.8 = (bf16[4,2,128,128]{3,2,1,0:T(8,128)(2,1)S(1)}, bf16[4,2,128,128]{3,2,1,0:T(8,128)(2,1)S(1)}, u32[]{:S(2)}, u32[]{:S(2)}) collective-permute-start(bf16[4,2,128,128]{3,2,1,0:T(8,128)(2,1)S(1)} %collective-permute-done.rest_1_), channel_id=1, source_target_pairs={{0,2},{1,3},{2,0},{3,1},{4,6},{5,7},{6,4},{7,5},{8,10},{9,11},{10,... | collective-permute-start | bytes 786440 | tf_op jit(solution)/shard_map/ppermute | solution.py:183
  25.0 14.0 %collective-permute-start.9 = (bf16[4,2,128,128]{3,2,1,0:T(8,128)(2,1)S(1)}, bf16[4,2,128,128]{3,2,1,0:T(8,128)(2,1)}, u32[]{:S(2)}, u32[]{:S(2)}) collective-permute-start(bf16[4,2,128,128]{3,2,1,0:T(8,128)(2,1)S(1)} %collective-permute-done.1.rest_2_), channel_id=1, source_target_pairs={{0,2},{1,3},{2,0},{3,1},{4,6},{5,7},{6,4},{7,5},{8,10},{9,11},{10,... | collective-permute-start | bytes 786440 | tf_op jit(solution)/shard_map/ppermute | solution.py:183
  25.1 14.0 %collective-permute-start.10 = (bf16[4,2,128,128]{3,2,1,0:T(8,128)(2,1)S(1)}, bf16[4,2,128,128]{3,2,1,0:T(8,128)(2,1)}, u32[]{:S(2)}, u32[]{:S(2)}) collective-permute-start(bf16[4,2,128,128]{3,2,1,0:T(8,128)(2,1)S(1)} %collective-permute-done.2.rest_3_), channel_id=1, source_target_pairs={{0,2},{1,3},{2,0},{3,1},{4,6},{5,7},{6,4},{7,5},{8,10},{9,11},{10,... | collective-permute-start | bytes 786440 | tf_op jit(solution)/shard_map/ppermute | solution.py:183
  25.5 17.5 %collective-permute-start.6 = (bf16[4,2,128,128]{3,2,1,0:T(8,128)(2,1)S(1)}, bf16[4,2,128,128]{3,2,1,0:T(8,128)(2,1)S(1)}, u32[]{:S(2)}, u32[]{:S(2)}) collective-permute-start(bf16[4,2,128,128]{3,2,1,0:T(8,128)(2,1)S(1)} %collective-permute-done.3.rest_0_), channel_id=1, source_target_pairs={{0,8},{1,9},{2,3},{3,2},{4,12},{5,13},{6,7},{7,6},{8,0},{9,1},{10,... | collective-permute-start | bytes 786440 | tf_op jit(solution)/shard_map/ppermute | solution.py:180
  38.5 5.0 %collective-permute-start.12 = (bf16[4,2,128,128]{3,2,1,0:T(8,128)(2,1)S(1)}, bf16[4,2,128,128]{3,2,1,0:T(8,128)(2,1)S(1)}, u32[]{:S(2)}, u32[]{:S(2)}) collective-permute-start(bf16[4,2,128,128]{3,2,1,0:T(8,128)(2,1)S(1)} %collective-permute-done.3.rest_0_), channel_id=1, source_target_pairs={{0,2},{1,3},{2,0},{3,1},{4,6},{5,7},{6,4},{7,5},{8,10},{9,11},{10,... | collective-permute-start | bytes 786440 | tf_op jit(solution)/shard_map/ppermute | solution.py:183
  38.5 5.0 %collective-permute-start.13 = (bf16[4,2,128,128]{3,2,1,0:T(8,128)(2,1)S(1)}, bf16[4,2,128,128]{3,2,1,0:T(8,128)(2,1)S(1)}, u32[]{:S(2)}, u32[]{:S(2)}) collective-permute-start(bf16[4,2,128,128]{3,2,1,0:T(8,128)(2,1)S(1)} %collective-permute-done.4.rest_1_), channel_id=1, source_target_pairs={{0,2},{1,3},{2,0},{3,1},{4,6},{5,7},{6,4},{7,5},{8,10},{9,11},{10,... | collective-permute-start | bytes 786440 | tf_op jit(solution)/shard_map/ppermute | solution.py:183
  39.0 4.5 %collective-permute-start.14 = (bf16[4,2,128,128]{3,2,1,0:T(8,128)(2,1)S(1)}, bf16[4,2,128,128]{3,2,1,0:T(8,128)(2,1)S(1)}, u32[]{:S(2)}, u32[]{:S(2)}) collective-permute-start(bf16[4,2,128,128]{3,2,1,0:T(8,128)(2,1)S(1)} %collective-permute-done.5.rest_2_), channel_id=1, source_target_pairs={{0,2},{1,3},{2,0},{3,1},{4,6},{5,7},{6,4},{7,5},{8,10},{9,11},{10,... | collective-permute-start | bytes 786440 | tf_op jit(solution)/shard_map/ppermute | solution.py:183
  43.0 2.9 %collective-permute-start.11 = (bf16[4,2,128,128]{3,2,1,0:T(8,128)(2,1)S(1)}, bf16[4,2,128,128]{3,2,1,0:T(8,128)(2,1)S(1)}, u32[]{:S(2)}, u32[]{:S(2)}) collective-permute-start(bf16[4,2,128,128]{3,2,1,0:T(8,128)(2,1)S(1)} %collective-permute-done.6.rest_0_), channel_id=1, source_target_pairs={{0,2},{1,3},{2,0},{3,1},{4,6},{5,7},{6,4},{7,5},{8,10},{9,11},{10,... | collective-permute-start | bytes 786440 | tf_op jit(solution)/shard_map/ppermute | solution.py:183

commit v13 on v10

--- a/solution.py
+++ b/solution.py
@@ -73,12 +73,13 @@
         for f in range(blocks):
             left = q_ref[seat, f * rows:(f + 1) * rows]
             start = f * (per_p + per_q)
+            right = jnp.concatenate([p_refs[i][f, k] for k in range(per_p)], axis=1)
+            product = jnp.dot(left, right, preferred_element_type=jnp.float32)
             for k in range(per_p):
-                product = jnp.dot(left, p_refs[i][f, k], preferred_element_type=jnp.float32)
                 base = ids[seat, start + k] * tile_count
                 for l in range(per_q):
                     spot = base + ids[seat, start + per_p + l]
-                    acc_ref[spot] += product[l * strip:(l + 1) * strip]
+                    acc_ref[spot] += product[l * strip:(l + 1) * strip, k * extent:(k + 1) * extent]
     if coded:
         code(acc_ref, out_ref, tile_count // cols)
 
@@ -106,7 +107,7 @@
         input_output_aliases={} if acc is None or coded else {len(operands) - 1: 0},
         cost_estimate=pl.CostEstimate(
             flops=2 * len(sets) * per_p * rows * extent * extent,
-            bytes_accessed=len(sets) * (1 << 20),
+            bytes_accessed=len(sets) * (1 << 18),
             transcendentals=0,
         ),
         compiler_params=pltpu.CompilerParams(vmem_limit_bytes=24 << 20),
@@ -186,21 +187,21 @@
         return add_products(q_here, sets, routes, acc, tile_count, cols, coded)
 
     first = [along(p_tiles, step) for step in range(3)]
-    sliced, *first = lax.optimization_barrier((sliced, *first))
+    sliced, first = lax.optimization_barrier((sliced, first))
     q_here = lax.all_to_all(sliced, seat, split_axis=0, concat_axis=0, tiled=True)
     second = [along(first[step], (step + 1) % 3) for step in range(3)]
     crossed = [across(each) for each in [p_tiles] + first]
-    q_here, second, crossed = lax.optimization_barrier((q_here, second, crossed))
+    acc = add(
+        None, [p_tiles] + first + crossed[:2], [(0, 0), (1, 0), (2, 0), (3, 0), (0, 1), (1, 1)]
+    )
+    second, acc = lax.optimization_barrier((second, acc))
     third = along(second[0], 2)
-    acc = add(
-        None,
-        [p_tiles] + first + crossed,
-        [(step, swapped) for swapped in (0, 1) for step in range(4)],
-    )
+    sets = second + crossed[2:] + [across(each) for each in second]
+    acc = add(acc, sets, [(4, 0), (5, 0), (6, 0), (2, 1), (3, 1), (4, 1), (5, 1), (6, 1)])
     third, acc = lax.optimization_barrier((third, acc))
-    sets = second + [across(each) for each in second]
-    acc = add(acc, sets, [(step, swapped) for swapped in (0, 1) for step in (4, 5, 6)])
-    coded = add(acc, [third, across(third)], [(7, 0), (7, 1)], coded=True)
+    beside = across(third)
+    acc = add(acc, [third], [(7, 0)])
+    coded = add(acc, [beside], [(7, 1)], coded=True)
     every = ("plane",) + seat
     tiles = tile_count // cols
     landed = lax.all_to_all(coded, every, split_axis=0, concat_axis=0, tiled=True)

time: 70.3 us -> 68.9 us (0.980)
  waiting for transfers between devices: 18.2 us -> 15.5 us
    ppermute x7, waiting for transfers between devices: 18.2 us -> 6.94 us  [along(): return lax.ppermute(values, seat, hops)]
    all_to_all x1, waiting for transfers between devices: 0.01 us -> 8.21 us  [body(): lax.all_to_all(sliced, seat, split_axis=0, concat_axis=0, tiled=True)]
    ppermute x7, starting transfers between devices: 8.72 us -> 9.59 us  [along(): return lax.ppermute(values, seat, hops)]
    pallas_call x3 -> x4, Pallas kernels: 7.14 us -> 7.67 us  [add_products(): pl.pallas_call(functools.partial(product_kernel, tile_count, cols, routes...]
  transfers between devices with their start and end apart: 16 -> 16, of which waited for: 3 -> 7; matrix products, arithmetic and copies ran while one was open for 0% -> 0% of each run, Pallas kernels for 11% -> 12%
where the time goes in v13:
time: 68.9 us; the launch traced here: 68.7 us
  blocking collectives  22.5 us (33%)
  starting transfers between devices  17.7 us (26%)
  waiting for transfers between devices  15.5 us (22%)
  Pallas kernels  11.3 us (16%)
  local copies, waits for them, and re-layouts  1.66 us (2%)
    all_to_all x1, blocking collectives, body(): lax.all_to_all(coded, every, split_axis=0, concat_axis=0, tiled=True)  22.5 us
    ppermute x7, starting transfers between devices, along(): return lax.ppermute(values, seat, hops)  9.59 us
    all_to_all x1, waiting for transfers between devices, body(): lax.all_to_all(sliced, seat, split_axis=0, concat_axis=0, tiled=True)  8.21 us
    pallas_call x4, Pallas kernels, add_products(): pl.pallas_call(functools.partial(product_kernel, tile_count, cols, routes...  7.67 us
    ppermute x7, waiting for transfers between devices, along(): return lax.ppermute(values, seat, hops)  6.94 us
    ppermute x8, starting transfers between devices, across(): return lax.ppermute(values, seat, [(s, s ^ cols) for s in range(SEATS)])  4.1 us
    all_to_all x1, starting transfers between devices, body(): lax.all_to_all(sliced, seat, split_axis=0, concat_axis=0, tiled=True)  3.99 us
    pallas_call x1, Pallas kernels, body(): pl.pallas_call(slice_kernel, out_shape=jax.ShapeDtypeStruct((SEATS, heigh...  2.32 us
  transfers between devices with their start and end apart: 16, of which 7 were waited for; matrix products, arithmetic and copies ran while one was open for 0% of the time, Pallas kernels for 12%

profile of v13, /device:TPU:1, one launch (start us, length us, event | category | flops | bytes accessed | tf_op | source)
XLA Modules:
  0.0 68.7 jit_solution(17967195598318134623)
XLA Ops:
  0.0 2.1 %collective-permute-start.2 = (bf16[4,2,128,128]{3,2,1,0:T(8,128)(2,1)}, bf16[4,2,128,128]{3,2,1,0:T(8,128)(2,1)S(1)}, u32[]{:S(2)}, u32[]{:S(2)}) collective-permute-start(bf16[4,2,128,128]{3,2,1,0:T(8,128)(2,1)} %rest_0_.1), channel_id=1, source_target_pairs={{0,8},{1,9},{2,3},{3,2},{4,12},{5,13},{6,7},{7,6},{8,0},{9,1},{10,... | collective-permute-start | bytes 786440 | tf_op jit(solution)/shard_map/ppermute | solution.py:181
  2.1 1.3 %collective-permute-start.1 = (bf16[4,2,128,128]{3,2,1,0:T(8,128)(2,1)}, bf16[4,2,128,128]{3,2,1,0:T(8,128)(2,1)S(1)}, u32[]{:S(2)}, u32[]{:S(2)}) collective-permute-start(bf16[4,2,128,128]{3,2,1,0:T(8,128)(2,1)} %rest_0_.1), channel_id=1, source_target_pairs={{0,4},{1,5},{2,10},{3,11},{4,0},{5,1},{6,14},{7,15},{8,12},{9,13},... | collective-permute-start | bytes 786440 | tf_op jit(solution)/shard_map/ppermute | solution.py:181
  3.4 1.2 %collective-permute-start = (bf16[4,2,128,128]{3,2,1,0:T(8,128)(2,1)}, bf16[4,2,128,128]{3,2,1,0:T(8,128)(2,1)S(1)}, u32[]{:S(2)}, u32[]{:S(2)}) collective-permute-start(bf16[4,2,128,128]{3,2,1,0:T(8,128)(2,1)} %rest_0_.1), channel_id=1, source_target_pairs={{0,1},{1,0},{2,6},{3,7},{4,5},{5,4},{6,2},{7,3},{8,9},{9,8},{10,14... | collective-permute-start | bytes 786440 | tf_op jit(solution)/shard_map/ppermute | solution.py:181
  4.6 2.3 %cut_columns.1 = bf16[16,208,128]{2,1,0:T(8,128)(2,1)} custom-call(s32[2,4]{1,0:T(2,128)} %bitcast.3, s32[4,6]{1,0:T(4,128)} %q_ids.1, bf16[4,6,128,128]{3,2,1,0:T(8,128)(2,1)} %q_ref.1), custom_call_target="tpu_custom_call" | custom-call | bytes 8388608 | tf_op jit(solution)/shard_map/cut_columns/pallas_call | solution.py:171
  6.9 0.0 copy-start
  6.9 0.0 collective-permute-done.2.rest_3_
  6.9 3.1 %collective-permute-done.1.rest_2_ = bf16[4,2,128,128]{3,2,1,0:T(8,128)(2,1)S(1)} collective-permute-done((bf16[4,2,128,128]{3,2,1,0:T(8,128)(2,1)}, bf16[4,2,128,128]{3,2,1,0:T(8,128)(2,1)S(1)}, u32[]{:S(2)}, u32[]{:S(2)}) %collective-permute-start.1) | collective-permute-done | bytes 262176 | tf_op jit(solution)/shard_map/ppermute | solution.py:181
  10.1 1.7 %collective-permute-done.rest_1_ = bf16[4,2,128,128]{3,2,1,0:T(8,128)(2,1)S(1)} collective-permute-done((bf16[4,2,128,128]{3,2,1,0:T(8,128)(2,1)}, bf16[4,2,128,128]{3,2,1,0:T(8,128)(2,1)S(1)}, u32[]{:S(2)}, u32[]{:S(2)}) %collective-permute-start) | collective-permute-done | bytes 262176 | tf_op jit(solution)/shard_map/ppermute | solution.py:181
  11.7 4.0 %all-to-all-start = ((bf16[16,208,128]{2,1,0:T(8,128)(2,1)}), bf16[16,208,128]{2,1,0:T(8,128)(2,1)S(1)}, u32[]{:S(2)}, u32[]{:S(2)}) async-start(bf16[16,208,128]{2,1,0:T(8,128)(2,1)} %cut_columns.1), calls=%async_computation | async-start | bytes 1703936 | tf_op jit(solution)/shard_map/all_to_all | solution.py:191
  15.7 0.0 copy-done
  15.7 0.3 collective-permute-start.6
  16.0 0.3 collective-permute-start.7
  16.3 1.4 %collective-permute-start.3 = (bf16[4,2,128,128]{3,2,1,0:T(8,128)(2,1)S(1)}, bf16[4,2,128,128]{3,2,1,0:T(8,128)(2,1)S(1)}, u32[]{:S(2)}, u32[]{:S(2)}) collective-permute-start(bf16[4,2,128,128]{3,2,1,0:T(8,128)(2,1)S(1)} %collective-permute-done.rest_1_), channel_id=1, source_target_pairs={{0,4},{1,5},{2,10},{3,11},{4,0},{5,1},{6,14},{7,15},{8,12},{9,13},... | collective-permute-start | bytes 786440 | tf_op jit(solution)/shard_map/ppermute | solution.py:181
  17.7 1.2 %collective-permute-start.4 = (bf16[4,2,128,128]{3,2,1,0:T(8,128)(2,1)S(1)}, bf16[4,2,128,128]{3,2,1,0:T(8,128)(2,1)S(1)}, u32[]{:S(2)}, u32[]{:S(2)}) collective-permute-start(bf16[4,2,128,128]{3,2,1,0:T(8,128)(2,1)S(1)} %collective-permute-done.1.rest_2_), channel_id=1, source_target_pairs={{0,8},{1,9},{2,3},{3,2},{4,12},{5,13},{6,7},{7,6},{8,0},{9,1},{10,... | collective-permute-start | bytes 786440 | tf_op jit(solution)/shard_map/ppermute | solution.py:181
  18.9 1.2 %collective-permute-start.5 = (bf16[4,2,128,128]{3,2,1,0:T(8,128)(2,1)S(1)}, bf16[4,2,128,128]{3,2,1,0:T(8,128)(2,1)S(1)}, u32[]{:S(2)}, u32[]{:S(2)}) collective-permute-start(bf16[4,2,128,128]{3,2,1,0:T(8,128)(2,1)S(1)} %collective-permute-done.2.rest_3_), channel_id=1, source_target_pairs={{0,1},{1,0},{2,6},{3,7},{4,5},{5,4},{6,2},{7,3},{8,9},{9,8},{10,14... | collective-permute-start | bytes 786440 | tf_op jit(solution)/shard_map/ppermute | solution.py:181
  20.1 0.0 collective-permute-done.6.rest_4_
  20.1 1.2 %collective-permute-start.9 = (bf16[4,2,128,128]{3,2,1,0:T(8,128)(2,1)S(1)}, bf16[4,2,128,128]{3,2,1,0:T(8,128)(2,1)S(1)}, u32[]{:S(2)}, u32[]{:S(2)}) collective-permute-start(bf16[4,2,128,128]{3,2,1,0:T(8,128)(2,1)S(1)} %collective-permute-done.1.rest_2_), channel_id=1, source_target_pairs={{0,2},{1,3},{2,0},{3,1},{4,6},{5,7},{6,4},{7,5},{8,10},{9,11},{10,... | collective-permute-start | bytes 786440 | tf_op jit(solution)/shard_map/ppermute | solution.py:184
  21.3 0.0 collective-permute-done.7.rest_5_
  21.3 0.0 copy-start.1
  21.3 0.7 %copy-done.1 = bf16[4,2,128,128]{3,2,1,0:T(8,128)(2,1)} copy-done((bf16[4,2,128,128]{3,2,1,0:T(8,128)(2,1)}, bf16[4,2,128,128]{3,2,1,0:T(8,128)(2,1)S(1)}, u32[]{:S(2)}) %copy-start.1) | copy-done | bytes 262168
  22.0 0.0 collective-permute-start.10
  22.1 8.2 %all-to-all-done.q_ref = bf16[16,208,128]{2,1,0:T(8,128)(2,1)S(1)} async-done(((bf16[16,208,128]{2,1,0:T(8,128)(2,1)}), bf16[16,208,128]{2,1,0:T(8,128)(2,1)S(1)}, u32[]{:S(2)}, u32[]{:S(2)}) %all-to-all-start) | async-done | bytes 852000 | tf_op jit(solution)/shard_map/all_to_all | solution.py:191
  30.3 0.0 copy-start.2
  30.3 0.9 %copy-done.2 = bf16[4,2,128,128]{3,2,1,0:T(8,128)(2,1)S(1)} copy-done((bf16[4,2,128,128]{3,2,1,0:T(8,128)(2,1)S(1)}, bf16[4,2,128,128]{3,2,1,0:T(8,128)(2,1)}, u32[]{:S(2)}) %copy-start.2) | copy-done | bytes 262168
  31.2 2.3 %products.4.rest_8_ = f32[256,8,128]{2,1,0:T(8,128)S(1)} custom-call(bf16[16,208,128]{2,1,0:T(8,128)(2,1)S(1)} %all-to-all-done.q_ref, bf16[4,2,128,128]{3,2,1,0:T(8,128)(2,1)S(1)} %copy-done, bf16[4,2,128,128]{3,2,1,0:T(8,128)(2,1)S(1)} %collective-permute-done.rest_1_, bf16[4,2,128,128]{3,2,1,0:T(8,128)(2,1)S(1)} %collective-permute-done.1.rest_2_, ...), custom_call_target="tpu_custom_call" | custom-call | flops 75497472 | bytes 1572864 | tf_op jit(solution)/shard_map/products/pallas_call | solution.py:96
  33.5 0.0 collective-permute-done.3.rest_0_
  33.6 0.0 collective-permute-done.4.rest_1_
  33.6 0.7 %collective-permute-done.5.rest_2_ = bf16[4,2,128,128]{3,2,1,0:T(8,128)(2,1)S(1)} collective-permute-done((bf16[4,2,128,128]{3,2,1,0:T(8,128)(2,1)S(1)}, bf16[4,2,128,128]{3,2,1,0:T(8,128)(2,1)S(1)}, u32[]{:S(2)}, u32[]{:S(2)}) %collective-permute-start.5) | collective-permute-done | bytes 262176 | tf_op jit(solution)/shard_map/ppermute | solution.py:181
  34.3 0.9 %collective-permute-start.12 = (bf16[4,2,128,128]{3,2,1,0:T(8,128)(2,1)S(1)}, bf16[4,2,128,128]{3,2,1,0:T(8,128)(2,1)S(1)}, u32[]{:S(2)}, u32[]{:S(2)}) collective-permute-start(bf16[4,2,128,128]{3,2,1,0:T(8,128)(2,1)S(1)} %collective-permute-done.4.rest_1_), channel_id=1, source_target_pairs={{0,2},{1,3},{2,0},{3,1},{4,6},{5,7},{6,4},{7,5},{8,10},{9,11},{10,... | collective-permute-start | bytes 786440 | tf_op jit(solution)/shard_map/ppermute | solution.py:184
  35.2 0.1 collective-permute-start.13
  35.3 0.4 collective-permute-start.11
  35.7 0.0 collective-permute-done.9.rest_3_
  35.7 1.2 %collective-permute-start.8 = (bf16[4,2,128,128]{3,2,1,0:T(8,128)(2,1)S(1)}, bf16[4,2,128,128]{3,2,1,0:T(8,128)(2,1)S(1)}, u32[]{:S(2)}, u32[]{:S(2)}) collective-permute-start(bf16[4,2,128,128]{3,2,1,0:T(8,128)(2,1)S(1)} %collective-permute-done.3.rest_0_), channel_id=1, source_target_pairs={{0,8},{1,9},{2,3},{3,2},{4,12},{5,13},{6,7},{7,6},{8,0},{9,1},{10,... | collective-permute-start | bytes 786440 | tf_op jit(solution)/shard_map/ppermute | solution.py:181
  36.9 0.0 collective-permute-done.10.rest_4_
  36.9 0.0 collective-permute-done.12.rest_6_
  36.9 0.0 collective-permute-done.13.rest_7_
  36.9 0.2 collective-permute-done.11.rest_5_
  37.1 2.8 %products.5.rest_1_ = f32[256,8,128]{2,1,0:T(8,128)S(1)} custom-call(bf16[16,208,128]{2,1,0:T(8,128)(2,1)S(1)} %all-to-all-done.q_ref, bf16[4,2,128,128]{3,2,1,0:T(8,128)(2,1)S(1)} %collective-permute-done.3.rest_0_, bf16[4,2,128,128]{3,2,1,0:T(8,128)(2,1)S(1)} %collective-permute-done.4.rest_1_, ...), custom_call_target="tpu_custom_call", output_to_operand_aliasing={{}: (9, {})} | custom-call | flops 100663296 | bytes 2097152 | tf_op jit(solution)/shard_map/products/pallas_call | solution.py:96
  39.9 1.3 %collective-permute-done.8.rest_0_ = bf16[4,2,128,128]{3,2,1,0:T(8,128)(2,1)S(1)} collective-permute-done((bf16[4,2,128,128]{3,2,1,0:T(8,128)(2,1)S(1)}, bf16[4,2,128,128]{3,2,1,0:T(8,128)(2,1)S(1)}, u32[]{:S(2)}, u32[]{:S(2)}) %collective-permute-start.8) | collective-permute-done | bytes 262176 | tf_op jit(solution)/shard_map/ppermute | solution.py:181
  41.2 0.9 %collective-permute-start.14 = (bf16[4,2,128,128]{3,2,1,0:T(8,128)(2,1)S(1)}, bf16[4,2,128,128]{3,2,1,0:T(8,128)(2,1)S(1)}, u32[]{:S(2)}, u32[]{:S(2)}) collective-permute-start(bf16[4,2,128,128]{3,2,1,0:T(8,128)(2,1)S(1)} %collective-permute-done.8.rest_0_), channel_id=1, source_target_pairs={{0,2},{1,3},{2,0},{3,1},{4,6},{5,7},{6,4},{7,5},{8,10},{9,11},{10,... | collective-permute-start | bytes 786440 | tf_op jit(solution)/shard_map/ppermute | solution.py:184
  42.2 1.0 %products.6.rest_1_ = f32[256,8,128]{2,1,0:T(8,128)S(1)} custom-call(bf16[16,208,128]{2,1,0:T(8,128)(2,1)S(1)} %all-to-all-done.q_ref, bf16[4,2,128,128]{3,2,1,0:T(8,128)(2,1)S(1)} %collective-permute-done.8.rest_0_, f32[256,8,128]{2,1,0:T(8,128)S(1)} %products.5.rest_1_), custom_call_target="tpu_custom_call", output_to_operand_aliasing={{}: (2, {})} | custom-call | flops 12582912 | bytes 262144 | tf_op jit(solution)/shard_map/products/pallas_call | solution.py:96
  43.2 0.2 collective-permute-done.14.rest_0_
  43.3 1.6 %products.7 = s32[32,5,8,128]{3,2,1,0:T(8,128)S(1)} custom-call(bf16[16,208,128]{2,1,0:T(8,128)(2,1)S(1)} %all-to-all-done.q_ref, bf16[4,2,128,128]{3,2,1,0:T(8,128)(2,1)S(1)} %collective-permute-done.14.rest_0_, f32[256,8,128]{2,1,0:T(8,128)S(1)} %products.6.rest_1_), custom_call_target="tpu_custom_call" | custom-call | flops 12582912 | bytes 262144 | tf_op jit(solution)/shard_map/products/pallas_call | solution.py:96
  44.9 22.5 %all_to_all.10 = s32[32,5,8,128]{3,2,1,0:T(8,128)S(1)} all-to-all(s32[32,5,8,128]{3,2,1,0:T(8,128)S(1)} %products.7), channel_id=1, replica_groups=mesh['plane'=2,'pair'=4,'core'=2,'col'=2] {'plane','pair','core','col'}, dimensions={0} | all-to-all | bytes 1310720 | tf_op jit(solution)/shard_map/all_to_all | solution.py:207
  67.4 1.3 %turn.1 = f32[128,1024]{1,0:T(8,128)} custom-call(s32[2,16,5,8,128]{4,3,2,1,0:T(8,128)S(1)} %bitcast.2), custom_call_target="tpu_custom_call" | custom-call | tf_op jit(solution)/shard_map/turn/pallas_call | solution.py:208
Async XLA Ops:
  0.0 6.9 %collective-permute-start.2 = (bf16[4,2,128,128]{3,2,1,0:T(8,128)(2,1)}, bf16[4,2,128,128]{3,2,1,0:T(8,128)(2,1)S(1)}, u32[]{:S(2)}, u32[]{:S(2)}) collective-permute-start(bf16[4,2,128,128]{3,2,1,0:T(8,128)(2,1)} %rest_0_.1), channel_id=1, source_target_pairs={{0,8},{1,9},{2,3},{3,2},{4,12},{5,13},{6,7},{7,6},{8,0},{9,1},{10,... | collective-permute-start | bytes 786440 | tf_op jit(solution)/shard_map/ppermute | solution.py:181
  2.1 8.0 %collective-permute-start.1 = (bf16[4,2,128,128]{3,2,1,0:T(8,128)(2,1)}, bf16[4,2,128,128]{3,2,1,0:T(8,128)(2,1)S(1)}, u32[]{:S(2)}, u32[]{:S(2)}) collective-permute-start(bf16[4,2,128,128]{3,2,1,0:T(8,128)(2,1)} %rest_0_.1), channel_id=1, source_target_pairs={{0,4},{1,5},{2,10},{3,11},{4,0},{5,1},{6,14},{7,15},{8,12},{9,13},... | collective-permute-start | bytes 786440 | tf_op jit(solution)/shard_map/ppermute | solution.py:181
  3.4 8.4 %collective-permute-start = (bf16[4,2,128,128]{3,2,1,0:T(8,128)(2,1)}, bf16[4,2,128,128]{3,2,1,0:T(8,128)(2,1)S(1)}, u32[]{:S(2)}, u32[]{:S(2)}) collective-permute-start(bf16[4,2,128,128]{3,2,1,0:T(8,128)(2,1)} %rest_0_.1), channel_id=1, source_target_pairs={{0,1},{1,0},{2,6},{3,7},{4,5},{5,4},{6,2},{7,3},{8,9},{9,8},{10,14... | collective-permute-start | bytes 786440 | tf_op jit(solution)/shard_map/ppermute | solution.py:181
  6.9 8.8 %copy-start = (bf16[4,2,128,128]{3,2,1,0:T(8,128)(2,1)S(1)}, bf16[4,2,128,128]{3,2,1,0:T(8,128)(2,1)}, u32[]{:S(2)}) copy-start(bf16[4,2,128,128]{3,2,1,0:T(8,128)(2,1)} %rest_0_.1) | copy-start | bytes 786436
  11.7 18.5 %all-to-all-start = ((bf16[16,208,128]{2,1,0:T(8,128)(2,1)}), bf16[16,208,128]{2,1,0:T(8,128)(2,1)S(1)}, u32[]{:S(2)}, u32[]{:S(2)}) async-start(bf16[16,208,128]{2,1,0:T(8,128)(2,1)} %cut_columns.1), calls=%async_computation | async-start | bytes 1703936 | tf_op jit(solution)/shard_map/all_to_all | solution.py:191
  15.7 4.4 %collective-permute-start.6 = (bf16[4,2,128,128]{3,2,1,0:T(8,128)(2,1)S(1)}, bf16[4,2,128,128]{3,2,1,0:T(8,128)(2,1)S(1)}, u32[]{:S(2)}, u32[]{:S(2)}) collective-permute-start(bf16[4,2,128,128]{3,2,1,0:T(8,128)(2,1)S(1)} %copy-done), channel_id=1, source_target_pairs={{0,2},{1,3},{2,0},{3,1},{4,6},{5,7},{6,4},{7,5},{8,10},{9,11},{10,... | collective-permute-start | bytes 786440 | tf_op jit(solution)/shard_map/ppermute | solution.py:184
  16.0 5.3 %collective-permute-start.7 = (bf16[4,2,128,128]{3,2,1,0:T(8,128)(2,1)S(1)}, bf16[4,2,128,128]{3,2,1,0:T(8,128)(2,1)S(1)}, u32[]{:S(2)}, u32[]{:S(2)}) collective-permute-start(bf16[4,2,128,128]{3,2,1,0:T(8,128)(2,1)S(1)} %collective-permute-done.rest_1_), channel_id=1, source_target_pairs={{0,2},{1,3},{2,0},{3,1},{4,6},{5,7},{6,4},{7,5},{8,10},{9,11},{10,... | collective-permute-start | bytes 786440 | tf_op jit(solution)/shard_map/ppermute | solution.py:184
  16.3 17.3 %collective-permute-start.3 = (bf16[4,2,128,128]{3,2,1,0:T(8,128)(2,1)S(1)}, bf16[4,2,128,128]{3,2,1,0:T(8,128)(2,1)S(1)}, u32[]{:S(2)}, u32[]{:S(2)}) collective-permute-start(bf16[4,2,128,128]{3,2,1,0:T(8,128)(2,1)S(1)} %collective-permute-done.rest_1_), channel_id=1, source_target_pairs={{0,4},{1,5},{2,10},{3,11},{4,0},{5,1},{6,14},{7,15},{8,12},{9,13},... | collective-permute-start | bytes 786440 | tf_op jit(solution)/shard_map/ppermute | solution.py:181
  17.7 15.9 %collective-permute-start.4 = (bf16[4,2,128,128]{3,2,1,0:T(8,128)(2,1)S(1)}, bf16[4,2,128,128]{3,2,1,0:T(8,128)(2,1)S(1)}, u32[]{:S(2)}, u32[]{:S(2)}) collective-permute-start(bf16[4,2,128,128]{3,2,1,0:T(8,128)(2,1)S(1)} %collective-permute-done.1.rest_2_), channel_id=1, source_target_pairs={{0,8},{1,9},{2,3},{3,2},{4,12},{5,13},{6,7},{7,6},{8,0},{9,1},{10,... | collective-permute-start | bytes 786440 | tf_op jit(solution)/shard_map/ppermute | solution.py:181
  18.9 15.4 %collective-permute-start.5 = (bf16[4,2,128,128]{3,2,1,0:T(8,128)(2,1)S(1)}, bf16[4,2,128,128]{3,2,1,0:T(8,128)(2,1)S(1)}, u32[]{:S(2)}, u32[]{:S(2)}) collective-permute-start(bf16[4,2,128,128]{3,2,1,0:T(8,128)(2,1)S(1)} %collective-permute-done.2.rest_3_), channel_id=1, source_target_pairs={{0,1},{1,0},{2,6},{3,7},{4,5},{5,4},{6,2},{7,3},{8,9},{9,8},{10,14... | collective-permute-start | bytes 786440 | tf_op jit(solution)/shard_map/ppermute | solution.py:181
  20.1 15.6 %collective-permute-start.9 = (bf16[4,2,128,128]{3,2,1,0:T(8,128)(2,1)S(1)}, bf16[4,2,128,128]{3,2,1,0:T(8,128)(2,1)S(1)}, u32[]{:S(2)}, u32[]{:S(2)}) collective-permute-start(bf16[4,2,128,128]{3,2,1,0:T(8,128)(2,1)S(1)} %collective-permute-done.1.rest_2_), channel_id=1, source_target_pairs={{0,2},{1,3},{2,0},{3,1},{4,6},{5,7},{6,4},{7,5},{8,10},{9,11},{10,... | collective-permute-start | bytes 786440 | tf_op jit(solution)/shard_map/ppermute | solution.py:184
  21.3 0.7 %copy-start.1 = (bf16[4,2,128,128]{3,2,1,0:T(8,128)(2,1)}, bf16[4,2,128,128]{3,2,1,0:T(8,128)(2,1)S(1)}, u32[]{:S(2)}) copy-start(bf16[4,2,128,128]{3,2,1,0:T(8,128)(2,1)S(1)} %collective-permute-done.7.rest_5_) | copy-start | bytes 786436
  22.0 14.9 %collective-permute-start.10 = (bf16[4,2,128,128]{3,2,1,0:T(8,128)(2,1)S(1)}, bf16[4,2,128,128]{3,2,1,0:T(8,128)(2,1)S(1)}, u32[]{:S(2)}, u32[]{:S(2)}) collective-permute-start(bf16[4,2,128,128]{3,2,1,0:T(8,128)(2,1)S(1)} %collective-permute-done.2.rest_3_), channel_id=1, source_target_pairs={{0,2},{1,3},{2,0},{3,1},{4,6},{5,7},{6,4},{7,5},{8,10},{9,11},{10,... | collective-permute-start | bytes 786440 | tf_op jit(solution)/shard_map/ppermute | solution.py:184
  30.3 1.0 %copy-start.2 = (bf16[4,2,128,128]{3,2,1,0:T(8,128)(2,1)S(1)}, bf16[4,2,128,128]{3,2,1,0:T(8,128)(2,1)}, u32[]{:S(2)}) copy-start(bf16[4,2,128,128]{3,2,1,0:T(8,128)(2,1)} %copy-done.1) | copy-start | bytes 786436
  34.3 2.6 %collective-permute-start.12 = (bf16[4,2,128,128]{3,2,1,0:T(8,128)(2,1)S(1)}, bf16[4,2,128,128]{3,2,1,0:T(8,128)(2,1)S(1)}, u32[]{:S(2)}, u32[]{:S(2)}) collective-permute-start(bf16[4,2,128,128]{3,2,1,0:T(8,128)(2,1)S(1)} %collective-permute-done.4.rest_1_), channel_id=1, source_target_pairs={{0,2},{1,3},{2,0},{3,1},{4,6},{5,7},{6,4},{7,5},{8,10},{9,11},{10,... | collective-permute-start | bytes 786440 | tf_op jit(solution)/shard_map/ppermute | solution.py:184
  35.2 1.7 %collective-permute-start.13 = (bf16[4,2,128,128]{3,2,1,0:T(8,128)(2,1)S(1)}, bf16[4,2,128,128]{3,2,1,0:T(8,128)(2,1)S(1)}, u32[]{:S(2)}, u32[]{:S(2)}) collective-permute-start(bf16[4,2,128,128]{3,2,1,0:T(8,128)(2,1)S(1)} %collective-permute-done.5.rest_2_), channel_id=1, source_target_pairs={{0,2},{1,3},{2,0},{3,1},{4,6},{5,7},{6,4},{7,5},{8,10},{9,11},{10,... | collective-permute-start | bytes 786440 | tf_op jit(solution)/shard_map/ppermute | solution.py:184
  35.3 1.8 %collective-permute-start.11 = (bf16[4,2,128,128]{3,2,1,0:T(8,128)(2,1)S(1)}, bf16[4,2,128,128]{3,2,1,0:T(8,128)(2,1)S(1)}, u32[]{:S(2)}, u32[]{:S(2)}) collective-permute-start(bf16[4,2,128,128]{3,2,1,0:T(8,128)(2,1)S(1)} %collective-permute-done.3.rest_0_), channel_id=1, source_target_pairs={{0,2},{1,3},{2,0},{3,1},{4,6},{5,7},{6,4},{7,5},{8,10},{9,11},{10,... | collective-permute-start | bytes 786440 | tf_op jit(solution)/shard_map/ppermute | solution.py:184
  35.7 5.5 %collective-permute-start.8 = (bf16[4,2,128,128]{3,2,1,0:T(8,128)(2,1)S(1)}, bf16[4,2,128,128]{3,2,1,0:T(8,128)(2,1)S(1)}, u32[]{:S(2)}, u32[]{:S(2)}) collective-permute-start(bf16[4,2,128,128]{3,2,1,0:T(8,128)(2,1)S(1)} %collective-permute-done.3.rest_0_), channel_id=1, source_target_pairs={{0,8},{1,9},{2,3},{3,2},{4,12},{5,13},{6,7},{7,6},{8,0},{9,1},{10,... | collective-permute-start | bytes 786440 | tf_op jit(solution)/shard_map/ppermute | solution.py:181
  41.2 2.1 %collective-permute-start.14 = (bf16[4,2,128,128]{3,2,1,0:T(8,128)(2,1)S(1)}, bf16[4,2,128,128]{3,2,1,0:T(8,128)(2,1)S(1)}, u32[]{:S(2)}, u32[]{:S(2)}) collective-permute-start(bf16[4,2,128,128]{3,2,1,0:T(8,128)(2,1)S(1)} %collective-permute-done.8.rest_0_), channel_id=1, source_target_pairs={{0,2},{1,3},{2,0},{3,1},{4,6},{5,7},{6,4},{7,5},{8,10},{9,11},{10,... | collective-permute-start | bytes 786440 | tf_op jit(solution)/shard_map/ppermute | solution.py:184

commit v14 on v13

--- a/solution.py
+++ b/solution.py
@@ -15,7 +15,7 @@
 
 def axes(core, cols):
     bits = [bit for bit in (1, 2, 4, 8) if bit != cols]
-    return bits[core:] + bits[:core]
+    return [bits[core], bits[1 - core], bits[2]]
 
 
 def origin(step, swapped, seat, cols):
@@ -186,22 +186,21 @@
     def add(acc, sets, routes, coded=False):
         return add_products(q_here, sets, routes, acc, tile_count, cols, coded)
 
-    first = [along(p_tiles, step) for step in range(3)]
-    sliced, first = lax.optimization_barrier((sliced, first))
+    one = along(p_tiles, 0)
+    sliced, one = lax.optimization_barrier((sliced, one))
     q_here = lax.all_to_all(sliced, seat, split_axis=0, concat_axis=0, tiled=True)
-    second = [along(first[step], (step + 1) % 3) for step in range(3)]
-    crossed = [across(each) for each in [p_tiles] + first]
+    second = [along(p_tiles, 1), along(p_tiles, 2), along(one, 1)]
     acc = add(
-        None, [p_tiles] + first + crossed[:2], [(0, 0), (1, 0), (2, 0), (3, 0), (0, 1), (1, 1)]
+        None, [p_tiles, one, across(p_tiles), across(one)], [(0, 0), (1, 0), (0, 1), (1, 1)]
     )
     second, acc = lax.optimization_barrier((second, acc))
-    third = along(second[0], 2)
-    sets = second + crossed[2:] + [across(each) for each in second]
-    acc = add(acc, sets, [(4, 0), (5, 0), (6, 0), (2, 1), (3, 1), (4, 1), (5, 1), (6, 1)])
+    third = [along(second[1], 1), along(second[1], 0), along(second[2], 2)]
+    sets = second + [across(each) for each in second]
+    acc = add(acc, sets, [(step, swapped) for swapped in (0, 1) for step in (2, 3, 4)])
     third, acc = lax.optimization_barrier((third, acc))
-    beside = across(third)
-    acc = add(acc, [third], [(7, 0)])
-    coded = add(acc, [beside], [(7, 1)], coded=True)
+    crossed = [across(each) for each in third]
+    acc = add(acc, third, [(5, 0), (6, 0), (7, 0)])
+    coded = add(acc, crossed, [(5, 1), (6, 1), (7, 1)], coded=True)
     every = ("plane",) + seat
     tiles = tile_count // cols
     landed = lax.all_to_all(coded, every, split_axis=0, concat_axis=0, tiled=True)

time: 68.9 us -> 71.1 us (1.032)
  waiting for transfers between devices: 15.5 us -> 19.2 us
  local copies, waits for them, and re-layouts: 1.66 us -> 0.01 us
    ppermute x7, starting transfers between devices: 9.59 us -> 6.71 us  [along(): return lax.ppermute(values, seat, hops)]
    all_to_all x1, starting transfers between devices: 3.99 us -> 6.53 us  [body(): lax.all_to_all(sliced, seat, split_axis=0, concat_axis=0, tiled=True)]
    all_to_all x1, waiting for transfers between devices: 8.21 us -> 10.6 us  [body(): lax.all_to_all(sliced, seat, split_axis=0, concat_axis=0, tiled=True)]
    unnamed x6 -> x2, local copies, waits for them, and re-layouts: 1.66 us -> 0.01 us
    ppermute x7, waiting for transfers between devices: 6.94 us -> 8.54 us  [along(): return lax.ppermute(values, seat, hops)]
  transfers between devices with their start and end apart: 16 -> 16, of which waited for: 7 -> 5; matrix products, arithmetic and copies ran while one was open for 0% -> 0% of each run, Pallas kernels for 12% -> 11%
where the time goes in v14:
time: 71.1 us; the launch traced here: 70.9 us
  blocking collectives  22.7 us (32%)
  waiting for transfers between devices  19.2 us (27%)
  starting transfers between devices  17.6 us (25%)
  Pallas kernels  11.3 us (16%)
    all_to_all x1, blocking collectives, body(): lax.all_to_all(coded, every, split_axis=0, concat_axis=0, tiled=True)  22.7 us
    all_to_all x1, waiting for transfers between devices, body(): lax.all_to_all(sliced, seat, split_axis=0, concat_axis=0, tiled=True)  10.6 us
    ppermute x7, waiting for transfers between devices, along(): return lax.ppermute(values, seat, hops)  8.54 us
    pallas_call x4, Pallas kernels, add_products(): pl.pallas_call(functools.partial(product_kernel, tile_count, cols, routes...  7.67 us
    ppermute x7, starting transfers between devices, along(): return lax.ppermute(values, seat, hops)  6.71 us
    all_to_all x1, starting transfers between devices, body(): lax.all_to_all(sliced, seat, split_axis=0, concat_axis=0, tiled=True)  6.53 us
    ppermute x8, starting transfers between devices, across(): return lax.ppermute(values, seat, [(s, s ^ cols) for s in range(SEATS)])  4.33 us
    pallas_call x1, Pallas kernels, body(): pl.pallas_call(slice_kernel, out_shape=jax.ShapeDtypeStruct((SEATS, heigh...  2.31 us
  transfers between devices with their start and end apart: 16, of which 5 were waited for; matrix products, arithmetic and copies ran while one was open for 0% of the time, Pallas kernels for 11%

profile of v14, /device:TPU:1, one launch (start us, length us, event | category | flops | bytes accessed | tf_op | source)
XLA Modules:
  0.0 70.9 jit_solution(11282241207381343138)
XLA Ops:
  0.0 2.0 %collective-permute-start = (bf16[4,2,128,128]{3,2,1,0:T(8,128)(2,1)}, bf16[4,2,128,128]{3,2,1,0:T(8,128)(2,1)S(1)}, u32[]{:S(2)}, u32[]{:S(2)}) collective-permute-start(bf16[4,2,128,128]{3,2,1,0:T(8,128)(2,1)} %rest_0_.1), channel_id=1, source_target_pairs={{0,1},{1,0},{2,6},{3,7},{4,5},{5,4},{6,2},{7,3},{8,9},{9,8},{10,14... | collective-permute-start | bytes 786440 | tf_op jit(solution)/shard_map/ppermute | solution.py:181
  2.0 2.3 %cut_columns.1 = bf16[16,208,128]{2,1,0:T(8,128)(2,1)} custom-call(s32[2,4]{1,0:T(2,128)} %bitcast.3, s32[4,6]{1,0:T(4,128)} %q_ids.1, bf16[4,6,128,128]{3,2,1,0:T(8,128)(2,1)} %q_ref.1), custom_call_target="tpu_custom_call" | custom-call | bytes 8388608 | tf_op jit(solution)/shard_map/cut_columns/pallas_call | solution.py:171
  4.4 0.0 copy-start
  4.4 1.9 %collective-permute-done.rest_1_ = bf16[4,2,128,128]{3,2,1,0:T(8,128)(2,1)S(1)} collective-permute-done((bf16[4,2,128,128]{3,2,1,0:T(8,128)(2,1)}, bf16[4,2,128,128]{3,2,1,0:T(8,128)(2,1)S(1)}, u32[]{:S(2)}, u32[]{:S(2)}) %collective-permute-start) | collective-permute-done | bytes 262176 | tf_op jit(solution)/shard_map/ppermute | solution.py:181
  6.3 6.5 %all-to-all-start = ((bf16[16,208,128]{2,1,0:T(8,128)(2,1)}), bf16[16,208,128]{2,1,0:T(8,128)(2,1)S(1)}, u32[]{:S(2)}, u32[]{:S(2)}) async-start(bf16[16,208,128]{2,1,0:T(8,128)(2,1)} %cut_columns.1), calls=%async_computation | async-start | bytes 1703936 | tf_op jit(solution)/shard_map/all_to_all | solution.py:191
  12.8 0.0 copy-done
  12.8 0.2 collective-permute-start.4
  13.0 0.4 collective-permute-start.5
  13.4 1.4 %collective-permute-start.1 = (bf16[4,2,128,128]{3,2,1,0:T(8,128)(2,1)S(1)}, bf16[4,2,128,128]{3,2,1,0:T(8,128)(2,1)S(1)}, u32[]{:S(2)}, u32[]{:S(2)}) collective-permute-start(bf16[4,2,128,128]{3,2,1,0:T(8,128)(2,1)S(1)} %copy-done), channel_id=1, source_target_pairs={{0,4},{1,5},{2,3},{3,2},{4,0},{5,1},{6,7},{7,6},{8,12},{9,13},{10,... | collective-permute-start | bytes 786440 | tf_op jit(solution)/shard_map/ppermute | solution.py:181
  14.8 1.2 %collective-permute-start.2 = (bf16[4,2,128,128]{3,2,1,0:T(8,128)(2,1)S(1)}, bf16[4,2,128,128]{3,2,1,0:T(8,128)(2,1)S(1)}, u32[]{:S(2)}, u32[]{:S(2)}) collective-permute-start(bf16[4,2,128,128]{3,2,1,0:T(8,128)(2,1)S(1)} %copy-done), channel_id=1, source_target_pairs={{0,8},{1,9},{2,10},{3,11},{4,12},{5,13},{6,14},{7,15},{8,0},{9,1},... | collective-permute-start | bytes 786440 | tf_op jit(solution)/shard_map/ppermute | solution.py:181
  16.0 0.3 collective-permute-start.3
  16.3 0.0 collective-permute-done.4.rest_2_
  16.3 0.0 collective-permute-done.5.rest_3_
  16.3 10.6 %all-to-all-done.q_ref = bf16[16,208,128]{2,1,0:T(8,128)(2,1)S(1)} async-done(((bf16[16,208,128]{2,1,0:T(8,128)(2,1)}), bf16[16,208,128]{2,1,0:T(8,128)(2,1)S(1)}, u32[]{:S(2)}, u32[]{:S(2)}) %all-to-all-start) | async-done | bytes 852000 | tf_op jit(solution)/shard_map/all_to_all | solution.py:191
  26.9 1.8 %products.4.rest_6_ = f32[256,8,128]{2,1,0:T(8,128)S(1)} custom-call(bf16[16,208,128]{2,1,0:T(8,128)(2,1)S(1)} %all-to-all-done.q_ref, bf16[4,2,128,128]{3,2,1,0:T(8,128)(2,1)S(1)} %copy-done, bf16[4,2,128,128]{3,2,1,0:T(8,128)(2,1)S(1)} %collective-permute-done.rest_1_, bf16[4,2,128,128]{3,2,1,0:T(8,128)(2,1)S(1)} %collective-permute-done.4.rest_2_, ...), custom_call_target="tpu_custom_call" | custom-call | flops 50331648 | bytes 1048576 | tf_op jit(solution)/shard_map/products/pallas_call | solution.py:96
  28.8 0.0 collective-permute-done.1.rest_0_
  28.8 1.9 %collective-permute-done.2.rest_1_ = bf16[4,2,128,128]{3,2,1,0:T(8,128)(2,1)S(1)} collective-permute-done((bf16[4,2,128,128]{3,2,1,0:T(8,128)(2,1)S(1)}, bf16[4,2,128,128]{3,2,1,0:T(8,128)(2,1)S(1)}, u32[]{:S(2)}, u32[]{:S(2)}) %collective-permute-start.2) | collective-permute-done | bytes 262176 | tf_op jit(solution)/shard_map/ppermute | solution.py:181
  30.6 0.0 collective-permute-done.3.rest_2_
  30.6 1.6 %collective-permute-start.10 = (bf16[4,2,128,128]{3,2,1,0:T(8,128)(2,1)S(1)}, bf16[4,2,128,128]{3,2,1,0:T(8,128)(2,1)S(1)}, u32[]{:S(2)}, u32[]{:S(2)}) collective-permute-start(bf16[4,2,128,128]{3,2,1,0:T(8,128)(2,1)S(1)} %collective-permute-done.2.rest_1_), channel_id=1, source_target_pairs={{0,2},{1,3},{2,0},{3,1},{4,6},{5,7},{6,4},{7,5},{8,10},{9,11},{10,... | collective-permute-start | bytes 786440 | tf_op jit(solution)/shard_map/ppermute | solution.py:184
  32.3 0.0 collective-permute-start.11
  32.3 0.5 collective-permute-start.9
  32.8 1.2 %collective-permute-start.6 = (bf16[4,2,128,128]{3,2,1,0:T(8,128)(2,1)S(1)}, bf16[4,2,128,128]{3,2,1,0:T(8,128)(2,1)S(1)}, u32[]{:S(2)}, u32[]{:S(2)}) collective-permute-start(bf16[4,2,128,128]{3,2,1,0:T(8,128)(2,1)S(1)} %collective-permute-done.2.rest_1_), channel_id=1, source_target_pairs={{0,4},{1,5},{2,3},{3,2},{4,0},{5,1},{6,7},{7,6},{8,12},{9,13},{10,... | collective-permute-start | bytes 786440 | tf_op jit(solution)/shard_map/ppermute | solution.py:181
  34.0 0.0 collective-permute-start.7
  34.0 0.0 collective-permute-done.10.rest_4_
  34.0 0.6 collective-permute-start.8
  34.6 0.0 collective-permute-done.11.rest_5_
  34.6 0.0 collective-permute-done.9.rest_3_
  34.6 2.3 %products.5.rest_3_ = f32[256,8,128]{2,1,0:T(8,128)S(1)} custom-call(bf16[16,208,128]{2,1,0:T(8,128)(2,1)S(1)} %all-to-all-done.q_ref, bf16[4,2,128,128]{3,2,1,0:T(8,128)(2,1)S(1)} %collective-permute-done.1.rest_0_, bf16[4,2,128,128]{3,2,1,0:T(8,128)(2,1)S(1)} %collective-permute-done.2.rest_1_, ...), custom_call_target="tpu_custom_call", output_to_operand_aliasing={{}: (7, {})} | custom-call | flops 75497472 | bytes 1572864 | tf_op jit(solution)/shard_map/products/pallas_call | solution.py:96
  36.9 3.7 %collective-permute-done.6.rest_0_ = bf16[4,2,128,128]{3,2,1,0:T(8,128)(2,1)S(1)} collective-permute-done((bf16[4,2,128,128]{3,2,1,0:T(8,128)(2,1)S(1)}, bf16[4,2,128,128]{3,2,1,0:T(8,128)(2,1)S(1)}, u32[]{:S(2)}, u32[]{:S(2)}) %collective-permute-start.6) | collective-permute-done | bytes 262176 | tf_op jit(solution)/shard_map/ppermute | solution.py:181
  40.6 1.0 %collective-permute-done.7.rest_1_ = bf16[4,2,128,128]{3,2,1,0:T(8,128)(2,1)S(1)} collective-permute-done((bf16[4,2,128,128]{3,2,1,0:T(8,128)(2,1)S(1)}, bf16[4,2,128,128]{3,2,1,0:T(8,128)(2,1)S(1)}, u32[]{:S(2)}, u32[]{:S(2)}) %collective-permute-start.7) | collective-permute-done | bytes 262176 | tf_op jit(solution)/shard_map/ppermute | solution.py:181
  41.6 0.0 collective-permute-done.8.rest_2_
  41.6 1.1 %collective-permute-start.12 = (bf16[4,2,128,128]{3,2,1,0:T(8,128)(2,1)S(1)}, bf16[4,2,128,128]{3,2,1,0:T(8,128)(2,1)S(1)}, u32[]{:S(2)}, u32[]{:S(2)}) collective-permute-start(bf16[4,2,128,128]{3,2,1,0:T(8,128)(2,1)S(1)} %collective-permute-done.6.rest_0_), channel_id=1, source_target_pairs={{0,2},{1,3},{2,0},{3,1},{4,6},{5,7},{6,4},{7,5},{8,10},{9,11},{10,... | collective-permute-start | bytes 786440 | tf_op jit(solution)/shard_map/ppermute | solution.py:184
  42.7 0.0 collective-permute-start.13
  42.7 0.5 collective-permute-start.14
  43.2 1.5 %products.6.rest_3_ = f32[256,8,128]{2,1,0:T(8,128)S(1)} custom-call(bf16[16,208,128]{2,1,0:T(8,128)(2,1)S(1)} %all-to-all-done.q_ref, bf16[4,2,128,128]{3,2,1,0:T(8,128)(2,1)S(1)} %collective-permute-done.6.rest_0_, bf16[4,2,128,128]{3,2,1,0:T(8,128)(2,1)S(1)} %collective-permute-done.7.rest_1_, ...), custom_call_target="tpu_custom_call", output_to_operand_aliasing={{}: (4, {})} | custom-call | flops 37748736 | bytes 786432 | tf_op jit(solution)/shard_map/products/pallas_call | solution.py:96
  44.7 0.0 collective-permute-done.12.rest_0_
  44.7 0.0 collective-permute-done.13.rest_1_
  44.7 0.0 collective-permute-done.14.rest_2_
  44.7 2.1 %products.7 = s32[32,5,8,128]{3,2,1,0:T(8,128)S(1)} custom-call(bf16[16,208,128]{2,1,0:T(8,128)(2,1)S(1)} %all-to-all-done.q_ref, bf16[4,2,128,128]{3,2,1,0:T(8,128)(2,1)S(1)} %collective-permute-done.12.rest_0_, bf16[4,2,128,128]{3,2,1,0:T(8,128)(2,1)S(1)} %collective-permute-done.13.rest_1_, bf16[4,2,128,128]{3,2,1,0:T(8,128)(2,1)S(1)} %collective-permute-done.14.rest_2_, ...), custom_call_target="tpu_custom_call" | custom-call | flops 37748736 | bytes 786432 | tf_op jit(solution)/shard_map/products/pallas_call | solution.py:96
  46.8 22.7 %all_to_all.10 = s32[32,5,8,128]{3,2,1,0:T(8,128)S(1)} all-to-all(s32[32,5,8,128]{3,2,1,0:T(8,128)S(1)} %products.7), channel_id=1, replica_groups=mesh['plane'=2,'pair'=4,'core'=2,'col'=2] {'plane','pair','core','col'}, dimensions={0} | all-to-all | bytes 1310720 | tf_op jit(solution)/shard_map/all_to_all | solution.py:206
  69.6 1.3 %turn.1 = f32[128,1024]{1,0:T(8,128)} custom-call(s32[2,16,5,8,128]{4,3,2,1,0:T(8,128)S(1)} %bitcast.2), custom_call_target="tpu_custom_call" | custom-call | tf_op jit(solution)/shard_map/turn/pallas_call | solution.py:207
Async XLA Ops:
  0.0 6.3 %collective-permute-start = (bf16[4,2,128,128]{3,2,1,0:T(8,128)(2,1)}, bf16[4,2,128,128]{3,2,1,0:T(8,128)(2,1)S(1)}, u32[]{:S(2)}, u32[]{:S(2)}) collective-permute-start(bf16[4,2,128,128]{3,2,1,0:T(8,128)(2,1)} %rest_0_.1), channel_id=1, source_target_pairs={{0,1},{1,0},{2,6},{3,7},{4,5},{5,4},{6,2},{7,3},{8,9},{9,8},{10,14... | collective-permute-start | bytes 786440 | tf_op jit(solution)/shard_map/ppermute | solution.py:181
  4.4 8.5 %copy-start = (bf16[4,2,128,128]{3,2,1,0:T(8,128)(2,1)S(1)}, bf16[4,2,128,128]{3,2,1,0:T(8,128)(2,1)}, u32[]{:S(2)}) copy-start(bf16[4,2,128,128]{3,2,1,0:T(8,128)(2,1)} %rest_0_.1) | copy-start | bytes 786436
  6.3 20.6 %all-to-all-start = ((bf16[16,208,128]{2,1,0:T(8,128)(2,1)}), bf16[16,208,128]{2,1,0:T(8,128)(2,1)S(1)}, u32[]{:S(2)}, u32[]{:S(2)}) async-start(bf16[16,208,128]{2,1,0:T(8,128)(2,1)} %cut_columns.1), calls=%async_computation | async-start | bytes 1703936 | tf_op jit(solution)/shard_map/all_to_all | solution.py:191
  12.8 3.4 %collective-permute-start.4 = (bf16[4,2,128,128]{3,2,1,0:T(8,128)(2,1)S(1)}, bf16[4,2,128,128]{3,2,1,0:T(8,128)(2,1)S(1)}, u32[]{:S(2)}, u32[]{:S(2)}) collective-permute-start(bf16[4,2,128,128]{3,2,1,0:T(8,128)(2,1)S(1)} %copy-done), channel_id=1, source_target_pairs={{0,2},{1,3},{2,0},{3,1},{4,6},{5,7},{6,4},{7,5},{8,10},{9,11},{10,... | collective-permute-start | bytes 786440 | tf_op jit(solution)/shard_map/ppermute | solution.py:184
  13.0 3.3 %collective-permute-start.5 = (bf16[4,2,128,128]{3,2,1,0:T(8,128)(2,1)S(1)}, bf16[4,2,128,128]{3,2,1,0:T(8,128)(2,1)S(1)}, u32[]{:S(2)}, u32[]{:S(2)}) collective-permute-start(bf16[4,2,128,128]{3,2,1,0:T(8,128)(2,1)S(1)} %collective-permute-done.rest_1_), channel_id=1, source_target_pairs={{0,2},{1,3},{2,0},{3,1},{4,6},{5,7},{6,4},{7,5},{8,10},{9,11},{10,... | collective-permute-start | bytes 786440 | tf_op jit(solution)/shard_map/ppermute | solution.py:184
  13.4 15.3 %collective-permute-start.1 = (bf16[4,2,128,128]{3,2,1,0:T(8,128)(2,1)S(1)}, bf16[4,2,128,128]{3,2,1,0:T(8,128)(2,1)S(1)}, u32[]{:S(2)}, u32[]{:S(2)}) collective-permute-start(bf16[4,2,128,128]{3,2,1,0:T(8,128)(2,1)S(1)} %copy-done), channel_id=1, source_target_pairs={{0,4},{1,5},{2,3},{3,2},{4,0},{5,1},{6,7},{7,6},{8,12},{9,13},{10,... | collective-permute-start | bytes 786440 | tf_op jit(solution)/shard_map/ppermute | solution.py:181
  14.8 15.8 %collective-permute-start.2 = (bf16[4,2,128,128]{3,2,1,0:T(8,128)(2,1)S(1)}, bf16[4,2,128,128]{3,2,1,0:T(8,128)(2,1)S(1)}, u32[]{:S(2)}, u32[]{:S(2)}) collective-permute-start(bf16[4,2,128,128]{3,2,1,0:T(8,128)(2,1)S(1)} %copy-done), channel_id=1, source_target_pairs={{0,8},{1,9},{2,10},{3,11},{4,12},{5,13},{6,14},{7,15},{8,0},{9,1},... | collective-permute-start | bytes 786440 | tf_op jit(solution)/shard_map/ppermute | solution.py:181
  16.0 14.7 %collective-permute-start.3 = (bf16[4,2,128,128]{3,2,1,0:T(8,128)(2,1)S(1)}, bf16[4,2,128,128]{3,2,1,0:T(8,128)(2,1)S(1)}, u32[]{:S(2)}, u32[]{:S(2)}) collective-permute-start(bf16[4,2,128,128]{3,2,1,0:T(8,128)(2,1)S(1)} %collective-permute-done.rest_1_), channel_id=1, source_target_pairs={{0,4},{1,5},{2,3},{3,2},{4,0},{5,1},{6,7},{7,6},{8,12},{9,13},{10,... | collective-permute-start | bytes 786440 | tf_op jit(solution)/shard_map/ppermute | solution.py:181
  30.6 3.3 %collective-permute-start.10 = (bf16[4,2,128,128]{3,2,1,0:T(8,128)(2,1)S(1)}, bf16[4,2,128,128]{3,2,1,0:T(8,128)(2,1)S(1)}, u32[]{:S(2)}, u32[]{:S(2)}) collective-permute-start(bf16[4,2,128,128]{3,2,1,0:T(8,128)(2,1)S(1)} %collective-permute-done.2.rest_1_), channel_id=1, source_target_pairs={{0,2},{1,3},{2,0},{3,1},{4,6},{5,7},{6,4},{7,5},{8,10},{9,11},{10,... | collective-permute-start | bytes 786440 | tf_op jit(solution)/shard_map/ppermute | solution.py:184
  32.3 2.3 %collective-permute-start.11 = (bf16[4,2,128,128]{3,2,1,0:T(8,128)(2,1)S(1)}, bf16[4,2,128,128]{3,2,1,0:T(8,128)(2,1)S(1)}, u32[]{:S(2)}, u32[]{:S(2)}) collective-permute-start(bf16[4,2,128,128]{3,2,1,0:T(8,128)(2,1)S(1)} %collective-permute-done.3.rest_2_), channel_id=1, source_target_pairs={{0,2},{1,3},{2,0},{3,1},{4,6},{5,7},{6,4},{7,5},{8,10},{9,11},{10,... | collective-permute-start | bytes 786440 | tf_op jit(solution)/shard_map/ppermute | solution.py:184
  32.3 2.3 %collective-permute-start.9 = (bf16[4,2,128,128]{3,2,1,0:T(8,128)(2,1)S(1)}, bf16[4,2,128,128]{3,2,1,0:T(8,128)(2,1)S(1)}, u32[]{:S(2)}, u32[]{:S(2)}) collective-permute-start(bf16[4,2,128,128]{3,2,1,0:T(8,128)(2,1)S(1)} %collective-permute-done.1.rest_0_), channel_id=1, source_target_pairs={{0,2},{1,3},{2,0},{3,1},{4,6},{5,7},{6,4},{7,5},{8,10},{9,11},{10,... | collective-permute-start | bytes 786440 | tf_op jit(solution)/shard_map/ppermute | solution.py:184
  32.8 7.8 %collective-permute-start.6 = (bf16[4,2,128,128]{3,2,1,0:T(8,128)(2,1)S(1)}, bf16[4,2,128,128]{3,2,1,0:T(8,128)(2,1)S(1)}, u32[]{:S(2)}, u32[]{:S(2)}) collective-permute-start(bf16[4,2,128,128]{3,2,1,0:T(8,128)(2,1)S(1)} %collective-permute-done.2.rest_1_), channel_id=1, source_target_pairs={{0,4},{1,5},{2,3},{3,2},{4,0},{5,1},{6,7},{7,6},{8,12},{9,13},{10,... | collective-permute-start | bytes 786440 | tf_op jit(solution)/shard_map/ppermute | solution.py:181
  34.0 7.6 %collective-permute-start.7 = (bf16[4,2,128,128]{3,2,1,0:T(8,128)(2,1)S(1)}, bf16[4,2,128,128]{3,2,1,0:T(8,128)(2,1)S(1)}, u32[]{:S(2)}, u32[]{:S(2)}) collective-permute-start(bf16[4,2,128,128]{3,2,1,0:T(8,128)(2,1)S(1)} %collective-permute-done.2.rest_1_), channel_id=1, source_target_pairs={{0,1},{1,0},{2,6},{3,7},{4,5},{5,4},{6,2},{7,3},{8,9},{9,8},{10,14... | collective-permute-start | bytes 786440 | tf_op jit(solution)/shard_map/ppermute | solution.py:181
  34.0 7.6 %collective-permute-start.8 = (bf16[4,2,128,128]{3,2,1,0:T(8,128)(2,1)S(1)}, bf16[4,2,128,128]{3,2,1,0:T(8,128)(2,1)S(1)}, u32[]{:S(2)}, u32[]{:S(2)}) collective-permute-start(bf16[4,2,128,128]{3,2,1,0:T(8,128)(2,1)S(1)} %collective-permute-done.3.rest_2_), channel_id=1, source_target_pairs={{0,8},{1,9},{2,10},{3,11},{4,12},{5,13},{6,14},{7,15},{8,0},{9,1},... | collective-permute-start | bytes 786440 | tf_op jit(solution)/shard_map/ppermute | solution.py:181
  41.6 3.1 %collective-permute-start.12 = (bf16[4,2,128,128]{3,2,1,0:T(8,128)(2,1)S(1)}, bf16[4,2,128,128]{3,2,1,0:T(8,128)(2,1)S(1)}, u32[]{:S(2)}, u32[]{:S(2)}) collective-permute-start(bf16[4,2,128,128]{3,2,1,0:T(8,128)(2,1)S(1)} %collective-permute-done.6.rest_0_), channel_id=1, source_target_pairs={{0,2},{1,3},{2,0},{3,1},{4,6},{5,7},{6,4},{7,5},{8,10},{9,11},{10,... | collective-permute-start | bytes 786440 | tf_op jit(solution)/shard_map/ppermute | solution.py:184
  42.7 2.0 %collective-permute-start.13 = (bf16[4,2,128,128]{3,2,1,0:T(8,128)(2,1)S(1)}, bf16[4,2,128,128]{3,2,1,0:T(8,128)(2,1)S(1)}, u32[]{:S(2)}, u32[]{:S(2)}) collective-permute-start(bf16[4,2,128,128]{3,2,1,0:T(8,128)(2,1)S(1)} %collective-permute-done.7.rest_1_), channel_id=1, source_target_pairs={{0,2},{1,3},{2,0},{3,1},{4,6},{5,7},{6,4},{7,5},{8,10},{9,11},{10,... | collective-permute-start | bytes 786440 | tf_op jit(solution)/shard_map/ppermute | solution.py:184
  42.7 2.0 %collective-permute-start.14 = (bf16[4,2,128,128]{3,2,1,0:T(8,128)(2,1)S(1)}, bf16[4,2,128,128]{3,2,1,0:T(8,128)(2,1)S(1)}, u32[]{:S(2)}, u32[]{:S(2)}) collective-permute-start(bf16[4,2,128,128]{3,2,1,0:T(8,128)(2,1)S(1)} %collective-permute-done.8.rest_2_), channel_id=1, source_target_pairs={{0,2},{1,3},{2,0},{3,1},{4,6},{5,7},{6,4},{7,5},{8,10},{9,11},{10,... | collective-permute-start | bytes 786440 | tf_op jit(solution)/shard_map/ppermute | solution.py:184

commit v15 on v13

v15 whole, which is shorter than its diff:
```python
import functools

import jax
import jax.numpy as jnp
from jax import lax
from jax.experimental import pallas as pl
from jax.experimental.pallas import tpu as pltpu
from jax.sharding import Mesh
from jax.sharding import PartitionSpec as P

SEATS = 16
SUB = 8
FLOOR = 100


def axes(core, cols):
    bits = [bit for bit in (1, 2, 4, 8) if bit != cols]
    return bits[core:] + bits[:core]


def pack_kernel(cols, p_ids, q_ids, p_ref, q_ref, own_ref, *rest):
    out_refs, strips = rest[:3], rest[3]
    blocks, per_q, extent, _ = q_ref.shape
    per_p = p_ids.shape[0]
    strip = extent // SEATS
    rows = per_q * strip
    lane = lax.broadcasted_iota(jnp.int32, (2 * SUB, extent), 1)
    ids = jnp.zeros((2 * SUB, extent), jnp.int32)
    for f in range(blocks):
        for k in range(per_p + per_q):
            value = p_ids[k, f] if k < per_p else q_ids[f, k - per_p]
            ids = jnp.where(lane == f * (per_p + per_q) + k, value, ids)
    ids = ids.astype(p_ref.dtype)
    for f in range(blocks):
        flipped = [q_ref[f, k].astype(jnp.float32).T for k in range(per_q)]
        for j in range(SEATS):
            pieces = [tile[j * strip:(j + 1) * strip] for tile in flipped]
            strips[j, f * rows:(f + 1) * rows] = jnp.concatenate(pieces, axis=0).astype(strips.dtype)
    here = lax.axis_index(("pair", "core", "col"))
    core = lax.axis_index("core")
    paths = [[()], [(0,), (0, 1), (0, 1, 2)], [(1,), (1, 2)], [(2,), (2, 0)]]
    for path, out_ref in zip(paths, (own_ref, *out_refs)):
        spots = []
        for steps in path:
            masks = [sum(axes(c, cols)[step] for step in steps) for c in range(2)]
            to = here ^ jnp.where(core == 0, masks[0], masks[1])
            spots += [to, to ^ cols]
        place = 0
        for to in spots[:-2]:
            out_ref[place:place + blocks * rows] = strips[to]
            place += blocks * rows
        for f in range(blocks):
            for k in range(per_p):
                out_ref[place:place + extent] = p_ref[f, k]
                place += extent
        out_ref[place:place + 2 * SUB] = ids
        place += 2 * SUB
        for to in (spots[-1], spots[-2]):
            out_ref[place:place + blocks * rows] = strips[to]
            place += blocks * rows


def rest_kernel(skip, in_ref, out_ref, sem):
    copy = pltpu.make_async_copy(in_ref.at[skip:], out_ref, sem)
    copy.start()
    copy.wait()


def rest_of(packet, skip):
    height, extent = packet.shape
    return pl.pallas_call(
        functools.partial(rest_kernel, skip),
        out_shape=jax.ShapeDtypeStruct((height - skip, extent), packet.dtype),
        in_specs=[pl.BlockSpec(memory_space=pl.ANY)],
        out_specs=pl.BlockSpec(memory_space=pl.ANY),
        scratch_shapes=[pltpu.SemaphoreType.DMA],
        compiler_params=pltpu.CompilerParams(vmem_limit_bytes=1 << 20),
        name="rest_of_packet",
    )(packet)


def product_kernel(sizes, tile_count, passed, first, coded, *refs):
    count = len(passed)
    packets, (out_ref, wide_ids, ids, id_sem, *sums) = refs[:count], refs[count + (not first):]
    acc_ref = sums[0] if coded else out_ref
    blocks, per_p, per_q = sizes
    strip, extent = acc_ref.shape[1:]
    rows = per_q * strip
    places = []
    for i, (before, swapped) in enumerate(passed):
        tiles = 2 * before * blocks * rows
        indices = tiles + blocks * per_p * extent
        mine = swapped * blocks * rows if before else indices + 2 * SUB + (1 - swapped) * blocks * rows
        places.append((tiles, mine))
        wide_ids[i:i + 1] = packets[i][indices:indices + 2 * SUB].astype(jnp.int32)[:1]
    id_copy = pltpu.make_async_copy(wide_ids, ids, id_sem)
    id_copy.start()
    if first:
        acc_ref[...] = jnp.zeros_like(acc_ref)
    else:
        acc_ref[...] = refs[count][...]
    id_copy.wait()
    for i, (tiles, mine) in enumerate(places):
        for f in range(blocks):
            left = packets[i][mine + f * rows:mine + (f + 1) * rows]
            base = tiles + f * per_p * extent
            right = [packets[i][base + k * extent:base + (k + 1) * extent] for k in range(per_p)]
            product = jnp.dot(
                left, jnp.concatenate(right, axis=1), preferred_element_type=jnp.float32
            )
            start = f * (per_p + per_q)
            for k in range(per_p):
                row = ids[i, start + k] * tile_count
                for l in range(per_q):
                    spot = row + ids[i, start + per_p + l]
                    acc_ref[spot] += product[l * strip:(l + 1) * strip, k * extent:(k + 1) * extent]
    if coded:
        code(acc_ref, out_ref, out_ref.shape[1] * 2 - 2)


def code(acc_ref, out_ref, tiles):
    extra = 24 // tiles
    half = 1 << (15 + extra)
    for d in range(out_ref.shape[0]):
        values = [acc_ref[d * tiles + t] for t in range(tiles)]
        left = functools.reduce(jnp.maximum, [jnp.abs(value) for value in values]) * 2.0**FLOOR
        scale = jnp.full(left.shape, 2.0 ** (FLOOR - 1) * half, jnp.float32)
        last = jnp.zeros(left.shape, jnp.int32)
        for i in reversed(range(7)):
            big = left >= 2.0 ** (1 << i)
            down = jnp.where(big, 2.0 ** -(1 << i), 1.0)
            left, scale = left * down, scale * down
            last = jnp.where(big, last + (1 << i), last)
        low = []
        for t, value in enumerate(values):
            whole = jnp.floor(value * scale + 0.5).astype(jnp.int32)
            whole = jnp.minimum(whole, half - 1) + half
            low.append(whole & 0xFFFF)
            last = last | ((whole >> 16) << (8 + extra * t))
        for j in range(tiles // 2):
            out_ref[d, j] = low[2 * j] | (low[2 * j + 1] << 16)
        out_ref[d, tiles // 2] = last


def add_products(sizes, tile_count, cols, packets, passed, acc, coded=False):
    blocks, per_p, per_q = sizes
    extent = packets[0].shape[1]
    sums = jax.ShapeDtypeStruct((tile_count * tile_count, extent // SEATS, extent), jnp.float32)
    made = sums
    if coded:
        shape = (tile_count * cols, tile_count // cols // 2 + 1) + sums.shape[1:]
        made = jax.ShapeDtypeStruct(shape, jnp.int32)
    operands = [*packets] + ([] if acc is None else [acc])
    return pl.pallas_call(
        functools.partial(product_kernel, sizes, tile_count, passed, acc is None, coded),
        out_shape=made,
        in_specs=[pl.BlockSpec(memory_space=pltpu.VMEM)] * len(operands),
        out_specs=pl.BlockSpec(memory_space=pltpu.VMEM),
        scratch_shapes=[
            pltpu.VMEM((SEATS, extent), jnp.int32),
            pltpu.SMEM((SEATS, extent), jnp.int32),
            pltpu.SemaphoreType.DMA,
        ]
        + [pltpu.VMEM(sums.shape, sums.dtype)] * coded,
        input_output_aliases={} if acc is None or coded else {len(operands) - 1: 0},
        cost_estimate=pl.CostEstimate(
            flops=2 * len(packets) * blocks * per_p * per_q * extent**3 // SEATS,
            bytes_accessed=len(packets) * (1 << 20),
            transcendentals=0,
        ),
        compiler_params=pltpu.CompilerParams(vmem_limit_bytes=24 << 20),
        name="products",
    )(*operands)


def finish_kernel(x_ref, out_ref):
    planes, seats, words, strip, extent = x_ref.shape
    tiles = 2 * (words - 1)
    extra = 24 // tiles
    half = 1 << (15 + extra)
    wholes = [None] * tiles
    for z in range(planes):
        last = x_ref[z, :, words - 1]
        scale = jnp.full(last.shape, 2.0 ** (1 - FLOOR) / half, jnp.float32)
        for i in range(7):
            scale = scale * jnp.where((last >> i) & 1 == 1, 2.0 ** (1 << i), 1.0)
        for t in range(tiles):
            whole = (x_ref[z, :, t // 2] >> (16 * (t % 2))) & 0xFFFF
            whole = whole | (((last >> (8 + extra * t)) & ((1 << extra) - 1)) << 16)
            value = (whole - half).astype(jnp.float32) * scale
            wholes[t] = value if z == 0 else wholes[t] + value
    for t in range(tiles):
        out_ref[:, t * extent:(t + 1) * extent] = wholes[t].reshape(seats * strip, extent).T


def body(p_tiles, p_cols, q_tiles, q_cols):
    blocks, per_p, extent, _ = p_tiles.shape
    per_q = q_tiles.shape[1]
    planes, cols = lax.axis_size("plane"), lax.axis_size("col")
    tile_count = planes * SEATS // cols
    strips = 2 * blocks * per_q * extent // SEATS
    whole = blocks * per_p * extent + 2 * SUB + strips
    seat = ("pair", "core", "col")

    own, *out = pl.pallas_call(
        functools.partial(pack_kernel, cols),
        out_shape=[
            jax.ShapeDtypeStruct((whole + passed * strips, extent), p_tiles.dtype)
            for passed in (0, 2, 1, 1)
        ],
        in_specs=[pl.BlockSpec(memory_space=pltpu.SMEM)] * 2
        + [pl.BlockSpec(memory_space=pltpu.VMEM)] * 2,
        scratch_shapes=[pltpu.VMEM((SEATS, strips // 2, extent), p_tiles.dtype)],
        name="pack",
    )(p_cols.T, q_cols, p_tiles, q_tiles)

    def along(values, step):
        hops = [(s, s ^ axes(s // cols % 2, cols)[step]) for s in range(SEATS)]
        return lax.ppermute(values, seat, hops)

    def across(values):
        return lax.ppermute(values, seat, [(s, s ^ cols) for s in range(SEATS)])

    def add(acc, packets, passed, coded=False):
        sizes = (blocks, per_p, per_q)
        return add_products(sizes, tile_count, cols, packets, passed, acc, coded)

    first = [along(out[step], step) for step in range(3)]
    second = [along(rest_of(first[step], strips), (step + 1) % 3) for step in range(3)]
    crossed = [across(each) for each in [own] + first]
    acc = add(
        None, [own] + first + crossed[:2], [(0, 0), (2, 0), (1, 0), (1, 0), (0, 1), (2, 1)]
    )
    second, acc = lax.optimization_barrier((second, acc))
    third = along(rest_of(second[0], strips), 2)
    acc = add(
        acc,
        second + crossed[2:] + [across(each) for each in second],
        [(1, 0), (0, 0), (0, 0), (1, 1), (1, 1), (1, 1), (0, 1), (0, 1)],
    )
    third, acc = lax.optimization_barrier((third, acc))
    beside = across(third)
    acc = add(acc, [third], [(0, 0)])
    coded = add(acc, [beside], [(0, 1)], coded=True)
    every = ("plane",) + seat
    tiles = tile_count // cols
    landed = lax.all_to_all(coded, every, split_axis=0, concat_axis=0, tiled=True)
    return pl.pallas_call(
        finish_kernel,
        out_shape=jax.ShapeDtypeStruct((extent, tiles * extent), jnp.float32),
        compiler_params=pltpu.CompilerParams(vmem_limit_bytes=16 << 20),
        name="turn",
    )(landed.reshape((planes, SEATS) + landed.shape[1:]))


def solution(mesh):
    rows, cols = mesh.devices.shape
    pairs = SEATS // (2 * cols)
    shape = (rows // (2 * pairs), pairs, 2, cols)
    every = ("plane", "pair", "core", "col")
    inner = Mesh(mesh.devices.reshape(shape), every)
    placed = (
        P(every, None, None, None),
        P(every, None),
        P(every, None, None, None),
        P(every, None),
    )
    return jax.shard_map(
        body, mesh=inner, in_specs=placed, out_specs=P(every[:3], "col"), check_vma=False
    )
```

time: 68.9 us -> 67.9 us (0.985)
  local copies, waits for them, and re-layouts: 1.66 us -> 0.01 us
  waiting for transfers between devices: 15.5 us -> 14.2 us
  Pallas kernels: 11.3 us -> 12.4 us
  blocking collectives: 22.5 us -> 23.4 us
    all_to_all x1 -> x0, waiting for transfers between devices: 8.21 us -> none  [body(): lax.all_to_all(sliced, seat, split_axis=0, concat_axis=0, tiled=True)]
    ppermute x7, waiting for transfers between devices: 6.94 us -> 13.3 us  [along(): return lax.ppermute(values, seat, hops)]
    all_to_all x1 -> x0, starting transfers between devices: 3.99 us -> none  [body(): lax.all_to_all(sliced, seat, split_axis=0, concat_axis=0, tiled=True)]
    ppermute x8, starting transfers between devices: 4.1 us -> 7.22 us  [across(): return lax.ppermute(values, seat, [(s, s ^ cols) for s in range(SEATS)])]
    unnamed x6 -> x2, local copies, waits for them, and re-layouts: 1.66 us -> 0.01 us
    pallas_call x5 -> x9, Pallas kernels: 9.99 us -> 11.2 us  [the longest x4 7.56 us: add_products(): pl.pallas_call(functools.partial(product_kernel, sizes, tile_count, passe...]
    all_to_all x1, blocking collectives: 22.5 us -> 23.4 us  [body(): lax.all_to_all(coded, every, split_axis=0, concat_axis=0, tiled=True)]
    ppermute x7, starting transfers between devices: 9.59 us -> 10.3 us  [along(): return lax.ppermute(values, seat, hops)]
  transfers between devices with their start and end apart: 16 -> 15, of which waited for: 7 -> 6; matrix products, arithmetic and copies ran while one was open for 0% -> 0% of each run, Pallas kernels for 12% -> 10%
where the time goes in v15:
time: 67.9 us; the launch traced here: 67.7 us
  blocking collectives  23.4 us (34%)
  starting transfers between devices  17.6 us (26%)
  waiting for transfers between devices  14.2 us (21%)
  Pallas kernels  12.4 us (18%)
    all_to_all x1, blocking collectives, body(): lax.all_to_all(coded, every, split_axis=0, concat_axis=0, tiled=True)  23.4 us
    ppermute x7, waiting for transfers between devices, along(): return lax.ppermute(values, seat, hops)  13.3 us
    ppermute x7, starting transfers between devices, along(): return lax.ppermute(values, seat, hops)  10.3 us
    pallas_call x4, Pallas kernels, add_products(): pl.pallas_call(functools.partial(product_kernel, sizes, tile_count, passe...  7.56 us
    ppermute x8, starting transfers between devices, across(): return lax.ppermute(values, seat, [(s, s ^ cols) for s in range(SEATS)])  7.22 us
    pallas_call x1, Pallas kernels, body(): pl.pallas_call(functools.partial(pack_kernel, cols), out_shape=[jax.Shape...  2.84 us
  transfers between devices with their start and end apart: 15, of which 6 were waited for; matrix products, arithmetic and copies ran while one was open for 0% of the time, Pallas kernels for 10%

profile of v15, /device:TPU:1, one launch (start us, length us, event | category | flops | bytes accessed | tf_op | source)
XLA Modules:
  0.0 67.7 jit_solution(16335380067386343481)
XLA Ops:
  0.0 2.8 %pack.1 = (bf16[1424,128]{1,0:T(8,128)(2,1)}, bf16[2192,128]{1,0:T(8,128)(2,1)}, bf16[1808,128]{1,0:T(8,128)(2,1)}, bf16[1808,128]{1,0:T(8,128)(2,1)}) custom-call(s32[2,4]{1,0:T(2,128)} %bitcast.3, s32[4,6]{1,0:T(4,128)} %q_ids.1, bf16[4,2,128,128]{3,2,1,0:T(8,128)(2,1)} %p_ref.1, bf16[4,6,128,128]{3,2,1,0:T(8,128)(2,1)} %q_ref.1), custom_call_target="tpu_custom_call" | custom-call | tf_op jit(solution)/shard_map/pack/pallas_call | solution.py:205
  2.8 2.0 %collective-permute-start = (bf16[2192,128]{1,0:T(8,128)(2,1)}, bf16[2192,128]{1,0:T(8,128)(2,1)S(1)}, u32[]{:S(2)}, u32[]{:S(2)}) collective-permute-start(bf16[2192,128]{1,0:T(8,128)(2,1)} %get-tuple-element.15), channel_id=1, source_target_pairs={{0,1},{1,0},{2,6},{3,7},{4,5},{5,4},{6,2},{7,3},{8,9},{9,8},{10,14... | collective-permute-start | bytes 1683464 | tf_op jit(solution)/shard_map/ppermute | solution.py:219
  4.9 1.3 %collective-permute-start.2 = (bf16[1808,128]{1,0:T(8,128)(2,1)}, bf16[1808,128]{1,0:T(8,128)(2,1)S(1)}, u32[]{:S(2)}, u32[]{:S(2)}) collective-permute-start(bf16[1808,128]{1,0:T(8,128)(2,1)} %get-tuple-element.16), channel_id=1, source_target_pairs={{0,4},{1,5},{2,10},{3,11},{4,0},{5,1},{6,14},{7,15},{8,12},{9,13},... | collective-permute-start | bytes 1388552 | tf_op jit(solution)/shard_map/ppermute | solution.py:219
  6.2 1.2 %collective-permute-start.4 = (bf16[1808,128]{1,0:T(8,128)(2,1)}, bf16[1808,128]{1,0:T(8,128)(2,1)S(1)}, u32[]{:S(2)}, u32[]{:S(2)}) collective-permute-start(bf16[1808,128]{1,0:T(8,128)(2,1)} %get-tuple-element.17), channel_id=1, source_target_pairs={{0,8},{1,9},{2,3},{3,2},{4,12},{5,13},{6,7},{7,6},{8,0},{9,1},{10,... | collective-permute-start | bytes 1388552 | tf_op jit(solution)/shard_map/ppermute | solution.py:219
  7.4 1.5 %collective-permute-start.6 = (bf16[1424,128]{1,0:T(8,128)(2,1)}, bf16[1424,128]{1,0:T(8,128)(2,1)S(1)}, u32[]{:S(2)}, u32[]{:S(2)}) collective-permute-start(bf16[1424,128]{1,0:T(8,128)(2,1)} %get-tuple-element.18.refs_0_), channel_id=1, source_target_pairs={{0,2},{1,3},{2,0},{3,1},{4,6},{5,7},{6,4},{7,5},{8,10},{9,11},{10,... | collective-permute-start | bytes 1093640 | tf_op jit(solution)/shard_map/ppermute | solution.py:222
  8.9 6.5 %collective-permute-done.in_ref.refs_1_ = bf16[2192,128]{1,0:T(8,128)(2,1)S(1)} collective-permute-done((bf16[2192,128]{1,0:T(8,128)(2,1)}, bf16[2192,128]{1,0:T(8,128)(2,1)S(1)}, u32[]{:S(2)}, u32[]{:S(2)}) %collective-permute-start) | collective-permute-done | bytes 561184 | tf_op jit(solution)/shard_map/ppermute | solution.py:219
  15.4 2.5 %collective-permute-start.7 = (bf16[2192,128]{1,0:T(8,128)(2,1)S(1)}, bf16[2192,128]{1,0:T(8,128)(2,1)S(1)}, u32[]{:S(2)}, u32[]{:S(2)}) collective-permute-start(bf16[2192,128]{1,0:T(8,128)(2,1)S(1)} %collective-permute-done.in_ref.refs_1_), channel_id=1, source_target_pairs={{0,2},{1,3},{2,0},{3,1},{4,6},{5,7},{6,4},{7,5},{8,10},{9,11},{10,... | collective-permute-start | bytes 1683464 | tf_op jit(solution)/shard_map/ppermute | solution.py:222
  17.9 0.3 rest_of_packet.4
  18.2 2.6 %collective-permute-start.1 = (bf16[1808,128]{1,0:T(8,128)(2,1)S(1)}, bf16[1808,128]{1,0:T(8,128)(2,1)S(1)}, u32[]{:S(2)}, u32[]{:S(2)}) collective-permute-start(bf16[1808,128]{1,0:T(8,128)(2,1)S(1)} %rest_of_packet.4), channel_id=1, source_target_pairs={{0,4},{1,5},{2,10},{3,11},{4,0},{5,1},{6,14},{7,15},{8,12},{9,13},... | collective-permute-start | bytes 1388552 | tf_op jit(solution)/shard_map/ppermute | solution.py:219
  20.7 0.0 collective-permute-done.2.in_ref.refs_2_
  20.8 0.2 rest_of_packet.5
  20.9 0.0 copy-start
  20.9 1.3 %collective-permute-start.3 = (bf16[1424,128]{1,0:T(8,128)(2,1)S(1)}, bf16[1424,128]{1,0:T(8,128)(2,1)S(1)}, u32[]{:S(2)}, u32[]{:S(2)}) collective-permute-start(bf16[1424,128]{1,0:T(8,128)(2,1)S(1)} %rest_of_packet.5), channel_id=1, source_target_pairs={{0,8},{1,9},{2,3},{3,2},{4,12},{5,13},{6,7},{7,6},{8,0},{9,1},{10,... | collective-permute-start | bytes 1093640 | tf_op jit(solution)/shard_map/ppermute | solution.py:219
  22.2 0.0 collective-permute-done.4.in_ref.refs_3_
  22.2 0.2 rest_of_packet.6
  22.4 0.6 collective-permute-start.5
  23.0 0.0 collective-permute-done.6.refs_4_
  23.0 0.8 %collective-permute-start.10 = (bf16[1808,128]{1,0:T(8,128)(2,1)S(1)}, bf16[1808,128]{1,0:T(8,128)(2,1)S(1)}, u32[]{:S(2)}, u32[]{:S(2)}) collective-permute-start(bf16[1808,128]{1,0:T(8,128)(2,1)S(1)} %collective-permute-done.4.in_ref.refs_3_), channel_id=1, source_target_pairs={{0,2},{1,3},{2,0},{3,1},{4,6},{5,7},{6,4},{7,5},{8,10},{9,11},{10,... | collective-permute-start | bytes 1388552 | tf_op jit(solution)/shard_map/ppermute | solution.py:222
  23.8 0.0 collective-permute-done.7.refs_5_
  23.8 0.1 collective-permute-start.9
  23.9 0.0 copy-done
  23.9 2.3 %products.4.refs_8_ = f32[256,8,128]{2,1,0:T(8,128)S(1)} custom-call(bf16[1424,128]{1,0:T(8,128)(2,1)S(1)} %copy-done, bf16[2192,128]{1,0:T(8,128)(2,1)S(1)} %collective-permute-done.in_ref.refs_1_, bf16[1808,128]{1,0:T(8,128)(2,1)S(1)} %collective-permute-done.2.in_ref.refs_2_, bf16[1808,128]{1,0:T(8,128)(2,1)S(1)} %collective-permute-done.4.in_ref.refs_3_, ...), custom_call_target="tpu_custom_call" | custom-call | flops 75497472 | bytes 6291456 | tf_op jit(solution)/shard_map/products/pallas_call | solution.py:154
  26.2 3.7 %collective-permute-done.3.refs_1_ = bf16[1424,128]{1,0:T(8,128)(2,1)S(1)} collective-permute-done((bf16[1424,128]{1,0:T(8,128)(2,1)S(1)}, bf16[1424,128]{1,0:T(8,128)(2,1)S(1)}, u32[]{:S(2)}, u32[]{:S(2)}) %collective-permute-start.3) | collective-permute-done | bytes 364576 | tf_op jit(solution)/shard_map/ppermute | solution.py:219
  29.8 1.1 %collective-permute-done.5.refs_2_ = bf16[1424,128]{1,0:T(8,128)(2,1)S(1)} collective-permute-done((bf16[1424,128]{1,0:T(8,128)(2,1)S(1)}, bf16[1424,128]{1,0:T(8,128)(2,1)S(1)}, u32[]{:S(2)}, u32[]{:S(2)}) %collective-permute-start.5) | collective-permute-done | bytes 364576 | tf_op jit(solution)/shard_map/ppermute | solution.py:219
  31.0 0.0 collective-permute-done.1.in_ref.refs_0_
  31.0 0.9 %collective-permute-start.11 = (bf16[1808,128]{1,0:T(8,128)(2,1)S(1)}, bf16[1808,128]{1,0:T(8,128)(2,1)S(1)}, u32[]{:S(2)}, u32[]{:S(2)}) collective-permute-start(bf16[1808,128]{1,0:T(8,128)(2,1)S(1)} %collective-permute-done.1.in_ref.refs_0_), channel_id=1, source_target_pairs={{0,2},{1,3},{2,0},{3,1},{4,6},{5,7},{6,4},{7,5},{8,10},{9,11},{10,... | collective-permute-start | bytes 1388552 | tf_op jit(solution)/shard_map/ppermute | solution.py:222
  31.9 0.0 collective-permute-start.12
  31.9 0.5 collective-permute-start.13
  32.4 0.2 rest_of_packet.7
  32.6 0.0 collective-permute-done.10.refs_4_
  32.6 1.3 %collective-permute-start.8 = (bf16[1424,128]{1,0:T(8,128)(2,1)S(1)}, bf16[1424,128]{1,0:T(8,128)(2,1)S(1)}, u32[]{:S(2)}, u32[]{:S(2)}) collective-permute-start(bf16[1424,128]{1,0:T(8,128)(2,1)S(1)} %rest_of_packet.7), channel_id=1, source_target_pairs={{0,8},{1,9},{2,3},{3,2},{4,12},{5,13},{6,7},{7,6},{8,0},{9,1},{10,... | collective-permute-start | bytes 1093640 | tf_op jit(solution)/shard_map/ppermute | solution.py:219
  33.9 0.0 collective-permute-done.9.refs_3_
  33.9 0.0 collective-permute-done.12.refs_6_
  33.9 0.5 collective-permute-done.13.refs_7_
  34.4 0.0 collective-permute-done.11.refs_5_
  34.4 2.7 %products.5.refs_1_ = f32[256,8,128]{2,1,0:T(8,128)S(1)} custom-call(bf16[1808,128]{1,0:T(8,128)(2,1)S(1)} %collective-permute-done.1.in_ref.refs_0_, bf16[1424,128]{1,0:T(8,128)(2,1)S(1)} %collective-permute-done.3.refs_1_, bf16[1424,128]{1,0:T(8,128)(2,1)S(1)} %collective-permute-done.5.refs_2_, ...), custom_call_target="tpu_custom_call", output_to_operand_aliasing={{}: (8, {})} | custom-call | flops 100663296 | bytes 8388608 | tf_op jit(solution)/shard_map/products/pallas_call | solution.py:154
  37.2 2.1 %collective-permute-done.8.refs_0_ = bf16[1424,128]{1,0:T(8,128)(2,1)S(1)} collective-permute-done((bf16[1424,128]{1,0:T(8,128)(2,1)S(1)}, bf16[1424,128]{1,0:T(8,128)(2,1)S(1)}, u32[]{:S(2)}, u32[]{:S(2)}) %collective-permute-start.8) | collective-permute-done | bytes 364576 | tf_op jit(solution)/shard_map/ppermute | solution.py:219
  39.3 0.9 %collective-permute-start.14 = (bf16[1424,128]{1,0:T(8,128)(2,1)S(1)}, bf16[1424,128]{1,0:T(8,128)(2,1)S(1)}, u32[]{:S(2)}, u32[]{:S(2)}) collective-permute-start(bf16[1424,128]{1,0:T(8,128)(2,1)S(1)} %collective-permute-done.8.refs_0_), channel_id=1, source_target_pairs={{0,2},{1,3},{2,0},{3,1},{4,6},{5,7},{6,4},{7,5},{8,10},{9,11},{10,... | collective-permute-start | bytes 1093640 | tf_op jit(solution)/shard_map/ppermute | solution.py:222
  40.1 0.9 %products.6.refs_1_ = f32[256,8,128]{2,1,0:T(8,128)S(1)} custom-call(bf16[1424,128]{1,0:T(8,128)(2,1)S(1)} %collective-permute-done.8.refs_0_, f32[256,8,128]{2,1,0:T(8,128)S(1)} %products.5.refs_1_), custom_call_target="tpu_custom_call", output_to_operand_aliasing={{}: (1, {})} | custom-call | flops 12582912 | bytes 1048576 | tf_op jit(solution)/shard_map/products/pallas_call | solution.py:154
  41.1 0.4 collective-permute-done.14.refs_0_
  41.4 1.6 %products.7 = s32[32,5,8,128]{3,2,1,0:T(8,128)S(1)} custom-call(bf16[1424,128]{1,0:T(8,128)(2,1)S(1)} %collective-permute-done.14.refs_0_, f32[256,8,128]{2,1,0:T(8,128)S(1)} %products.6.refs_1_), custom_call_target="tpu_custom_call" | custom-call | flops 12582912 | bytes 1048576 | tf_op jit(solution)/shard_map/products/pallas_call | solution.py:154
  43.0 23.4 %all_to_all.5 = s32[32,5,8,128]{3,2,1,0:T(8,128)S(1)} all-to-all(s32[32,5,8,128]{3,2,1,0:T(8,128)S(1)} %products.7), channel_id=1, replica_groups=mesh['plane'=2,'pair'=4,'core'=2,'col'=2] {'plane','pair','core','col'}, dimensions={0} | all-to-all | bytes 1310720 | tf_op jit(solution)/shard_map/all_to_all | solution.py:247
  66.5 1.3 %turn.1 = f32[128,1024]{1,0:T(8,128)} custom-call(s32[2,16,5,8,128]{4,3,2,1,0:T(8,128)S(1)} %bitcast.2), custom_call_target="tpu_custom_call" | custom-call | tf_op jit(solution)/shard_map/turn/pallas_call | solution.py:248
Async XLA Ops:
  2.8 12.5 %collective-permute-start = (bf16[2192,128]{1,0:T(8,128)(2,1)}, bf16[2192,128]{1,0:T(8,128)(2,1)S(1)}, u32[]{:S(2)}, u32[]{:S(2)}) collective-permute-start(bf16[2192,128]{1,0:T(8,128)(2,1)} %get-tuple-element.15), channel_id=1, source_target_pairs={{0,1},{1,0},{2,6},{3,7},{4,5},{5,4},{6,2},{7,3},{8,9},{9,8},{10,14... | collective-permute-start | bytes 1683464 | tf_op jit(solution)/shard_map/ppermute | solution.py:219
  4.9 15.9 %collective-permute-start.2 = (bf16[1808,128]{1,0:T(8,128)(2,1)}, bf16[1808,128]{1,0:T(8,128)(2,1)S(1)}, u32[]{:S(2)}, u32[]{:S(2)}) collective-permute-start(bf16[1808,128]{1,0:T(8,128)(2,1)} %get-tuple-element.16), channel_id=1, source_target_pairs={{0,4},{1,5},{2,10},{3,11},{4,0},{5,1},{6,14},{7,15},{8,12},{9,13},... | collective-permute-start | bytes 1388552 | tf_op jit(solution)/shard_map/ppermute | solution.py:219
  6.2 16.0 %collective-permute-start.4 = (bf16[1808,128]{1,0:T(8,128)(2,1)}, bf16[1808,128]{1,0:T(8,128)(2,1)S(1)}, u32[]{:S(2)}, u32[]{:S(2)}) collective-permute-start(bf16[1808,128]{1,0:T(8,128)(2,1)} %get-tuple-element.17), channel_id=1, source_target_pairs={{0,8},{1,9},{2,3},{3,2},{4,12},{5,13},{6,7},{7,6},{8,0},{9,1},{10,... | collective-permute-start | bytes 1388552 | tf_op jit(solution)/shard_map/ppermute | solution.py:219
  7.4 15.5 %collective-permute-start.6 = (bf16[1424,128]{1,0:T(8,128)(2,1)}, bf16[1424,128]{1,0:T(8,128)(2,1)S(1)}, u32[]{:S(2)}, u32[]{:S(2)}) collective-permute-start(bf16[1424,128]{1,0:T(8,128)(2,1)} %get-tuple-element.18.refs_0_), channel_id=1, source_target_pairs={{0,2},{1,3},{2,0},{3,1},{4,6},{5,7},{6,4},{7,5},{8,10},{9,11},{10,... | collective-permute-start | bytes 1093640 | tf_op jit(solution)/shard_map/ppermute | solution.py:222
  15.4 8.4 %collective-permute-start.7 = (bf16[2192,128]{1,0:T(8,128)(2,1)S(1)}, bf16[2192,128]{1,0:T(8,128)(2,1)S(1)}, u32[]{:S(2)}, u32[]{:S(2)}) collective-permute-start(bf16[2192,128]{1,0:T(8,128)(2,1)S(1)} %collective-permute-done.in_ref.refs_1_), channel_id=1, source_target_pairs={{0,2},{1,3},{2,0},{3,1},{4,6},{5,7},{6,4},{7,5},{8,10},{9,11},{10,... | collective-permute-start | bytes 1683464 | tf_op jit(solution)/shard_map/ppermute | solution.py:222
  18.2 12.8 %collective-permute-start.1 = (bf16[1808,128]{1,0:T(8,128)(2,1)S(1)}, bf16[1808,128]{1,0:T(8,128)(2,1)S(1)}, u32[]{:S(2)}, u32[]{:S(2)}) collective-permute-start(bf16[1808,128]{1,0:T(8,128)(2,1)S(1)} %rest_of_packet.4), channel_id=1, source_target_pairs={{0,4},{1,5},{2,10},{3,11},{4,0},{5,1},{6,14},{7,15},{8,12},{9,13},... | collective-permute-start | bytes 1388552 | tf_op jit(solution)/shard_map/ppermute | solution.py:219
  20.9 3.0 %copy-start = (bf16[1424,128]{1,0:T(8,128)(2,1)S(1)}, bf16[1424,128]{1,0:T(8,128)(2,1)}, u32[]{:S(2)}) copy-start(bf16[1424,128]{1,0:T(8,128)(2,1)} %get-tuple-element.18.refs_0_) | copy-start | bytes 1093636
  20.9 8.9 %collective-permute-start.3 = (bf16[1424,128]{1,0:T(8,128)(2,1)S(1)}, bf16[1424,128]{1,0:T(8,128)(2,1)S(1)}, u32[]{:S(2)}, u32[]{:S(2)}) collective-permute-start(bf16[1424,128]{1,0:T(8,128)(2,1)S(1)} %rest_of_packet.5), channel_id=1, source_target_pairs={{0,8},{1,9},{2,3},{3,2},{4,12},{5,13},{6,7},{7,6},{8,0},{9,1},{10,... | collective-permute-start | bytes 1093640 | tf_op jit(solution)/shard_map/ppermute | solution.py:219
  22.4 8.6 %collective-permute-start.5 = (bf16[1424,128]{1,0:T(8,128)(2,1)S(1)}, bf16[1424,128]{1,0:T(8,128)(2,1)S(1)}, u32[]{:S(2)}, u32[]{:S(2)}) collective-permute-start(bf16[1424,128]{1,0:T(8,128)(2,1)S(1)} %rest_of_packet.6), channel_id=1, source_target_pairs={{0,1},{1,0},{2,6},{3,7},{4,5},{5,4},{6,2},{7,3},{8,9},{9,8},{10,14... | collective-permute-start | bytes 1093640 | tf_op jit(solution)/shard_map/ppermute | solution.py:219
  23.0 9.6 %collective-permute-start.10 = (bf16[1808,128]{1,0:T(8,128)(2,1)S(1)}, bf16[1808,128]{1,0:T(8,128)(2,1)S(1)}, u32[]{:S(2)}, u32[]{:S(2)}) collective-permute-start(bf16[1808,128]{1,0:T(8,128)(2,1)S(1)} %collective-permute-done.4.in_ref.refs_3_), channel_id=1, source_target_pairs={{0,2},{1,3},{2,0},{3,1},{4,6},{5,7},{6,4},{7,5},{8,10},{9,11},{10,... | collective-permute-start | bytes 1388552 | tf_op jit(solution)/shard_map/ppermute | solution.py:222
  23.8 10.1 %collective-permute-start.9 = (bf16[1808,128]{1,0:T(8,128)(2,1)S(1)}, bf16[1808,128]{1,0:T(8,128)(2,1)S(1)}, u32[]{:S(2)}, u32[]{:S(2)}) collective-permute-start(bf16[1808,128]{1,0:T(8,128)(2,1)S(1)} %collective-permute-done.2.in_ref.refs_2_), channel_id=1, source_target_pairs={{0,2},{1,3},{2,0},{3,1},{4,6},{5,7},{6,4},{7,5},{8,10},{9,11},{10,... | collective-permute-start | bytes 1388552 | tf_op jit(solution)/shard_map/ppermute | solution.py:222
  31.0 3.4 %collective-permute-start.11 = (bf16[1808,128]{1,0:T(8,128)(2,1)S(1)}, bf16[1808,128]{1,0:T(8,128)(2,1)S(1)}, u32[]{:S(2)}, u32[]{:S(2)}) collective-permute-start(bf16[1808,128]{1,0:T(8,128)(2,1)S(1)} %collective-permute-done.1.in_ref.refs_0_), channel_id=1, source_target_pairs={{0,2},{1,3},{2,0},{3,1},{4,6},{5,7},{6,4},{7,5},{8,10},{9,11},{10,... | collective-permute-start | bytes 1388552 | tf_op jit(solution)/shard_map/ppermute | solution.py:222
  31.9 2.0 %collective-permute-start.12 = (bf16[1424,128]{1,0:T(8,128)(2,1)S(1)}, bf16[1424,128]{1,0:T(8,128)(2,1)S(1)}, u32[]{:S(2)}, u32[]{:S(2)}) collective-permute-start(bf16[1424,128]{1,0:T(8,128)(2,1)S(1)} %collective-permute-done.3.refs_1_), channel_id=1, source_target_pairs={{0,2},{1,3},{2,0},{3,1},{4,6},{5,7},{6,4},{7,5},{8,10},{9,11},{10,... | collective-permute-start | bytes 1093640 | tf_op jit(solution)/shard_map/ppermute | solution.py:222
  31.9 2.5 %collective-permute-start.13 = (bf16[1424,128]{1,0:T(8,128)(2,1)S(1)}, bf16[1424,128]{1,0:T(8,128)(2,1)S(1)}, u32[]{:S(2)}, u32[]{:S(2)}) collective-permute-start(bf16[1424,128]{1,0:T(8,128)(2,1)S(1)} %collective-permute-done.5.refs_2_), channel_id=1, source_target_pairs={{0,2},{1,3},{2,0},{3,1},{4,6},{5,7},{6,4},{7,5},{8,10},{9,11},{10,... | collective-permute-start | bytes 1093640 | tf_op jit(solution)/shard_map/ppermute | solution.py:222
  32.6 6.7 %collective-permute-start.8 = (bf16[1424,128]{1,0:T(8,128)(2,1)S(1)}, bf16[1424,128]{1,0:T(8,128)(2,1)S(1)}, u32[]{:S(2)}, u32[]{:S(2)}) collective-permute-start(bf16[1424,128]{1,0:T(8,128)(2,1)S(1)} %rest_of_packet.7), channel_id=1, source_target_pairs={{0,8},{1,9},{2,3},{3,2},{4,12},{5,13},{6,7},{7,6},{8,0},{9,1},{10,... | collective-permute-start | bytes 1093640 | tf_op jit(solution)/shard_map/ppermute | solution.py:219
  39.3 2.2 %collective-permute-start.14 = (bf16[1424,128]{1,0:T(8,128)(2,1)S(1)}, bf16[1424,128]{1,0:T(8,128)(2,1)S(1)}, u32[]{:S(2)}, u32[]{:S(2)}) collective-permute-start(bf16[1424,128]{1,0:T(8,128)(2,1)S(1)} %collective-permute-done.8.refs_0_), channel_id=1, source_target_pairs={{0,2},{1,3},{2,0},{3,1},{4,6},{5,7},{6,4},{7,5},{8,10},{9,11},{10,... | collective-permute-start | bytes 1093640 | tf_op jit(solution)/shard_map/ppermute | solution.py:222

commit v16 on v15

--- a/solution.py
+++ b/solution.py
@@ -19,7 +19,7 @@
 
 
 def pack_kernel(cols, p_ids, q_ids, p_ref, q_ref, own_ref, *rest):
-    out_refs, strips = rest[:3], rest[3]
+    out_refs, strips = rest[:4], rest[4]
     blocks, per_q, extent, _ = q_ref.shape
     per_p = p_ids.shape[0]
     strip = extent // SEATS
@@ -38,7 +38,7 @@
             strips[j, f * rows:(f + 1) * rows] = jnp.concatenate(pieces, axis=0).astype(strips.dtype)
     here = lax.axis_index(("pair", "core", "col"))
     core = lax.axis_index("core")
-    paths = [[()], [(0,), (0, 1), (0, 1, 2)], [(1,), (1, 2)], [(2,), (2, 0)]]
+    paths = [[()], [(0,), (0, 1)], [(1,), (1, 2)], [(2,), (2, 0)], [(0, 1, 2)]]
     for path, out_ref in zip(paths, (own_ref, *out_refs)):
         spots = []
         for steps in path:
@@ -206,7 +206,7 @@
         functools.partial(pack_kernel, cols),
         out_shape=[
             jax.ShapeDtypeStruct((whole + passed * strips, extent), p_tiles.dtype)
-            for passed in (0, 2, 1, 1)
+            for passed in (0, 1, 1, 1, 0)
         ],
         in_specs=[pl.BlockSpec(memory_space=pltpu.SMEM)] * 2
         + [pl.BlockSpec(memory_space=pltpu.VMEM)] * 2,
@@ -225,23 +225,21 @@
         sizes = (blocks, per_p, per_q)
         return add_products(sizes, tile_count, cols, packets, passed, acc, coded)
 
+    def opposite(values):
+        return lax.ppermute(values, seat, [(s, s ^ (SEATS - 1 - cols)) for s in range(SEATS)])
+
     first = [along(out[step], step) for step in range(3)]
+    beside = across(own)
+    far = opposite(out[3])
     second = [along(rest_of(first[step], strips), (step + 1) % 3) for step in range(3)]
-    crossed = [across(each) for each in [own] + first]
+    acc = add(None, [own, beside] + first, [(0, 0), (0, 1), (1, 0), (1, 0), (1, 0)])
+    second, acc = lax.optimization_barrier((second, acc))
+    crossed = [across(each) for each in [far] + first]
+    more = [across(each) for each in second]
     acc = add(
-        None, [own] + first + crossed[:2], [(0, 0), (2, 0), (1, 0), (1, 0), (0, 1), (2, 1)]
+        acc, [far] + second + crossed, [(0, 0)] * 4 + [(0, 1)] + [(1, 1)] * 3
     )
-    second, acc = lax.optimization_barrier((second, acc))
-    third = along(rest_of(second[0], strips), 2)
-    acc = add(
-        acc,
-        second + crossed[2:] + [across(each) for each in second],
-        [(1, 0), (0, 0), (0, 0), (1, 1), (1, 1), (1, 1), (0, 1), (0, 1)],
-    )
-    third, acc = lax.optimization_barrier((third, acc))
-    beside = across(third)
-    acc = add(acc, [third], [(0, 0)])
-    coded = add(acc, [beside], [(0, 1)], coded=True)
+    coded = add(acc, more, [(0, 1)] * 3, coded=True)
     every = ("plane",) + seat
     tiles = tile_count // cols
     landed = lax.all_to_all(coded, every, split_axis=0, concat_axis=0, tiled=True)

time: 67.9 us -> 67.1 us (0.988)
  waiting for transfers between devices: 14.2 us -> 10.5 us
  starting transfers between devices: 17.6 us -> 20.6 us
  Pallas kernels: 12.4 us -> 11.5 us
  blocking collectives: 23.4 us -> 24.2 us
    ppermute x7 -> x6, waiting for transfers between devices: 13.3 us -> 8.78 us  [along(): return lax.ppermute(values, seat, hops)]
    ppermute x8, starting transfers between devices: 7.22 us -> 11.5 us  [across(): return lax.ppermute(values, seat, [(s, s ^ cols) for s in range(SEATS)])]
    ppermute x0 -> x1, waiting for transfers between devices: none -> 1.68 us  [opposite(): lax.ppermute(values, seat, [(s, s ^ SEATS - 1 - cols) for s in range(SEAT...]
    ppermute x7 -> x6, starting transfers between devices: 10.3 us -> 9.06 us  [along(): return lax.ppermute(values, seat, hops)]
    ppermute x8, waiting for transfers between devices: 0.87 us -> 0.02 us  [across(): return lax.ppermute(values, seat, [(s, s ^ cols) for s in range(SEATS)])]
    all_to_all x1, blocking collectives: 23.4 us -> 24.2 us  [body(): lax.all_to_all(coded, every, split_axis=0, concat_axis=0, tiled=True)]
    pallas_call x4 -> x3, Pallas kernels: 7.56 us -> 6.88 us  [add_products(): pl.pallas_call(functools.partial(product_kernel, sizes, tile_count, passe...]
  transfers between devices with their start and end apart: 15 -> 15, of which waited for: 6 -> 5; matrix products, arithmetic and copies ran while one was open for 0% -> 0% of each run, Pallas kernels for 10% -> 8%
where the time goes in v16:
time: 67.1 us; the launch traced here: 66.9 us
  blocking collectives  24.2 us (36%)
  starting transfers between devices  20.6 us (31%)
  Pallas kernels  11.5 us (17%)
  waiting for transfers between devices  10.5 us (16%)
    all_to_all x1, blocking collectives, body(): lax.all_to_all(coded, every, split_axis=0, concat_axis=0, tiled=True)  24.2 us
    ppermute x8, starting transfers between devices, across(): return lax.ppermute(values, seat, [(s, s ^ cols) for s in range(SEATS)])  11.5 us
    ppermute x6, starting transfers between devices, along(): return lax.ppermute(values, seat, hops)  9.06 us
    ppermute x6, waiting for transfers between devices, along(): return lax.ppermute(values, seat, hops)  8.78 us
    pallas_call x3, Pallas kernels, add_products(): pl.pallas_call(functools.partial(product_kernel, sizes, tile_count, passe...  6.88 us
    pallas_call x1, Pallas kernels, body(): pl.pallas_call(functools.partial(pack_kernel, cols), out_shape=[jax.Shape...  2.93 us
    ppermute x1, waiting for transfers between devices, opposite(): lax.ppermute(values, seat, [(s, s ^ SEATS - 1 - cols) for s in range(SEAT...  1.68 us
  transfers between devices with their start and end apart: 15, of which 5 were waited for; matrix products, arithmetic and copies ran while one was open for 0% of the time, Pallas kernels for 8%

profile of v16, /device:TPU:1, one launch (start us, length us, event | category | flops | bytes accessed | tf_op | source)
XLA Modules:
  0.0 66.9 jit_solution(11641019337262078927)
XLA Ops:
  0.0 2.9 %pack.1 = (bf16[1424,128]{1,0:T(8,128)(2,1)}, bf16[1808,128]{1,0:T(8,128)(2,1)}, bf16[1808,128]{1,0:T(8,128)(2,1)}, bf16[1808,128]{1,0:T(8,128)(2,1)}, bf16[1424,128]{1,0:T(8,128)(2,1)}) custom-call(s32[2,4]{1,0:T(2,128)} %bitcast.3, s32[4,6]{1,0:T(4,128)} %q_ids.1, bf16[4,2,128,128]{3,2,1,0:T(8,128)(2,1)} %p_ref.1, bf16[4,6,128,128]{3,2,1,0:T(8,128)(2,1)} %q_ref.1), custom_call_target="tpu_custom_call" | custom-call | tf_op jit(solution)/shard_map/pack/pallas_call | solution.py:205
  2.9 2.0 %collective-permute-start = (bf16[1808,128]{1,0:T(8,128)(2,1)}, bf16[1808,128]{1,0:T(8,128)(2,1)S(1)}, u32[]{:S(2)}, u32[]{:S(2)}) collective-permute-start(bf16[1808,128]{1,0:T(8,128)(2,1)} %get-tuple-element.14), channel_id=1, source_target_pairs={{0,1},{1,0},{2,6},{3,7},{4,5},{5,4},{6,2},{7,3},{8,9},{9,8},{10,14... | collective-permute-start | bytes 1388552 | tf_op jit(solution)/shard_map/ppermute | solution.py:219
  5.0 1.3 %collective-permute-start.2 = (bf16[1808,128]{1,0:T(8,128)(2,1)}, bf16[1808,128]{1,0:T(8,128)(2,1)S(1)}, u32[]{:S(2)}, u32[]{:S(2)}) collective-permute-start(bf16[1808,128]{1,0:T(8,128)(2,1)} %get-tuple-element.15), channel_id=1, source_target_pairs={{0,4},{1,5},{2,10},{3,11},{4,0},{5,1},{6,14},{7,15},{8,12},{9,13},... | collective-permute-start | bytes 1388552 | tf_op jit(solution)/shard_map/ppermute | solution.py:219
  6.3 1.2 %collective-permute-start.4 = (bf16[1808,128]{1,0:T(8,128)(2,1)}, bf16[1808,128]{1,0:T(8,128)(2,1)S(1)}, u32[]{:S(2)}, u32[]{:S(2)}) collective-permute-start(bf16[1808,128]{1,0:T(8,128)(2,1)} %get-tuple-element.16), channel_id=1, source_target_pairs={{0,8},{1,9},{2,3},{3,2},{4,12},{5,13},{6,7},{7,6},{8,0},{9,1},{10,... | collective-permute-start | bytes 1388552 | tf_op jit(solution)/shard_map/ppermute | solution.py:219
  7.5 1.5 %collective-permute-start.6 = (bf16[1424,128]{1,0:T(8,128)(2,1)}, bf16[1424,128]{1,0:T(8,128)(2,1)S(1)}, u32[]{:S(2)}, u32[]{:S(2)}) collective-permute-start(bf16[1424,128]{1,0:T(8,128)(2,1)} %get-tuple-element.17.refs_0_), channel_id=1, source_target_pairs={{0,2},{1,3},{2,0},{3,1},{4,6},{5,7},{6,4},{7,5},{8,10},{9,11},{10,... | collective-permute-start | bytes 1093640 | tf_op jit(solution)/shard_map/ppermute | solution.py:222
  9.0 0.0 collective-permute-start.10
  9.0 4.3 %collective-permute-done.in_ref.refs_2_ = bf16[1808,128]{1,0:T(8,128)(2,1)S(1)} collective-permute-done((bf16[1808,128]{1,0:T(8,128)(2,1)}, bf16[1808,128]{1,0:T(8,128)(2,1)S(1)}, u32[]{:S(2)}, u32[]{:S(2)}) %collective-permute-start) | collective-permute-done | bytes 462880 | tf_op jit(solution)/shard_map/ppermute | solution.py:219
  13.4 0.2 rest_of_packet.3
  13.5 1.9 %collective-permute-start.1 = (bf16[1424,128]{1,0:T(8,128)(2,1)S(1)}, bf16[1424,128]{1,0:T(8,128)(2,1)S(1)}, u32[]{:S(2)}, u32[]{:S(2)}) collective-permute-start(bf16[1424,128]{1,0:T(8,128)(2,1)S(1)} %rest_of_packet.3), channel_id=1, source_target_pairs={{0,4},{1,5},{2,10},{3,11},{4,0},{5,1},{6,14},{7,15},{8,12},{9,13},... | collective-permute-start | bytes 1093640 | tf_op jit(solution)/shard_map/ppermute | solution.py:219
  15.4 0.0 collective-permute-done.2.in_ref.refs_3_
  15.4 0.2 rest_of_packet.4
  15.6 0.0 copy-start
  15.6 2.3 %collective-permute-start.3 = (bf16[1424,128]{1,0:T(8,128)(2,1)S(1)}, bf16[1424,128]{1,0:T(8,128)(2,1)S(1)}, u32[]{:S(2)}, u32[]{:S(2)}) collective-permute-start(bf16[1424,128]{1,0:T(8,128)(2,1)S(1)} %rest_of_packet.4), channel_id=1, source_target_pairs={{0,8},{1,9},{2,3},{3,2},{4,12},{5,13},{6,7},{7,6},{8,0},{9,1},{10,... | collective-permute-start | bytes 1093640 | tf_op jit(solution)/shard_map/ppermute | solution.py:219
  17.9 2.2 %collective-permute-done.4.in_ref.refs_4_ = bf16[1808,128]{1,0:T(8,128)(2,1)S(1)} collective-permute-done((bf16[1808,128]{1,0:T(8,128)(2,1)}, bf16[1808,128]{1,0:T(8,128)(2,1)S(1)}, u32[]{:S(2)}, u32[]{:S(2)}) %collective-permute-start.4) | collective-permute-done | bytes 462880 | tf_op jit(solution)/shard_map/ppermute | solution.py:219
  20.1 2.8 %collective-permute-start.12 = (bf16[1808,128]{1,0:T(8,128)(2,1)S(1)}, bf16[1808,128]{1,0:T(8,128)(2,1)S(1)}, u32[]{:S(2)}, u32[]{:S(2)}) collective-permute-start(bf16[1808,128]{1,0:T(8,128)(2,1)S(1)} %collective-permute-done.in_ref.refs_2_), channel_id=1, source_target_pairs={{0,2},{1,3},{2,0},{3,1},{4,6},{5,7},{6,4},{7,5},{8,10},{9,11},{10,... | collective-permute-start | bytes 1388552 | tf_op jit(solution)/shard_map/ppermute | solution.py:222
  22.8 0.2 rest_of_packet.5
  23.0 0.0 collective-permute-done.6.refs_1_
  23.0 0.3 collective-permute-start.5
  23.3 1.7 %collective-permute-done.10.refs_0_ = bf16[1424,128]{1,0:T(8,128)(2,1)S(1)} collective-permute-done((bf16[1424,128]{1,0:T(8,128)(2,1)}, bf16[1424,128]{1,0:T(8,128)(2,1)S(1)}, u32[]{:S(2)}, u32[]{:S(2)}) %collective-permute-start.10) | collective-permute-done | bytes 364576 | tf_op jit(solution)/shard_map/ppermute | solution.py:229
  25.0 3.5 %collective-permute-start.11 = (bf16[1424,128]{1,0:T(8,128)(2,1)S(1)}, bf16[1424,128]{1,0:T(8,128)(2,1)S(1)}, u32[]{:S(2)}, u32[]{:S(2)}) collective-permute-start(bf16[1424,128]{1,0:T(8,128)(2,1)S(1)} %collective-permute-done.10.refs_0_), channel_id=1, source_target_pairs={{0,2},{1,3},{2,0},{3,1},{4,6},{5,7},{6,4},{7,5},{8,10},{9,11},{10,... | collective-permute-start | bytes 1093640 | tf_op jit(solution)/shard_map/ppermute | solution.py:222
  28.5 1.9 %collective-permute-done.1.refs_1_ = bf16[1424,128]{1,0:T(8,128)(2,1)S(1)} collective-permute-done((bf16[1424,128]{1,0:T(8,128)(2,1)S(1)}, bf16[1424,128]{1,0:T(8,128)(2,1)S(1)}, u32[]{:S(2)}, u32[]{:S(2)}) %collective-permute-start.1) | collective-permute-done | bytes 364576 | tf_op jit(solution)/shard_map/ppermute | solution.py:219
  30.4 1.4 %collective-permute-start.13 = (bf16[1808,128]{1,0:T(8,128)(2,1)S(1)}, bf16[1808,128]{1,0:T(8,128)(2,1)S(1)}, u32[]{:S(2)}, u32[]{:S(2)}) collective-permute-start(bf16[1808,128]{1,0:T(8,128)(2,1)S(1)} %collective-permute-done.2.in_ref.refs_3_), channel_id=1, source_target_pairs={{0,2},{1,3},{2,0},{3,1},{4,6},{5,7},{6,4},{7,5},{8,10},{9,11},{10,... | collective-permute-start | bytes 1388552 | tf_op jit(solution)/shard_map/ppermute | solution.py:222
  31.8 0.3 collective-permute-done.3.refs_2_
  32.1 1.7 %collective-permute-start.14 = (bf16[1808,128]{1,0:T(8,128)(2,1)S(1)}, bf16[1808,128]{1,0:T(8,128)(2,1)S(1)}, u32[]{:S(2)}, u32[]{:S(2)}) collective-permute-start(bf16[1808,128]{1,0:T(8,128)(2,1)S(1)} %collective-permute-done.4.in_ref.refs_4_), channel_id=1, source_target_pairs={{0,2},{1,3},{2,0},{3,1},{4,6},{5,7},{6,4},{7,5},{8,10},{9,11},{10,... | collective-permute-start | bytes 1388552 | tf_op jit(solution)/shard_map/ppermute | solution.py:222
  33.8 0.0 copy-done
  33.8 2.0 %products.3.refs_8_ = f32[256,8,128]{2,1,0:T(8,128)S(1)} custom-call(bf16[1424,128]{1,0:T(8,128)(2,1)S(1)} %copy-done, bf16[1424,128]{1,0:T(8,128)(2,1)S(1)} %collective-permute-done.6.refs_1_, bf16[1808,128]{1,0:T(8,128)(2,1)S(1)} %collective-permute-done.in_ref.refs_2_, bf16[1808,128]{1,0:T(8,128)(2,1)S(1)} %collective-permute-done.2.in_ref.refs_3_, ...), custom_call_target="tpu_custom_call" | custom-call | flops 62914560 | bytes 5242880 | tf_op jit(solution)/shard_map/products/pallas_call | solution.py:154
  35.9 0.0 collective-permute-done.5.refs_3_
  35.9 0.1 collective-permute-start.7
  36.0 0.0 collective-permute-done.11.refs_4_
  36.0 0.5 collective-permute-start.8
  36.5 0.0 collective-permute-done.12.refs_5_
  36.5 0.1 collective-permute-start.9
  36.6 0.0 collective-permute-done.13.refs_6_
  36.6 0.0 collective-permute-done.14.refs_7_
  36.6 2.7 %products.4.refs_3_ = f32[256,8,128]{2,1,0:T(8,128)S(1)} custom-call(bf16[1424,128]{1,0:T(8,128)(2,1)S(1)} %collective-permute-done.10.refs_0_, bf16[1424,128]{1,0:T(8,128)(2,1)S(1)} %collective-permute-done.1.refs_1_, bf16[1424,128]{1,0:T(8,128)(2,1)S(1)} %collective-permute-done.3.refs_2_, ...), custom_call_target="tpu_custom_call", output_to_operand_aliasing={{}: (8, {})} | custom-call | flops 100663296 | bytes 8388608 | tf_op jit(solution)/shard_map/products/pallas_call | solution.py:154
  39.3 0.0 collective-permute-done.7.refs_0_
  39.3 0.0 collective-permute-done.8.refs_1_
  39.3 0.0 collective-permute-done.9.refs_2_
  39.3 2.1 %products.5 = s32[32,5,8,128]{3,2,1,0:T(8,128)S(1)} custom-call(bf16[1424,128]{1,0:T(8,128)(2,1)S(1)} %collective-permute-done.7.refs_0_, bf16[1424,128]{1,0:T(8,128)(2,1)S(1)} %collective-permute-done.8.refs_1_, bf16[1424,128]{1,0:T(8,128)(2,1)S(1)} %collective-permute-done.9.refs_2_, f32[256,8,128]{2,1,0:T(8,128)S(1)} %products.4.refs_3_), custom_call_target="tpu_custom_call" | custom-call | flops 37748736 | bytes 3145728 | tf_op jit(solution)/shard_map/products/pallas_call | solution.py:154
  41.5 24.2 %all_to_all.5 = s32[32,5,8,128]{3,2,1,0:T(8,128)S(1)} all-to-all(s32[32,5,8,128]{3,2,1,0:T(8,128)S(1)} %products.5), channel_id=1, replica_groups=mesh['plane'=2,'pair'=4,'core'=2,'col'=2] {'plane','pair','core','col'}, dimensions={0} | all-to-all | bytes 1310720 | tf_op jit(solution)/shard_map/all_to_all | solution.py:245
  65.6 1.3 %turn.1 = f32[128,1024]{1,0:T(8,128)} custom-call(s32[2,16,5,8,128]{4,3,2,1,0:T(8,128)S(1)} %bitcast.2), custom_call_target="tpu_custom_call" | custom-call | tf_op jit(solution)/shard_map/turn/pallas_call | solution.py:246
Async XLA Ops:
  2.9 10.4 %collective-permute-start = (bf16[1808,128]{1,0:T(8,128)(2,1)}, bf16[1808,128]{1,0:T(8,128)(2,1)S(1)}, u32[]{:S(2)}, u32[]{:S(2)}) collective-permute-start(bf16[1808,128]{1,0:T(8,128)(2,1)} %get-tuple-element.14), channel_id=1, source_target_pairs={{0,1},{1,0},{2,6},{3,7},{4,5},{5,4},{6,2},{7,3},{8,9},{9,8},{10,14... | collective-permute-start | bytes 1388552 | tf_op jit(solution)/shard_map/ppermute | solution.py:219
  5.0 10.4 %collective-permute-start.2 = (bf16[1808,128]{1,0:T(8,128)(2,1)}, bf16[1808,128]{1,0:T(8,128)(2,1)S(1)}, u32[]{:S(2)}, u32[]{:S(2)}) collective-permute-start(bf16[1808,128]{1,0:T(8,128)(2,1)} %get-tuple-element.15), channel_id=1, source_target_pairs={{0,4},{1,5},{2,10},{3,11},{4,0},{5,1},{6,14},{7,15},{8,12},{9,13},... | collective-permute-start | bytes 1388552 | tf_op jit(solution)/shard_map/ppermute | solution.py:219
  6.3 13.8 %collective-permute-start.4 = (bf16[1808,128]{1,0:T(8,128)(2,1)}, bf16[1808,128]{1,0:T(8,128)(2,1)S(1)}, u32[]{:S(2)}, u32[]{:S(2)}) collective-permute-start(bf16[1808,128]{1,0:T(8,128)(2,1)} %get-tuple-element.16), channel_id=1, source_target_pairs={{0,8},{1,9},{2,3},{3,2},{4,12},{5,13},{6,7},{7,6},{8,0},{9,1},{10,... | collective-permute-start | bytes 1388552 | tf_op jit(solution)/shard_map/ppermute | solution.py:219
  7.5 15.5 %collective-permute-start.6 = (bf16[1424,128]{1,0:T(8,128)(2,1)}, bf16[1424,128]{1,0:T(8,128)(2,1)S(1)}, u32[]{:S(2)}, u32[]{:S(2)}) collective-permute-start(bf16[1424,128]{1,0:T(8,128)(2,1)} %get-tuple-element.17.refs_0_), channel_id=1, source_target_pairs={{0,2},{1,3},{2,0},{3,1},{4,6},{5,7},{6,4},{7,5},{8,10},{9,11},{10,... | collective-permute-start | bytes 1093640 | tf_op jit(solution)/shard_map/ppermute | solution.py:222
  9.0 16.0 %collective-permute-start.10 = (bf16[1424,128]{1,0:T(8,128)(2,1)}, bf16[1424,128]{1,0:T(8,128)(2,1)S(1)}, u32[]{:S(2)}, u32[]{:S(2)}) collective-permute-start(bf16[1424,128]{1,0:T(8,128)(2,1)} %get-tuple-element.21), channel_id=1, source_target_pairs={{0,13},{1,12},{2,15},{3,14},{4,9},{5,8},{6,11},{7,10},{8,5},{9,4},... | collective-permute-start | bytes 1093640 | tf_op jit(solution)/shard_map/ppermute | solution.py:229
  13.5 16.9 %collective-permute-start.1 = (bf16[1424,128]{1,0:T(8,128)(2,1)S(1)}, bf16[1424,128]{1,0:T(8,128)(2,1)S(1)}, u32[]{:S(2)}, u32[]{:S(2)}) collective-permute-start(bf16[1424,128]{1,0:T(8,128)(2,1)S(1)} %rest_of_packet.3), channel_id=1, source_target_pairs={{0,4},{1,5},{2,10},{3,11},{4,0},{5,1},{6,14},{7,15},{8,12},{9,13},... | collective-permute-start | bytes 1093640 | tf_op jit(solution)/shard_map/ppermute | solution.py:219
  15.6 18.3 %copy-start = (bf16[1424,128]{1,0:T(8,128)(2,1)S(1)}, bf16[1424,128]{1,0:T(8,128)(2,1)}, u32[]{:S(2)}) copy-start(bf16[1424,128]{1,0:T(8,128)(2,1)} %get-tuple-element.17.refs_0_) | copy-start | bytes 1093636
  15.6 16.5 %collective-permute-start.3 = (bf16[1424,128]{1,0:T(8,128)(2,1)S(1)}, bf16[1424,128]{1,0:T(8,128)(2,1)S(1)}, u32[]{:S(2)}, u32[]{:S(2)}) collective-permute-start(bf16[1424,128]{1,0:T(8,128)(2,1)S(1)} %rest_of_packet.4), channel_id=1, source_target_pairs={{0,8},{1,9},{2,3},{3,2},{4,12},{5,13},{6,7},{7,6},{8,0},{9,1},{10,... | collective-permute-start | bytes 1093640 | tf_op jit(solution)/shard_map/ppermute | solution.py:219
  20.1 16.4 %collective-permute-start.12 = (bf16[1808,128]{1,0:T(8,128)(2,1)S(1)}, bf16[1808,128]{1,0:T(8,128)(2,1)S(1)}, u32[]{:S(2)}, u32[]{:S(2)}) collective-permute-start(bf16[1808,128]{1,0:T(8,128)(2,1)S(1)} %collective-permute-done.in_ref.refs_2_), channel_id=1, source_target_pairs={{0,2},{1,3},{2,0},{3,1},{4,6},{5,7},{6,4},{7,5},{8,10},{9,11},{10,... | collective-permute-start | bytes 1388552 | tf_op jit(solution)/shard_map/ppermute | solution.py:222
  23.0 12.9 %collective-permute-start.5 = (bf16[1424,128]{1,0:T(8,128)(2,1)S(1)}, bf16[1424,128]{1,0:T(8,128)(2,1)S(1)}, u32[]{:S(2)}, u32[]{:S(2)}) collective-permute-start(bf16[1424,128]{1,0:T(8,128)(2,1)S(1)} %rest_of_packet.5), channel_id=1, source_target_pairs={{0,1},{1,0},{2,6},{3,7},{4,5},{5,4},{6,2},{7,3},{8,9},{9,8},{10,14... | collective-permute-start | bytes 1093640 | tf_op jit(solution)/shard_map/ppermute | solution.py:219
  25.0 11.0 %collective-permute-start.11 = (bf16[1424,128]{1,0:T(8,128)(2,1)S(1)}, bf16[1424,128]{1,0:T(8,128)(2,1)S(1)}, u32[]{:S(2)}, u32[]{:S(2)}) collective-permute-start(bf16[1424,128]{1,0:T(8,128)(2,1)S(1)} %collective-permute-done.10.refs_0_), channel_id=1, source_target_pairs={{0,2},{1,3},{2,0},{3,1},{4,6},{5,7},{6,4},{7,5},{8,10},{9,11},{10,... | collective-permute-start | bytes 1093640 | tf_op jit(solution)/shard_map/ppermute | solution.py:222
  30.4 6.1 %collective-permute-start.13 = (bf16[1808,128]{1,0:T(8,128)(2,1)S(1)}, bf16[1808,128]{1,0:T(8,128)(2,1)S(1)}, u32[]{:S(2)}, u32[]{:S(2)}) collective-permute-start(bf16[1808,128]{1,0:T(8,128)(2,1)S(1)} %collective-permute-done.2.in_ref.refs_3_), channel_id=1, source_target_pairs={{0,2},{1,3},{2,0},{3,1},{4,6},{5,7},{6,4},{7,5},{8,10},{9,11},{10,... | collective-permute-start | bytes 1388552 | tf_op jit(solution)/shard_map/ppermute | solution.py:222
  32.1 4.5 %collective-permute-start.14 = (bf16[1808,128]{1,0:T(8,128)(2,1)S(1)}, bf16[1808,128]{1,0:T(8,128)(2,1)S(1)}, u32[]{:S(2)}, u32[]{:S(2)}) collective-permute-start(bf16[1808,128]{1,0:T(8,128)(2,1)S(1)} %collective-permute-done.4.in_ref.refs_4_), channel_id=1, source_target_pairs={{0,2},{1,3},{2,0},{3,1},{4,6},{5,7},{6,4},{7,5},{8,10},{9,11},{10,... | collective-permute-start | bytes 1388552 | tf_op jit(solution)/shard_map/ppermute | solution.py:222
  35.9 3.4 %collective-permute-start.7 = (bf16[1424,128]{1,0:T(8,128)(2,1)S(1)}, bf16[1424,128]{1,0:T(8,128)(2,1)S(1)}, u32[]{:S(2)}, u32[]{:S(2)}) collective-permute-start(bf16[1424,128]{1,0:T(8,128)(2,1)S(1)} %collective-permute-done.1.refs_1_), channel_id=1, source_target_pairs={{0,2},{1,3},{2,0},{3,1},{4,6},{5,7},{6,4},{7,5},{8,10},{9,11},{10,... | collective-permute-start | bytes 1093640 | tf_op jit(solution)/shard_map/ppermute | solution.py:222
  36.0 3.4 %collective-permute-start.8 = (bf16[1424,128]{1,0:T(8,128)(2,1)S(1)}, bf16[1424,128]{1,0:T(8,128)(2,1)S(1)}, u32[]{:S(2)}, u32[]{:S(2)}) collective-permute-start(bf16[1424,128]{1,0:T(8,128)(2,1)S(1)} %collective-permute-done.3.refs_2_), channel_id=1, source_target_pairs={{0,2},{1,3},{2,0},{3,1},{4,6},{5,7},{6,4},{7,5},{8,10},{9,11},{10,... | collective-permute-start | bytes 1093640 | tf_op jit(solution)/shard_map/ppermute | solution.py:222
  36.5 2.9 %collective-permute-start.9 = (bf16[1424,128]{1,0:T(8,128)(2,1)S(1)}, bf16[1424,128]{1,0:T(8,128)(2,1)S(1)}, u32[]{:S(2)}, u32[]{:S(2)}) collective-permute-start(bf16[1424,128]{1,0:T(8,128)(2,1)S(1)} %collective-permute-done.5.refs_3_), channel_id=1, source_target_pairs={{0,2},{1,3},{2,0},{3,1},{4,6},{5,7},{6,4},{7,5},{8,10},{9,11},{10,... | collective-permute-start | bytes 1093640 | tf_op jit(solution)/shard_map/ppermute | solution.py:222

commit v17 on v16

--- a/solution.py
+++ b/solution.py
@@ -233,13 +233,14 @@
     far = opposite(out[3])
     second = [along(rest_of(first[step], strips), (step + 1) % 3) for step in range(3)]
     acc = add(None, [own, beside] + first, [(0, 0), (0, 1), (1, 0), (1, 0), (1, 0)])
-    second, acc = lax.optimization_barrier((second, acc))
-    crossed = [across(each) for each in [far] + first]
-    more = [across(each) for each in second]
+    first[2], second, acc = lax.optimization_barrier((first[2], second, acc))
     acc = add(
-        acc, [far] + second + crossed, [(0, 0)] * 4 + [(0, 1)] + [(1, 1)] * 3
+        acc,
+        [far, across(far), across(first[0])] + second,
+        [(0, 0), (0, 1), (1, 1), (0, 0), (0, 0), (0, 0)],
     )
-    coded = add(acc, more, [(0, 1)] * 3, coded=True)
+    crossed = [across(each) for each in first[1:] + second]
+    coded = add(acc, crossed, [(1, 1), (1, 1), (0, 1), (0, 1), (0, 1)], coded=True)
     every = ("plane",) + seat
     tiles = tile_count // cols
     landed = lax.all_to_all(coded, every, split_axis=0, concat_axis=0, tiled=True)

time: 67.1 us -> 65.7 us (0.979)
  waiting for transfers between devices: 10.5 us -> 6.71 us
  starting transfers between devices: 20.6 us -> 22.7 us
    ppermute x6, waiting for transfers between devices: 8.78 us -> 6.54 us  [along(): return lax.ppermute(values, seat, hops)]
    ppermute x1, waiting for transfers between devices: 1.68 us -> 0.01 us  [opposite(): lax.ppermute(values, seat, [(s, s ^ SEATS - 1 - cols) for s in range(SEAT...]
    ppermute x8, starting transfers between devices: 11.5 us -> 13 us  [across(): return lax.ppermute(values, seat, [(s, s ^ cols) for s in range(SEATS)])]
  transfers between devices with their start and end apart: 15 -> 15, of which waited for: 5 -> 3; matrix products, arithmetic and copies ran while one was open for 0% -> 0% of each run, Pallas kernels for 8% -> 7%
where the time goes in v17:
time: 65.7 us; the launch traced here: 65.5 us
  blocking collectives  24.5 us (37%)
  starting transfers between devices  22.7 us (35%)
  Pallas kernels  11.5 us (18%)
  waiting for transfers between devices  6.71 us (10%)
    all_to_all x1, blocking collectives, body(): lax.all_to_all(coded, every, split_axis=0, concat_axis=0, tiled=True)  24.5 us
    ppermute x8, starting transfers between devices, across(): return lax.ppermute(values, seat, [(s, s ^ cols) for s in range(SEATS)])  13 us
    ppermute x6, starting transfers between devices, along(): return lax.ppermute(values, seat, hops)  9.7 us
    pallas_call x3, Pallas kernels, add_products(): pl.pallas_call(functools.partial(product_kernel, sizes, tile_count, passe...  6.88 us
    ppermute x6, waiting for transfers between devices, along(): return lax.ppermute(values, seat, hops)  6.54 us
    pallas_call x1, Pallas kernels, body(): pl.pallas_call(functools.partial(pack_kernel, cols), out_shape=[jax.Shape...  2.93 us
  transfers between devices with their start and end apart: 15, of which 3 were waited for; matrix products, arithmetic and copies ran while one was open for 0% of the time, Pallas kernels for 7%

profile of v17, /device:TPU:1, one launch (start us, length us, event | category | flops | bytes accessed | tf_op | source)
XLA Modules:
  0.0 65.5 jit_solution(2537166063225925066)
XLA Ops:
  0.0 2.9 %pack.1 = (bf16[1424,128]{1,0:T(8,128)(2,1)}, bf16[1808,128]{1,0:T(8,128)(2,1)}, bf16[1808,128]{1,0:T(8,128)(2,1)}, bf16[1808,128]{1,0:T(8,128)(2,1)}, bf16[1424,128]{1,0:T(8,128)(2,1)}) custom-call(s32[2,4]{1,0:T(2,128)} %bitcast.3, s32[4,6]{1,0:T(4,128)} %q_ids.1, bf16[4,2,128,128]{3,2,1,0:T(8,128)(2,1)} %p_ref.1, bf16[4,6,128,128]{3,2,1,0:T(8,128)(2,1)} %q_ref.1), custom_call_target="tpu_custom_call" | custom-call | tf_op jit(solution)/shard_map/pack/pallas_call | solution.py:205
  2.9 2.0 %collective-permute-start.3 = (bf16[1808,128]{1,0:T(8,128)(2,1)}, bf16[1808,128]{1,0:T(8,128)(2,1)S(1)}, u32[]{:S(2)}, u32[]{:S(2)}) collective-permute-start(bf16[1808,128]{1,0:T(8,128)(2,1)} %get-tuple-element.17), channel_id=1, source_target_pairs={{0,1},{1,0},{2,6},{3,7},{4,5},{5,4},{6,2},{7,3},{8,9},{9,8},{10,14... | collective-permute-start | bytes 1388552 | tf_op jit(solution)/shard_map/ppermute | solution.py:219
  5.0 1.3 %collective-permute-start = (bf16[1808,128]{1,0:T(8,128)(2,1)}, bf16[1808,128]{1,0:T(8,128)(2,1)S(1)}, u32[]{:S(2)}, u32[]{:S(2)}) collective-permute-start(bf16[1808,128]{1,0:T(8,128)(2,1)} %get-tuple-element.15), channel_id=1, source_target_pairs={{0,4},{1,5},{2,10},{3,11},{4,0},{5,1},{6,14},{7,15},{8,12},{9,13},... | collective-permute-start | bytes 1388552 | tf_op jit(solution)/shard_map/ppermute | solution.py:219
  6.3 1.2 %collective-permute-start.2 = (bf16[1808,128]{1,0:T(8,128)(2,1)}, bf16[1808,128]{1,0:T(8,128)(2,1)S(1)}, u32[]{:S(2)}, u32[]{:S(2)}) collective-permute-start(bf16[1808,128]{1,0:T(8,128)(2,1)} %get-tuple-element.16), channel_id=1, source_target_pairs={{0,8},{1,9},{2,3},{3,2},{4,12},{5,13},{6,7},{7,6},{8,0},{9,1},{10,... | collective-permute-start | bytes 1388552 | tf_op jit(solution)/shard_map/ppermute | solution.py:219
  7.5 1.5 %collective-permute-start.7 = (bf16[1424,128]{1,0:T(8,128)(2,1)}, bf16[1424,128]{1,0:T(8,128)(2,1)S(1)}, u32[]{:S(2)}, u32[]{:S(2)}) collective-permute-start(bf16[1424,128]{1,0:T(8,128)(2,1)} %get-tuple-element.18.refs_0_), channel_id=1, source_target_pairs={{0,2},{1,3},{2,0},{3,1},{4,6},{5,7},{6,4},{7,5},{8,10},{9,11},{10,... | collective-permute-start | bytes 1093640 | tf_op jit(solution)/shard_map/ppermute | solution.py:222
  9.0 0.0 collective-permute-start.12
  9.0 4.3 %collective-permute-done.3.in_ref.refs_2_ = bf16[1808,128]{1,0:T(8,128)(2,1)S(1)} collective-permute-done((bf16[1808,128]{1,0:T(8,128)(2,1)}, bf16[1808,128]{1,0:T(8,128)(2,1)S(1)}, u32[]{:S(2)}, u32[]{:S(2)}) %collective-permute-start.3) | collective-permute-done | bytes 462880 | tf_op jit(solution)/shard_map/ppermute | solution.py:219
  13.4 0.2 rest_of_packet.3
  13.5 1.9 %collective-permute-start.4 = (bf16[1424,128]{1,0:T(8,128)(2,1)S(1)}, bf16[1424,128]{1,0:T(8,128)(2,1)S(1)}, u32[]{:S(2)}, u32[]{:S(2)}) collective-permute-start(bf16[1424,128]{1,0:T(8,128)(2,1)S(1)} %rest_of_packet.3), channel_id=1, source_target_pairs={{0,4},{1,5},{2,10},{3,11},{4,0},{5,1},{6,14},{7,15},{8,12},{9,13},... | collective-permute-start | bytes 1093640 | tf_op jit(solution)/shard_map/ppermute | solution.py:219
  15.4 0.0 collective-permute-done.in_ref.refs_3_
  15.4 0.2 rest_of_packet.4
  15.6 0.0 copy-start
  15.6 2.3 %collective-permute-start.5 = (bf16[1424,128]{1,0:T(8,128)(2,1)S(1)}, bf16[1424,128]{1,0:T(8,128)(2,1)S(1)}, u32[]{:S(2)}, u32[]{:S(2)}) collective-permute-start(bf16[1424,128]{1,0:T(8,128)(2,1)S(1)} %rest_of_packet.4), channel_id=1, source_target_pairs={{0,8},{1,9},{2,3},{3,2},{4,12},{5,13},{6,7},{7,6},{8,0},{9,1},{10,... | collective-permute-start | bytes 1093640 | tf_op jit(solution)/shard_map/ppermute | solution.py:219
  17.9 2.2 %collective-permute-done.2.in_ref.refs_4_ = bf16[1808,128]{1,0:T(8,128)(2,1)S(1)} collective-permute-done((bf16[1808,128]{1,0:T(8,128)(2,1)}, bf16[1808,128]{1,0:T(8,128)(2,1)S(1)}, u32[]{:S(2)}, u32[]{:S(2)}) %collective-permute-start.2) | collective-permute-done | bytes 462880 | tf_op jit(solution)/shard_map/ppermute | solution.py:219
  20.1 0.2 rest_of_packet.5
  20.2 0.9 %collective-permute-start.6 = (bf16[1424,128]{1,0:T(8,128)(2,1)S(1)}, bf16[1424,128]{1,0:T(8,128)(2,1)S(1)}, u32[]{:S(2)}, u32[]{:S(2)}) collective-permute-start(bf16[1424,128]{1,0:T(8,128)(2,1)S(1)} %rest_of_packet.5), channel_id=1, source_target_pairs={{0,1},{1,0},{2,6},{3,7},{4,5},{5,4},{6,2},{7,3},{8,9},{9,8},{10,14... | collective-permute-start | bytes 1093640 | tf_op jit(solution)/shard_map/ppermute | solution.py:219
  21.2 0.0 collective-permute-done.7.refs_1_
  21.2 4.8 %collective-permute-start.14 = (bf16[1808,128]{1,0:T(8,128)(2,1)S(1)}, bf16[1808,128]{1,0:T(8,128)(2,1)S(1)}, u32[]{:S(2)}, u32[]{:S(2)}) collective-permute-start(bf16[1808,128]{1,0:T(8,128)(2,1)S(1)} %collective-permute-done.3.in_ref.refs_2_), channel_id=1, source_target_pairs={{0,2},{1,3},{2,0},{3,1},{4,6},{5,7},{6,4},{7,5},{8,10},{9,11},{10,... | collective-permute-start | bytes 1388552 | tf_op jit(solution)/shard_map/ppermute | solution.py:222
  26.0 0.0 collective-permute-done.12.refs_0_
  26.0 2.5 %collective-permute-start.13 = (bf16[1424,128]{1,0:T(8,128)(2,1)S(1)}, bf16[1424,128]{1,0:T(8,128)(2,1)S(1)}, u32[]{:S(2)}, u32[]{:S(2)}) collective-permute-start(bf16[1424,128]{1,0:T(8,128)(2,1)S(1)} %collective-permute-done.12.refs_0_), channel_id=1, source_target_pairs={{0,2},{1,3},{2,0},{3,1},{4,6},{5,7},{6,4},{7,5},{8,10},{9,11},{10,... | collective-permute-start | bytes 1093640 | tf_op jit(solution)/shard_map/ppermute | solution.py:222
  28.5 0.0 copy-done
  28.5 2.0 %products.3.refs_6_ = f32[256,8,128]{2,1,0:T(8,128)S(1)} custom-call(bf16[1424,128]{1,0:T(8,128)(2,1)S(1)} %copy-done, bf16[1424,128]{1,0:T(8,128)(2,1)S(1)} %collective-permute-done.7.refs_1_, bf16[1808,128]{1,0:T(8,128)(2,1)S(1)} %collective-permute-done.3.in_ref.refs_2_, bf16[1808,128]{1,0:T(8,128)(2,1)S(1)} %collective-permute-done.in_ref.refs_3_, ...), custom_call_target="tpu_custom_call" | custom-call | flops 62914560 | bytes 5242880 | tf_op jit(solution)/shard_map/products/pallas_call | solution.py:154
  30.5 0.0 collective-permute-done.4.refs_3_
  30.5 2.7 %collective-permute-start.1 = (bf16[1808,128]{1,0:T(8,128)(2,1)S(1)}, bf16[1808,128]{1,0:T(8,128)(2,1)S(1)}, u32[]{:S(2)}, u32[]{:S(2)}) collective-permute-start(bf16[1808,128]{1,0:T(8,128)(2,1)S(1)} %collective-permute-done.in_ref.refs_3_), channel_id=1, source_target_pairs={{0,2},{1,3},{2,0},{3,1},{4,6},{5,7},{6,4},{7,5},{8,10},{9,11},{10,... | collective-permute-start | bytes 1388552 | tf_op jit(solution)/shard_map/ppermute | solution.py:222
  33.3 0.0 collective-permute-done.5.refs_4_
  33.3 0.0 collective-permute-done.6.refs_5_
  33.3 0.9 %collective-permute-start.8 = (bf16[1808,128]{1,0:T(8,128)(2,1)S(1)}, bf16[1808,128]{1,0:T(8,128)(2,1)S(1)}, u32[]{:S(2)}, u32[]{:S(2)}) collective-permute-start(bf16[1808,128]{1,0:T(8,128)(2,1)S(1)} %collective-permute-done.2.in_ref.refs_4_), channel_id=1, source_target_pairs={{0,2},{1,3},{2,0},{3,1},{4,6},{5,7},{6,4},{7,5},{8,10},{9,11},{10,... | collective-permute-start | bytes 1388552 | tf_op jit(solution)/shard_map/ppermute | solution.py:222
  34.2 0.0 collective-permute-start.10
  34.2 0.0 collective-permute-done.13.refs_1_
  34.2 0.5 collective-permute-start.11
  34.7 0.0 collective-permute-done.14.refs_2_
  34.7 0.1 collective-permute-start.9
  34.8 2.2 %products.4.refs_5_ = f32[256,8,128]{2,1,0:T(8,128)S(1)} custom-call(bf16[1424,128]{1,0:T(8,128)(2,1)S(1)} %collective-permute-done.12.refs_0_, bf16[1424,128]{1,0:T(8,128)(2,1)S(1)} %collective-permute-done.13.refs_1_, bf16[1808,128]{1,0:T(8,128)(2,1)S(1)} %collective-permute-done.14.refs_2_, ...), custom_call_target="tpu_custom_call", output_to_operand_aliasing={{}: (6, {})} | custom-call | flops 75497472 | bytes 6291456 | tf_op jit(solution)/shard_map/products/pallas_call | solution.py:154
  37.0 0.0 collective-permute-done.1.refs_0_
  37.0 0.0 collective-permute-done.10.refs_3_
  37.0 0.0 collective-permute-done.11.refs_4_
  37.0 0.2 collective-permute-done.9.refs_2_
  37.2 0.0 collective-permute-done.8.refs_1_
  37.2 2.6 %products.5 = s32[32,5,8,128]{3,2,1,0:T(8,128)S(1)} custom-call(bf16[1808,128]{1,0:T(8,128)(2,1)S(1)} %collective-permute-done.1.refs_0_, bf16[1808,128]{1,0:T(8,128)(2,1)S(1)} %collective-permute-done.8.refs_1_, bf16[1424,128]{1,0:T(8,128)(2,1)S(1)} %collective-permute-done.9.refs_2_, bf16[1424,128]{1,0:T(8,128)(2,1)S(1)} %collective-permute-done.10.refs_3_, ...), custom_call_target="tpu_custom_call" | custom-call | flops 62914560 | bytes 5242880 | tf_op jit(solution)/shard_map/products/pallas_call | solution.py:154
  39.8 24.5 %all_to_all.5 = s32[32,5,8,128]{3,2,1,0:T(8,128)S(1)} all-to-all(s32[32,5,8,128]{3,2,1,0:T(8,128)S(1)} %products.5), channel_id=1, replica_groups=mesh['plane'=2,'pair'=4,'core'=2,'col'=2] {'plane','pair','core','col'}, dimensions={0} | all-to-all | bytes 1310720 | tf_op jit(solution)/shard_map/all_to_all | solution.py:246
  64.3 1.3 %turn.1 = f32[128,1024]{1,0:T(8,128)} custom-call(s32[2,16,5,8,128]{4,3,2,1,0:T(8,128)S(1)} %bitcast.2), custom_call_target="tpu_custom_call" | custom-call | tf_op jit(solution)/shard_map/turn/pallas_call | solution.py:247
Async XLA Ops:
  2.9 10.4 %collective-permute-start.3 = (bf16[1808,128]{1,0:T(8,128)(2,1)}, bf16[1808,128]{1,0:T(8,128)(2,1)S(1)}, u32[]{:S(2)}, u32[]{:S(2)}) collective-permute-start(bf16[1808,128]{1,0:T(8,128)(2,1)} %get-tuple-element.17), channel_id=1, source_target_pairs={{0,1},{1,0},{2,6},{3,7},{4,5},{5,4},{6,2},{7,3},{8,9},{9,8},{10,14... | collective-permute-start | bytes 1388552 | tf_op jit(solution)/shard_map/ppermute | solution.py:219
  5.0 10.4 %collective-permute-start = (bf16[1808,128]{1,0:T(8,128)(2,1)}, bf16[1808,128]{1,0:T(8,128)(2,1)S(1)}, u32[]{:S(2)}, u32[]{:S(2)}) collective-permute-start(bf16[1808,128]{1,0:T(8,128)(2,1)} %get-tuple-element.15), channel_id=1, source_target_pairs={{0,4},{1,5},{2,10},{3,11},{4,0},{5,1},{6,14},{7,15},{8,12},{9,13},... | collective-permute-start | bytes 1388552 | tf_op jit(solution)/shard_map/ppermute | solution.py:219
  6.3 13.8 %collective-permute-start.2 = (bf16[1808,128]{1,0:T(8,128)(2,1)}, bf16[1808,128]{1,0:T(8,128)(2,1)S(1)}, u32[]{:S(2)}, u32[]{:S(2)}) collective-permute-start(bf16[1808,128]{1,0:T(8,128)(2,1)} %get-tuple-element.16), channel_id=1, source_target_pairs={{0,8},{1,9},{2,3},{3,2},{4,12},{5,13},{6,7},{7,6},{8,0},{9,1},{10,... | collective-permute-start | bytes 1388552 | tf_op jit(solution)/shard_map/ppermute | solution.py:219
  7.5 13.7 %collective-permute-start.7 = (bf16[1424,128]{1,0:T(8,128)(2,1)}, bf16[1424,128]{1,0:T(8,128)(2,1)S(1)}, u32[]{:S(2)}, u32[]{:S(2)}) collective-permute-start(bf16[1424,128]{1,0:T(8,128)(2,1)} %get-tuple-element.18.refs_0_), channel_id=1, source_target_pairs={{0,2},{1,3},{2,0},{3,1},{4,6},{5,7},{6,4},{7,5},{8,10},{9,11},{10,... | collective-permute-start | bytes 1093640 | tf_op jit(solution)/shard_map/ppermute | solution.py:222
  9.0 16.9 %collective-permute-start.12 = (bf16[1424,128]{1,0:T(8,128)(2,1)}, bf16[1424,128]{1,0:T(8,128)(2,1)S(1)}, u32[]{:S(2)}, u32[]{:S(2)}) collective-permute-start(bf16[1424,128]{1,0:T(8,128)(2,1)} %get-tuple-element.23), channel_id=1, source_target_pairs={{0,13},{1,12},{2,15},{3,14},{4,9},{5,8},{6,11},{7,10},{8,5},{9,4},... | collective-permute-start | bytes 1093640 | tf_op jit(solution)/shard_map/ppermute | solution.py:229
  13.5 17.0 %collective-permute-start.4 = (bf16[1424,128]{1,0:T(8,128)(2,1)S(1)}, bf16[1424,128]{1,0:T(8,128)(2,1)S(1)}, u32[]{:S(2)}, u32[]{:S(2)}) collective-permute-start(bf16[1424,128]{1,0:T(8,128)(2,1)S(1)} %rest_of_packet.3), channel_id=1, source_target_pairs={{0,4},{1,5},{2,10},{3,11},{4,0},{5,1},{6,14},{7,15},{8,12},{9,13},... | collective-permute-start | bytes 1093640 | tf_op jit(solution)/shard_map/ppermute | solution.py:219
  15.6 12.9 %copy-start = (bf16[1424,128]{1,0:T(8,128)(2,1)S(1)}, bf16[1424,128]{1,0:T(8,128)(2,1)}, u32[]{:S(2)}) copy-start(bf16[1424,128]{1,0:T(8,128)(2,1)} %get-tuple-element.18.refs_0_) | copy-start | bytes 1093636
  15.6 17.7 %collective-permute-start.5 = (bf16[1424,128]{1,0:T(8,128)(2,1)S(1)}, bf16[1424,128]{1,0:T(8,128)(2,1)S(1)}, u32[]{:S(2)}, u32[]{:S(2)}) collective-permute-start(bf16[1424,128]{1,0:T(8,128)(2,1)S(1)} %rest_of_packet.4), channel_id=1, source_target_pairs={{0,8},{1,9},{2,3},{3,2},{4,12},{5,13},{6,7},{7,6},{8,0},{9,1},{10,... | collective-permute-start | bytes 1093640 | tf_op jit(solution)/shard_map/ppermute | solution.py:219
  20.2 13.0 %collective-permute-start.6 = (bf16[1424,128]{1,0:T(8,128)(2,1)S(1)}, bf16[1424,128]{1,0:T(8,128)(2,1)S(1)}, u32[]{:S(2)}, u32[]{:S(2)}) collective-permute-start(bf16[1424,128]{1,0:T(8,128)(2,1)S(1)} %rest_of_packet.5), channel_id=1, source_target_pairs={{0,1},{1,0},{2,6},{3,7},{4,5},{5,4},{6,2},{7,3},{8,9},{9,8},{10,14... | collective-permute-start | bytes 1093640 | tf_op jit(solution)/shard_map/ppermute | solution.py:219
  21.2 13.5 %collective-permute-start.14 = (bf16[1808,128]{1,0:T(8,128)(2,1)S(1)}, bf16[1808,128]{1,0:T(8,128)(2,1)S(1)}, u32[]{:S(2)}, u32[]{:S(2)}) collective-permute-start(bf16[1808,128]{1,0:T(8,128)(2,1)S(1)} %collective-permute-done.3.in_ref.refs_2_), channel_id=1, source_target_pairs={{0,2},{1,3},{2,0},{3,1},{4,6},{5,7},{6,4},{7,5},{8,10},{9,11},{10,... | collective-permute-start | bytes 1388552 | tf_op jit(solution)/shard_map/ppermute | solution.py:222
  26.0 8.2 %collective-permute-start.13 = (bf16[1424,128]{1,0:T(8,128)(2,1)S(1)}, bf16[1424,128]{1,0:T(8,128)(2,1)S(1)}, u32[]{:S(2)}, u32[]{:S(2)}) collective-permute-start(bf16[1424,128]{1,0:T(8,128)(2,1)S(1)} %collective-permute-done.12.refs_0_), channel_id=1, source_target_pairs={{0,2},{1,3},{2,0},{3,1},{4,6},{5,7},{6,4},{7,5},{8,10},{9,11},{10,... | collective-permute-start | bytes 1093640 | tf_op jit(solution)/shard_map/ppermute | solution.py:222
  30.5 6.5 %collective-permute-start.1 = (bf16[1808,128]{1,0:T(8,128)(2,1)S(1)}, bf16[1808,128]{1,0:T(8,128)(2,1)S(1)}, u32[]{:S(2)}, u32[]{:S(2)}) collective-permute-start(bf16[1808,128]{1,0:T(8,128)(2,1)S(1)} %collective-permute-done.in_ref.refs_3_), channel_id=1, source_target_pairs={{0,2},{1,3},{2,0},{3,1},{4,6},{5,7},{6,4},{7,5},{8,10},{9,11},{10,... | collective-permute-start | bytes 1388552 | tf_op jit(solution)/shard_map/ppermute | solution.py:222
  33.3 3.9 %collective-permute-start.8 = (bf16[1808,128]{1,0:T(8,128)(2,1)S(1)}, bf16[1808,128]{1,0:T(8,128)(2,1)S(1)}, u32[]{:S(2)}, u32[]{:S(2)}) collective-permute-start(bf16[1808,128]{1,0:T(8,128)(2,1)S(1)} %collective-permute-done.2.in_ref.refs_4_), channel_id=1, source_target_pairs={{0,2},{1,3},{2,0},{3,1},{4,6},{5,7},{6,4},{7,5},{8,10},{9,11},{10,... | collective-permute-start | bytes 1388552 | tf_op jit(solution)/shard_map/ppermute | solution.py:222
  34.2 2.8 %collective-permute-start.10 = (bf16[1424,128]{1,0:T(8,128)(2,1)S(1)}, bf16[1424,128]{1,0:T(8,128)(2,1)S(1)}, u32[]{:S(2)}, u32[]{:S(2)}) collective-permute-start(bf16[1424,128]{1,0:T(8,128)(2,1)S(1)} %collective-permute-done.5.refs_4_), channel_id=1, source_target_pairs={{0,2},{1,3},{2,0},{3,1},{4,6},{5,7},{6,4},{7,5},{8,10},{9,11},{10,... | collective-permute-start | bytes 1093640 | tf_op jit(solution)/shard_map/ppermute | solution.py:222
  34.2 2.8 %collective-permute-start.11 = (bf16[1424,128]{1,0:T(8,128)(2,1)S(1)}, bf16[1424,128]{1,0:T(8,128)(2,1)S(1)}, u32[]{:S(2)}, u32[]{:S(2)}) collective-permute-start(bf16[1424,128]{1,0:T(8,128)(2,1)S(1)} %collective-permute-done.6.refs_5_), channel_id=1, source_target_pairs={{0,2},{1,3},{2,0},{3,1},{4,6},{5,7},{6,4},{7,5},{8,10},{9,11},{10,... | collective-permute-start | bytes 1093640 | tf_op jit(solution)/shard_map/ppermute | solution.py:222
  34.7 2.5 %collective-permute-start.9 = (bf16[1424,128]{1,0:T(8,128)(2,1)S(1)}, bf16[1424,128]{1,0:T(8,128)(2,1)S(1)}, u32[]{:S(2)}, u32[]{:S(2)}) collective-permute-start(bf16[1424,128]{1,0:T(8,128)(2,1)S(1)} %collective-permute-done.4.refs_3_), channel_id=1, source_target_pairs={{0,2},{1,3},{2,0},{3,1},{4,6},{5,7},{6,4},{7,5},{8,10},{9,11},{10,... | collective-permute-start | bytes 1093640 | tf_op jit(solution)/shard_map/ppermute | solution.py:222

commit v18 on v17

--- a/solution.py
+++ b/solution.py
@@ -109,11 +109,16 @@
                 left, jnp.concatenate(right, axis=1), preferred_element_type=jnp.float32
             )
             start = f * (per_p + per_q)
-            for k in range(per_p):
-                row = ids[i, start + k] * tile_count
-                for l in range(per_q):
-                    spot = row + ids[i, start + per_p + l]
-                    acc_ref[spot] += product[l * strip:(l + 1) * strip, k * extent:(k + 1) * extent]
+            spots = [
+                ids[i, start + k] * tile_count + ids[i, start + per_p + l]
+                for k in range(per_p)
+                for l in range(per_q)
+            ]
+            before = [acc_ref[spot] for spot in spots]
+            for n, spot in enumerate(spots):
+                k, l = divmod(n, per_q)
+                term = product[l * strip:(l + 1) * strip, k * extent:(k + 1) * extent]
+                acc_ref[spot] = before[n] + term
     if coded:
         code(acc_ref, out_ref, out_ref.shape[1] * 2 - 2)
 

time: 65.7 us -> 64.9 us (0.988)
  Pallas kernels: 11.5 us -> 8.95 us
  waiting for transfers between devices: 6.71 us -> 8.37 us
    pallas_call x3, Pallas kernels: 6.88 us -> 4.29 us  [add_products(): pl.pallas_call(functools.partial(product_kernel, sizes, tile_count, passe...]
    ppermute x8, waiting for transfers between devices: 0.17 us -> 1.15 us  [across(): return lax.ppermute(values, seat, [(s, s ^ cols) for s in range(SEATS)])]
    ppermute x6, waiting for transfers between devices: 6.54 us -> 7.22 us  [along(): return lax.ppermute(values, seat, hops)]
  transfers between devices with their start and end apart: 15 -> 15, of which waited for: 3 -> 6; matrix products, arithmetic and copies ran while one was open for 0% -> 0% of each run, Pallas kernels for 7% -> 5%
where the time goes in v18:
time: 64.9 us; the launch traced here: 64.7 us
  blocking collectives  24.5 us (38%)
  starting transfers between devices  22.8 us (35%)
  Pallas kernels  8.95 us (14%)
  waiting for transfers between devices  8.37 us (13%)
    all_to_all x1, blocking collectives, body(): lax.all_to_all(coded, every, split_axis=0, concat_axis=0, tiled=True)  24.5 us
    ppermute x8, starting transfers between devices, across(): return lax.ppermute(values, seat, [(s, s ^ cols) for s in range(SEATS)])  13.1 us
    ppermute x6, starting transfers between devices, along(): return lax.ppermute(values, seat, hops)  9.7 us
    ppermute x6, waiting for transfers between devices, along(): return lax.ppermute(values, seat, hops)  7.22 us
    pallas_call x3, Pallas kernels, add_products(): pl.pallas_call(functools.partial(product_kernel, sizes, tile_count, passe...  4.29 us
    pallas_call x1, Pallas kernels, body(): pl.pallas_call(functools.partial(pack_kernel, cols), out_shape=[jax.Shape...  2.93 us
  transfers between devices with their start and end apart: 15, of which 6 were waited for; matrix products, arithmetic and copies ran while one was open for 0% of the time, Pallas kernels for 5%

profile of v18, /device:TPU:1, one launch (start us, length us, event | category | flops | bytes accessed | tf_op | source)
XLA Modules:
  0.0 64.7 jit_solution(10998786571006904510)
XLA Ops:
  0.0 2.9 %pack.1 = (bf16[1424,128]{1,0:T(8,128)(2,1)}, bf16[1808,128]{1,0:T(8,128)(2,1)}, bf16[1808,128]{1,0:T(8,128)(2,1)}, bf16[1808,128]{1,0:T(8,128)(2,1)}, bf16[1424,128]{1,0:T(8,128)(2,1)}) custom-call(s32[2,4]{1,0:T(2,128)} %bitcast.3, s32[4,6]{1,0:T(4,128)} %q_ids.1, bf16[4,2,128,128]{3,2,1,0:T(8,128)(2,1)} %p_ref.1, bf16[4,6,128,128]{3,2,1,0:T(8,128)(2,1)} %q_ref.1), custom_call_target="tpu_custom_call" | custom-call | tf_op jit(solution)/shard_map/pack/pallas_call | solution.py:210
  2.9 2.0 %collective-permute-start.3 = (bf16[1808,128]{1,0:T(8,128)(2,1)}, bf16[1808,128]{1,0:T(8,128)(2,1)S(1)}, u32[]{:S(2)}, u32[]{:S(2)}) collective-permute-start(bf16[1808,128]{1,0:T(8,128)(2,1)} %get-tuple-element.17), channel_id=1, source_target_pairs={{0,1},{1,0},{2,6},{3,7},{4,5},{5,4},{6,2},{7,3},{8,9},{9,8},{10,14... | collective-permute-start | bytes 1388552 | tf_op jit(solution)/shard_map/ppermute | solution.py:224
  5.0 1.3 %collective-permute-start = (bf16[1808,128]{1,0:T(8,128)(2,1)}, bf16[1808,128]{1,0:T(8,128)(2,1)S(1)}, u32[]{:S(2)}, u32[]{:S(2)}) collective-permute-start(bf16[1808,128]{1,0:T(8,128)(2,1)} %get-tuple-element.15), channel_id=1, source_target_pairs={{0,4},{1,5},{2,10},{3,11},{4,0},{5,1},{6,14},{7,15},{8,12},{9,13},... | collective-permute-start | bytes 1388552 | tf_op jit(solution)/shard_map/ppermute | solution.py:224
  6.3 1.2 %collective-permute-start.2 = (bf16[1808,128]{1,0:T(8,128)(2,1)}, bf16[1808,128]{1,0:T(8,128)(2,1)S(1)}, u32[]{:S(2)}, u32[]{:S(2)}) collective-permute-start(bf16[1808,128]{1,0:T(8,128)(2,1)} %get-tuple-element.16), channel_id=1, source_target_pairs={{0,8},{1,9},{2,3},{3,2},{4,12},{5,13},{6,7},{7,6},{8,0},{9,1},{10,... | collective-permute-start | bytes 1388552 | tf_op jit(solution)/shard_map/ppermute | solution.py:224
  7.5 1.5 %collective-permute-start.7 = (bf16[1424,128]{1,0:T(8,128)(2,1)}, bf16[1424,128]{1,0:T(8,128)(2,1)S(1)}, u32[]{:S(2)}, u32[]{:S(2)}) collective-permute-start(bf16[1424,128]{1,0:T(8,128)(2,1)} %get-tuple-element.18.refs_0_), channel_id=1, source_target_pairs={{0,2},{1,3},{2,0},{3,1},{4,6},{5,7},{6,4},{7,5},{8,10},{9,11},{10,... | collective-permute-start | bytes 1093640 | tf_op jit(solution)/shard_map/ppermute | solution.py:227
  9.0 0.0 collective-permute-start.12
  9.0 4.3 %collective-permute-done.3.in_ref.refs_2_ = bf16[1808,128]{1,0:T(8,128)(2,1)S(1)} collective-permute-done((bf16[1808,128]{1,0:T(8,128)(2,1)}, bf16[1808,128]{1,0:T(8,128)(2,1)S(1)}, u32[]{:S(2)}, u32[]{:S(2)}) %collective-permute-start.3) | collective-permute-done | bytes 462880 | tf_op jit(solution)/shard_map/ppermute | solution.py:224
  13.4 0.2 rest_of_packet.3
  13.5 1.9 %collective-permute-start.4 = (bf16[1424,128]{1,0:T(8,128)(2,1)S(1)}, bf16[1424,128]{1,0:T(8,128)(2,1)S(1)}, u32[]{:S(2)}, u32[]{:S(2)}) collective-permute-start(bf16[1424,128]{1,0:T(8,128)(2,1)S(1)} %rest_of_packet.3), channel_id=1, source_target_pairs={{0,4},{1,5},{2,10},{3,11},{4,0},{5,1},{6,14},{7,15},{8,12},{9,13},... | collective-permute-start | bytes 1093640 | tf_op jit(solution)/shard_map/ppermute | solution.py:224
  15.4 0.0 collective-permute-done.in_ref.refs_3_
  15.4 0.2 rest_of_packet.4
  15.6 0.0 copy-start
  15.6 2.3 %collective-permute-start.5 = (bf16[1424,128]{1,0:T(8,128)(2,1)S(1)}, bf16[1424,128]{1,0:T(8,128)(2,1)S(1)}, u32[]{:S(2)}, u32[]{:S(2)}) collective-permute-start(bf16[1424,128]{1,0:T(8,128)(2,1)S(1)} %rest_of_packet.4), channel_id=1, source_target_pairs={{0,8},{1,9},{2,3},{3,2},{4,12},{5,13},{6,7},{7,6},{8,0},{9,1},{10,... | collective-permute-start | bytes 1093640 | tf_op jit(solution)/shard_map/ppermute | solution.py:224
  17.9 2.2 %collective-permute-done.2.in_ref.refs_4_ = bf16[1808,128]{1,0:T(8,128)(2,1)S(1)} collective-permute-done((bf16[1808,128]{1,0:T(8,128)(2,1)}, bf16[1808,128]{1,0:T(8,128)(2,1)S(1)}, u32[]{:S(2)}, u32[]{:S(2)}) %collective-permute-start.2) | collective-permute-done | bytes 462880 | tf_op jit(solution)/shard_map/ppermute | solution.py:224
  20.1 0.2 rest_of_packet.5
  20.2 0.9 %collective-permute-start.6 = (bf16[1424,128]{1,0:T(8,128)(2,1)S(1)}, bf16[1424,128]{1,0:T(8,128)(2,1)S(1)}, u32[]{:S(2)}, u32[]{:S(2)}) collective-permute-start(bf16[1424,128]{1,0:T(8,128)(2,1)S(1)} %rest_of_packet.5), channel_id=1, source_target_pairs={{0,1},{1,0},{2,6},{3,7},{4,5},{5,4},{6,2},{7,3},{8,9},{9,8},{10,14... | collective-permute-start | bytes 1093640 | tf_op jit(solution)/shard_map/ppermute | solution.py:224
  21.2 0.0 collective-permute-done.7.refs_1_
  21.2 4.8 %collective-permute-start.14 = (bf16[1808,128]{1,0:T(8,128)(2,1)S(1)}, bf16[1808,128]{1,0:T(8,128)(2,1)S(1)}, u32[]{:S(2)}, u32[]{:S(2)}) collective-permute-start(bf16[1808,128]{1,0:T(8,128)(2,1)S(1)} %collective-permute-done.3.in_ref.refs_2_), channel_id=1, source_target_pairs={{0,2},{1,3},{2,0},{3,1},{4,6},{5,7},{6,4},{7,5},{8,10},{9,11},{10,... | collective-permute-start | bytes 1388552 | tf_op jit(solution)/shard_map/ppermute | solution.py:227
  26.0 0.0 collective-permute-done.12.refs_0_
  26.0 2.5 %collective-permute-start.13 = (bf16[1424,128]{1,0:T(8,128)(2,1)S(1)}, bf16[1424,128]{1,0:T(8,128)(2,1)S(1)}, u32[]{:S(2)}, u32[]{:S(2)}) collective-permute-start(bf16[1424,128]{1,0:T(8,128)(2,1)S(1)} %collective-permute-done.12.refs_0_), channel_id=1, source_target_pairs={{0,2},{1,3},{2,0},{3,1},{4,6},{5,7},{6,4},{7,5},{8,10},{9,11},{10,... | collective-permute-start | bytes 1093640 | tf_op jit(solution)/shard_map/ppermute | solution.py:227
  28.5 0.0 copy-done
  28.5 1.2 %products.3.refs_6_ = f32[256,8,128]{2,1,0:T(8,128)S(1)} custom-call(bf16[1424,128]{1,0:T(8,128)(2,1)S(1)} %copy-done, bf16[1424,128]{1,0:T(8,128)(2,1)S(1)} %collective-permute-done.7.refs_1_, bf16[1808,128]{1,0:T(8,128)(2,1)S(1)} %collective-permute-done.3.in_ref.refs_2_, bf16[1808,128]{1,0:T(8,128)(2,1)S(1)} %collective-permute-done.in_ref.refs_3_, ...), custom_call_target="tpu_custom_call" | custom-call | flops 62914560 | bytes 5242880 | tf_op jit(solution)/shard_map/products/pallas_call | solution.py:159
  29.7 0.7 %collective-permute-done.4.refs_3_ = bf16[1424,128]{1,0:T(8,128)(2,1)S(1)} collective-permute-done((bf16[1424,128]{1,0:T(8,128)(2,1)S(1)}, bf16[1424,128]{1,0:T(8,128)(2,1)S(1)}, u32[]{:S(2)}, u32[]{:S(2)}) %collective-permute-start.4) | collective-permute-done | bytes 364576 | tf_op jit(solution)/shard_map/ppermute | solution.py:224
  30.4 2.8 %collective-permute-start.1 = (bf16[1808,128]{1,0:T(8,128)(2,1)S(1)}, bf16[1808,128]{1,0:T(8,128)(2,1)S(1)}, u32[]{:S(2)}, u32[]{:S(2)}) collective-permute-start(bf16[1808,128]{1,0:T(8,128)(2,1)S(1)} %collective-permute-done.in_ref.refs_3_), channel_id=1, source_target_pairs={{0,2},{1,3},{2,0},{3,1},{4,6},{5,7},{6,4},{7,5},{8,10},{9,11},{10,... | collective-permute-start | bytes 1388552 | tf_op jit(solution)/shard_map/ppermute | solution.py:227
  33.3 0.0 collective-permute-done.5.refs_4_
  33.3 0.0 collective-permute-done.6.refs_5_
  33.3 0.9 %collective-permute-start.8 = (bf16[1808,128]{1,0:T(8,128)(2,1)S(1)}, bf16[1808,128]{1,0:T(8,128)(2,1)S(1)}, u32[]{:S(2)}, u32[]{:S(2)}) collective-permute-start(bf16[1808,128]{1,0:T(8,128)(2,1)S(1)} %collective-permute-done.2.in_ref.refs_4_), channel_id=1, source_target_pairs={{0,2},{1,3},{2,0},{3,1},{4,6},{5,7},{6,4},{7,5},{8,10},{9,11},{10,... | collective-permute-start | bytes 1388552 | tf_op jit(solution)/shard_map/ppermute | solution.py:227
  34.2 0.0 collective-permute-start.10
  34.2 0.0 collective-permute-done.13.refs_1_
  34.2 0.5 collective-permute-start.11
  34.7 0.0 collective-permute-done.14.refs_2_
  34.7 0.1 collective-permute-start.9
  34.8 1.3 %products.4.refs_5_ = f32[256,8,128]{2,1,0:T(8,128)S(1)} custom-call(bf16[1424,128]{1,0:T(8,128)(2,1)S(1)} %collective-permute-done.12.refs_0_, bf16[1424,128]{1,0:T(8,128)(2,1)S(1)} %collective-permute-done.13.refs_1_, bf16[1808,128]{1,0:T(8,128)(2,1)S(1)} %collective-permute-done.14.refs_2_, ...), custom_call_target="tpu_custom_call", output_to_operand_aliasing={{}: (6, {})} | custom-call | flops 75497472 | bytes 6291456 | tf_op jit(solution)/shard_map/products/pallas_call | solution.py:159
  36.0 0.0 collective-permute-done.1.refs_0_
  36.1 0.1 collective-permute-done.10.refs_3_
  36.2 0.5 collective-permute-done.11.refs_4_
  36.7 0.5 collective-permute-done.9.refs_2_
  37.2 0.0 collective-permute-done.8.refs_1_
  37.2 1.8 %products.5 = s32[32,5,8,128]{3,2,1,0:T(8,128)S(1)} custom-call(bf16[1808,128]{1,0:T(8,128)(2,1)S(1)} %collective-permute-done.1.refs_0_, bf16[1808,128]{1,0:T(8,128)(2,1)S(1)} %collective-permute-done.8.refs_1_, bf16[1424,128]{1,0:T(8,128)(2,1)S(1)} %collective-permute-done.9.refs_2_, bf16[1424,128]{1,0:T(8,128)(2,1)S(1)} %collective-permute-done.10.refs_3_, ...), custom_call_target="tpu_custom_call" | custom-call | flops 62914560 | bytes 5242880 | tf_op jit(solution)/shard_map/products/pallas_call | solution.py:159
  39.0 24.5 %all_to_all.5 = s32[32,5,8,128]{3,2,1,0:T(8,128)S(1)} all-to-all(s32[32,5,8,128]{3,2,1,0:T(8,128)S(1)} %products.5), channel_id=1, replica_groups=mesh['plane'=2,'pair'=4,'core'=2,'col'=2] {'plane','pair','core','col'}, dimensions={0} | all-to-all | bytes 1310720 | tf_op jit(solution)/shard_map/all_to_all | solution.py:251
  63.4 1.3 %turn.1 = f32[128,1024]{1,0:T(8,128)} custom-call(s32[2,16,5,8,128]{4,3,2,1,0:T(8,128)S(1)} %bitcast.2), custom_call_target="tpu_custom_call" | custom-call | tf_op jit(solution)/shard_map/turn/pallas_call | solution.py:252
Async XLA Ops:
  2.9 10.4 %collective-permute-start.3 = (bf16[1808,128]{1,0:T(8,128)(2,1)}, bf16[1808,128]{1,0:T(8,128)(2,1)S(1)}, u32[]{:S(2)}, u32[]{:S(2)}) collective-permute-start(bf16[1808,128]{1,0:T(8,128)(2,1)} %get-tuple-element.17), channel_id=1, source_target_pairs={{0,1},{1,0},{2,6},{3,7},{4,5},{5,4},{6,2},{7,3},{8,9},{9,8},{10,14... | collective-permute-start | bytes 1388552 | tf_op jit(solution)/shard_map/ppermute | solution.py:224
  5.0 10.4 %collective-permute-start = (bf16[1808,128]{1,0:T(8,128)(2,1)}, bf16[1808,128]{1,0:T(8,128)(2,1)S(1)}, u32[]{:S(2)}, u32[]{:S(2)}) collective-permute-start(bf16[1808,128]{1,0:T(8,128)(2,1)} %get-tuple-element.15), channel_id=1, source_target_pairs={{0,4},{1,5},{2,10},{3,11},{4,0},{5,1},{6,14},{7,15},{8,12},{9,13},... | collective-permute-start | bytes 1388552 | tf_op jit(solution)/shard_map/ppermute | solution.py:224
  6.3 13.8 %collective-permute-start.2 = (bf16[1808,128]{1,0:T(8,128)(2,1)}, bf16[1808,128]{1,0:T(8,128)(2,1)S(1)}, u32[]{:S(2)}, u32[]{:S(2)}) collective-permute-start(bf16[1808,128]{1,0:T(8,128)(2,1)} %get-tuple-element.16), channel_id=1, source_target_pairs={{0,8},{1,9},{2,3},{3,2},{4,12},{5,13},{6,7},{7,6},{8,0},{9,1},{10,... | collective-permute-start | bytes 1388552 | tf_op jit(solution)/shard_map/ppermute | solution.py:224
  7.5 13.7 %collective-permute-start.7 = (bf16[1424,128]{1,0:T(8,128)(2,1)}, bf16[1424,128]{1,0:T(8,128)(2,1)S(1)}, u32[]{:S(2)}, u32[]{:S(2)}) collective-permute-start(bf16[1424,128]{1,0:T(8,128)(2,1)} %get-tuple-element.18.refs_0_), channel_id=1, source_target_pairs={{0,2},{1,3},{2,0},{3,1},{4,6},{5,7},{6,4},{7,5},{8,10},{9,11},{10,... | collective-permute-start | bytes 1093640 | tf_op jit(solution)/shard_map/ppermute | solution.py:227
  9.0 16.9 %collective-permute-start.12 = (bf16[1424,128]{1,0:T(8,128)(2,1)}, bf16[1424,128]{1,0:T(8,128)(2,1)S(1)}, u32[]{:S(2)}, u32[]{:S(2)}) collective-permute-start(bf16[1424,128]{1,0:T(8,128)(2,1)} %get-tuple-element.23), channel_id=1, source_target_pairs={{0,13},{1,12},{2,15},{3,14},{4,9},{5,8},{6,11},{7,10},{8,5},{9,4},... | collective-permute-start | bytes 1093640 | tf_op jit(solution)/shard_map/ppermute | solution.py:234
  13.5 16.9 %collective-permute-start.4 = (bf16[1424,128]{1,0:T(8,128)(2,1)S(1)}, bf16[1424,128]{1,0:T(8,128)(2,1)S(1)}, u32[]{:S(2)}, u32[]{:S(2)}) collective-permute-start(bf16[1424,128]{1,0:T(8,128)(2,1)S(1)} %rest_of_packet.3), channel_id=1, source_target_pairs={{0,4},{1,5},{2,10},{3,11},{4,0},{5,1},{6,14},{7,15},{8,12},{9,13},... | collective-permute-start | bytes 1093640 | tf_op jit(solution)/shard_map/ppermute | solution.py:224
  15.6 12.9 %copy-start = (bf16[1424,128]{1,0:T(8,128)(2,1)S(1)}, bf16[1424,128]{1,0:T(8,128)(2,1)}, u32[]{:S(2)}) copy-start(bf16[1424,128]{1,0:T(8,128)(2,1)} %get-tuple-element.18.refs_0_) | copy-start | bytes 1093636
  15.6 17.7 %collective-permute-start.5 = (bf16[1424,128]{1,0:T(8,128)(2,1)S(1)}, bf16[1424,128]{1,0:T(8,128)(2,1)S(1)}, u32[]{:S(2)}, u32[]{:S(2)}) collective-permute-start(bf16[1424,128]{1,0:T(8,128)(2,1)S(1)} %rest_of_packet.4), channel_id=1, source_target_pairs={{0,8},{1,9},{2,3},{3,2},{4,12},{5,13},{6,7},{7,6},{8,0},{9,1},{10,... | collective-permute-start | bytes 1093640 | tf_op jit(solution)/shard_map/ppermute | solution.py:224
  20.2 13.0 %collective-permute-start.6 = (bf16[1424,128]{1,0:T(8,128)(2,1)S(1)}, bf16[1424,128]{1,0:T(8,128)(2,1)S(1)}, u32[]{:S(2)}, u32[]{:S(2)}) collective-permute-start(bf16[1424,128]{1,0:T(8,128)(2,1)S(1)} %rest_of_packet.5), channel_id=1, source_target_pairs={{0,1},{1,0},{2,6},{3,7},{4,5},{5,4},{6,2},{7,3},{8,9},{9,8},{10,14... | collective-permute-start | bytes 1093640 | tf_op jit(solution)/shard_map/ppermute | solution.py:224
  21.2 13.5 %collective-permute-start.14 = (bf16[1808,128]{1,0:T(8,128)(2,1)S(1)}, bf16[1808,128]{1,0:T(8,128)(2,1)S(1)}, u32[]{:S(2)}, u32[]{:S(2)}) collective-permute-start(bf16[1808,128]{1,0:T(8,128)(2,1)S(1)} %collective-permute-done.3.in_ref.refs_2_), channel_id=1, source_target_pairs={{0,2},{1,3},{2,0},{3,1},{4,6},{5,7},{6,4},{7,5},{8,10},{9,11},{10,... | collective-permute-start | bytes 1388552 | tf_op jit(solution)/shard_map/ppermute | solution.py:227
  26.0 8.2 %collective-permute-start.13 = (bf16[1424,128]{1,0:T(8,128)(2,1)S(1)}, bf16[1424,128]{1,0:T(8,128)(2,1)S(1)}, u32[]{:S(2)}, u32[]{:S(2)}) collective-permute-start(bf16[1424,128]{1,0:T(8,128)(2,1)S(1)} %collective-permute-done.12.refs_0_), channel_id=1, source_target_pairs={{0,2},{1,3},{2,0},{3,1},{4,6},{5,7},{6,4},{7,5},{8,10},{9,11},{10,... | collective-permute-start | bytes 1093640 | tf_op jit(solution)/shard_map/ppermute | solution.py:227
  30.4 5.6 %collective-permute-start.1 = (bf16[1808,128]{1,0:T(8,128)(2,1)S(1)}, bf16[1808,128]{1,0:T(8,128)(2,1)S(1)}, u32[]{:S(2)}, u32[]{:S(2)}) collective-permute-start(bf16[1808,128]{1,0:T(8,128)(2,1)S(1)} %collective-permute-done.in_ref.refs_3_), channel_id=1, source_target_pairs={{0,2},{1,3},{2,0},{3,1},{4,6},{5,7},{6,4},{7,5},{8,10},{9,11},{10,... | collective-permute-start | bytes 1388552 | tf_op jit(solution)/shard_map/ppermute | solution.py:227
  33.3 3.9 %collective-permute-start.8 = (bf16[1808,128]{1,0:T(8,128)(2,1)S(1)}, bf16[1808,128]{1,0:T(8,128)(2,1)S(1)}, u32[]{:S(2)}, u32[]{:S(2)}) collective-permute-start(bf16[1808,128]{1,0:T(8,128)(2,1)S(1)} %collective-permute-done.2.in_ref.refs_4_), channel_id=1, source_target_pairs={{0,2},{1,3},{2,0},{3,1},{4,6},{5,7},{6,4},{7,5},{8,10},{9,11},{10,... | collective-permute-start | bytes 1388552 | tf_op jit(solution)/shard_map/ppermute | solution.py:227
  34.2 2.0 %collective-permute-start.10 = (bf16[1424,128]{1,0:T(8,128)(2,1)S(1)}, bf16[1424,128]{1,0:T(8,128)(2,1)S(1)}, u32[]{:S(2)}, u32[]{:S(2)}) collective-permute-start(bf16[1424,128]{1,0:T(8,128)(2,1)S(1)} %collective-permute-done.5.refs_4_), channel_id=1, source_target_pairs={{0,2},{1,3},{2,0},{3,1},{4,6},{5,7},{6,4},{7,5},{8,10},{9,11},{10,... | collective-permute-start | bytes 1093640 | tf_op jit(solution)/shard_map/ppermute | solution.py:227
  34.2 2.5 %collective-permute-start.11 = (bf16[1424,128]{1,0:T(8,128)(2,1)S(1)}, bf16[1424,128]{1,0:T(8,128)(2,1)S(1)}, u32[]{:S(2)}, u32[]{:S(2)}) collective-permute-start(bf16[1424,128]{1,0:T(8,128)(2,1)S(1)} %collective-permute-done.6.refs_5_), channel_id=1, source_target_pairs={{0,2},{1,3},{2,0},{3,1},{4,6},{5,7},{6,4},{7,5},{8,10},{9,11},{10,... | collective-permute-start | bytes 1093640 | tf_op jit(solution)/shard_map/ppermute | solution.py:227
  34.7 2.5 %collective-permute-start.9 = (bf16[1424,128]{1,0:T(8,128)(2,1)S(1)}, bf16[1424,128]{1,0:T(8,128)(2,1)S(1)}, u32[]{:S(2)}, u32[]{:S(2)}) collective-permute-start(bf16[1424,128]{1,0:T(8,128)(2,1)S(1)} %collective-permute-done.4.refs_3_), channel_id=1, source_target_pairs={{0,2},{1,3},{2,0},{3,1},{4,6},{5,7},{6,4},{7,5},{8,10},{9,11},{10,... | collective-permute-start | bytes 1093640 | tf_op jit(solution)/shard_map/ppermute | solution.py:227

commit v19 on v18

--- a/solution.py
+++ b/solution.py
@@ -18,28 +18,18 @@
     return bits[core:] + bits[:core]
 
 
-def pack_kernel(cols, p_ids, q_ids, p_ref, q_ref, own_ref, *rest):
-    out_refs, strips = rest[:4], rest[4]
+def pack_kernel(cols, p_ids, q_ids, p_ref, q_ref, *rest):
+    out_refs, (strips, ids, sems) = rest[:-3], rest[-3:]
     blocks, per_q, extent, _ = q_ref.shape
     per_p = p_ids.shape[0]
     strip = extent // SEATS
     rows = per_q * strip
-    lane = lax.broadcasted_iota(jnp.int32, (2 * SUB, extent), 1)
-    ids = jnp.zeros((2 * SUB, extent), jnp.int32)
-    for f in range(blocks):
-        for k in range(per_p + per_q):
-            value = p_ids[k, f] if k < per_p else q_ids[f, k - per_p]
-            ids = jnp.where(lane == f * (per_p + per_q) + k, value, ids)
-    ids = ids.astype(p_ref.dtype)
-    for f in range(blocks):
-        flipped = [q_ref[f, k].astype(jnp.float32).T for k in range(per_q)]
-        for j in range(SEATS):
-            pieces = [tile[j * strip:(j + 1) * strip] for tile in flipped]
-            strips[j, f * rows:(f + 1) * rows] = jnp.concatenate(pieces, axis=0).astype(strips.dtype)
+    height, tiles = blocks * rows, p_ref.shape[0]
     here = lax.axis_index(("pair", "core", "col"))
     core = lax.axis_index("core")
     paths = [[()], [(0,), (0, 1)], [(1,), (1, 2)], [(2,), (2, 0)], [(0, 1, 2)]]
-    for path, out_ref in zip(paths, (own_ref, *out_refs)):
+    copies, later = [], []
+    for path, out_ref in zip(paths, out_refs):
         spots = []
         for steps in path:
             masks = [sum(axes(c, cols)[step] for step in steps) for c in range(2)]
@@ -47,17 +37,37 @@
             spots += [to, to ^ cols]
         place = 0
         for to in spots[:-2]:
-            out_ref[place:place + blocks * rows] = strips[to]
-            place += blocks * rows
-        for f in range(blocks):
-            for k in range(per_p):
-                out_ref[place:place + extent] = p_ref[f, k]
-                place += extent
-        out_ref[place:place + 2 * SUB] = ids
+            later.append((strips.at[to], out_ref.at[place:place + height]))
+            place += height
+        copies.append((p_ref, out_ref.at[place:place + tiles]))
+        place += tiles
+        later.append((ids, out_ref.at[place:place + 2 * SUB]))
         place += 2 * SUB
         for to in (spots[-1], spots[-2]):
-            out_ref[place:place + blocks * rows] = strips[to]
-            place += blocks * rows
+            later.append((strips.at[to], out_ref.at[place:place + height]))
+            place += height
+    copies = [
+        pltpu.make_async_copy(source, target, sems.at[n])
+        for n, (source, target) in enumerate(copies + later)
+    ]
+    for copy in copies[:len(paths)]:
+        copy.start()
+    lane = lax.broadcasted_iota(jnp.int32, ids.shape, 1)
+    words = jnp.zeros(ids.shape, jnp.int32)
+    for f in range(blocks):
+        for k in range(per_p + per_q):
+            value = p_ids[k, f] if k < per_p else q_ids[f, k - per_p]
+            words = jnp.where(lane == f * (per_p + per_q) + k, value, words)
+    ids[...] = words.astype(ids.dtype)
+    for f in range(blocks):
+        flipped = [q_ref[f, k].astype(jnp.float32).T for k in range(per_q)]
+        for j in range(SEATS):
+            pieces = [tile[j * strip:(j + 1) * strip] for tile in flipped]
+            strips[j, f * rows:(f + 1) * rows] = jnp.concatenate(pieces, axis=0).astype(strips.dtype)
+    for copy in copies[len(paths):]:
+        copy.start()
+    for copy in copies:
+        copy.wait()
 
 
 def rest_kernel(skip, in_ref, out_ref, sem):
@@ -214,10 +224,15 @@
             for passed in (0, 1, 1, 1, 0)
         ],
         in_specs=[pl.BlockSpec(memory_space=pltpu.SMEM)] * 2
-        + [pl.BlockSpec(memory_space=pltpu.VMEM)] * 2,
-        scratch_shapes=[pltpu.VMEM((SEATS, strips // 2, extent), p_tiles.dtype)],
+        + [pl.BlockSpec(memory_space=pl.ANY), pl.BlockSpec(memory_space=pltpu.VMEM)],
+        out_specs=[pl.BlockSpec(memory_space=pl.ANY)] * 5,
+        scratch_shapes=[
+            pltpu.VMEM((SEATS, strips // 2, extent), p_tiles.dtype),
+            pltpu.VMEM((2 * SUB, extent), p_tiles.dtype),
+            pltpu.SemaphoreType.DMA((26,)),
+        ],
         name="pack",
-    )(p_cols.T, q_cols, p_tiles, q_tiles)
+    )(p_cols.T, q_cols, p_tiles.reshape(-1, extent), q_tiles)
 
     def along(values, step):
         hops = [(s, s ^ axes(s // cols % 2, cols)[step]) for s in range(SEATS)]

time: 64.9 us -> 104 us (1.60)
  Pallas kernels: 8.95 us -> 48.2 us
    pallas_call x1, Pallas kernels: 2.93 us -> 42.2 us  [body(): pl.pallas_call(functools.partial(pack_kernel, cols), out_shape=[jax.Shape...]
  transfers between devices with their start and end apart: 15 -> 15, of which waited for: 6 -> 6; matrix products, arithmetic and copies ran while one was open for 0% -> 0% of each run, Pallas kernels for 5% -> 3%
where the time goes in v19:
time: 104 us
  Pallas kernels  48.2 us (46%)
  blocking collectives  24.5 us (24%)
  starting transfers between devices  22.9 us (22%)
  waiting for transfers between devices  8.36 us (8%)
    pallas_call x1, Pallas kernels, body(): pl.pallas_call(functools.partial(pack_kernel, cols), out_shape=[jax.Shape...  42.2 us
    all_to_all x1, blocking collectives, body(): lax.all_to_all(coded, every, split_axis=0, concat_axis=0, tiled=True)  24.5 us
    ppermute x8, starting transfers between devices, across(): return lax.ppermute(values, seat, [(s, s ^ cols) for s in range(SEATS)])  13.2 us
    ppermute x6, starting transfers between devices, along(): return lax.ppermute(values, seat, hops)  9.76 us
    ppermute x6, waiting for transfers between devices, along(): return lax.ppermute(values, seat, hops)  7.2 us
    pallas_call x3, Pallas kernels, add_products(): pl.pallas_call(functools.partial(product_kernel, sizes, tile_count, passe...  4.29 us
  transfers between devices with their start and end apart: 15, of which 6 were waited for; matrix products, arithmetic and copies ran while one was open for 0% of the time, Pallas kernels for 3%

profile of v19, /device:TPU:1, one launch (start us, length us, event | category | flops | bytes accessed | tf_op | source)
XLA Modules:
  0.0 104.1 jit_solution(7794840871095328961)
XLA Ops:
  0.0 42.2 %pack.1 = (bf16[1424,128]{1,0:T(8,128)(2,1)}, bf16[1808,128]{1,0:T(8,128)(2,1)}, bf16[1808,128]{1,0:T(8,128)(2,1)}, bf16[1808,128]{1,0:T(8,128)(2,1)}, bf16[1424,128]{1,0:T(8,128)(2,1)}) custom-call(s32[2,4]{1,0:T(2,128)} %bitcast.5, s32[4,6]{1,0:T(4,128)} %q_ids.1, bf16[1024,128]{1,0:T(8,128)(2,1)} %bitcast.4, bf16[4,6,128,128]{3,2,1,0:T(8,128)(2,1)} %q_ref.1), custom_call_target="tpu_custom_call" | custom-call | tf_op jit(solution)/shard_map/pack/pallas_call | solution.py:220
  42.2 2.1 %collective-permute-start.3 = (bf16[1808,128]{1,0:T(8,128)(2,1)}, bf16[1808,128]{1,0:T(8,128)(2,1)S(1)}, u32[]{:S(2)}, u32[]{:S(2)}) collective-permute-start(bf16[1808,128]{1,0:T(8,128)(2,1)} %get-tuple-element.17), channel_id=1, source_target_pairs={{0,1},{1,0},{2,6},{3,7},{4,5},{5,4},{6,2},{7,3},{8,9},{9,8},{10,14... | collective-permute-start | bytes 1388552 | tf_op jit(solution)/shard_map/ppermute | solution.py:239
  44.3 1.3 %collective-permute-start = (bf16[1808,128]{1,0:T(8,128)(2,1)}, bf16[1808,128]{1,0:T(8,128)(2,1)S(1)}, u32[]{:S(2)}, u32[]{:S(2)}) collective-permute-start(bf16[1808,128]{1,0:T(8,128)(2,1)} %get-tuple-element.15), channel_id=1, source_target_pairs={{0,4},{1,5},{2,10},{3,11},{4,0},{5,1},{6,14},{7,15},{8,12},{9,13},... | collective-permute-start | bytes 1388552 | tf_op jit(solution)/shard_map/ppermute | solution.py:239
  45.6 1.2 %collective-permute-start.2 = (bf16[1808,128]{1,0:T(8,128)(2,1)}, bf16[1808,128]{1,0:T(8,128)(2,1)S(1)}, u32[]{:S(2)}, u32[]{:S(2)}) collective-permute-start(bf16[1808,128]{1,0:T(8,128)(2,1)} %get-tuple-element.16), channel_id=1, source_target_pairs={{0,8},{1,9},{2,3},{3,2},{4,12},{5,13},{6,7},{7,6},{8,0},{9,1},{10,... | collective-permute-start | bytes 1388552 | tf_op jit(solution)/shard_map/ppermute | solution.py:239
  46.9 1.5 %collective-permute-start.7 = (bf16[1424,128]{1,0:T(8,128)(2,1)}, bf16[1424,128]{1,0:T(8,128)(2,1)S(1)}, u32[]{:S(2)}, u32[]{:S(2)}) collective-permute-start(bf16[1424,128]{1,0:T(8,128)(2,1)} %get-tuple-element.18.refs_0_), channel_id=1, source_target_pairs={{0,2},{1,3},{2,0},{3,1},{4,6},{5,7},{6,4},{7,5},{8,10},{9,11},{10,... | collective-permute-start | bytes 1093640 | tf_op jit(solution)/shard_map/ppermute | solution.py:242
  48.4 0.0 collective-permute-start.12
  48.4 4.3 %collective-permute-done.3.in_ref.refs_2_ = bf16[1808,128]{1,0:T(8,128)(2,1)S(1)} collective-permute-done((bf16[1808,128]{1,0:T(8,128)(2,1)}, bf16[1808,128]{1,0:T(8,128)(2,1)S(1)}, u32[]{:S(2)}, u32[]{:S(2)}) %collective-permute-start.3) | collective-permute-done | bytes 462880 | tf_op jit(solution)/shard_map/ppermute | solution.py:239
  52.7 0.2 rest_of_packet.3
  52.9 1.9 %collective-permute-start.4 = (bf16[1424,128]{1,0:T(8,128)(2,1)S(1)}, bf16[1424,128]{1,0:T(8,128)(2,1)S(1)}, u32[]{:S(2)}, u32[]{:S(2)}) collective-permute-start(bf16[1424,128]{1,0:T(8,128)(2,1)S(1)} %rest_of_packet.3), channel_id=1, source_target_pairs={{0,4},{1,5},{2,10},{3,11},{4,0},{5,1},{6,14},{7,15},{8,12},{9,13},... | collective-permute-start | bytes 1093640 | tf_op jit(solution)/shard_map/ppermute | solution.py:239
  54.8 0.0 collective-permute-done.in_ref.refs_3_
  54.8 0.2 rest_of_packet.4
  54.9 0.0 copy-start
  54.9 2.3 %collective-permute-start.5 = (bf16[1424,128]{1,0:T(8,128)(2,1)S(1)}, bf16[1424,128]{1,0:T(8,128)(2,1)S(1)}, u32[]{:S(2)}, u32[]{:S(2)}) collective-permute-start(bf16[1424,128]{1,0:T(8,128)(2,1)S(1)} %rest_of_packet.4), channel_id=1, source_target_pairs={{0,8},{1,9},{2,3},{3,2},{4,12},{5,13},{6,7},{7,6},{8,0},{9,1},{10,... | collective-permute-start | bytes 1093640 | tf_op jit(solution)/shard_map/ppermute | solution.py:239
  57.3 2.2 %collective-permute-done.2.in_ref.refs_4_ = bf16[1808,128]{1,0:T(8,128)(2,1)S(1)} collective-permute-done((bf16[1808,128]{1,0:T(8,128)(2,1)}, bf16[1808,128]{1,0:T(8,128)(2,1)S(1)}, u32[]{:S(2)}, u32[]{:S(2)}) %collective-permute-start.2) | collective-permute-done | bytes 462880 | tf_op jit(solution)/shard_map/ppermute | solution.py:239
  59.4 0.2 rest_of_packet.5
  59.6 0.9 collective-permute-start.6
  60.5 0.0 collective-permute-done.7.refs_1_
  60.5 4.8 %collective-permute-start.14 = (bf16[1808,128]{1,0:T(8,128)(2,1)S(1)}, bf16[1808,128]{1,0:T(8,128)(2,1)S(1)}, u32[]{:S(2)}, u32[]{:S(2)}) collective-permute-start(bf16[1808,128]{1,0:T(8,128)(2,1)S(1)} %collective-permute-done.3.in_ref.refs_2_), channel_id=1, source_target_pairs={{0,2},{1,3},{2,0},{3,1},{4,6},{5,7},{6,4},{7,5},{8,10},{9,11},{10,... | collective-permute-start | bytes 1388552 | tf_op jit(solution)/shard_map/ppermute | solution.py:242
  65.3 0.0 collective-permute-done.12.refs_0_
  65.3 2.5 %collective-permute-start.13 = (bf16[1424,128]{1,0:T(8,128)(2,1)S(1)}, bf16[1424,128]{1,0:T(8,128)(2,1)S(1)}, u32[]{:S(2)}, u32[]{:S(2)}) collective-permute-start(bf16[1424,128]{1,0:T(8,128)(2,1)S(1)} %collective-permute-done.12.refs_0_), channel_id=1, source_target_pairs={{0,2},{1,3},{2,0},{3,1},{4,6},{5,7},{6,4},{7,5},{8,10},{9,11},{10,... | collective-permute-start | bytes 1093640 | tf_op jit(solution)/shard_map/ppermute | solution.py:242
  67.9 0.0 copy-done
  67.9 1.2 %products.3.refs_6_ = f32[256,8,128]{2,1,0:T(8,128)S(1)} custom-call(bf16[1424,128]{1,0:T(8,128)(2,1)S(1)} %copy-done, bf16[1424,128]{1,0:T(8,128)(2,1)S(1)} %collective-permute-done.7.refs_1_, bf16[1808,128]{1,0:T(8,128)(2,1)S(1)} %collective-permute-done.3.in_ref.refs_2_, bf16[1808,128]{1,0:T(8,128)(2,1)S(1)} %collective-permute-done.in_ref.refs_3_, ...), custom_call_target="tpu_custom_call" | custom-call | flops 62914560 | bytes 5242880 | tf_op jit(solution)/shard_map/products/pallas_call | solution.py:169
  69.1 0.7 collective-permute-done.4.refs_3_
  69.8 2.8 %collective-permute-start.1 = (bf16[1808,128]{1,0:T(8,128)(2,1)S(1)}, bf16[1808,128]{1,0:T(8,128)(2,1)S(1)}, u32[]{:S(2)}, u32[]{:S(2)}) collective-permute-start(bf16[1808,128]{1,0:T(8,128)(2,1)S(1)} %collective-permute-done.in_ref.refs_3_), channel_id=1, source_target_pairs={{0,2},{1,3},{2,0},{3,1},{4,6},{5,7},{6,4},{7,5},{8,10},{9,11},{10,... | collective-permute-start | bytes 1388552 | tf_op jit(solution)/shard_map/ppermute | solution.py:242
  72.6 0.0 collective-permute-done.5.refs_4_
  72.6 0.0 collective-permute-done.6.refs_5_
  72.6 0.9 collective-permute-start.8
  73.5 0.0 collective-permute-start.10
  73.5 0.0 collective-permute-done.13.refs_1_
  73.5 0.5 collective-permute-start.11
  74.1 0.0 collective-permute-done.14.refs_2_
  74.1 0.1 collective-permute-start.9
  74.1 1.3 %products.4.refs_5_ = f32[256,8,128]{2,1,0:T(8,128)S(1)} custom-call(bf16[1424,128]{1,0:T(8,128)(2,1)S(1)} %collective-permute-done.12.refs_0_, bf16[1424,128]{1,0:T(8,128)(2,1)S(1)} %collective-permute-done.13.refs_1_, bf16[1808,128]{1,0:T(8,128)(2,1)S(1)} %collective-permute-done.14.refs_2_, ...), custom_call_target="tpu_custom_call", output_to_operand_aliasing={{}: (6, {})} | custom-call | flops 75497472 | bytes 6291456 | tf_op jit(solution)/shard_map/products/pallas_call | solution.py:169
  75.4 0.0 collective-permute-done.1.refs_0_
  75.4 0.1 collective-permute-done.10.refs_3_
  75.5 0.5 collective-permute-done.11.refs_4_
  76.0 0.5 collective-permute-done.9.refs_2_
  76.6 0.0 collective-permute-done.8.refs_1_
  76.6 1.8 %products.5 = s32[32,5,8,128]{3,2,1,0:T(8,128)S(1)} custom-call(bf16[1808,128]{1,0:T(8,128)(2,1)S(1)} %collective-permute-done.1.refs_0_, bf16[1808,128]{1,0:T(8,128)(2,1)S(1)} %collective-permute-done.8.refs_1_, bf16[1424,128]{1,0:T(8,128)(2,1)S(1)} %collective-permute-done.9.refs_2_, bf16[1424,128]{1,0:T(8,128)(2,1)S(1)} %collective-permute-done.10.refs_3_, ...), custom_call_target="tpu_custom_call" | custom-call | flops 62914560 | bytes 5242880 | tf_op jit(solution)/shard_map/products/pallas_call | solution.py:169
  78.3 24.5 %all_to_all.5 = s32[32,5,8,128]{3,2,1,0:T(8,128)S(1)} all-to-all(s32[32,5,8,128]{3,2,1,0:T(8,128)S(1)} %products.5), channel_id=1, replica_groups=mesh['plane'=2,'pair'=4,'core'=2,'col'=2] {'plane','pair','core','col'}, dimensions={0} | all-to-all | bytes 1310720 | tf_op jit(solution)/shard_map/all_to_all | solution.py:266
  102.8 1.3 %turn.1 = f32[128,1024]{1,0:T(8,128)} custom-call(s32[2,16,5,8,128]{4,3,2,1,0:T(8,128)S(1)} %bitcast.3), custom_call_target="tpu_custom_call" | custom-call | tf_op jit(solution)/shard_map/turn/pallas_call | solution.py:267
Async XLA Ops:
  42.2 10.5 %collective-permute-start.3 = (bf16[1808,128]{1,0:T(8,128)(2,1)}, bf16[1808,128]{1,0:T(8,128)(2,1)S(1)}, u32[]{:S(2)}, u32[]{:S(2)}) collective-permute-start(bf16[1808,128]{1,0:T(8,128)(2,1)} %get-tuple-element.17), channel_id=1, source_target_pairs={{0,1},{1,0},{2,6},{3,7},{4,5},{5,4},{6,2},{7,3},{8,9},{9,8},{10,14... | collective-permute-start | bytes 1388552 | tf_op jit(solution)/shard_map/ppermute | solution.py:239
  44.3 10.4 %collective-permute-start = (bf16[1808,128]{1,0:T(8,128)(2,1)}, bf16[1808,128]{1,0:T(8,128)(2,1)S(1)}, u32[]{:S(2)}, u32[]{:S(2)}) collective-permute-start(bf16[1808,128]{1,0:T(8,128)(2,1)} %get-tuple-element.15), channel_id=1, source_target_pairs={{0,4},{1,5},{2,10},{3,11},{4,0},{5,1},{6,14},{7,15},{8,12},{9,13},... | collective-permute-start | bytes 1388552 | tf_op jit(solution)/shard_map/ppermute | solution.py:239
  45.6 13.8 %collective-permute-start.2 = (bf16[1808,128]{1,0:T(8,128)(2,1)}, bf16[1808,128]{1,0:T(8,128)(2,1)S(1)}, u32[]{:S(2)}, u32[]{:S(2)}) collective-permute-start(bf16[1808,128]{1,0:T(8,128)(2,1)} %get-tuple-element.16), channel_id=1, source_target_pairs={{0,8},{1,9},{2,3},{3,2},{4,12},{5,13},{6,7},{7,6},{8,0},{9,1},{10,... | collective-permute-start | bytes 1388552 | tf_op jit(solution)/shard_map/ppermute | solution.py:239
  46.9 13.7 %collective-permute-start.7 = (bf16[1424,128]{1,0:T(8,128)(2,1)}, bf16[1424,128]{1,0:T(8,128)(2,1)S(1)}, u32[]{:S(2)}, u32[]{:S(2)}) collective-permute-start(bf16[1424,128]{1,0:T(8,128)(2,1)} %get-tuple-element.18.refs_0_), channel_id=1, source_target_pairs={{0,2},{1,3},{2,0},{3,1},{4,6},{5,7},{6,4},{7,5},{8,10},{9,11},{10,... | collective-permute-start | bytes 1093640 | tf_op jit(solution)/shard_map/ppermute | solution.py:242
  48.4 16.9 %collective-permute-start.12 = (bf16[1424,128]{1,0:T(8,128)(2,1)}, bf16[1424,128]{1,0:T(8,128)(2,1)S(1)}, u32[]{:S(2)}, u32[]{:S(2)}) collective-permute-start(bf16[1424,128]{1,0:T(8,128)(2,1)} %get-tuple-element.23), channel_id=1, source_target_pairs={{0,13},{1,12},{2,15},{3,14},{4,9},{5,8},{6,11},{7,10},{8,5},{9,4},... | collective-permute-start | bytes 1093640 | tf_op jit(solution)/shard_map/ppermute | solution.py:249
  52.9 16.9 %collective-permute-start.4 = (bf16[1424,128]{1,0:T(8,128)(2,1)S(1)}, bf16[1424,128]{1,0:T(8,128)(2,1)S(1)}, u32[]{:S(2)}, u32[]{:S(2)}) collective-permute-start(bf16[1424,128]{1,0:T(8,128)(2,1)S(1)} %rest_of_packet.3), channel_id=1, source_target_pairs={{0,4},{1,5},{2,10},{3,11},{4,0},{5,1},{6,14},{7,15},{8,12},{9,13},... | collective-permute-start | bytes 1093640 | tf_op jit(solution)/shard_map/ppermute | solution.py:239
  54.9 12.9 %copy-start = (bf16[1424,128]{1,0:T(8,128)(2,1)S(1)}, bf16[1424,128]{1,0:T(8,128)(2,1)}, u32[]{:S(2)}) copy-start(bf16[1424,128]{1,0:T(8,128)(2,1)} %get-tuple-element.18.refs_0_) | copy-start | bytes 1093636
  54.9 17.7 %collective-permute-start.5 = (bf16[1424,128]{1,0:T(8,128)(2,1)S(1)}, bf16[1424,128]{1,0:T(8,128)(2,1)S(1)}, u32[]{:S(2)}, u32[]{:S(2)}) collective-permute-start(bf16[1424,128]{1,0:T(8,128)(2,1)S(1)} %rest_of_packet.4), channel_id=1, source_target_pairs={{0,8},{1,9},{2,3},{3,2},{4,12},{5,13},{6,7},{7,6},{8,0},{9,1},{10,... | collective-permute-start | bytes 1093640 | tf_op jit(solution)/shard_map/ppermute | solution.py:239
  59.6 13.0 %collective-permute-start.6 = (bf16[1424,128]{1,0:T(8,128)(2,1)S(1)}, bf16[1424,128]{1,0:T(8,128)(2,1)S(1)}, u32[]{:S(2)}, u32[]{:S(2)}) collective-permute-start(bf16[1424,128]{1,0:T(8,128)(2,1)S(1)} %rest_of_packet.5), channel_id=1, source_target_pairs={{0,1},{1,0},{2,6},{3,7},{4,5},{5,4},{6,2},{7,3},{8,9},{9,8},{10,14... | collective-permute-start | bytes 1093640 | tf_op jit(solution)/shard_map/ppermute | solution.py:239
  60.5 13.5 %collective-permute-start.14 = (bf16[1808,128]{1,0:T(8,128)(2,1)S(1)}, bf16[1808,128]{1,0:T(8,128)(2,1)S(1)}, u32[]{:S(2)}, u32[]{:S(2)}) collective-permute-start(bf16[1808,128]{1,0:T(8,128)(2,1)S(1)} %collective-permute-done.3.in_ref.refs_2_), channel_id=1, source_target_pairs={{0,2},{1,3},{2,0},{3,1},{4,6},{5,7},{6,4},{7,5},{8,10},{9,11},{10,... | collective-permute-start | bytes 1388552 | tf_op jit(solution)/shard_map/ppermute | solution.py:242
  65.3 8.2 %collective-permute-start.13 = (bf16[1424,128]{1,0:T(8,128)(2,1)S(1)}, bf16[1424,128]{1,0:T(8,128)(2,1)S(1)}, u32[]{:S(2)}, u32[]{:S(2)}) collective-permute-start(bf16[1424,128]{1,0:T(8,128)(2,1)S(1)} %collective-permute-done.12.refs_0_), channel_id=1, source_target_pairs={{0,2},{1,3},{2,0},{3,1},{4,6},{5,7},{6,4},{7,5},{8,10},{9,11},{10,... | collective-permute-start | bytes 1093640 | tf_op jit(solution)/shard_map/ppermute | solution.py:242
  69.8 5.6 %collective-permute-start.1 = (bf16[1808,128]{1,0:T(8,128)(2,1)S(1)}, bf16[1808,128]{1,0:T(8,128)(2,1)S(1)}, u32[]{:S(2)}, u32[]{:S(2)}) collective-permute-start(bf16[1808,128]{1,0:T(8,128)(2,1)S(1)} %collective-permute-done.in_ref.refs_3_), channel_id=1, source_target_pairs={{0,2},{1,3},{2,0},{3,1},{4,6},{5,7},{6,4},{7,5},{8,10},{9,11},{10,... | collective-permute-start | bytes 1388552 | tf_op jit(solution)/shard_map/ppermute | solution.py:242
  72.6 3.9 %collective-permute-start.8 = (bf16[1808,128]{1,0:T(8,128)(2,1)S(1)}, bf16[1808,128]{1,0:T(8,128)(2,1)S(1)}, u32[]{:S(2)}, u32[]{:S(2)}) collective-permute-start(bf16[1808,128]{1,0:T(8,128)(2,1)S(1)} %collective-permute-done.2.in_ref.refs_4_), channel_id=1, source_target_pairs={{0,2},{1,3},{2,0},{3,1},{4,6},{5,7},{6,4},{7,5},{8,10},{9,11},{10,... | collective-permute-start | bytes 1388552 | tf_op jit(solution)/shard_map/ppermute | solution.py:242
  73.5 2.0 %collective-permute-start.10 = (bf16[1424,128]{1,0:T(8,128)(2,1)S(1)}, bf16[1424,128]{1,0:T(8,128)(2,1)S(1)}, u32[]{:S(2)}, u32[]{:S(2)}) collective-permute-start(bf16[1424,128]{1,0:T(8,128)(2,1)S(1)} %collective-permute-done.5.refs_4_), channel_id=1, source_target_pairs={{0,2},{1,3},{2,0},{3,1},{4,6},{5,7},{6,4},{7,5},{8,10},{9,11},{10,... | collective-permute-start | bytes 1093640 | tf_op jit(solution)/shard_map/ppermute | solution.py:242
  73.5 2.5 %collective-permute-start.11 = (bf16[1424,128]{1,0:T(8,128)(2,1)S(1)}, bf16[1424,128]{1,0:T(8,128)(2,1)S(1)}, u32[]{:S(2)}, u32[]{:S(2)}) collective-permute-start(bf16[1424,128]{1,0:T(8,128)(2,1)S(1)} %collective-permute-done.6.refs_5_), channel_id=1, source_target_pairs={{0,2},{1,3},{2,0},{3,1},{4,6},{5,7},{6,4},{7,5},{8,10},{9,11},{10,... | collective-permute-start | bytes 1093640 | tf_op jit(solution)/shard_map/ppermute | solution.py:242
  74.1 2.5 %collective-permute-start.9 = (bf16[1424,128]{1,0:T(8,128)(2,1)S(1)}, bf16[1424,128]{1,0:T(8,128)(2,1)S(1)}, u32[]{:S(2)}, u32[]{:S(2)}) collective-permute-start(bf16[1424,128]{1,0:T(8,128)(2,1)S(1)} %collective-permute-done.4.refs_3_), channel_id=1, source_target_pairs={{0,2},{1,3},{2,0},{3,1},{4,6},{5,7},{6,4},{7,5},{8,10},{9,11},{10,... | collective-permute-start | bytes 1093640 | tf_op jit(solution)/shard_map/ppermute | solution.py:242

commit v20 on v19

--- a/solution.py
+++ b/solution.py
@@ -224,7 +224,7 @@
             for passed in (0, 1, 1, 1, 0)
         ],
         in_specs=[pl.BlockSpec(memory_space=pltpu.SMEM)] * 2
-        + [pl.BlockSpec(memory_space=pl.ANY), pl.BlockSpec(memory_space=pltpu.VMEM)],
+        + [pl.BlockSpec(memory_space=pltpu.VMEM)] * 2,
         out_specs=[pl.BlockSpec(memory_space=pl.ANY)] * 5,
         scratch_shapes=[
             pltpu.VMEM((SEATS, strips // 2, extent), p_tiles.dtype),

time: 104 us -> 64.8 us (0.62)
  Pallas kernels: 48.2 us -> 8.8 us
    pallas_call x1, Pallas kernels: 42.2 us -> 2.77 us  [body(): pl.pallas_call(functools.partial(pack_kernel, cols), out_shape=[jax.Shape...]
  transfers between devices with their start and end apart: 15 -> 15, of which waited for: 6 -> 6; matrix products, arithmetic and copies ran while one was open for 0% -> 0% of each run, Pallas kernels for 3% -> 5%
where the time goes in v20:
time: 64.8 us; the launch traced here: 64.6 us
  blocking collectives  24.5 us (38%)
  starting transfers between devices  22.9 us (35%)
  Pallas kernels  8.8 us (14%)
  waiting for transfers between devices  8.36 us (13%)
    all_to_all x1, blocking collectives, body(): lax.all_to_all(coded, every, split_axis=0, concat_axis=0, tiled=True)  24.5 us
    ppermute x8, starting transfers between devices, across(): return lax.ppermute(values, seat, [(s, s ^ cols) for s in range(SEATS)])  13.2 us
    ppermute x6, starting transfers between devices, along(): return lax.ppermute(values, seat, hops)  9.76 us
    ppermute x6, waiting for transfers between devices, along(): return lax.ppermute(values, seat, hops)  7.2 us
    pallas_call x3, Pallas kernels, add_products(): pl.pallas_call(functools.partial(product_kernel, sizes, tile_count, passe...  4.29 us
    pallas_call x1, Pallas kernels, body(): pl.pallas_call(functools.partial(pack_kernel, cols), out_shape=[jax.Shape...  2.77 us
  transfers between devices with their start and end apart: 15, of which 6 were waited for; matrix products, arithmetic and copies ran while one was open for 0% of the time, Pallas kernels for 5%

profile of v20, /device:TPU:1, one launch (start us, length us, event | category | flops | bytes accessed | tf_op | source)
XLA Modules:
  0.0 64.6 jit_solution(16888916811410950435)
XLA Ops:
  0.0 2.8 %pack.1 = (bf16[1424,128]{1,0:T(8,128)(2,1)}, bf16[1808,128]{1,0:T(8,128)(2,1)}, bf16[1808,128]{1,0:T(8,128)(2,1)}, bf16[1808,128]{1,0:T(8,128)(2,1)}, bf16[1424,128]{1,0:T(8,128)(2,1)}) custom-call(s32[2,4]{1,0:T(2,128)} %bitcast.5, s32[4,6]{1,0:T(4,128)} %q_ids.1, bf16[1024,128]{1,0:T(8,128)(2,1)} %bitcast.4, bf16[4,6,128,128]{3,2,1,0:T(8,128)(2,1)} %q_ref.1), custom_call_target="tpu_custom_call" | custom-call | tf_op jit(solution)/shard_map/pack/pallas_call | solution.py:220
  2.8 2.1 %collective-permute-start.3 = (bf16[1808,128]{1,0:T(8,128)(2,1)}, bf16[1808,128]{1,0:T(8,128)(2,1)S(1)}, u32[]{:S(2)}, u32[]{:S(2)}) collective-permute-start(bf16[1808,128]{1,0:T(8,128)(2,1)} %get-tuple-element.17), channel_id=1, source_target_pairs={{0,1},{1,0},{2,6},{3,7},{4,5},{5,4},{6,2},{7,3},{8,9},{9,8},{10,14... | collective-permute-start | bytes 1388552 | tf_op jit(solution)/shard_map/ppermute | solution.py:239
  4.9 1.3 %collective-permute-start = (bf16[1808,128]{1,0:T(8,128)(2,1)}, bf16[1808,128]{1,0:T(8,128)(2,1)S(1)}, u32[]{:S(2)}, u32[]{:S(2)}) collective-permute-start(bf16[1808,128]{1,0:T(8,128)(2,1)} %get-tuple-element.15), channel_id=1, source_target_pairs={{0,4},{1,5},{2,10},{3,11},{4,0},{5,1},{6,14},{7,15},{8,12},{9,13},... | collective-permute-start | bytes 1388552 | tf_op jit(solution)/shard_map/ppermute | solution.py:239
  6.2 1.2 %collective-permute-start.2 = (bf16[1808,128]{1,0:T(8,128)(2,1)}, bf16[1808,128]{1,0:T(8,128)(2,1)S(1)}, u32[]{:S(2)}, u32[]{:S(2)}) collective-permute-start(bf16[1808,128]{1,0:T(8,128)(2,1)} %get-tuple-element.16), channel_id=1, source_target_pairs={{0,8},{1,9},{2,3},{3,2},{4,12},{5,13},{6,7},{7,6},{8,0},{9,1},{10,... | collective-permute-start | bytes 1388552 | tf_op jit(solution)/shard_map/ppermute | solution.py:239
  7.4 1.5 %collective-permute-start.7 = (bf16[1424,128]{1,0:T(8,128)(2,1)}, bf16[1424,128]{1,0:T(8,128)(2,1)S(1)}, u32[]{:S(2)}, u32[]{:S(2)}) collective-permute-start(bf16[1424,128]{1,0:T(8,128)(2,1)} %get-tuple-element.18.refs_0_), channel_id=1, source_target_pairs={{0,2},{1,3},{2,0},{3,1},{4,6},{5,7},{6,4},{7,5},{8,10},{9,11},{10,... | collective-permute-start | bytes 1093640 | tf_op jit(solution)/shard_map/ppermute | solution.py:242
  8.9 0.0 collective-permute-start.12
  8.9 4.3 %collective-permute-done.3.in_ref.refs_2_ = bf16[1808,128]{1,0:T(8,128)(2,1)S(1)} collective-permute-done((bf16[1808,128]{1,0:T(8,128)(2,1)}, bf16[1808,128]{1,0:T(8,128)(2,1)S(1)}, u32[]{:S(2)}, u32[]{:S(2)}) %collective-permute-start.3) | collective-permute-done | bytes 462880 | tf_op jit(solution)/shard_map/ppermute | solution.py:239
  13.3 0.2 rest_of_packet.3
  13.5 1.9 %collective-permute-start.4 = (bf16[1424,128]{1,0:T(8,128)(2,1)S(1)}, bf16[1424,128]{1,0:T(8,128)(2,1)S(1)}, u32[]{:S(2)}, u32[]{:S(2)}) collective-permute-start(bf16[1424,128]{1,0:T(8,128)(2,1)S(1)} %rest_of_packet.3), channel_id=1, source_target_pairs={{0,4},{1,5},{2,10},{3,11},{4,0},{5,1},{6,14},{7,15},{8,12},{9,13},... | collective-permute-start | bytes 1093640 | tf_op jit(solution)/shard_map/ppermute | solution.py:239
  15.3 0.0 collective-permute-done.in_ref.refs_3_
  15.3 0.2 rest_of_packet.4
  15.5 0.0 copy-start
  15.5 2.3 %collective-permute-start.5 = (bf16[1424,128]{1,0:T(8,128)(2,1)S(1)}, bf16[1424,128]{1,0:T(8,128)(2,1)S(1)}, u32[]{:S(2)}, u32[]{:S(2)}) collective-permute-start(bf16[1424,128]{1,0:T(8,128)(2,1)S(1)} %rest_of_packet.4), channel_id=1, source_target_pairs={{0,8},{1,9},{2,3},{3,2},{4,12},{5,13},{6,7},{7,6},{8,0},{9,1},{10,... | collective-permute-start | bytes 1093640 | tf_op jit(solution)/shard_map/ppermute | solution.py:239
  17.8 2.2 %collective-permute-done.2.in_ref.refs_4_ = bf16[1808,128]{1,0:T(8,128)(2,1)S(1)} collective-permute-done((bf16[1808,128]{1,0:T(8,128)(2,1)}, bf16[1808,128]{1,0:T(8,128)(2,1)S(1)}, u32[]{:S(2)}, u32[]{:S(2)}) %collective-permute-start.2) | collective-permute-done | bytes 462880 | tf_op jit(solution)/shard_map/ppermute | solution.py:239
  20.0 0.2 rest_of_packet.5
  20.2 0.9 %collective-permute-start.6 = (bf16[1424,128]{1,0:T(8,128)(2,1)S(1)}, bf16[1424,128]{1,0:T(8,128)(2,1)S(1)}, u32[]{:S(2)}, u32[]{:S(2)}) collective-permute-start(bf16[1424,128]{1,0:T(8,128)(2,1)S(1)} %rest_of_packet.5), channel_id=1, source_target_pairs={{0,1},{1,0},{2,6},{3,7},{4,5},{5,4},{6,2},{7,3},{8,9},{9,8},{10,14... | collective-permute-start | bytes 1093640 | tf_op jit(solution)/shard_map/ppermute | solution.py:239
  21.1 0.0 collective-permute-done.7.refs_1_
  21.1 4.8 %collective-permute-start.14 = (bf16[1808,128]{1,0:T(8,128)(2,1)S(1)}, bf16[1808,128]{1,0:T(8,128)(2,1)S(1)}, u32[]{:S(2)}, u32[]{:S(2)}) collective-permute-start(bf16[1808,128]{1,0:T(8,128)(2,1)S(1)} %collective-permute-done.3.in_ref.refs_2_), channel_id=1, source_target_pairs={{0,2},{1,3},{2,0},{3,1},{4,6},{5,7},{6,4},{7,5},{8,10},{9,11},{10,... | collective-permute-start | bytes 1388552 | tf_op jit(solution)/shard_map/ppermute | solution.py:242
  25.9 0.0 collective-permute-done.12.refs_0_
  25.9 2.5 %collective-permute-start.13 = (bf16[1424,128]{1,0:T(8,128)(2,1)S(1)}, bf16[1424,128]{1,0:T(8,128)(2,1)S(1)}, u32[]{:S(2)}, u32[]{:S(2)}) collective-permute-start(bf16[1424,128]{1,0:T(8,128)(2,1)S(1)} %collective-permute-done.12.refs_0_), channel_id=1, source_target_pairs={{0,2},{1,3},{2,0},{3,1},{4,6},{5,7},{6,4},{7,5},{8,10},{9,11},{10,... | collective-permute-start | bytes 1093640 | tf_op jit(solution)/shard_map/ppermute | solution.py:242
  28.4 0.0 copy-done
  28.4 1.2 %products.3.refs_6_ = f32[256,8,128]{2,1,0:T(8,128)S(1)} custom-call(bf16[1424,128]{1,0:T(8,128)(2,1)S(1)} %copy-done, bf16[1424,128]{1,0:T(8,128)(2,1)S(1)} %collective-permute-done.7.refs_1_, bf16[1808,128]{1,0:T(8,128)(2,1)S(1)} %collective-permute-done.3.in_ref.refs_2_, bf16[1808,128]{1,0:T(8,128)(2,1)S(1)} %collective-permute-done.in_ref.refs_3_, ...), custom_call_target="tpu_custom_call" | custom-call | flops 62914560 | bytes 5242880 | tf_op jit(solution)/shard_map/products/pallas_call | solution.py:169
  29.7 0.7 %collective-permute-done.4.refs_3_ = bf16[1424,128]{1,0:T(8,128)(2,1)S(1)} collective-permute-done((bf16[1424,128]{1,0:T(8,128)(2,1)S(1)}, bf16[1424,128]{1,0:T(8,128)(2,1)S(1)}, u32[]{:S(2)}, u32[]{:S(2)}) %collective-permute-start.4) | collective-permute-done | bytes 364576 | tf_op jit(solution)/shard_map/ppermute | solution.py:239
  30.3 2.8 %collective-permute-start.1 = (bf16[1808,128]{1,0:T(8,128)(2,1)S(1)}, bf16[1808,128]{1,0:T(8,128)(2,1)S(1)}, u32[]{:S(2)}, u32[]{:S(2)}) collective-permute-start(bf16[1808,128]{1,0:T(8,128)(2,1)S(1)} %collective-permute-done.in_ref.refs_3_), channel_id=1, source_target_pairs={{0,2},{1,3},{2,0},{3,1},{4,6},{5,7},{6,4},{7,5},{8,10},{9,11},{10,... | collective-permute-start | bytes 1388552 | tf_op jit(solution)/shard_map/ppermute | solution.py:242
  33.2 0.0 collective-permute-done.5.refs_4_
  33.2 0.0 collective-permute-done.6.refs_5_
  33.2 0.9 %collective-permute-start.8 = (bf16[1808,128]{1,0:T(8,128)(2,1)S(1)}, bf16[1808,128]{1,0:T(8,128)(2,1)S(1)}, u32[]{:S(2)}, u32[]{:S(2)}) collective-permute-start(bf16[1808,128]{1,0:T(8,128)(2,1)S(1)} %collective-permute-done.2.in_ref.refs_4_), channel_id=1, source_target_pairs={{0,2},{1,3},{2,0},{3,1},{4,6},{5,7},{6,4},{7,5},{8,10},{9,11},{10,... | collective-permute-start | bytes 1388552 | tf_op jit(solution)/shard_map/ppermute | solution.py:242
  34.1 0.0 collective-permute-start.10
  34.1 0.0 collective-permute-done.13.refs_1_
  34.1 0.5 collective-permute-start.11
  34.6 0.0 collective-permute-done.14.refs_2_
  34.6 0.1 collective-permute-start.9
  34.7 1.3 %products.4.refs_5_ = f32[256,8,128]{2,1,0:T(8,128)S(1)} custom-call(bf16[1424,128]{1,0:T(8,128)(2,1)S(1)} %collective-permute-done.12.refs_0_, bf16[1424,128]{1,0:T(8,128)(2,1)S(1)} %collective-permute-done.13.refs_1_, bf16[1808,128]{1,0:T(8,128)(2,1)S(1)} %collective-permute-done.14.refs_2_, ...), custom_call_target="tpu_custom_call", output_to_operand_aliasing={{}: (6, {})} | custom-call | flops 75497472 | bytes 6291456 | tf_op jit(solution)/shard_map/products/pallas_call | solution.py:169
  36.0 0.0 collective-permute-done.1.refs_0_
  36.0 0.1 collective-permute-done.10.refs_3_
  36.1 0.5 collective-permute-done.11.refs_4_
  36.6 0.5 collective-permute-done.9.refs_2_
  37.1 0.0 collective-permute-done.8.refs_1_
  37.1 1.8 %products.5 = s32[32,5,8,128]{3,2,1,0:T(8,128)S(1)} custom-call(bf16[1808,128]{1,0:T(8,128)(2,1)S(1)} %collective-permute-done.1.refs_0_, bf16[1808,128]{1,0:T(8,128)(2,1)S(1)} %collective-permute-done.8.refs_1_, bf16[1424,128]{1,0:T(8,128)(2,1)S(1)} %collective-permute-done.9.refs_2_, bf16[1424,128]{1,0:T(8,128)(2,1)S(1)} %collective-permute-done.10.refs_3_, ...), custom_call_target="tpu_custom_call" | custom-call | flops 62914560 | bytes 5242880 | tf_op jit(solution)/shard_map/products/pallas_call | solution.py:169
  38.9 24.5 %all_to_all.5 = s32[32,5,8,128]{3,2,1,0:T(8,128)S(1)} all-to-all(s32[32,5,8,128]{3,2,1,0:T(8,128)S(1)} %products.5), channel_id=1, replica_groups=mesh['plane'=2,'pair'=4,'core'=2,'col'=2] {'plane','pair','core','col'}, dimensions={0} | all-to-all | bytes 1310720 | tf_op jit(solution)/shard_map/all_to_all | solution.py:266
  63.4 1.3 %turn.1 = f32[128,1024]{1,0:T(8,128)} custom-call(s32[2,16,5,8,128]{4,3,2,1,0:T(8,128)S(1)} %bitcast.3), custom_call_target="tpu_custom_call" | custom-call | tf_op jit(solution)/shard_map/turn/pallas_call | solution.py:267
Async XLA Ops:
  2.8 10.5 %collective-permute-start.3 = (bf16[1808,128]{1,0:T(8,128)(2,1)}, bf16[1808,128]{1,0:T(8,128)(2,1)S(1)}, u32[]{:S(2)}, u32[]{:S(2)}) collective-permute-start(bf16[1808,128]{1,0:T(8,128)(2,1)} %get-tuple-element.17), channel_id=1, source_target_pairs={{0,1},{1,0},{2,6},{3,7},{4,5},{5,4},{6,2},{7,3},{8,9},{9,8},{10,14... | collective-permute-start | bytes 1388552 | tf_op jit(solution)/shard_map/ppermute | solution.py:239
  4.9 10.4 %collective-permute-start = (bf16[1808,128]{1,0:T(8,128)(2,1)}, bf16[1808,128]{1,0:T(8,128)(2,1)S(1)}, u32[]{:S(2)}, u32[]{:S(2)}) collective-permute-start(bf16[1808,128]{1,0:T(8,128)(2,1)} %get-tuple-element.15), channel_id=1, source_target_pairs={{0,4},{1,5},{2,10},{3,11},{4,0},{5,1},{6,14},{7,15},{8,12},{9,13},... | collective-permute-start | bytes 1388552 | tf_op jit(solution)/shard_map/ppermute | solution.py:239
  6.2 13.8 %collective-permute-start.2 = (bf16[1808,128]{1,0:T(8,128)(2,1)}, bf16[1808,128]{1,0:T(8,128)(2,1)S(1)}, u32[]{:S(2)}, u32[]{:S(2)}) collective-permute-start(bf16[1808,128]{1,0:T(8,128)(2,1)} %get-tuple-element.16), channel_id=1, source_target_pairs={{0,8},{1,9},{2,3},{3,2},{4,12},{5,13},{6,7},{7,6},{8,0},{9,1},{10,... | collective-permute-start | bytes 1388552 | tf_op jit(solution)/shard_map/ppermute | solution.py:239
  7.4 13.7 %collective-permute-start.7 = (bf16[1424,128]{1,0:T(8,128)(2,1)}, bf16[1424,128]{1,0:T(8,128)(2,1)S(1)}, u32[]{:S(2)}, u32[]{:S(2)}) collective-permute-start(bf16[1424,128]{1,0:T(8,128)(2,1)} %get-tuple-element.18.refs_0_), channel_id=1, source_target_pairs={{0,2},{1,3},{2,0},{3,1},{4,6},{5,7},{6,4},{7,5},{8,10},{9,11},{10,... | collective-permute-start | bytes 1093640 | tf_op jit(solution)/shard_map/ppermute | solution.py:242
  8.9 16.9 %collective-permute-start.12 = (bf16[1424,128]{1,0:T(8,128)(2,1)}, bf16[1424,128]{1,0:T(8,128)(2,1)S(1)}, u32[]{:S(2)}, u32[]{:S(2)}) collective-permute-start(bf16[1424,128]{1,0:T(8,128)(2,1)} %get-tuple-element.23), channel_id=1, source_target_pairs={{0,13},{1,12},{2,15},{3,14},{4,9},{5,8},{6,11},{7,10},{8,5},{9,4},... | collective-permute-start | bytes 1093640 | tf_op jit(solution)/shard_map/ppermute | solution.py:249
  13.5 16.9 %collective-permute-start.4 = (bf16[1424,128]{1,0:T(8,128)(2,1)S(1)}, bf16[1424,128]{1,0:T(8,128)(2,1)S(1)}, u32[]{:S(2)}, u32[]{:S(2)}) collective-permute-start(bf16[1424,128]{1,0:T(8,128)(2,1)S(1)} %rest_of_packet.3), channel_id=1, source_target_pairs={{0,4},{1,5},{2,10},{3,11},{4,0},{5,1},{6,14},{7,15},{8,12},{9,13},... | collective-permute-start | bytes 1093640 | tf_op jit(solution)/shard_map/ppermute | solution.py:239
  15.5 12.9 %copy-start = (bf16[1424,128]{1,0:T(8,128)(2,1)S(1)}, bf16[1424,128]{1,0:T(8,128)(2,1)}, u32[]{:S(2)}) copy-start(bf16[1424,128]{1,0:T(8,128)(2,1)} %get-tuple-element.18.refs_0_) | copy-start | bytes 1093636
  15.5 17.7 %collective-permute-start.5 = (bf16[1424,128]{1,0:T(8,128)(2,1)S(1)}, bf16[1424,128]{1,0:T(8,128)(2,1)S(1)}, u32[]{:S(2)}, u32[]{:S(2)}) collective-permute-start(bf16[1424,128]{1,0:T(8,128)(2,1)S(1)} %rest_of_packet.4), channel_id=1, source_target_pairs={{0,8},{1,9},{2,3},{3,2},{4,12},{5,13},{6,7},{7,6},{8,0},{9,1},{10,... | collective-permute-start | bytes 1093640 | tf_op jit(solution)/shard_map/ppermute | solution.py:239
  20.2 13.0 %collective-permute-start.6 = (bf16[1424,128]{1,0:T(8,128)(2,1)S(1)}, bf16[1424,128]{1,0:T(8,128)(2,1)S(1)}, u32[]{:S(2)}, u32[]{:S(2)}) collective-permute-start(bf16[1424,128]{1,0:T(8,128)(2,1)S(1)} %rest_of_packet.5), channel_id=1, source_target_pairs={{0,1},{1,0},{2,6},{3,7},{4,5},{5,4},{6,2},{7,3},{8,9},{9,8},{10,14... | collective-permute-start | bytes 1093640 | tf_op jit(solution)/shard_map/ppermute | solution.py:239
  21.1 13.5 %collective-permute-start.14 = (bf16[1808,128]{1,0:T(8,128)(2,1)S(1)}, bf16[1808,128]{1,0:T(8,128)(2,1)S(1)}, u32[]{:S(2)}, u32[]{:S(2)}) collective-permute-start(bf16[1808,128]{1,0:T(8,128)(2,1)S(1)} %collective-permute-done.3.in_ref.refs_2_), channel_id=1, source_target_pairs={{0,2},{1,3},{2,0},{3,1},{4,6},{5,7},{6,4},{7,5},{8,10},{9,11},{10,... | collective-permute-start | bytes 1388552 | tf_op jit(solution)/shard_map/ppermute | solution.py:242
  25.9 8.2 %collective-permute-start.13 = (bf16[1424,128]{1,0:T(8,128)(2,1)S(1)}, bf16[1424,128]{1,0:T(8,128)(2,1)S(1)}, u32[]{:S(2)}, u32[]{:S(2)}) collective-permute-start(bf16[1424,128]{1,0:T(8,128)(2,1)S(1)} %collective-permute-done.12.refs_0_), channel_id=1, source_target_pairs={{0,2},{1,3},{2,0},{3,1},{4,6},{5,7},{6,4},{7,5},{8,10},{9,11},{10,... | collective-permute-start | bytes 1093640 | tf_op jit(solution)/shard_map/ppermute | solution.py:242
  30.3 5.6 %collective-permute-start.1 = (bf16[1808,128]{1,0:T(8,128)(2,1)S(1)}, bf16[1808,128]{1,0:T(8,128)(2,1)S(1)}, u32[]{:S(2)}, u32[]{:S(2)}) collective-permute-start(bf16[1808,128]{1,0:T(8,128)(2,1)S(1)} %collective-permute-done.in_ref.refs_3_), channel_id=1, source_target_pairs={{0,2},{1,3},{2,0},{3,1},{4,6},{5,7},{6,4},{7,5},{8,10},{9,11},{10,... | collective-permute-start | bytes 1388552 | tf_op jit(solution)/shard_map/ppermute | solution.py:242
  33.2 3.9 %collective-permute-start.8 = (bf16[1808,128]{1,0:T(8,128)(2,1)S(1)}, bf16[1808,128]{1,0:T(8,128)(2,1)S(1)}, u32[]{:S(2)}, u32[]{:S(2)}) collective-permute-start(bf16[1808,128]{1,0:T(8,128)(2,1)S(1)} %collective-permute-done.2.in_ref.refs_4_), channel_id=1, source_target_pairs={{0,2},{1,3},{2,0},{3,1},{4,6},{5,7},{6,4},{7,5},{8,10},{9,11},{10,... | collective-permute-start | bytes 1388552 | tf_op jit(solution)/shard_map/ppermute | solution.py:242
  34.1 2.0 %collective-permute-start.10 = (bf16[1424,128]{1,0:T(8,128)(2,1)S(1)}, bf16[1424,128]{1,0:T(8,128)(2,1)S(1)}, u32[]{:S(2)}, u32[]{:S(2)}) collective-permute-start(bf16[1424,128]{1,0:T(8,128)(2,1)S(1)} %collective-permute-done.5.refs_4_), channel_id=1, source_target_pairs={{0,2},{1,3},{2,0},{3,1},{4,6},{5,7},{6,4},{7,5},{8,10},{9,11},{10,... | collective-permute-start | bytes 1093640 | tf_op jit(solution)/shard_map/ppermute | solution.py:242
  34.1 2.5 %collective-permute-start.11 = (bf16[1424,128]{1,0:T(8,128)(2,1)S(1)}, bf16[1424,128]{1,0:T(8,128)(2,1)S(1)}, u32[]{:S(2)}, u32[]{:S(2)}) collective-permute-start(bf16[1424,128]{1,0:T(8,128)(2,1)S(1)} %collective-permute-done.6.refs_5_), channel_id=1, source_target_pairs={{0,2},{1,3},{2,0},{3,1},{4,6},{5,7},{6,4},{7,5},{8,10},{9,11},{10,... | collective-permute-start | bytes 1093640 | tf_op jit(solution)/shard_map/ppermute | solution.py:242
  34.6 2.5 %collective-permute-start.9 = (bf16[1424,128]{1,0:T(8,128)(2,1)S(1)}, bf16[1424,128]{1,0:T(8,128)(2,1)S(1)}, u32[]{:S(2)}, u32[]{:S(2)}) collective-permute-start(bf16[1424,128]{1,0:T(8,128)(2,1)S(1)} %collective-permute-done.4.refs_3_), channel_id=1, source_target_pairs={{0,2},{1,3},{2,0},{3,1},{4,6},{5,7},{6,4},{7,5},{8,10},{9,11},{10,... | collective-permute-start | bytes 1093640 | tf_op jit(solution)/shard_map/ppermute | solution.py:242

commit v21 on v18

--- a/solution.py
+++ b/solution.py
@@ -19,7 +19,7 @@
 
 
 def pack_kernel(cols, p_ids, q_ids, p_ref, q_ref, own_ref, *rest):
-    out_refs, strips = rest[:4], rest[4]
+    out_refs, strips = rest[:3], rest[3]
     blocks, per_q, extent, _ = q_ref.shape
     per_p = p_ids.shape[0]
     strip = extent // SEATS
@@ -38,7 +38,7 @@
             strips[j, f * rows:(f + 1) * rows] = jnp.concatenate(pieces, axis=0).astype(strips.dtype)
     here = lax.axis_index(("pair", "core", "col"))
     core = lax.axis_index("core")
-    paths = [[()], [(0,), (0, 1)], [(1,), (1, 2)], [(2,), (2, 0)], [(0, 1, 2)]]
+    paths = [[()], [(0,), (0, 1), (0, 1, 2)], [(1,), (1, 2)], [(2,), (2, 0)]]
     for path, out_ref in zip(paths, (own_ref, *out_refs)):
         spots = []
         for steps in path:
@@ -211,7 +211,7 @@
         functools.partial(pack_kernel, cols),
         out_shape=[
             jax.ShapeDtypeStruct((whole + passed * strips, extent), p_tiles.dtype)
-            for passed in (0, 1, 1, 1, 0)
+            for passed in (0, 2, 1, 1)
         ],
         in_specs=[pl.BlockSpec(memory_space=pltpu.SMEM)] * 2
         + [pl.BlockSpec(memory_space=pltpu.VMEM)] * 2,
@@ -230,22 +230,20 @@
         sizes = (blocks, per_p, per_q)
         return add_products(sizes, tile_count, cols, packets, passed, acc, coded)
 
-    def opposite(values):
-        return lax.ppermute(values, seat, [(s, s ^ (SEATS - 1 - cols)) for s in range(SEATS)])
-
     first = [along(out[step], step) for step in range(3)]
+    second = [along(rest_of(first[step], strips), (step + 1) % 3) for step in range(3)]
+    third = along(rest_of(second[0], strips), 2)
     beside = across(own)
-    far = opposite(out[3])
-    second = [along(rest_of(first[step], strips), (step + 1) % 3) for step in range(3)]
-    acc = add(None, [own, beside] + first, [(0, 0), (0, 1), (1, 0), (1, 0), (1, 0)])
-    first[2], second, acc = lax.optimization_barrier((first[2], second, acc))
-    acc = add(
-        acc,
-        [far, across(far), across(first[0])] + second,
-        [(0, 0), (0, 1), (1, 1), (0, 0), (0, 0), (0, 0)],
-    )
-    crossed = [across(each) for each in first[1:] + second]
-    coded = add(acc, crossed, [(1, 1), (1, 1), (0, 1), (0, 1), (0, 1)], coded=True)
+    acc = add(None, [own, beside] + first, [(0, 0), (0, 1), (2, 0), (1, 0), (1, 0)])
+    first[2], acc = lax.optimization_barrier((first[2], acc))
+    crossed = [across(each) for each in first]
+    second[1:], acc = lax.optimization_barrier((second[1:], acc))
+    more = [across(each) for each in second]
+    acc = add(acc, second + crossed[:2], [(1, 0), (0, 0), (0, 0), (2, 1), (1, 1)])
+    third, acc = lax.optimization_barrier((third, acc))
+    beside = across(third)
+    acc = add(acc, [third, crossed[2]] + more, [(0, 0), (1, 1), (1, 1), (0, 1), (0, 1)])
+    coded = add(acc, [beside], [(0, 1)], coded=True)
     every = ("plane",) + seat
     tiles = tile_count // cols
     landed = lax.all_to_all(coded, every, split_axis=0, concat_axis=0, tiled=True)

time: 64.9 us -> 68.1 us (1.049)
  starting transfers between devices: 22.8 us -> 25.5 us
  blocking collectives: 24.5 us -> 23.1 us
  Pallas kernels: 8.95 us -> 9.99 us
  waiting for transfers between devices: 8.37 us -> 9.29 us
    ppermute x6 -> x7, starting transfers between devices: 9.7 us -> 12.8 us  [along(): return lax.ppermute(values, seat, hops)]
    ppermute x6 -> x7, waiting for transfers between devices: 7.22 us -> 8.64 us  [along(): return lax.ppermute(values, seat, hops)]
    all_to_all x1, blocking collectives: 24.5 us -> 23.1 us  [body(): lax.all_to_all(coded, every, split_axis=0, concat_axis=0, tiled=True)]
    pallas_call x3 -> x4, Pallas kernels: 4.29 us -> 5.12 us  [add_products(): pl.pallas_call(functools.partial(product_kernel, sizes, tile_count, passe...]
  transfers between devices with their start and end apart: 15 -> 15, of which waited for: 6 -> 4; matrix products, arithmetic and copies ran while one was open for 0% -> 0% of each run, Pallas kernels for 5% -> 6%
where the time goes in v21:
time: 68.1 us; the launch traced here: 67.9 us
  starting transfers between devices  25.5 us (37%)
  blocking collectives  23.1 us (34%)
  Pallas kernels  9.99 us (15%)
  waiting for transfers between devices  9.29 us (14%)
    all_to_all x1, blocking collectives, body(): lax.all_to_all(coded, every, split_axis=0, concat_axis=0, tiled=True)  23.1 us
    ppermute x7, starting transfers between devices, along(): return lax.ppermute(values, seat, hops)  12.8 us
    ppermute x8, starting transfers between devices, across(): return lax.ppermute(values, seat, [(s, s ^ cols) for s in range(SEATS)])  12.7 us
    ppermute x7, waiting for transfers between devices, along(): return lax.ppermute(values, seat, hops)  8.64 us
    pallas_call x4, Pallas kernels, add_products(): pl.pallas_call(functools.partial(product_kernel, sizes, tile_count, passe...  5.12 us
    pallas_call x1, Pallas kernels, body(): pl.pallas_call(functools.partial(pack_kernel, cols), out_shape=[jax.Shape...  2.84 us
  transfers between devices with their start and end apart: 15, of which 4 were waited for; matrix products, arithmetic and copies ran while one was open for 0% of the time, Pallas kernels for 6%

profile of v21, /device:TPU:1, one launch (start us, length us, event | category | flops | bytes accessed | tf_op | source)
XLA Modules:
  0.0 67.9 jit_solution(6110080443265603402)
XLA Ops:
  0.0 2.8 %pack.1 = (bf16[1424,128]{1,0:T(8,128)(2,1)}, bf16[2192,128]{1,0:T(8,128)(2,1)}, bf16[1808,128]{1,0:T(8,128)(2,1)}, bf16[1808,128]{1,0:T(8,128)(2,1)}) custom-call(s32[2,4]{1,0:T(2,128)} %bitcast.3, s32[4,6]{1,0:T(4,128)} %q_ids.1, bf16[4,2,128,128]{3,2,1,0:T(8,128)(2,1)} %p_ref.1, bf16[4,6,128,128]{3,2,1,0:T(8,128)(2,1)} %q_ref.1), custom_call_target="tpu_custom_call" | custom-call | tf_op jit(solution)/shard_map/pack/pallas_call | solution.py:210
  2.8 2.0 %collective-permute-start = (bf16[2192,128]{1,0:T(8,128)(2,1)}, bf16[2192,128]{1,0:T(8,128)(2,1)S(1)}, u32[]{:S(2)}, u32[]{:S(2)}) collective-permute-start(bf16[2192,128]{1,0:T(8,128)(2,1)} %get-tuple-element.16), channel_id=1, source_target_pairs={{0,1},{1,0},{2,6},{3,7},{4,5},{5,4},{6,2},{7,3},{8,9},{9,8},{10,14... | collective-permute-start | bytes 1683464 | tf_op jit(solution)/shard_map/ppermute | solution.py:224
  4.9 1.3 %collective-permute-start.3 = (bf16[1808,128]{1,0:T(8,128)(2,1)}, bf16[1808,128]{1,0:T(8,128)(2,1)S(1)}, u32[]{:S(2)}, u32[]{:S(2)}) collective-permute-start(bf16[1808,128]{1,0:T(8,128)(2,1)} %get-tuple-element.17), channel_id=1, source_target_pairs={{0,4},{1,5},{2,10},{3,11},{4,0},{5,1},{6,14},{7,15},{8,12},{9,13},... | collective-permute-start | bytes 1388552 | tf_op jit(solution)/shard_map/ppermute | solution.py:224
  6.2 0.0 copy-start
  6.2 1.2 %collective-permute-start.5 = (bf16[1808,128]{1,0:T(8,128)(2,1)}, bf16[1808,128]{1,0:T(8,128)(2,1)S(1)}, u32[]{:S(2)}, u32[]{:S(2)}) collective-permute-start(bf16[1808,128]{1,0:T(8,128)(2,1)} %get-tuple-element.18), channel_id=1, source_target_pairs={{0,8},{1,9},{2,3},{3,2},{4,12},{5,13},{6,7},{7,6},{8,0},{9,1},{10,... | collective-permute-start | bytes 1388552 | tf_op jit(solution)/shard_map/ppermute | solution.py:224
  7.4 8.0 %collective-permute-done.in_ref.refs_2_ = bf16[2192,128]{1,0:T(8,128)(2,1)S(1)} collective-permute-done((bf16[2192,128]{1,0:T(8,128)(2,1)}, bf16[2192,128]{1,0:T(8,128)(2,1)S(1)}, u32[]{:S(2)}, u32[]{:S(2)}) %collective-permute-start) | collective-permute-done | bytes 561184 | tf_op jit(solution)/shard_map/ppermute | solution.py:224
  15.4 0.3 rest_of_packet.4
  15.7 1.9 %collective-permute-start.1 = (bf16[1808,128]{1,0:T(8,128)(2,1)S(1)}, bf16[1808,128]{1,0:T(8,128)(2,1)S(1)}, u32[]{:S(2)}, u32[]{:S(2)}) collective-permute-start(bf16[1808,128]{1,0:T(8,128)(2,1)S(1)} %rest_of_packet.4), channel_id=1, source_target_pairs={{0,4},{1,5},{2,10},{3,11},{4,0},{5,1},{6,14},{7,15},{8,12},{9,13},... | collective-permute-start | bytes 1388552 | tf_op jit(solution)/shard_map/ppermute | solution.py:224
  17.6 0.0 copy-done
  17.6 3.4 %collective-permute-start.7 = (bf16[1424,128]{1,0:T(8,128)(2,1)S(1)}, bf16[1424,128]{1,0:T(8,128)(2,1)S(1)}, u32[]{:S(2)}, u32[]{:S(2)}) collective-permute-start(bf16[1424,128]{1,0:T(8,128)(2,1)S(1)} %copy-done), channel_id=1, source_target_pairs={{0,2},{1,3},{2,0},{3,1},{4,6},{5,7},{6,4},{7,5},{8,10},{9,11},{10,... | collective-permute-start | bytes 1093640 | tf_op jit(solution)/shard_map/ppermute | solution.py:227
  20.9 0.0 collective-permute-start.8
  20.9 0.0 collective-permute-done.3.in_ref.refs_3_
  21.0 0.5 collective-permute-start.9
  21.5 0.2 rest_of_packet.6
  21.6 0.0 collective-permute-done.5.in_ref.refs_4_
  21.6 1.3 %collective-permute-start.4 = (bf16[1424,128]{1,0:T(8,128)(2,1)S(1)}, bf16[1424,128]{1,0:T(8,128)(2,1)S(1)}, u32[]{:S(2)}, u32[]{:S(2)}) collective-permute-start(bf16[1424,128]{1,0:T(8,128)(2,1)S(1)} %rest_of_packet.6), channel_id=1, source_target_pairs={{0,8},{1,9},{2,3},{3,2},{4,12},{5,13},{6,7},{7,6},{8,0},{9,1},{10,... | collective-permute-start | bytes 1093640 | tf_op jit(solution)/shard_map/ppermute | solution.py:224
  22.9 0.2 rest_of_packet.7
  23.1 0.7 collective-permute-done.1.in_ref.refs_0_
  23.8 1.7 %collective-permute-start.6 = (bf16[1424,128]{1,0:T(8,128)(2,1)S(1)}, bf16[1424,128]{1,0:T(8,128)(2,1)S(1)}, u32[]{:S(2)}, u32[]{:S(2)}) collective-permute-start(bf16[1424,128]{1,0:T(8,128)(2,1)S(1)} %rest_of_packet.7), channel_id=1, source_target_pairs={{0,1},{1,0},{2,6},{3,7},{4,5},{5,4},{6,2},{7,3},{8,9},{9,8},{10,14... | collective-permute-start | bytes 1093640 | tf_op jit(solution)/shard_map/ppermute | solution.py:224
  25.4 0.2 rest_of_packet.5
  25.6 0.0 collective-permute-done.7.refs_1_
  25.6 3.3 %collective-permute-start.2 = (bf16[1424,128]{1,0:T(8,128)(2,1)S(1)}, bf16[1424,128]{1,0:T(8,128)(2,1)S(1)}, u32[]{:S(2)}, u32[]{:S(2)}) collective-permute-start(bf16[1424,128]{1,0:T(8,128)(2,1)S(1)} %rest_of_packet.5), channel_id=1, source_target_pairs={{0,8},{1,9},{2,3},{3,2},{4,12},{5,13},{6,7},{7,6},{8,0},{9,1},{10,... | collective-permute-start | bytes 1093640 | tf_op jit(solution)/shard_map/ppermute | solution.py:224
  28.9 1.2 %products.4.refs_5_ = f32[256,8,128]{2,1,0:T(8,128)S(1)} custom-call(bf16[1424,128]{1,0:T(8,128)(2,1)S(1)} %copy-done, bf16[1424,128]{1,0:T(8,128)(2,1)S(1)} %collective-permute-done.7.refs_1_, bf16[2192,128]{1,0:T(8,128)(2,1)S(1)} %collective-permute-done.in_ref.refs_2_, bf16[1808,128]{1,0:T(8,128)(2,1)S(1)} %collective-permute-done.3.in_ref.refs_3_, ...), custom_call_target="tpu_custom_call" | custom-call | flops 62914560 | bytes 5242880 | tf_op jit(solution)/shard_map/products/pallas_call | solution.py:159
  30.2 0.0 collective-permute-done.4.refs_1_
  30.2 2.4 %collective-permute-start.11 = (bf16[1808,128]{1,0:T(8,128)(2,1)S(1)}, bf16[1808,128]{1,0:T(8,128)(2,1)S(1)}, u32[]{:S(2)}, u32[]{:S(2)}) collective-permute-start(bf16[1808,128]{1,0:T(8,128)(2,1)S(1)} %collective-permute-done.5.in_ref.refs_4_), channel_id=1, source_target_pairs={{0,2},{1,3},{2,0},{3,1},{4,6},{5,7},{6,4},{7,5},{8,10},{9,11},{10,... | collective-permute-start | bytes 1388552 | tf_op jit(solution)/shard_map/ppermute | solution.py:227
  32.6 0.0 collective-permute-done.6.refs_2_
  32.6 5.8 %collective-permute-start.12 = (bf16[1808,128]{1,0:T(8,128)(2,1)S(1)}, bf16[1808,128]{1,0:T(8,128)(2,1)S(1)}, u32[]{:S(2)}, u32[]{:S(2)}) collective-permute-start(bf16[1808,128]{1,0:T(8,128)(2,1)S(1)} %collective-permute-done.1.in_ref.refs_0_), channel_id=1, source_target_pairs={{0,2},{1,3},{2,0},{3,1},{4,6},{5,7},{6,4},{7,5},{8,10},{9,11},{10,... | collective-permute-start | bytes 1388552 | tf_op jit(solution)/shard_map/ppermute | solution.py:227
  38.4 0.0 collective-permute-done.9.refs_4_
  38.4 0.0 collective-permute-start.13
  38.4 0.0 collective-permute-done.8.refs_3_
  38.4 0.5 collective-permute-start.14
  38.9 1.2 %products.5.refs_5_ = f32[256,8,128]{2,1,0:T(8,128)S(1)} custom-call(bf16[1808,128]{1,0:T(8,128)(2,1)S(1)} %collective-permute-done.1.in_ref.refs_0_, bf16[1424,128]{1,0:T(8,128)(2,1)S(1)} %collective-permute-done.4.refs_1_, bf16[1424,128]{1,0:T(8,128)(2,1)S(1)} %collective-permute-done.6.refs_2_, ...), custom_call_target="tpu_custom_call", output_to_operand_aliasing={{}: (5, {})} | custom-call | flops 62914560 | bytes 5242880 | tf_op jit(solution)/shard_map/products/pallas_call | solution.py:159
  40.1 0.0 collective-permute-done.2.refs_0_
  40.1 0.1 collective-permute-start.10
  40.3 0.0 collective-permute-done.11.refs_1_
  40.3 0.1 collective-permute-done.13.refs_3_
  40.4 0.5 collective-permute-done.14.refs_4_
  40.9 0.0 collective-permute-done.12.refs_2_
  40.9 1.2 %products.6.refs_1_ = f32[256,8,128]{2,1,0:T(8,128)S(1)} custom-call(bf16[1424,128]{1,0:T(8,128)(2,1)S(1)} %collective-permute-done.2.refs_0_, bf16[1808,128]{1,0:T(8,128)(2,1)S(1)} %collective-permute-done.11.refs_1_, bf16[1808,128]{1,0:T(8,128)(2,1)S(1)} %collective-permute-done.12.refs_2_, ...), custom_call_target="tpu_custom_call", output_to_operand_aliasing={{}: (5, {})} | custom-call | flops 62914560 | bytes 5242880 | tf_op jit(solution)/shard_map/products/pallas_call | solution.py:159
  42.1 0.0 collective-permute-done.10.refs_0_
  42.1 1.5 %products.7 = s32[32,5,8,128]{3,2,1,0:T(8,128)S(1)} custom-call(bf16[1424,128]{1,0:T(8,128)(2,1)S(1)} %collective-permute-done.10.refs_0_, f32[256,8,128]{2,1,0:T(8,128)S(1)} %products.6.refs_1_), custom_call_target="tpu_custom_call" | custom-call | flops 12582912 | bytes 1048576 | tf_op jit(solution)/shard_map/products/pallas_call | solution.py:159
  43.6 23.1 %all_to_all.5 = s32[32,5,8,128]{3,2,1,0:T(8,128)S(1)} all-to-all(s32[32,5,8,128]{3,2,1,0:T(8,128)S(1)} %products.7), channel_id=1, replica_groups=mesh['plane'=2,'pair'=4,'core'=2,'col'=2] {'plane','pair','core','col'}, dimensions={0} | all-to-all | bytes 1310720 | tf_op jit(solution)/shard_map/all_to_all | solution.py:249
  66.7 1.3 %turn.1 = f32[128,1024]{1,0:T(8,128)} custom-call(s32[2,16,5,8,128]{4,3,2,1,0:T(8,128)S(1)} %bitcast.2), custom_call_target="tpu_custom_call" | custom-call | tf_op jit(solution)/shard_map/turn/pallas_call | solution.py:250
Async XLA Ops:
  2.8 12.5 %collective-permute-start = (bf16[2192,128]{1,0:T(8,128)(2,1)}, bf16[2192,128]{1,0:T(8,128)(2,1)S(1)}, u32[]{:S(2)}, u32[]{:S(2)}) collective-permute-start(bf16[2192,128]{1,0:T(8,128)(2,1)} %get-tuple-element.16), channel_id=1, source_target_pairs={{0,1},{1,0},{2,6},{3,7},{4,5},{5,4},{6,2},{7,3},{8,9},{9,8},{10,14... | collective-permute-start | bytes 1683464 | tf_op jit(solution)/shard_map/ppermute | solution.py:224
  4.9 16.1 %collective-permute-start.3 = (bf16[1808,128]{1,0:T(8,128)(2,1)}, bf16[1808,128]{1,0:T(8,128)(2,1)S(1)}, u32[]{:S(2)}, u32[]{:S(2)}) collective-permute-start(bf16[1808,128]{1,0:T(8,128)(2,1)} %get-tuple-element.17), channel_id=1, source_target_pairs={{0,4},{1,5},{2,10},{3,11},{4,0},{5,1},{6,14},{7,15},{8,12},{9,13},... | collective-permute-start | bytes 1388552 | tf_op jit(solution)/shard_map/ppermute | solution.py:224
  6.2 11.4 %copy-start = (bf16[1424,128]{1,0:T(8,128)(2,1)S(1)}, bf16[1424,128]{1,0:T(8,128)(2,1)}, u32[]{:S(2)}) copy-start(bf16[1424,128]{1,0:T(8,128)(2,1)} %get-tuple-element.19.refs_0_) | copy-start | bytes 1093636
  6.2 15.4 %collective-permute-start.5 = (bf16[1808,128]{1,0:T(8,128)(2,1)}, bf16[1808,128]{1,0:T(8,128)(2,1)S(1)}, u32[]{:S(2)}, u32[]{:S(2)}) collective-permute-start(bf16[1808,128]{1,0:T(8,128)(2,1)} %get-tuple-element.18), channel_id=1, source_target_pairs={{0,8},{1,9},{2,3},{3,2},{4,12},{5,13},{6,7},{7,6},{8,0},{9,1},{10,... | collective-permute-start | bytes 1388552 | tf_op jit(solution)/shard_map/ppermute | solution.py:224
  15.7 8.1 %collective-permute-start.1 = (bf16[1808,128]{1,0:T(8,128)(2,1)S(1)}, bf16[1808,128]{1,0:T(8,128)(2,1)S(1)}, u32[]{:S(2)}, u32[]{:S(2)}) collective-permute-start(bf16[1808,128]{1,0:T(8,128)(2,1)S(1)} %rest_of_packet.4), channel_id=1, source_target_pairs={{0,4},{1,5},{2,10},{3,11},{4,0},{5,1},{6,14},{7,15},{8,12},{9,13},... | collective-permute-start | bytes 1388552 | tf_op jit(solution)/shard_map/ppermute | solution.py:224
  17.6 8.0 %collective-permute-start.7 = (bf16[1424,128]{1,0:T(8,128)(2,1)S(1)}, bf16[1424,128]{1,0:T(8,128)(2,1)S(1)}, u32[]{:S(2)}, u32[]{:S(2)}) collective-permute-start(bf16[1424,128]{1,0:T(8,128)(2,1)S(1)} %copy-done), channel_id=1, source_target_pairs={{0,2},{1,3},{2,0},{3,1},{4,6},{5,7},{6,4},{7,5},{8,10},{9,11},{10,... | collective-permute-start | bytes 1093640 | tf_op jit(solution)/shard_map/ppermute | solution.py:227
  20.9 17.5 %collective-permute-start.8 = (bf16[2192,128]{1,0:T(8,128)(2,1)S(1)}, bf16[2192,128]{1,0:T(8,128)(2,1)S(1)}, u32[]{:S(2)}, u32[]{:S(2)}) collective-permute-start(bf16[2192,128]{1,0:T(8,128)(2,1)S(1)} %collective-permute-done.in_ref.refs_2_), channel_id=1, source_target_pairs={{0,2},{1,3},{2,0},{3,1},{4,6},{5,7},{6,4},{7,5},{8,10},{9,11},{10,... | collective-permute-start | bytes 1683464 | tf_op jit(solution)/shard_map/ppermute | solution.py:227
  21.0 17.4 %collective-permute-start.9 = (bf16[1808,128]{1,0:T(8,128)(2,1)S(1)}, bf16[1808,128]{1,0:T(8,128)(2,1)S(1)}, u32[]{:S(2)}, u32[]{:S(2)}) collective-permute-start(bf16[1808,128]{1,0:T(8,128)(2,1)S(1)} %collective-permute-done.3.in_ref.refs_3_), channel_id=1, source_target_pairs={{0,2},{1,3},{2,0},{3,1},{4,6},{5,7},{6,4},{7,5},{8,10},{9,11},{10,... | collective-permute-start | bytes 1388552 | tf_op jit(solution)/shard_map/ppermute | solution.py:227
  21.6 8.6 %collective-permute-start.4 = (bf16[1424,128]{1,0:T(8,128)(2,1)S(1)}, bf16[1424,128]{1,0:T(8,128)(2,1)S(1)}, u32[]{:S(2)}, u32[]{:S(2)}) collective-permute-start(bf16[1424,128]{1,0:T(8,128)(2,1)S(1)} %rest_of_packet.6), channel_id=1, source_target_pairs={{0,8},{1,9},{2,3},{3,2},{4,12},{5,13},{6,7},{7,6},{8,0},{9,1},{10,... | collective-permute-start | bytes 1093640 | tf_op jit(solution)/shard_map/ppermute | solution.py:224
  23.8 8.9 %collective-permute-start.6 = (bf16[1424,128]{1,0:T(8,128)(2,1)S(1)}, bf16[1424,128]{1,0:T(8,128)(2,1)S(1)}, u32[]{:S(2)}, u32[]{:S(2)}) collective-permute-start(bf16[1424,128]{1,0:T(8,128)(2,1)S(1)} %rest_of_packet.7), channel_id=1, source_target_pairs={{0,1},{1,0},{2,6},{3,7},{4,5},{5,4},{6,2},{7,3},{8,9},{9,8},{10,14... | collective-permute-start | bytes 1093640 | tf_op jit(solution)/shard_map/ppermute | solution.py:224
  25.6 14.5 %collective-permute-start.2 = (bf16[1424,128]{1,0:T(8,128)(2,1)S(1)}, bf16[1424,128]{1,0:T(8,128)(2,1)S(1)}, u32[]{:S(2)}, u32[]{:S(2)}) collective-permute-start(bf16[1424,128]{1,0:T(8,128)(2,1)S(1)} %rest_of_packet.5), channel_id=1, source_target_pairs={{0,8},{1,9},{2,3},{3,2},{4,12},{5,13},{6,7},{7,6},{8,0},{9,1},{10,... | collective-permute-start | bytes 1093640 | tf_op jit(solution)/shard_map/ppermute | solution.py:224
  30.2 10.1 %collective-permute-start.11 = (bf16[1808,128]{1,0:T(8,128)(2,1)S(1)}, bf16[1808,128]{1,0:T(8,128)(2,1)S(1)}, u32[]{:S(2)}, u32[]{:S(2)}) collective-permute-start(bf16[1808,128]{1,0:T(8,128)(2,1)S(1)} %collective-permute-done.5.in_ref.refs_4_), channel_id=1, source_target_pairs={{0,2},{1,3},{2,0},{3,1},{4,6},{5,7},{6,4},{7,5},{8,10},{9,11},{10,... | collective-permute-start | bytes 1388552 | tf_op jit(solution)/shard_map/ppermute | solution.py:227
  32.6 8.3 %collective-permute-start.12 = (bf16[1808,128]{1,0:T(8,128)(2,1)S(1)}, bf16[1808,128]{1,0:T(8,128)(2,1)S(1)}, u32[]{:S(2)}, u32[]{:S(2)}) collective-permute-start(bf16[1808,128]{1,0:T(8,128)(2,1)S(1)} %collective-permute-done.1.in_ref.refs_0_), channel_id=1, source_target_pairs={{0,2},{1,3},{2,0},{3,1},{4,6},{5,7},{6,4},{7,5},{8,10},{9,11},{10,... | collective-permute-start | bytes 1388552 | tf_op jit(solution)/shard_map/ppermute | solution.py:227
  38.4 2.0 %collective-permute-start.13 = (bf16[1424,128]{1,0:T(8,128)(2,1)S(1)}, bf16[1424,128]{1,0:T(8,128)(2,1)S(1)}, u32[]{:S(2)}, u32[]{:S(2)}) collective-permute-start(bf16[1424,128]{1,0:T(8,128)(2,1)S(1)} %collective-permute-done.4.refs_1_), channel_id=1, source_target_pairs={{0,2},{1,3},{2,0},{3,1},{4,6},{5,7},{6,4},{7,5},{8,10},{9,11},{10,... | collective-permute-start | bytes 1093640 | tf_op jit(solution)/shard_map/ppermute | solution.py:227
  38.4 2.5 %collective-permute-start.14 = (bf16[1424,128]{1,0:T(8,128)(2,1)S(1)}, bf16[1424,128]{1,0:T(8,128)(2,1)S(1)}, u32[]{:S(2)}, u32[]{:S(2)}) collective-permute-start(bf16[1424,128]{1,0:T(8,128)(2,1)S(1)} %collective-permute-done.6.refs_2_), channel_id=1, source_target_pairs={{0,2},{1,3},{2,0},{3,1},{4,6},{5,7},{6,4},{7,5},{8,10},{9,11},{10,... | collective-permute-start | bytes 1093640 | tf_op jit(solution)/shard_map/ppermute | solution.py:227
  40.1 2.0 %collective-permute-start.10 = (bf16[1424,128]{1,0:T(8,128)(2,1)S(1)}, bf16[1424,128]{1,0:T(8,128)(2,1)S(1)}, u32[]{:S(2)}, u32[]{:S(2)}) collective-permute-start(bf16[1424,128]{1,0:T(8,128)(2,1)S(1)} %collective-permute-done.2.refs_0_), channel_id=1, source_target_pairs={{0,2},{1,3},{2,0},{3,1},{4,6},{5,7},{6,4},{7,5},{8,10},{9,11},{10,... | collective-permute-start | bytes 1093640 | tf_op jit(solution)/shard_map/ppermute | solution.py:227

commit v22 on v18

--- a/solution.py
+++ b/solution.py
@@ -238,14 +238,11 @@
     far = opposite(out[3])
     second = [along(rest_of(first[step], strips), (step + 1) % 3) for step in range(3)]
     acc = add(None, [own, beside] + first, [(0, 0), (0, 1), (1, 0), (1, 0), (1, 0)])
-    first[2], second, acc = lax.optimization_barrier((first[2], second, acc))
-    acc = add(
-        acc,
-        [far, across(far), across(first[0])] + second,
-        [(0, 0), (0, 1), (1, 1), (0, 0), (0, 0), (0, 0)],
-    )
-    crossed = [across(each) for each in first[1:] + second]
-    coded = add(acc, crossed, [(1, 1), (1, 1), (0, 1), (0, 1), (0, 1)], coded=True)
+    first[2], far, second, acc = lax.optimization_barrier((first[2], far, second, acc))
+    crossed = [across(each) for each in first + [far] + second]
+    acc = add(acc, crossed[:2] + [far] + second, [(1, 1), (1, 1), (0, 0), (0, 0), (0, 0), (0, 0)])
+    acc = add(acc, crossed[2:5], [(1, 1), (0, 1), (0, 1)])
+    coded = add(acc, crossed[5:], [(0, 1), (0, 1)], coded=True)
     every = ("plane",) + seat
     tiles = tile_count // cols
     landed = lax.all_to_all(coded, every, split_axis=0, concat_axis=0, tiled=True)

time: 64.9 us -> 64.6 us (level)
  starting transfers between devices: 22.8 us -> 20.5 us
  waiting for transfers between devices: 8.37 us -> 10.2 us
  Pallas kernels: 8.95 us -> 9.78 us
  blocking collectives: 24.5 us -> 23.8 us
    ppermute x6, waiting for transfers between devices: 7.22 us -> 10 us  [along(): return lax.ppermute(values, seat, hops)]
    ppermute x8, starting transfers between devices: 13.1 us -> 10.8 us  [across(): return lax.ppermute(values, seat, [(s, s ^ cols) for s in range(SEATS)])]
    ppermute x8, waiting for transfers between devices: 1.15 us -> 0.2 us  [across(): return lax.ppermute(values, seat, [(s, s ^ cols) for s in range(SEATS)])]
    pallas_call x3 -> x4, Pallas kernels: 4.29 us -> 5.11 us  [add_products(): pl.pallas_call(functools.partial(product_kernel, sizes, tile_count, passe...]
  transfers between devices with their start and end apart: 15 -> 15, of which waited for: 6 -> 6; matrix products, arithmetic and copies ran while one was open for 0% -> 0% of each run, Pallas kernels for 5% -> 6%
where the time goes in v22:
time: 64.6 us; the launch traced here: 64.4 us
  blocking collectives  23.8 us (37%)
  starting transfers between devices  20.5 us (32%)
  waiting for transfers between devices  10.2 us (16%)
  Pallas kernels  9.78 us (15%)
    all_to_all x1, blocking collectives, body(): lax.all_to_all(coded, every, split_axis=0, concat_axis=0, tiled=True)  23.8 us
    ppermute x8, starting transfers between devices, across(): return lax.ppermute(values, seat, [(s, s ^ cols) for s in range(SEATS)])  10.8 us
    ppermute x6, waiting for transfers between devices, along(): return lax.ppermute(values, seat, hops)  10 us
    ppermute x6, starting transfers between devices, along(): return lax.ppermute(values, seat, hops)  9.7 us
    pallas_call x4, Pallas kernels, add_products(): pl.pallas_call(functools.partial(product_kernel, sizes, tile_count, passe...  5.11 us
    pallas_call x1, Pallas kernels, body(): pl.pallas_call(functools.partial(pack_kernel, cols), out_shape=[jax.Shape...  2.93 us
  transfers between devices with their start and end apart: 15, of which 6 were waited for; matrix products, arithmetic and copies ran while one was open for 0% of the time, Pallas kernels for 6%

profile of v22, /device:TPU:1, one launch (start us, length us, event | category | flops | bytes accessed | tf_op | source)
XLA Modules:
  0.0 64.4 jit_solution(17884948715544406882)
XLA Ops:
  0.0 2.9 %pack.1 = (bf16[1424,128]{1,0:T(8,128)(2,1)}, bf16[1808,128]{1,0:T(8,128)(2,1)}, bf16[1808,128]{1,0:T(8,128)(2,1)}, bf16[1808,128]{1,0:T(8,128)(2,1)}, bf16[1424,128]{1,0:T(8,128)(2,1)}) custom-call(s32[2,4]{1,0:T(2,128)} %bitcast.3, s32[4,6]{1,0:T(4,128)} %q_ids.1, bf16[4,2,128,128]{3,2,1,0:T(8,128)(2,1)} %p_ref.1, bf16[4,6,128,128]{3,2,1,0:T(8,128)(2,1)} %q_ref.1), custom_call_target="tpu_custom_call" | custom-call | tf_op jit(solution)/shard_map/pack/pallas_call | solution.py:210
  2.9 2.0 %collective-permute-start.2 = (bf16[1808,128]{1,0:T(8,128)(2,1)}, bf16[1808,128]{1,0:T(8,128)(2,1)S(1)}, u32[]{:S(2)}, u32[]{:S(2)}) collective-permute-start(bf16[1808,128]{1,0:T(8,128)(2,1)} %get-tuple-element.18), channel_id=1, source_target_pairs={{0,1},{1,0},{2,6},{3,7},{4,5},{5,4},{6,2},{7,3},{8,9},{9,8},{10,14... | collective-permute-start | bytes 1388552 | tf_op jit(solution)/shard_map/ppermute | solution.py:224
  5.0 1.3 %collective-permute-start.4 = (bf16[1808,128]{1,0:T(8,128)(2,1)}, bf16[1808,128]{1,0:T(8,128)(2,1)S(1)}, u32[]{:S(2)}, u32[]{:S(2)}) collective-permute-start(bf16[1808,128]{1,0:T(8,128)(2,1)} %get-tuple-element.19), channel_id=1, source_target_pairs={{0,4},{1,5},{2,10},{3,11},{4,0},{5,1},{6,14},{7,15},{8,12},{9,13},... | collective-permute-start | bytes 1388552 | tf_op jit(solution)/shard_map/ppermute | solution.py:224
  6.3 1.2 %collective-permute-start = (bf16[1808,128]{1,0:T(8,128)(2,1)}, bf16[1808,128]{1,0:T(8,128)(2,1)S(1)}, u32[]{:S(2)}, u32[]{:S(2)}) collective-permute-start(bf16[1808,128]{1,0:T(8,128)(2,1)} %get-tuple-element.16), channel_id=1, source_target_pairs={{0,8},{1,9},{2,3},{3,2},{4,12},{5,13},{6,7},{7,6},{8,0},{9,1},{10,... | collective-permute-start | bytes 1388552 | tf_op jit(solution)/shard_map/ppermute | solution.py:224
  7.5 1.5 %collective-permute-start.7 = (bf16[1424,128]{1,0:T(8,128)(2,1)}, bf16[1424,128]{1,0:T(8,128)(2,1)S(1)}, u32[]{:S(2)}, u32[]{:S(2)}) collective-permute-start(bf16[1424,128]{1,0:T(8,128)(2,1)} %get-tuple-element.20.refs_0_), channel_id=1, source_target_pairs={{0,2},{1,3},{2,0},{3,1},{4,6},{5,7},{6,4},{7,5},{8,10},{9,11},{10,... | collective-permute-start | bytes 1093640 | tf_op jit(solution)/shard_map/ppermute | solution.py:227
  9.0 0.0 collective-permute-start.1
  9.0 4.3 %collective-permute-done.2.in_ref.refs_2_ = bf16[1808,128]{1,0:T(8,128)(2,1)S(1)} collective-permute-done((bf16[1808,128]{1,0:T(8,128)(2,1)}, bf16[1808,128]{1,0:T(8,128)(2,1)S(1)}, u32[]{:S(2)}, u32[]{:S(2)}) %collective-permute-start.2) | collective-permute-done | bytes 462880 | tf_op jit(solution)/shard_map/ppermute | solution.py:224
  13.4 0.2 rest_of_packet.3
  13.5 1.9 %collective-permute-start.3 = (bf16[1424,128]{1,0:T(8,128)(2,1)S(1)}, bf16[1424,128]{1,0:T(8,128)(2,1)S(1)}, u32[]{:S(2)}, u32[]{:S(2)}) collective-permute-start(bf16[1424,128]{1,0:T(8,128)(2,1)S(1)} %rest_of_packet.3), channel_id=1, source_target_pairs={{0,4},{1,5},{2,10},{3,11},{4,0},{5,1},{6,14},{7,15},{8,12},{9,13},... | collective-permute-start | bytes 1093640 | tf_op jit(solution)/shard_map/ppermute | solution.py:224
  15.4 0.0 collective-permute-done.4.in_ref.refs_3_
  15.4 0.2 rest_of_packet.4
  15.6 0.0 copy-start
  15.6 2.3 %collective-permute-start.5 = (bf16[1424,128]{1,0:T(8,128)(2,1)S(1)}, bf16[1424,128]{1,0:T(8,128)(2,1)S(1)}, u32[]{:S(2)}, u32[]{:S(2)}) collective-permute-start(bf16[1424,128]{1,0:T(8,128)(2,1)S(1)} %rest_of_packet.4), channel_id=1, source_target_pairs={{0,8},{1,9},{2,3},{3,2},{4,12},{5,13},{6,7},{7,6},{8,0},{9,1},{10,... | collective-permute-start | bytes 1093640 | tf_op jit(solution)/shard_map/ppermute | solution.py:224
  17.9 2.2 %collective-permute-done.in_ref.refs_4_ = bf16[1808,128]{1,0:T(8,128)(2,1)S(1)} collective-permute-done((bf16[1808,128]{1,0:T(8,128)(2,1)}, bf16[1808,128]{1,0:T(8,128)(2,1)S(1)}, u32[]{:S(2)}, u32[]{:S(2)}) %collective-permute-start) | collective-permute-done | bytes 462880 | tf_op jit(solution)/shard_map/ppermute | solution.py:224
  20.1 0.2 rest_of_packet.5
  20.2 0.9 %collective-permute-start.6 = (bf16[1424,128]{1,0:T(8,128)(2,1)S(1)}, bf16[1424,128]{1,0:T(8,128)(2,1)S(1)}, u32[]{:S(2)}, u32[]{:S(2)}) collective-permute-start(bf16[1424,128]{1,0:T(8,128)(2,1)S(1)} %rest_of_packet.5), channel_id=1, source_target_pairs={{0,1},{1,0},{2,6},{3,7},{4,5},{5,4},{6,2},{7,3},{8,9},{9,8},{10,14... | collective-permute-start | bytes 1093640 | tf_op jit(solution)/shard_map/ppermute | solution.py:224
  21.2 0.0 collective-permute-done.7.refs_1_
  21.2 4.8 %collective-permute-start.13 = (bf16[1808,128]{1,0:T(8,128)(2,1)S(1)}, bf16[1808,128]{1,0:T(8,128)(2,1)S(1)}, u32[]{:S(2)}, u32[]{:S(2)}) collective-permute-start(bf16[1808,128]{1,0:T(8,128)(2,1)S(1)} %collective-permute-done.2.in_ref.refs_2_), channel_id=1, source_target_pairs={{0,2},{1,3},{2,0},{3,1},{4,6},{5,7},{6,4},{7,5},{8,10},{9,11},{10,... | collective-permute-start | bytes 1388552 | tf_op jit(solution)/shard_map/ppermute | solution.py:227
  26.0 0.0 collective-permute-done.1.refs_2_
  26.0 2.5 %collective-permute-start.14 = (bf16[1808,128]{1,0:T(8,128)(2,1)S(1)}, bf16[1808,128]{1,0:T(8,128)(2,1)S(1)}, u32[]{:S(2)}, u32[]{:S(2)}) collective-permute-start(bf16[1808,128]{1,0:T(8,128)(2,1)S(1)} %collective-permute-done.4.in_ref.refs_3_), channel_id=1, source_target_pairs={{0,2},{1,3},{2,0},{3,1},{4,6},{5,7},{6,4},{7,5},{8,10},{9,11},{10,... | collective-permute-start | bytes 1388552 | tf_op jit(solution)/shard_map/ppermute | solution.py:227
  28.5 0.0 copy-done
  28.5 1.2 %products.4.refs_6_ = f32[256,8,128]{2,1,0:T(8,128)S(1)} custom-call(bf16[1424,128]{1,0:T(8,128)(2,1)S(1)} %copy-done, bf16[1424,128]{1,0:T(8,128)(2,1)S(1)} %collective-permute-done.7.refs_1_, bf16[1808,128]{1,0:T(8,128)(2,1)S(1)} %collective-permute-done.2.in_ref.refs_2_, bf16[1808,128]{1,0:T(8,128)(2,1)S(1)} %collective-permute-done.4.in_ref.refs_3_, ...), custom_call_target="tpu_custom_call" | custom-call | flops 62914560 | bytes 5242880 | tf_op jit(solution)/shard_map/products/pallas_call | solution.py:159
  29.7 0.7 %collective-permute-done.3.refs_3_ = bf16[1424,128]{1,0:T(8,128)(2,1)S(1)} collective-permute-done((bf16[1424,128]{1,0:T(8,128)(2,1)S(1)}, bf16[1424,128]{1,0:T(8,128)(2,1)S(1)}, u32[]{:S(2)}, u32[]{:S(2)}) %collective-permute-start.3) | collective-permute-done | bytes 364576 | tf_op jit(solution)/shard_map/ppermute | solution.py:224
  30.4 1.7 %collective-permute-done.5.refs_4_ = bf16[1424,128]{1,0:T(8,128)(2,1)S(1)} collective-permute-done((bf16[1424,128]{1,0:T(8,128)(2,1)S(1)}, bf16[1424,128]{1,0:T(8,128)(2,1)S(1)}, u32[]{:S(2)}, u32[]{:S(2)}) %collective-permute-start.5) | collective-permute-done | bytes 364576 | tf_op jit(solution)/shard_map/ppermute | solution.py:224
  32.1 1.1 %collective-permute-done.6.refs_5_ = bf16[1424,128]{1,0:T(8,128)(2,1)S(1)} collective-permute-done((bf16[1424,128]{1,0:T(8,128)(2,1)S(1)}, bf16[1424,128]{1,0:T(8,128)(2,1)S(1)}, u32[]{:S(2)}, u32[]{:S(2)}) %collective-permute-start.6) | collective-permute-done | bytes 364576 | tf_op jit(solution)/shard_map/ppermute | solution.py:224
  33.2 1.0 %collective-permute-start.10 = (bf16[1808,128]{1,0:T(8,128)(2,1)S(1)}, bf16[1808,128]{1,0:T(8,128)(2,1)S(1)}, u32[]{:S(2)}, u32[]{:S(2)}) collective-permute-start(bf16[1808,128]{1,0:T(8,128)(2,1)S(1)} %collective-permute-done.in_ref.refs_4_), channel_id=1, source_target_pairs={{0,2},{1,3},{2,0},{3,1},{4,6},{5,7},{6,4},{7,5},{8,10},{9,11},{10,... | collective-permute-start | bytes 1388552 | tf_op jit(solution)/shard_map/ppermute | solution.py:227
  34.2 0.0 collective-permute-start.11
  34.2 0.5 collective-permute-start.12
  34.7 0.0 collective-permute-done.13.refs_0_
  34.7 0.0 collective-permute-start.8
  34.7 0.0 collective-permute-done.14.refs_1_
  34.7 0.5 collective-permute-start.9
  35.2 1.3 %products.5.refs_3_ = f32[256,8,128]{2,1,0:T(8,128)S(1)} custom-call(bf16[1808,128]{1,0:T(8,128)(2,1)S(1)} %collective-permute-done.13.refs_0_, bf16[1808,128]{1,0:T(8,128)(2,1)S(1)} %collective-permute-done.14.refs_1_, bf16[1424,128]{1,0:T(8,128)(2,1)S(1)} %collective-permute-done.1.refs_2_, ...), custom_call_target="tpu_custom_call", output_to_operand_aliasing={{}: (6, {})} | custom-call | flops 75497472 | bytes 6291456 | tf_op jit(solution)/shard_map/products/pallas_call | solution.py:159
  36.5 0.0 collective-permute-done.11.refs_1_
  36.5 0.2 collective-permute-done.12.refs_2_
  36.7 0.0 collective-permute-done.10.refs_0_
  36.7 1.0 %products.6.refs_2_ = f32[256,8,128]{2,1,0:T(8,128)S(1)} custom-call(bf16[1808,128]{1,0:T(8,128)(2,1)S(1)} %collective-permute-done.10.refs_0_, bf16[1424,128]{1,0:T(8,128)(2,1)S(1)} %collective-permute-done.11.refs_1_, bf16[1424,128]{1,0:T(8,128)(2,1)S(1)} %collective-permute-done.12.refs_2_, ...), custom_call_target="tpu_custom_call", output_to_operand_aliasing={{}: (3, {})} | custom-call | flops 37748736 | bytes 3145728 | tf_op jit(solution)/shard_map/products/pallas_call | solution.py:159
  37.7 0.0 collective-permute-done.8.refs_0_
  37.7 0.0 collective-permute-done.9.refs_1_
  37.7 1.6 %products.7 = s32[32,5,8,128]{3,2,1,0:T(8,128)S(1)} custom-call(bf16[1424,128]{1,0:T(8,128)(2,1)S(1)} %collective-permute-done.8.refs_0_, bf16[1424,128]{1,0:T(8,128)(2,1)S(1)} %collective-permute-done.9.refs_1_, f32[256,8,128]{2,1,0:T(8,128)S(1)} %products.6.refs_2_), custom_call_target="tpu_custom_call" | custom-call | flops 25165824 | bytes 2097152 | tf_op jit(solution)/shard_map/products/pallas_call | solution.py:159
  39.3 23.8 %all_to_all.5 = s32[32,5,8,128]{3,2,1,0:T(8,128)S(1)} all-to-all(s32[32,5,8,128]{3,2,1,0:T(8,128)S(1)} %products.7), channel_id=1, replica_groups=mesh['plane'=2,'pair'=4,'core'=2,'col'=2] {'plane','pair','core','col'}, dimensions={0} | all-to-all | bytes 1310720 | tf_op jit(solution)/shard_map/all_to_all | solution.py:248
  63.1 1.3 %turn.1 = f32[128,1024]{1,0:T(8,128)} custom-call(s32[2,16,5,8,128]{4,3,2,1,0:T(8,128)S(1)} %bitcast.2), custom_call_target="tpu_custom_call" | custom-call | tf_op jit(solution)/shard_map/turn/pallas_call | solution.py:249
Async XLA Ops:
  2.9 10.4 %collective-permute-start.2 = (bf16[1808,128]{1,0:T(8,128)(2,1)}, bf16[1808,128]{1,0:T(8,128)(2,1)S(1)}, u32[]{:S(2)}, u32[]{:S(2)}) collective-permute-start(bf16[1808,128]{1,0:T(8,128)(2,1)} %get-tuple-element.18), channel_id=1, source_target_pairs={{0,1},{1,0},{2,6},{3,7},{4,5},{5,4},{6,2},{7,3},{8,9},{9,8},{10,14... | collective-permute-start | bytes 1388552 | tf_op jit(solution)/shard_map/ppermute | solution.py:224
  5.0 10.4 %collective-permute-start.4 = (bf16[1808,128]{1,0:T(8,128)(2,1)}, bf16[1808,128]{1,0:T(8,128)(2,1)S(1)}, u32[]{:S(2)}, u32[]{:S(2)}) collective-permute-start(bf16[1808,128]{1,0:T(8,128)(2,1)} %get-tuple-element.19), channel_id=1, source_target_pairs={{0,4},{1,5},{2,10},{3,11},{4,0},{5,1},{6,14},{7,15},{8,12},{9,13},... | collective-permute-start | bytes 1388552 | tf_op jit(solution)/shard_map/ppermute | solution.py:224
  6.3 13.8 %collective-permute-start = (bf16[1808,128]{1,0:T(8,128)(2,1)}, bf16[1808,128]{1,0:T(8,128)(2,1)S(1)}, u32[]{:S(2)}, u32[]{:S(2)}) collective-permute-start(bf16[1808,128]{1,0:T(8,128)(2,1)} %get-tuple-element.16), channel_id=1, source_target_pairs={{0,8},{1,9},{2,3},{3,2},{4,12},{5,13},{6,7},{7,6},{8,0},{9,1},{10,... | collective-permute-start | bytes 1388552 | tf_op jit(solution)/shard_map/ppermute | solution.py:224
  7.5 13.7 %collective-permute-start.7 = (bf16[1424,128]{1,0:T(8,128)(2,1)}, bf16[1424,128]{1,0:T(8,128)(2,1)S(1)}, u32[]{:S(2)}, u32[]{:S(2)}) collective-permute-start(bf16[1424,128]{1,0:T(8,128)(2,1)} %get-tuple-element.20.refs_0_), channel_id=1, source_target_pairs={{0,2},{1,3},{2,0},{3,1},{4,6},{5,7},{6,4},{7,5},{8,10},{9,11},{10,... | collective-permute-start | bytes 1093640 | tf_op jit(solution)/shard_map/ppermute | solution.py:227
  9.0 16.9 %collective-permute-start.1 = (bf16[1424,128]{1,0:T(8,128)(2,1)}, bf16[1424,128]{1,0:T(8,128)(2,1)S(1)}, u32[]{:S(2)}, u32[]{:S(2)}) collective-permute-start(bf16[1424,128]{1,0:T(8,128)(2,1)} %get-tuple-element.17), channel_id=1, source_target_pairs={{0,13},{1,12},{2,15},{3,14},{4,9},{5,8},{6,11},{7,10},{8,5},{9,4},... | collective-permute-start | bytes 1093640 | tf_op jit(solution)/shard_map/ppermute | solution.py:234
  13.5 16.9 %collective-permute-start.3 = (bf16[1424,128]{1,0:T(8,128)(2,1)S(1)}, bf16[1424,128]{1,0:T(8,128)(2,1)S(1)}, u32[]{:S(2)}, u32[]{:S(2)}) collective-permute-start(bf16[1424,128]{1,0:T(8,128)(2,1)S(1)} %rest_of_packet.3), channel_id=1, source_target_pairs={{0,4},{1,5},{2,10},{3,11},{4,0},{5,1},{6,14},{7,15},{8,12},{9,13},... | collective-permute-start | bytes 1093640 | tf_op jit(solution)/shard_map/ppermute | solution.py:224
  15.6 12.9 %copy-start = (bf16[1424,128]{1,0:T(8,128)(2,1)S(1)}, bf16[1424,128]{1,0:T(8,128)(2,1)}, u32[]{:S(2)}) copy-start(bf16[1424,128]{1,0:T(8,128)(2,1)} %get-tuple-element.20.refs_0_) | copy-start | bytes 1093636
  15.6 16.5 %collective-permute-start.5 = (bf16[1424,128]{1,0:T(8,128)(2,1)S(1)}, bf16[1424,128]{1,0:T(8,128)(2,1)S(1)}, u32[]{:S(2)}, u32[]{:S(2)}) collective-permute-start(bf16[1424,128]{1,0:T(8,128)(2,1)S(1)} %rest_of_packet.4), channel_id=1, source_target_pairs={{0,8},{1,9},{2,3},{3,2},{4,12},{5,13},{6,7},{7,6},{8,0},{9,1},{10,... | collective-permute-start | bytes 1093640 | tf_op jit(solution)/shard_map/ppermute | solution.py:224
  20.2 13.0 %collective-permute-start.6 = (bf16[1424,128]{1,0:T(8,128)(2,1)S(1)}, bf16[1424,128]{1,0:T(8,128)(2,1)S(1)}, u32[]{:S(2)}, u32[]{:S(2)}) collective-permute-start(bf16[1424,128]{1,0:T(8,128)(2,1)S(1)} %rest_of_packet.5), channel_id=1, source_target_pairs={{0,1},{1,0},{2,6},{3,7},{4,5},{5,4},{6,2},{7,3},{8,9},{9,8},{10,14... | collective-permute-start | bytes 1093640 | tf_op jit(solution)/shard_map/ppermute | solution.py:224
  21.2 13.5 %collective-permute-start.13 = (bf16[1808,128]{1,0:T(8,128)(2,1)S(1)}, bf16[1808,128]{1,0:T(8,128)(2,1)S(1)}, u32[]{:S(2)}, u32[]{:S(2)}) collective-permute-start(bf16[1808,128]{1,0:T(8,128)(2,1)S(1)} %collective-permute-done.2.in_ref.refs_2_), channel_id=1, source_target_pairs={{0,2},{1,3},{2,0},{3,1},{4,6},{5,7},{6,4},{7,5},{8,10},{9,11},{10,... | collective-permute-start | bytes 1388552 | tf_op jit(solution)/shard_map/ppermute | solution.py:227
  26.0 8.8 %collective-permute-start.14 = (bf16[1808,128]{1,0:T(8,128)(2,1)S(1)}, bf16[1808,128]{1,0:T(8,128)(2,1)S(1)}, u32[]{:S(2)}, u32[]{:S(2)}) collective-permute-start(bf16[1808,128]{1,0:T(8,128)(2,1)S(1)} %collective-permute-done.4.in_ref.refs_3_), channel_id=1, source_target_pairs={{0,2},{1,3},{2,0},{3,1},{4,6},{5,7},{6,4},{7,5},{8,10},{9,11},{10,... | collective-permute-start | bytes 1388552 | tf_op jit(solution)/shard_map/ppermute | solution.py:227
  33.2 3.4 %collective-permute-start.10 = (bf16[1808,128]{1,0:T(8,128)(2,1)S(1)}, bf16[1808,128]{1,0:T(8,128)(2,1)S(1)}, u32[]{:S(2)}, u32[]{:S(2)}) collective-permute-start(bf16[1808,128]{1,0:T(8,128)(2,1)S(1)} %collective-permute-done.in_ref.refs_4_), channel_id=1, source_target_pairs={{0,2},{1,3},{2,0},{3,1},{4,6},{5,7},{6,4},{7,5},{8,10},{9,11},{10,... | collective-permute-start | bytes 1388552 | tf_op jit(solution)/shard_map/ppermute | solution.py:227
  34.2 2.3 %collective-permute-start.11 = (bf16[1424,128]{1,0:T(8,128)(2,1)S(1)}, bf16[1424,128]{1,0:T(8,128)(2,1)S(1)}, u32[]{:S(2)}, u32[]{:S(2)}) collective-permute-start(bf16[1424,128]{1,0:T(8,128)(2,1)S(1)} %collective-permute-done.1.refs_2_), channel_id=1, source_target_pairs={{0,2},{1,3},{2,0},{3,1},{4,6},{5,7},{6,4},{7,5},{8,10},{9,11},{10,... | collective-permute-start | bytes 1093640 | tf_op jit(solution)/shard_map/ppermute | solution.py:227
  34.2 2.5 %collective-permute-start.12 = (bf16[1424,128]{1,0:T(8,128)(2,1)S(1)}, bf16[1424,128]{1,0:T(8,128)(2,1)S(1)}, u32[]{:S(2)}, u32[]{:S(2)}) collective-permute-start(bf16[1424,128]{1,0:T(8,128)(2,1)S(1)} %collective-permute-done.3.refs_3_), channel_id=1, source_target_pairs={{0,2},{1,3},{2,0},{3,1},{4,6},{5,7},{6,4},{7,5},{8,10},{9,11},{10,... | collective-permute-start | bytes 1093640 | tf_op jit(solution)/shard_map/ppermute | solution.py:227
  34.7 3.0 %collective-permute-start.8 = (bf16[1424,128]{1,0:T(8,128)(2,1)S(1)}, bf16[1424,128]{1,0:T(8,128)(2,1)S(1)}, u32[]{:S(2)}, u32[]{:S(2)}) collective-permute-start(bf16[1424,128]{1,0:T(8,128)(2,1)S(1)} %collective-permute-done.5.refs_4_), channel_id=1, source_target_pairs={{0,2},{1,3},{2,0},{3,1},{4,6},{5,7},{6,4},{7,5},{8,10},{9,11},{10,... | collective-permute-start | bytes 1093640 | tf_op jit(solution)/shard_map/ppermute | solution.py:227
  34.7 3.0 %collective-permute-start.9 = (bf16[1424,128]{1,0:T(8,128)(2,1)S(1)}, bf16[1424,128]{1,0:T(8,128)(2,1)S(1)}, u32[]{:S(2)}, u32[]{:S(2)}) collective-permute-start(bf16[1424,128]{1,0:T(8,128)(2,1)S(1)} %collective-permute-done.6.refs_5_), channel_id=1, source_target_pairs={{0,2},{1,3},{2,0},{3,1},{4,6},{5,7},{6,4},{7,5},{8,10},{9,11},{10,... | collective-permute-start | bytes 1093640 | tf_op jit(solution)/shard_map/ppermute | solution.py:227

commit v23 on v22

--- a/solution.py
+++ b/solution.py
@@ -239,10 +239,10 @@
     second = [along(rest_of(first[step], strips), (step + 1) % 3) for step in range(3)]
     acc = add(None, [own, beside] + first, [(0, 0), (0, 1), (1, 0), (1, 0), (1, 0)])
     first[2], far, second, acc = lax.optimization_barrier((first[2], far, second, acc))
-    crossed = [across(each) for each in first + [far] + second]
+    crossed = [across(each) for each in first]
     acc = add(acc, crossed[:2] + [far] + second, [(1, 1), (1, 1), (0, 0), (0, 0), (0, 0), (0, 0)])
-    acc = add(acc, crossed[2:5], [(1, 1), (0, 1), (0, 1)])
-    coded = add(acc, crossed[5:], [(0, 1), (0, 1)], coded=True)
+    crossed = crossed[2:] + [across(each) for each in [far] + second]
+    coded = add(acc, crossed, [(1, 1), (0, 1), (0, 1), (0, 1), (0, 1)], coded=True)
     every = ("plane",) + seat
     tiles = tile_count // cols
     landed = lax.all_to_all(coded, every, split_axis=0, concat_axis=0, tiled=True)

time: 64.6 us -> 64.6 us (level)
  waiting for transfers between devices: 10.2 us -> 12.9 us
  starting transfers between devices: 20.5 us -> 18.8 us
  Pallas kernels: 9.78 us -> 8.95 us
    ppermute x1, waiting for transfers between devices: 0.01 us -> 1.68 us  [opposite(): lax.ppermute(values, seat, [(s, s ^ SEATS - 1 - cols) for s in range(SEAT...]
    ppermute x8, starting transfers between devices: 10.8 us -> 9.74 us  [across(): return lax.ppermute(values, seat, [(s, s ^ cols) for s in range(SEATS)])]
    ppermute x8, waiting for transfers between devices: 0.2 us -> 1.23 us  [across(): return lax.ppermute(values, seat, [(s, s ^ cols) for s in range(SEATS)])]
    pallas_call x4 -> x3, Pallas kernels: 5.11 us -> 4.28 us  [add_products(): pl.pallas_call(functools.partial(product_kernel, sizes, tile_count, passe...]
  transfers between devices with their start and end apart: 15 -> 15, of which waited for: 6 -> 9; matrix products, arithmetic and copies ran while one was open for 0% -> 0% of each run, Pallas kernels for 6% -> 5%
where the time goes in v23:
time: 64.6 us; the launch traced here: 64.4 us
  blocking collectives  23.7 us (37%)
  starting transfers between devices  18.8 us (29%)
  waiting for transfers between devices  12.9 us (20%)
  Pallas kernels  8.95 us (14%)
    all_to_all x1, blocking collectives, body(): lax.all_to_all(coded, every, split_axis=0, concat_axis=0, tiled=True)  23.7 us
    ppermute x6, waiting for transfers between devices, along(): return lax.ppermute(values, seat, hops)  10 us
    ppermute x8, starting transfers between devices, across(): return lax.ppermute(values, seat, [(s, s ^ cols) for s in range(SEATS)])  9.74 us
    ppermute x6, starting transfers between devices, along(): return lax.ppermute(values, seat, hops)  9.06 us
    pallas_call x3, Pallas kernels, add_products(): pl.pallas_call(functools.partial(product_kernel, sizes, tile_count, passe...  4.28 us
    pallas_call x1, Pallas kernels, body(): pl.pallas_call(functools.partial(pack_kernel, cols), out_shape=[jax.Shape...  2.93 us
    ppermute x1, waiting for transfers between devices, opposite(): lax.ppermute(values, seat, [(s, s ^ SEATS - 1 - cols) for s in range(SEAT...  1.68 us
  transfers between devices with their start and end apart: 15, of which 9 were waited for; matrix products, arithmetic and copies ran while one was open for 0% of the time, Pallas kernels for 5%

profile of v23, /device:TPU:1, one launch (start us, length us, event | category | flops | bytes accessed | tf_op | source)
XLA Modules:
  0.0 64.4 jit_solution(7541100334089459117)
XLA Ops:
  0.0 2.9 %pack.1 = (bf16[1424,128]{1,0:T(8,128)(2,1)}, bf16[1808,128]{1,0:T(8,128)(2,1)}, bf16[1808,128]{1,0:T(8,128)(2,1)}, bf16[1808,128]{1,0:T(8,128)(2,1)}, bf16[1424,128]{1,0:T(8,128)(2,1)}) custom-call(s32[2,4]{1,0:T(2,128)} %bitcast.3, s32[4,6]{1,0:T(4,128)} %q_ids.1, bf16[4,2,128,128]{3,2,1,0:T(8,128)(2,1)} %p_ref.1, bf16[4,6,128,128]{3,2,1,0:T(8,128)(2,1)} %q_ref.1), custom_call_target="tpu_custom_call" | custom-call | tf_op jit(solution)/shard_map/pack/pallas_call | solution.py:210
  2.9 2.0 %collective-permute-start.2 = (bf16[1808,128]{1,0:T(8,128)(2,1)}, bf16[1808,128]{1,0:T(8,128)(2,1)S(1)}, u32[]{:S(2)}, u32[]{:S(2)}) collective-permute-start(bf16[1808,128]{1,0:T(8,128)(2,1)} %get-tuple-element.18), channel_id=1, source_target_pairs={{0,1},{1,0},{2,6},{3,7},{4,5},{5,4},{6,2},{7,3},{8,9},{9,8},{10,14... | collective-permute-start | bytes 1388552 | tf_op jit(solution)/shard_map/ppermute | solution.py:224
  5.0 1.3 %collective-permute-start.4 = (bf16[1808,128]{1,0:T(8,128)(2,1)}, bf16[1808,128]{1,0:T(8,128)(2,1)S(1)}, u32[]{:S(2)}, u32[]{:S(2)}) collective-permute-start(bf16[1808,128]{1,0:T(8,128)(2,1)} %get-tuple-element.19), channel_id=1, source_target_pairs={{0,4},{1,5},{2,10},{3,11},{4,0},{5,1},{6,14},{7,15},{8,12},{9,13},... | collective-permute-start | bytes 1388552 | tf_op jit(solution)/shard_map/ppermute | solution.py:224
  6.3 1.2 %collective-permute-start = (bf16[1808,128]{1,0:T(8,128)(2,1)}, bf16[1808,128]{1,0:T(8,128)(2,1)S(1)}, u32[]{:S(2)}, u32[]{:S(2)}) collective-permute-start(bf16[1808,128]{1,0:T(8,128)(2,1)} %get-tuple-element.16), channel_id=1, source_target_pairs={{0,8},{1,9},{2,3},{3,2},{4,12},{5,13},{6,7},{7,6},{8,0},{9,1},{10,... | collective-permute-start | bytes 1388552 | tf_op jit(solution)/shard_map/ppermute | solution.py:224
  7.5 1.5 %collective-permute-start.7 = (bf16[1424,128]{1,0:T(8,128)(2,1)}, bf16[1424,128]{1,0:T(8,128)(2,1)S(1)}, u32[]{:S(2)}, u32[]{:S(2)}) collective-permute-start(bf16[1424,128]{1,0:T(8,128)(2,1)} %get-tuple-element.20.refs_0_), channel_id=1, source_target_pairs={{0,2},{1,3},{2,0},{3,1},{4,6},{5,7},{6,4},{7,5},{8,10},{9,11},{10,... | collective-permute-start | bytes 1093640 | tf_op jit(solution)/shard_map/ppermute | solution.py:227
  9.0 0.0 collective-permute-start.1
  9.0 4.3 %collective-permute-done.2.in_ref.refs_2_ = bf16[1808,128]{1,0:T(8,128)(2,1)S(1)} collective-permute-done((bf16[1808,128]{1,0:T(8,128)(2,1)}, bf16[1808,128]{1,0:T(8,128)(2,1)S(1)}, u32[]{:S(2)}, u32[]{:S(2)}) %collective-permute-start.2) | collective-permute-done | bytes 462880 | tf_op jit(solution)/shard_map/ppermute | solution.py:224
  13.4 0.2 rest_of_packet.3
  13.5 1.9 %collective-permute-start.3 = (bf16[1424,128]{1,0:T(8,128)(2,1)S(1)}, bf16[1424,128]{1,0:T(8,128)(2,1)S(1)}, u32[]{:S(2)}, u32[]{:S(2)}) collective-permute-start(bf16[1424,128]{1,0:T(8,128)(2,1)S(1)} %rest_of_packet.3), channel_id=1, source_target_pairs={{0,4},{1,5},{2,10},{3,11},{4,0},{5,1},{6,14},{7,15},{8,12},{9,13},... | collective-permute-start | bytes 1093640 | tf_op jit(solution)/shard_map/ppermute | solution.py:224
  15.4 0.0 collective-permute-done.4.in_ref.refs_3_
  15.4 0.2 rest_of_packet.4
  15.6 0.0 copy-start
  15.6 2.3 %collective-permute-start.5 = (bf16[1424,128]{1,0:T(8,128)(2,1)S(1)}, bf16[1424,128]{1,0:T(8,128)(2,1)S(1)}, u32[]{:S(2)}, u32[]{:S(2)}) collective-permute-start(bf16[1424,128]{1,0:T(8,128)(2,1)S(1)} %rest_of_packet.4), channel_id=1, source_target_pairs={{0,8},{1,9},{2,3},{3,2},{4,12},{5,13},{6,7},{7,6},{8,0},{9,1},{10,... | collective-permute-start | bytes 1093640 | tf_op jit(solution)/shard_map/ppermute | solution.py:224
  17.9 2.2 %collective-permute-done.in_ref.refs_4_ = bf16[1808,128]{1,0:T(8,128)(2,1)S(1)} collective-permute-done((bf16[1808,128]{1,0:T(8,128)(2,1)}, bf16[1808,128]{1,0:T(8,128)(2,1)S(1)}, u32[]{:S(2)}, u32[]{:S(2)}) %collective-permute-start) | collective-permute-done | bytes 462880 | tf_op jit(solution)/shard_map/ppermute | solution.py:224
  20.1 2.8 %collective-permute-start.13 = (bf16[1808,128]{1,0:T(8,128)(2,1)S(1)}, bf16[1808,128]{1,0:T(8,128)(2,1)S(1)}, u32[]{:S(2)}, u32[]{:S(2)}) collective-permute-start(bf16[1808,128]{1,0:T(8,128)(2,1)S(1)} %collective-permute-done.2.in_ref.refs_2_), channel_id=1, source_target_pairs={{0,2},{1,3},{2,0},{3,1},{4,6},{5,7},{6,4},{7,5},{8,10},{9,11},{10,... | collective-permute-start | bytes 1388552 | tf_op jit(solution)/shard_map/ppermute | solution.py:227
  22.8 0.2 rest_of_packet.5
  23.0 0.0 collective-permute-done.7.refs_1_
  23.0 0.3 collective-permute-start.6
  23.3 1.7 %collective-permute-done.1.refs_2_ = bf16[1424,128]{1,0:T(8,128)(2,1)S(1)} collective-permute-done((bf16[1424,128]{1,0:T(8,128)(2,1)}, bf16[1424,128]{1,0:T(8,128)(2,1)S(1)}, u32[]{:S(2)}, u32[]{:S(2)}) %collective-permute-start.1) | collective-permute-done | bytes 364576 | tf_op jit(solution)/shard_map/ppermute | solution.py:234
  25.0 3.5 %collective-permute-start.14 = (bf16[1808,128]{1,0:T(8,128)(2,1)S(1)}, bf16[1808,128]{1,0:T(8,128)(2,1)S(1)}, u32[]{:S(2)}, u32[]{:S(2)}) collective-permute-start(bf16[1808,128]{1,0:T(8,128)(2,1)S(1)} %collective-permute-done.4.in_ref.refs_3_), channel_id=1, source_target_pairs={{0,2},{1,3},{2,0},{3,1},{4,6},{5,7},{6,4},{7,5},{8,10},{9,11},{10,... | collective-permute-start | bytes 1388552 | tf_op jit(solution)/shard_map/ppermute | solution.py:227
  28.5 0.0 copy-done
  28.5 1.2 %products.3.refs_6_ = f32[256,8,128]{2,1,0:T(8,128)S(1)} custom-call(bf16[1424,128]{1,0:T(8,128)(2,1)S(1)} %copy-done, bf16[1424,128]{1,0:T(8,128)(2,1)S(1)} %collective-permute-done.7.refs_1_, bf16[1808,128]{1,0:T(8,128)(2,1)S(1)} %collective-permute-done.2.in_ref.refs_2_, bf16[1808,128]{1,0:T(8,128)(2,1)S(1)} %collective-permute-done.4.in_ref.refs_3_, ...), custom_call_target="tpu_custom_call" | custom-call | flops 62914560 | bytes 5242880 | tf_op jit(solution)/shard_map/products/pallas_call | solution.py:159
  29.7 0.7 %collective-permute-done.3.refs_3_ = bf16[1424,128]{1,0:T(8,128)(2,1)S(1)} collective-permute-done((bf16[1424,128]{1,0:T(8,128)(2,1)S(1)}, bf16[1424,128]{1,0:T(8,128)(2,1)S(1)}, u32[]{:S(2)}, u32[]{:S(2)}) %collective-permute-start.3) | collective-permute-done | bytes 364576 | tf_op jit(solution)/shard_map/ppermute | solution.py:224
  30.4 1.7 %collective-permute-done.5.refs_4_ = bf16[1424,128]{1,0:T(8,128)(2,1)S(1)} collective-permute-done((bf16[1424,128]{1,0:T(8,128)(2,1)S(1)}, bf16[1424,128]{1,0:T(8,128)(2,1)S(1)}, u32[]{:S(2)}, u32[]{:S(2)}) %collective-permute-start.5) | collective-permute-done | bytes 364576 | tf_op jit(solution)/shard_map/ppermute | solution.py:224
  32.1 1.1 %collective-permute-done.6.refs_5_ = bf16[1424,128]{1,0:T(8,128)(2,1)S(1)} collective-permute-done((bf16[1424,128]{1,0:T(8,128)(2,1)S(1)}, bf16[1424,128]{1,0:T(8,128)(2,1)S(1)}, u32[]{:S(2)}, u32[]{:S(2)}) %collective-permute-start.6) | collective-permute-done | bytes 364576 | tf_op jit(solution)/shard_map/ppermute | solution.py:224
  33.2 1.0 %collective-permute-start.8 = (bf16[1808,128]{1,0:T(8,128)(2,1)S(1)}, bf16[1808,128]{1,0:T(8,128)(2,1)S(1)}, u32[]{:S(2)}, u32[]{:S(2)}) collective-permute-start(bf16[1808,128]{1,0:T(8,128)(2,1)S(1)} %collective-permute-done.in_ref.refs_4_), channel_id=1, source_target_pairs={{0,2},{1,3},{2,0},{3,1},{4,6},{5,7},{6,4},{7,5},{8,10},{9,11},{10,... | collective-permute-start | bytes 1388552 | tf_op jit(solution)/shard_map/ppermute | solution.py:227
  34.2 0.0 collective-permute-start.10
  34.2 0.5 collective-permute-start.11
  34.7 0.0 collective-permute-done.13.refs_0_
  34.7 0.0 collective-permute-start.12
  34.7 0.0 collective-permute-done.14.refs_1_
  34.7 0.5 collective-permute-start.9
  35.2 1.3 %products.4.refs_5_ = f32[256,8,128]{2,1,0:T(8,128)S(1)} custom-call(bf16[1808,128]{1,0:T(8,128)(2,1)S(1)} %collective-permute-done.13.refs_0_, bf16[1808,128]{1,0:T(8,128)(2,1)S(1)} %collective-permute-done.14.refs_1_, bf16[1424,128]{1,0:T(8,128)(2,1)S(1)} %collective-permute-done.1.refs_2_, ...), custom_call_target="tpu_custom_call", output_to_operand_aliasing={{}: (6, {})} | custom-call | flops 75497472 | bytes 6291456 | tf_op jit(solution)/shard_map/products/pallas_call | solution.py:159
  36.5 0.0 collective-permute-done.10.refs_2_
  36.5 0.2 collective-permute-done.11.refs_3_
  36.7 0.5 collective-permute-done.12.refs_4_
  37.2 0.5 collective-permute-done.9.refs_1_
  37.7 0.0 collective-permute-done.8.refs_0_
  37.7 1.8 %products.5 = s32[32,5,8,128]{3,2,1,0:T(8,128)S(1)} custom-call(bf16[1808,128]{1,0:T(8,128)(2,1)S(1)} %collective-permute-done.8.refs_0_, bf16[1424,128]{1,0:T(8,128)(2,1)S(1)} %collective-permute-done.9.refs_1_, bf16[1424,128]{1,0:T(8,128)(2,1)S(1)} %collective-permute-done.10.refs_2_, bf16[1424,128]{1,0:T(8,128)(2,1)S(1)} %collective-permute-done.11.refs_3_, ...), custom_call_target="tpu_custom_call" | custom-call | flops 62914560 | bytes 5242880 | tf_op jit(solution)/shard_map/products/pallas_call | solution.py:159
  39.5 23.7 %all_to_all.5 = s32[32,5,8,128]{3,2,1,0:T(8,128)S(1)} all-to-all(s32[32,5,8,128]{3,2,1,0:T(8,128)S(1)} %products.5), channel_id=1, replica_groups=mesh['plane'=2,'pair'=4,'core'=2,'col'=2] {'plane','pair','core','col'}, dimensions={0} | all-to-all | bytes 1310720 | tf_op jit(solution)/shard_map/all_to_all | solution.py:248
  63.2 1.3 %turn.1 = f32[128,1024]{1,0:T(8,128)} custom-call(s32[2,16,5,8,128]{4,3,2,1,0:T(8,128)S(1)} %bitcast.2), custom_call_target="tpu_custom_call" | custom-call | tf_op jit(solution)/shard_map/turn/pallas_call | solution.py:249
Async XLA Ops:
  2.9 10.4 %collective-permute-start.2 = (bf16[1808,128]{1,0:T(8,128)(2,1)}, bf16[1808,128]{1,0:T(8,128)(2,1)S(1)}, u32[]{:S(2)}, u32[]{:S(2)}) collective-permute-start(bf16[1808,128]{1,0:T(8,128)(2,1)} %get-tuple-element.18), channel_id=1, source_target_pairs={{0,1},{1,0},{2,6},{3,7},{4,5},{5,4},{6,2},{7,3},{8,9},{9,8},{10,14... | collective-permute-start | bytes 1388552 | tf_op jit(solution)/shard_map/ppermute | solution.py:224
  5.0 10.4 %collective-permute-start.4 = (bf16[1808,128]{1,0:T(8,128)(2,1)}, bf16[1808,128]{1,0:T(8,128)(2,1)S(1)}, u32[]{:S(2)}, u32[]{:S(2)}) collective-permute-start(bf16[1808,128]{1,0:T(8,128)(2,1)} %get-tuple-element.19), channel_id=1, source_target_pairs={{0,4},{1,5},{2,10},{3,11},{4,0},{5,1},{6,14},{7,15},{8,12},{9,13},... | collective-permute-start | bytes 1388552 | tf_op jit(solution)/shard_map/ppermute | solution.py:224
  6.3 13.8 %collective-permute-start = (bf16[1808,128]{1,0:T(8,128)(2,1)}, bf16[1808,128]{1,0:T(8,128)(2,1)S(1)}, u32[]{:S(2)}, u32[]{:S(2)}) collective-permute-start(bf16[1808,128]{1,0:T(8,128)(2,1)} %get-tuple-element.16), channel_id=1, source_target_pairs={{0,8},{1,9},{2,3},{3,2},{4,12},{5,13},{6,7},{7,6},{8,0},{9,1},{10,... | collective-permute-start | bytes 1388552 | tf_op jit(solution)/shard_map/ppermute | solution.py:224
  7.5 15.5 %collective-permute-start.7 = (bf16[1424,128]{1,0:T(8,128)(2,1)}, bf16[1424,128]{1,0:T(8,128)(2,1)S(1)}, u32[]{:S(2)}, u32[]{:S(2)}) collective-permute-start(bf16[1424,128]{1,0:T(8,128)(2,1)} %get-tuple-element.20.refs_0_), channel_id=1, source_target_pairs={{0,2},{1,3},{2,0},{3,1},{4,6},{5,7},{6,4},{7,5},{8,10},{9,11},{10,... | collective-permute-start | bytes 1093640 | tf_op jit(solution)/shard_map/ppermute | solution.py:227
  9.0 16.0 %collective-permute-start.1 = (bf16[1424,128]{1,0:T(8,128)(2,1)}, bf16[1424,128]{1,0:T(8,128)(2,1)S(1)}, u32[]{:S(2)}, u32[]{:S(2)}) collective-permute-start(bf16[1424,128]{1,0:T(8,128)(2,1)} %get-tuple-element.17), channel_id=1, source_target_pairs={{0,13},{1,12},{2,15},{3,14},{4,9},{5,8},{6,11},{7,10},{8,5},{9,4},... | collective-permute-start | bytes 1093640 | tf_op jit(solution)/shard_map/ppermute | solution.py:234
  13.5 16.9 %collective-permute-start.3 = (bf16[1424,128]{1,0:T(8,128)(2,1)S(1)}, bf16[1424,128]{1,0:T(8,128)(2,1)S(1)}, u32[]{:S(2)}, u32[]{:S(2)}) collective-permute-start(bf16[1424,128]{1,0:T(8,128)(2,1)S(1)} %rest_of_packet.3), channel_id=1, source_target_pairs={{0,4},{1,5},{2,10},{3,11},{4,0},{5,1},{6,14},{7,15},{8,12},{9,13},... | collective-permute-start | bytes 1093640 | tf_op jit(solution)/shard_map/ppermute | solution.py:224
  15.6 12.9 %copy-start = (bf16[1424,128]{1,0:T(8,128)(2,1)S(1)}, bf16[1424,128]{1,0:T(8,128)(2,1)}, u32[]{:S(2)}) copy-start(bf16[1424,128]{1,0:T(8,128)(2,1)} %get-tuple-element.20.refs_0_) | copy-start | bytes 1093636
  15.6 16.5 %collective-permute-start.5 = (bf16[1424,128]{1,0:T(8,128)(2,1)S(1)}, bf16[1424,128]{1,0:T(8,128)(2,1)S(1)}, u32[]{:S(2)}, u32[]{:S(2)}) collective-permute-start(bf16[1424,128]{1,0:T(8,128)(2,1)S(1)} %rest_of_packet.4), channel_id=1, source_target_pairs={{0,8},{1,9},{2,3},{3,2},{4,12},{5,13},{6,7},{7,6},{8,0},{9,1},{10,... | collective-permute-start | bytes 1093640 | tf_op jit(solution)/shard_map/ppermute | solution.py:224
  20.1 14.6 %collective-permute-start.13 = (bf16[1808,128]{1,0:T(8,128)(2,1)S(1)}, bf16[1808,128]{1,0:T(8,128)(2,1)S(1)}, u32[]{:S(2)}, u32[]{:S(2)}) collective-permute-start(bf16[1808,128]{1,0:T(8,128)(2,1)S(1)} %collective-permute-done.2.in_ref.refs_2_), channel_id=1, source_target_pairs={{0,2},{1,3},{2,0},{3,1},{4,6},{5,7},{6,4},{7,5},{8,10},{9,11},{10,... | collective-permute-start | bytes 1388552 | tf_op jit(solution)/shard_map/ppermute | solution.py:227
  23.0 10.2 %collective-permute-start.6 = (bf16[1424,128]{1,0:T(8,128)(2,1)S(1)}, bf16[1424,128]{1,0:T(8,128)(2,1)S(1)}, u32[]{:S(2)}, u32[]{:S(2)}) collective-permute-start(bf16[1424,128]{1,0:T(8,128)(2,1)S(1)} %rest_of_packet.5), channel_id=1, source_target_pairs={{0,1},{1,0},{2,6},{3,7},{4,5},{5,4},{6,2},{7,3},{8,9},{9,8},{10,14... | collective-permute-start | bytes 1093640 | tf_op jit(solution)/shard_map/ppermute | solution.py:224
  25.0 9.7 %collective-permute-start.14 = (bf16[1808,128]{1,0:T(8,128)(2,1)S(1)}, bf16[1808,128]{1,0:T(8,128)(2,1)S(1)}, u32[]{:S(2)}, u32[]{:S(2)}) collective-permute-start(bf16[1808,128]{1,0:T(8,128)(2,1)S(1)} %collective-permute-done.4.in_ref.refs_3_), channel_id=1, source_target_pairs={{0,2},{1,3},{2,0},{3,1},{4,6},{5,7},{6,4},{7,5},{8,10},{9,11},{10,... | collective-permute-start | bytes 1388552 | tf_op jit(solution)/shard_map/ppermute | solution.py:227
  33.2 4.5 %collective-permute-start.8 = (bf16[1808,128]{1,0:T(8,128)(2,1)S(1)}, bf16[1808,128]{1,0:T(8,128)(2,1)S(1)}, u32[]{:S(2)}, u32[]{:S(2)}) collective-permute-start(bf16[1808,128]{1,0:T(8,128)(2,1)S(1)} %collective-permute-done.in_ref.refs_4_), channel_id=1, source_target_pairs={{0,2},{1,3},{2,0},{3,1},{4,6},{5,7},{6,4},{7,5},{8,10},{9,11},{10,... | collective-permute-start | bytes 1388552 | tf_op jit(solution)/shard_map/ppermute | solution.py:227
  34.2 2.3 %collective-permute-start.10 = (bf16[1424,128]{1,0:T(8,128)(2,1)S(1)}, bf16[1424,128]{1,0:T(8,128)(2,1)S(1)}, u32[]{:S(2)}, u32[]{:S(2)}) collective-permute-start(bf16[1424,128]{1,0:T(8,128)(2,1)S(1)} %collective-permute-done.3.refs_3_), channel_id=1, source_target_pairs={{0,2},{1,3},{2,0},{3,1},{4,6},{5,7},{6,4},{7,5},{8,10},{9,11},{10,... | collective-permute-start | bytes 1093640 | tf_op jit(solution)/shard_map/ppermute | solution.py:227
  34.2 2.5 %collective-permute-start.11 = (bf16[1424,128]{1,0:T(8,128)(2,1)S(1)}, bf16[1424,128]{1,0:T(8,128)(2,1)S(1)}, u32[]{:S(2)}, u32[]{:S(2)}) collective-permute-start(bf16[1424,128]{1,0:T(8,128)(2,1)S(1)} %collective-permute-done.5.refs_4_), channel_id=1, source_target_pairs={{0,2},{1,3},{2,0},{3,1},{4,6},{5,7},{6,4},{7,5},{8,10},{9,11},{10,... | collective-permute-start | bytes 1093640 | tf_op jit(solution)/shard_map/ppermute | solution.py:227
  34.7 2.5 %collective-permute-start.12 = (bf16[1424,128]{1,0:T(8,128)(2,1)S(1)}, bf16[1424,128]{1,0:T(8,128)(2,1)S(1)}, u32[]{:S(2)}, u32[]{:S(2)}) collective-permute-start(bf16[1424,128]{1,0:T(8,128)(2,1)S(1)} %collective-permute-done.6.refs_5_), channel_id=1, source_target_pairs={{0,2},{1,3},{2,0},{3,1},{4,6},{5,7},{6,4},{7,5},{8,10},{9,11},{10,... | collective-permute-start | bytes 1093640 | tf_op jit(solution)/shard_map/ppermute | solution.py:227
  34.7 3.0 %collective-permute-start.9 = (bf16[1424,128]{1,0:T(8,128)(2,1)S(1)}, bf16[1424,128]{1,0:T(8,128)(2,1)S(1)}, u32[]{:S(2)}, u32[]{:S(2)}) collective-permute-start(bf16[1424,128]{1,0:T(8,128)(2,1)S(1)} %collective-permute-done.1.refs_2_), channel_id=1, source_target_pairs={{0,2},{1,3},{2,0},{3,1},{4,6},{5,7},{6,4},{7,5},{8,10},{9,11},{10,... | collective-permute-start | bytes 1093640 | tf_op jit(solution)/shard_map/ppermute | solution.py:227

commit v24 on v18

--- a/solution.py
+++ b/solution.py
@@ -237,15 +237,18 @@
     beside = across(own)
     far = opposite(out[3])
     second = [along(rest_of(first[step], strips), (step + 1) % 3) for step in range(3)]
-    acc = add(None, [own, beside] + first, [(0, 0), (0, 1), (1, 0), (1, 0), (1, 0)])
+    crossed = [across(first[0])]
+    acc = add(
+        None, [own, beside] + first + crossed, [(0, 0), (0, 1), (1, 0), (1, 0), (1, 0), (1, 1)]
+    )
     first[2], second, acc = lax.optimization_barrier((first[2], second, acc))
     acc = add(
         acc,
-        [far, across(far), across(first[0])] + second,
+        [far, across(far), across(first[1])] + second,
         [(0, 0), (0, 1), (1, 1), (0, 0), (0, 0), (0, 0)],
     )
-    crossed = [across(each) for each in first[1:] + second]
-    coded = add(acc, crossed, [(1, 1), (1, 1), (0, 1), (0, 1), (0, 1)], coded=True)
+    crossed = [across(each) for each in [first[2]] + second]
+    coded = add(acc, crossed, [(1, 1), (0, 1), (0, 1), (0, 1)], coded=True)
     every = ("plane",) + seat
     tiles = tile_count // cols
     landed = lax.all_to_all(coded, every, split_axis=0, concat_axis=0, tiled=True)

time: 64.9 us -> 64.7 us (level)
  waiting for transfers between devices: 8.37 us -> 10.6 us
  starting transfers between devices: 22.8 us -> 21.3 us
  blocking collectives: 24.5 us -> 23.5 us
    ppermute x8, starting transfers between devices: 13.1 us -> 9.7 us  [across(): return lax.ppermute(values, seat, [(s, s ^ cols) for s in range(SEATS)])]
    ppermute x6, waiting for transfers between devices: 7.22 us -> 9.2 us  [along(): return lax.ppermute(values, seat, hops)]
    ppermute x6, starting transfers between devices: 9.7 us -> 11.6 us  [along(): return lax.ppermute(values, seat, hops)]
    all_to_all x1, blocking collectives: 24.5 us -> 23.5 us  [body(): lax.all_to_all(coded, every, split_axis=0, concat_axis=0, tiled=True)]
  transfers between devices with their start and end apart: 15 -> 15, of which waited for: 6 -> 7; matrix products, arithmetic and copies ran while one was open for 0% -> 0% of each run, Pallas kernels for 5% -> 5%
where the time goes in v24:
time: 64.7 us; the launch traced here: 64.5 us
  blocking collectives  23.5 us (36%)
  starting transfers between devices  21.3 us (33%)
  waiting for transfers between devices  10.6 us (16%)
  Pallas kernels  8.97 us (14%)
    all_to_all x1, blocking collectives, body(): lax.all_to_all(coded, every, split_axis=0, concat_axis=0, tiled=True)  23.5 us
    ppermute x6, starting transfers between devices, along(): return lax.ppermute(values, seat, hops)  11.6 us
    ppermute x8, starting transfers between devices, across(): return lax.ppermute(values, seat, [(s, s ^ cols) for s in range(SEATS)])  9.7 us
    ppermute x6, waiting for transfers between devices, along(): return lax.ppermute(values, seat, hops)  9.2 us
    pallas_call x3, Pallas kernels, add_products(): pl.pallas_call(functools.partial(product_kernel, sizes, tile_count, passe...  4.31 us
    pallas_call x1, Pallas kernels, body(): pl.pallas_call(functools.partial(pack_kernel, cols), out_shape=[jax.Shape...  2.93 us
  transfers between devices with their start and end apart: 15, of which 7 were waited for; matrix products, arithmetic and copies ran while one was open for 0% of the time, Pallas kernels for 5%

profile of v24, /device:TPU:1, one launch (start us, length us, event | category | flops | bytes accessed | tf_op | source)
XLA Modules:
  0.0 64.5 jit_solution(6392223362896705880)
XLA Ops:
  0.0 2.9 %pack.1 = (bf16[1424,128]{1,0:T(8,128)(2,1)}, bf16[1808,128]{1,0:T(8,128)(2,1)}, bf16[1808,128]{1,0:T(8,128)(2,1)}, bf16[1808,128]{1,0:T(8,128)(2,1)}, bf16[1424,128]{1,0:T(8,128)(2,1)}) custom-call(s32[2,4]{1,0:T(2,128)} %bitcast.3, s32[4,6]{1,0:T(4,128)} %q_ids.1, bf16[4,2,128,128]{3,2,1,0:T(8,128)(2,1)} %p_ref.1, bf16[4,6,128,128]{3,2,1,0:T(8,128)(2,1)} %q_ref.1), custom_call_target="tpu_custom_call" | custom-call | tf_op jit(solution)/shard_map/pack/pallas_call | solution.py:210
  2.9 2.0 %collective-permute-start.1 = (bf16[1808,128]{1,0:T(8,128)(2,1)}, bf16[1808,128]{1,0:T(8,128)(2,1)S(1)}, u32[]{:S(2)}, u32[]{:S(2)}) collective-permute-start(bf16[1808,128]{1,0:T(8,128)(2,1)} %get-tuple-element.16), channel_id=1, source_target_pairs={{0,1},{1,0},{2,6},{3,7},{4,5},{5,4},{6,2},{7,3},{8,9},{9,8},{10,14... | collective-permute-start | bytes 1388552 | tf_op jit(solution)/shard_map/ppermute | solution.py:224
  5.0 1.3 %collective-permute-start.3 = (bf16[1808,128]{1,0:T(8,128)(2,1)}, bf16[1808,128]{1,0:T(8,128)(2,1)S(1)}, u32[]{:S(2)}, u32[]{:S(2)}) collective-permute-start(bf16[1808,128]{1,0:T(8,128)(2,1)} %get-tuple-element.17), channel_id=1, source_target_pairs={{0,4},{1,5},{2,10},{3,11},{4,0},{5,1},{6,14},{7,15},{8,12},{9,13},... | collective-permute-start | bytes 1388552 | tf_op jit(solution)/shard_map/ppermute | solution.py:224
  6.3 1.2 %collective-permute-start = (bf16[1808,128]{1,0:T(8,128)(2,1)}, bf16[1808,128]{1,0:T(8,128)(2,1)S(1)}, u32[]{:S(2)}, u32[]{:S(2)}) collective-permute-start(bf16[1808,128]{1,0:T(8,128)(2,1)} %get-tuple-element.15), channel_id=1, source_target_pairs={{0,8},{1,9},{2,3},{3,2},{4,12},{5,13},{6,7},{7,6},{8,0},{9,1},{10,... | collective-permute-start | bytes 1388552 | tf_op jit(solution)/shard_map/ppermute | solution.py:224
  7.5 1.5 %collective-permute-start.6 = (bf16[1424,128]{1,0:T(8,128)(2,1)}, bf16[1424,128]{1,0:T(8,128)(2,1)S(1)}, u32[]{:S(2)}, u32[]{:S(2)}) collective-permute-start(bf16[1424,128]{1,0:T(8,128)(2,1)} %get-tuple-element.18.refs_0_), channel_id=1, source_target_pairs={{0,2},{1,3},{2,0},{3,1},{4,6},{5,7},{6,4},{7,5},{8,10},{9,11},{10,... | collective-permute-start | bytes 1093640 | tf_op jit(solution)/shard_map/ppermute | solution.py:227
  9.0 0.0 collective-permute-start.12
  9.0 4.3 %collective-permute-done.1.in_ref.refs_2_ = bf16[1808,128]{1,0:T(8,128)(2,1)S(1)} collective-permute-done((bf16[1808,128]{1,0:T(8,128)(2,1)}, bf16[1808,128]{1,0:T(8,128)(2,1)S(1)}, u32[]{:S(2)}, u32[]{:S(2)}) %collective-permute-start.1) | collective-permute-done | bytes 462880 | tf_op jit(solution)/shard_map/ppermute | solution.py:224
  13.4 3.9 %collective-permute-start.7 = (bf16[1808,128]{1,0:T(8,128)(2,1)S(1)}, bf16[1808,128]{1,0:T(8,128)(2,1)S(1)}, u32[]{:S(2)}, u32[]{:S(2)}) collective-permute-start(bf16[1808,128]{1,0:T(8,128)(2,1)S(1)} %collective-permute-done.1.in_ref.refs_2_), channel_id=1, source_target_pairs={{0,2},{1,3},{2,0},{3,1},{4,6},{5,7},{6,4},{7,5},{8,10},{9,11},{10,... | collective-permute-start | bytes 1388552 | tf_op jit(solution)/shard_map/ppermute | solution.py:227
  17.3 0.2 rest_of_packet.3
  17.4 0.0 collective-permute-done.3.in_ref.refs_3_
  17.4 3.4 %collective-permute-start.2 = (bf16[1424,128]{1,0:T(8,128)(2,1)S(1)}, bf16[1424,128]{1,0:T(8,128)(2,1)S(1)}, u32[]{:S(2)}, u32[]{:S(2)}) collective-permute-start(bf16[1424,128]{1,0:T(8,128)(2,1)S(1)} %rest_of_packet.3), channel_id=1, source_target_pairs={{0,4},{1,5},{2,10},{3,11},{4,0},{5,1},{6,14},{7,15},{8,12},{9,13},... | collective-permute-start | bytes 1093640 | tf_op jit(solution)/shard_map/ppermute | solution.py:224
  20.8 0.2 rest_of_packet.4
  21.0 0.0 copy-start
  21.0 0.0 collective-permute-done.in_ref.refs_4_
  21.0 3.6 %collective-permute-start.4 = (bf16[1424,128]{1,0:T(8,128)(2,1)S(1)}, bf16[1424,128]{1,0:T(8,128)(2,1)S(1)}, u32[]{:S(2)}, u32[]{:S(2)}) collective-permute-start(bf16[1424,128]{1,0:T(8,128)(2,1)S(1)} %rest_of_packet.4), channel_id=1, source_target_pairs={{0,8},{1,9},{2,3},{3,2},{4,12},{5,13},{6,7},{7,6},{8,0},{9,1},{10,... | collective-permute-start | bytes 1093640 | tf_op jit(solution)/shard_map/ppermute | solution.py:224
  24.6 0.2 rest_of_packet.5
  24.8 0.0 collective-permute-done.6.refs_1_
  24.8 0.1 collective-permute-start.5
  24.8 0.2 collective-permute-done.12.refs_0_
  25.0 3.2 %collective-permute-start.13 = (bf16[1424,128]{1,0:T(8,128)(2,1)S(1)}, bf16[1424,128]{1,0:T(8,128)(2,1)S(1)}, u32[]{:S(2)}, u32[]{:S(2)}) collective-permute-start(bf16[1424,128]{1,0:T(8,128)(2,1)S(1)} %collective-permute-done.12.refs_0_), channel_id=1, source_target_pairs={{0,2},{1,3},{2,0},{3,1},{4,6},{5,7},{6,4},{7,5},{8,10},{9,11},{10,... | collective-permute-start | bytes 1093640 | tf_op jit(solution)/shard_map/ppermute | solution.py:227
  28.2 0.0 collective-permute-done.7.refs_5_
  28.2 0.0 collective-permute-start.14
  28.2 0.0 copy-done
  28.2 1.3 %products.3.refs_6_ = f32[256,8,128]{2,1,0:T(8,128)S(1)} custom-call(bf16[1424,128]{1,0:T(8,128)(2,1)S(1)} %copy-done, bf16[1424,128]{1,0:T(8,128)(2,1)S(1)} %collective-permute-done.6.refs_1_, bf16[1808,128]{1,0:T(8,128)(2,1)S(1)} %collective-permute-done.1.in_ref.refs_2_, bf16[1808,128]{1,0:T(8,128)(2,1)S(1)} %collective-permute-done.3.in_ref.refs_3_, ...), custom_call_target="tpu_custom_call" | custom-call | flops 75497472 | bytes 6291456 | tf_op jit(solution)/shard_map/products/pallas_call | solution.py:159
  29.6 0.9 %collective-permute-done.2.refs_3_ = bf16[1424,128]{1,0:T(8,128)(2,1)S(1)} collective-permute-done((bf16[1424,128]{1,0:T(8,128)(2,1)S(1)}, bf16[1424,128]{1,0:T(8,128)(2,1)S(1)}, u32[]{:S(2)}, u32[]{:S(2)}) %collective-permute-start.2) | collective-permute-done | bytes 364576 | tf_op jit(solution)/shard_map/ppermute | solution.py:224
  30.4 4.0 %collective-permute-done.4.refs_4_ = bf16[1424,128]{1,0:T(8,128)(2,1)S(1)} collective-permute-done((bf16[1424,128]{1,0:T(8,128)(2,1)S(1)}, bf16[1424,128]{1,0:T(8,128)(2,1)S(1)}, u32[]{:S(2)}, u32[]{:S(2)}) %collective-permute-start.4) | collective-permute-done | bytes 364576 | tf_op jit(solution)/shard_map/ppermute | solution.py:224
  34.4 0.0 collective-permute-done.5.refs_5_
  34.4 0.6 collective-permute-start.8
  35.0 0.0 collective-permute-start.10
  35.0 0.5 collective-permute-start.11
  35.5 0.0 collective-permute-done.13.refs_1_
  35.5 0.0 collective-permute-start.9
  35.5 0.0 collective-permute-done.14.refs_2_
  35.5 1.3 %products.4.refs_4_ = f32[256,8,128]{2,1,0:T(8,128)S(1)} custom-call(bf16[1424,128]{1,0:T(8,128)(2,1)S(1)} %collective-permute-done.12.refs_0_, bf16[1424,128]{1,0:T(8,128)(2,1)S(1)} %collective-permute-done.13.refs_1_, bf16[1808,128]{1,0:T(8,128)(2,1)S(1)} %collective-permute-done.14.refs_2_, ...), custom_call_target="tpu_custom_call", output_to_operand_aliasing={{}: (6, {})} | custom-call | flops 75497472 | bytes 6291456 | tf_op jit(solution)/shard_map/products/pallas_call | solution.py:159
  36.8 0.2 collective-permute-done.10.refs_2_
  37.0 0.5 collective-permute-done.11.refs_3_
  37.5 0.5 collective-permute-done.9.refs_1_
  38.0 0.0 collective-permute-done.8.refs_0_
  38.0 1.7 %products.5 = s32[32,5,8,128]{3,2,1,0:T(8,128)S(1)} custom-call(bf16[1808,128]{1,0:T(8,128)(2,1)S(1)} %collective-permute-done.8.refs_0_, bf16[1424,128]{1,0:T(8,128)(2,1)S(1)} %collective-permute-done.9.refs_1_, bf16[1424,128]{1,0:T(8,128)(2,1)S(1)} %collective-permute-done.10.refs_2_, bf16[1424,128]{1,0:T(8,128)(2,1)S(1)} %collective-permute-done.11.refs_3_, ...), custom_call_target="tpu_custom_call" | custom-call | flops 50331648 | bytes 4194304 | tf_op jit(solution)/shard_map/products/pallas_call | solution.py:159
  39.7 23.5 %all_to_all.5 = s32[32,5,8,128]{3,2,1,0:T(8,128)S(1)} all-to-all(s32[32,5,8,128]{3,2,1,0:T(8,128)S(1)} %products.5), channel_id=1, replica_groups=mesh['plane'=2,'pair'=4,'core'=2,'col'=2] {'plane','pair','core','col'}, dimensions={0} | all-to-all | bytes 1310720 | tf_op jit(solution)/shard_map/all_to_all | solution.py:254
  63.3 1.3 %turn.1 = f32[128,1024]{1,0:T(8,128)} custom-call(s32[2,16,5,8,128]{4,3,2,1,0:T(8,128)S(1)} %bitcast.2), custom_call_target="tpu_custom_call" | custom-call | tf_op jit(solution)/shard_map/turn/pallas_call | solution.py:255
Async XLA Ops:
  2.9 10.4 %collective-permute-start.1 = (bf16[1808,128]{1,0:T(8,128)(2,1)}, bf16[1808,128]{1,0:T(8,128)(2,1)S(1)}, u32[]{:S(2)}, u32[]{:S(2)}) collective-permute-start(bf16[1808,128]{1,0:T(8,128)(2,1)} %get-tuple-element.16), channel_id=1, source_target_pairs={{0,1},{1,0},{2,6},{3,7},{4,5},{5,4},{6,2},{7,3},{8,9},{9,8},{10,14... | collective-permute-start | bytes 1388552 | tf_op jit(solution)/shard_map/ppermute | solution.py:224
  5.0 12.5 %collective-permute-start.3 = (bf16[1808,128]{1,0:T(8,128)(2,1)}, bf16[1808,128]{1,0:T(8,128)(2,1)S(1)}, u32[]{:S(2)}, u32[]{:S(2)}) collective-permute-start(bf16[1808,128]{1,0:T(8,128)(2,1)} %get-tuple-element.17), channel_id=1, source_target_pairs={{0,4},{1,5},{2,10},{3,11},{4,0},{5,1},{6,14},{7,15},{8,12},{9,13},... | collective-permute-start | bytes 1388552 | tf_op jit(solution)/shard_map/ppermute | solution.py:224
  6.3 14.7 %collective-permute-start = (bf16[1808,128]{1,0:T(8,128)(2,1)}, bf16[1808,128]{1,0:T(8,128)(2,1)S(1)}, u32[]{:S(2)}, u32[]{:S(2)}) collective-permute-start(bf16[1808,128]{1,0:T(8,128)(2,1)} %get-tuple-element.15), channel_id=1, source_target_pairs={{0,8},{1,9},{2,3},{3,2},{4,12},{5,13},{6,7},{7,6},{8,0},{9,1},{10,... | collective-permute-start | bytes 1388552 | tf_op jit(solution)/shard_map/ppermute | solution.py:224
  7.5 17.2 %collective-permute-start.6 = (bf16[1424,128]{1,0:T(8,128)(2,1)}, bf16[1424,128]{1,0:T(8,128)(2,1)S(1)}, u32[]{:S(2)}, u32[]{:S(2)}) collective-permute-start(bf16[1424,128]{1,0:T(8,128)(2,1)} %get-tuple-element.18.refs_0_), channel_id=1, source_target_pairs={{0,2},{1,3},{2,0},{3,1},{4,6},{5,7},{6,4},{7,5},{8,10},{9,11},{10,... | collective-permute-start | bytes 1093640 | tf_op jit(solution)/shard_map/ppermute | solution.py:227
  9.0 16.0 %collective-permute-start.12 = (bf16[1424,128]{1,0:T(8,128)(2,1)}, bf16[1424,128]{1,0:T(8,128)(2,1)S(1)}, u32[]{:S(2)}, u32[]{:S(2)}) collective-permute-start(bf16[1424,128]{1,0:T(8,128)(2,1)} %get-tuple-element.23), channel_id=1, source_target_pairs={{0,13},{1,12},{2,15},{3,14},{4,9},{5,8},{6,11},{7,10},{8,5},{9,4},... | collective-permute-start | bytes 1093640 | tf_op jit(solution)/shard_map/ppermute | solution.py:234
  13.4 14.8 %collective-permute-start.7 = (bf16[1808,128]{1,0:T(8,128)(2,1)S(1)}, bf16[1808,128]{1,0:T(8,128)(2,1)S(1)}, u32[]{:S(2)}, u32[]{:S(2)}) collective-permute-start(bf16[1808,128]{1,0:T(8,128)(2,1)S(1)} %collective-permute-done.1.in_ref.refs_2_), channel_id=1, source_target_pairs={{0,2},{1,3},{2,0},{3,1},{4,6},{5,7},{6,4},{7,5},{8,10},{9,11},{10,... | collective-permute-start | bytes 1388552 | tf_op jit(solution)/shard_map/ppermute | solution.py:227
  17.4 13.0 %collective-permute-start.2 = (bf16[1424,128]{1,0:T(8,128)(2,1)S(1)}, bf16[1424,128]{1,0:T(8,128)(2,1)S(1)}, u32[]{:S(2)}, u32[]{:S(2)}) collective-permute-start(bf16[1424,128]{1,0:T(8,128)(2,1)S(1)} %rest_of_packet.3), channel_id=1, source_target_pairs={{0,4},{1,5},{2,10},{3,11},{4,0},{5,1},{6,14},{7,15},{8,12},{9,13},... | collective-permute-start | bytes 1093640 | tf_op jit(solution)/shard_map/ppermute | solution.py:224
  21.0 7.2 %copy-start = (bf16[1424,128]{1,0:T(8,128)(2,1)S(1)}, bf16[1424,128]{1,0:T(8,128)(2,1)}, u32[]{:S(2)}) copy-start(bf16[1424,128]{1,0:T(8,128)(2,1)} %get-tuple-element.18.refs_0_) | copy-start | bytes 1093636
  21.0 13.4 %collective-permute-start.4 = (bf16[1424,128]{1,0:T(8,128)(2,1)S(1)}, bf16[1424,128]{1,0:T(8,128)(2,1)S(1)}, u32[]{:S(2)}, u32[]{:S(2)}) collective-permute-start(bf16[1424,128]{1,0:T(8,128)(2,1)S(1)} %rest_of_packet.4), channel_id=1, source_target_pairs={{0,8},{1,9},{2,3},{3,2},{4,12},{5,13},{6,7},{7,6},{8,0},{9,1},{10,... | collective-permute-start | bytes 1093640 | tf_op jit(solution)/shard_map/ppermute | solution.py:224
  24.8 9.7 %collective-permute-start.5 = (bf16[1424,128]{1,0:T(8,128)(2,1)S(1)}, bf16[1424,128]{1,0:T(8,128)(2,1)S(1)}, u32[]{:S(2)}, u32[]{:S(2)}) collective-permute-start(bf16[1424,128]{1,0:T(8,128)(2,1)S(1)} %rest_of_packet.5), channel_id=1, source_target_pairs={{0,1},{1,0},{2,6},{3,7},{4,5},{5,4},{6,2},{7,3},{8,9},{9,8},{10,14... | collective-permute-start | bytes 1093640 | tf_op jit(solution)/shard_map/ppermute | solution.py:224
  25.0 10.5 %collective-permute-start.13 = (bf16[1424,128]{1,0:T(8,128)(2,1)S(1)}, bf16[1424,128]{1,0:T(8,128)(2,1)S(1)}, u32[]{:S(2)}, u32[]{:S(2)}) collective-permute-start(bf16[1424,128]{1,0:T(8,128)(2,1)S(1)} %collective-permute-done.12.refs_0_), channel_id=1, source_target_pairs={{0,2},{1,3},{2,0},{3,1},{4,6},{5,7},{6,4},{7,5},{8,10},{9,11},{10,... | collective-permute-start | bytes 1093640 | tf_op jit(solution)/shard_map/ppermute | solution.py:227
  28.2 7.3 %collective-permute-start.14 = (bf16[1808,128]{1,0:T(8,128)(2,1)S(1)}, bf16[1808,128]{1,0:T(8,128)(2,1)S(1)}, u32[]{:S(2)}, u32[]{:S(2)}) collective-permute-start(bf16[1808,128]{1,0:T(8,128)(2,1)S(1)} %collective-permute-done.3.in_ref.refs_3_), channel_id=1, source_target_pairs={{0,2},{1,3},{2,0},{3,1},{4,6},{5,7},{6,4},{7,5},{8,10},{9,11},{10,... | collective-permute-start | bytes 1388552 | tf_op jit(solution)/shard_map/ppermute | solution.py:227
  34.4 3.6 %collective-permute-start.8 = (bf16[1808,128]{1,0:T(8,128)(2,1)S(1)}, bf16[1808,128]{1,0:T(8,128)(2,1)S(1)}, u32[]{:S(2)}, u32[]{:S(2)}) collective-permute-start(bf16[1808,128]{1,0:T(8,128)(2,1)S(1)} %collective-permute-done.in_ref.refs_4_), channel_id=1, source_target_pairs={{0,2},{1,3},{2,0},{3,1},{4,6},{5,7},{6,4},{7,5},{8,10},{9,11},{10,... | collective-permute-start | bytes 1388552 | tf_op jit(solution)/shard_map/ppermute | solution.py:227
  35.0 2.0 %collective-permute-start.10 = (bf16[1424,128]{1,0:T(8,128)(2,1)S(1)}, bf16[1424,128]{1,0:T(8,128)(2,1)S(1)}, u32[]{:S(2)}, u32[]{:S(2)}) collective-permute-start(bf16[1424,128]{1,0:T(8,128)(2,1)S(1)} %collective-permute-done.4.refs_4_), channel_id=1, source_target_pairs={{0,2},{1,3},{2,0},{3,1},{4,6},{5,7},{6,4},{7,5},{8,10},{9,11},{10,... | collective-permute-start | bytes 1093640 | tf_op jit(solution)/shard_map/ppermute | solution.py:227
  35.0 2.5 %collective-permute-start.11 = (bf16[1424,128]{1,0:T(8,128)(2,1)S(1)}, bf16[1424,128]{1,0:T(8,128)(2,1)S(1)}, u32[]{:S(2)}, u32[]{:S(2)}) collective-permute-start(bf16[1424,128]{1,0:T(8,128)(2,1)S(1)} %collective-permute-done.5.refs_5_), channel_id=1, source_target_pairs={{0,2},{1,3},{2,0},{3,1},{4,6},{5,7},{6,4},{7,5},{8,10},{9,11},{10,... | collective-permute-start | bytes 1093640 | tf_op jit(solution)/shard_map/ppermute | solution.py:227
  35.5 2.5 %collective-permute-start.9 = (bf16[1424,128]{1,0:T(8,128)(2,1)S(1)}, bf16[1424,128]{1,0:T(8,128)(2,1)S(1)}, u32[]{:S(2)}, u32[]{:S(2)}) collective-permute-start(bf16[1424,128]{1,0:T(8,128)(2,1)S(1)} %collective-permute-done.2.refs_3_), channel_id=1, source_target_pairs={{0,2},{1,3},{2,0},{3,1},{4,6},{5,7},{6,4},{7,5},{8,10},{9,11},{10,... | collective-permute-start | bytes 1093640 | tf_op jit(solution)/shard_map/ppermute | solution.py:227

commit v25 on v23

--- a/solution.py
+++ b/solution.py
@@ -99,15 +99,19 @@
         acc_ref[...] = jnp.zeros_like(acc_ref)
     else:
         acc_ref[...] = refs[count][...]
+
+    def multiply(i, f):
+        tiles, mine = places[i]
+        left = packets[i][mine + f * rows:mine + (f + 1) * rows]
+        base = tiles + f * per_p * extent
+        right = [packets[i][base + k * extent:base + (k + 1) * extent] for k in range(per_p)]
+        return jnp.dot(left, jnp.concatenate(right, axis=1), preferred_element_type=jnp.float32)
+
+    early = [multiply(0, f) for f in range(blocks)]
     id_copy.wait()
-    for i, (tiles, mine) in enumerate(places):
+    for i in range(count):
         for f in range(blocks):
-            left = packets[i][mine + f * rows:mine + (f + 1) * rows]
-            base = tiles + f * per_p * extent
-            right = [packets[i][base + k * extent:base + (k + 1) * extent] for k in range(per_p)]
-            product = jnp.dot(
-                left, jnp.concatenate(right, axis=1), preferred_element_type=jnp.float32
-            )
+            product = early[f] if i == 0 else multiply(i, f)
             start = f * (per_p + per_q)
             spots = [
                 ids[i, start + k] * tile_count + ids[i, start + per_p + l]

time: 64.6 us -> 64.6 us (level)
  transfers between devices with their start and end apart: 15 -> 15, of which waited for: 9 -> 9; matrix products, arithmetic and copies ran while one was open for 0% -> 0% of each run, Pallas kernels for 5% -> 4%
where the time goes in v25:
time: 64.6 us; the launch traced here: 64.4 us
  blocking collectives  23.7 us (37%)
  starting transfers between devices  18.8 us (29%)
  waiting for transfers between devices  13.1 us (20%)
  Pallas kernels  8.83 us (14%)
    all_to_all x1, blocking collectives, body(): lax.all_to_all(coded, every, split_axis=0, concat_axis=0, tiled=True)  23.7 us
    ppermute x6, waiting for transfers between devices, along(): return lax.ppermute(values, seat, hops)  10.1 us
    ppermute x8, starting transfers between devices, across(): return lax.ppermute(values, seat, [(s, s ^ cols) for s in range(SEATS)])  9.74 us
    ppermute x6, starting transfers between devices, along(): return lax.ppermute(values, seat, hops)  9.06 us
    pallas_call x3, Pallas kernels, add_products(): pl.pallas_call(functools.partial(product_kernel, sizes, tile_count, passe...  4.16 us
    pallas_call x1, Pallas kernels, body(): pl.pallas_call(functools.partial(pack_kernel, cols), out_shape=[jax.Shape...  2.93 us
    ppermute x1, waiting for transfers between devices, opposite(): lax.ppermute(values, seat, [(s, s ^ SEATS - 1 - cols) for s in range(SEAT...  1.68 us
  transfers between devices with their start and end apart: 15, of which 9 were waited for; matrix products, arithmetic and copies ran while one was open for 0% of the time, Pallas kernels for 4%

profile of v25, /device:TPU:1, one launch (start us, length us, event | category | flops | bytes accessed | tf_op | source)
XLA Modules:
  0.0 64.4 jit_solution(6925363204513317389)
XLA Ops:
  0.0 2.9 %pack.1 = (bf16[1424,128]{1,0:T(8,128)(2,1)}, bf16[1808,128]{1,0:T(8,128)(2,1)}, bf16[1808,128]{1,0:T(8,128)(2,1)}, bf16[1808,128]{1,0:T(8,128)(2,1)}, bf16[1424,128]{1,0:T(8,128)(2,1)}) custom-call(s32[2,4]{1,0:T(2,128)} %bitcast.3, s32[4,6]{1,0:T(4,128)} %q_ids.1, bf16[4,2,128,128]{3,2,1,0:T(8,128)(2,1)} %p_ref.1, bf16[4,6,128,128]{3,2,1,0:T(8,128)(2,1)} %q_ref.1), custom_call_target="tpu_custom_call" | custom-call | tf_op jit(solution)/shard_map/pack/pallas_call | solution.py:214
  2.9 2.0 %collective-permute-start.2 = (bf16[1808,128]{1,0:T(8,128)(2,1)}, bf16[1808,128]{1,0:T(8,128)(2,1)S(1)}, u32[]{:S(2)}, u32[]{:S(2)}) collective-permute-start(bf16[1808,128]{1,0:T(8,128)(2,1)} %get-tuple-element.18), channel_id=1, source_target_pairs={{0,1},{1,0},{2,6},{3,7},{4,5},{5,4},{6,2},{7,3},{8,9},{9,8},{10,14... | collective-permute-start | bytes 1388552 | tf_op jit(solution)/shard_map/ppermute | solution.py:228
  5.0 1.3 %collective-permute-start.4 = (bf16[1808,128]{1,0:T(8,128)(2,1)}, bf16[1808,128]{1,0:T(8,128)(2,1)S(1)}, u32[]{:S(2)}, u32[]{:S(2)}) collective-permute-start(bf16[1808,128]{1,0:T(8,128)(2,1)} %get-tuple-element.19), channel_id=1, source_target_pairs={{0,4},{1,5},{2,10},{3,11},{4,0},{5,1},{6,14},{7,15},{8,12},{9,13},... | collective-permute-start | bytes 1388552 | tf_op jit(solution)/shard_map/ppermute | solution.py:228
  6.3 1.2 %collective-permute-start = (bf16[1808,128]{1,0:T(8,128)(2,1)}, bf16[1808,128]{1,0:T(8,128)(2,1)S(1)}, u32[]{:S(2)}, u32[]{:S(2)}) collective-permute-start(bf16[1808,128]{1,0:T(8,128)(2,1)} %get-tuple-element.16), channel_id=1, source_target_pairs={{0,8},{1,9},{2,3},{3,2},{4,12},{5,13},{6,7},{7,6},{8,0},{9,1},{10,... | collective-permute-start | bytes 1388552 | tf_op jit(solution)/shard_map/ppermute | solution.py:228
  7.5 1.5 %collective-permute-start.7 = (bf16[1424,128]{1,0:T(8,128)(2,1)}, bf16[1424,128]{1,0:T(8,128)(2,1)S(1)}, u32[]{:S(2)}, u32[]{:S(2)}) collective-permute-start(bf16[1424,128]{1,0:T(8,128)(2,1)} %get-tuple-element.20.refs_0_), channel_id=1, source_target_pairs={{0,2},{1,3},{2,0},{3,1},{4,6},{5,7},{6,4},{7,5},{8,10},{9,11},{10,... | collective-permute-start | bytes 1093640 | tf_op jit(solution)/shard_map/ppermute | solution.py:231
  9.0 0.0 collective-permute-start.1
  9.0 4.3 %collective-permute-done.2.in_ref.refs_2_ = bf16[1808,128]{1,0:T(8,128)(2,1)S(1)} collective-permute-done((bf16[1808,128]{1,0:T(8,128)(2,1)}, bf16[1808,128]{1,0:T(8,128)(2,1)S(1)}, u32[]{:S(2)}, u32[]{:S(2)}) %collective-permute-start.2) | collective-permute-done | bytes 462880 | tf_op jit(solution)/shard_map/ppermute | solution.py:228
  13.4 0.2 rest_of_packet.3
  13.5 1.9 %collective-permute-start.3 = (bf16[1424,128]{1,0:T(8,128)(2,1)S(1)}, bf16[1424,128]{1,0:T(8,128)(2,1)S(1)}, u32[]{:S(2)}, u32[]{:S(2)}) collective-permute-start(bf16[1424,128]{1,0:T(8,128)(2,1)S(1)} %rest_of_packet.3), channel_id=1, source_target_pairs={{0,4},{1,5},{2,10},{3,11},{4,0},{5,1},{6,14},{7,15},{8,12},{9,13},... | collective-permute-start | bytes 1093640 | tf_op jit(solution)/shard_map/ppermute | solution.py:228
  15.4 0.0 collective-permute-done.4.in_ref.refs_3_
  15.4 0.2 rest_of_packet.4
  15.6 0.0 copy-start
  15.6 2.3 %collective-permute-start.5 = (bf16[1424,128]{1,0:T(8,128)(2,1)S(1)}, bf16[1424,128]{1,0:T(8,128)(2,1)S(1)}, u32[]{:S(2)}, u32[]{:S(2)}) collective-permute-start(bf16[1424,128]{1,0:T(8,128)(2,1)S(1)} %rest_of_packet.4), channel_id=1, source_target_pairs={{0,8},{1,9},{2,3},{3,2},{4,12},{5,13},{6,7},{7,6},{8,0},{9,1},{10,... | collective-permute-start | bytes 1093640 | tf_op jit(solution)/shard_map/ppermute | solution.py:228
  17.9 2.2 %collective-permute-done.in_ref.refs_4_ = bf16[1808,128]{1,0:T(8,128)(2,1)S(1)} collective-permute-done((bf16[1808,128]{1,0:T(8,128)(2,1)}, bf16[1808,128]{1,0:T(8,128)(2,1)S(1)}, u32[]{:S(2)}, u32[]{:S(2)}) %collective-permute-start) | collective-permute-done | bytes 462880 | tf_op jit(solution)/shard_map/ppermute | solution.py:228
  20.1 2.8 %collective-permute-start.13 = (bf16[1808,128]{1,0:T(8,128)(2,1)S(1)}, bf16[1808,128]{1,0:T(8,128)(2,1)S(1)}, u32[]{:S(2)}, u32[]{:S(2)}) collective-permute-start(bf16[1808,128]{1,0:T(8,128)(2,1)S(1)} %collective-permute-done.2.in_ref.refs_2_), channel_id=1, source_target_pairs={{0,2},{1,3},{2,0},{3,1},{4,6},{5,7},{6,4},{7,5},{8,10},{9,11},{10,... | collective-permute-start | bytes 1388552 | tf_op jit(solution)/shard_map/ppermute | solution.py:231
  22.8 0.2 rest_of_packet.5
  23.0 0.0 collective-permute-done.7.refs_1_
  23.0 0.3 collective-permute-start.6
  23.3 1.7 %collective-permute-done.1.refs_2_ = bf16[1424,128]{1,0:T(8,128)(2,1)S(1)} collective-permute-done((bf16[1424,128]{1,0:T(8,128)(2,1)}, bf16[1424,128]{1,0:T(8,128)(2,1)S(1)}, u32[]{:S(2)}, u32[]{:S(2)}) %collective-permute-start.1) | collective-permute-done | bytes 364576 | tf_op jit(solution)/shard_map/ppermute | solution.py:238
  25.0 3.5 %collective-permute-start.14 = (bf16[1808,128]{1,0:T(8,128)(2,1)S(1)}, bf16[1808,128]{1,0:T(8,128)(2,1)S(1)}, u32[]{:S(2)}, u32[]{:S(2)}) collective-permute-start(bf16[1808,128]{1,0:T(8,128)(2,1)S(1)} %collective-permute-done.4.in_ref.refs_3_), channel_id=1, source_target_pairs={{0,2},{1,3},{2,0},{3,1},{4,6},{5,7},{6,4},{7,5},{8,10},{9,11},{10,... | collective-permute-start | bytes 1388552 | tf_op jit(solution)/shard_map/ppermute | solution.py:231
  28.5 0.0 copy-done
  28.5 1.2 %products.3.refs_6_ = f32[256,8,128]{2,1,0:T(8,128)S(1)} custom-call(bf16[1424,128]{1,0:T(8,128)(2,1)S(1)} %copy-done, bf16[1424,128]{1,0:T(8,128)(2,1)S(1)} %collective-permute-done.7.refs_1_, bf16[1808,128]{1,0:T(8,128)(2,1)S(1)} %collective-permute-done.2.in_ref.refs_2_, bf16[1808,128]{1,0:T(8,128)(2,1)S(1)} %collective-permute-done.4.in_ref.refs_3_, ...), custom_call_target="tpu_custom_call" | custom-call | flops 62914560 | bytes 5242880 | tf_op jit(solution)/shard_map/products/pallas_call | solution.py:163
  29.6 0.8 %collective-permute-done.3.refs_3_ = bf16[1424,128]{1,0:T(8,128)(2,1)S(1)} collective-permute-done((bf16[1424,128]{1,0:T(8,128)(2,1)S(1)}, bf16[1424,128]{1,0:T(8,128)(2,1)S(1)}, u32[]{:S(2)}, u32[]{:S(2)}) %collective-permute-start.3) | collective-permute-done | bytes 364576 | tf_op jit(solution)/shard_map/ppermute | solution.py:228
  30.4 1.7 %collective-permute-done.5.refs_4_ = bf16[1424,128]{1,0:T(8,128)(2,1)S(1)} collective-permute-done((bf16[1424,128]{1,0:T(8,128)(2,1)S(1)}, bf16[1424,128]{1,0:T(8,128)(2,1)S(1)}, u32[]{:S(2)}, u32[]{:S(2)}) %collective-permute-start.5) | collective-permute-done | bytes 364576 | tf_op jit(solution)/shard_map/ppermute | solution.py:228
  32.1 1.1 %collective-permute-done.6.refs_5_ = bf16[1424,128]{1,0:T(8,128)(2,1)S(1)} collective-permute-done((bf16[1424,128]{1,0:T(8,128)(2,1)S(1)}, bf16[1424,128]{1,0:T(8,128)(2,1)S(1)}, u32[]{:S(2)}, u32[]{:S(2)}) %collective-permute-start.6) | collective-permute-done | bytes 364576 | tf_op jit(solution)/shard_map/ppermute | solution.py:228
  33.2 1.0 %collective-permute-start.8 = (bf16[1808,128]{1,0:T(8,128)(2,1)S(1)}, bf16[1808,128]{1,0:T(8,128)(2,1)S(1)}, u32[]{:S(2)}, u32[]{:S(2)}) collective-permute-start(bf16[1808,128]{1,0:T(8,128)(2,1)S(1)} %collective-permute-done.in_ref.refs_4_), channel_id=1, source_target_pairs={{0,2},{1,3},{2,0},{3,1},{4,6},{5,7},{6,4},{7,5},{8,10},{9,11},{10,... | collective-permute-start | bytes 1388552 | tf_op jit(solution)/shard_map/ppermute | solution.py:231
  34.2 0.0 collective-permute-start.10
  34.2 0.5 collective-permute-start.11
  34.7 0.0 collective-permute-done.13.refs_0_
  34.7 0.0 collective-permute-start.12
  34.7 0.0 collective-permute-done.14.refs_1_
  34.7 0.5 collective-permute-start.9
  35.2 1.2 %products.4.refs_5_ = f32[256,8,128]{2,1,0:T(8,128)S(1)} custom-call(bf16[1808,128]{1,0:T(8,128)(2,1)S(1)} %collective-permute-done.13.refs_0_, bf16[1808,128]{1,0:T(8,128)(2,1)S(1)} %collective-permute-done.14.refs_1_, bf16[1424,128]{1,0:T(8,128)(2,1)S(1)} %collective-permute-done.1.refs_2_, ...), custom_call_target="tpu_custom_call", output_to_operand_aliasing={{}: (6, {})} | custom-call | flops 75497472 | bytes 6291456 | tf_op jit(solution)/shard_map/products/pallas_call | solution.py:163
  36.5 0.0 collective-permute-done.10.refs_2_
  36.5 0.2 collective-permute-done.11.refs_3_
  36.7 0.5 collective-permute-done.12.refs_4_
  37.2 0.5 collective-permute-done.9.refs_1_
  37.7 0.0 collective-permute-done.8.refs_0_
  37.7 1.8 %products.5 = s32[32,5,8,128]{3,2,1,0:T(8,128)S(1)} custom-call(bf16[1808,128]{1,0:T(8,128)(2,1)S(1)} %collective-permute-done.8.refs_0_, bf16[1424,128]{1,0:T(8,128)(2,1)S(1)} %collective-permute-done.9.refs_1_, bf16[1424,128]{1,0:T(8,128)(2,1)S(1)} %collective-permute-done.10.refs_2_, bf16[1424,128]{1,0:T(8,128)(2,1)S(1)} %collective-permute-done.11.refs_3_, ...), custom_call_target="tpu_custom_call" | custom-call | flops 62914560 | bytes 5242880 | tf_op jit(solution)/shard_map/products/pallas_call | solution.py:163
  39.5 23.7 %all_to_all.5 = s32[32,5,8,128]{3,2,1,0:T(8,128)S(1)} all-to-all(s32[32,5,8,128]{3,2,1,0:T(8,128)S(1)} %products.5), channel_id=1, replica_groups=mesh['plane'=2,'pair'=4,'core'=2,'col'=2] {'plane','pair','core','col'}, dimensions={0} | all-to-all | bytes 1310720 | tf_op jit(solution)/shard_map/all_to_all | solution.py:252
  63.2 1.3 %turn.1 = f32[128,1024]{1,0:T(8,128)} custom-call(s32[2,16,5,8,128]{4,3,2,1,0:T(8,128)S(1)} %bitcast.2), custom_call_target="tpu_custom_call" | custom-call | tf_op jit(solution)/shard_map/turn/pallas_call | solution.py:253
Async XLA Ops:
  2.9 10.4 %collective-permute-start.2 = (bf16[1808,128]{1,0:T(8,128)(2,1)}, bf16[1808,128]{1,0:T(8,128)(2,1)S(1)}, u32[]{:S(2)}, u32[]{:S(2)}) collective-permute-start(bf16[1808,128]{1,0:T(8,128)(2,1)} %get-tuple-element.18), channel_id=1, source_target_pairs={{0,1},{1,0},{2,6},{3,7},{4,5},{5,4},{6,2},{7,3},{8,9},{9,8},{10,14... | collective-permute-start | bytes 1388552 | tf_op jit(solution)/shard_map/ppermute | solution.py:228
  5.0 10.4 %collective-permute-start.4 = (bf16[1808,128]{1,0:T(8,128)(2,1)}, bf16[1808,128]{1,0:T(8,128)(2,1)S(1)}, u32[]{:S(2)}, u32[]{:S(2)}) collective-permute-start(bf16[1808,128]{1,0:T(8,128)(2,1)} %get-tuple-element.19), channel_id=1, source_target_pairs={{0,4},{1,5},{2,10},{3,11},{4,0},{5,1},{6,14},{7,15},{8,12},{9,13},... | collective-permute-start | bytes 1388552 | tf_op jit(solution)/shard_map/ppermute | solution.py:228
  6.3 13.8 %collective-permute-start = (bf16[1808,128]{1,0:T(8,128)(2,1)}, bf16[1808,128]{1,0:T(8,128)(2,1)S(1)}, u32[]{:S(2)}, u32[]{:S(2)}) collective-permute-start(bf16[1808,128]{1,0:T(8,128)(2,1)} %get-tuple-element.16), channel_id=1, source_target_pairs={{0,8},{1,9},{2,3},{3,2},{4,12},{5,13},{6,7},{7,6},{8,0},{9,1},{10,... | collective-permute-start | bytes 1388552 | tf_op jit(solution)/shard_map/ppermute | solution.py:228
  7.5 15.5 %collective-permute-start.7 = (bf16[1424,128]{1,0:T(8,128)(2,1)}, bf16[1424,128]{1,0:T(8,128)(2,1)S(1)}, u32[]{:S(2)}, u32[]{:S(2)}) collective-permute-start(bf16[1424,128]{1,0:T(8,128)(2,1)} %get-tuple-element.20.refs_0_), channel_id=1, source_target_pairs={{0,2},{1,3},{2,0},{3,1},{4,6},{5,7},{6,4},{7,5},{8,10},{9,11},{10,... | collective-permute-start | bytes 1093640 | tf_op jit(solution)/shard_map/ppermute | solution.py:231
  9.0 16.0 %collective-permute-start.1 = (bf16[1424,128]{1,0:T(8,128)(2,1)}, bf16[1424,128]{1,0:T(8,128)(2,1)S(1)}, u32[]{:S(2)}, u32[]{:S(2)}) collective-permute-start(bf16[1424,128]{1,0:T(8,128)(2,1)} %get-tuple-element.17), channel_id=1, source_target_pairs={{0,13},{1,12},{2,15},{3,14},{4,9},{5,8},{6,11},{7,10},{8,5},{9,4},... | collective-permute-start | bytes 1093640 | tf_op jit(solution)/shard_map/ppermute | solution.py:238
  13.5 16.9 %collective-permute-start.3 = (bf16[1424,128]{1,0:T(8,128)(2,1)S(1)}, bf16[1424,128]{1,0:T(8,128)(2,1)S(1)}, u32[]{:S(2)}, u32[]{:S(2)}) collective-permute-start(bf16[1424,128]{1,0:T(8,128)(2,1)S(1)} %rest_of_packet.3), channel_id=1, source_target_pairs={{0,4},{1,5},{2,10},{3,11},{4,0},{5,1},{6,14},{7,15},{8,12},{9,13},... | collective-permute-start | bytes 1093640 | tf_op jit(solution)/shard_map/ppermute | solution.py:228
  15.6 12.9 %copy-start = (bf16[1424,128]{1,0:T(8,128)(2,1)S(1)}, bf16[1424,128]{1,0:T(8,128)(2,1)}, u32[]{:S(2)}) copy-start(bf16[1424,128]{1,0:T(8,128)(2,1)} %get-tuple-element.20.refs_0_) | copy-start | bytes 1093636
  15.6 16.5 %collective-permute-start.5 = (bf16[1424,128]{1,0:T(8,128)(2,1)S(1)}, bf16[1424,128]{1,0:T(8,128)(2,1)S(1)}, u32[]{:S(2)}, u32[]{:S(2)}) collective-permute-start(bf16[1424,128]{1,0:T(8,128)(2,1)S(1)} %rest_of_packet.4), channel_id=1, source_target_pairs={{0,8},{1,9},{2,3},{3,2},{4,12},{5,13},{6,7},{7,6},{8,0},{9,1},{10,... | collective-permute-start | bytes 1093640 | tf_op jit(solution)/shard_map/ppermute | solution.py:228
  20.1 14.6 %collective-permute-start.13 = (bf16[1808,128]{1,0:T(8,128)(2,1)S(1)}, bf16[1808,128]{1,0:T(8,128)(2,1)S(1)}, u32[]{:S(2)}, u32[]{:S(2)}) collective-permute-start(bf16[1808,128]{1,0:T(8,128)(2,1)S(1)} %collective-permute-done.2.in_ref.refs_2_), channel_id=1, source_target_pairs={{0,2},{1,3},{2,0},{3,1},{4,6},{5,7},{6,4},{7,5},{8,10},{9,11},{10,... | collective-permute-start | bytes 1388552 | tf_op jit(solution)/shard_map/ppermute | solution.py:231
  23.0 10.2 %collective-permute-start.6 = (bf16[1424,128]{1,0:T(8,128)(2,1)S(1)}, bf16[1424,128]{1,0:T(8,128)(2,1)S(1)}, u32[]{:S(2)}, u32[]{:S(2)}) collective-permute-start(bf16[1424,128]{1,0:T(8,128)(2,1)S(1)} %rest_of_packet.5), channel_id=1, source_target_pairs={{0,1},{1,0},{2,6},{3,7},{4,5},{5,4},{6,2},{7,3},{8,9},{9,8},{10,14... | collective-permute-start | bytes 1093640 | tf_op jit(solution)/shard_map/ppermute | solution.py:228
  25.0 9.7 %collective-permute-start.14 = (bf16[1808,128]{1,0:T(8,128)(2,1)S(1)}, bf16[1808,128]{1,0:T(8,128)(2,1)S(1)}, u32[]{:S(2)}, u32[]{:S(2)}) collective-permute-start(bf16[1808,128]{1,0:T(8,128)(2,1)S(1)} %collective-permute-done.4.in_ref.refs_3_), channel_id=1, source_target_pairs={{0,2},{1,3},{2,0},{3,1},{4,6},{5,7},{6,4},{7,5},{8,10},{9,11},{10,... | collective-permute-start | bytes 1388552 | tf_op jit(solution)/shard_map/ppermute | solution.py:231
  33.2 4.5 %collective-permute-start.8 = (bf16[1808,128]{1,0:T(8,128)(2,1)S(1)}, bf16[1808,128]{1,0:T(8,128)(2,1)S(1)}, u32[]{:S(2)}, u32[]{:S(2)}) collective-permute-start(bf16[1808,128]{1,0:T(8,128)(2,1)S(1)} %collective-permute-done.in_ref.refs_4_), channel_id=1, source_target_pairs={{0,2},{1,3},{2,0},{3,1},{4,6},{5,7},{6,4},{7,5},{8,10},{9,11},{10,... | collective-permute-start | bytes 1388552 | tf_op jit(solution)/shard_map/ppermute | solution.py:231
  34.2 2.3 %collective-permute-start.10 = (bf16[1424,128]{1,0:T(8,128)(2,1)S(1)}, bf16[1424,128]{1,0:T(8,128)(2,1)S(1)}, u32[]{:S(2)}, u32[]{:S(2)}) collective-permute-start(bf16[1424,128]{1,0:T(8,128)(2,1)S(1)} %collective-permute-done.3.refs_3_), channel_id=1, source_target_pairs={{0,2},{1,3},{2,0},{3,1},{4,6},{5,7},{6,4},{7,5},{8,10},{9,11},{10,... | collective-permute-start | bytes 1093640 | tf_op jit(solution)/shard_map/ppermute | solution.py:231
  34.2 2.5 %collective-permute-start.11 = (bf16[1424,128]{1,0:T(8,128)(2,1)S(1)}, bf16[1424,128]{1,0:T(8,128)(2,1)S(1)}, u32[]{:S(2)}, u32[]{:S(2)}) collective-permute-start(bf16[1424,128]{1,0:T(8,128)(2,1)S(1)} %collective-permute-done.5.refs_4_), channel_id=1, source_target_pairs={{0,2},{1,3},{2,0},{3,1},{4,6},{5,7},{6,4},{7,5},{8,10},{9,11},{10,... | collective-permute-start | bytes 1093640 | tf_op jit(solution)/shard_map/ppermute | solution.py:231
  34.7 2.5 %collective-permute-start.12 = (bf16[1424,128]{1,0:T(8,128)(2,1)S(1)}, bf16[1424,128]{1,0:T(8,128)(2,1)S(1)}, u32[]{:S(2)}, u32[]{:S(2)}) collective-permute-start(bf16[1424,128]{1,0:T(8,128)(2,1)S(1)} %collective-permute-done.6.refs_5_), channel_id=1, source_target_pairs={{0,2},{1,3},{2,0},{3,1},{4,6},{5,7},{6,4},{7,5},{8,10},{9,11},{10,... | collective-permute-start | bytes 1093640 | tf_op jit(solution)/shard_map/ppermute | solution.py:231
  34.7 3.0 %collective-permute-start.9 = (bf16[1424,128]{1,0:T(8,128)(2,1)S(1)}, bf16[1424,128]{1,0:T(8,128)(2,1)S(1)}, u32[]{:S(2)}, u32[]{:S(2)}) collective-permute-start(bf16[1424,128]{1,0:T(8,128)(2,1)S(1)} %collective-permute-done.1.refs_2_), channel_id=1, source_target_pairs={{0,2},{1,3},{2,0},{3,1},{4,6},{5,7},{6,4},{7,5},{8,10},{9,11},{10,... | collective-permute-start | bytes 1093640 | tf_op jit(solution)/shard_map/ppermute | solution.py:231

commit v26 on v23

--- a/solution.py
+++ b/solution.py
@@ -31,8 +31,13 @@
             value = p_ids[k, f] if k < per_p else q_ids[f, k - per_p]
             ids = jnp.where(lane == f * (per_p + per_q) + k, value, ids)
     ids = ids.astype(p_ref.dtype)
+    line = lax.broadcasted_iota(jnp.int32, (extent, extent), 0)
+    unit = (line == lax.broadcasted_iota(jnp.int32, (extent, extent), 1)).astype(q_ref.dtype)
     for f in range(blocks):
-        flipped = [q_ref[f, k].astype(jnp.float32).T for k in range(per_q)]
+        flipped = [
+            lax.dot_general(unit, q_ref[f, k], (((1,), (1,)), ((), ())), preferred_element_type=jnp.float32)
+            for k in range(per_q)
+        ]
         for j in range(SEATS):
             pieces = [tile[j * strip:(j + 1) * strip] for tile in flipped]
             strips[j, f * rows:(f + 1) * rows] = jnp.concatenate(pieces, axis=0).astype(strips.dtype)

time: 64.6 us -> 65 us (level)
  no operation moved by 1% of the time
where the time goes in v26:
time: 65 us; the launch traced here: 64.8 us
  blocking collectives  23.7 us (36%)
  starting transfers between devices  18.8 us (29%)
  waiting for transfers between devices  12.9 us (20%)
  Pallas kernels  9.31 us (14%)
    all_to_all x1, blocking collectives, body(): lax.all_to_all(coded, every, split_axis=0, concat_axis=0, tiled=True)  23.7 us
    ppermute x6, waiting for transfers between devices, along(): return lax.ppermute(values, seat, hops)  10 us
    ppermute x8, starting transfers between devices, across(): return lax.ppermute(values, seat, [(s, s ^ cols) for s in range(SEATS)])  9.74 us
    ppermute x6, starting transfers between devices, along(): return lax.ppermute(values, seat, hops)  9.05 us
    pallas_call x3, Pallas kernels, add_products(): pl.pallas_call(functools.partial(product_kernel, sizes, tile_count, passe...  4.28 us
    pallas_call x1, Pallas kernels, body(): pl.pallas_call(functools.partial(pack_kernel, cols), out_shape=[jax.Shape...  3.29 us
    ppermute x1, waiting for transfers between devices, opposite(): lax.ppermute(values, seat, [(s, s ^ SEATS - 1 - cols) for s in range(SEAT...  1.7 us
  transfers between devices with their start and end apart: 15, of which 9 were waited for; matrix products, arithmetic and copies ran while one was open for 0% of the time, Pallas kernels for 5%

profile of v26, /device:TPU:1, one launch (start us, length us, event | category | flops | bytes accessed | tf_op | source)
XLA Modules:
  0.0 64.8 jit_solution(1545973642333023125)
XLA Ops:
  0.0 3.3 %pack.1 = (bf16[1424,128]{1,0:T(8,128)(2,1)}, bf16[1808,128]{1,0:T(8,128)(2,1)}, bf16[1808,128]{1,0:T(8,128)(2,1)}, bf16[1808,128]{1,0:T(8,128)(2,1)}, bf16[1424,128]{1,0:T(8,128)(2,1)}) custom-call(s32[2,4]{1,0:T(2,128)} %bitcast.3, s32[4,6]{1,0:T(4,128)} %q_ids.1, bf16[4,2,128,128]{3,2,1,0:T(8,128)(2,1)} %p_ref.1, bf16[4,6,128,128]{3,2,1,0:T(8,128)(2,1)} %q_ref.1), custom_call_target="tpu_custom_call" | custom-call | tf_op jit(solution)/shard_map/pack/pallas_call | solution.py:215
  3.3 2.0 %collective-permute-start.2 = (bf16[1808,128]{1,0:T(8,128)(2,1)}, bf16[1808,128]{1,0:T(8,128)(2,1)S(1)}, u32[]{:S(2)}, u32[]{:S(2)}) collective-permute-start(bf16[1808,128]{1,0:T(8,128)(2,1)} %get-tuple-element.18), channel_id=1, source_target_pairs={{0,1},{1,0},{2,6},{3,7},{4,5},{5,4},{6,2},{7,3},{8,9},{9,8},{10,14... | collective-permute-start | bytes 1388552 | tf_op jit(solution)/shard_map/ppermute | solution.py:229
  5.3 1.3 %collective-permute-start.4 = (bf16[1808,128]{1,0:T(8,128)(2,1)}, bf16[1808,128]{1,0:T(8,128)(2,1)S(1)}, u32[]{:S(2)}, u32[]{:S(2)}) collective-permute-start(bf16[1808,128]{1,0:T(8,128)(2,1)} %get-tuple-element.19), channel_id=1, source_target_pairs={{0,4},{1,5},{2,10},{3,11},{4,0},{5,1},{6,14},{7,15},{8,12},{9,13},... | collective-permute-start | bytes 1388552 | tf_op jit(solution)/shard_map/ppermute | solution.py:229
  6.6 1.2 %collective-permute-start = (bf16[1808,128]{1,0:T(8,128)(2,1)}, bf16[1808,128]{1,0:T(8,128)(2,1)S(1)}, u32[]{:S(2)}, u32[]{:S(2)}) collective-permute-start(bf16[1808,128]{1,0:T(8,128)(2,1)} %get-tuple-element.16), channel_id=1, source_target_pairs={{0,8},{1,9},{2,3},{3,2},{4,12},{5,13},{6,7},{7,6},{8,0},{9,1},{10,... | collective-permute-start | bytes 1388552 | tf_op jit(solution)/shard_map/ppermute | solution.py:229
  7.9 1.5 %collective-permute-start.7 = (bf16[1424,128]{1,0:T(8,128)(2,1)}, bf16[1424,128]{1,0:T(8,128)(2,1)S(1)}, u32[]{:S(2)}, u32[]{:S(2)}) collective-permute-start(bf16[1424,128]{1,0:T(8,128)(2,1)} %get-tuple-element.20.refs_0_), channel_id=1, source_target_pairs={{0,2},{1,3},{2,0},{3,1},{4,6},{5,7},{6,4},{7,5},{8,10},{9,11},{10,... | collective-permute-start | bytes 1093640 | tf_op jit(solution)/shard_map/ppermute | solution.py:232
  9.4 0.0 collective-permute-start.1
  9.4 4.3 %collective-permute-done.2.in_ref.refs_2_ = bf16[1808,128]{1,0:T(8,128)(2,1)S(1)} collective-permute-done((bf16[1808,128]{1,0:T(8,128)(2,1)}, bf16[1808,128]{1,0:T(8,128)(2,1)S(1)}, u32[]{:S(2)}, u32[]{:S(2)}) %collective-permute-start.2) | collective-permute-done | bytes 462880 | tf_op jit(solution)/shard_map/ppermute | solution.py:229
  13.7 0.2 rest_of_packet.3
  13.9 1.9 %collective-permute-start.3 = (bf16[1424,128]{1,0:T(8,128)(2,1)S(1)}, bf16[1424,128]{1,0:T(8,128)(2,1)S(1)}, u32[]{:S(2)}, u32[]{:S(2)}) collective-permute-start(bf16[1424,128]{1,0:T(8,128)(2,1)S(1)} %rest_of_packet.3), channel_id=1, source_target_pairs={{0,4},{1,5},{2,10},{3,11},{4,0},{5,1},{6,14},{7,15},{8,12},{9,13},... | collective-permute-start | bytes 1093640 | tf_op jit(solution)/shard_map/ppermute | solution.py:229
  15.8 0.0 collective-permute-done.4.in_ref.refs_3_
  15.8 0.2 rest_of_packet.4
  15.9 0.0 copy-start
  15.9 2.3 %collective-permute-start.5 = (bf16[1424,128]{1,0:T(8,128)(2,1)S(1)}, bf16[1424,128]{1,0:T(8,128)(2,1)S(1)}, u32[]{:S(2)}, u32[]{:S(2)}) collective-permute-start(bf16[1424,128]{1,0:T(8,128)(2,1)S(1)} %rest_of_packet.4), channel_id=1, source_target_pairs={{0,8},{1,9},{2,3},{3,2},{4,12},{5,13},{6,7},{7,6},{8,0},{9,1},{10,... | collective-permute-start | bytes 1093640 | tf_op jit(solution)/shard_map/ppermute | solution.py:229
  18.3 2.2 %collective-permute-done.in_ref.refs_4_ = bf16[1808,128]{1,0:T(8,128)(2,1)S(1)} collective-permute-done((bf16[1808,128]{1,0:T(8,128)(2,1)}, bf16[1808,128]{1,0:T(8,128)(2,1)S(1)}, u32[]{:S(2)}, u32[]{:S(2)}) %collective-permute-start) | collective-permute-done | bytes 462880 | tf_op jit(solution)/shard_map/ppermute | solution.py:229
  20.4 2.8 %collective-permute-start.13 = (bf16[1808,128]{1,0:T(8,128)(2,1)S(1)}, bf16[1808,128]{1,0:T(8,128)(2,1)S(1)}, u32[]{:S(2)}, u32[]{:S(2)}) collective-permute-start(bf16[1808,128]{1,0:T(8,128)(2,1)S(1)} %collective-permute-done.2.in_ref.refs_2_), channel_id=1, source_target_pairs={{0,2},{1,3},{2,0},{3,1},{4,6},{5,7},{6,4},{7,5},{8,10},{9,11},{10,... | collective-permute-start | bytes 1388552 | tf_op jit(solution)/shard_map/ppermute | solution.py:232
  23.2 0.2 rest_of_packet.5
  23.4 0.0 collective-permute-done.7.refs_1_
  23.4 0.3 collective-permute-start.6
  23.7 1.7 %collective-permute-done.1.refs_2_ = bf16[1424,128]{1,0:T(8,128)(2,1)S(1)} collective-permute-done((bf16[1424,128]{1,0:T(8,128)(2,1)}, bf16[1424,128]{1,0:T(8,128)(2,1)S(1)}, u32[]{:S(2)}, u32[]{:S(2)}) %collective-permute-start.1) | collective-permute-done | bytes 364576 | tf_op jit(solution)/shard_map/ppermute | solution.py:239
  25.4 3.5 %collective-permute-start.14 = (bf16[1808,128]{1,0:T(8,128)(2,1)S(1)}, bf16[1808,128]{1,0:T(8,128)(2,1)S(1)}, u32[]{:S(2)}, u32[]{:S(2)}) collective-permute-start(bf16[1808,128]{1,0:T(8,128)(2,1)S(1)} %collective-permute-done.4.in_ref.refs_3_), channel_id=1, source_target_pairs={{0,2},{1,3},{2,0},{3,1},{4,6},{5,7},{6,4},{7,5},{8,10},{9,11},{10,... | collective-permute-start | bytes 1388552 | tf_op jit(solution)/shard_map/ppermute | solution.py:232
  28.8 0.0 copy-done
  28.8 1.2 %products.3.refs_6_ = f32[256,8,128]{2,1,0:T(8,128)S(1)} custom-call(bf16[1424,128]{1,0:T(8,128)(2,1)S(1)} %copy-done, bf16[1424,128]{1,0:T(8,128)(2,1)S(1)} %collective-permute-done.7.refs_1_, bf16[1808,128]{1,0:T(8,128)(2,1)S(1)} %collective-permute-done.2.in_ref.refs_2_, bf16[1808,128]{1,0:T(8,128)(2,1)S(1)} %collective-permute-done.4.in_ref.refs_3_, ...), custom_call_target="tpu_custom_call" | custom-call | flops 62914560 | bytes 5242880 | tf_op jit(solution)/shard_map/products/pallas_call | solution.py:164
  30.1 0.7 %collective-permute-done.3.refs_3_ = bf16[1424,128]{1,0:T(8,128)(2,1)S(1)} collective-permute-done((bf16[1424,128]{1,0:T(8,128)(2,1)S(1)}, bf16[1424,128]{1,0:T(8,128)(2,1)S(1)}, u32[]{:S(2)}, u32[]{:S(2)}) %collective-permute-start.3) | collective-permute-done | bytes 364576 | tf_op jit(solution)/shard_map/ppermute | solution.py:229
  30.8 1.7 %collective-permute-done.5.refs_4_ = bf16[1424,128]{1,0:T(8,128)(2,1)S(1)} collective-permute-done((bf16[1424,128]{1,0:T(8,128)(2,1)S(1)}, bf16[1424,128]{1,0:T(8,128)(2,1)S(1)}, u32[]{:S(2)}, u32[]{:S(2)}) %collective-permute-start.5) | collective-permute-done | bytes 364576 | tf_op jit(solution)/shard_map/ppermute | solution.py:229
  32.5 1.1 %collective-permute-done.6.refs_5_ = bf16[1424,128]{1,0:T(8,128)(2,1)S(1)} collective-permute-done((bf16[1424,128]{1,0:T(8,128)(2,1)S(1)}, bf16[1424,128]{1,0:T(8,128)(2,1)S(1)}, u32[]{:S(2)}, u32[]{:S(2)}) %collective-permute-start.6) | collective-permute-done | bytes 364576 | tf_op jit(solution)/shard_map/ppermute | solution.py:229
  33.6 1.0 %collective-permute-start.8 = (bf16[1808,128]{1,0:T(8,128)(2,1)S(1)}, bf16[1808,128]{1,0:T(8,128)(2,1)S(1)}, u32[]{:S(2)}, u32[]{:S(2)}) collective-permute-start(bf16[1808,128]{1,0:T(8,128)(2,1)S(1)} %collective-permute-done.in_ref.refs_4_), channel_id=1, source_target_pairs={{0,2},{1,3},{2,0},{3,1},{4,6},{5,7},{6,4},{7,5},{8,10},{9,11},{10,... | collective-permute-start | bytes 1388552 | tf_op jit(solution)/shard_map/ppermute | solution.py:232
  34.5 0.0 collective-permute-start.10
  34.6 0.5 collective-permute-start.11
  35.1 0.0 collective-permute-done.13.refs_0_
  35.1 0.0 collective-permute-start.12
  35.1 0.0 collective-permute-done.14.refs_1_
  35.1 0.5 collective-permute-start.9
  35.6 1.3 %products.4.refs_5_ = f32[256,8,128]{2,1,0:T(8,128)S(1)} custom-call(bf16[1808,128]{1,0:T(8,128)(2,1)S(1)} %collective-permute-done.13.refs_0_, bf16[1808,128]{1,0:T(8,128)(2,1)S(1)} %collective-permute-done.14.refs_1_, bf16[1424,128]{1,0:T(8,128)(2,1)S(1)} %collective-permute-done.1.refs_2_, ...), custom_call_target="tpu_custom_call", output_to_operand_aliasing={{}: (6, {})} | custom-call | flops 75497472 | bytes 6291456 | tf_op jit(solution)/shard_map/products/pallas_call | solution.py:164
  36.9 0.0 collective-permute-done.10.refs_2_
  36.9 0.2 collective-permute-done.11.refs_3_
  37.0 0.5 collective-permute-done.12.refs_4_
  37.6 0.5 collective-permute-done.9.refs_1_
  38.1 0.0 collective-permute-done.8.refs_0_
  38.1 1.8 %products.5 = s32[32,5,8,128]{3,2,1,0:T(8,128)S(1)} custom-call(bf16[1808,128]{1,0:T(8,128)(2,1)S(1)} %collective-permute-done.8.refs_0_, bf16[1424,128]{1,0:T(8,128)(2,1)S(1)} %collective-permute-done.9.refs_1_, bf16[1424,128]{1,0:T(8,128)(2,1)S(1)} %collective-permute-done.10.refs_2_, bf16[1424,128]{1,0:T(8,128)(2,1)S(1)} %collective-permute-done.11.refs_3_, ...), custom_call_target="tpu_custom_call" | custom-call | flops 62914560 | bytes 5242880 | tf_op jit(solution)/shard_map/products/pallas_call | solution.py:164
  39.9 23.7 %all_to_all.5 = s32[32,5,8,128]{3,2,1,0:T(8,128)S(1)} all-to-all(s32[32,5,8,128]{3,2,1,0:T(8,128)S(1)} %products.5), channel_id=1, replica_groups=mesh['plane'=2,'pair'=4,'core'=2,'col'=2] {'plane','pair','core','col'}, dimensions={0} | all-to-all | bytes 1310720 | tf_op jit(solution)/shard_map/all_to_all | solution.py:253
  63.5 1.3 %turn.1 = f32[128,1024]{1,0:T(8,128)} custom-call(s32[2,16,5,8,128]{4,3,2,1,0:T(8,128)S(1)} %bitcast.2), custom_call_target="tpu_custom_call" | custom-call | tf_op jit(solution)/shard_map/turn/pallas_call | solution.py:254
Async XLA Ops:
  3.3 10.4 %collective-permute-start.2 = (bf16[1808,128]{1,0:T(8,128)(2,1)}, bf16[1808,128]{1,0:T(8,128)(2,1)S(1)}, u32[]{:S(2)}, u32[]{:S(2)}) collective-permute-start(bf16[1808,128]{1,0:T(8,128)(2,1)} %get-tuple-element.18), channel_id=1, source_target_pairs={{0,1},{1,0},{2,6},{3,7},{4,5},{5,4},{6,2},{7,3},{8,9},{9,8},{10,14... | collective-permute-start | bytes 1388552 | tf_op jit(solution)/shard_map/ppermute | solution.py:229
  5.3 10.4 %collective-permute-start.4 = (bf16[1808,128]{1,0:T(8,128)(2,1)}, bf16[1808,128]{1,0:T(8,128)(2,1)S(1)}, u32[]{:S(2)}, u32[]{:S(2)}) collective-permute-start(bf16[1808,128]{1,0:T(8,128)(2,1)} %get-tuple-element.19), channel_id=1, source_target_pairs={{0,4},{1,5},{2,10},{3,11},{4,0},{5,1},{6,14},{7,15},{8,12},{9,13},... | collective-permute-start | bytes 1388552 | tf_op jit(solution)/shard_map/ppermute | solution.py:229
  6.6 13.8 %collective-permute-start = (bf16[1808,128]{1,0:T(8,128)(2,1)}, bf16[1808,128]{1,0:T(8,128)(2,1)S(1)}, u32[]{:S(2)}, u32[]{:S(2)}) collective-permute-start(bf16[1808,128]{1,0:T(8,128)(2,1)} %get-tuple-element.16), channel_id=1, source_target_pairs={{0,8},{1,9},{2,3},{3,2},{4,12},{5,13},{6,7},{7,6},{8,0},{9,1},{10,... | collective-permute-start | bytes 1388552 | tf_op jit(solution)/shard_map/ppermute | solution.py:229
  7.9 15.5 %collective-permute-start.7 = (bf16[1424,128]{1,0:T(8,128)(2,1)}, bf16[1424,128]{1,0:T(8,128)(2,1)S(1)}, u32[]{:S(2)}, u32[]{:S(2)}) collective-permute-start(bf16[1424,128]{1,0:T(8,128)(2,1)} %get-tuple-element.20.refs_0_), channel_id=1, source_target_pairs={{0,2},{1,3},{2,0},{3,1},{4,6},{5,7},{6,4},{7,5},{8,10},{9,11},{10,... | collective-permute-start | bytes 1093640 | tf_op jit(solution)/shard_map/ppermute | solution.py:232
  9.4 16.0 %collective-permute-start.1 = (bf16[1424,128]{1,0:T(8,128)(2,1)}, bf16[1424,128]{1,0:T(8,128)(2,1)S(1)}, u32[]{:S(2)}, u32[]{:S(2)}) collective-permute-start(bf16[1424,128]{1,0:T(8,128)(2,1)} %get-tuple-element.17), channel_id=1, source_target_pairs={{0,13},{1,12},{2,15},{3,14},{4,9},{5,8},{6,11},{7,10},{8,5},{9,4},... | collective-permute-start | bytes 1093640 | tf_op jit(solution)/shard_map/ppermute | solution.py:239
  13.9 16.9 %collective-permute-start.3 = (bf16[1424,128]{1,0:T(8,128)(2,1)S(1)}, bf16[1424,128]{1,0:T(8,128)(2,1)S(1)}, u32[]{:S(2)}, u32[]{:S(2)}) collective-permute-start(bf16[1424,128]{1,0:T(8,128)(2,1)S(1)} %rest_of_packet.3), channel_id=1, source_target_pairs={{0,4},{1,5},{2,10},{3,11},{4,0},{5,1},{6,14},{7,15},{8,12},{9,13},... | collective-permute-start | bytes 1093640 | tf_op jit(solution)/shard_map/ppermute | solution.py:229
  15.9 12.9 %copy-start = (bf16[1424,128]{1,0:T(8,128)(2,1)S(1)}, bf16[1424,128]{1,0:T(8,128)(2,1)}, u32[]{:S(2)}) copy-start(bf16[1424,128]{1,0:T(8,128)(2,1)} %get-tuple-element.20.refs_0_) | copy-start | bytes 1093636
  15.9 16.5 %collective-permute-start.5 = (bf16[1424,128]{1,0:T(8,128)(2,1)S(1)}, bf16[1424,128]{1,0:T(8,128)(2,1)S(1)}, u32[]{:S(2)}, u32[]{:S(2)}) collective-permute-start(bf16[1424,128]{1,0:T(8,128)(2,1)S(1)} %rest_of_packet.4), channel_id=1, source_target_pairs={{0,8},{1,9},{2,3},{3,2},{4,12},{5,13},{6,7},{7,6},{8,0},{9,1},{10,... | collective-permute-start | bytes 1093640 | tf_op jit(solution)/shard_map/ppermute | solution.py:229
  20.4 14.6 %collective-permute-start.13 = (bf16[1808,128]{1,0:T(8,128)(2,1)S(1)}, bf16[1808,128]{1,0:T(8,128)(2,1)S(1)}, u32[]{:S(2)}, u32[]{:S(2)}) collective-permute-start(bf16[1808,128]{1,0:T(8,128)(2,1)S(1)} %collective-permute-done.2.in_ref.refs_2_), channel_id=1, source_target_pairs={{0,2},{1,3},{2,0},{3,1},{4,6},{5,7},{6,4},{7,5},{8,10},{9,11},{10,... | collective-permute-start | bytes 1388552 | tf_op jit(solution)/shard_map/ppermute | solution.py:232
  23.4 10.2 %collective-permute-start.6 = (bf16[1424,128]{1,0:T(8,128)(2,1)S(1)}, bf16[1424,128]{1,0:T(8,128)(2,1)S(1)}, u32[]{:S(2)}, u32[]{:S(2)}) collective-permute-start(bf16[1424,128]{1,0:T(8,128)(2,1)S(1)} %rest_of_packet.5), channel_id=1, source_target_pairs={{0,1},{1,0},{2,6},{3,7},{4,5},{5,4},{6,2},{7,3},{8,9},{9,8},{10,14... | collective-permute-start | bytes 1093640 | tf_op jit(solution)/shard_map/ppermute | solution.py:229
  25.4 9.7 %collective-permute-start.14 = (bf16[1808,128]{1,0:T(8,128)(2,1)S(1)}, bf16[1808,128]{1,0:T(8,128)(2,1)S(1)}, u32[]{:S(2)}, u32[]{:S(2)}) collective-permute-start(bf16[1808,128]{1,0:T(8,128)(2,1)S(1)} %collective-permute-done.4.in_ref.refs_3_), channel_id=1, source_target_pairs={{0,2},{1,3},{2,0},{3,1},{4,6},{5,7},{6,4},{7,5},{8,10},{9,11},{10,... | collective-permute-start | bytes 1388552 | tf_op jit(solution)/shard_map/ppermute | solution.py:232
  33.6 4.5 %collective-permute-start.8 = (bf16[1808,128]{1,0:T(8,128)(2,1)S(1)}, bf16[1808,128]{1,0:T(8,128)(2,1)S(1)}, u32[]{:S(2)}, u32[]{:S(2)}) collective-permute-start(bf16[1808,128]{1,0:T(8,128)(2,1)S(1)} %collective-permute-done.in_ref.refs_4_), channel_id=1, source_target_pairs={{0,2},{1,3},{2,0},{3,1},{4,6},{5,7},{6,4},{7,5},{8,10},{9,11},{10,... | collective-permute-start | bytes 1388552 | tf_op jit(solution)/shard_map/ppermute | solution.py:232
  34.5 2.3 %collective-permute-start.10 = (bf16[1424,128]{1,0:T(8,128)(2,1)S(1)}, bf16[1424,128]{1,0:T(8,128)(2,1)S(1)}, u32[]{:S(2)}, u32[]{:S(2)}) collective-permute-start(bf16[1424,128]{1,0:T(8,128)(2,1)S(1)} %collective-permute-done.3.refs_3_), channel_id=1, source_target_pairs={{0,2},{1,3},{2,0},{3,1},{4,6},{5,7},{6,4},{7,5},{8,10},{9,11},{10,... | collective-permute-start | bytes 1093640 | tf_op jit(solution)/shard_map/ppermute | solution.py:232
  34.6 2.5 %collective-permute-start.11 = (bf16[1424,128]{1,0:T(8,128)(2,1)S(1)}, bf16[1424,128]{1,0:T(8,128)(2,1)S(1)}, u32[]{:S(2)}, u32[]{:S(2)}) collective-permute-start(bf16[1424,128]{1,0:T(8,128)(2,1)S(1)} %collective-permute-done.5.refs_4_), channel_id=1, source_target_pairs={{0,2},{1,3},{2,0},{3,1},{4,6},{5,7},{6,4},{7,5},{8,10},{9,11},{10,... | collective-permute-start | bytes 1093640 | tf_op jit(solution)/shard_map/ppermute | solution.py:232
  35.1 2.5 %collective-permute-start.12 = (bf16[1424,128]{1,0:T(8,128)(2,1)S(1)}, bf16[1424,128]{1,0:T(8,128)(2,1)S(1)}, u32[]{:S(2)}, u32[]{:S(2)}) collective-permute-start(bf16[1424,128]{1,0:T(8,128)(2,1)S(1)} %collective-permute-done.6.refs_5_), channel_id=1, source_target_pairs={{0,2},{1,3},{2,0},{3,1},{4,6},{5,7},{6,4},{7,5},{8,10},{9,11},{10,... | collective-permute-start | bytes 1093640 | tf_op jit(solution)/shard_map/ppermute | solution.py:232
  35.1 3.0 %collective-permute-start.9 = (bf16[1424,128]{1,0:T(8,128)(2,1)S(1)}, bf16[1424,128]{1,0:T(8,128)(2,1)S(1)}, u32[]{:S(2)}, u32[]{:S(2)}) collective-permute-start(bf16[1424,128]{1,0:T(8,128)(2,1)S(1)} %collective-permute-done.1.refs_2_), channel_id=1, source_target_pairs={{0,2},{1,3},{2,0},{3,1},{4,6},{5,7},{6,4},{7,5},{8,10},{9,11},{10,... | collective-permute-start | bytes 1093640 | tf_op jit(solution)/shard_map/ppermute | solution.py:232

commit v27 on v20

--- a/solution.py
+++ b/solution.py
@@ -109,15 +109,19 @@
         acc_ref[...] = jnp.zeros_like(acc_ref)
     else:
         acc_ref[...] = refs[count][...]
+
+    def multiply(i, f):
+        tiles, mine = places[i]
+        left = packets[i][mine + f * rows:mine + (f + 1) * rows]
+        base = tiles + f * per_p * extent
+        right = [packets[i][base + k * extent:base + (k + 1) * extent] for k in range(per_p)]
+        return jnp.dot(left, jnp.concatenate(right, axis=1), preferred_element_type=jnp.float32)
+
+    early = [multiply(0, f) for f in range(blocks)]
     id_copy.wait()
-    for i, (tiles, mine) in enumerate(places):
+    for i in range(count):
         for f in range(blocks):
-            left = packets[i][mine + f * rows:mine + (f + 1) * rows]
-            base = tiles + f * per_p * extent
-            right = [packets[i][base + k * extent:base + (k + 1) * extent] for k in range(per_p)]
-            product = jnp.dot(
-                left, jnp.concatenate(right, axis=1), preferred_element_type=jnp.float32
-            )
+            product = early[f] if i == 0 else multiply(i, f)
             start = f * (per_p + per_q)
             spots = [
                 ids[i, start + k] * tile_count + ids[i, start + per_p + l]
@@ -253,14 +257,11 @@
     far = opposite(out[3])
     second = [along(rest_of(first[step], strips), (step + 1) % 3) for step in range(3)]
     acc = add(None, [own, beside] + first, [(0, 0), (0, 1), (1, 0), (1, 0), (1, 0)])
-    first[2], second, acc = lax.optimization_barrier((first[2], second, acc))
-    acc = add(
-        acc,
-        [far, across(far), across(first[0])] + second,
-        [(0, 0), (0, 1), (1, 1), (0, 0), (0, 0), (0, 0)],
-    )
-    crossed = [across(each) for each in first[1:] + second]
-    coded = add(acc, crossed, [(1, 1), (1, 1), (0, 1), (0, 1), (0, 1)], coded=True)
+    first[2], far, second, acc = lax.optimization_barrier((first[2], far, second, acc))
+    crossed = [across(each) for each in first]
+    acc = add(acc, crossed[:2] + [far] + second, [(1, 1), (1, 1), (0, 0), (0, 0), (0, 0), (0, 0)])
+    crossed = crossed[2:] + [across(each) for each in [far] + second]
+    coded = add(acc, crossed, [(1, 1), (0, 1), (0, 1), (0, 1), (0, 1)], coded=True)
     every = ("plane",) + seat
     tiles = tile_count // cols
     landed = lax.all_to_all(coded, every, split_axis=0, concat_axis=0, tiled=True)

time: 64.8 us -> 64.5 us (level)
  waiting for transfers between devices: 8.36 us -> 13 us
  starting transfers between devices: 22.9 us -> 18.9 us
  blocking collectives: 24.5 us -> 23.7 us
    ppermute x8, starting transfers between devices: 13.2 us -> 9.77 us  [across(): return lax.ppermute(values, seat, [(s, s ^ cols) for s in range(SEATS)])]
    ppermute x6, waiting for transfers between devices: 7.2 us -> 10.1 us  [along(): return lax.ppermute(values, seat, hops)]
    ppermute x1, waiting for transfers between devices: 0.01 us -> 1.66 us  [opposite(): lax.ppermute(values, seat, [(s, s ^ SEATS - 1 - cols) for s in range(SEAT...]
    all_to_all x1, blocking collectives: 24.5 us -> 23.7 us  [body(): lax.all_to_all(coded, every, split_axis=0, concat_axis=0, tiled=True)]
  transfers between devices with their start and end apart: 15 -> 15, of which waited for: 6 -> 9; matrix products, arithmetic and copies ran while one was open for 0% -> 0% of each run, Pallas kernels for 5% -> 4%
where the time goes in v27:
time: 64.5 us; the launch traced here: 64.4 us
  blocking collectives  23.7 us (37%)
  starting transfers between devices  18.9 us (29%)
  waiting for transfers between devices  13 us (20%)
  Pallas kernels  8.67 us (13%)
    all_to_all x1, blocking collectives, body(): lax.all_to_all(coded, every, split_axis=0, concat_axis=0, tiled=True)  23.7 us
    ppermute x6, waiting for transfers between devices, along(): return lax.ppermute(values, seat, hops)  10.1 us
    ppermute x8, starting transfers between devices, across(): return lax.ppermute(values, seat, [(s, s ^ cols) for s in range(SEATS)])  9.77 us
    ppermute x6, starting transfers between devices, along(): return lax.ppermute(values, seat, hops)  9.12 us
    pallas_call x3, Pallas kernels, add_products(): pl.pallas_call(functools.partial(product_kernel, sizes, tile_count, passe...  4.16 us
    pallas_call x1, Pallas kernels, body(): pl.pallas_call(functools.partial(pack_kernel, cols), out_shape=[jax.Shape...  2.77 us
    ppermute x1, waiting for transfers between devices, opposite(): lax.ppermute(values, seat, [(s, s ^ SEATS - 1 - cols) for s in range(SEAT...  1.66 us
  transfers between devices with their start and end apart: 15, of which 9 were waited for; matrix products, arithmetic and copies ran while one was open for 0% of the time, Pallas kernels for 4%

profile of v27, /device:TPU:1, one launch (start us, length us, event | category | flops | bytes accessed | tf_op | source)
XLA Modules:
  0.0 64.4 jit_solution(8125859142410665277)
XLA Ops:
  0.0 2.8 %pack.1 = (bf16[1424,128]{1,0:T(8,128)(2,1)}, bf16[1808,128]{1,0:T(8,128)(2,1)}, bf16[1808,128]{1,0:T(8,128)(2,1)}, bf16[1808,128]{1,0:T(8,128)(2,1)}, bf16[1424,128]{1,0:T(8,128)(2,1)}) custom-call(s32[2,4]{1,0:T(2,128)} %bitcast.5, s32[4,6]{1,0:T(4,128)} %q_ids.1, bf16[1024,128]{1,0:T(8,128)(2,1)} %bitcast.4, bf16[4,6,128,128]{3,2,1,0:T(8,128)(2,1)} %q_ref.1), custom_call_target="tpu_custom_call" | custom-call | tf_op jit(solution)/shard_map/pack/pallas_call | solution.py:224
  2.8 2.1 %collective-permute-start.2 = (bf16[1808,128]{1,0:T(8,128)(2,1)}, bf16[1808,128]{1,0:T(8,128)(2,1)S(1)}, u32[]{:S(2)}, u32[]{:S(2)}) collective-permute-start(bf16[1808,128]{1,0:T(8,128)(2,1)} %get-tuple-element.18), channel_id=1, source_target_pairs={{0,1},{1,0},{2,6},{3,7},{4,5},{5,4},{6,2},{7,3},{8,9},{9,8},{10,14... | collective-permute-start | bytes 1388552 | tf_op jit(solution)/shard_map/ppermute | solution.py:243
  4.9 1.3 %collective-permute-start.4 = (bf16[1808,128]{1,0:T(8,128)(2,1)}, bf16[1808,128]{1,0:T(8,128)(2,1)S(1)}, u32[]{:S(2)}, u32[]{:S(2)}) collective-permute-start(bf16[1808,128]{1,0:T(8,128)(2,1)} %get-tuple-element.19), channel_id=1, source_target_pairs={{0,4},{1,5},{2,10},{3,11},{4,0},{5,1},{6,14},{7,15},{8,12},{9,13},... | collective-permute-start | bytes 1388552 | tf_op jit(solution)/shard_map/ppermute | solution.py:243
  6.2 1.2 %collective-permute-start = (bf16[1808,128]{1,0:T(8,128)(2,1)}, bf16[1808,128]{1,0:T(8,128)(2,1)S(1)}, u32[]{:S(2)}, u32[]{:S(2)}) collective-permute-start(bf16[1808,128]{1,0:T(8,128)(2,1)} %get-tuple-element.16), channel_id=1, source_target_pairs={{0,8},{1,9},{2,3},{3,2},{4,12},{5,13},{6,7},{7,6},{8,0},{9,1},{10,... | collective-permute-start | bytes 1388552 | tf_op jit(solution)/shard_map/ppermute | solution.py:243
  7.4 1.5 %collective-permute-start.7 = (bf16[1424,128]{1,0:T(8,128)(2,1)}, bf16[1424,128]{1,0:T(8,128)(2,1)S(1)}, u32[]{:S(2)}, u32[]{:S(2)}) collective-permute-start(bf16[1424,128]{1,0:T(8,128)(2,1)} %get-tuple-element.20.refs_0_), channel_id=1, source_target_pairs={{0,2},{1,3},{2,0},{3,1},{4,6},{5,7},{6,4},{7,5},{8,10},{9,11},{10,... | collective-permute-start | bytes 1093640 | tf_op jit(solution)/shard_map/ppermute | solution.py:246
  8.9 0.0 collective-permute-start.1
  8.9 4.3 %collective-permute-done.2.in_ref.refs_2_ = bf16[1808,128]{1,0:T(8,128)(2,1)S(1)} collective-permute-done((bf16[1808,128]{1,0:T(8,128)(2,1)}, bf16[1808,128]{1,0:T(8,128)(2,1)S(1)}, u32[]{:S(2)}, u32[]{:S(2)}) %collective-permute-start.2) | collective-permute-done | bytes 462880 | tf_op jit(solution)/shard_map/ppermute | solution.py:243
  13.3 0.2 rest_of_packet.3
  13.5 1.9 %collective-permute-start.3 = (bf16[1424,128]{1,0:T(8,128)(2,1)S(1)}, bf16[1424,128]{1,0:T(8,128)(2,1)S(1)}, u32[]{:S(2)}, u32[]{:S(2)}) collective-permute-start(bf16[1424,128]{1,0:T(8,128)(2,1)S(1)} %rest_of_packet.3), channel_id=1, source_target_pairs={{0,4},{1,5},{2,10},{3,11},{4,0},{5,1},{6,14},{7,15},{8,12},{9,13},... | collective-permute-start | bytes 1093640 | tf_op jit(solution)/shard_map/ppermute | solution.py:243
  15.3 0.0 collective-permute-done.4.in_ref.refs_3_
  15.3 0.2 rest_of_packet.4
  15.5 0.0 copy-start
  15.5 2.3 %collective-permute-start.5 = (bf16[1424,128]{1,0:T(8,128)(2,1)S(1)}, bf16[1424,128]{1,0:T(8,128)(2,1)S(1)}, u32[]{:S(2)}, u32[]{:S(2)}) collective-permute-start(bf16[1424,128]{1,0:T(8,128)(2,1)S(1)} %rest_of_packet.4), channel_id=1, source_target_pairs={{0,8},{1,9},{2,3},{3,2},{4,12},{5,13},{6,7},{7,6},{8,0},{9,1},{10,... | collective-permute-start | bytes 1093640 | tf_op jit(solution)/shard_map/ppermute | solution.py:243
  17.8 2.2 %collective-permute-done.in_ref.refs_4_ = bf16[1808,128]{1,0:T(8,128)(2,1)S(1)} collective-permute-done((bf16[1808,128]{1,0:T(8,128)(2,1)}, bf16[1808,128]{1,0:T(8,128)(2,1)S(1)}, u32[]{:S(2)}, u32[]{:S(2)}) %collective-permute-start) | collective-permute-done | bytes 462880 | tf_op jit(solution)/shard_map/ppermute | solution.py:243
  20.0 2.8 %collective-permute-start.13 = (bf16[1808,128]{1,0:T(8,128)(2,1)S(1)}, bf16[1808,128]{1,0:T(8,128)(2,1)S(1)}, u32[]{:S(2)}, u32[]{:S(2)}) collective-permute-start(bf16[1808,128]{1,0:T(8,128)(2,1)S(1)} %collective-permute-done.2.in_ref.refs_2_), channel_id=1, source_target_pairs={{0,2},{1,3},{2,0},{3,1},{4,6},{5,7},{6,4},{7,5},{8,10},{9,11},{10,... | collective-permute-start | bytes 1388552 | tf_op jit(solution)/shard_map/ppermute | solution.py:246
  22.8 0.2 rest_of_packet.5
  22.9 0.0 collective-permute-done.7.refs_1_
  22.9 0.3 collective-permute-start.6
  23.2 1.7 %collective-permute-done.1.refs_2_ = bf16[1424,128]{1,0:T(8,128)(2,1)S(1)} collective-permute-done((bf16[1424,128]{1,0:T(8,128)(2,1)}, bf16[1424,128]{1,0:T(8,128)(2,1)S(1)}, u32[]{:S(2)}, u32[]{:S(2)}) %collective-permute-start.1) | collective-permute-done | bytes 364576 | tf_op jit(solution)/shard_map/ppermute | solution.py:253
  24.9 3.5 %collective-permute-start.14 = (bf16[1808,128]{1,0:T(8,128)(2,1)S(1)}, bf16[1808,128]{1,0:T(8,128)(2,1)S(1)}, u32[]{:S(2)}, u32[]{:S(2)}) collective-permute-start(bf16[1808,128]{1,0:T(8,128)(2,1)S(1)} %collective-permute-done.4.in_ref.refs_3_), channel_id=1, source_target_pairs={{0,2},{1,3},{2,0},{3,1},{4,6},{5,7},{6,4},{7,5},{8,10},{9,11},{10,... | collective-permute-start | bytes 1388552 | tf_op jit(solution)/shard_map/ppermute | solution.py:246
  28.4 0.0 copy-done
  28.4 1.2 %products.3.refs_6_ = f32[256,8,128]{2,1,0:T(8,128)S(1)} custom-call(bf16[1424,128]{1,0:T(8,128)(2,1)S(1)} %copy-done, bf16[1424,128]{1,0:T(8,128)(2,1)S(1)} %collective-permute-done.7.refs_1_, bf16[1808,128]{1,0:T(8,128)(2,1)S(1)} %collective-permute-done.2.in_ref.refs_2_, bf16[1808,128]{1,0:T(8,128)(2,1)S(1)} %collective-permute-done.4.in_ref.refs_3_, ...), custom_call_target="tpu_custom_call" | custom-call | flops 62914560 | bytes 5242880 | tf_op jit(solution)/shard_map/products/pallas_call | solution.py:173
  29.6 0.8 %collective-permute-done.3.refs_3_ = bf16[1424,128]{1,0:T(8,128)(2,1)S(1)} collective-permute-done((bf16[1424,128]{1,0:T(8,128)(2,1)S(1)}, bf16[1424,128]{1,0:T(8,128)(2,1)S(1)}, u32[]{:S(2)}, u32[]{:S(2)}) %collective-permute-start.3) | collective-permute-done | bytes 364576 | tf_op jit(solution)/shard_map/ppermute | solution.py:243
  30.3 1.6 %collective-permute-done.5.refs_4_ = bf16[1424,128]{1,0:T(8,128)(2,1)S(1)} collective-permute-done((bf16[1424,128]{1,0:T(8,128)(2,1)S(1)}, bf16[1424,128]{1,0:T(8,128)(2,1)S(1)}, u32[]{:S(2)}, u32[]{:S(2)}) %collective-permute-start.5) | collective-permute-done | bytes 364576 | tf_op jit(solution)/shard_map/ppermute | solution.py:243
  32.0 1.2 %collective-permute-done.6.refs_5_ = bf16[1424,128]{1,0:T(8,128)(2,1)S(1)} collective-permute-done((bf16[1424,128]{1,0:T(8,128)(2,1)S(1)}, bf16[1424,128]{1,0:T(8,128)(2,1)S(1)}, u32[]{:S(2)}, u32[]{:S(2)}) %collective-permute-start.6) | collective-permute-done | bytes 364576 | tf_op jit(solution)/shard_map/ppermute | solution.py:243
  33.2 0.9 %collective-permute-start.8 = (bf16[1808,128]{1,0:T(8,128)(2,1)S(1)}, bf16[1808,128]{1,0:T(8,128)(2,1)S(1)}, u32[]{:S(2)}, u32[]{:S(2)}) collective-permute-start(bf16[1808,128]{1,0:T(8,128)(2,1)S(1)} %collective-permute-done.in_ref.refs_4_), channel_id=1, source_target_pairs={{0,2},{1,3},{2,0},{3,1},{4,6},{5,7},{6,4},{7,5},{8,10},{9,11},{10,... | collective-permute-start | bytes 1388552 | tf_op jit(solution)/shard_map/ppermute | solution.py:246
  34.1 0.0 collective-permute-start.10
  34.1 0.5 collective-permute-start.11
  34.6 0.0 collective-permute-done.13.refs_0_
  34.6 0.0 collective-permute-start.12
  34.6 0.0 collective-permute-done.14.refs_1_
  34.6 0.5 collective-permute-start.9
  35.1 1.2 %products.4.refs_5_ = f32[256,8,128]{2,1,0:T(8,128)S(1)} custom-call(bf16[1808,128]{1,0:T(8,128)(2,1)S(1)} %collective-permute-done.13.refs_0_, bf16[1808,128]{1,0:T(8,128)(2,1)S(1)} %collective-permute-done.14.refs_1_, bf16[1424,128]{1,0:T(8,128)(2,1)S(1)} %collective-permute-done.1.refs_2_, ...), custom_call_target="tpu_custom_call", output_to_operand_aliasing={{}: (6, {})} | custom-call | flops 75497472 | bytes 6291456 | tf_op jit(solution)/shard_map/products/pallas_call | solution.py:173
  36.4 0.0 collective-permute-done.10.refs_2_
  36.4 0.2 collective-permute-done.11.refs_3_
  36.6 0.5 collective-permute-done.12.refs_4_
  37.1 0.5 collective-permute-done.9.refs_1_
  37.6 0.0 collective-permute-done.8.refs_0_
  37.6 1.8 %products.5 = s32[32,5,8,128]{3,2,1,0:T(8,128)S(1)} custom-call(bf16[1808,128]{1,0:T(8,128)(2,1)S(1)} %collective-permute-done.8.refs_0_, bf16[1424,128]{1,0:T(8,128)(2,1)S(1)} %collective-permute-done.9.refs_1_, bf16[1424,128]{1,0:T(8,128)(2,1)S(1)} %collective-permute-done.10.refs_2_, bf16[1424,128]{1,0:T(8,128)(2,1)S(1)} %collective-permute-done.11.refs_3_, ...), custom_call_target="tpu_custom_call" | custom-call | flops 62914560 | bytes 5242880 | tf_op jit(solution)/shard_map/products/pallas_call | solution.py:173
  39.4 23.7 %all_to_all.5 = s32[32,5,8,128]{3,2,1,0:T(8,128)S(1)} all-to-all(s32[32,5,8,128]{3,2,1,0:T(8,128)S(1)} %products.5), channel_id=1, replica_groups=mesh['plane'=2,'pair'=4,'core'=2,'col'=2] {'plane','pair','core','col'}, dimensions={0} | all-to-all | bytes 1310720 | tf_op jit(solution)/shard_map/all_to_all | solution.py:267
  63.1 1.3 %turn.1 = f32[128,1024]{1,0:T(8,128)} custom-call(s32[2,16,5,8,128]{4,3,2,1,0:T(8,128)S(1)} %bitcast.3), custom_call_target="tpu_custom_call" | custom-call | tf_op jit(solution)/shard_map/turn/pallas_call | solution.py:268
Async XLA Ops:
  2.8 10.5 %collective-permute-start.2 = (bf16[1808,128]{1,0:T(8,128)(2,1)}, bf16[1808,128]{1,0:T(8,128)(2,1)S(1)}, u32[]{:S(2)}, u32[]{:S(2)}) collective-permute-start(bf16[1808,128]{1,0:T(8,128)(2,1)} %get-tuple-element.18), channel_id=1, source_target_pairs={{0,1},{1,0},{2,6},{3,7},{4,5},{5,4},{6,2},{7,3},{8,9},{9,8},{10,14... | collective-permute-start | bytes 1388552 | tf_op jit(solution)/shard_map/ppermute | solution.py:243
  4.9 10.4 %collective-permute-start.4 = (bf16[1808,128]{1,0:T(8,128)(2,1)}, bf16[1808,128]{1,0:T(8,128)(2,1)S(1)}, u32[]{:S(2)}, u32[]{:S(2)}) collective-permute-start(bf16[1808,128]{1,0:T(8,128)(2,1)} %get-tuple-element.19), channel_id=1, source_target_pairs={{0,4},{1,5},{2,10},{3,11},{4,0},{5,1},{6,14},{7,15},{8,12},{9,13},... | collective-permute-start | bytes 1388552 | tf_op jit(solution)/shard_map/ppermute | solution.py:243
  6.2 13.8 %collective-permute-start = (bf16[1808,128]{1,0:T(8,128)(2,1)}, bf16[1808,128]{1,0:T(8,128)(2,1)S(1)}, u32[]{:S(2)}, u32[]{:S(2)}) collective-permute-start(bf16[1808,128]{1,0:T(8,128)(2,1)} %get-tuple-element.16), channel_id=1, source_target_pairs={{0,8},{1,9},{2,3},{3,2},{4,12},{5,13},{6,7},{7,6},{8,0},{9,1},{10,... | collective-permute-start | bytes 1388552 | tf_op jit(solution)/shard_map/ppermute | solution.py:243
  7.4 15.5 %collective-permute-start.7 = (bf16[1424,128]{1,0:T(8,128)(2,1)}, bf16[1424,128]{1,0:T(8,128)(2,1)S(1)}, u32[]{:S(2)}, u32[]{:S(2)}) collective-permute-start(bf16[1424,128]{1,0:T(8,128)(2,1)} %get-tuple-element.20.refs_0_), channel_id=1, source_target_pairs={{0,2},{1,3},{2,0},{3,1},{4,6},{5,7},{6,4},{7,5},{8,10},{9,11},{10,... | collective-permute-start | bytes 1093640 | tf_op jit(solution)/shard_map/ppermute | solution.py:246
  8.9 16.0 %collective-permute-start.1 = (bf16[1424,128]{1,0:T(8,128)(2,1)}, bf16[1424,128]{1,0:T(8,128)(2,1)S(1)}, u32[]{:S(2)}, u32[]{:S(2)}) collective-permute-start(bf16[1424,128]{1,0:T(8,128)(2,1)} %get-tuple-element.17), channel_id=1, source_target_pairs={{0,13},{1,12},{2,15},{3,14},{4,9},{5,8},{6,11},{7,10},{8,5},{9,4},... | collective-permute-start | bytes 1093640 | tf_op jit(solution)/shard_map/ppermute | solution.py:253
  13.5 16.9 %collective-permute-start.3 = (bf16[1424,128]{1,0:T(8,128)(2,1)S(1)}, bf16[1424,128]{1,0:T(8,128)(2,1)S(1)}, u32[]{:S(2)}, u32[]{:S(2)}) collective-permute-start(bf16[1424,128]{1,0:T(8,128)(2,1)S(1)} %rest_of_packet.3), channel_id=1, source_target_pairs={{0,4},{1,5},{2,10},{3,11},{4,0},{5,1},{6,14},{7,15},{8,12},{9,13},... | collective-permute-start | bytes 1093640 | tf_op jit(solution)/shard_map/ppermute | solution.py:243
  15.5 12.9 %copy-start = (bf16[1424,128]{1,0:T(8,128)(2,1)S(1)}, bf16[1424,128]{1,0:T(8,128)(2,1)}, u32[]{:S(2)}) copy-start(bf16[1424,128]{1,0:T(8,128)(2,1)} %get-tuple-element.20.refs_0_) | copy-start | bytes 1093636
  15.5 16.5 %collective-permute-start.5 = (bf16[1424,128]{1,0:T(8,128)(2,1)S(1)}, bf16[1424,128]{1,0:T(8,128)(2,1)S(1)}, u32[]{:S(2)}, u32[]{:S(2)}) collective-permute-start(bf16[1424,128]{1,0:T(8,128)(2,1)S(1)} %rest_of_packet.4), channel_id=1, source_target_pairs={{0,8},{1,9},{2,3},{3,2},{4,12},{5,13},{6,7},{7,6},{8,0},{9,1},{10,... | collective-permute-start | bytes 1093640 | tf_op jit(solution)/shard_map/ppermute | solution.py:243
  20.0 14.6 %collective-permute-start.13 = (bf16[1808,128]{1,0:T(8,128)(2,1)S(1)}, bf16[1808,128]{1,0:T(8,128)(2,1)S(1)}, u32[]{:S(2)}, u32[]{:S(2)}) collective-permute-start(bf16[1808,128]{1,0:T(8,128)(2,1)S(1)} %collective-permute-done.2.in_ref.refs_2_), channel_id=1, source_target_pairs={{0,2},{1,3},{2,0},{3,1},{4,6},{5,7},{6,4},{7,5},{8,10},{9,11},{10,... | collective-permute-start | bytes 1388552 | tf_op jit(solution)/shard_map/ppermute | solution.py:246
  22.9 10.2 %collective-permute-start.6 = (bf16[1424,128]{1,0:T(8,128)(2,1)S(1)}, bf16[1424,128]{1,0:T(8,128)(2,1)S(1)}, u32[]{:S(2)}, u32[]{:S(2)}) collective-permute-start(bf16[1424,128]{1,0:T(8,128)(2,1)S(1)} %rest_of_packet.5), channel_id=1, source_target_pairs={{0,1},{1,0},{2,6},{3,7},{4,5},{5,4},{6,2},{7,3},{8,9},{9,8},{10,14... | collective-permute-start | bytes 1093640 | tf_op jit(solution)/shard_map/ppermute | solution.py:243
  24.9 9.7 %collective-permute-start.14 = (bf16[1808,128]{1,0:T(8,128)(2,1)S(1)}, bf16[1808,128]{1,0:T(8,128)(2,1)S(1)}, u32[]{:S(2)}, u32[]{:S(2)}) collective-permute-start(bf16[1808,128]{1,0:T(8,128)(2,1)S(1)} %collective-permute-done.4.in_ref.refs_3_), channel_id=1, source_target_pairs={{0,2},{1,3},{2,0},{3,1},{4,6},{5,7},{6,4},{7,5},{8,10},{9,11},{10,... | collective-permute-start | bytes 1388552 | tf_op jit(solution)/shard_map/ppermute | solution.py:246
  33.2 4.5 %collective-permute-start.8 = (bf16[1808,128]{1,0:T(8,128)(2,1)S(1)}, bf16[1808,128]{1,0:T(8,128)(2,1)S(1)}, u32[]{:S(2)}, u32[]{:S(2)}) collective-permute-start(bf16[1808,128]{1,0:T(8,128)(2,1)S(1)} %collective-permute-done.in_ref.refs_4_), channel_id=1, source_target_pairs={{0,2},{1,3},{2,0},{3,1},{4,6},{5,7},{6,4},{7,5},{8,10},{9,11},{10,... | collective-permute-start | bytes 1388552 | tf_op jit(solution)/shard_map/ppermute | solution.py:246
  34.1 2.3 %collective-permute-start.10 = (bf16[1424,128]{1,0:T(8,128)(2,1)S(1)}, bf16[1424,128]{1,0:T(8,128)(2,1)S(1)}, u32[]{:S(2)}, u32[]{:S(2)}) collective-permute-start(bf16[1424,128]{1,0:T(8,128)(2,1)S(1)} %collective-permute-done.3.refs_3_), channel_id=1, source_target_pairs={{0,2},{1,3},{2,0},{3,1},{4,6},{5,7},{6,4},{7,5},{8,10},{9,11},{10,... | collective-permute-start | bytes 1093640 | tf_op jit(solution)/shard_map/ppermute | solution.py:246
  34.1 2.5 %collective-permute-start.11 = (bf16[1424,128]{1,0:T(8,128)(2,1)S(1)}, bf16[1424,128]{1,0:T(8,128)(2,1)S(1)}, u32[]{:S(2)}, u32[]{:S(2)}) collective-permute-start(bf16[1424,128]{1,0:T(8,128)(2,1)S(1)} %collective-permute-done.5.refs_4_), channel_id=1, source_target_pairs={{0,2},{1,3},{2,0},{3,1},{4,6},{5,7},{6,4},{7,5},{8,10},{9,11},{10,... | collective-permute-start | bytes 1093640 | tf_op jit(solution)/shard_map/ppermute | solution.py:246
  34.6 2.5 %collective-permute-start.12 = (bf16[1424,128]{1,0:T(8,128)(2,1)S(1)}, bf16[1424,128]{1,0:T(8,128)(2,1)S(1)}, u32[]{:S(2)}, u32[]{:S(2)}) collective-permute-start(bf16[1424,128]{1,0:T(8,128)(2,1)S(1)} %collective-permute-done.6.refs_5_), channel_id=1, source_target_pairs={{0,2},{1,3},{2,0},{3,1},{4,6},{5,7},{6,4},{7,5},{8,10},{9,11},{10,... | collective-permute-start | bytes 1093640 | tf_op jit(solution)/shard_map/ppermute | solution.py:246
  34.6 3.0 %collective-permute-start.9 = (bf16[1424,128]{1,0:T(8,128)(2,1)S(1)}, bf16[1424,128]{1,0:T(8,128)(2,1)S(1)}, u32[]{:S(2)}, u32[]{:S(2)}) collective-permute-start(bf16[1424,128]{1,0:T(8,128)(2,1)S(1)} %collective-permute-done.1.refs_2_), channel_id=1, source_target_pairs={{0,2},{1,3},{2,0},{3,1},{4,6},{5,7},{6,4},{7,5},{8,10},{9,11},{10,... | collective-permute-start | bytes 1093640 | tf_op jit(solution)/shard_map/ppermute | solution.py:246
